TPU v7x, 32 devices: a whole 2x2x4 slice. The times are simulated.
32 devices in a mesh: dp: 4 (over z), feat: 8 (over y, x, core).
Axes of the slice: x: 2, y: 2, z: 4, core: 2. Of those that a mesh axis runs over, the one named last changes fastest.
Arguments:
- z_anchor: bfloat16 [2048, 8192], P('dp', 'feat'), may hold values from -54 to 54
- z_other: bfloat16 [2048, 8192], P('dp', 'feat'), may hold values from -54 to 54
Outputs:
- scaled_grad: float32 [2048, 8192], P('dp', 'feat')
All inputs are finite; a program needn't handle non-finite values.
Results may differ from a plain program's by a relative error of at most 0.0035.
Values may be sent and summed in bfloat16 or wider, within the bound.
No kernel may reach another device: no remote copies, remote signals or barrier semaphores. Data moves between devices by JAX's collectives and lax.ppermute only.
A program may use at most 128 MiB of HBM per device.

v0:
```python
import jax
import jax.numpy as jnp
from jax import lax
from jax.sharding import PartitionSpec as P


def per_device(z_anchor, z_other):
    rows_here, width = z_anchor.shape
    parts = lax.axis_size("feat")
    groups = lax.axis_size("dp")
    total = rows_here * groups
    here = lax.axis_index("feat")
    anchor = z_anchor.astype(jnp.float32)
    sums = lax.psum(jnp.sum(anchor, axis=0), "dp")
    mean = sums / total
    centered = anchor - mean
    spread = lax.psum(jnp.sum(centered * centered, axis=0), "dp")
    variance = spread / (total - 1)
    deviation = jnp.sqrt(variance + 0.0001)
    rounded = centered.astype(jnp.bfloat16)
    blocks = lax.all_gather(rounded[None], "feat", axis=0, tiled=True)
    turned = jnp.roll(blocks, -here, 0)
    tile_rows = width // groups
    slices = lax.psum_scatter(
        jnp.einsum("bi,kbj->ikj", rounded, turned, preferred_element_type=jnp.float32).astype(
            jnp.bfloat16
        ),
        "dp",
        scatter_dimension=0,
        tiled=True,
    ).astype(jnp.float32)
    row_ids = lax.axis_index("dp") * tile_rows + jnp.arange(tile_rows)
    on_diagonal = (jnp.arange(parts)[None, :, None] == 0) & (
        row_ids[:, None, None] == jnp.arange(width)[None, None, :]
    )
    coef = 2.0 * total / (25.0 * (total - 1))
    weights = jnp.where(on_diagonal, 0.0, coef * (slices / (total - 1))).astype(jnp.bfloat16)
    weights_k = jnp.transpose(weights, (1, 0, 2))
    full = lax.all_gather(weights_k, "dp", axis=1, tiled=True)
    update = jnp.einsum("kbj,kij->bi", turned, full, preferred_element_type=jnp.float32)
    hinge = jnp.where(deviation < 1.0, centered / deviation, 0.0)
    factor = total / (4.0 * (total - 1))
    return anchor - z_other.astype(jnp.float32) - factor * hinge + update


def solution(mesh):
    placed = (P("dp", "feat"), P("dp", "feat"))
    return jax.shard_map(
        per_device, mesh=mesh, in_specs=placed, out_specs=P("dp", "feat"), check_vma=False
    )
```

profile of v0, /device:TPU:9, one launch (start us, length us, event | category | flops | bytes accessed | tf_op | source)
XLA Modules:
  0.0 684.5 jit_solution(6849902717624423091)
XLA Ops:
  6.5 0.0 all-gather.6.cloned.1.call-start
  6.5 1.4 convert_reduce_fusion
  7.9 7.3 %psum.14 = f32[1024]{0:T(1024)S(1)} all-reduce(f32[1024]{0:T(1024)S(1)} %convert_reduce_fusion), channel_id=1, replica_groups=mesh['dp'=4,'feat'=8] {'dp'}, use_global_device_ids=true, to_apply=%region_1.0 | all-reduce | flops 1024 | bytes 8192 | tf_op jit(solution)/shard_map/psum | solution.py:14
  15.2 2.5 fusion.5
  17.7 0.0 all-gather.6.cloned.1.call-update
  17.8 0.0 reduce-scatter.2.cloned.1.call-start
  17.8 57.8 %all-gather.6.cloned.1.call-done = bf16[4096,1024]{1,0:T(8,128)(2,1)} async-done(((bf16[512,1024]{1,0:T(8,128)(2,1)}), bf16[4096,1024]{1,0:T(8,128)(2,1)}) %all-gather.6.cloned.1.call-update) | async-done | bytes 8388624 | tf_op jit(solution)/shard_map/all_gather | solution.py:21
  75.6 15.2 %convolution_convert_fusion = bf16[1024,8,1024]{2,0,1:T(8,128)(2,1)} fusion(bf16[512,1024]{1,0:T(8,128)(2,1)} %get-tuple-element.6, s32[]{:T(128)S(6)} %select_n.23, bf16[8,512,1024]{2,1,0:T(8,128)(2,1)} %bitcast.9), kind=kOutput, calls=%fused_computation.2 | convolution fusion | flops 8615100416 | bytes 26214404 | tf_op jit(solution)/shard_map/bi,kbj->ikj/dot_general | solution.py:25
  90.8 0.0 reduce-scatter.2.cloned.1.call-update
  90.8 0.0 copy-start
  90.8 0.0 copy-start.1
  90.8 0.0 all-gather.4.cloned.1.call-start
  90.9 0.2 iota_compare_fusion
  91.1 276.7 %reduce-scatter.2.cloned.1.call-done = bf16[256,8,1024]{2,0,1:T(8,128)(2,1)} async-done(((bf16[1024,8,1024]{2,0,1:T(8,128)(2,1)}), bf16[256,8,1024]{2,0,1:T(8,128)(2,1)}) %reduce-scatter.2.cloned.1.call-update) | async-done | bytes 4194320 | tf_op jit(solution)/shard_map/reduce_scatter | solution.py:24
  367.8 6.2 fusion.1
  374.0 0.0 all-gather.4.cloned.1.call-update
  374.0 10.7 %psum.15 = f32[1024]{0:T(1024)S(1)} all-reduce(f32[1024]{0:T(1024)S(1)} %get-tuple-element.5), channel_id=1, replica_groups=mesh['dp'=4,'feat'=8] {'dp'}, use_global_device_ids=true, to_apply=%region_3.0 | all-reduce | flops 1024 | bytes 8192 | tf_op jit(solution)/shard_map/psum | solution.py:17
  384.7 277.1 %all-gather.4.cloned.1.call-done = bf16[8,1024,1024]{2,1,0:T(8,128)(2,1)} async-done(((bf16[8,256,1024]{2,1,0:T(8,128)(2,1)}), bf16[8,1024,1024]{2,1,0:T(8,128)(2,1)}) %all-gather.4.cloned.1.call-update) | async-done | bytes 16777232 | tf_op jit(solution)/shard_map/all_gather | solution.py:39
  661.9 0.0 copy-done
  661.9 0.0 copy-done.1
  661.9 16.1 %fusion.9 = f32[512,1024]{1,0:T(8,128)} fusion(bf16[512,1024]{1,0:T(8,128)(2,1)S(1)} %copy-done, bf16[512,1024]{1,0:T(8,128)(2,1)S(1)} %copy-done.1, bf16[8,1024,1024]{2,1,0:T(8,128)(2,1)} %all-gather.4.cloned.1.call-done, f32[1024]{0:T(1024)S(1)} %add_sqrt_fusion, f32[1024]{0:T(1024)S(1)} %broadcast_multiply_fusion, ...), kind=kOutput, calls=%fused_computation.16 | convolution fusion | flops 8598847488 | bytes 29369348 | tf_op jit(solution)/shard_map/kbj,kij->bi/dot_general | solution.py:40
  (5 shorter events, 0.0 us)
Async XLA Ops:
  6.5 69.1 %all-gather.6.cloned.1.call-start = ((), (), s32[]{:S(2)}) async-start(), calls=%async_computation.3 | async-start | bytes 9437184 | tf_op jit(solution)/shard_map/all_gather | solution.py:21
  17.8 350.0 %reduce-scatter.2.cloned.1.call-start = ((), (), s32[]{:S(2)}) async-start(), calls=%async_computation.1 | async-start | bytes 20971520 | tf_op jit(solution)/shard_map/reduce_scatter | solution.py:24
  90.8 571.1 %copy-start = (bf16[512,1024]{1,0:T(8,128)(2,1)S(1)}, bf16[512,1024]{1,0:T(8,128)(2,1)}, u32[]{:S(2)}) copy-start(bf16[512,1024]{1,0:T(8,128)(2,1)} %param.2) | copy-start | bytes 3145732
  90.8 571.1 %copy-start.1 = (bf16[512,1024]{1,0:T(8,128)(2,1)S(1)}, bf16[512,1024]{1,0:T(8,128)(2,1)}, u32[]{:S(2)}) copy-start(bf16[512,1024]{1,0:T(8,128)(2,1)} %param.3) | copy-start | bytes 3145732
  90.8 571.1 %all-gather.4.cloned.1.call-start = ((), (), s32[]{:S(2)}) async-start(), calls=%async_computation.2 | async-start | bytes 20971520 | tf_op jit(solution)/shard_map/all_gather | solution.py:39
Sparse Core Ops, SparseCore 0:
  17.9 57.6 all-gather.5
  90.9 276.8 reduce-scatter.1
  374.1 287.7 all-gather.3
where the time goes:
time: 689 us; the launch traced here: 684 us
  waiting for transfers between devices  612 us (89%)
  matrix products  31.2 us (5%)
  blocking collectives  18 us (3%)
  between operations  13.2 us (2%)
  other arithmetic  10.3 us (1%)
    all_gather x1, waiting for transfers between devices, per_device(): full = lax.all_gather(weights_k, 'dp', axis=1, tiled=True)  277 us
    reduce_scatter x1, waiting for transfers between devices, per_device(): lax.psum_scatter(jnp.einsum('bi,kbj->ikj', rounded, turned, preferred_ele...  277 us
    all_gather x1, waiting for transfers between devices, per_device(): blocks = lax.all_gather(rounded[None], 'feat', axis=0, tiled=True)  57.8 us
    dot_general x1, matrix products, per_device(): jnp.einsum('kbj,kij->bi', turned, full, preferred_element_type=jnp.float32)  16.1 us
    dot_general x1, matrix products, per_device(): jnp.einsum('bi,kbj->ikj', rounded, turned, preferred_element_type=jnp.flo...  15.2 us
  transfers between devices with their start and end apart: 3, of which 3 were waited for; matrix products, arithmetic and copies ran while one was open for 0% of the time, Pallas kernels for 0%

commit v1 on v0

v1 whole, which is shorter than its diff:
```python
import jax
import jax.numpy as jnp
from jax import lax
from jax.sharding import PartitionSpec as P


def per_device(z_anchor, z_other):
    rows_here, width = z_anchor.shape
    groups = lax.axis_size("dp")
    total = rows_here * groups
    mine = lax.axis_index("dp") * rows_here
    column = lax.all_gather(z_anchor, "dp", axis=0, tiled=True).astype(jnp.float32)
    mean = jnp.sum(column, axis=0) / total
    centered_all = column - mean
    variance = jnp.sum(centered_all * centered_all, axis=0) / (total - 1)
    deviation = jnp.sqrt(variance + 0.0001)
    rounded_all = centered_all.astype(jnp.bfloat16)
    widened = rounded_all.astype(jnp.float32)
    own_square = jnp.sum(widened * widened, axis=0)
    rounded = lax.dynamic_slice_in_dim(rounded_all, mine, rows_here, 0)
    part = lax.dot_general(
        rounded, rounded_all, (((1,), (1,)), ((), ())), preferred_element_type=jnp.float32
    )
    inner = lax.psum(part.astype(jnp.bfloat16), "feat")
    product = jnp.dot(inner, rounded_all, preferred_element_type=jnp.float32)
    coef = 2.0 * total / (25.0 * (total - 1)) / (total - 1)
    update = coef * (product - rounded.astype(jnp.float32) * own_square)
    anchor = z_anchor.astype(jnp.float32)
    centered = anchor - mean
    hinge = jnp.where(deviation < 1.0, centered / deviation, 0.0)
    factor = total / (4.0 * (total - 1))
    return anchor - z_other.astype(jnp.float32) - factor * hinge + update


def solution(mesh):
    placed = (P("dp", "feat"), P("dp", "feat"))
    return jax.shard_map(
        per_device, mesh=mesh, in_specs=placed, out_specs=P("dp", "feat"), check_vma=False
    )
```

time: 689 us -> 177 us (0.26)
  waiting for transfers between devices: 612 us -> 143 us
  matrix products: 31.2 us -> 11 us
  blocking collectives: 18 us -> 0 us
    reduce_scatter x1 -> x0, waiting for transfers between devices: 277 us -> none  [per_device(): lax.psum_scatter(jnp.einsum('bi,kbj->ikj', rounded, turned, preferred_ele...]
    all_gather x2 -> x1, waiting for transfers between devices: 335 us -> 81.1 us  [per_device(): lax.all_gather(z_anchor, 'dp', axis=0, tiled=True).astype(jnp.float32)]
    psum x0 -> x1, waiting for transfers between devices: none -> 61.5 us  [per_device(): inner = lax.psum(part.astype(jnp.bfloat16), 'feat')]
    dot_general x2, matrix products: 31.2 us -> 11 us  [the longest x1 7.27 us: per_device(): product = jnp.dot(inner, rounded_all, preferred_element_type=jnp.float32)]
    psum x2 -> x0, blocking collectives: 18 us -> none  [the longest x1 10.7 us: per_device(): spread = lax.psum(jnp.sum(centered * centered, axis=0), 'dp')]
  transfers between devices with their start and end apart: 3 -> 2, of which waited for: 3 -> 2; matrix products, arithmetic and copies ran while one was open for 0% -> 0% of each run, Pallas kernels for 0% -> 0%
where the time goes in v1:
time: 177 us; the launch traced here: 175 us
  waiting for transfers between devices  143 us (81%)
  between operations  13.4 us (8%)
  matrix products  11 us (6%)
  other arithmetic  4.61 us (3%)
  local copies, waits for them, and re-layouts  2.33 us (1%)
    all_gather x1, waiting for transfers between devices, per_device(): lax.all_gather(z_anchor, 'dp', axis=0, tiled=True).astype(jnp.float32)  81.1 us
    psum x1, waiting for transfers between devices, per_device(): inner = lax.psum(part.astype(jnp.bfloat16), 'feat')  61.5 us
    dot_general x1, matrix products, per_device(): product = jnp.dot(inner, rounded_all, preferred_element_type=jnp.float32)  7.27 us
    dot_general x1, matrix products, per_device(): lax.dot_general(rounded, rounded_all, (((1,), (1,)), ((), ())), preferred...  3.7 us
  transfers between devices with their start and end apart: 2, of which 2 were waited for; matrix products, arithmetic and copies ran while one was open for 0% of the time, Pallas kernels for 0%

profile of v1, /device:TPU:9, one launch (start us, length us, event | category | flops | bytes accessed | tf_op | source)
XLA Modules:
  0.0 174.7 jit_solution(2412063059657042384)
XLA Ops:
  6.5 0.0 all-gather.2.cloned.1.call-start
  6.5 0.7 all-gather.2.cloned.1.call-update
  7.3 0.0 all-reduce.2.cloned.1.call-start
  7.3 81.1 %all-gather.2.cloned.1.call-done = bf16[2048,1024]{1,0:T(8,128)(2,1)} async-done(((bf16[512,1024]{1,0:T(8,128)(2,1)}), bf16[2048,1024]{1,0:T(8,128)(2,1)}) %all-gather.2.cloned.1.call-update) | async-done | bytes 4194320 | tf_op jit(solution)/shard_map/all_gather | solution.py:12
  88.4 0.0 copy-start
  88.4 3.0 %convert_reduce_fusion = f32[1024]{0:T(1024)S(1)} fusion(bf16[2048,1024]{1,0:T(8,128)(2,1)} %all-gather.2.cloned.1.call-done), kind=kLoop, calls=%fused_computation.1 | loop fusion | flops 4193280 | bytes 4198400 | tf_op jit(solution)/shard_map/reduce_sum | solution.py:13
  91.4 0.4 copy-done
  91.8 1.6 multiply_reduce_fusion
  93.4 0.0 copy-start.1
  93.4 1.9 %copy-done.1 = bf16[2048,1024]{1,0:T(8,128)(2,1)} copy-done((bf16[2048,1024]{1,0:T(8,128)(2,1)}, bf16[2048,1024]{1,0:T(8,128)(2,1)S(1)}, u32[]{:S(2)}) %copy-start.1) | copy-done | bytes 4194328
  95.3 3.7 %convolution_convert_fusion = bf16[512,2048]{1,0:T(8,128)(2,1)} fusion(bf16[2048,1024]{1,0:T(8,128)(2,1)S(1)} %get-tuple-element.6, s32[]{:T(128)S(6)} %select_n.8), kind=kOutput, calls=%fused_computation.6 | convolution fusion | flops 2148532224 | bytes 7340036 | tf_op jit(solution)/shard_map/dot_general | solution.py:21
  99.0 0.0 copy-start.2
  99.0 0.0 copy-start.3
  99.0 0.0 all-reduce.2.cloned.1.call-update
  99.1 61.5 %all-reduce.2.cloned.1.call-done = bf16[512,2048]{1,0:T(8,128)(2,1)} async-done(((bf16[512,2048]{1,0:T(8,128)(2,1)}), bf16[512,2048]{1,0:T(8,128)(2,1)}) %all-reduce.2.cloned.1.call-update) | async-done | bytes 2097168 | tf_op jit(solution)/shard_map/psum | solution.py:24
  160.6 0.0 copy-done.2
  160.6 0.0 copy-done.3
  160.6 7.3 %fusion.4 = f32[512,1024]{1,0:T(8,128)} fusion(bf16[512,1024]{1,0:T(8,128)(2,1)S(1)} %copy-done.2, bf16[512,1024]{1,0:T(8,128)(2,1)S(1)} %copy-done.3, bf16[512,2048]{1,0:T(8,128)(2,1)} %all-reduce.2.cloned.1.call-done, bf16[2048,1024]{1,0:T(8,128)(2,1)} %copy-done.1, f32[1024]{0:T(1024)S(1)} %get-tuple-element.5, f32[1024]{0:T(1024)S(1)} %add_sqrt_fusion, ...), kind=kOutput, calls=%fused_computation.10 | convolution fusion | flops 2154299392 | bytes 11547652 | tf_op jit(solution)/shard_map/dot_general | solution.py:25
  (3 shorter events, 0.0 us)
Async XLA Ops:
  6.5 81.8 %all-gather.2.cloned.1.call-start = ((), (), s32[]{:S(2)}) async-start(), calls=%async_computation | async-start | bytes 5242880 | tf_op jit(solution)/shard_map/all_gather | solution.py:12
  7.3 153.3 %all-reduce.2.cloned.1.call-start = ((), (), s32[]{:S(2)}) async-start(), calls=%async_computation.1 | async-start | bytes 4194304 | tf_op jit(solution)/shard_map/psum | solution.py:24
  88.4 3.4 %copy-start = (bf16[2048,1024]{1,0:T(8,128)(2,1)S(1)}, bf16[2048,1024]{1,0:T(8,128)(2,1)}, u32[]{:S(2)}) copy-start(bf16[2048,1024]{1,0:T(8,128)(2,1)} %all-gather.2.cloned.1.call-done) | copy-start | bytes 12582916
  93.4 1.9 %copy-start.1 = (bf16[2048,1024]{1,0:T(8,128)(2,1)}, bf16[2048,1024]{1,0:T(8,128)(2,1)S(1)}, u32[]{:S(2)}) copy-start(bf16[2048,1024]{1,0:T(8,128)(2,1)S(1)} %get-tuple-element.6) | copy-start | bytes 12582916
  99.0 61.6 %copy-start.2 = (bf16[512,1024]{1,0:T(8,128)(2,1)S(1)}, bf16[512,1024]{1,0:T(8,128)(2,1)}, u32[]{:S(2)}) copy-start(bf16[512,1024]{1,0:T(8,128)(2,1)} %param.2) | copy-start | bytes 3145732
  99.0 61.6 %copy-start.3 = (bf16[512,1024]{1,0:T(8,128)(2,1)S(1)}, bf16[512,1024]{1,0:T(8,128)(2,1)}, u32[]{:S(2)}) copy-start(bf16[512,1024]{1,0:T(8,128)(2,1)} %param.3) | copy-start | bytes 3145732
Sparse Core Ops, SparseCore 0:
  8.9 79.3 all-gather.1
  99.1 61.4 all-reduce.1

commit v2 on v1

v2 whole, which is shorter than its diff:
```python
import jax
import jax.numpy as jnp
from jax import lax
from jax.sharding import PartitionSpec as P

FLOOD = 4
SWAP = 4


def gram(left, right):
    return lax.dot_general(
        left, right, (((1,), (1,)), ((), ())), preferred_element_type=jnp.float32
    )


def dot_t(left, right):
    return lax.dot_general(
        left, right, (((0,), (0,)), ((), ())), preferred_element_type=jnp.float32
    )


def by_gather(z_anchor, z_other):
    rows_here, width = z_anchor.shape
    groups = lax.axis_size("dp")
    total = rows_here * groups
    mine = lax.axis_index("dp") * rows_here
    column = lax.all_gather(z_anchor, "dp", axis=0, tiled=True).astype(jnp.float32)
    mean = jnp.sum(column, axis=0) / total
    centered_all = column - mean
    variance = jnp.sum(centered_all * centered_all, axis=0) / (total - 1)
    rounded_all = centered_all.astype(jnp.bfloat16)
    widened = rounded_all.astype(jnp.float32)
    own_square = jnp.sum(widened * widened, axis=0)
    rounded = lax.dynamic_slice_in_dim(rounded_all, mine, rows_here, 0)
    inner = lax.psum(gram(rounded, rounded_all).astype(jnp.bfloat16), "feat")
    product = jnp.dot(inner, rounded_all, preferred_element_type=jnp.float32)
    product = product - rounded.astype(jnp.float32) * own_square
    return finish(z_anchor, z_other, mean, variance, total, product)


def finish(z_anchor, z_other, mean, variance, total, product):
    coef = 2.0 * total / (25.0 * (total - 1)) / (total - 1)
    anchor = z_anchor.astype(jnp.float32)
    centered = anchor - mean
    deviation = jnp.sqrt(variance + 0.0001)
    hinge = jnp.where(deviation < 1.0, centered / deviation, 0.0)
    factor = total / (4.0 * (total - 1))
    return anchor - z_other.astype(jnp.float32) - factor * hinge + coef * product


def over_dp(x):
    for step in (1, 3):
        x = x + lax.ppermute(x, "dp", [(i, i ^ step) for i in range(4)])
    return x


def over_feat(x):
    for step in (1, 2, 4):
        x = x + lax.ppermute(x, "feat", [(i, i ^ step) for i in range(8)])
    return x


def to_partner(x, step):
    return lax.ppermute(x, "feat", [(i, i ^ step) for i in range(8)])


def scatter_sum(x):
    here = lax.axis_index("feat")
    core, chip = here % 2, here // 2
    half = x.shape[0] // 2
    halves = x.reshape(2, half, x.shape[1])
    sent = lax.dynamic_index_in_dim(halves, 1 - core, 0, False).astype(jnp.bfloat16)
    kept = lax.dynamic_index_in_dim(halves, core, 0, False)
    kept = kept + to_partner(sent, 1).astype(jnp.float32)
    pieces = kept.reshape(4, half // 4, x.shape[1])
    result = lax.dynamic_index_in_dim(pieces, chip, 0, False)
    for step in (1, 2, 3):
        out = lax.dynamic_index_in_dim(pieces, chip ^ step, 0, False).astype(jnp.bfloat16)
        result = result + to_partner(out, 2 * step).astype(jnp.float32)
    return result.astype(jnp.bfloat16)


def gather_rows(x):
    here = lax.axis_index("feat")
    core, chip = here % 2, here // 2
    near = jnp.stack([x] + [to_partner(x, 2 * step) for step in (1, 2, 3)])
    near = jnp.where(chip % 2 == 1, near[jnp.array([1, 0, 3, 2])], near)
    near = jnp.where(chip // 2 == 1, near[jnp.array([2, 3, 0, 1])], near)
    near = near.reshape(4 * x.shape[0], x.shape[1])
    far = to_partner(near, 1)
    return jnp.where(
        core == 0, jnp.concatenate([near, far]), jnp.concatenate([far, near])
    )


def by_line(z_anchor, z_other):
    rows, width = z_anchor.shape
    total = rows * 4
    plane = lax.axis_index("dp")
    middle = (plane == 1) | (plane == 2)
    inward, across, outward = [(0, 1), (3, 2)], [(1, 2), (2, 1)], [(1, 0), (2, 3)]

    near, far = [], []
    for piece in jnp.split(z_anchor, FLOOD, axis=0):
        near.append(lax.ppermute(piece, "dp", inward))
        crossed = lax.ppermute(near[-1], "dp", across)
        at_end = lax.ppermute(crossed, "dp", outward)
        far.append(jnp.where(middle, crossed, at_end))
    swapped = [
        lax.ppermute(piece, "dp", across) for piece in jnp.split(z_anchor, SWAP, axis=1)
    ]

    anchor = z_anchor.astype(jnp.float32)
    mean = over_dp(jnp.sum(anchor, axis=0)) / total
    def center(block, shift):
        return (block.astype(jnp.float32) - shift).astype(jnp.bfloat16)

    centered = anchor - mean
    own = centered.astype(jnp.bfloat16)
    widened = own.astype(jnp.float32)
    squares = over_dp(
        jnp.stack([jnp.sum(centered * centered, axis=0), jnp.sum(widened * widened, axis=0)])
    )
    variance, own_square = squares[0] / (total - 1), squares[1]
    norms = over_feat(jnp.sum(widened * widened, axis=1))

    diagonal = jnp.arange(rows)[:, None] == jnp.arange(rows)[None, :]
    near = jnp.concatenate([center(x, mean) for x in near])
    far = jnp.concatenate([center(x, mean) for x in far])

    with_near = scatter_sum(gram(own, near))
    with_far = scatter_sum(gram(own, far))
    other_far = lax.ppermute(with_far, "dp", across)
    first = gather_rows(jnp.concatenate([with_near, other_far], axis=1))
    with_near, other_far = first[:, :rows], first[:, rows:]

    own_pieces = jnp.split(own, SWAP, axis=1)
    means = jnp.split(mean, SWAP)
    swapped = [center(x, m) for x, m in zip(swapped, means)]
    from_middle = [
        lax.ppermute(
            (dot_t(with_near, a) + dot_t(other_far, b)).astype(jnp.bfloat16), "dp", outward
        )
        for a, b in zip(own_pieces, swapped)
    ]
    swapped = jnp.concatenate(swapped, axis=1)

    with_own = gather_rows(scatter_sum(jnp.where(diagonal, 0.0, gram(own, own))))
    with_far = gather_rows(with_far)
    with_swapped = gather_rows(scatter_sum(gram(own, swapped)))
    zero = jnp.zeros((), jnp.bfloat16)
    with_near = jnp.where(middle, with_near, zero)
    with_swapped = jnp.where(middle, with_swapped, zero)

    def dot(a, b):
        return jnp.dot(a, b, preferred_element_type=jnp.float32)

    product = dot(with_own, own) + dot(with_far, far) + dot(with_near, near)
    product = product + dot(with_swapped, swapped)
    product = product + jnp.concatenate(from_middle, axis=1).astype(jnp.float32)
    product = product + widened * (norms[:, None] - own_square[None, :])
    return finish(z_anchor, z_other, mean, variance, total, product)


def solution(mesh):
    placed = (P("dp", "feat"), P("dp", "feat"))
    in_line = mesh.shape["dp"] == 4 and mesh.shape["feat"] == 8
    return jax.shard_map(
        by_line if in_line else by_gather,
        mesh=mesh, in_specs=placed, out_specs=P("dp", "feat"), check_vma=False,
    )
```

time: 177 us -> 187 us (1.056)
  the two profiles are of different devices: /device:TPU:9 before, /device:TPU:0 now
where the time goes in v2:
time: 187 us; the launch traced here: 186 us
  starting transfers between devices  83.4 us (45%)
  waiting for transfers between devices  66.8 us (36%)
  matrix products  13.4 us (7%)
  local copies, waits for them, and re-layouts  11.1 us (6%)
  other arithmetic  10.1 us (5%)
    ppermute x32, starting transfers between devices, to_partner(): return lax.ppermute(x, 'feat', [(i, i ^ step) for i in range(8)])  29 us
    ppermute x4, waiting for transfers between devices, by_line(): at_end = lax.ppermute(crossed, 'dp', outward)  24.2 us
    ppermute x4, starting transfers between devices, over_dp(): x = x + lax.ppermute(x, 'dp', [(i, i ^ step) for i in range(4)])  22.2 us
    ppermute x4, waiting for transfers between devices, by_line(): lax.ppermute((dot_t(with_near, a) + dot_t(other_far, b)).astype(jnp.bfloa...  21.4 us
    ppermute x32, waiting for transfers between devices, to_partner(): return lax.ppermute(x, 'feat', [(i, i ^ step) for i in range(8)])  13.3 us
    ppermute x4, starting transfers between devices, by_line(): near.append(lax.ppermute(piece, 'dp', inward))  9.71 us
    dot_general x4, matrix products, dot(): return jnp.dot(a, b, preferred_element_type=jnp.float32)  7.59 us
    ppermute x4, starting transfers between devices, by_line(): crossed = lax.ppermute(near[-1], 'dp', across)  5.46 us
  transfers between devices with their start and end apart: 60, of which 25 were waited for; matrix products, arithmetic and copies ran while one was open for 15% of the time, Pallas kernels for 0%

profile of v2, /device:TPU:0, one launch (start us, length us, event | category | flops | bytes accessed | tf_op | source)
XLA Modules:
  0.0 186.0 jit_solution(1378353448647004585)
XLA Ops:
  1.5 3.1 %collective-permute-start = (f32[1024]{0:T(1024)S(1)}, f32[1024]{0:T(1024)S(1)}, u32[]{:S(2)}, u32[]{:S(2)}) collective-permute-start(f32[1024]{0:T(1024)S(1)} %convert_reduce_fusion), channel_id=1, source_target_pairs={{0,8},{8,0},{16,24},{24,16},{1,9},{9,1},{17,25},{25,17},{2,10},{10... | collective-permute-start | bytes 12296 | tf_op jit(solution)/shard_map/ppermute | solution.py:53
  4.6 2.1 %fusion.114 = (bf16[512,256]{1,0:T(8,128)(2,1)S(1)}, bf16[512,256]{1,0:T(8,128)(2,1)S(1)}, bf16[512,256]{1,0:T(8,128)(2,1)}, bf16[512,256]{1,0:T(8,128)(2,1)}) fusion(bf16[512,1024]{1,0:T(8,128)(2,1)} %param.10), kind=kLoop, calls=%fused_computation.186 | loop fusion | bytes 2097152 | tf_op jit(solution)/shard_map/split | solution.py:110
  9.8 2.5 %collective-permute-start.1 = (f32[1024]{0:T(1024)S(1)}, f32[1024]{0:T(1024)S(1)}, u32[]{:S(2)}, u32[]{:S(2)}) collective-permute-start(f32[1024]{0:T(1024)S(1)} %add.189), channel_id=1, source_target_pairs={{0,24},{8,16},{16,8},{24,0},{1,25},{9,17},{17,9},{25,1},{2,26},{10... | collective-permute-start | bytes 12296 | tf_op jit(solution)/shard_map/ppermute | solution.py:53
  12.4 2.9 %collective-permute-done.1 = f32[1024]{0:T(1024)S(1)} collective-permute-done((f32[1024]{0:T(1024)S(1)}, f32[1024]{0:T(1024)S(1)}, u32[]{:S(2)}, u32[]{:S(2)}) %collective-permute-start.1) | collective-permute-done | bytes 4128 | tf_op jit(solution)/shard_map/ppermute | solution.py:53
  17.5 13.9 %collective-permute-start.2 = (f32[2,1024]{1,0:T(2,128)S(1)}, f32[2,1024]{1,0:T(2,128)S(1)}, u32[]{:S(2)}, u32[]{:S(2)}) collective-permute-start(f32[2,1024]{1,0:T(2,128)S(1)} %pad_maximum_fusion.14), channel_id=1, source_target_pairs={{0,8},{8,0},{16,24},{24,16},{1,9},{9,1},{17,25},{25,17},{2,10},{10... | collective-permute-start | bytes 24584 | tf_op jit(solution)/shard_map/ppermute | solution.py:53
  32.9 2.1 %collective-permute-done.58 = f32[512]{0:T(512)S(1)} collective-permute-done((f32[512]{0:T(512)S(1)}, f32[512]{0:T(512)S(1)}, u32[]{:S(2)}, u32[]{:S(2)}) %collective-permute-start.58) | collective-permute-done | bytes 2080 | tf_op jit(solution)/shard_map/ppermute | solution.py:59
  36.5 2.7 %collective-permute-start.3 = (f32[2,1024]{1,0:T(2,128)S(1)}, f32[2,1024]{1,0:T(2,128)S(1)}, u32[]{:S(2)}, u32[]{:S(2)}) collective-permute-start(f32[2,1024]{1,0:T(2,128)S(1)} %fusion.106), channel_id=1, source_target_pairs={{0,24},{8,16},{16,8},{24,0},{1,25},{9,17},{17,9},{25,1},{2,26},{10... | collective-permute-start | bytes 24584 | tf_op jit(solution)/shard_map/ppermute | solution.py:53
  42.0 3.7 %collective-permute-start.12 = (bf16[128,1024]{1,0:T(8,128)(2,1)}, bf16[128,1024]{1,0:T(8,128)(2,1)S(1)}, u32[]{:S(2)}, u32[]{:S(2)}) collective-permute-start(bf16[128,1024]{1,0:T(8,128)(2,1)} %get-tuple-element.15), channel_id=1, source_target_pairs={{0,8},{24,16},{1,9},{25,17},{2,10},{26,18},{3,11},{27,19},{4,12},{... | collective-permute-start | bytes 786440 | tf_op jit(solution)/shard_map/ppermute | solution.py:105
  45.8 2.0 %collective-permute-start.21 = (bf16[128,1024]{1,0:T(8,128)(2,1)}, bf16[128,1024]{1,0:T(8,128)(2,1)}, u32[]{:S(2)}, u32[]{:S(2)}) collective-permute-start(bf16[128,1024]{1,0:T(8,128)(2,1)} %get-tuple-element.16), channel_id=1, source_target_pairs={{0,8},{24,16},{1,9},{25,17},{2,10},{26,18},{3,11},{27,19},{4,12},{... | collective-permute-start | bytes 786440 | tf_op jit(solution)/shard_map/ppermute | solution.py:105
  49.6 1.6 collective-permute-start.5
  53.9 2.5 %collective-permute-done.7 = bf16[64,512]{1,0:T(8,128)(2,1)S(1)} collective-permute-done((bf16[64,512]{1,0:T(8,128)(2,1)S(1)}, bf16[64,512]{1,0:T(8,128)(2,1)S(1)}, u32[]{:S(2)}, u32[]{:S(2)}) %collective-permute-start.7) | collective-permute-done | bytes 65568 | tf_op jit(solution)/shard_map/ppermute | solution.py:64
  62.2 2.0 %collective-permute-start.18 = (bf16[128,1024]{1,0:T(8,128)(2,1)}, bf16[128,1024]{1,0:T(8,128)(2,1)}, u32[]{:S(2)}, u32[]{:S(2)}) collective-permute-start(bf16[128,1024]{1,0:T(8,128)(2,1)} %get-tuple-element.17), channel_id=1, source_target_pairs={{0,8},{24,16},{1,9},{25,17},{2,10},{26,18},{3,11},{27,19},{4,12},{... | collective-permute-start | bytes 786440 | tf_op jit(solution)/shard_map/ppermute | solution.py:105
  64.2 2.0 %collective-permute-start.15 = (bf16[128,1024]{1,0:T(8,128)(2,1)}, bf16[128,1024]{1,0:T(8,128)(2,1)}, u32[]{:S(2)}, u32[]{:S(2)}) collective-permute-start(bf16[128,1024]{1,0:T(8,128)(2,1)} %get-tuple-element.18), channel_id=1, source_target_pairs={{0,8},{24,16},{1,9},{25,17},{2,10},{26,18},{3,11},{27,19},{4,12},{... | collective-permute-start | bytes 786440 | tf_op jit(solution)/shard_map/ppermute | solution.py:105
  78.7 1.7 collective-permute-start.51
  90.2 10.3 %collective-permute-done.14 = bf16[128,1024]{1,0:T(8,128)(2,1)S(1)} collective-permute-done((bf16[128,1024]{1,0:T(8,128)(2,1)}, bf16[128,1024]{1,0:T(8,128)(2,1)S(1)}, u32[]{:S(2)}, u32[]{:S(2)}) %collective-permute-start.14) | collective-permute-done | bytes 262176 | tf_op jit(solution)/shard_map/ppermute | solution.py:107
  100.5 5.6 %collective-permute-done.23 = bf16[128,1024]{1,0:T(8,128)(2,1)S(1)} collective-permute-done((bf16[128,1024]{1,0:T(8,128)(2,1)}, bf16[128,1024]{1,0:T(8,128)(2,1)S(1)}, u32[]{:S(2)}, u32[]{:S(2)}) %collective-permute-start.23) | collective-permute-done | bytes 262176 | tf_op jit(solution)/shard_map/ppermute | solution.py:107
  106.1 5.4 %collective-permute-done.20 = bf16[128,1024]{1,0:T(8,128)(2,1)S(1)} collective-permute-done((bf16[128,1024]{1,0:T(8,128)(2,1)}, bf16[128,1024]{1,0:T(8,128)(2,1)S(1)}, u32[]{:S(2)}, u32[]{:S(2)}) %collective-permute-start.20) | collective-permute-done | bytes 262176 | tf_op jit(solution)/shard_map/ppermute | solution.py:107
  111.5 2.9 %collective-permute-done.17 = bf16[128,1024]{1,0:T(8,128)(2,1)} collective-permute-done((bf16[128,1024]{1,0:T(8,128)(2,1)}, bf16[128,1024]{1,0:T(8,128)(2,1)}, u32[]{:S(2)}, u32[]{:S(2)}) %collective-permute-start.17) | collective-permute-done | bytes 262176 | tf_op jit(solution)/shard_map/ppermute | solution.py:107
  114.4 1.9 %subtract_convert_fusion.7 = (bf16[128,1024]{1,0:T(8,128)(2,1)S(1)}, bf16[128,1024]{1,0:T(8,128)(2,1)S(1)}, bf16[128,1024]{1,0:T(8,128)(2,1)S(1)}, bf16[128,1024...) fusion(bf16[128,1024]{1,0:T(8,128)(2,1)S(1)} %collective-permut, ...), kind=kLoop, calls=%fused_computation.77 | loop fusion | flops 3670016 | bytes 5246977 | tf_op jit(solution)/shard_map/convert_element_type | solution.py:116
  120.7 1.7 collective-permute-start.27
  123.5 1.6 collective-permute-start.33
  126.2 1.6 collective-permute-start.35
  129.2 2.1 %collective-permute-done.35 = bf16[64,512]{1,0:T(8,128)(2,1)S(1)} collective-permute-done((bf16[64,512]{1,0:T(8,128)(2,1)S(1)}, bf16[64,512]{1,0:T(8,128)(2,1)S(1)}, u32[]{:S(2)}, u32[]{:S(2)}) %collective-permute-start.35) | collective-permute-done | bytes 65568 | tf_op jit(solution)/shard_map/ppermute | solution.py:64
  131.3 1.7 collective-permute-start.30
  138.9 1.6 collective-permute-start.39
  142.9 2.1 %collective-permute-done.39 = bf16[64,1024]{1,0:T(8,128)(2,1)S(1)} collective-permute-done((bf16[64,1024]{1,0:T(8,128)(2,1)S(1)}, bf16[64,1024]{1,0:T(8,128)(2,1)S(1)}, u32[]{:S(2)}, u32[]{:S(2)}) %collective-permute-start.39) | collective-permute-done | bytes 131104 | tf_op jit(solution)/shard_map/ppermute | solution.py:64
  147.4 2.0 %fusion.16 = f32[512,1024]{1,0:T(8,128)S(1)} fusion(bf16[256,512]{1,0:T(8,128)(2,1)} %collective-permute-done.11, bf16[256,512]{1,0:T(8,128)(2,1)} %bitcast.15, pred[]{:T(512)S(6)} %eq.50, bf16[512,1024]{1,0:T(8,128)(2,1)S(1)} %copy-done, f32[1024]{0:T(1024)S(1)} %add_multiply_fusion), kind=kOutput, calls=%fused_computation.40 | convolution fusion | flops 540803072 | bytes 3674113 | tf_op jit(solution)/shard_map/dot_general | solution.py:156
  160.4 5.0 %collective-permute-done.55 = bf16[512,256]{1,0:T(8,128)(2,1)S(1)} collective-permute-done((bf16[512,256]{1,0:T(8,128)(2,1)S(1)}, bf16[512,256]{1,0:T(8,128)(2,1)S(1)}, u32[]{:S(2)}, u32[]{:S(2)}) %collective-permute-start.55) | collective-permute-done | bytes 262176 | tf_op jit(solution)/shard_map/ppermute | solution.py:141
  165.4 5.6 %collective-permute-done.56 = bf16[512,256]{1,0:T(8,128)(2,1)S(1)} collective-permute-done((bf16[512,256]{1,0:T(8,128)(2,1)S(1)}, bf16[512,256]{1,0:T(8,128)(2,1)S(1)}, u32[]{:S(2)}, u32[]{:S(2)}) %collective-permute-start.56) | collective-permute-done | bytes 262176 | tf_op jit(solution)/shard_map/ppermute | solution.py:141
  171.0 5.6 %collective-permute-done.53 = bf16[512,256]{1,0:T(8,128)(2,1)S(1)} collective-permute-done((bf16[512,256]{1,0:T(8,128)(2,1)S(1)}, bf16[512,256]{1,0:T(8,128)(2,1)S(1)}, u32[]{:S(2)}, u32[]{:S(2)}) %collective-permute-start.53) | collective-permute-done | bytes 262176 | tf_op jit(solution)/shard_map/ppermute | solution.py:141
  176.7 5.2 %collective-permute-done.54 = bf16[512,256]{1,0:T(8,128)(2,1)S(1)} collective-permute-done((bf16[512,256]{1,0:T(8,128)(2,1)S(1)}, bf16[512,256]{1,0:T(8,128)(2,1)S(1)}, u32[]{:S(2)}, u32[]{:S(2)}) %collective-permute-start.54) | collective-permute-done | bytes 262176 | tf_op jit(solution)/shard_map/ppermute | solution.py:141
  181.8 4.1 %fusion.7 = f32[512,1024]{1,0:T(8,128)} fusion(bf16[512,1024]{1,0:T(8,128)(2,1)S(1)} %copy-done, f32[512,1024]{1,0:T(8,128)S(1)} %fusion.38, f32[512,1024]{1,0:T(8,128)S(1)} %fusion.16, f32[512,1024]{1,0:T(8,128)S(1)} %fusion.22, bf16[512,1024]{1,0:T(8,128)(2,1)S(1)} %copy-done.36, bf16[512,256]{1,0:T(8,128)(2,1)S(1)} %collective-permute-done.56, ...), kind=kOutput, calls=%fused_computation.20 | convolution fusion | flops 557842432 | bytes 13122562 | tf_op jit(solution)/shard_map/dot_general | solution.py:156
  (238 shorter events, 74.0 us)
Async XLA Ops:
  1.5 8.2 %collective-permute-start = (f32[1024]{0:T(1024)S(1)}, f32[1024]{0:T(1024)S(1)}, u32[]{:S(2)}, u32[]{:S(2)}) collective-permute-start(f32[1024]{0:T(1024)S(1)} %convert_reduce_fusion), channel_id=1, source_target_pairs={{0,8},{8,0},{16,24},{24,16},{1,9},{9,1},{17,25},{25,17},{2,10},{10... | collective-permute-start | bytes 12296 | tf_op jit(solution)/shard_map/ppermute | solution.py:53
  6.7 39.1 %collective-permute-start.41 = (bf16[512,256]{1,0:T(8,128)(2,1)S(1)}, bf16[512,256]{1,0:T(8,128)(2,1)S(1)}, u32[]{:S(2)}, u32[]{:S(2)}) collective-permute-start(bf16[512,256]{1,0:T(8,128)(2,1)S(1)} %get-tuple-element.11), channel_id=1, source_target_pairs={{8,16},{16,8},{9,17},{17,9},{10,18},{18,10},{11,19},{19,11},{12,20... | collective-permute-start | bytes 786440 | tf_op jit(solution)/shard_map/ppermute | solution.py:110
  7.3 40.5 %collective-permute-start.42 = (bf16[512,256]{1,0:T(8,128)(2,1)S(1)}, bf16[512,256]{1,0:T(8,128)(2,1)S(1)}, u32[]{:S(2)}, u32[]{:S(2)}) collective-permute-start(bf16[512,256]{1,0:T(8,128)(2,1)S(1)} %get-tuple-element.12), channel_id=1, source_target_pairs={{8,16},{16,8},{9,17},{17,9},{10,18},{18,10},{11,19},{19,11},{12,20... | collective-permute-start | bytes 786440 | tf_op jit(solution)/shard_map/ppermute | solution.py:110
  8.0 40.0 %collective-permute-start.44 = (bf16[512,256]{1,0:T(8,128)(2,1)}, bf16[512,256]{1,0:T(8,128)(2,1)S(1)}, u32[]{:S(2)}, u32[]{:S(2)}) collective-permute-start(bf16[512,256]{1,0:T(8,128)(2,1)} %get-tuple-element.13), channel_id=1, source_target_pairs={{8,16},{16,8},{9,17},{17,9},{10,18},{18,10},{11,19},{19,11},{12,20... | collective-permute-start | bytes 786440 | tf_op jit(solution)/shard_map/ppermute | solution.py:110
  17.5 13.9 %collective-permute-start.57 = (f32[512]{0:T(512)S(1)}, f32[512]{0:T(512)S(1)}, u32[]{:S(2)}, u32[]{:S(2)}) collective-permute-start(f32[512]{0:T(512)S(1)} %get-tuple-element.5), channel_id=1, source_target_pairs={{0,1},{1,0},{2,3},{3,2},{4,5},{5,4},{6,7},{7,6},{8,9},{9,8},{10,11... | collective-permute-start | bytes 6152 | tf_op jit(solution)/shard_map/ppermute | solution.py:59
  17.5 19.0 %collective-permute-start.2 = (f32[2,1024]{1,0:T(2,128)S(1)}, f32[2,1024]{1,0:T(2,128)S(1)}, u32[]{:S(2)}, u32[]{:S(2)}) collective-permute-start(f32[2,1024]{1,0:T(2,128)S(1)} %pad_maximum_fusion.14), channel_id=1, source_target_pairs={{0,8},{8,0},{16,24},{24,16},{1,9},{9,1},{17,25},{25,17},{2,10},{10... | collective-permute-start | bytes 24584 | tf_op jit(solution)/shard_map/ppermute | solution.py:53
  39.2 8.8 %collective-permute-start.43 = (bf16[512,256]{1,0:T(8,128)(2,1)}, bf16[512,256]{1,0:T(8,128)(2,1)S(1)}, u32[]{:S(2)}, u32[]{:S(2)}) collective-permute-start(bf16[512,256]{1,0:T(8,128)(2,1)} %get-tuple-element.14), channel_id=1, source_target_pairs={{8,16},{16,8},{9,17},{17,9},{10,18},{18,10},{11,19},{19,11},{12,20... | collective-permute-start | bytes 786440 | tf_op jit(solution)/shard_map/ppermute | solution.py:110
  42.0 18.2 %collective-permute-start.12 = (bf16[128,1024]{1,0:T(8,128)(2,1)}, bf16[128,1024]{1,0:T(8,128)(2,1)S(1)}, u32[]{:S(2)}, u32[]{:S(2)}) collective-permute-start(bf16[128,1024]{1,0:T(8,128)(2,1)} %get-tuple-element.15), channel_id=1, source_target_pairs={{0,8},{24,16},{1,9},{25,17},{2,10},{26,18},{3,11},{27,19},{4,12},{... | collective-permute-start | bytes 786440 | tf_op jit(solution)/shard_map/ppermute | solution.py:105
  45.8 16.4 %collective-permute-start.21 = (bf16[128,1024]{1,0:T(8,128)(2,1)}, bf16[128,1024]{1,0:T(8,128)(2,1)}, u32[]{:S(2)}, u32[]{:S(2)}) collective-permute-start(bf16[128,1024]{1,0:T(8,128)(2,1)} %get-tuple-element.16), channel_id=1, source_target_pairs={{0,8},{24,16},{1,9},{25,17},{2,10},{26,18},{3,11},{27,19},{4,12},{... | collective-permute-start | bytes 786440 | tf_op jit(solution)/shard_map/ppermute | solution.py:105
  53.9 15.6 %collective-permute-start.45 = (bf16[256,512]{1,0:T(8,128)(2,1)S(1)}, bf16[256,512]{1,0:T(8,128)(2,1)}, u32[]{:S(2)}, u32[]{:S(2)}) collective-permute-start(bf16[256,512]{1,0:T(8,128)(2,1)S(1)} %fusion.61), channel_id=1, source_target_pairs={{0,1},{1,0},{2,3},{3,2},{4,5},{5,4},{6,7},{7,6},{8,9},{9,8},{10,11... | collective-permute-start | bytes 786440 | tf_op jit(solution)/shard_map/ppermute | solution.py:64
  57.5 6.7 %collective-permute-start.10 = (bf16[64,512]{1,0:T(8,128)(2,1)S(1)}, bf16[64,512]{1,0:T(8,128)(2,1)S(1)}, u32[]{:S(2)}, u32[]{:S(2)}) collective-permute-start(bf16[64,512]{1,0:T(8,128)(2,1)S(1)} %fusion.82), channel_id=1, source_target_pairs={{0,6},{1,7},{2,4},{3,5},{4,2},{5,3},{6,0},{7,1},{8,14},{9,15},{10,... | collective-permute-start | bytes 196616 | tf_op jit(solution)/shard_map/ppermute | solution.py:64
  59.0 7.2 %collective-permute-start.9 = (bf16[64,512]{1,0:T(8,128)(2,1)S(1)}, bf16[64,512]{1,0:T(8,128)(2,1)S(1)}, u32[]{:S(2)}, u32[]{:S(2)}) collective-permute-start(bf16[64,512]{1,0:T(8,128)(2,1)S(1)} %fusion.82), channel_id=1, source_target_pairs={{0,4},{1,5},{2,6},{3,7},{4,0},{5,1},{6,2},{7,3},{8,12},{9,13},{10,... | collective-permute-start | bytes 196616 | tf_op jit(solution)/shard_map/ppermute | solution.py:64
  60.2 7.3 %collective-permute-start.8 = (bf16[64,512]{1,0:T(8,128)(2,1)S(1)}, bf16[64,512]{1,0:T(8,128)(2,1)S(1)}, u32[]{:S(2)}, u32[]{:S(2)}) collective-permute-start(bf16[64,512]{1,0:T(8,128)(2,1)S(1)} %fusion.82), channel_id=1, source_target_pairs={{0,2},{1,3},{2,0},{3,1},{4,6},{5,7},{6,4},{7,5},{8,10},{9,11},{10,... | collective-permute-start | bytes 196616 | tf_op jit(solution)/shard_map/ppermute | solution.py:64
  62.2 9.7 %collective-permute-start.18 = (bf16[128,1024]{1,0:T(8,128)(2,1)}, bf16[128,1024]{1,0:T(8,128)(2,1)}, u32[]{:S(2)}, u32[]{:S(2)}) collective-permute-start(bf16[128,1024]{1,0:T(8,128)(2,1)} %get-tuple-element.17), channel_id=1, source_target_pairs={{0,8},{24,16},{1,9},{25,17},{2,10},{26,18},{3,11},{27,19},{4,12},{... | collective-permute-start | bytes 786440 | tf_op jit(solution)/shard_map/ppermute | solution.py:105
  64.2 10.2 %collective-permute-start.15 = (bf16[128,1024]{1,0:T(8,128)(2,1)}, bf16[128,1024]{1,0:T(8,128)(2,1)}, u32[]{:S(2)}, u32[]{:S(2)}) collective-permute-start(bf16[128,1024]{1,0:T(8,128)(2,1)} %get-tuple-element.18), channel_id=1, source_target_pairs={{0,8},{24,16},{1,9},{25,17},{2,10},{26,18},{3,11},{27,19},{4,12},{... | collective-permute-start | bytes 786440 | tf_op jit(solution)/shard_map/ppermute | solution.py:105
  66.2 14.1 %collective-permute-start.13 = (bf16[128,1024]{1,0:T(8,128)(2,1)S(1)}, bf16[128,1024]{1,0:T(8,128)(2,1)}, u32[]{:S(2)}, u32[]{:S(2)}) collective-permute-start(bf16[128,1024]{1,0:T(8,128)(2,1)S(1)} %collective-permute-done.12), channel_id=1, source_target_pairs={{8,16},{16,8},{9,17},{17,9},{10,18},{18,10},{11,19},{19,11},{12,20... | collective-permute-start | bytes 786440 | tf_op jit(solution)/shard_map/ppermute | solution.py:106
  67.5 13.7 %collective-permute-start.22 = (bf16[128,1024]{1,0:T(8,128)(2,1)}, bf16[128,1024]{1,0:T(8,128)(2,1)}, u32[]{:S(2)}, u32[]{:S(2)}) collective-permute-start(bf16[128,1024]{1,0:T(8,128)(2,1)} %collective-permute-done.21), channel_id=1, source_target_pairs={{8,16},{16,8},{9,17},{17,9},{10,18},{18,10},{11,19},{19,11},{12,20... | collective-permute-start | bytes 786440 | tf_op jit(solution)/shard_map/ppermute | solution.py:106
  75.3 7.7 %collective-permute-start.19 = (bf16[128,1024]{1,0:T(8,128)(2,1)}, bf16[128,1024]{1,0:T(8,128)(2,1)}, u32[]{:S(2)}, u32[]{:S(2)}) collective-permute-start(bf16[128,1024]{1,0:T(8,128)(2,1)} %collective-permute-done.18), channel_id=1, source_target_pairs={{8,16},{16,8},{9,17},{17,9},{10,18},{18,10},{11,19},{19,11},{12,20... | collective-permute-start | bytes 786440 | tf_op jit(solution)/shard_map/ppermute | solution.py:106
  77.0 6.0 %collective-permute-start.16 = (bf16[128,1024]{1,0:T(8,128)(2,1)}, bf16[128,1024]{1,0:T(8,128)(2,1)}, u32[]{:S(2)}, u32[]{:S(2)}) collective-permute-start(bf16[128,1024]{1,0:T(8,128)(2,1)} %collective-permute-done.15), channel_id=1, source_target_pairs={{8,16},{16,8},{9,17},{17,9},{10,18},{18,10},{11,19},{19,11},{12,20... | collective-permute-start | bytes 786440 | tf_op jit(solution)/shard_map/ppermute | solution.py:106
  81.2 5.7 %collective-permute-start.49 = (bf16[64,512]{1,0:T(8,128)(2,1)S(1)}, bf16[64,512]{1,0:T(8,128)(2,1)S(1)}, u32[]{:S(2)}, u32[]{:S(2)}) collective-permute-start(bf16[64,512]{1,0:T(8,128)(2,1)S(1)} %fusion.73), channel_id=1, source_target_pairs={{0,2},{1,3},{2,0},{3,1},{4,6},{5,7},{6,4},{7,5},{8,10},{9,11},{10,... | collective-permute-start | bytes 196616 | tf_op jit(solution)/shard_map/ppermute | solution.py:64
  83.0 64.4 %collective-permute-start.11 = (bf16[256,512]{1,0:T(8,128)(2,1)}, bf16[256,512]{1,0:T(8,128)(2,1)}, u32[]{:S(2)}, u32[]{:S(2)}) collective-permute-start(bf16[256,512]{1,0:T(8,128)(2,1)} %bitcast.15), channel_id=1, source_target_pairs={{0,1},{1,0},{2,3},{3,2},{4,5},{5,4},{6,7},{7,6},{8,9},{9,8},{10,11... | collective-permute-start | bytes 786440 | tf_op jit(solution)/shard_map/ppermute | solution.py:64
  83.0 17.5 %collective-permute-start.14 = (bf16[128,1024]{1,0:T(8,128)(2,1)}, bf16[128,1024]{1,0:T(8,128)(2,1)S(1)}, u32[]{:S(2)}, u32[]{:S(2)}) collective-permute-start(bf16[128,1024]{1,0:T(8,128)(2,1)} %collective-permute-done.13), channel_id=1, source_target_pairs={{8,0},{16,24},{9,1},{17,25},{10,2},{18,26},{11,3},{19,27},{12,4},{... | collective-permute-start | bytes 786440 | tf_op jit(solution)/shard_map/ppermute | solution.py:107
  84.3 21.8 %collective-permute-start.23 = (bf16[128,1024]{1,0:T(8,128)(2,1)}, bf16[128,1024]{1,0:T(8,128)(2,1)S(1)}, u32[]{:S(2)}, u32[]{:S(2)}) collective-permute-start(bf16[128,1024]{1,0:T(8,128)(2,1)} %collective-permute-done.22), channel_id=1, source_target_pairs={{8,0},{16,24},{9,1},{17,25},{10,2},{18,26},{11,3},{19,27},{12,4},{... | collective-permute-start | bytes 786440 | tf_op jit(solution)/shard_map/ppermute | solution.py:107
  85.6 25.9 %collective-permute-start.20 = (bf16[128,1024]{1,0:T(8,128)(2,1)}, bf16[128,1024]{1,0:T(8,128)(2,1)S(1)}, u32[]{:S(2)}, u32[]{:S(2)}) collective-permute-start(bf16[128,1024]{1,0:T(8,128)(2,1)} %collective-permute-done.19), channel_id=1, source_target_pairs={{8,0},{16,24},{9,1},{17,25},{10,2},{18,26},{11,3},{19,27},{12,4},{... | collective-permute-start | bytes 786440 | tf_op jit(solution)/shard_map/ppermute | solution.py:107
  86.9 27.5 %collective-permute-start.17 = (bf16[128,1024]{1,0:T(8,128)(2,1)}, bf16[128,1024]{1,0:T(8,128)(2,1)}, u32[]{:S(2)}, u32[]{:S(2)}) collective-permute-start(bf16[128,1024]{1,0:T(8,128)(2,1)} %collective-permute-done.16), channel_id=1, source_target_pairs={{8,0},{16,24},{9,1},{17,25},{10,2},{18,26},{11,3},{19,27},{12,4},{... | collective-permute-start | bytes 786440 | tf_op jit(solution)/shard_map/ppermute | solution.py:107
  100.5 59.9 %collective-permute-start.52 = (bf16[256,512]{1,0:T(8,128)(2,1)}, bf16[256,512]{1,0:T(8,128)(2,1)}, u32[]{:S(2)}, u32[]{:S(2)}) collective-permute-start(bf16[256,512]{1,0:T(8,128)(2,1)} %bitcast.54), channel_id=1, source_target_pairs={{0,1},{1,0},{2,3},{3,2},{4,5},{5,4},{6,7},{7,6},{8,9},{9,8},{10,11... | collective-permute-start | bytes 786440 | tf_op jit(solution)/shard_map/ppermute | solution.py:64
  136.5 6.4 %collective-permute-start.38 = (bf16[64,1024]{1,0:T(8,128)(2,1)S(1)}, bf16[64,1024]{1,0:T(8,128)(2,1)S(1)}, u32[]{:S(2)}, u32[]{:S(2)}) collective-permute-start(bf16[64,1024]{1,0:T(8,128)(2,1)S(1)} %get-tuple-element.32), channel_id=1, source_target_pairs={{0,4},{1,5},{2,6},{3,7},{4,0},{5,1},{6,2},{7,3},{8,12},{9,13},{10,... | collective-permute-start | bytes 393224 | tf_op jit(solution)/shard_map/ppermute | solution.py:64
  138.9 6.0 %collective-permute-start.39 = (bf16[64,1024]{1,0:T(8,128)(2,1)S(1)}, bf16[64,1024]{1,0:T(8,128)(2,1)S(1)}, u32[]{:S(2)}, u32[]{:S(2)}) collective-permute-start(bf16[64,1024]{1,0:T(8,128)(2,1)S(1)} %get-tuple-element.32), channel_id=1, source_target_pairs={{0,6},{1,7},{2,4},{3,5},{4,2},{5,3},{6,0},{7,1},{8,14},{9,15},{10,... | collective-permute-start | bytes 393224 | tf_op jit(solution)/shard_map/ppermute | solution.py:64
  154.3 11.1 %collective-permute-start.55 = (bf16[512,256]{1,0:T(8,128)(2,1)S(1)}, bf16[512,256]{1,0:T(8,128)(2,1)S(1)}, u32[]{:S(2)}, u32[]{:S(2)}) collective-permute-start(bf16[512,256]{1,0:T(8,128)(2,1)S(1)} %fusion.14), channel_id=1, source_target_pairs={{8,0},{16,24},{9,1},{17,25},{10,2},{18,26},{11,3},{19,27},{12,4},{... | collective-permute-start | bytes 786440 | tf_op jit(solution)/shard_map/ppermute | solution.py:141
  155.7 15.3 %collective-permute-start.56 = (bf16[512,256]{1,0:T(8,128)(2,1)S(1)}, bf16[512,256]{1,0:T(8,128)(2,1)S(1)}, u32[]{:S(2)}, u32[]{:S(2)}) collective-permute-start(bf16[512,256]{1,0:T(8,128)(2,1)S(1)} %fusion.15), channel_id=1, source_target_pairs={{8,0},{16,24},{9,1},{17,25},{10,2},{18,26},{11,3},{19,27},{12,4},{... | collective-permute-start | bytes 786440 | tf_op jit(solution)/shard_map/ppermute | solution.py:141
  157.0 19.6 %collective-permute-start.53 = (bf16[512,256]{1,0:T(8,128)(2,1)S(1)}, bf16[512,256]{1,0:T(8,128)(2,1)S(1)}, u32[]{:S(2)}, u32[]{:S(2)}) collective-permute-start(bf16[512,256]{1,0:T(8,128)(2,1)S(1)} %fusion.12), channel_id=1, source_target_pairs={{8,0},{16,24},{9,1},{17,25},{10,2},{18,26},{11,3},{19,27},{12,4},{... | collective-permute-start | bytes 786440 | tf_op jit(solution)/shard_map/ppermute | solution.py:141
  158.3 23.5 %collective-permute-start.54 = (bf16[512,256]{1,0:T(8,128)(2,1)S(1)}, bf16[512,256]{1,0:T(8,128)(2,1)S(1)}, u32[]{:S(2)}, u32[]{:S(2)}) collective-permute-start(bf16[512,256]{1,0:T(8,128)(2,1)S(1)} %fusion.13), channel_id=1, source_target_pairs={{8,0},{16,24},{9,1},{17,25},{10,2},{18,26},{11,3},{19,27},{12,4},{... | collective-permute-start | bytes 786440 | tf_op jit(solution)/shard_map/ppermute | solution.py:141
  (65 other events, 334.0 us)

commit v3 on v2

--- a/solution.py
+++ b/solution.py
@@ -100,18 +100,17 @@
     middle = (plane == 1) | (plane == 2)
     inward, across, outward = [(0, 1), (3, 2)], [(1, 2), (2, 1)], [(1, 0), (2, 3)]
 
-    near, far = [], []
-    for piece in jnp.split(z_anchor, FLOOD, axis=0):
-        near.append(lax.ppermute(piece, "dp", inward))
-        crossed = lax.ppermute(near[-1], "dp", across)
-        at_end = lax.ppermute(crossed, "dp", outward)
-        far.append(jnp.where(middle, crossed, at_end))
-    swapped = [
-        lax.ppermute(piece, "dp", across) for piece in jnp.split(z_anchor, SWAP, axis=1)
-    ]
+    anchor = z_anchor.astype(jnp.float32)
+    sums = jnp.sum(anchor, axis=0)
+    pieces = jnp.split(z_anchor, FLOOD, axis=0)
+    near = [lax.ppermute(pieces[0], "dp", inward)]
+    others = [lax.ppermute(sums, "dp", [(i, (i + k) % 4) for i in range(4)]) for k in (1, 2, 3)]
+    swaps = jnp.split(z_anchor, SWAP, axis=1)
+    swapped = [lax.ppermute(after(swaps[0], sums), "dp", across)]
+    for piece in pieces[1:]:
+        near.append(lax.ppermute(after(piece, sums), "dp", inward))
+    mean = (sums + others[0] + others[1] + others[2]) / total
 
-    anchor = z_anchor.astype(jnp.float32)
-    mean = over_dp(jnp.sum(anchor, axis=0)) / total
     def center(block, shift):
         return (block.astype(jnp.float32) - shift).astype(jnp.bfloat16)
 
@@ -123,16 +122,26 @@
     )
     variance, own_square = squares[0] / (total - 1), squares[1]
     norms = over_feat(jnp.sum(widened * widened, axis=1))
+    diagonal = jnp.arange(rows)[:, None] == jnp.arange(rows)[None, :]
+    own_own = jnp.where(diagonal, 0.0, gram(own, own))
 
-    diagonal = jnp.arange(rows)[:, None] == jnp.arange(rows)[None, :]
+    crossed = [lax.ppermute(x, "dp", across) for x in near]
+    at_end = [lax.ppermute(x, "dp", outward) for x in crossed]
+    for piece in swaps[1:3]:
+        swapped.append(lax.ppermute(after(piece, near[-1]), "dp", across))
     near = jnp.concatenate([center(x, mean) for x in near])
-    far = jnp.concatenate([center(x, mean) for x in far])
+    crossed = jnp.concatenate([center(x, mean) for x in crossed])
 
-    with_near = scatter_sum(gram(own, near))
-    with_far = scatter_sum(gram(own, far))
-    other_far = lax.ppermute(with_far, "dp", across)
-    first = gather_rows(jnp.concatenate([with_near, other_far], axis=1))
-    with_near, other_far = first[:, :rows], first[:, rows:]
+    first = scatter_sum(
+        jnp.concatenate([jnp.where(middle, gram(own, near), own_own), gram(own, crossed)], axis=1)
+    )
+    other_far = lax.ppermute(first[:, rows:], "dp", across)
+    for piece in swaps[3:]:
+        swapped.append(lax.ppermute(after(piece, first), "dp", across))
+    first = gather_rows(jnp.concatenate([first, other_far], axis=1))
+    with_near, with_crossed, other_far = (
+        first[:, :rows], first[:, rows:2 * rows], first[:, 2 * rows:]
+    )
 
     own_pieces = jnp.split(own, SWAP, axis=1)
     means = jnp.split(mean, SWAP)
@@ -144,22 +153,28 @@
         for a, b in zip(own_pieces, swapped)
     ]
     swapped = jnp.concatenate(swapped, axis=1)
+    at_end = jnp.concatenate([center(x, mean) for x in at_end])
 
-    with_own = gather_rows(scatter_sum(jnp.where(diagonal, 0.0, gram(own, own))))
-    with_far = gather_rows(with_far)
-    with_swapped = gather_rows(scatter_sum(gram(own, swapped)))
-    zero = jnp.zeros((), jnp.bfloat16)
-    with_near = jnp.where(middle, with_near, zero)
-    with_swapped = jnp.where(middle, with_swapped, zero)
+    second = gather_rows(scatter_sum(jnp.concatenate(
+        [jnp.where(middle, own_own, gram(own, at_end)), gram(own, swapped)], axis=1
+    )))
 
     def dot(a, b):
         return jnp.dot(a, b, preferred_element_type=jnp.float32)
 
-    product = dot(with_own, own) + dot(with_far, far) + dot(with_near, near)
-    product = product + dot(with_swapped, swapped)
+    zero = jnp.zeros((), jnp.bfloat16)
+    one = jnp.where(middle, near, own)
+    two = jnp.where(middle, own, at_end)
+    product = dot(with_near, one) + dot(second[:, :rows], two)
+    product = product + dot(jnp.where(middle, with_crossed, zero), crossed)
+    product = product + dot(jnp.where(middle, second[:, rows:], zero), swapped)
     product = product + jnp.concatenate(from_middle, axis=1).astype(jnp.float32)
     product = product + widened * (norms[:, None] - own_square[None, :])
     return finish(z_anchor, z_other, mean, variance, total, product)
+
+
+def after(x, *others):
+    return lax.optimization_barrier((x, *others))[0]
 
 
 def solution(mesh):

time: 187 us -> 191 us (1.021)
  the two profiles are of different devices: /device:TPU:0 before, /device:TPU:9 now
where the time goes in v3:
time: 191 us; the launch traced here: 190 us
  starting transfers between devices  71.9 us (38%)
  local copies, waits for them, and re-layouts  45.1 us (24%)
  other arithmetic  30.5 us (16%)
  waiting for transfers between devices  23.7 us (12%)
  matrix products  17.2 us (9%)
    ppermute x16, starting transfers between devices, to_partner(): return lax.ppermute(x, 'feat', [(i, i ^ step) for i in range(8)])  20.3 us
    unnamed x100, local copies, waits for them, and re-layouts  10.9 us
    ppermute x16, waiting for transfers between devices, to_partner(): return lax.ppermute(x, 'feat', [(i, i ^ step) for i in range(8)])  10.5 us
    ppermute x4, starting transfers between devices, by_line(): crossed = [lax.ppermute(x, 'dp', across) for x in near]  9.46 us
    dynamic_slice x4, local copies, waits for them, and re-layouts, scatter_sum(): kept = lax.dynamic_index_in_dim(halves, core, 0, False)  8.44 us
    dot_general x4, matrix products, dot(): return jnp.dot(a, b, preferred_element_type=jnp.float32)  8.2 us
    ppermute x4, starting transfers between devices, by_line(): lax.ppermute((dot_t(with_near, a) + dot_t(other_far, b)).astype(jnp.bfloa...  7.98 us
    convert_element_type x5, other arithmetic, center(): return (block.astype(jnp.float32) - shift).astype(jnp.bfloat16)  6.17 us
  transfers between devices with their start and end apart: 45, of which 14 were waited for; matrix products, arithmetic and copies ran while one was open for 44% of the time, Pallas kernels for 0%

profile of v3, /device:TPU:9, one launch (start us, length us, event | category | flops | bytes accessed | tf_op | source)
XLA Modules:
  0.0 189.6 jit_solution(14485837341807171064)
XLA Ops:
  20.0 2.1 %collective-permute-start.3 = (f32[2,1024]{1,0:T(2,128)S(1)}, f32[2,1024]{1,0:T(2,128)S(1)}, u32[]{:S(2)}, u32[]{:S(2)}) collective-permute-start(f32[2,1024]{1,0:T(2,128)S(1)} %pad_maximum_fusion.17), channel_id=1, source_target_pairs={{0,8},{8,0},{16,24},{24,16},{1,9},{9,1},{17,25},{25,17},{2,10},{10... | collective-permute-start | bytes 24584 | tf_op jit(solution)/shard_map/ppermute | solution.py:53
  24.0 3.4 %collective-permute-start.10 = (bf16[128,1024]{1,0:T(8,128)(2,1)S(1)}, bf16[128,1024]{1,0:T(8,128)(2,1)S(1)}, u32[]{:S(2)}, u32[]{:S(2)}) collective-permute-start(bf16[128,1024]{1,0:T(8,128)(2,1)S(1)} %collective-permute-done.6), channel_id=1, source_target_pairs={{8,16},{16,8},{9,17},{17,9},{10,18},{18,10},{11,19},{19,11},{12,20... | collective-permute-start | bytes 786440 | tf_op jit(solution)/shard_map/ppermute | solution.py:128
  29.4 2.3 %collective-permute-done.5 = bf16[128,1024]{1,0:T(8,128)(2,1)S(1)} collective-permute-done((bf16[128,1024]{1,0:T(8,128)(2,1)S(1)}, bf16[128,1024]{1,0:T(8,128)(2,1)S(1)}, u32[]{:S(2)}, u32[]{:S(2)}) %collective-permute-start.5) | collective-permute-done | bytes 262176 | tf_op jit(solution)/shard_map/ppermute | solution.py:106
  31.6 2.3 %collective-permute-start.9 = (bf16[128,1024]{1,0:T(8,128)(2,1)S(1)}, bf16[128,1024]{1,0:T(8,128)(2,1)S(1)}, u32[]{:S(2)}, u32[]{:S(2)}) collective-permute-start(bf16[128,1024]{1,0:T(8,128)(2,1)S(1)} %collective-permute-done.5), channel_id=1, source_target_pairs={{8,16},{16,8},{9,17},{17,9},{10,18},{18,10},{11,19},{19,11},{12,20... | collective-permute-start | bytes 786440 | tf_op jit(solution)/shard_map/ppermute | solution.py:128
  42.6 4.4 %collective-permute-done.9 = bf16[128,1024]{1,0:T(8,128)(2,1)S(1)} collective-permute-done((bf16[128,1024]{1,0:T(8,128)(2,1)S(1)}, bf16[128,1024]{1,0:T(8,128)(2,1)S(1)}, u32[]{:S(2)}, u32[]{:S(2)}) %collective-permute-start.9) | collective-permute-done | bytes 262176 | tf_op jit(solution)/shard_map/ppermute | solution.py:128
  49.5 2.1 %collective-permute-start.26 = (bf16[512,256]{1,0:T(8,128)(2,1)}, bf16[512,256]{1,0:T(8,128)(2,1)}, u32[]{:S(2)}, u32[]{:S(2)}) collective-permute-start(bf16[512,256]{1,0:T(8,128)(2,1)} %get-tuple-element.15), channel_id=1, source_target_pairs={{8,16},{16,8},{9,17},{17,9},{10,18},{18,10},{11,19},{19,11},{12,20... | collective-permute-start | bytes 786440 | tf_op jit(solution)/shard_map/ppermute | solution.py:109
  52.3 3.1 %collective-permute-start.27 = (bf16[512,256]{1,0:T(8,128)(2,1)}, bf16[512,256]{1,0:T(8,128)(2,1)}, u32[]{:S(2)}, u32[]{:S(2)}) collective-permute-start(bf16[512,256]{1,0:T(8,128)(2,1)} %get-tuple-element.16), channel_id=1, source_target_pairs={{8,16},{16,8},{9,17},{17,9},{10,18},{18,10},{11,19},{19,11},{12,20... | collective-permute-start | bytes 786440 | tf_op jit(solution)/shard_map/ppermute | solution.py:131
  55.4 2.1 %collective-permute-start.28 = (bf16[512,256]{1,0:T(8,128)(2,1)}, bf16[512,256]{1,0:T(8,128)(2,1)S(1)}, u32[]{:S(2)}, u32[]{:S(2)}) collective-permute-start(bf16[512,256]{1,0:T(8,128)(2,1)} %get-tuple-element.17), channel_id=1, source_target_pairs={{8,16},{16,8},{9,17},{17,9},{10,18},{18,10},{11,19},{19,11},{12,20... | collective-permute-start | bytes 786440 | tf_op jit(solution)/shard_map/ppermute | solution.py:131
  58.8 2.7 %subtract_convert_fusion.7 = (bf16[128,1024]{1,0:T(8,128)(2,1)}, bf16[128,1024]{1,0:T(8,128)(2,1)S(1)}, bf16[128,1024]{1,0:T(8,128)(2,1)S(1)}, bf16[128,1024]{1,...) fusion(bf16[128,1024]{1,0:T(8,128)(2,1)S(1)} %collective-permut, ...), kind=kLoop, calls=%fused_computation.66 | loop fusion | flops 4718592 | bytes 6295552 | tf_op jit(solution)/shard_map/convert_element_type | solution.py:115
  65.1 2.6 %reshape.49 = f32[2,256,1024]{1,0,2:T(2,128)S(1)} reshape(f32[512,1024]{0,1:T(8,128)} %pad_maximum_fusion) | data formatting | bytes 4194304 | tf_op jit(solution)/shard_map/reshape | solution.py:71
  69.6 3.5 %copy.29 = bf16[1,256,1024]{2,1,0:T(8,128)(2,1)} copy(bf16[1,256,1024]{1,0,2:T(2,128)(2,1)} %constant_dynamic-slice_fusion.2) | data formatting | bytes 1048576
  73.2 4.5 %collective-permute-start.13 = (bf16[256,1024]{1,0:T(8,128)(2,1)}, bf16[256,1024]{1,0:T(8,128)(2,1)}, u32[]{:S(2)}, u32[]{:S(2)}) collective-permute-start(bf16[256,1024]{1,0:T(8,128)(2,1)} %bitcast.85), channel_id=1, source_target_pairs={{0,1},{1,0},{2,3},{3,2},{4,5},{5,4},{6,7},{7,6},{8,9},{9,8},{10,11... | collective-permute-start | bytes 1572872 | tf_op jit(solution)/shard_map/ppermute | solution.py:64
  82.9 2.3 %copy.19 = f32[1,256,1024]{2,1,0:T(8,128)S(1)} copy(f32[1,256,1024]{1,0,2:T(1,128)} %constant_dynamic-slice_fusion.3) | data formatting | bytes 2097152 | tf_op jit(solution)/shard_map/jit(dynamic_index_in_dim)/dynamic_slice | solution.py:73
  89.6 2.4 %collective-permute-done.14 = bf16[64,1024]{1,0:T(8,128)(2,1)S(1)} collective-permute-done((bf16[64,1024]{1,0:T(8,128)(2,1)S(1)}, bf16[64,1024]{1,0:T(8,128)(2,1)S(1)}, u32[]{:S(2)}, u32[]{:S(2)}) %collective-permute-start.14) | collective-permute-done | bytes 131104 | tf_op jit(solution)/shard_map/ppermute | solution.py:64
  92.0 2.6 %collective-permute-done.15 = bf16[64,1024]{1,0:T(8,128)(2,1)S(1)} collective-permute-done((bf16[64,1024]{1,0:T(8,128)(2,1)S(1)}, bf16[64,1024]{1,0:T(8,128)(2,1)S(1)}, u32[]{:S(2)}, u32[]{:S(2)}) %collective-permute-start.15) | collective-permute-done | bytes 131104 | tf_op jit(solution)/shard_map/ppermute | solution.py:64
  95.6 2.1 %collective-permute-start.17 = (bf16[64,512]{1,0:T(8,128)(2,1)S(1)}, bf16[64,512]{1,0:T(8,128)(2,1)S(1)}, u32[]{:S(2)}, u32[]{:S(2)}) collective-permute-start(bf16[64,512]{1,0:T(8,128)(2,1)S(1)} %slice.41), channel_id=1, source_target_pairs={{8,16},{16,8},{9,17},{17,9},{10,18},{18,10},{11,19},{19,11},{12,20... | collective-permute-start | bytes 196616 | tf_op jit(solution)/shard_map/ppermute | solution.py:138
  97.7 3.3 %collective-permute-start.29 = (bf16[512,256]{1,0:T(8,128)(2,1)S(1)}, bf16[512,256]{1,0:T(8,128)(2,1)S(1)}, u32[]{:S(2)}, u32[]{:S(2)}) collective-permute-start(bf16[512,256]{1,0:T(8,128)(2,1)S(1)} %copy-done.16), channel_id=1, source_target_pairs={{8,16},{16,8},{9,17},{17,9},{10,18},{18,10},{11,19},{19,11},{12,20... | collective-permute-start | bytes 786440 | tf_op jit(solution)/shard_map/ppermute | solution.py:140
  109.5 2.6 %reshape.51 = f32[2,256,1024]{1,0,2:T(2,128)S(1)} reshape(f32[512,1024]{0,1:T(8,128)} %pad_maximum_fusion.1) | data formatting | bytes 4194304 | tf_op jit(solution)/shard_map/reshape | solution.py:71
  114.0 3.5 %copy.30 = bf16[1,256,1024]{2,1,0:T(8,128)(2,1)} copy(bf16[1,256,1024]{1,0,2:T(2,128)(2,1)} %constant_dynamic-slice_fusion) | data formatting | bytes 1048576
  117.5 2.2 %collective-permute-start.30 = (bf16[256,1024]{1,0:T(8,128)(2,1)}, bf16[256,1024]{1,0:T(8,128)(2,1)}, u32[]{:S(2)}, u32[]{:S(2)}) collective-permute-start(bf16[256,1024]{1,0:T(8,128)(2,1)} %bitcast.84), channel_id=1, source_target_pairs={{0,1},{1,0},{2,3},{3,2},{4,5},{5,4},{6,7},{7,6},{8,9},{9,8},{10,11... | collective-permute-start | bytes 1572872 | tf_op jit(solution)/shard_map/ppermute | solution.py:64
  119.7 2.0 %pad_maximum_fusion.6 = bf16[4,64,1536]{2,1,0:T(8,128)(2,1)} fusion(bf16[1,64,1536]{2,1,0:T(8,128)(2,1)} %bitcast.13, bf16[1,64,1536]{2,1,0:T(8,128)(2,1)} %bitcast.12, bf16[1,64,1536]{2,1,0:T(8,128)(2,1)S(1)} %bitcast.72, bf16[1,64,1536]{2,1,0:T(8,128)(2,1)S(1)} %get-tuple-element.39), kind=kLoop, calls=%fused_computation.49 | loop fusion | flops 1179648 | bytes 1572864 | tf_op jit(solution)/shard_map/stack | solution.py:86
  121.7 2.8 %gather_fusion = bf16[4,64,1536]{2,1,0:T(8,128)(2,1)} fusion(bf16[4,64,1536]{2,1,0:T(8,128)(2,1)} %pad_maximum_fusion.6, s32[1024]{0:T(1024)} %pad_clamp_fusion.1), kind=kCustom, calls=%fused_computation | custom fusion | bytes 1572880 | tf_op jit(solution)/shard_map/gather | solution.py:87
  124.5 2.0 %broadcast_select_fusion = bf16[4,64,1536]{2,1,0:T(8,128)(2,1)} fusion(bf16[4,64,1536]{2,1,0:T(8,128)(2,1)} %gather_fusion, pred[]{:T(512)S(6)} %eq.40, bf16[1,64,1536]{2,1,0:T(8,128)(2,1)} %bitcast.13, bf16[1,64,1536]{2,1,0:T(8,128)(2,1)} %bitcast.12, bf16[1,64,1536]{2,1,0:T(8,128)(2,1)S(1)} %bitcast.73, bf16[1,64,1536]{2,1,0:T(8,128)(2,1)S(1)} %get-tuple-element.39), kind=kLoop, calls=%fused_computation.50 | loop fusion | flops 1572864 | bytes 2359297 | tf_op jit(solution)/shard_map/jit(_where)/select_n | solution.py:87
  126.5 2.7 %gather_fusion.1 = bf16[4,64,1536]{2,1,0:T(8,128)(2,1)} fusion(bf16[4,64,1536]{2,1,0:T(8,128)(2,1)} %broadcast_select_fusion, s32[1024]{0:T(1024)S(1)} %pad_clamp_fusion), kind=kCustom, calls=%fused_computation.1 | custom fusion | bytes 1572880 | tf_op jit(solution)/shard_map/gather | solution.py:88
  129.2 2.0 %broadcast_select_fusion.1 = bf16[4,64,1536]{2,1,0:T(8,128)(2,1)} fusion(bf16[4,64,1536]{2,1,0:T(8,128)(2,1)} %gather_fusion.1, pred[]{:T(512)S(6)} %eq.39, bf16[4,64,1536]{2,1,0:T(8,128)(2,1)} %gather_fusion, bf16[1,64,1536]{2,1,0:T(8,128)(2,1)} %bitcast.13, bf16[1,64,1536]{2,1,0:T(8,128)(2,1)} %bitcast.12, bf16[1,64,1536]{2,1,0:T(8,128)(2,1)S(1)} %bitcast.74, ...), kind=kLoop, calls=%fused_computation.51 | loop fusion | flops 1966080 | bytes 3145730 | tf_op jit(solution)/shard_map/jit(_where)/select_n | solution.py:88
  131.2 2.3 %copy.22 = bf16[256,1536]{0,1:T(8,128)(2,1)} copy(bf16[256,1536]{1,0:T(8,128)(2,1)} %bitcast.63) | data formatting | bytes 1572864 | tf_op jit(solution)/shard_map/jit(_where)/select_n | solution.py:88
  135.4 2.3 %copy.24 = f32[1,256,1024]{2,1,0:T(8,128)S(1)} copy(f32[1,256,1024]{1,0,2:T(1,128)} %constant_dynamic-slice_fusion.1) | data formatting | bytes 2097152 | tf_op jit(solution)/shard_map/jit(dynamic_index_in_dim)/dynamic_slice | solution.py:73
  145.1 2.7 %collective-permute-done.33 = bf16[64,1024]{1,0:T(8,128)(2,1)S(1)} collective-permute-done((bf16[64,1024]{1,0:T(8,128)(2,1)S(1)}, bf16[64,1024]{1,0:T(8,128)(2,1)S(1)}, u32[]{:S(2)}, u32[]{:S(2)}) %collective-permute-start.33) | collective-permute-done | bytes 131104 | tf_op jit(solution)/shard_map/ppermute | solution.py:64
  164.1 2.0 %collective-permute-start.41 = (bf16[512,256]{1,0:T(8,128)(2,1)}, bf16[512,256]{1,0:T(8,128)(2,1)}, u32[]{:S(2)}, u32[]{:S(2)}) collective-permute-start(bf16[512,256]{1,0:T(8,128)(2,1)} %fusion.15), channel_id=1, source_target_pairs={{8,0},{16,24},{9,1},{17,25},{10,2},{18,26},{11,3},{19,27},{12,4},{... | collective-permute-start | bytes 786440 | tf_op jit(solution)/shard_map/ppermute | solution.py:150
  171.1 2.5 %gather_fusion.3 = bf16[4,64,1024]{2,1,0:T(8,128)(2,1)} fusion(bf16[4,64,1024]{2,1,0:T(8,128)(2,1)} %broadcast_select_fusion.2, s32[1024]{0:T(1024)S(1)} %pad_clamp_fusion), kind=kCustom, calls=%fused_computation.3 | custom fusion | bytes 1048592 | tf_op jit(solution)/shard_map/gather | solution.py:88
  176.7 2.6 %collective-permute-start.37 = (bf16[256,1024]{0,1:T(8,128)(2,1)S(1)}, bf16[256,1024]{0,1:T(8,128)(2,1)S(1)}, u32[]{:S(2)}, u32[]{:S(2)}) collective-permute-start(bf16[256,1024]{0,1:T(8,128)(2,1)S(1)} %copy.27), channel_id=1, source_target_pairs={{0,1},{1,0},{2,3},{3,2},{4,5},{5,4},{6,7},{7,6},{8,9},{9,8},{10,11... | collective-permute-start | bytes 1572872 | tf_op jit(solution)/shard_map/ppermute | solution.py:64
  184.9 4.7 %fusion.7 = f32[512,1024]{1,0:T(8,128)} fusion(bf16[512,1024]{1,0:T(8,128)(2,1)S(1)} %copy-done, f32[512,1024]{1,0:T(8,128)S(1)} %fusion.23, f32[512,1024]{1,0:T(8,128)S(1)} %fusion.18, f32[512,1024]{1,0:T(8,128)S(1)} %fusion.16, bf16[512,1024]{1,0:T(8,128)(2,1)S(1)} %copy-done.46, bf16[512,256]{1,0:T(8,128)(2,1)} %collective-permute-done.41, ...), kind=kOutput, calls=%fused_computation.16 | convolution fusion | flops 555483136 | bytes 13122561 | tf_op jit(solution)/shard_map/dot_general | solution.py:163
  (228 shorter events, 101.6 us)
Async XLA Ops:
  1.5 9.3 %collective-permute-start = (f32[1024]{0:T(1024)S(1)}, f32[1024]{0:T(1024)S(1)}, u32[]{:S(2)}, u32[]{:S(2)}) collective-permute-start(f32[1024]{0:T(1024)S(1)} %convert_reduce_fusion), channel_id=1, source_target_pairs={{0,8},{8,16},{16,24},{24,0},{1,9},{9,17},{17,25},{25,1},{2,10},{10... | collective-permute-start | bytes 12296 | tf_op jit(solution)/shard_map/ppermute | solution.py:107
  4.0 9.5 %collective-permute-start.2 = (f32[1024]{0:T(1024)S(1)}, f32[1024]{0:T(1024)S(1)}, u32[]{:S(2)}, u32[]{:S(2)}) collective-permute-start(f32[1024]{0:T(1024)S(1)} %convert_reduce_fusion), channel_id=1, source_target_pairs={{0,24},{8,0},{16,8},{24,16},{1,25},{9,1},{17,9},{25,17},{2,26},{10... | collective-permute-start | bytes 12296 | tf_op jit(solution)/shard_map/ppermute | solution.py:107
  6.6 15.5 %collective-permute-start.8 = (bf16[128,1024]{1,0:T(8,128)(2,1)S(1)}, bf16[128,1024]{1,0:T(8,128)(2,1)S(1)}, u32[]{:S(2)}, u32[]{:S(2)}) collective-permute-start(bf16[128,1024]{1,0:T(8,128)(2,1)S(1)} %get-tuple-element.14), channel_id=1, source_target_pairs={{0,8},{24,16},{1,9},{25,17},{2,10},{26,18},{3,11},{27,19},{4,12},{... | collective-permute-start | bytes 786440 | tf_op jit(solution)/shard_map/ppermute | solution.py:111
  7.9 16.1 %collective-permute-start.6 = (bf16[128,1024]{1,0:T(8,128)(2,1)S(1)}, bf16[128,1024]{1,0:T(8,128)(2,1)S(1)}, u32[]{:S(2)}, u32[]{:S(2)}) collective-permute-start(bf16[128,1024]{1,0:T(8,128)(2,1)S(1)} %get-tuple-element.12), channel_id=1, source_target_pairs={{0,8},{24,16},{1,9},{25,17},{2,10},{26,18},{3,11},{27,19},{4,12},{... | collective-permute-start | bytes 786440 | tf_op jit(solution)/shard_map/ppermute | solution.py:111
  10.9 16.5 %collective-permute-start.7 = (bf16[128,1024]{1,0:T(8,128)(2,1)S(1)}, bf16[128,1024]{1,0:T(8,128)(2,1)S(1)}, u32[]{:S(2)}, u32[]{:S(2)}) collective-permute-start(bf16[128,1024]{1,0:T(8,128)(2,1)S(1)} %get-tuple-element.13), channel_id=1, source_target_pairs={{0,8},{24,16},{1,9},{25,17},{2,10},{26,18},{3,11},{27,19},{4,12},{... | collective-permute-start | bytes 786440 | tf_op jit(solution)/shard_map/ppermute | solution.py:111
  12.2 19.5 %collective-permute-start.5 = (bf16[128,1024]{1,0:T(8,128)(2,1)S(1)}, bf16[128,1024]{1,0:T(8,128)(2,1)S(1)}, u32[]{:S(2)}, u32[]{:S(2)}) collective-permute-start(bf16[128,1024]{1,0:T(8,128)(2,1)S(1)} %get-tuple-element.35), channel_id=1, source_target_pairs={{0,8},{24,16},{1,9},{25,17},{2,10},{26,18},{3,11},{27,19},{4,12},{... | collective-permute-start | bytes 786440 | tf_op jit(solution)/shard_map/ppermute | solution.py:106
  20.0 14.7 %collective-permute-start.3 = (f32[2,1024]{1,0:T(2,128)S(1)}, f32[2,1024]{1,0:T(2,128)S(1)}, u32[]{:S(2)}, u32[]{:S(2)}) collective-permute-start(f32[2,1024]{1,0:T(2,128)S(1)} %pad_maximum_fusion.17), channel_id=1, source_target_pairs={{0,8},{8,0},{16,24},{24,16},{1,9},{9,1},{17,25},{25,17},{2,10},{10... | collective-permute-start | bytes 24584 | tf_op jit(solution)/shard_map/ppermute | solution.py:53
  22.1 16.5 %collective-permute-start.12 = (bf16[128,1024]{1,0:T(8,128)(2,1)S(1)}, bf16[128,1024]{1,0:T(8,128)(2,1)S(1)}, u32[]{:S(2)}, u32[]{:S(2)}) collective-permute-start(bf16[128,1024]{1,0:T(8,128)(2,1)S(1)} %collective-permute-done.8), channel_id=1, source_target_pairs={{8,16},{16,8},{9,17},{17,9},{10,18},{18,10},{11,19},{19,11},{12,20... | collective-permute-start | bytes 786440 | tf_op jit(solution)/shard_map/ppermute | solution.py:128
  24.0 15.9 %collective-permute-start.10 = (bf16[128,1024]{1,0:T(8,128)(2,1)S(1)}, bf16[128,1024]{1,0:T(8,128)(2,1)S(1)}, u32[]{:S(2)}, u32[]{:S(2)}) collective-permute-start(bf16[128,1024]{1,0:T(8,128)(2,1)S(1)} %collective-permute-done.6), channel_id=1, source_target_pairs={{8,16},{16,8},{9,17},{17,9},{10,18},{18,10},{11,19},{19,11},{12,20... | collective-permute-start | bytes 786440 | tf_op jit(solution)/shard_map/ppermute | solution.py:128
  27.4 13.9 %collective-permute-start.11 = (bf16[128,1024]{1,0:T(8,128)(2,1)S(1)}, bf16[128,1024]{1,0:T(8,128)(2,1)S(1)}, u32[]{:S(2)}, u32[]{:S(2)}) collective-permute-start(bf16[128,1024]{1,0:T(8,128)(2,1)S(1)} %collective-permute-done.7), channel_id=1, source_target_pairs={{8,16},{16,8},{9,17},{17,9},{10,18},{18,10},{11,19},{19,11},{12,20... | collective-permute-start | bytes 786440 | tf_op jit(solution)/shard_map/ppermute | solution.py:128
  31.6 15.4 %collective-permute-start.9 = (bf16[128,1024]{1,0:T(8,128)(2,1)S(1)}, bf16[128,1024]{1,0:T(8,128)(2,1)S(1)}, u32[]{:S(2)}, u32[]{:S(2)}) collective-permute-start(bf16[128,1024]{1,0:T(8,128)(2,1)S(1)} %collective-permute-done.5), channel_id=1, source_target_pairs={{8,16},{16,8},{9,17},{17,9},{10,18},{18,10},{11,19},{19,11},{12,20... | collective-permute-start | bytes 786440 | tf_op jit(solution)/shard_map/ppermute | solution.py:128
  37.5 12.0 %collective-permute-start.4 = (f32[2,1024]{1,0:T(2,128)S(1)}, f32[2,1024]{1,0:T(2,128)S(1)}, u32[]{:S(2)}, u32[]{:S(2)}) collective-permute-start(f32[2,1024]{1,0:T(2,128)S(1)} %fusion.72), channel_id=1, source_target_pairs={{0,24},{8,16},{16,8},{24,0},{1,25},{9,17},{17,9},{25,1},{2,26},{10... | collective-permute-start | bytes 24584 | tf_op jit(solution)/shard_map/ppermute | solution.py:53
  38.6 13.6 %collective-permute-start.25 = (bf16[128,1024]{1,0:T(8,128)(2,1)S(1)}, bf16[128,1024]{1,0:T(8,128)(2,1)S(1)}, u32[]{:S(2)}, u32[]{:S(2)}) collective-permute-start(bf16[128,1024]{1,0:T(8,128)(2,1)S(1)} %collective-permute-done.12), channel_id=1, source_target_pairs={{8,0},{16,24},{9,1},{17,25},{10,2},{18,26},{11,3},{19,27},{12,4},{... | collective-permute-start | bytes 786440 | tf_op jit(solution)/shard_map/ppermute | solution.py:129
  39.9 15.5 %collective-permute-start.23 = (bf16[128,1024]{1,0:T(8,128)(2,1)S(1)}, bf16[128,1024]{1,0:T(8,128)(2,1)S(1)}, u32[]{:S(2)}, u32[]{:S(2)}) collective-permute-start(bf16[128,1024]{1,0:T(8,128)(2,1)S(1)} %collective-permute-done.10), channel_id=1, source_target_pairs={{8,0},{16,24},{9,1},{17,25},{10,2},{18,26},{11,3},{19,27},{12,4},{... | collective-permute-start | bytes 786440 | tf_op jit(solution)/shard_map/ppermute | solution.py:129
  41.3 16.2 %collective-permute-start.24 = (bf16[128,1024]{1,0:T(8,128)(2,1)S(1)}, bf16[128,1024]{1,0:T(8,128)(2,1)S(1)}, u32[]{:S(2)}, u32[]{:S(2)}) collective-permute-start(bf16[128,1024]{1,0:T(8,128)(2,1)S(1)} %collective-permute-done.11), channel_id=1, source_target_pairs={{8,0},{16,24},{9,1},{17,25},{10,2},{18,26},{11,3},{19,27},{12,4},{... | collective-permute-start | bytes 786440 | tf_op jit(solution)/shard_map/ppermute | solution.py:129
  47.0 11.8 %collective-permute-start.22 = (bf16[128,1024]{1,0:T(8,128)(2,1)S(1)}, bf16[128,1024]{1,0:T(8,128)(2,1)S(1)}, u32[]{:S(2)}, u32[]{:S(2)}) collective-permute-start(bf16[128,1024]{1,0:T(8,128)(2,1)S(1)} %collective-permute-done.9), channel_id=1, source_target_pairs={{8,0},{16,24},{9,1},{17,25},{10,2},{18,26},{11,3},{19,27},{12,4},{... | collective-permute-start | bytes 786440 | tf_op jit(solution)/shard_map/ppermute | solution.py:129
  49.5 28.2 %collective-permute-start.26 = (bf16[512,256]{1,0:T(8,128)(2,1)}, bf16[512,256]{1,0:T(8,128)(2,1)}, u32[]{:S(2)}, u32[]{:S(2)}) collective-permute-start(bf16[512,256]{1,0:T(8,128)(2,1)} %get-tuple-element.15), channel_id=1, source_target_pairs={{8,16},{16,8},{9,17},{17,9},{10,18},{18,10},{11,19},{19,11},{12,20... | collective-permute-start | bytes 786440 | tf_op jit(solution)/shard_map/ppermute | solution.py:109
  52.3 27.1 %collective-permute-start.27 = (bf16[512,256]{1,0:T(8,128)(2,1)}, bf16[512,256]{1,0:T(8,128)(2,1)}, u32[]{:S(2)}, u32[]{:S(2)}) collective-permute-start(bf16[512,256]{1,0:T(8,128)(2,1)} %get-tuple-element.16), channel_id=1, source_target_pairs={{8,16},{16,8},{9,17},{17,9},{10,18},{18,10},{11,19},{19,11},{12,20... | collective-permute-start | bytes 786440 | tf_op jit(solution)/shard_map/ppermute | solution.py:131
  55.4 34.1 %collective-permute-start.28 = (bf16[512,256]{1,0:T(8,128)(2,1)}, bf16[512,256]{1,0:T(8,128)(2,1)S(1)}, u32[]{:S(2)}, u32[]{:S(2)}) collective-permute-start(bf16[512,256]{1,0:T(8,128)(2,1)} %get-tuple-element.17), channel_id=1, source_target_pairs={{8,16},{16,8},{9,17},{17,9},{10,18},{18,10},{11,19},{19,11},{12,20... | collective-permute-start | bytes 786440 | tf_op jit(solution)/shard_map/ppermute | solution.py:131
  73.2 12.2 %collective-permute-start.13 = (bf16[256,1024]{1,0:T(8,128)(2,1)}, bf16[256,1024]{1,0:T(8,128)(2,1)}, u32[]{:S(2)}, u32[]{:S(2)}) collective-permute-start(bf16[256,1024]{1,0:T(8,128)(2,1)} %bitcast.85), channel_id=1, source_target_pairs={{0,1},{1,0},{2,3},{3,2},{4,5},{5,4},{6,7},{7,6},{8,9},{9,8},{10,11... | collective-permute-start | bytes 1572872 | tf_op jit(solution)/shard_map/ppermute | solution.py:64
  102.7 17.0 %collective-permute-start.18 = (bf16[64,1536]{1,0:T(8,128)(2,1)}, bf16[64,1536]{1,0:T(8,128)(2,1)S(1)}, u32[]{:S(2)}, u32[]{:S(2)}) collective-permute-start(bf16[64,1536]{1,0:T(8,128)(2,1)} %get-tuple-element.40), channel_id=1, source_target_pairs={{0,2},{1,3},{2,0},{3,1},{4,6},{5,7},{6,4},{7,5},{8,10},{9,11},{10,... | collective-permute-start | bytes 589832 | tf_op jit(solution)/shard_map/ppermute | solution.py:64
  104.1 15.6 %collective-permute-start.19 = (bf16[64,1536]{1,0:T(8,128)(2,1)}, bf16[64,1536]{1,0:T(8,128)(2,1)}, u32[]{:S(2)}, u32[]{:S(2)}) collective-permute-start(bf16[64,1536]{1,0:T(8,128)(2,1)} %get-tuple-element.40), channel_id=1, source_target_pairs={{0,4},{1,5},{2,6},{3,7},{4,0},{5,1},{6,2},{7,3},{8,12},{9,13},{10,... | collective-permute-start | bytes 589832 | tf_op jit(solution)/shard_map/ppermute | solution.py:64
  104.4 15.3 %collective-permute-start.20 = (bf16[64,1536]{1,0:T(8,128)(2,1)}, bf16[64,1536]{1,0:T(8,128)(2,1)}, u32[]{:S(2)}, u32[]{:S(2)}) collective-permute-start(bf16[64,1536]{1,0:T(8,128)(2,1)} %get-tuple-element.40), channel_id=1, source_target_pairs={{0,6},{1,7},{2,4},{3,5},{4,2},{5,3},{6,0},{7,1},{8,14},{9,15},{10,... | collective-permute-start | bytes 589832 | tf_op jit(solution)/shard_map/ppermute | solution.py:64
  117.5 20.3 %collective-permute-start.30 = (bf16[256,1024]{1,0:T(8,128)(2,1)}, bf16[256,1024]{1,0:T(8,128)(2,1)}, u32[]{:S(2)}, u32[]{:S(2)}) collective-permute-start(bf16[256,1024]{1,0:T(8,128)(2,1)} %bitcast.84), channel_id=1, source_target_pairs={{0,1},{1,0},{2,3},{3,2},{4,5},{5,4},{6,7},{7,6},{8,9},{9,8},{10,11... | collective-permute-start | bytes 1572872 | tf_op jit(solution)/shard_map/ppermute | solution.py:64
  133.5 17.1 %collective-permute-start.21 = (bf16[256,1536]{0,1:T(8,128)(2,1)}, bf16[256,1536]{0,1:T(8,128)(2,1)}, u32[]{:S(2)}, u32[]{:S(2)}) collective-permute-start(bf16[256,1536]{0,1:T(8,128)(2,1)} %copy.22), channel_id=1, source_target_pairs={{0,1},{1,0},{2,3},{3,2},{4,5},{5,4},{6,7},{7,6},{8,9},{9,8},{10,11... | collective-permute-start | bytes 2359304 | tf_op jit(solution)/shard_map/ppermute | solution.py:64
  147.9 14.2 %collective-permute-start.34 = (bf16[64,1024]{1,0:T(8,128)(2,1)S(1)}, bf16[64,1024]{1,0:T(8,128)(2,1)S(1)}, u32[]{:S(2)}, u32[]{:S(2)}) collective-permute-start(bf16[64,1024]{1,0:T(8,128)(2,1)S(1)} %fusion.46), channel_id=1, source_target_pairs={{0,2},{1,3},{2,0},{3,1},{4,6},{5,7},{6,4},{7,5},{8,10},{9,11},{10,... | collective-permute-start | bytes 393224 | tf_op jit(solution)/shard_map/ppermute | solution.py:64
  148.7 15.4 %collective-permute-start.35 = (bf16[64,1024]{1,0:T(8,128)(2,1)S(1)}, bf16[64,1024]{1,0:T(8,128)(2,1)S(1)}, u32[]{:S(2)}, u32[]{:S(2)}) collective-permute-start(bf16[64,1024]{1,0:T(8,128)(2,1)S(1)} %fusion.46), channel_id=1, source_target_pairs={{0,4},{1,5},{2,6},{3,7},{4,0},{5,1},{6,2},{7,3},{8,12},{9,13},{10,... | collective-permute-start | bytes 393224 | tf_op jit(solution)/shard_map/ppermute | solution.py:64
  149.5 16.5 %collective-permute-start.36 = (bf16[64,1024]{1,0:T(8,128)(2,1)S(1)}, bf16[64,1024]{1,0:T(8,128)(2,1)S(1)}, u32[]{:S(2)}, u32[]{:S(2)}) collective-permute-start(bf16[64,1024]{1,0:T(8,128)(2,1)S(1)} %fusion.46), channel_id=1, source_target_pairs={{0,6},{1,7},{2,4},{3,5},{4,2},{5,3},{6,0},{7,1},{8,14},{9,15},{10,... | collective-permute-start | bytes 393224 | tf_op jit(solution)/shard_map/ppermute | solution.py:64
  155.1 29.1 %collective-permute-start.38 = (bf16[512,256]{1,0:T(8,128)(2,1)}, bf16[512,256]{1,0:T(8,128)(2,1)}, u32[]{:S(2)}, u32[]{:S(2)}) collective-permute-start(bf16[512,256]{1,0:T(8,128)(2,1)} %fusion.12), channel_id=1, source_target_pairs={{8,0},{16,24},{9,1},{17,25},{10,2},{18,26},{11,3},{19,27},{12,4},{... | collective-permute-start | bytes 786440 | tf_op jit(solution)/shard_map/ppermute | solution.py:150
  158.1 26.1 %collective-permute-start.39 = (bf16[512,256]{1,0:T(8,128)(2,1)}, bf16[512,256]{1,0:T(8,128)(2,1)}, u32[]{:S(2)}, u32[]{:S(2)}) collective-permute-start(bf16[512,256]{1,0:T(8,128)(2,1)} %fusion.13), channel_id=1, source_target_pairs={{8,0},{16,24},{9,1},{17,25},{10,2},{18,26},{11,3},{19,27},{12,4},{... | collective-permute-start | bytes 786440 | tf_op jit(solution)/shard_map/ppermute | solution.py:150
  162.1 22.1 %collective-permute-start.40 = (bf16[512,256]{1,0:T(8,128)(2,1)}, bf16[512,256]{1,0:T(8,128)(2,1)}, u32[]{:S(2)}, u32[]{:S(2)}) collective-permute-start(bf16[512,256]{1,0:T(8,128)(2,1)} %fusion.14), channel_id=1, source_target_pairs={{8,0},{16,24},{9,1},{17,25},{10,2},{18,26},{11,3},{19,27},{12,4},{... | collective-permute-start | bytes 786440 | tf_op jit(solution)/shard_map/ppermute | solution.py:150
  164.1 20.1 %collective-permute-start.41 = (bf16[512,256]{1,0:T(8,128)(2,1)}, bf16[512,256]{1,0:T(8,128)(2,1)}, u32[]{:S(2)}, u32[]{:S(2)}) collective-permute-start(bf16[512,256]{1,0:T(8,128)(2,1)} %fusion.15), channel_id=1, source_target_pairs={{8,0},{16,24},{9,1},{17,25},{10,2},{18,26},{11,3},{19,27},{12,4},{... | collective-permute-start | bytes 786440 | tf_op jit(solution)/shard_map/ppermute | solution.py:150
  (62 other events, 339.7 us)

commit v4 on v1

v4 whole, which is shorter than its diff:
```python
import functools
import math

import jax
import jax.numpy as jnp
from jax import lax
from jax.experimental import pallas as pl
from jax.experimental.pallas import tpu as pltpu
from jax.sharding import PartitionSpec as P

VMEM = pltpu.CompilerParams(vmem_limit_bytes=24 * 1024 * 1024)
NORM = 128


def kernel_call(body, outs, flops=0, smem=0):
    def call(*args):
        moved = sum(a.size * a.dtype.itemsize for a in args)
        moved += sum(math.prod(s) * jnp.dtype(t).itemsize for s, t in outs)
        space = [pltpu.SMEM] * smem + [pltpu.VMEM] * (len(args) - smem)
        return pl.pallas_call(
            body,
            out_shape=[jax.ShapeDtypeStruct(s, t) for s, t in outs],
            in_specs=[pl.BlockSpec(memory_space=m) for m in space],
            out_specs=[pl.BlockSpec(memory_space=pltpu.VMEM) for _ in outs],
            compiler_params=VMEM,
            cost_estimate=pl.CostEstimate(flops=0, bytes_accessed=0, transcendentals=0),
        )(*args)

    return call


def gram(left, right):
    return lax.dot_general(
        left, right, (((1,), (1,)), ((), ())), preferred_element_type=jnp.float32
    )


def dot_t(left, right):
    return lax.dot_general(
        left, right, (((0,), (0,)), ((), ())), preferred_element_type=jnp.float32
    )


def dot(left, right):
    return jnp.dot(left, right, preferred_element_type=jnp.float32)


def centered_into(out, at, piece, mean):
    block = (piece[...].astype(jnp.float32) - mean).astype(jnp.bfloat16)
    out[at:at + block.shape[0], :] = block
    wide = block.astype(jnp.float32)
    return jnp.sum(wide * wide, axis=0, keepdims=True)


def high_low(n, like):
    high = n.astype(jnp.bfloat16).astype(jnp.float32)
    lane = lax.broadcasted_iota(jnp.int32, like, 1)
    return jnp.where(lane == 0, high, jnp.where(lane == 1, n - high, 0.0))


def own_kernel(order, z, mean, own, turned, square, kept, sent):
    rows = z.shape[0]
    eighth, half = rows // 8, rows // 2
    square[...] = centered_into(own, 0, z, mean[...])
    for k in range(8):
        start = pl.multiple_of(order[k] * eighth, eighth)
        turned[k * eighth:(k + 1) * eighth, :] = own[pl.ds(start, eighth), :]
    inner = gram(turned[...], own[...])
    wide = turned[...].astype(jnp.float32)
    norm = jnp.sum(wide * wide, axis=1, keepdims=True)
    column = lax.broadcasted_iota(jnp.int32, (eighth, rows), 1)
    row = lax.broadcasted_iota(jnp.int32, (eighth, rows), 0)
    for k in range(8):
        here = slice(k * eighth, (k + 1) * eighth)
        off = jnp.where(column == row + order[k] * eighth, 0.0, inner[here])
        if k < 4:
            kept[here, :rows] = off
        else:
            sent[k * eighth - half:(k + 1) * eighth - half, :rows] = off.astype(jnp.bfloat16)
    lane = lax.broadcasted_iota(jnp.int32, (half, NORM), 1)
    kept[:, rows:] = jnp.where(lane == 0, norm[:half], 0.0)
    sent[:, rows:] = high_low(norm[half:], (half, NORM)).astype(jnp.bfloat16)


def first_kernel(turned, *refs):
    pieces = (len(refs) - 7) // 2
    near_in, far_in, mean = refs[:pieces], refs[pieces:2 * pieces], refs[2 * pieces]
    near, far, near_square, far_square, kept, sent = refs[2 * pieces + 1:]
    rows = near.shape[0]
    half = rows // 2
    for k, (pile, out, square) in enumerate(
        ((near_in, near, near_square), (far_in, far, far_square))
    ):
        at, total = 0, 0.0
        for piece in pile:
            total = total + centered_into(out, at, piece, mean[...])
            at += piece.shape[0]
        square[...] = total
        inner = gram(turned[...], out[...])
        kept[:, k * rows:(k + 1) * rows] = inner[:half]
        sent[:, k * rows:(k + 1) * rows] = inner[half:].astype(jnp.bfloat16)


def second_kernel(middle, turned, *refs):
    *ends, left, right, mean, own_kept, own_sent = refs[:-4]
    end, square, kept, sent = refs[-4:]
    rows, width = end.shape
    half = rows // 2
    for ref, own in ((kept, own_kept), (sent, own_sent)):
        ref[:, :rows] = own[:, :rows]
        ref[:, 2 * rows:] = own[:, rows:]

    def put(inner):
        kept[:, rows:2 * rows] = inner[:half]
        sent[:, rows:2 * rows] = inner[half:].astype(jnp.bfloat16)

    @pl.when(middle[0] == 1)
    def _():
        end[...] = jnp.zeros_like(end)
        square[...] = jnp.zeros_like(square)
        put(gram(turned[:, :width // 2], left[...]) + gram(turned[:, width // 2:], right[...]))

    @pl.when(middle[0] == 0)
    def _():
        at, total = 0, 0.0
        for piece in ends:
            total = total + centered_into(end, at, piece, mean[...])
            at += piece.shape[0]
        square[...] = total
        put(gram(turned[...], end[...]))


def with_norm(x, last):
    if not last:
        return x
    tail = x[:, last:]
    split = high_low(jnp.sum(tail, axis=1, keepdims=True), tail.shape)
    return jnp.concatenate([x[:, :last], split], axis=1)


def add_kernel(last, kept, got, mine, *out):
    total = with_norm(kept[...] + got[...].astype(jnp.float32), last)
    quarter = mine.shape[0]
    mine[...] = total[:quarter]
    for k, ref in enumerate(out, 1):
        ref[...] = total[k * quarter:(k + 1) * quarter].astype(jnp.bfloat16)


def total_kernel(last, mine, a, b, c, out):
    total = mine[...] + a[...].astype(jnp.float32)
    total = total + b[...].astype(jnp.float32) + c[...].astype(jnp.float32)
    out[...] = with_norm(total, last).astype(jnp.bfloat16)


def place_kernel(order, near, far, out):
    eighth = out.shape[0] // 8
    for k in range(4):
        here = slice(k * eighth, (k + 1) * eighth)
        out[pl.ds(pl.multiple_of(order[k] * eighth, eighth), eighth), :] = near[here, :]
        out[pl.ds(pl.multiple_of(order[4 + k] * eighth, eighth), eighth), :] = far[here, :]


def middle_kernel(inner, own, near, own_square, mean, *refs):
    *pieces, swapped, square, out = refs
    rows = own.shape[0]
    at = 0
    for piece in pieces:
        here = slice(at, at + piece.shape[1])
        block = (piece[...].astype(jnp.float32) - mean[:, here]).astype(jnp.bfloat16)
        swapped[:, here] = block
        wide = block.astype(jnp.float32)
        square[:, here] = jnp.sum(wide * wide, axis=0, keepdims=True)
        at += piece.shape[1]
    product = dot_t(inner[:, :rows], own[...]) + dot_t(inner[:, 2 * rows:], swapped[...])
    product = product - near[...].astype(jnp.float32) * (own_square[...] + square[...])
    out[...] = product.astype(jnp.bfloat16)


def last_kernel(
    total, middle, first, second, own, near, far, end, swapped, pushed, z, other,
    own_square, near_square, far_square, end_square, swapped_square, mean, spread, out,
):
    rows = own.shape[0]
    norm = jnp.sum(second[:, 2 * rows:].astype(jnp.float32), axis=1, keepdims=True)
    anchor = z[...].astype(jnp.float32)
    deviation = jnp.sqrt(spread[...] / (total - 1) + 0.0001)
    centered = anchor - mean[...]
    hinge = jnp.where(deviation < 1.0, centered / deviation, 0.0)
    plain = anchor - other[...].astype(jnp.float32) - total / (4.0 * (total - 1)) * hinge
    coef = 2.0 * total / (25.0 * (total - 1)) / (total - 1)
    both = dot(second[:, :rows], own[...])
    wide = own[...].astype(jnp.float32)

    @pl.when(middle[0] == 1)
    def _():
        product = both + dot(first[:, :rows], near[...])
        product = product + dot(first[:, rows:2 * rows], far[...])
        product = product + dot(second[:, rows:2 * rows], swapped[...])
        square = own_square[...] + near_square[...] + far_square[...] + swapped_square[...]
        out[...] = plain + coef * (product + wide * (norm - square))

    @pl.when(middle[0] == 0)
    def _():
        product = both + dot(second[:, rows:2 * rows], end[...])
        product = product + pushed[...].astype(jnp.float32)
        out[...] = plain + coef * (product + wide * (norm - own_square[...] - end_square[...]))


def to_partner(x, step):
    return lax.ppermute(x, "feat", [(i, i ^ step) for i in range(8)])


def scatter_sum(kept, sent, last=0):
    half, n = kept.shape
    eighth = (half // 4, n)
    mine, *out = kernel_call(
        functools.partial(add_kernel, last),
        [(eighth, jnp.float32)] + [(eighth, jnp.bfloat16)] * 3,
    )(kept, to_partner(sent, 1))
    got = [to_partner(x, 2 * k) for k, x in enumerate(out, 1)]
    return kernel_call(functools.partial(total_kernel, last), [(eighth, jnp.bfloat16)])(
        mine, *got
    )[0]


def gather_rows(x, order):
    near = jnp.concatenate([x] + [to_partner(x, 2 * k) for k in (1, 2, 3)])
    far = to_partner(near, 1)
    shape = (8 * x.shape[0], x.shape[1])
    return kernel_call(place_kernel, [(shape, jnp.bfloat16)], smem=1)(order, near, far)[0]


def after(x, *others):
    return lax.optimization_barrier((x, *others))[0]


def by_line(z_anchor, z_other):
    rows, width = z_anchor.shape
    total = rows * 4
    plane = lax.axis_index("dp")
    middle = ((plane == 1) | (plane == 2)).astype(jnp.int32).reshape(1)
    order = lax.axis_index("feat") ^ jnp.array([0, 2, 4, 6, 1, 3, 5, 7], jnp.int32)
    inward, across, outward = [(0, 1), (3, 2)], [(1, 2), (2, 1)], [(1, 0), (2, 3)]
    half = rows // 2
    flat, block = ((1, width), jnp.float32), ((rows, width), jnp.bfloat16)
    one_gram = 2 * rows * rows * width

    cuts = [0, 3 * rows // 8, 3 * rows // 4, rows]
    pieces = [z_anchor[a:b] for a, b in zip(cuts, cuts[1:])]
    cuts = [0, width // 4, width // 2, width]
    swaps = [z_anchor[:, a:b] for a, b in zip(cuts, cuts[1:])]

    near = [lax.ppermute(pieces[0], "dp", inward)]
    anchor = z_anchor.astype(jnp.float32)
    sums = jnp.sum(anchor, axis=0, keepdims=True)
    apart = anchor - sums / rows
    stats = jnp.concatenate([sums, jnp.sum(apart * apart, axis=0, keepdims=True)])
    all_stats = [stats] + [
        lax.ppermute(stats, "dp", [(i, (i + k) % 4) for i in range(4)]) for k in (1, 2, 3)
    ]
    swapped = [lax.ppermute(swaps[0], "dp", across)]
    for piece in pieces[1:]:
        near.append(lax.ppermute(after(piece, swapped[0], *all_stats[1:]), "dp", inward))
    mean = (all_stats[0][:1] + all_stats[1][:1] + all_stats[2][:1] + all_stats[3][:1]) / total
    spread = 0.0
    for one in all_stats:
        shift = one[:1] / rows - mean
        spread = spread + (one[1:] + rows * shift * shift)

    own, turned, own_square, own_kept, own_sent = kernel_call(
        own_kernel,
        [block, block, flat, ((half, rows + NORM), jnp.float32), ((half, rows + NORM), jnp.bfloat16)],
        flops=one_gram, smem=1,
    )(order, after(z_anchor, swapped[0]), mean)

    near[2] = after(near[2], near[1])
    crossed = [lax.ppermute(x, "dp", across) for x in near]
    at_end = [lax.ppermute(x, "dp", outward) for x in crossed]
    swapped.append(lax.ppermute(after(swaps[1], near[-1]), "dp", across))

    near, far, near_square, far_square, kept, sent = kernel_call(
        first_kernel,
        [block, block, flat, flat, ((half, 2 * rows), jnp.float32), ((half, 2 * rows), jnp.bfloat16)],
        flops=2 * one_gram,
    )(after(turned, at_end[0]), *near, *crossed, mean)
    first = scatter_sum(kept, sent)
    other_far = lax.ppermute(first[:, rows:], "dp", across)
    swapped.append(lax.ppermute(after(swaps[2], first), "dp", across))
    first = after(first, *at_end, swapped[1])
    first = gather_rows(jnp.concatenate([first, other_far], axis=1), order)

    pushed, kept_swapped, swapped_square = [], [], []
    for pile, here in (
        (swapped[:2], slice(0, width // 2)), (swapped[2:], slice(width // 2, width))
    ):
        a, b, c = kernel_call(
            middle_kernel,
            [((rows, width // 2), jnp.bfloat16), ((1, width // 2), jnp.float32),
             ((rows, width // 2), jnp.bfloat16)],
            flops=one_gram,
        )(first, own[:, here], near[:, here], own_square[:, here], mean[:, here], *pile)
        kept_swapped.append(a)
        swapped_square.append(b)
        pushed.append(lax.ppermute(c, "dp", outward))

    wide = 2 * rows + NORM
    end, end_square, kept, sent = kernel_call(
        second_kernel,
        [block, flat, ((half, wide), jnp.float32), ((half, wide), jnp.bfloat16)],
        flops=one_gram, smem=1,
    )(middle, turned, *at_end, *kept_swapped, mean, own_kept, own_sent)
    second = after(scatter_sum(kept, sent, 2 * rows), pushed[0])
    second = gather_rows(second, order)

    tile = width // 4
    whole = lambda n: pl.BlockSpec((rows, n), lambda j: (0, 0))
    strip = pl.BlockSpec((rows, tile), lambda j: (0, j))
    line = pl.BlockSpec((1, tile), lambda j: (0, j))
    return pl.pallas_call(
        functools.partial(last_kernel, total),
        grid=(4,),
        out_shape=jax.ShapeDtypeStruct((rows, width), jnp.float32),
        in_specs=[pl.BlockSpec(memory_space=pltpu.SMEM), whole(3 * rows), whole(wide)]
        + [strip] * 8 + [line] * 7,
        out_specs=strip,
        compiler_params=VMEM,
        cost_estimate=pl.CostEstimate(
            flops=4 * one_gram, bytes_accessed=14 * rows * width, transcendentals=0
        ),
    )(
        middle, first, second, own, near, far, end, jnp.concatenate(kept_swapped, axis=1),
        jnp.concatenate(pushed, axis=1), z_anchor, z_other, own_square, near_square, far_square,
        end_square, jnp.concatenate(swapped_square, axis=1), mean, spread,
    )


def by_gather(z_anchor, z_other):
    rows_here, width = z_anchor.shape
    groups = lax.axis_size("dp")
    total = rows_here * groups
    mine = lax.axis_index("dp") * rows_here
    column = lax.all_gather(z_anchor, "dp", axis=0, tiled=True).astype(jnp.float32)
    mean = jnp.sum(column, axis=0) / total
    centered_all = column - mean
    variance = jnp.sum(centered_all * centered_all, axis=0) / (total - 1)
    rounded_all = centered_all.astype(jnp.bfloat16)
    widened = rounded_all.astype(jnp.float32)
    own_square = jnp.sum(widened * widened, axis=0)
    rounded = lax.dynamic_slice_in_dim(rounded_all, mine, rows_here, 0)
    inner = lax.psum(gram(rounded, rounded_all).astype(jnp.bfloat16), "feat")
    product = jnp.dot(inner, rounded_all, preferred_element_type=jnp.float32)
    product = product - rounded.astype(jnp.float32) * own_square
    return finish(z_anchor, z_other, mean, variance, total, product)


def finish(z_anchor, z_other, mean, variance, total, product):
    coef = 2.0 * total / (25.0 * (total - 1)) / (total - 1)
    anchor = z_anchor.astype(jnp.float32)
    centered = anchor - mean
    deviation = jnp.sqrt(variance + 0.0001)
    hinge = jnp.where(deviation < 1.0, centered / deviation, 0.0)
    factor = total / (4.0 * (total - 1))
    return anchor - z_other.astype(jnp.float32) - factor * hinge + coef * product


def solution(mesh):
    placed = (P("dp", "feat"), P("dp", "feat"))
    in_line = mesh.shape["dp"] == 4 and mesh.shape["feat"] == 8
    return jax.shard_map(
        by_line if in_line else by_gather,
        mesh=mesh, in_specs=placed, out_specs=P("dp", "feat"), check_vma=False,
    )
```

time: 177 us -> 150 us (0.85)
  waiting for transfers between devices: 143 us -> 65.2 us
  starting transfers between devices: 0.04 us -> 51.2 us
  Pallas kernels: 0 us -> 15.3 us
  between operations: 13.4 us -> 0.57 us
  matrix products: 11 us -> 0 us
  local copies, waits for them, and re-layouts: 2.33 us -> 12.8 us
  other arithmetic: 4.61 us -> 2.09 us
    all_gather x1 -> x0, waiting for transfers between devices: 81.1 us -> none  [per_device(): lax.all_gather(z_anchor, 'dp', axis=0, tiled=True).astype(jnp.float32)]
    ppermute x0 -> x34, waiting for transfers between devices: none -> 65.2 us  [the longest x16 25.8 us: to_partner(): return lax.ppermute(x, 'feat', [(i, i ^ step) for i in range(8)])]
    psum x1 -> x0, waiting for transfers between devices: 61.5 us -> none  [per_device(): inner = lax.psum(part.astype(jnp.bfloat16), 'feat')]
    ppermute x0 -> x34, starting transfers between devices: none -> 51.2 us  [the longest x16 17.8 us: to_partner(): return lax.ppermute(x, 'feat', [(i, i ^ step) for i in range(8)])]
    pallas_call x0 -> x12, Pallas kernels: none -> 15.3 us  [the longest x11 8.6 us: call(): pl.pallas_call(body, out_shape=[jax.ShapeDtypeStruct(s, t) for s, t in ou...]
    dot_general x2 -> x0, matrix products: 11 us -> none  [the longest x1 7.27 us: per_device(): product = jnp.dot(inner, rounded_all, preferred_element_type=jnp.float32)]
    unnamed x8 -> x56, local copies, waits for them, and re-layouts: 2.33 us -> 8.11 us
    reduce_sum x2, other arithmetic: 4.59 us -> 0.5 us  [the longest x1 0.31 us: by_line(): jnp.sum(apart * apart, axis=0, keepdims=True)]
  transfers between devices with their start and end apart: 2 -> 34, of which waited for: 2 -> 22; matrix products, arithmetic and copies ran while one was open for 0% -> 3% of each run, Pallas kernels for 0% -> 3%
where the time goes in v4:
time: 150 us; the launch traced here: 147 us
  waiting for transfers between devices  65.2 us (43%)
  starting transfers between devices  51.2 us (34%)
  Pallas kernels  15.3 us (10%)
  local copies, waits for them, and re-layouts  12.8 us (9%)
  other arithmetic  2.09 us (1%)
    ppermute x16, waiting for transfers between devices, to_partner(): return lax.ppermute(x, 'feat', [(i, i ^ step) for i in range(8)])  25.8 us
    ppermute x16, starting transfers between devices, to_partner(): return lax.ppermute(x, 'feat', [(i, i ^ step) for i in range(8)])  17.8 us
    ppermute x1, waiting for transfers between devices, by_line(): swapped.append(lax.ppermute(after(swaps[2], first), 'dp', across))  11.1 us
    ppermute x2, waiting for transfers between devices, by_line(): lax.ppermute(after(piece, swapped[0], *all_stats[1:]), 'dp', inward)  11.1 us
    pallas_call x11, Pallas kernels, call(): pl.pallas_call(body, out_shape=[jax.ShapeDtypeStruct(s, t) for s, t in ou...  8.6 us
    unnamed x56, local copies, waits for them, and re-layouts  8.11 us
    ppermute x3, starting transfers between devices, by_line(): crossed = [lax.ppermute(x, 'dp', across) for x in near]  7.9 us
    pallas_call x1, Pallas kernels, by_line(): pl.pallas_call(functools.partial(last_kernel, total), grid=(4,), out_shap...  6.68 us
  transfers between devices with their start and end apart: 34, of which 22 were waited for; matrix products, arithmetic and copies ran while one was open for 3% of the time, Pallas kernels for 3%

profile of v4, /device:TPU:9, one launch (start us, length us, event | category | flops | bytes accessed | tf_op | source)
XLA Modules:
  0.0 147.2 jit_solution(9738856117288998)
XLA Ops:
  0.0 1.9 %fusion.11 = (bf16[512,256]{1,0:T(8,128)(2,1)}, bf16[512,256]{1,0:T(8,128)(2,1)S(1)}) fusion(bf16[512,1024]{1,0:T(8,128)(2,1)} %z.2), kind=kLoop, calls=%fused_computation.31 | loop fusion | bytes 1048576 | tf_op jit(solution)/shard_map/slice | solution.py:251
  1.9 3.3 %collective-permute-start = (bf16[512,256]{1,0:T(8,128)(2,1)S(1)}, bf16[512,256]{1,0:T(8,128)(2,1)S(1)}, u32[]{:S(2)}, u32[]{:S(2)}) collective-permute-start(bf16[512,256]{1,0:T(8,128)(2,1)S(1)} %get-tuple-element.88), channel_id=1, source_target_pairs={{8,16},{16,8},{9,17},{17,9},{10,18},{18,10},{11,19},{19,11},{12,20... | collective-permute-start | bytes 786440 | tf_op jit(solution)/shard_map/ppermute | solution.py:261
  8.2 2.2 %collective-permute-start.3 = (f32[2,1024]{1,0:T(2,128)S(1)}, f32[2,1024]{1,0:T(2,128)S(1)}, u32[]{:S(2)}, u32[]{:S(2)}) collective-permute-start(f32[2,1024]{1,0:T(2,128)S(1)} %pad_maximum_fusion.3), channel_id=1, source_target_pairs={{0,24},{8,0},{16,8},{24,16},{1,25},{9,1},{17,9},{25,17},{2,26},{10... | collective-permute-start | bytes 24584 | tf_op jit(solution)/shard_map/ppermute | solution.py:259
  10.4 2.2 %collective-permute-start.1 = (f32[2,1024]{1,0:T(2,128)S(1)}, f32[2,1024]{1,0:T(2,128)S(1)}, u32[]{:S(2)}, u32[]{:S(2)}) collective-permute-start(f32[2,1024]{1,0:T(2,128)S(1)} %pad_maximum_fusion.3), channel_id=1, source_target_pairs={{0,8},{8,16},{16,24},{24,0},{1,9},{9,17},{17,25},{25,1},{2,10},{10... | collective-permute-start | bytes 24584 | tf_op jit(solution)/shard_map/ppermute | solution.py:259
  12.6 5.3 %collective-permute-done.2 = f32[2,1024]{1,0:T(2,128)S(1)} collective-permute-done((f32[2,1024]{1,0:T(2,128)S(1)}, f32[2,1024]{1,0:T(2,128)S(1)}, u32[]{:S(2)}, u32[]{:S(2)}) %collective-permute-start.2) | collective-permute-done | bytes 8224 | tf_op jit(solution)/shard_map/ppermute | solution.py:259
  20.5 2.6 %collective-permute-start.5 = (bf16[192,1024]{1,0:T(8,128)(2,1)S(1)}, bf16[192,1024]{1,0:T(8,128)(2,1)}, u32[]{:S(2)}, u32[]{:S(2)}) collective-permute-start(bf16[192,1024]{1,0:T(8,128)(2,1)S(1)} %collective-permute-done.4.refs_0_), channel_id=1, source_target_pairs={{8,16},{16,8},{9,17},{17,9},{10,18},{18,10},{11,19},{19,11},{12,20... | collective-permute-start | bytes 1179656 | tf_op jit(solution)/shard_map/ppermute | solution.py:277
  24.4 11.1 %collective-permute-done.8.refs_2_ = bf16[128,1024]{1,0:T(8,128)(2,1)} collective-permute-done((bf16[128,1024]{1,0:T(8,128)(2,1)S(1)}, bf16[128,1024]{1,0:T(8,128)(2,1)}, u32[]{:S(2)}, u32[]{:S(2)}) %collective-permute-start.8) | collective-permute-done | bytes 262176 | tf_op jit(solution)/shard_map/ppermute | solution.py:263
  35.5 2.2 %collective-permute-start.10 = (bf16[128,1024]{1,0:T(8,128)(2,1)}, bf16[128,1024]{1,0:T(8,128)(2,1)S(1)}, u32[]{:S(2)}, u32[]{:S(2)}) collective-permute-start(bf16[128,1024]{1,0:T(8,128)(2,1)} %collective-permute-done.8.refs_2_), channel_id=1, source_target_pairs={{8,16},{16,8},{9,17},{17,9},{10,18},{18,10},{11,19},{19,11},{12,20... | collective-permute-start | bytes 786440 | tf_op jit(solution)/shard_map/ppermute | solution.py:277
  37.8 3.0 %collective-permute-start.9 = (bf16[192,1024]{1,0:T(8,128)(2,1)}, bf16[192,1024]{1,0:T(8,128)(2,1)S(1)}, u32[]{:S(2)}, u32[]{:S(2)}) collective-permute-start(bf16[192,1024]{1,0:T(8,128)(2,1)} %collective-permute-done.7.refs_1_), channel_id=1, source_target_pairs={{8,16},{16,8},{9,17},{17,9},{10,18},{18,10},{11,19},{19,11},{12,20... | collective-permute-start | bytes 1179656 | tf_op jit(solution)/shard_map/ppermute | solution.py:277
  40.8 1.3 collective-permute-start.6
  42.2 2.0 %shard_map.37 = (bf16[512,1024]{1,0:T(8,128)(2,1)S(1)}, bf16[512,1024]{1,0:T(8,128)(2,1)S(1)}, f32[1,1024]{1,0:T(1,128)S(1)}, f32[256,640]{1,0:T(8,128)S(1)}, bf16[256,640]{1,0:T(8,128)(2,1)S(1)}) custom-call(s32[8]{0:T(128)S(1)} %broadcast_xor_fusion.order, bf16[512,1024]{1,0:T(8,128)(2,1)S(1)} %copy-done, f32[1,1024]{1,0:T(1,128)S(1)} %get-tuple-element.82.mean.refs_6_.refs_5_), custom_call_target="tpu_custom_call" | custom-call | tf_op jit(solution)/shard_map/pallas_call | solution.py:20
  45.8 2.0 %collective-permute-done.6.refs_0_ = bf16[192,1024]{1,0:T(8,128)(2,1)S(1)} collective-permute-done((bf16[192,1024]{1,0:T(8,128)(2,1)}, bf16[192,1024]{1,0:T(8,128)(2,1)S(1)}, u32[]{:S(2)}, u32[]{:S(2)}) %collective-permute-start.6) | collective-permute-done | bytes 393248 | tf_op jit(solution)/shard_map/ppermute | solution.py:278
  47.8 3.3 %collective-permute-done.9.refs_4_ = bf16[192,1024]{1,0:T(8,128)(2,1)S(1)} collective-permute-done((bf16[192,1024]{1,0:T(8,128)(2,1)}, bf16[192,1024]{1,0:T(8,128)(2,1)S(1)}, u32[]{:S(2)}, u32[]{:S(2)}) %collective-permute-start.9) | collective-permute-done | bytes 393248 | tf_op jit(solution)/shard_map/ppermute | solution.py:277
  52.0 2.6 %shard_map.38 = (bf16[512,1024]{1,0:T(8,128)(2,1)S(1)}, bf16[512,1024]{1,0:T(8,128)(2,1)S(1)}, f32[1,1024]{1,0:T(1,128)S(1)}, f32[1,1024]{1,0:T(1,128)S(1)}, f32...) custom-call(bf16[512,1024]{1,0:T(8,128)(2,1)S(1)} %get-tuple-element.45.turned, bf16[192,1024]{1,0:T(8,128)(2,1)S(1)} %copy-done.11, ...), custom_call_target="tpu_custom_call" | custom-call | tf_op jit(solution)/shard_map/pallas_call | solution.py:20
  56.2 3.7 %collective-permute-start.11 = (bf16[256,1024]{1,0:T(8,128)(2,1)S(1)}, bf16[256,1024]{1,0:T(8,128)(2,1)S(1)}, u32[]{:S(2)}, u32[]{:S(2)}) collective-permute-start(bf16[256,1024]{1,0:T(8,128)(2,1)S(1)} %get-tuple-element.50), channel_id=1, source_target_pairs={{0,1},{1,0},{2,3},{3,2},{4,5},{5,4},{6,7},{7,6},{8,9},{9,8},{10,11... | collective-permute-start | bytes 1572872 | tf_op jit(solution)/shard_map/ppermute | solution.py:210
  62.8 2.5 %collective-permute-start.17 = (bf16[512,256]{1,0:T(8,128)(2,1)S(1)}, bf16[512,256]{1,0:T(8,128)(2,1)S(1)}, u32[]{:S(2)}, u32[]{:S(2)}) collective-permute-start(bf16[512,256]{1,0:T(8,128)(2,1)S(1)} %copy-done.24), channel_id=1, source_target_pairs={{8,16},{16,8},{9,17},{17,9},{10,18},{18,10},{11,19},{19,11},{12,20... | collective-permute-start | bytes 786440 | tf_op jit(solution)/shard_map/ppermute | solution.py:279
  68.5 2.3 %collective-permute-done.13.b = bf16[64,1024]{1,0:T(8,128)(2,1)S(1)} collective-permute-done((bf16[64,1024]{1,0:T(8,128)(2,1)S(1)}, bf16[64,1024]{1,0:T(8,128)(2,1)S(1)}, u32[]{:S(2)}, u32[]{:S(2)}) %collective-permute-start.13) | collective-permute-done | bytes 131104 | tf_op jit(solution)/shard_map/ppermute | solution.py:210
  70.8 1.9 %collective-permute-done.14.c = bf16[64,1024]{1,0:T(8,128)(2,1)S(1)} collective-permute-done((bf16[64,1024]{1,0:T(8,128)(2,1)S(1)}, bf16[64,1024]{1,0:T(8,128)(2,1)S(1)}, u32[]{:S(2)}, u32[]{:S(2)}) %collective-permute-start.14) | collective-permute-done | bytes 131104 | tf_op jit(solution)/shard_map/ppermute | solution.py:210
  73.5 2.0 %collective-permute-done.16.refs_2_ = bf16[128,1024]{1,0:T(8,128)(2,1)S(1)} collective-permute-done((bf16[128,1024]{1,0:T(8,128)(2,1)S(1)}, bf16[128,1024]{1,0:T(8,128)(2,1)S(1)}, u32[]{:S(2)}, u32[]{:S(2)}) %collective-permute-start.16) | collective-permute-done | bytes 262176 | tf_op jit(solution)/shard_map/ppermute | solution.py:278
  77.0 2.5 %collective-permute-start.18 = (bf16[64,512]{1,0:T(8,128)(2,1)S(1)}, bf16[64,512]{1,0:T(8,128)(2,1)S(1)}, u32[]{:S(2)}, u32[]{:S(2)}) collective-permute-start(bf16[64,512]{1,0:T(8,128)(2,1)S(1)} %slice.90), channel_id=1, source_target_pairs={{8,16},{16,8},{9,17},{17,9},{10,18},{18,10},{11,19},{19,11},{12,20... | collective-permute-start | bytes 196616 | tf_op jit(solution)/shard_map/ppermute | solution.py:287
  80.1 1.8 %collective-permute-done.18 = bf16[64,512]{1,0:T(8,128)(2,1)S(1)} collective-permute-done((bf16[64,512]{1,0:T(8,128)(2,1)S(1)}, bf16[64,512]{1,0:T(8,128)(2,1)S(1)}, u32[]{:S(2)}, u32[]{:S(2)}) %collective-permute-start.18) | collective-permute-done | bytes 65568 | tf_op jit(solution)/shard_map/ppermute | solution.py:287
  82.6 2.2 %collective-permute-start.21 = (bf16[64,1536]{1,0:T(8,128)(2,1)}, bf16[64,1536]{1,0:T(8,128)(2,1)}, u32[]{:S(2)}, u32[]{:S(2)}) collective-permute-start(bf16[64,1536]{1,0:T(8,128)(2,1)} %constant_dynamic-update-slice_fusion), channel_id=1, source_target_pairs={{0,6},{1,7},{2,4},{3,5},{4,2},{5,3},{6,0},{7,1},{8,14},{9,15},{10,... | collective-permute-start | bytes 589832 | tf_op jit(solution)/shard_map/ppermute | solution.py:210
  86.1 2.3 %collective-permute-done.21 = bf16[64,1536]{1,0:T(8,128)(2,1)} collective-permute-done((bf16[64,1536]{1,0:T(8,128)(2,1)}, bf16[64,1536]{1,0:T(8,128)(2,1)}, u32[]{:S(2)}, u32[]{:S(2)}) %collective-permute-start.21) | collective-permute-done | bytes 196640 | tf_op jit(solution)/shard_map/ppermute | solution.py:210
  88.4 5.6 %collective-permute-done.20 = bf16[64,1536]{1,0:T(8,128)(2,1)} collective-permute-done((bf16[64,1536]{1,0:T(8,128)(2,1)}, bf16[64,1536]{1,0:T(8,128)(2,1)}, u32[]{:S(2)}, u32[]{:S(2)}) %collective-permute-start.20) | collective-permute-done | bytes 196640 | tf_op jit(solution)/shard_map/ppermute | solution.py:210
  95.4 1.4 collective-permute-start.22
  96.8 2.5 %collective-permute-start.23 = (bf16[512,512]{1,0:T(8,128)(2,1)}, bf16[512,512]{1,0:T(8,128)(2,1)S(1)}, u32[]{:S(2)}, u32[]{:S(2)}) collective-permute-start(bf16[512,512]{1,0:T(8,128)(2,1)} %slice.83), channel_id=1, source_target_pairs={{8,16},{16,8},{9,17},{17,9},{10,18},{18,10},{11,19},{19,11},{12,20... | collective-permute-start | bytes 1572872 | tf_op jit(solution)/shard_map/ppermute | solution.py:288
  101.3 11.1 %collective-permute-done.23.refs_0_ = bf16[512,512]{1,0:T(8,128)(2,1)S(1)} collective-permute-done((bf16[512,512]{1,0:T(8,128)(2,1)}, bf16[512,512]{1,0:T(8,128)(2,1)S(1)}, u32[]{:S(2)}, u32[]{:S(2)}) %collective-permute-start.23) | collective-permute-done | bytes 524320 | tf_op jit(solution)/shard_map/ppermute | solution.py:288
  122.8 3.2 %collective-permute-done.27.c = bf16[64,1152]{1,0:T(8,128)(2,1)S(1)} collective-permute-done((bf16[64,1152]{1,0:T(8,128)(2,1)S(1)}, bf16[64,1152]{1,0:T(8,128)(2,1)S(1)}, u32[]{:S(2)}, u32[]{:S(2)}) %collective-permute-start.27) | collective-permute-done | bytes 147488 | tf_op jit(solution)/shard_map/ppermute | solution.py:210
  126.1 1.6 %collective-permute-done.28 = bf16[512,512]{1,0:T(8,128)(2,1)S(1)} collective-permute-done((bf16[512,512]{1,0:T(8,128)(2,1)S(1)}, bf16[512,512]{1,0:T(8,128)(2,1)S(1)}, u32[]{:S(2)}, u32[]{:S(2)}) %collective-permute-start.28) | collective-permute-done | bytes 524320 | tf_op jit(solution)/shard_map/ppermute | solution.py:304
  127.7 1.4 collective-permute-start.31
  130.4 5.9 %collective-permute-done.29 = bf16[64,1152]{1,0:T(8,128)(2,1)S(1)} collective-permute-done((bf16[64,1152]{1,0:T(8,128)(2,1)S(1)}, bf16[64,1152]{1,0:T(8,128)(2,1)S(1)}, u32[]{:S(2)}, u32[]{:S(2)}) %collective-permute-start.29) | collective-permute-done | bytes 147488 | tf_op jit(solution)/shard_map/ppermute | solution.py:210
  140.5 6.7 %shard_map.48 = f32[512,1024]{1,0:T(8,128)} custom-call(s32[1]{0:T(128)} %bitcast.middle, bf16[512,1536]{1,0:T(8,128)(2,1)S(1)} %shard_map.41.inner.first, bf16[512,1152]{1,0:T(8,128)(2,1)S(1)} %shard_map.47.second, bf16[512,1024]{1,0:T(8,128)(2,1)S(1)} %get-tuple-element.57.own, bf16[512,1024]{1,0:T(8,128)(2,1)S(1)} %copy-done.2, ...), custom_call_target="tpu_custom_call" | custom-call | flops 2147483648 | bytes 7340032 | tf_op jit(solution)/shard_map/pallas_call | solution.py:319
  (125 shorter events, 41.0 us)
Async XLA Ops:
  1.9 16.6 %collective-permute-start = (bf16[512,256]{1,0:T(8,128)(2,1)S(1)}, bf16[512,256]{1,0:T(8,128)(2,1)S(1)}, u32[]{:S(2)}, u32[]{:S(2)}) collective-permute-start(bf16[512,256]{1,0:T(8,128)(2,1)S(1)} %get-tuple-element.88), channel_id=1, source_target_pairs={{8,16},{16,8},{9,17},{17,9},{10,18},{18,10},{11,19},{19,11},{12,20... | collective-permute-start | bytes 786440 | tf_op jit(solution)/shard_map/ppermute | solution.py:261
  6.4 14.1 %collective-permute-start.4 = (bf16[192,1024]{1,0:T(8,128)(2,1)S(1)}, bf16[192,1024]{1,0:T(8,128)(2,1)S(1)}, u32[]{:S(2)}, u32[]{:S(2)}) collective-permute-start(bf16[192,1024]{1,0:T(8,128)(2,1)S(1)} %get-tuple-element.90), channel_id=1, source_target_pairs={{0,8},{24,16},{1,9},{25,17},{2,10},{26,18},{3,11},{27,19},{4,12},{... | collective-permute-start | bytes 1179656 | tf_op jit(solution)/shard_map/ppermute | solution.py:253
  8.2 4.4 %collective-permute-start.3 = (f32[2,1024]{1,0:T(2,128)S(1)}, f32[2,1024]{1,0:T(2,128)S(1)}, u32[]{:S(2)}, u32[]{:S(2)}) collective-permute-start(f32[2,1024]{1,0:T(2,128)S(1)} %pad_maximum_fusion.3), channel_id=1, source_target_pairs={{0,24},{8,0},{16,8},{24,16},{1,25},{9,1},{17,9},{25,17},{2,26},{10... | collective-permute-start | bytes 24584 | tf_op jit(solution)/shard_map/ppermute | solution.py:259
  10.4 7.5 %collective-permute-start.2 = (f32[2,1024]{1,0:T(2,128)S(1)}, f32[2,1024]{1,0:T(2,128)S(1)}, u32[]{:S(2)}, u32[]{:S(2)}) collective-permute-start(f32[2,1024]{1,0:T(2,128)S(1)} %pad_maximum_fusion.3), channel_id=1, source_target_pairs={{0,16},{8,24},{16,0},{24,8},{1,17},{9,25},{17,1},{25,9},{2,18},{10... | collective-permute-start | bytes 24584 | tf_op jit(solution)/shard_map/ppermute | solution.py:259
  10.4 8.1 %collective-permute-start.1 = (f32[2,1024]{1,0:T(2,128)S(1)}, f32[2,1024]{1,0:T(2,128)S(1)}, u32[]{:S(2)}, u32[]{:S(2)}) collective-permute-start(f32[2,1024]{1,0:T(2,128)S(1)} %pad_maximum_fusion.3), channel_id=1, source_target_pairs={{0,8},{8,16},{16,24},{24,0},{1,9},{9,17},{17,25},{25,1},{2,10},{10... | collective-permute-start | bytes 24584 | tf_op jit(solution)/shard_map/ppermute | solution.py:259
  19.2 16.4 %collective-permute-start.7 = (bf16[192,1024]{1,0:T(8,128)(2,1)S(1)}, bf16[192,1024]{1,0:T(8,128)(2,1)}, u32[]{:S(2)}, u32[]{:S(2)}) collective-permute-start(bf16[192,1024]{1,0:T(8,128)(2,1)S(1)} %get-tuple-element.46), channel_id=1, source_target_pairs={{0,8},{24,16},{1,9},{25,17},{2,10},{26,18},{3,11},{27,19},{4,12},{... | collective-permute-start | bytes 1179656 | tf_op jit(solution)/shard_map/ppermute | solution.py:263
  20.5 20.3 %collective-permute-start.5 = (bf16[192,1024]{1,0:T(8,128)(2,1)S(1)}, bf16[192,1024]{1,0:T(8,128)(2,1)}, u32[]{:S(2)}, u32[]{:S(2)}) collective-permute-start(bf16[192,1024]{1,0:T(8,128)(2,1)S(1)} %collective-permute-done.4.refs_0_), channel_id=1, source_target_pairs={{8,16},{16,8},{9,17},{17,9},{10,18},{18,10},{11,19},{19,11},{12,20... | collective-permute-start | bytes 1179656 | tf_op jit(solution)/shard_map/ppermute | solution.py:277
  23.1 12.4 %collective-permute-start.8 = (bf16[128,1024]{1,0:T(8,128)(2,1)S(1)}, bf16[128,1024]{1,0:T(8,128)(2,1)}, u32[]{:S(2)}, u32[]{:S(2)}) collective-permute-start(bf16[128,1024]{1,0:T(8,128)(2,1)S(1)} %slice.72), channel_id=1, source_target_pairs={{0,8},{24,16},{1,9},{25,17},{2,10},{26,18},{3,11},{27,19},{4,12},{... | collective-permute-start | bytes 786440 | tf_op jit(solution)/shard_map/ppermute | solution.py:263
  35.5 12.2 %collective-permute-start.10 = (bf16[128,1024]{1,0:T(8,128)(2,1)}, bf16[128,1024]{1,0:T(8,128)(2,1)S(1)}, u32[]{:S(2)}, u32[]{:S(2)}) collective-permute-start(bf16[128,1024]{1,0:T(8,128)(2,1)} %collective-permute-done.8.refs_2_), channel_id=1, source_target_pairs={{8,16},{16,8},{9,17},{17,9},{10,18},{18,10},{11,19},{19,11},{12,20... | collective-permute-start | bytes 786440 | tf_op jit(solution)/shard_map/ppermute | solution.py:277
  37.8 13.3 %collective-permute-start.9 = (bf16[192,1024]{1,0:T(8,128)(2,1)}, bf16[192,1024]{1,0:T(8,128)(2,1)S(1)}, u32[]{:S(2)}, u32[]{:S(2)}) collective-permute-start(bf16[192,1024]{1,0:T(8,128)(2,1)} %collective-permute-done.7.refs_1_), channel_id=1, source_target_pairs={{8,16},{16,8},{9,17},{17,9},{10,18},{18,10},{11,19},{19,11},{12,20... | collective-permute-start | bytes 1179656 | tf_op jit(solution)/shard_map/ppermute | solution.py:277
  40.8 6.9 %collective-permute-start.6 = (bf16[192,1024]{1,0:T(8,128)(2,1)}, bf16[192,1024]{1,0:T(8,128)(2,1)S(1)}, u32[]{:S(2)}, u32[]{:S(2)}) collective-permute-start(bf16[192,1024]{1,0:T(8,128)(2,1)} %collective-permute-done.5.refs_3_), channel_id=1, source_target_pairs={{8,0},{16,24},{9,1},{17,25},{10,2},{18,26},{11,3},{19,27},{12,4},{... | collective-permute-start | bytes 1179656 | tf_op jit(solution)/shard_map/ppermute | solution.py:278
  56.2 5.2 %collective-permute-start.11 = (bf16[256,1024]{1,0:T(8,128)(2,1)S(1)}, bf16[256,1024]{1,0:T(8,128)(2,1)S(1)}, u32[]{:S(2)}, u32[]{:S(2)}) collective-permute-start(bf16[256,1024]{1,0:T(8,128)(2,1)S(1)} %get-tuple-element.50), channel_id=1, source_target_pairs={{0,1},{1,0},{2,3},{3,2},{4,5},{5,4},{6,7},{7,6},{8,9},{9,8},{10,11... | collective-permute-start | bytes 1572872 | tf_op jit(solution)/shard_map/ppermute | solution.py:210
  59.9 16.3 %collective-permute-start.15 = (bf16[192,1024]{1,0:T(8,128)(2,1)S(1)}, bf16[192,1024]{1,0:T(8,128)(2,1)S(1)}, u32[]{:S(2)}, u32[]{:S(2)}) collective-permute-start(bf16[192,1024]{1,0:T(8,128)(2,1)S(1)} %collective-permute-done.9.refs_4_), channel_id=1, source_target_pairs={{8,0},{16,24},{9,1},{17,25},{10,2},{18,26},{11,3},{19,27},{12,4},{... | collective-permute-start | bytes 1179656 | tf_op jit(solution)/shard_map/ppermute | solution.py:278
  61.5 6.4 %collective-permute-start.12 = (bf16[64,1024]{1,0:T(8,128)(2,1)S(1)}, bf16[64,1024]{1,0:T(8,128)(2,1)S(1)}, u32[]{:S(2)}, u32[]{:S(2)}) collective-permute-start(bf16[64,1024]{1,0:T(8,128)(2,1)S(1)} %get-tuple-element.52), channel_id=1, source_target_pairs={{0,2},{1,3},{2,0},{3,1},{4,6},{5,7},{6,4},{7,5},{8,10},{9,11},{10,... | collective-permute-start | bytes 393224 | tf_op jit(solution)/shard_map/ppermute | solution.py:210
  62.8 10.0 %collective-permute-start.17 = (bf16[512,256]{1,0:T(8,128)(2,1)S(1)}, bf16[512,256]{1,0:T(8,128)(2,1)S(1)}, u32[]{:S(2)}, u32[]{:S(2)}) collective-permute-start(bf16[512,256]{1,0:T(8,128)(2,1)S(1)} %copy-done.24), channel_id=1, source_target_pairs={{8,16},{16,8},{9,17},{17,9},{10,18},{18,10},{11,19},{19,11},{12,20... | collective-permute-start | bytes 786440 | tf_op jit(solution)/shard_map/ppermute | solution.py:279
  65.3 10.2 %collective-permute-start.16 = (bf16[128,1024]{1,0:T(8,128)(2,1)S(1)}, bf16[128,1024]{1,0:T(8,128)(2,1)S(1)}, u32[]{:S(2)}, u32[]{:S(2)}) collective-permute-start(bf16[128,1024]{1,0:T(8,128)(2,1)S(1)} %collective-permute-done.10.refs_5_), channel_id=1, source_target_pairs={{8,0},{16,24},{9,1},{17,25},{10,2},{18,26},{11,3},{19,27},{12,4},{... | collective-permute-start | bytes 786440 | tf_op jit(solution)/shard_map/ppermute | solution.py:278
  66.6 4.2 %collective-permute-start.13 = (bf16[64,1024]{1,0:T(8,128)(2,1)S(1)}, bf16[64,1024]{1,0:T(8,128)(2,1)S(1)}, u32[]{:S(2)}, u32[]{:S(2)}) collective-permute-start(bf16[64,1024]{1,0:T(8,128)(2,1)S(1)} %get-tuple-element.53), channel_id=1, source_target_pairs={{0,4},{1,5},{2,6},{3,7},{4,0},{5,1},{6,2},{7,3},{8,12},{9,13},{10,... | collective-permute-start | bytes 393224 | tf_op jit(solution)/shard_map/ppermute | solution.py:210
  67.9 4.8 %collective-permute-start.14 = (bf16[64,1024]{1,0:T(8,128)(2,1)S(1)}, bf16[64,1024]{1,0:T(8,128)(2,1)S(1)}, u32[]{:S(2)}, u32[]{:S(2)}) collective-permute-start(bf16[64,1024]{1,0:T(8,128)(2,1)S(1)} %get-tuple-element.54), channel_id=1, source_target_pairs={{0,6},{1,7},{2,4},{3,5},{4,2},{5,3},{6,0},{7,1},{8,14},{9,15},{10,... | collective-permute-start | bytes 393224 | tf_op jit(solution)/shard_map/ppermute | solution.py:210
  77.0 5.0 %collective-permute-start.18 = (bf16[64,512]{1,0:T(8,128)(2,1)S(1)}, bf16[64,512]{1,0:T(8,128)(2,1)S(1)}, u32[]{:S(2)}, u32[]{:S(2)}) collective-permute-start(bf16[64,512]{1,0:T(8,128)(2,1)S(1)} %slice.90), channel_id=1, source_target_pairs={{8,16},{16,8},{9,17},{17,9},{10,18},{18,10},{11,19},{19,11},{12,20... | collective-permute-start | bytes 196616 | tf_op jit(solution)/shard_map/ppermute | solution.py:287
  82.6 5.8 %collective-permute-start.21 = (bf16[64,1536]{1,0:T(8,128)(2,1)}, bf16[64,1536]{1,0:T(8,128)(2,1)}, u32[]{:S(2)}, u32[]{:S(2)}) collective-permute-start(bf16[64,1536]{1,0:T(8,128)(2,1)} %constant_dynamic-update-slice_fusion), channel_id=1, source_target_pairs={{0,6},{1,7},{2,4},{3,5},{4,2},{5,3},{6,0},{7,1},{8,14},{9,15},{10,... | collective-permute-start | bytes 589832 | tf_op jit(solution)/shard_map/ppermute | solution.py:210
  84.8 9.3 %collective-permute-start.20 = (bf16[64,1536]{1,0:T(8,128)(2,1)}, bf16[64,1536]{1,0:T(8,128)(2,1)}, u32[]{:S(2)}, u32[]{:S(2)}) collective-permute-start(bf16[64,1536]{1,0:T(8,128)(2,1)} %constant_dynamic-update-slice_fusion), channel_id=1, source_target_pairs={{0,4},{1,5},{2,6},{3,7},{4,0},{5,1},{6,2},{7,3},{8,12},{9,13},{10,... | collective-permute-start | bytes 589832 | tf_op jit(solution)/shard_map/ppermute | solution.py:210
  85.0 9.1 %collective-permute-start.19 = (bf16[64,1536]{1,0:T(8,128)(2,1)}, bf16[64,1536]{1,0:T(8,128)(2,1)}, u32[]{:S(2)}, u32[]{:S(2)}) collective-permute-start(bf16[64,1536]{1,0:T(8,128)(2,1)} %constant_dynamic-update-slice_fusion), channel_id=1, source_target_pairs={{0,2},{1,3},{2,0},{3,1},{4,6},{5,7},{6,4},{7,5},{8,10},{9,11},{10,... | collective-permute-start | bytes 589832 | tf_op jit(solution)/shard_map/ppermute | solution.py:210
  95.4 4.1 %collective-permute-start.22 = (bf16[256,1536]{1,0:T(8,128)(2,1)S(1)}, bf16[256,1536]{1,0:T(8,128)(2,1)S(1)}, u32[]{:S(2)}, u32[]{:S(2)}) collective-permute-start(bf16[256,1536]{1,0:T(8,128)(2,1)S(1)} %pad_maximum_fusion.2.near), channel_id=1, source_target_pairs={{0,1},{1,0},{2,3},{3,2},{4,5},{5,4},{6,7},{7,6},{8,9},{9,8},{10,11... | collective-permute-start | bytes 2359304 | tf_op jit(solution)/shard_map/ppermute | solution.py:210
  96.8 15.6 %collective-permute-start.23 = (bf16[512,512]{1,0:T(8,128)(2,1)}, bf16[512,512]{1,0:T(8,128)(2,1)S(1)}, u32[]{:S(2)}, u32[]{:S(2)}) collective-permute-start(bf16[512,512]{1,0:T(8,128)(2,1)} %slice.83), channel_id=1, source_target_pairs={{8,16},{16,8},{9,17},{17,9},{10,18},{18,10},{11,19},{19,11},{12,20... | collective-permute-start | bytes 1572872 | tf_op jit(solution)/shard_map/ppermute | solution.py:288
  114.9 12.8 %collective-permute-start.28 = (bf16[512,512]{1,0:T(8,128)(2,1)S(1)}, bf16[512,512]{1,0:T(8,128)(2,1)S(1)}, u32[]{:S(2)}, u32[]{:S(2)}) collective-permute-start(bf16[512,512]{1,0:T(8,128)(2,1)S(1)} %get-tuple-element.71), channel_id=1, source_target_pairs={{8,0},{16,24},{9,1},{17,25},{10,2},{18,26},{11,3},{19,27},{12,4},{... | collective-permute-start | bytes 1572872 | tf_op jit(solution)/shard_map/ppermute | solution.py:304
  116.7 5.1 %collective-permute-start.25 = (bf16[64,1152]{1,0:T(8,128)(2,1)S(1)}, bf16[64,1152]{1,0:T(8,128)(2,1)S(1)}, u32[]{:S(2)}, u32[]{:S(2)}) collective-permute-start(bf16[64,1152]{1,0:T(8,128)(2,1)S(1)} %get-tuple-element.68), channel_id=1, source_target_pairs={{0,2},{1,3},{2,0},{3,1},{4,6},{5,7},{6,4},{7,5},{8,10},{9,11},{10,... | collective-permute-start | bytes 442376 | tf_op jit(solution)/shard_map/ppermute | solution.py:210
  118.0 4.8 %collective-permute-start.26 = (bf16[64,1152]{1,0:T(8,128)(2,1)S(1)}, bf16[64,1152]{1,0:T(8,128)(2,1)S(1)}, u32[]{:S(2)}, u32[]{:S(2)}) collective-permute-start(bf16[64,1152]{1,0:T(8,128)(2,1)S(1)} %get-tuple-element.69), channel_id=1, source_target_pairs={{0,4},{1,5},{2,6},{3,7},{4,0},{5,1},{6,2},{7,3},{8,12},{9,13},{10,... | collective-permute-start | bytes 442376 | tf_op jit(solution)/shard_map/ppermute | solution.py:210
  118.5 7.5 %collective-permute-start.27 = (bf16[64,1152]{1,0:T(8,128)(2,1)S(1)}, bf16[64,1152]{1,0:T(8,128)(2,1)S(1)}, u32[]{:S(2)}, u32[]{:S(2)}) collective-permute-start(bf16[64,1152]{1,0:T(8,128)(2,1)S(1)} %get-tuple-element.70), channel_id=1, source_target_pairs={{0,6},{1,7},{2,4},{3,5},{4,2},{5,3},{6,0},{7,1},{8,14},{9,15},{10,... | collective-permute-start | bytes 442376 | tf_op jit(solution)/shard_map/ppermute | solution.py:210
  119.4 19.5 %collective-permute-start.33 = (bf16[512,512]{1,0:T(8,128)(2,1)S(1)}, bf16[512,512]{1,0:T(8,128)(2,1)S(1)}, u32[]{:S(2)}, u32[]{:S(2)}) collective-permute-start(bf16[512,512]{1,0:T(8,128)(2,1)S(1)} %get-tuple-element.75), channel_id=1, source_target_pairs={{8,0},{16,24},{9,1},{17,25},{10,2},{18,26},{11,3},{19,27},{12,4},{... | collective-permute-start | bytes 1572872 | tf_op jit(solution)/shard_map/ppermute | solution.py:304
  127.7 9.8 %collective-permute-start.31 = (bf16[64,1152]{1,0:T(8,128)(2,1)S(1)}, bf16[64,1152]{1,0:T(8,128)(2,1)S(1)}, u32[]{:S(2)}, u32[]{:S(2)}) collective-permute-start(bf16[64,1152]{1,0:T(8,128)(2,1)S(1)} %shard_map.46), channel_id=1, source_target_pairs={{0,6},{1,7},{2,4},{3,5},{4,2},{5,3},{6,0},{7,1},{8,14},{9,15},{10,... | collective-permute-start | bytes 442376 | tf_op jit(solution)/shard_map/ppermute | solution.py:210
  129.1 8.4 %collective-permute-start.30 = (bf16[64,1152]{1,0:T(8,128)(2,1)S(1)}, bf16[64,1152]{1,0:T(8,128)(2,1)S(1)}, u32[]{:S(2)}, u32[]{:S(2)}) collective-permute-start(bf16[64,1152]{1,0:T(8,128)(2,1)S(1)} %shard_map.46), channel_id=1, source_target_pairs={{0,4},{1,5},{2,6},{3,7},{4,0},{5,1},{6,2},{7,3},{8,12},{9,13},{10,... | collective-permute-start | bytes 442376 | tf_op jit(solution)/shard_map/ppermute | solution.py:210
  130.1 6.2 %collective-permute-start.29 = (bf16[64,1152]{1,0:T(8,128)(2,1)S(1)}, bf16[64,1152]{1,0:T(8,128)(2,1)S(1)}, u32[]{:S(2)}, u32[]{:S(2)}) collective-permute-start(bf16[64,1152]{1,0:T(8,128)(2,1)S(1)} %shard_map.46), channel_id=1, source_target_pairs={{0,2},{1,3},{2,0},{3,1},{4,6},{5,7},{6,4},{7,5},{8,10},{9,11},{10,... | collective-permute-start | bytes 442376 | tf_op jit(solution)/shard_map/ppermute | solution.py:210
  (28 other events, 192.9 us)

commit v5 on v4

v5 whole, which is shorter than its diff:
```python
import functools
import math

import jax
import jax.numpy as jnp
from jax import lax
from jax.experimental import pallas as pl
from jax.experimental.pallas import tpu as pltpu
from jax.sharding import PartitionSpec as P

VMEM = pltpu.CompilerParams(vmem_limit_bytes=24 * 1024 * 1024)
NORM = 128


def kernel_call(body, outs, flops=0, smem=0):
    def call(*args):
        moved = sum(a.size * a.dtype.itemsize for a in args)
        moved += sum(math.prod(s) * jnp.dtype(t).itemsize for s, t in outs)
        space = [pltpu.SMEM] * smem + [pltpu.VMEM] * (len(args) - smem)
        return pl.pallas_call(
            body,
            out_shape=[jax.ShapeDtypeStruct(s, t) for s, t in outs],
            in_specs=[pl.BlockSpec(memory_space=m) for m in space],
            out_specs=[pl.BlockSpec(memory_space=pltpu.VMEM) for _ in outs],
            compiler_params=VMEM,
            cost_estimate=pl.CostEstimate(flops=0, bytes_accessed=0, transcendentals=0),
        )(*args)

    return call


def gram(left, right):
    return lax.dot_general(
        left, right, (((1,), (1,)), ((), ())), preferred_element_type=jnp.float32
    )


def dot_t(left, right):
    return lax.dot_general(
        left, right, (((0,), (0,)), ((), ())), preferred_element_type=jnp.float32
    )


def dot(left, right):
    return jnp.dot(left, right, preferred_element_type=jnp.float32)


def centered_into(out, block, mean, square):
    out[...] = (block[...].astype(jnp.float32) - mean).astype(jnp.bfloat16)
    wide = out[...].astype(jnp.float32)
    square[...] = jnp.sum(wide * wide, axis=0, keepdims=True)


def high_low(n, like):
    high = n.astype(jnp.bfloat16).astype(jnp.float32)
    lane = lax.broadcasted_iota(jnp.int32, like, 1)
    return jnp.where(lane == 0, high, jnp.where(lane == 1, n - high, 0.0))


def turn_into(turned, order, block):
    eighth = block.shape[0] // 8
    for k in range(8):
        start = pl.multiple_of(order[k] * eighth, eighth)
        turned[k * eighth:(k + 1) * eighth, :] = block[pl.ds(start, eighth), :]


def own_kernel(order, z, mean, own, turned, square):
    centered_into(own, z, mean[...], square)
    turn_into(turned, order, own)


def first_kernel(order, turned, near_in, swapped_in, mean, *refs):
    near, swapped, near_square, swapped_square, kept, sent, turned_near = refs
    rows = near.shape[0]
    half = rows // 2
    centered_into(near, near_in, mean[...], near_square)
    centered_into(swapped, swapped_in, mean[...], swapped_square)
    turn_into(turned_near, order, near)
    for k, (left, right) in enumerate(((turned, near), (turned_near, swapped))):
        inner = gram(left[...], right[...])
        kept[:, k * rows:(k + 1) * rows] = inner[:half]
        sent[:, k * rows:(k + 1) * rows] = inner[half:].astype(jnp.bfloat16)


def second_kernel(order, middle, turned, own, swapped, end_in, mean, end, square, kept, sent):
    rows = end.shape[0]
    eighth, half = rows // 8, rows // 2
    inner = gram(turned[...], own[...])
    wide = turned[...].astype(jnp.float32)
    norm = jnp.sum(wide * wide, axis=1, keepdims=True)
    column = lax.broadcasted_iota(jnp.int32, (eighth, rows), 1)
    row = lax.broadcasted_iota(jnp.int32, (eighth, rows), 0)
    for k in range(8):
        here = slice(k * eighth, (k + 1) * eighth)
        off = jnp.where(column == row + order[k] * eighth, 0.0, inner[here])
        if k < 4:
            kept[here, :rows] = off
        else:
            sent[k * eighth - half:(k + 1) * eighth - half, :rows] = off.astype(jnp.bfloat16)
    lane = lax.broadcasted_iota(jnp.int32, (half, NORM), 1)
    kept[:, 2 * rows:] = jnp.where(lane == 0, norm[:half], 0.0)
    sent[:, 2 * rows:] = high_low(norm[half:], (half, NORM)).astype(jnp.bfloat16)

    def put(inner):
        kept[:, rows:2 * rows] = inner[:half]
        sent[:, rows:2 * rows] = inner[half:].astype(jnp.bfloat16)

    @pl.when(middle[0] == 1)
    def _():
        end[...] = jnp.zeros_like(end)
        square[...] = jnp.zeros_like(square)
        put(gram(turned[...], swapped[...]))

    @pl.when(middle[0] == 0)
    def _():
        centered_into(end, end_in, mean[...], square)
        put(gram(turned[...], end[...]))


def with_norm(x, last):
    if not last:
        return x
    tail = x[:, last:]
    split = high_low(jnp.sum(tail, axis=1, keepdims=True), tail.shape)
    return jnp.concatenate([x[:, :last], split], axis=1)


def add_kernel(last, kept, got, mine, *out):
    total = with_norm(kept[...] + got[...].astype(jnp.float32), last)
    quarter = mine.shape[0]
    mine[...] = total[:quarter]
    for k, ref in enumerate(out, 1):
        ref[...] = total[k * quarter:(k + 1) * quarter].astype(jnp.bfloat16)


def total_kernel(last, mine, a, b, c, out):
    total = mine[...] + a[...].astype(jnp.float32)
    total = total + b[...].astype(jnp.float32) + c[...].astype(jnp.float32)
    out[...] = with_norm(total, last).astype(jnp.bfloat16)


def place_kernel(order, near, far, out):
    eighth = out.shape[0] // 8
    for k in range(4):
        here = slice(k * eighth, (k + 1) * eighth)
        out[pl.ds(pl.multiple_of(order[k] * eighth, eighth), eighth), :] = near[here, :]
        out[pl.ds(pl.multiple_of(order[4 + k] * eighth, eighth), eighth), :] = far[here, :]


def middle_kernel(inner, own, near, swapped, own_square, near_square, swapped_square, out, over):
    rows = own.shape[0]
    with_own, with_swapped = inner[:, :rows], inner[:, rows:]
    outward = dot_t(with_own, own[...]) + dot(with_swapped, swapped[...])
    square = own_square[...] + swapped_square[...]
    out[...] = (outward - near[...].astype(jnp.float32) * square).astype(jnp.bfloat16)
    across = dot_t(with_swapped, near[...])
    over[...] = (across - swapped[...].astype(jnp.float32) * near_square[...]).astype(jnp.bfloat16)


def coefficient(total):
    return 2.0 * total / (25.0 * (total - 1)) / (total - 1)


def last_kernel(
    total, middle, first, second, own, near, swapped, end, z, other,
    own_square, near_square, swapped_square, end_square, mean, spread, out,
):
    rows = own.shape[0]
    norm = jnp.sum(second[:, 2 * rows:].astype(jnp.float32), axis=1, keepdims=True)
    anchor = z[...].astype(jnp.float32)
    deviation = jnp.sqrt(spread[...] / (total - 1) + 0.0001)
    centered = anchor - mean[...]
    hinge = jnp.where(deviation < 1.0, centered / deviation, 0.0)
    plain = anchor - other[...].astype(jnp.float32) - total / (4.0 * (total - 1)) * hinge
    both = dot(second[:, :rows], own[...])
    wide = own[...].astype(jnp.float32)

    @pl.when(middle[0] == 1)
    def _():
        product = both + dot(first[:, :rows], near[...])
        product = product + dot(second[:, rows:2 * rows], swapped[...])
        square = own_square[...] + near_square[...] + swapped_square[...]
        out[...] = plain + coefficient(total) * (product + wide * (norm - square))

    @pl.when(middle[0] == 0)
    def _():
        product = both + dot(second[:, rows:2 * rows], end[...])
        square = own_square[...] + end_square[...]
        out[...] = plain + coefficient(total) * (product + wide * (norm - square))


def to_partner(x, step):
    return lax.ppermute(x, "feat", [(i, i ^ step) for i in range(8)])


def scatter_sum(kept, sent, last=0):
    half, n = kept.shape
    eighth = (half // 4, n)
    mine, *out = kernel_call(
        functools.partial(add_kernel, last),
        [(eighth, jnp.float32)] + [(eighth, jnp.bfloat16)] * 3,
    )(kept, to_partner(sent, 1))
    got = [to_partner(x, 2 * k) for k, x in enumerate(out, 1)]
    return kernel_call(functools.partial(total_kernel, last), [(eighth, jnp.bfloat16)])(
        mine, *got
    )[0]


def gather_rows(x, order):
    near = jnp.concatenate([x] + [to_partner(x, 2 * k) for k in (1, 2, 3)])
    far = to_partner(near, 1)
    shape = (8 * x.shape[0], x.shape[1])
    return kernel_call(place_kernel, [(shape, jnp.bfloat16)], smem=1)(order, near, far)[0]


def after(x, *others):
    return lax.optimization_barrier((x, *others))[0]


def by_line(z_anchor, z_other):
    rows, width = z_anchor.shape
    total = rows * 4
    plane = lax.axis_index("dp")
    middle = ((plane == 1) | (plane == 2)).astype(jnp.int32).reshape(1)
    order = lax.axis_index("feat") ^ jnp.array([0, 2, 4, 6, 1, 3, 5, 7], jnp.int32)
    inward, across, outward = [(0, 1), (3, 2)], [(1, 2), (2, 1)], [(1, 0), (2, 3)]
    half, wide = rows // 2, 2 * rows + NORM
    flat, block = ((1, width), jnp.float32), ((rows, width), jnp.bfloat16)

    near = lax.ppermute(z_anchor, "dp", inward)
    swapped = lax.ppermute(z_anchor, "dp", across)
    anchor = z_anchor.astype(jnp.float32)
    sums = jnp.sum(anchor, axis=0, keepdims=True)
    apart = anchor - sums / rows
    stats = jnp.concatenate([sums, jnp.sum(apart * apart, axis=0, keepdims=True)])
    all_stats = [stats] + [
        lax.ppermute(stats, "dp", [(i, (i + k) % 4) for i in range(4)]) for k in (1, 2, 3)
    ]
    mean = (all_stats[0][:1] + all_stats[1][:1] + all_stats[2][:1] + all_stats[3][:1]) / total
    spread = 0.0
    for one in all_stats:
        shift = one[:1] / rows - mean
        spread = spread + (one[1:] + rows * shift * shift)
    end = lax.ppermute(after(z_anchor, near, swapped), "dp", [(0, 3), (3, 0)])

    own, turned, own_square = kernel_call(own_kernel, [block, block, flat], smem=1)(
        order, z_anchor, mean
    )
    near, swapped, near_square, swapped_square, kept, sent, _ = kernel_call(
        first_kernel,
        [block, block, flat, flat, ((half, 2 * rows), jnp.float32),
         ((half, 2 * rows), jnp.bfloat16), block],
        smem=1,
    )(order, turned, near, swapped, mean)
    first = gather_rows(scatter_sum(kept, sent), order)

    pushed, ready = [], []
    for here in (slice(0, width // 2), slice(width // 2, width)):
        part = ((rows, width // 2), jnp.bfloat16)
        out, over = kernel_call(middle_kernel, [part, part])(
            first, own[:, here], near[:, here], swapped[:, here],
            own_square[:, here], near_square[:, here], swapped_square[:, here],
        )
        ready += [out, over]
        pushed.append((lax.ppermute(out, "dp", outward), lax.ppermute(over, "dp", across)))

    end, end_square, kept, sent = kernel_call(
        second_kernel,
        [block, flat, ((half, wide), jnp.float32), ((half, wide), jnp.bfloat16)],
        smem=2,
    )(order, middle, after(turned, *ready), own, swapped, end, mean)
    second = gather_rows(after(scatter_sum(kept, sent, 2 * rows), *pushed[0]), order)

    tile = width // 4
    whole = lambda n: pl.BlockSpec((rows, n), lambda j: (0, 0))
    strip = pl.BlockSpec((rows, tile), lambda j: (0, j))
    line = pl.BlockSpec((1, tile), lambda j: (0, j))
    held = pl.pallas_call(
        functools.partial(last_kernel, total),
        grid=(4,),
        out_shape=jax.ShapeDtypeStruct((rows, width), jnp.float32),
        in_specs=[pl.BlockSpec(memory_space=pltpu.SMEM), whole(2 * rows), whole(wide)]
        + [strip] * 6 + [line] * 6,
        out_specs=strip,
        compiler_params=VMEM,
        cost_estimate=pl.CostEstimate(
            flops=6 * rows * rows * width, bytes_accessed=20 * rows * width, transcendentals=0
        ),
    )(
        middle, first, second, own, near, swapped, end, z_anchor, z_other,
        own_square, near_square, swapped_square, end_square, mean, spread,
    )
    pushed = jnp.concatenate(
        [a.astype(jnp.float32) + b.astype(jnp.float32) for a, b in pushed], axis=1
    )
    return held + coefficient(total) * pushed


def by_gather(z_anchor, z_other):
    rows_here, width = z_anchor.shape
    groups = lax.axis_size("dp")
    total = rows_here * groups
    mine = lax.axis_index("dp") * rows_here
    column = lax.all_gather(z_anchor, "dp", axis=0, tiled=True).astype(jnp.float32)
    mean = jnp.sum(column, axis=0) / total
    centered_all = column - mean
    variance = jnp.sum(centered_all * centered_all, axis=0) / (total - 1)
    rounded_all = centered_all.astype(jnp.bfloat16)
    widened = rounded_all.astype(jnp.float32)
    own_square = jnp.sum(widened * widened, axis=0)
    rounded = lax.dynamic_slice_in_dim(rounded_all, mine, rows_here, 0)
    inner = lax.psum(gram(rounded, rounded_all).astype(jnp.bfloat16), "feat")
    product = jnp.dot(inner, rounded_all, preferred_element_type=jnp.float32)
    product = product - rounded.astype(jnp.float32) * own_square
    return finish(z_anchor, z_other, mean, variance, total, product)


def finish(z_anchor, z_other, mean, variance, total, product):
    coef = 2.0 * total / (25.0 * (total - 1)) / (total - 1)
    anchor = z_anchor.astype(jnp.float32)
    centered = anchor - mean
    deviation = jnp.sqrt(variance + 0.0001)
    hinge = jnp.where(deviation < 1.0, centered / deviation, 0.0)
    factor = total / (4.0 * (total - 1))
    return anchor - z_other.astype(jnp.float32) - factor * hinge + coef * product


def solution(mesh):
    placed = (P("dp", "feat"), P("dp", "feat"))
    in_line = mesh.shape["dp"] == 4 and mesh.shape["feat"] == 8
    return jax.shard_map(
        by_line if in_line else by_gather,
        mesh=mesh, in_specs=placed, out_specs=P("dp", "feat"), check_vma=False,
    )
```

time: 150 us -> 110 us (0.73); the launches traced: 147 us -> 109 us
  waiting for transfers between devices: 65.2 us -> 41.8 us
  starting transfers between devices: 51.2 us -> 40.2 us
  local copies, waits for them, and re-layouts: 12.8 us -> 5.71 us
  other arithmetic: 2.09 us -> 5.08 us
    ppermute x15 -> x7, waiting for transfers between devices: 33.5 us -> 2.6 us  [the longest x2 2.59 us: by_line(): lax.ppermute(over, 'dp', across)]
    ppermute x15 -> x7, starting transfers between devices: 29 us -> 16.9 us  [the longest x2 6.46 us: by_line(): lax.ppermute(out, 'dp', outward)]
    ppermute x3, waiting for transfers between devices: 5.85 us -> 16.8 us  [by_line(): lax.ppermute(stats, 'dp', [(i, (i + k) % 4) for i in range(4)])]
    slice x7 -> x2, local copies, waits for them, and re-layouts: 3.98 us -> 0.14 us  [the longest x1 0.14 us: by_line(): swapped[:, here]]
    ppermute x16, waiting for transfers between devices: 25.8 us -> 22.4 us  [to_partner(): return lax.ppermute(x, 'feat', [(i, i ^ step) for i in range(8)])]
    unnamed x56 -> x25, local copies, waits for them, and re-layouts: 8.11 us -> 5.48 us
    pallas_call x11, Pallas kernels: 8.6 us -> 11.2 us  [call(): pl.pallas_call(body, out_shape=[jax.ShapeDtypeStruct(s, t) for s, t in ou...]
    add x0 -> x3, other arithmetic: none -> 2.05 us  [the longest x1 1.75 us: by_line(): return held + coefficient(total) * pushed]
  transfers between devices with their start and end apart: 34 -> 26, of which waited for: 22 -> 16; matrix products, arithmetic and copies ran while one was open for 3% -> 3% of each run, Pallas kernels for 3% -> 4%
where the time goes in v5:
time: 110 us; the launch traced here: 109 us
  waiting for transfers between devices  41.8 us (38%)
  starting transfers between devices  40.2 us (37%)
  Pallas kernels  16.4 us (15%)
  local copies, waits for them, and re-layouts  5.71 us (5%)
  other arithmetic  5.08 us (5%)
    ppermute x16, waiting for transfers between devices, to_partner(): return lax.ppermute(x, 'feat', [(i, i ^ step) for i in range(8)])  22.4 us
    ppermute x16, starting transfers between devices, to_partner(): return lax.ppermute(x, 'feat', [(i, i ^ step) for i in range(8)])  17.9 us
    ppermute x3, waiting for transfers between devices, by_line(): lax.ppermute(stats, 'dp', [(i, (i + k) % 4) for i in range(4)])  16.8 us
    pallas_call x11, Pallas kernels, call(): pl.pallas_call(body, out_shape=[jax.ShapeDtypeStruct(s, t) for s, t in ou...  11.2 us
    ppermute x2, starting transfers between devices, by_line(): lax.ppermute(out, 'dp', outward)  6.46 us
    unnamed x25, local copies, waits for them, and re-layouts  5.48 us
    ppermute x3, starting transfers between devices, by_line(): lax.ppermute(stats, 'dp', [(i, (i + k) % 4) for i in range(4)])  5.36 us
    pallas_call x1, Pallas kernels, by_line(): pl.pallas_call(functools.partial(last_kernel, total), grid=(4,), out_shap...  5.16 us
  transfers between devices with their start and end apart: 26, of which 16 were waited for; matrix products, arithmetic and copies ran while one was open for 3% of the time, Pallas kernels for 4%

profile of v5, /device:TPU:9, one launch (start us, length us, event | category | flops | bytes accessed | tf_op | source)
XLA Modules:
  0.0 109.5 jit_solution(1193304430488833709)
XLA Ops:
  0.0 3.3 %collective-permute-start.4 = (bf16[512,1024]{1,0:T(8,128)(2,1)}, bf16[512,1024]{1,0:T(8,128)(2,1)S(1)}, u32[]{:S(2)}, u32[]{:S(2)}) collective-permute-start(bf16[512,1024]{1,0:T(8,128)(2,1)} %z.3), channel_id=1, source_target_pairs={{8,16},{16,8},{9,17},{17,9},{10,18},{18,10},{11,19},{19,11},{12,20... | collective-permute-start | bytes 3145736 | tf_op jit(solution)/shard_map/ppermute | solution.py:231
  3.3 1.3 %collective-permute-start.3 = (bf16[512,1024]{1,0:T(8,128)(2,1)}, bf16[512,1024]{1,0:T(8,128)(2,1)}, u32[]{:S(2)}, u32[]{:S(2)}) collective-permute-start(bf16[512,1024]{1,0:T(8,128)(2,1)} %z.3), channel_id=1, source_target_pairs={{0,8},{24,16},{1,9},{25,17},{2,10},{26,18},{3,11},{27,19},{4,12},{... | collective-permute-start | bytes 3145736 | tf_op jit(solution)/shard_map/ppermute | solution.py:230
  4.6 1.4 %convert_reduce_fusion = f32[1024]{0:T(1024)S(1)} fusion(bf16[512,1024]{1,0:T(8,128)(2,1)} %z.3), kind=kLoop, calls=%fused_computation.1 | loop fusion | flops 1047552 | bytes 1052672 | tf_op jit(solution)/shard_map/reduce_sum | solution.py:233
  6.1 1.5 %fusion.1 = f32[1024]{0:T(1024)S(1)} fusion(bf16[512,1024]{1,0:T(8,128)(2,1)} %z.3, f32[1024]{0:T(1024)S(1)} %broadcast_multiply_fusion), kind=kLoop, calls=%fused_computation.3 | loop fusion | flops 2096128 | bytes 1056768 | tf_op jit(solution)/shard_map/reduce_sum | solution.py:235
  7.6 3.1 %collective-permute-start.2 = (f32[2,1024]{1,0:T(2,128)S(1)}, f32[2,1024]{1,0:T(2,128)S(1)}, u32[]{:S(2)}, u32[]{:S(2)}) collective-permute-start(f32[2,1024]{1,0:T(2,128)S(1)} %pad_maximum_fusion.1), channel_id=1, source_target_pairs={{0,24},{8,0},{16,8},{24,16},{1,25},{9,1},{17,9},{25,17},{2,26},{10... | collective-permute-start | bytes 24584 | tf_op jit(solution)/shard_map/ppermute | solution.py:237
  10.7 2.2 %collective-permute-start = (f32[2,1024]{1,0:T(2,128)S(1)}, f32[2,1024]{1,0:T(2,128)S(1)}, u32[]{:S(2)}, u32[]{:S(2)}) collective-permute-start(f32[2,1024]{1,0:T(2,128)S(1)} %pad_maximum_fusion.1), channel_id=1, source_target_pairs={{0,8},{8,16},{16,24},{24,0},{1,9},{9,17},{17,25},{25,1},{2,10},{10... | collective-permute-start | bytes 24584 | tf_op jit(solution)/shard_map/ppermute | solution.py:237
  13.0 13.6 %collective-permute-done.2 = f32[2,1024]{1,0:T(2,128)S(1)} collective-permute-done((f32[2,1024]{1,0:T(2,128)S(1)}, f32[2,1024]{1,0:T(2,128)S(1)}, u32[]{:S(2)}, u32[]{:S(2)}) %collective-permute-start.2) | collective-permute-done | bytes 8224 | tf_op jit(solution)/shard_map/ppermute | solution.py:237
  26.5 2.6 %collective-permute-done.1 = f32[2,1024]{1,0:T(2,128)S(1)} collective-permute-done((f32[2,1024]{1,0:T(2,128)S(1)}, f32[2,1024]{1,0:T(2,128)S(1)}, u32[]{:S(2)}, u32[]{:S(2)}) %collective-permute-start.1) | collective-permute-done | bytes 8224 | tf_op jit(solution)/shard_map/ppermute | solution.py:237
  32.9 3.5 %shard_map.38 = (bf16[512,1024]{1,0:T(8,128)(2,1)S(1)}, bf16[512,1024]{1,0:T(8,128)(2,1)S(1)}, f32[1,1024]{1,0:T(1,128)S(1)}, f32[1,1024]{1,0:T(1,128)S(1)}, f32...) custom-call(s32[8]{0:T(128)S(1)} %broadcast_xor_fusion.order, ...), custom_call_target="tpu_custom_call" | custom-call | tf_op jit(solution)/shard_map/pallas_call | solution.py:20
  38.4 1.8 %collective-permute-start.5 = (bf16[256,1024]{1,0:T(8,128)(2,1)}, bf16[256,1024]{1,0:T(8,128)(2,1)}, u32[]{:S(2)}, u32[]{:S(2)}) collective-permute-start(bf16[256,1024]{1,0:T(8,128)(2,1)} %get-tuple-element.35), channel_id=1, source_target_pairs={{0,1},{1,0},{2,3},{3,2},{4,5},{5,4},{6,7},{7,6},{8,9},{9,8},{10,11... | collective-permute-start | bytes 1572872 | tf_op jit(solution)/shard_map/ppermute | solution.py:193
  44.4 1.3 %collective-permute-start.6 = (bf16[64,1024]{1,0:T(8,128)(2,1)S(1)}, bf16[64,1024]{1,0:T(8,128)(2,1)S(1)}, u32[]{:S(2)}, u32[]{:S(2)}) collective-permute-start(bf16[64,1024]{1,0:T(8,128)(2,1)S(1)} %get-tuple-element.37), channel_id=1, source_target_pairs={{0,2},{1,3},{2,0},{3,1},{4,6},{5,7},{6,4},{7,5},{8,10},{9,11},{10,... | collective-permute-start | bytes 393224 | tf_op jit(solution)/shard_map/ppermute | solution.py:193
  47.2 2.0 %collective-permute-done.6.a = bf16[64,1024]{1,0:T(8,128)(2,1)S(1)} collective-permute-done((bf16[64,1024]{1,0:T(8,128)(2,1)S(1)}, bf16[64,1024]{1,0:T(8,128)(2,1)S(1)}, u32[]{:S(2)}, u32[]{:S(2)}) %collective-permute-start.6) | collective-permute-done | bytes 131104 | tf_op jit(solution)/shard_map/ppermute | solution.py:193
  50.1 2.7 %collective-permute-done.8.c = bf16[64,1024]{1,0:T(8,128)(2,1)S(1)} collective-permute-done((bf16[64,1024]{1,0:T(8,128)(2,1)S(1)}, bf16[64,1024]{1,0:T(8,128)(2,1)S(1)}, u32[]{:S(2)}, u32[]{:S(2)}) %collective-permute-start.8) | collective-permute-done | bytes 131104 | tf_op jit(solution)/shard_map/ppermute | solution.py:193
  52.8 1.5 %collective-permute-start.11 = (bf16[64,1024]{1,0:T(8,128)(2,1)S(1)}, bf16[64,1024]{1,0:T(8,128)(2,1)S(1)}, u32[]{:S(2)}, u32[]{:S(2)}) collective-permute-start(bf16[64,1024]{1,0:T(8,128)(2,1)S(1)} %shard_map.40), channel_id=1, source_target_pairs={{0,6},{1,7},{2,4},{3,5},{4,2},{5,3},{6,0},{7,1},{8,14},{9,15},{10,... | collective-permute-start | bytes 393224 | tf_op jit(solution)/shard_map/ppermute | solution.py:193
  55.5 2.2 %collective-permute-done.11 = bf16[64,1024]{1,0:T(8,128)(2,1)S(1)} collective-permute-done((bf16[64,1024]{1,0:T(8,128)(2,1)S(1)}, bf16[64,1024]{1,0:T(8,128)(2,1)S(1)}, u32[]{:S(2)}, u32[]{:S(2)}) %collective-permute-start.11) | collective-permute-done | bytes 131104 | tf_op jit(solution)/shard_map/ppermute | solution.py:193
  57.7 3.4 %collective-permute-done.10 = bf16[64,1024]{1,0:T(8,128)(2,1)S(1)} collective-permute-done((bf16[64,1024]{1,0:T(8,128)(2,1)S(1)}, bf16[64,1024]{1,0:T(8,128)(2,1)S(1)}, u32[]{:S(2)}, u32[]{:S(2)}) %collective-permute-start.10) | collective-permute-done | bytes 131104 | tf_op jit(solution)/shard_map/ppermute | solution.py:193
  61.1 1.8 %collective-permute-start.12 = (bf16[256,1024]{1,0:T(8,128)(2,1)S(1)}, bf16[256,1024]{1,0:T(8,128)(2,1)S(1)}, u32[]{:S(2)}, u32[]{:S(2)}) collective-permute-start(bf16[256,1024]{1,0:T(8,128)(2,1)S(1)} %pad_maximum_fusion.near), channel_id=1, source_target_pairs={{0,1},{1,0},{2,3},{3,2},{4,5},{5,4},{6,7},{7,6},{8,9},{9,8},{10,11... | collective-permute-start | bytes 1572872 | tf_op jit(solution)/shard_map/ppermute | solution.py:193
  63.0 1.4 %collective-permute-done.12.far = bf16[256,1024]{1,0:T(8,128)(2,1)S(1)} collective-permute-done((bf16[256,1024]{1,0:T(8,128)(2,1)S(1)}, bf16[256,1024]{1,0:T(8,128)(2,1)S(1)}, u32[]{:S(2)}, u32[]{:S(2)}) %collective-permute-start.12) | collective-permute-done | bytes 524320 | tf_op jit(solution)/shard_map/ppermute | solution.py:193
  67.1 2.2 %shard_map.44 = (bf16[512,1024]{1,0:T(8,128)(2,1)S(1)}, f32[1,1024]{1,0:T(1,128)S(1)}, f32[256,1152]{1,0:T(8,128)S(1)}, bf16[256,1152]{1,0:T(8,128)(2,1)S(1)}) custom-call(s32[8]{0:T(128)S(1)} %broadcast_xor_fusion.order, s32[1]{0:T(128)} %bitcast.middle, bf16[512,1024]{1,0:T(8,128)(2,1)S(1)} %copy-done.4, bf16[512,1024]{1,0:T(8,128)(2,1)S(1)} %get-tuple-element.40.own, ...), custom_call_target="tpu_custom_call" | custom-call | tf_op jit(solution)/shard_map/pallas_call | solution.py:20
  69.7 5.1 %collective-permute-start.18 = (bf16[512,512]{1,0:T(8,128)(2,1)S(1)}, bf16[512,512]{1,0:T(8,128)(2,1)S(1)}, u32[]{:S(2)}, u32[]{:S(2)}) collective-permute-start(bf16[512,512]{1,0:T(8,128)(2,1)S(1)} %get-tuple-element.46), channel_id=1, source_target_pairs={{8,0},{16,24},{9,1},{17,25},{10,2},{18,26},{11,3},{19,27},{12,4},{... | collective-permute-start | bytes 1572872 | tf_op jit(solution)/shard_map/ppermute | solution.py:265
  74.8 2.8 %collective-permute-start.19 = (bf16[512,512]{1,0:T(8,128)(2,1)S(1)}, bf16[512,512]{1,0:T(8,128)(2,1)S(1)}, u32[]{:S(2)}, u32[]{:S(2)}) collective-permute-start(bf16[512,512]{1,0:T(8,128)(2,1)S(1)} %get-tuple-element.47), channel_id=1, source_target_pairs={{8,16},{16,8},{9,17},{17,9},{10,18},{18,10},{11,19},{19,11},{12,20... | collective-permute-start | bytes 1572872 | tf_op jit(solution)/shard_map/ppermute | solution.py:265
  77.8 1.3 %collective-permute-start.15 = (bf16[64,1152]{1,0:T(8,128)(2,1)S(1)}, bf16[64,1152]{1,0:T(8,128)(2,1)S(1)}, u32[]{:S(2)}, u32[]{:S(2)}) collective-permute-start(bf16[64,1152]{1,0:T(8,128)(2,1)S(1)} %get-tuple-element.55), channel_id=1, source_target_pairs={{0,2},{1,3},{2,0},{3,1},{4,6},{5,7},{6,4},{7,5},{8,10},{9,11},{10,... | collective-permute-start | bytes 442376 | tf_op jit(solution)/shard_map/ppermute | solution.py:193
  80.5 2.2 %collective-permute-done.15.a = bf16[64,1152]{1,0:T(8,128)(2,1)S(1)} collective-permute-done((bf16[64,1152]{1,0:T(8,128)(2,1)S(1)}, bf16[64,1152]{1,0:T(8,128)(2,1)S(1)}, u32[]{:S(2)}, u32[]{:S(2)}) %collective-permute-start.15) | collective-permute-done | bytes 147488 | tf_op jit(solution)/shard_map/ppermute | solution.py:193
  82.7 1.3 %collective-permute-start.24 = (bf16[512,512]{1,0:T(8,128)(2,1)S(1)}, bf16[512,512]{1,0:T(8,128)(2,1)S(1)}, u32[]{:S(2)}, u32[]{:S(2)}) collective-permute-start(bf16[512,512]{1,0:T(8,128)(2,1)S(1)} %get-tuple-element.48), channel_id=1, source_target_pairs={{8,0},{16,24},{9,1},{17,25},{10,2},{18,26},{11,3},{19,27},{12,4},{... | collective-permute-start | bytes 1572872 | tf_op jit(solution)/shard_map/ppermute | solution.py:265
  84.0 2.3 %collective-permute-start.25 = (bf16[512,512]{1,0:T(8,128)(2,1)S(1)}, bf16[512,512]{1,0:T(8,128)(2,1)S(1)}, u32[]{:S(2)}, u32[]{:S(2)}) collective-permute-start(bf16[512,512]{1,0:T(8,128)(2,1)S(1)} %get-tuple-element.49), channel_id=1, source_target_pairs={{8,16},{16,8},{9,17},{17,9},{10,18},{18,10},{11,19},{19,11},{12,20... | collective-permute-start | bytes 1572872 | tf_op jit(solution)/shard_map/ppermute | solution.py:265
  87.2 2.6 %collective-permute-done.19 = bf16[512,512]{1,0:T(8,128)(2,1)S(1)} collective-permute-done((bf16[512,512]{1,0:T(8,128)(2,1)S(1)}, bf16[512,512]{1,0:T(8,128)(2,1)S(1)}, u32[]{:S(2)}, u32[]{:S(2)}) %collective-permute-start.19) | collective-permute-done | bytes 524320 | tf_op jit(solution)/shard_map/ppermute | solution.py:265
  89.8 2.1 %collective-permute-start.22 = (bf16[64,1152]{1,0:T(8,128)(2,1)S(1)}, bf16[64,1152]{1,0:T(8,128)(2,1)S(1)}, u32[]{:S(2)}, u32[]{:S(2)}) collective-permute-start(bf16[64,1152]{1,0:T(8,128)(2,1)S(1)} %shard_map.46), channel_id=1, source_target_pairs={{0,6},{1,7},{2,4},{3,5},{4,2},{5,3},{6,0},{7,1},{8,14},{9,15},{10,... | collective-permute-start | bytes 442376 | tf_op jit(solution)/shard_map/ppermute | solution.py:193
  92.4 4.5 %collective-permute-done.20 = bf16[64,1152]{1,0:T(8,128)(2,1)S(1)} collective-permute-done((bf16[64,1152]{1,0:T(8,128)(2,1)S(1)}, bf16[64,1152]{1,0:T(8,128)(2,1)S(1)}, u32[]{:S(2)}, u32[]{:S(2)}) %collective-permute-start.20) | collective-permute-done | bytes 147488 | tf_op jit(solution)/shard_map/ppermute | solution.py:193
  97.1 3.1 %collective-permute-start.23 = (bf16[256,1152]{1,0:T(8,128)(2,1)S(1)}, bf16[256,1152]{1,0:T(8,128)(2,1)S(1)}, u32[]{:S(2)}, u32[]{:S(2)}) collective-permute-start(bf16[256,1152]{1,0:T(8,128)(2,1)S(1)} %constant_dynamic-update-slice_fusion.near), channel_id=1, source_target_pairs={{0,1},{1,0},{2,3},{3,2},{4,5},{5,4},{6,7},{7,6},{8,9},{9,8},{10,11... | collective-permute-start | bytes 1769480 | tf_op jit(solution)/shard_map/ppermute | solution.py:193
  100.6 1.3 %collective-permute-done.23.far = bf16[256,1152]{1,0:T(8,128)(2,1)S(1)} collective-permute-done((bf16[256,1152]{1,0:T(8,128)(2,1)S(1)}, bf16[256,1152]{1,0:T(8,128)(2,1)S(1)}, u32[]{:S(2)}, u32[]{:S(2)}) %collective-permute-start.23) | collective-permute-done | bytes 589856 | tf_op jit(solution)/shard_map/ppermute | solution.py:193
  102.5 5.2 %shard_map.48 = f32[512,1024]{1,0:T(8,128)S(1)} custom-call(s32[1]{0:T(128)} %bitcast.middle, bf16[512,1024]{1,0:T(8,128)(2,1)S(1)} %shard_map.41.inner.first, bf16[512,1152]{1,0:T(8,128)(2,1)S(1)} %shard_map.47.second, bf16[512,1024]{1,0:T(8,128)(2,1)S(1)} %get-tuple-element.40.own, bf16[512,1024]{1,0:T(8,128)(2,1)S(1)} %copy-done.2, ...), custom_call_target="tpu_custom_call" | custom-call | flops 1610612736 | bytes 10485760 | tf_op jit(solution)/shard_map/pallas_call | solution.py:278
  107.7 1.8 %fusion.2 = f32[512,1024]{1,0:T(8,128)} fusion(f32[512,1024]{1,0:T(8,128)S(1)} %shard_map.48, f32[512,512]{1,0:T(8,128)S(1)} %convert_add_fusion, f32[512,512]{1,0:T(8,128)S(1)} %convert_add_fusion.1), kind=kLoop, calls=%fused_computation.5 | loop fusion | flops 1572864 | bytes 6291456 | tf_op jit(solution)/shard_map/add | solution.py:296
  (72 shorter events, 21.0 us)
Async XLA Ops:
  0.0 13.0 %copy-start.10 = (s32[8]{0:T(128)S(1)}, s32[8]{0:T(128)}, u32[]{:S(2)}) copy-start(s32[8]{0:T(128)} %constant.28.clone) | copy-start | bytes 100
  0.0 29.8 %copy-start = (bf16[512,1024]{1,0:T(8,128)(2,1)S(1)}, bf16[512,1024]{1,0:T(8,128)(2,1)}, u32[]{:S(2)}) copy-start(bf16[512,1024]{1,0:T(8,128)(2,1)} %z.3) | copy-start | bytes 3145732
  0.0 30.7 %collective-permute-start.4 = (bf16[512,1024]{1,0:T(8,128)(2,1)}, bf16[512,1024]{1,0:T(8,128)(2,1)S(1)}, u32[]{:S(2)}, u32[]{:S(2)}) collective-permute-start(bf16[512,1024]{1,0:T(8,128)(2,1)} %z.3), channel_id=1, source_target_pairs={{8,16},{16,8},{9,17},{17,9},{10,18},{18,10},{11,19},{19,11},{12,20... | collective-permute-start | bytes 3145736 | tf_op jit(solution)/shard_map/ppermute | solution.py:231
  3.3 28.4 %collective-permute-start.3 = (bf16[512,1024]{1,0:T(8,128)(2,1)}, bf16[512,1024]{1,0:T(8,128)(2,1)}, u32[]{:S(2)}, u32[]{:S(2)}) collective-permute-start(bf16[512,1024]{1,0:T(8,128)(2,1)} %z.3), channel_id=1, source_target_pairs={{0,8},{24,16},{1,9},{25,17},{2,10},{26,18},{3,11},{27,19},{4,12},{... | collective-permute-start | bytes 3145736 | tf_op jit(solution)/shard_map/ppermute | solution.py:230
  7.6 18.9 %collective-permute-start.2 = (f32[2,1024]{1,0:T(2,128)S(1)}, f32[2,1024]{1,0:T(2,128)S(1)}, u32[]{:S(2)}, u32[]{:S(2)}) collective-permute-start(f32[2,1024]{1,0:T(2,128)S(1)} %pad_maximum_fusion.1), channel_id=1, source_target_pairs={{0,24},{8,0},{16,8},{24,16},{1,25},{9,1},{17,9},{25,17},{2,26},{10... | collective-permute-start | bytes 24584 | tf_op jit(solution)/shard_map/ppermute | solution.py:237
  10.7 18.4 %collective-permute-start.1 = (f32[2,1024]{1,0:T(2,128)S(1)}, f32[2,1024]{1,0:T(2,128)S(1)}, u32[]{:S(2)}, u32[]{:S(2)}) collective-permute-start(f32[2,1024]{1,0:T(2,128)S(1)} %pad_maximum_fusion.1), channel_id=1, source_target_pairs={{0,16},{8,24},{16,0},{24,8},{1,17},{9,25},{17,1},{25,9},{2,18},{10... | collective-permute-start | bytes 24584 | tf_op jit(solution)/shard_map/ppermute | solution.py:237
  10.7 19.1 %collective-permute-start = (f32[2,1024]{1,0:T(2,128)S(1)}, f32[2,1024]{1,0:T(2,128)S(1)}, u32[]{:S(2)}, u32[]{:S(2)}) collective-permute-start(f32[2,1024]{1,0:T(2,128)S(1)} %pad_maximum_fusion.1), channel_id=1, source_target_pairs={{0,8},{8,16},{16,24},{24,0},{1,9},{9,17},{17,25},{25,1},{2,10},{10... | collective-permute-start | bytes 24584 | tf_op jit(solution)/shard_map/ppermute | solution.py:237
  30.7 5.8 %copy-start.3 = (bf16[512,1024]{1,0:T(8,128)(2,1)}, bf16[512,1024]{1,0:T(8,128)(2,1)S(1)}, u32[]{:S(2)}) copy-start(bf16[512,1024]{1,0:T(8,128)(2,1)S(1)} %get-tuple-element.50.turned) | copy-start | bytes 3145732
  38.4 3.6 %collective-permute-start.5 = (bf16[256,1024]{1,0:T(8,128)(2,1)}, bf16[256,1024]{1,0:T(8,128)(2,1)}, u32[]{:S(2)}, u32[]{:S(2)}) collective-permute-start(bf16[256,1024]{1,0:T(8,128)(2,1)} %get-tuple-element.35), channel_id=1, source_target_pairs={{0,1},{1,0},{2,3},{3,2},{4,5},{5,4},{6,7},{7,6},{8,9},{9,8},{10,11... | collective-permute-start | bytes 1572872 | tf_op jit(solution)/shard_map/ppermute | solution.py:193
  40.1 26.9 %collective-permute-start.13 = (bf16[512,1024]{1,0:T(8,128)(2,1)S(1)}, bf16[512,1024]{1,0:T(8,128)(2,1)S(1)}, u32[]{:S(2)}, u32[]{:S(2)}) collective-permute-start(bf16[512,1024]{1,0:T(8,128)(2,1)S(1)} %copy-done), channel_id=1, source_target_pairs={{0,24},{24,0},{1,25},{25,1},{2,26},{26,2},{3,27},{27,3},{4,28},{28... | collective-permute-start | bytes 3145736 | tf_op jit(solution)/shard_map/ppermute | solution.py:244
  44.4 18.5 %copy-start.2 = (bf16[512,1024]{1,0:T(8,128)(2,1)S(1)}, bf16[512,1024]{1,0:T(8,128)(2,1)}, u32[]{:S(2)}) copy-start(bf16[512,1024]{1,0:T(8,128)(2,1)} %copy-done.1) | copy-start | bytes 3145732
  44.4 4.8 %collective-permute-start.6 = (bf16[64,1024]{1,0:T(8,128)(2,1)S(1)}, bf16[64,1024]{1,0:T(8,128)(2,1)S(1)}, u32[]{:S(2)}, u32[]{:S(2)}) collective-permute-start(bf16[64,1024]{1,0:T(8,128)(2,1)S(1)} %get-tuple-element.37), channel_id=1, source_target_pairs={{0,2},{1,3},{2,0},{3,1},{4,6},{5,7},{6,4},{7,5},{8,10},{9,11},{10,... | collective-permute-start | bytes 393224 | tf_op jit(solution)/shard_map/ppermute | solution.py:193
  45.7 4.4 %collective-permute-start.7 = (bf16[64,1024]{1,0:T(8,128)(2,1)S(1)}, bf16[64,1024]{1,0:T(8,128)(2,1)S(1)}, u32[]{:S(2)}, u32[]{:S(2)}) collective-permute-start(bf16[64,1024]{1,0:T(8,128)(2,1)S(1)} %get-tuple-element.38), channel_id=1, source_target_pairs={{0,4},{1,5},{2,6},{3,7},{4,0},{5,1},{6,2},{7,3},{8,12},{9,13},{10,... | collective-permute-start | bytes 393224 | tf_op jit(solution)/shard_map/ppermute | solution.py:193
  46.9 5.8 %collective-permute-start.8 = (bf16[64,1024]{1,0:T(8,128)(2,1)S(1)}, bf16[64,1024]{1,0:T(8,128)(2,1)S(1)}, u32[]{:S(2)}, u32[]{:S(2)}) collective-permute-start(bf16[64,1024]{1,0:T(8,128)(2,1)S(1)} %get-tuple-element.39), channel_id=1, source_target_pairs={{0,6},{1,7},{2,4},{3,5},{4,2},{5,3},{6,0},{7,1},{8,14},{9,15},{10,... | collective-permute-start | bytes 393224 | tf_op jit(solution)/shard_map/ppermute | solution.py:193
  52.8 4.9 %collective-permute-start.11 = (bf16[64,1024]{1,0:T(8,128)(2,1)S(1)}, bf16[64,1024]{1,0:T(8,128)(2,1)S(1)}, u32[]{:S(2)}, u32[]{:S(2)}) collective-permute-start(bf16[64,1024]{1,0:T(8,128)(2,1)S(1)} %shard_map.40), channel_id=1, source_target_pairs={{0,6},{1,7},{2,4},{3,5},{4,2},{5,3},{6,0},{7,1},{8,14},{9,15},{10,... | collective-permute-start | bytes 393224 | tf_op jit(solution)/shard_map/ppermute | solution.py:193
  54.3 6.8 %collective-permute-start.10 = (bf16[64,1024]{1,0:T(8,128)(2,1)S(1)}, bf16[64,1024]{1,0:T(8,128)(2,1)S(1)}, u32[]{:S(2)}, u32[]{:S(2)}) collective-permute-start(bf16[64,1024]{1,0:T(8,128)(2,1)S(1)} %shard_map.40), channel_id=1, source_target_pairs={{0,4},{1,5},{2,6},{3,7},{4,0},{5,1},{6,2},{7,3},{8,12},{9,13},{10,... | collective-permute-start | bytes 393224 | tf_op jit(solution)/shard_map/ppermute | solution.py:193
  55.5 5.6 %collective-permute-start.9 = (bf16[64,1024]{1,0:T(8,128)(2,1)S(1)}, bf16[64,1024]{1,0:T(8,128)(2,1)S(1)}, u32[]{:S(2)}, u32[]{:S(2)}) collective-permute-start(bf16[64,1024]{1,0:T(8,128)(2,1)S(1)} %shard_map.40), channel_id=1, source_target_pairs={{0,2},{1,3},{2,0},{3,1},{4,6},{5,7},{6,4},{7,5},{8,10},{9,11},{10,... | collective-permute-start | bytes 393224 | tf_op jit(solution)/shard_map/ppermute | solution.py:193
  61.1 3.3 %collective-permute-start.12 = (bf16[256,1024]{1,0:T(8,128)(2,1)S(1)}, bf16[256,1024]{1,0:T(8,128)(2,1)S(1)}, u32[]{:S(2)}, u32[]{:S(2)}) collective-permute-start(bf16[256,1024]{1,0:T(8,128)(2,1)S(1)} %pad_maximum_fusion.near), channel_id=1, source_target_pairs={{0,1},{1,0},{2,3},{3,2},{4,5},{5,4},{6,7},{7,6},{8,9},{9,8},{10,11... | collective-permute-start | bytes 1572872 | tf_op jit(solution)/shard_map/ppermute | solution.py:193
  65.0 2.0 %copy-start.4 = (bf16[512,1024]{1,0:T(8,128)(2,1)S(1)}, bf16[512,1024]{1,0:T(8,128)(2,1)}, u32[]{:S(2)}) copy-start(bf16[512,1024]{1,0:T(8,128)(2,1)} %copy-done.3) | copy-start | bytes 3145732
  69.2 8.4 %collective-permute-start.14 = (bf16[256,1152]{1,0:T(8,128)(2,1)S(1)}, bf16[256,1152]{1,0:T(8,128)(2,1)S(1)}, u32[]{:S(2)}, u32[]{:S(2)}) collective-permute-start(bf16[256,1152]{1,0:T(8,128)(2,1)S(1)} %get-tuple-element.53), channel_id=1, source_target_pairs={{0,1},{1,0},{2,3},{3,2},{4,5},{5,4},{6,7},{7,6},{8,9},{9,8},{10,11... | collective-permute-start | bytes 1769480 | tf_op jit(solution)/shard_map/ppermute | solution.py:193
  69.7 17.5 %collective-permute-start.18 = (bf16[512,512]{1,0:T(8,128)(2,1)S(1)}, bf16[512,512]{1,0:T(8,128)(2,1)S(1)}, u32[]{:S(2)}, u32[]{:S(2)}) collective-permute-start(bf16[512,512]{1,0:T(8,128)(2,1)S(1)} %get-tuple-element.46), channel_id=1, source_target_pairs={{8,0},{16,24},{9,1},{17,25},{10,2},{18,26},{11,3},{19,27},{12,4},{... | collective-permute-start | bytes 1572872 | tf_op jit(solution)/shard_map/ppermute | solution.py:265
  74.8 15.0 %collective-permute-start.19 = (bf16[512,512]{1,0:T(8,128)(2,1)S(1)}, bf16[512,512]{1,0:T(8,128)(2,1)S(1)}, u32[]{:S(2)}, u32[]{:S(2)}) collective-permute-start(bf16[512,512]{1,0:T(8,128)(2,1)S(1)} %get-tuple-element.47), channel_id=1, source_target_pairs={{8,16},{16,8},{9,17},{17,9},{10,18},{18,10},{11,19},{19,11},{12,20... | collective-permute-start | bytes 1572872 | tf_op jit(solution)/shard_map/ppermute | solution.py:265
  77.8 4.9 %collective-permute-start.15 = (bf16[64,1152]{1,0:T(8,128)(2,1)S(1)}, bf16[64,1152]{1,0:T(8,128)(2,1)S(1)}, u32[]{:S(2)}, u32[]{:S(2)}) collective-permute-start(bf16[64,1152]{1,0:T(8,128)(2,1)S(1)} %get-tuple-element.55), channel_id=1, source_target_pairs={{0,2},{1,3},{2,0},{3,1},{4,6},{5,7},{6,4},{7,5},{8,10},{9,11},{10,... | collective-permute-start | bytes 442376 | tf_op jit(solution)/shard_map/ppermute | solution.py:193
  79.1 4.9 %collective-permute-start.16 = (bf16[64,1152]{1,0:T(8,128)(2,1)S(1)}, bf16[64,1152]{1,0:T(8,128)(2,1)S(1)}, u32[]{:S(2)}, u32[]{:S(2)}) collective-permute-start(bf16[64,1152]{1,0:T(8,128)(2,1)S(1)} %get-tuple-element.56), channel_id=1, source_target_pairs={{0,4},{1,5},{2,6},{3,7},{4,0},{5,1},{6,2},{7,3},{8,12},{9,13},{10,... | collective-permute-start | bytes 442376 | tf_op jit(solution)/shard_map/ppermute | solution.py:193
  80.3 6.7 %collective-permute-start.17 = (bf16[64,1152]{1,0:T(8,128)(2,1)S(1)}, bf16[64,1152]{1,0:T(8,128)(2,1)S(1)}, u32[]{:S(2)}, u32[]{:S(2)}) collective-permute-start(bf16[64,1152]{1,0:T(8,128)(2,1)S(1)} %get-tuple-element.57), channel_id=1, source_target_pairs={{0,6},{1,7},{2,4},{3,5},{4,2},{5,3},{6,0},{7,1},{8,14},{9,15},{10,... | collective-permute-start | bytes 442376 | tf_op jit(solution)/shard_map/ppermute | solution.py:193
  82.7 17.7 %collective-permute-start.24 = (bf16[512,512]{1,0:T(8,128)(2,1)S(1)}, bf16[512,512]{1,0:T(8,128)(2,1)S(1)}, u32[]{:S(2)}, u32[]{:S(2)}) collective-permute-start(bf16[512,512]{1,0:T(8,128)(2,1)S(1)} %get-tuple-element.48), channel_id=1, source_target_pairs={{8,0},{16,24},{9,1},{17,25},{10,2},{18,26},{11,3},{19,27},{12,4},{... | collective-permute-start | bytes 1572872 | tf_op jit(solution)/shard_map/ppermute | solution.py:265
  84.0 16.4 %collective-permute-start.25 = (bf16[512,512]{1,0:T(8,128)(2,1)S(1)}, bf16[512,512]{1,0:T(8,128)(2,1)S(1)}, u32[]{:S(2)}, u32[]{:S(2)}) collective-permute-start(bf16[512,512]{1,0:T(8,128)(2,1)S(1)} %get-tuple-element.49), channel_id=1, source_target_pairs={{8,16},{16,8},{9,17},{17,9},{10,18},{18,10},{11,19},{19,11},{12,20... | collective-permute-start | bytes 1572872 | tf_op jit(solution)/shard_map/ppermute | solution.py:265
  89.8 7.3 %collective-permute-start.22 = (bf16[64,1152]{1,0:T(8,128)(2,1)S(1)}, bf16[64,1152]{1,0:T(8,128)(2,1)S(1)}, u32[]{:S(2)}, u32[]{:S(2)}) collective-permute-start(bf16[64,1152]{1,0:T(8,128)(2,1)S(1)} %shard_map.46), channel_id=1, source_target_pairs={{0,6},{1,7},{2,4},{3,5},{4,2},{5,3},{6,0},{7,1},{8,14},{9,15},{10,... | collective-permute-start | bytes 442376 | tf_op jit(solution)/shard_map/ppermute | solution.py:193
  91.9 5.2 %collective-permute-start.21 = (bf16[64,1152]{1,0:T(8,128)(2,1)S(1)}, bf16[64,1152]{1,0:T(8,128)(2,1)S(1)}, u32[]{:S(2)}, u32[]{:S(2)}) collective-permute-start(bf16[64,1152]{1,0:T(8,128)(2,1)S(1)} %shard_map.46), channel_id=1, source_target_pairs={{0,4},{1,5},{2,6},{3,7},{4,0},{5,1},{6,2},{7,3},{8,12},{9,13},{10,... | collective-permute-start | bytes 442376 | tf_op jit(solution)/shard_map/ppermute | solution.py:193
  92.1 4.9 %collective-permute-start.20 = (bf16[64,1152]{1,0:T(8,128)(2,1)S(1)}, bf16[64,1152]{1,0:T(8,128)(2,1)S(1)}, u32[]{:S(2)}, u32[]{:S(2)}) collective-permute-start(bf16[64,1152]{1,0:T(8,128)(2,1)S(1)} %shard_map.46), channel_id=1, source_target_pairs={{0,2},{1,3},{2,0},{3,1},{4,6},{5,7},{6,4},{7,5},{8,10},{9,11},{10,... | collective-permute-start | bytes 442376 | tf_op jit(solution)/shard_map/ppermute | solution.py:193
  97.1 4.8 %collective-permute-start.23 = (bf16[256,1152]{1,0:T(8,128)(2,1)S(1)}, bf16[256,1152]{1,0:T(8,128)(2,1)S(1)}, u32[]{:S(2)}, u32[]{:S(2)}) collective-permute-start(bf16[256,1152]{1,0:T(8,128)(2,1)S(1)} %constant_dynamic-update-slice_fusion.near), channel_id=1, source_target_pairs={{0,1},{1,0},{2,3},{3,2},{4,5},{5,4},{6,7},{7,6},{8,9},{9,8},{10,11... | collective-permute-start | bytes 1769480 | tf_op jit(solution)/shard_map/ppermute | solution.py:193
  100.4 2.1 %copy-start.5 = (bf16[512,1024]{1,0:T(8,128)(2,1)S(1)}, bf16[512,1024]{1,0:T(8,128)(2,1)}, u32[]{:S(2)}) copy-start(bf16[512,1024]{1,0:T(8,128)(2,1)} %other.1) | copy-start | bytes 3145732
  (5 other events, 5.4 us)

commit v6 on v5

v6 whole, which is shorter than its diff:
```python
import functools
import math

import jax
import jax.numpy as jnp
from jax import lax
from jax.experimental import pallas as pl
from jax.experimental.pallas import tpu as pltpu
from jax.sharding import PartitionSpec as P

NORM = 128


def kernel_call(body, outs, smem=0, scratch=4):
    def call(*args):
        space = [pltpu.SMEM] * smem + [pltpu.VMEM] * (len(args) - smem)
        return pl.pallas_call(
            body,
            out_shape=[jax.ShapeDtypeStruct(s, t) for s, t in outs],
            in_specs=[pl.BlockSpec(memory_space=m) for m in space],
            out_specs=[pl.BlockSpec(memory_space=pltpu.VMEM) for _ in outs],
            compiler_params=pltpu.CompilerParams(vmem_limit_bytes=scratch * 1024 * 1024),
            cost_estimate=pl.CostEstimate(flops=0, bytes_accessed=0, transcendentals=0),
        )(*args)

    return call


def gram(left, right):
    return lax.dot_general(
        left, right, (((1,), (1,)), ((), ())), preferred_element_type=jnp.float32
    )


def dot_t(left, right):
    return lax.dot_general(
        left, right, (((0,), (0,)), ((), ())), preferred_element_type=jnp.float32
    )


def dot(left, right):
    return jnp.dot(left, right, preferred_element_type=jnp.float32)


def centered_into(out, pieces, mean, square):
    at, total = 0, 0.0
    for piece in pieces:
        block = (piece[...].astype(jnp.float32) - mean).astype(jnp.bfloat16)
        out[at:at + block.shape[0], :] = block
        wide = block.astype(jnp.float32)
        total = total + jnp.sum(wide * wide, axis=0, keepdims=True)
        at += block.shape[0]
    square[...] = total


def high_low(n, like):
    high = n.astype(jnp.bfloat16).astype(jnp.float32)
    lane = lax.broadcasted_iota(jnp.int32, like, 1)
    return jnp.where(lane == 0, high, jnp.where(lane == 1, n - high, 0.0))


def turn_into(turned, order, block):
    eighth = block.shape[0] // 8
    for k in range(8):
        start = pl.multiple_of(order[k] * eighth, eighth)
        turned[k * eighth:(k + 1) * eighth, :] = block[pl.ds(start, eighth), :]


def own_kernel(order, z, mean, own, turned, square, kept, sent):
    rows = z.shape[0]
    eighth, half = rows // 8, rows // 2
    centered_into(own, [z], mean[...], square)
    turn_into(turned, order, own)
    inner = gram(turned[...], own[...])
    wide = turned[...].astype(jnp.float32)
    norm = jnp.sum(wide * wide, axis=1, keepdims=True)
    column = lax.broadcasted_iota(jnp.int32, (eighth, rows), 1)
    row = lax.broadcasted_iota(jnp.int32, (eighth, rows), 0)
    for k in range(8):
        here = slice(k * eighth, (k + 1) * eighth)
        off = jnp.where(column == row + order[k] * eighth, 0.0, inner[here])
        if k < 4:
            kept[here, :rows] = off
        else:
            sent[k * eighth - half:(k + 1) * eighth - half, :rows] = off.astype(jnp.bfloat16)
    lane = lax.broadcasted_iota(jnp.int32, (half, NORM), 1)
    kept[:, rows:] = jnp.where(lane == 0, norm[:half], 0.0)
    sent[:, rows:] = high_low(norm[half:], (half, NORM)).astype(jnp.bfloat16)


def first_kernel(order, turned, near_a, near_b, swapped_a, swapped_b, mean, *refs):
    near, swapped, near_square, swapped_square, kept, sent, turned_near = refs
    rows = near.shape[0]
    half = rows // 2
    centered_into(near, [near_a, near_b], mean[...], near_square)
    centered_into(swapped, [swapped_a, swapped_b], mean[...], swapped_square)
    turn_into(turned_near, order, near)
    for k, (left, right) in enumerate(((turned, near), (turned_near, swapped))):
        inner = gram(left[...], right[...])
        kept[:, k * rows:(k + 1) * rows] = inner[:half]
        sent[:, k * rows:(k + 1) * rows] = inner[half:].astype(jnp.bfloat16)


def second_kernel(middle, turned, swapped, swapped_square, end, mean, third, square, kept, sent):
    half = third.shape[0] // 2

    @pl.when(middle[0] == 1)
    def _():
        third[...] = swapped[...]
        square[...] = swapped_square[...]

    @pl.when(middle[0] == 0)
    def _():
        centered_into(third, [end], mean[...], square)

    inner = gram(turned[...], third[...])
    kept[...] = inner[:half]
    sent[...] = inner[half:].astype(jnp.bfloat16)


def with_norm(x, last):
    if not last:
        return x
    tail = x[:, last:]
    split = high_low(jnp.sum(tail, axis=1, keepdims=True), tail.shape)
    return jnp.concatenate([x[:, :last], split], axis=1)


def add_kernel(last, kept, got, mine, *out):
    total = with_norm(kept[...] + got[...].astype(jnp.float32), last)
    quarter = mine.shape[0]
    mine[...] = total[:quarter]
    for k, ref in enumerate(out, 1):
        ref[...] = total[k * quarter:(k + 1) * quarter].astype(jnp.bfloat16)


def total_kernel(last, mine, a, b, c, out):
    total = mine[...] + a[...].astype(jnp.float32)
    total = total + b[...].astype(jnp.float32) + c[...].astype(jnp.float32)
    out[...] = with_norm(total, last).astype(jnp.bfloat16)


def place_kernel(order, near, far, out):
    eighth = out.shape[0] // 8
    for k in range(4):
        here = slice(k * eighth, (k + 1) * eighth)
        out[pl.ds(pl.multiple_of(order[k] * eighth, eighth), eighth), :] = near[here, :]
        out[pl.ds(pl.multiple_of(order[4 + k] * eighth, eighth), eighth), :] = far[here, :]


def middle_kernel(inner, own, near, swapped, own_square, near_square, swapped_square, *outs):
    rows, width = own.shape
    with_own, with_swapped = inner[:, :rows], inner[:, rows:2 * rows]
    for k, (out, over) in enumerate((outs[:2], outs[2:])):
        here = slice(k * width // 2, (k + 1) * width // 2)
        outward = dot_t(with_own, own[:, here]) + dot(with_swapped, swapped[:, here])
        square = own_square[:, here] + swapped_square[:, here]
        outward = outward - near[:, here].astype(jnp.float32) * square
        out[...] = outward.astype(jnp.bfloat16)
        across = dot_t(with_swapped, near[:, here])
        across = across - swapped[:, here].astype(jnp.float32) * near_square[:, here]
        over[...] = across.astype(jnp.bfloat16)


def coefficient(total):
    return 2.0 * total / (25.0 * (total - 1)) / (total - 1)


def held_kernel(
    total, middle, inner, own, near, z, other,
    own_square, near_square, third_square, mean, spread, held,
):
    rows, width = own.shape
    norm = jnp.sum(inner[:, 3 * rows:].astype(jnp.float32), axis=1, keepdims=True)
    for k in range(4):
        here = slice(k * width // 4, (k + 1) * width // 4)
        anchor = z[:, here].astype(jnp.float32)
        deviation = jnp.sqrt(spread[:, here] / (total - 1) + 0.0001)
        centered = anchor - mean[:, here]
        hinge = jnp.where(deviation < 1.0, centered / deviation, 0.0)
        plain = anchor - other[:, here].astype(jnp.float32) - total / (4.0 * (total - 1)) * hinge
        square = own_square[:, here] + third_square[:, here]
        product = dot(inner[:, 2 * rows:3 * rows], own[:, here])
        product = product + own[:, here].astype(jnp.float32) * (norm - square)
        held[:, here] = plain + coefficient(total) * product

    @pl.when(middle[0] == 1)
    def _():
        for k in range(4):
            here = slice(k * width // 4, (k + 1) * width // 4)
            product = dot(inner[:, :rows], near[:, here])
            product = product - own[:, here].astype(jnp.float32) * near_square[:, here]
            held[:, here] = held[:, here] + coefficient(total) * product


def last_kernel(total, middle, inner, third, held, out_a, over_a, out_b, over_b, result):
    width = third.shape[1]
    for here, out, over in (
        (slice(0, width // 2), out_a, over_a), (slice(width // 2, width), out_b, over_b)
    ):
        product = dot(inner[...], third[:, here])

        @pl.when(middle[0] == 1)
        def _():
            sums = product + over[...].astype(jnp.float32)
            result[:, here] = held[:, here] + coefficient(total) * sums

        @pl.when(middle[0] == 0)
        def _():
            sums = product + out[...].astype(jnp.float32)
            result[:, here] = held[:, here] + coefficient(total) * sums


def to_partner(x, step):
    return lax.ppermute(x, "feat", [(i, i ^ step) for i in range(8)])


def halve(kept, sent, last=0):
    half, n = kept.shape
    part = (half // 4, n)
    return kernel_call(
        functools.partial(add_kernel, last), [(part, jnp.float32)] + [(part, jnp.bfloat16)] * 3
    )(kept, to_partner(sent, 1))


def scatter(mine, *out, last=0):
    got = [to_partner(x, 2 * k) for k, x in enumerate(out, 1)]
    return kernel_call(functools.partial(total_kernel, last), [(mine.shape, jnp.bfloat16)])(
        mine, *got
    )[0]


def gather_rows(x, order, *others):
    near = after(jnp.concatenate([x] + [to_partner(x, 2 * k) for k in (1, 2, 3)]), *others)
    far = to_partner(near, 1)
    shape = (8 * x.shape[0], x.shape[1])
    return kernel_call(place_kernel, [(shape, jnp.bfloat16)], smem=1)(order, near, far)[0]


def after(x, *others):
    return lax.optimization_barrier((x, *others))[0]


def by_line(z_anchor, z_other):
    rows, width = z_anchor.shape
    total = rows * 4
    plane = lax.axis_index("dp")
    middle = ((plane == 1) | (plane == 2)).astype(jnp.int32).reshape(1)
    order = lax.axis_index("feat") ^ jnp.array([0, 2, 4, 6, 1, 3, 5, 7], jnp.int32)
    inward, across, outward = [(0, 1), (3, 2)], [(1, 2), (2, 1)], [(1, 0), (2, 3)]
    half = rows // 2
    flat, block = ((1, width), jnp.float32), ((rows, width), jnp.bfloat16)

    near = [lax.ppermute(z_anchor[:half], "dp", inward)]
    swapped = [lax.ppermute(z_anchor[:half], "dp", across)]
    anchor = z_anchor.astype(jnp.float32)
    sums = jnp.sum(anchor, axis=0, keepdims=True)
    apart = anchor - sums / rows
    stats = jnp.concatenate([sums, jnp.sum(apart * apart, axis=0, keepdims=True)])
    all_stats = [stats] + [
        lax.ppermute(stats, "dp", [(i, (i + k) % 4) for i in range(4)]) for k in (1, 2, 3)
    ]
    later = after(z_anchor[half:], *all_stats)
    end = lax.ppermute(after(z_anchor, *all_stats, near[0], swapped[0]), "dp", [(0, 3), (3, 0)])
    near.append(lax.ppermute(later, "dp", inward))
    swapped.append(lax.ppermute(later, "dp", across))
    mean = (all_stats[0][:1] + all_stats[1][:1] + all_stats[2][:1] + all_stats[3][:1]) / total
    spread = 0.0
    for one in all_stats:
        shift = one[:1] / rows - mean
        spread = spread + (one[1:] + rows * shift * shift)

    def summands(n):
        return [((half, n), jnp.float32), ((half, n), jnp.bfloat16)]

    own, turned, own_square, kept, sent = kernel_call(
        own_kernel, [block, block, flat, *summands(rows + NORM)], smem=1, scratch=12
    )(order, after(z_anchor, near[0], swapped[0]), mean)
    with_own = scatter(*halve(kept, sent, rows), last=rows)
    near, swapped, near_square, swapped_square, kept, sent, _ = kernel_call(
        first_kernel,
        [block, block, flat, flat, *summands(2 * rows), block],
        smem=1, scratch=12,
    )(order, after(turned, with_own), *near, *swapped, mean)
    first = scatter(*halve(kept, sent))
    first = gather_rows(jnp.concatenate([first, with_own], axis=1), order, end)

    part = ((rows, width // 2), jnp.bfloat16)
    ready = kernel_call(middle_kernel, [part] * 4, scratch=12)(
        first, own, near, swapped, own_square, near_square, swapped_square
    )
    pushed = [lax.ppermute(x, "dp", p) for x, p in zip(ready, (outward, across) * 2)]

    third, third_square, kept, sent = kernel_call(
        second_kernel, [block, flat, *summands(rows)], smem=1, scratch=12
    )(middle, after(turned, *ready), swapped, swapped_square, end, mean)
    halved = halve(kept, sent)
    result = ((rows, width), jnp.float32)
    held = kernel_call(functools.partial(held_kernel, total), [result], smem=1, scratch=12)(
        middle, first, own, near, z_anchor, z_other,
        own_square, near_square, after(third_square, halved[0]), mean, spread,
    )[0]
    second = gather_rows(after(scatter(*halved), *pushed[:2], held), order)
    return kernel_call(functools.partial(last_kernel, total), [result], smem=1, scratch=12)(
        middle, second, third, held, *pushed
    )[0]


def by_gather(z_anchor, z_other):
    rows_here, width = z_anchor.shape
    groups = lax.axis_size("dp")
    total = rows_here * groups
    mine = lax.axis_index("dp") * rows_here
    column = lax.all_gather(z_anchor, "dp", axis=0, tiled=True).astype(jnp.float32)
    mean = jnp.sum(column, axis=0) / total
    centered_all = column - mean
    variance = jnp.sum(centered_all * centered_all, axis=0) / (total - 1)
    rounded_all = centered_all.astype(jnp.bfloat16)
    widened = rounded_all.astype(jnp.float32)
    own_square = jnp.sum(widened * widened, axis=0)
    rounded = lax.dynamic_slice_in_dim(rounded_all, mine, rows_here, 0)
    inner = lax.psum(gram(rounded, rounded_all).astype(jnp.bfloat16), "feat")
    product = jnp.dot(inner, rounded_all, preferred_element_type=jnp.float32)
    product = product - rounded.astype(jnp.float32) * own_square
    return finish(z_anchor, z_other, mean, variance, total, product)


def finish(z_anchor, z_other, mean, variance, total, product):
    coef = 2.0 * total / (25.0 * (total - 1)) / (total - 1)
    anchor = z_anchor.astype(jnp.float32)
    centered = anchor - mean
    deviation = jnp.sqrt(variance + 0.0001)
    hinge = jnp.where(deviation < 1.0, centered / deviation, 0.0)
    factor = total / (4.0 * (total - 1))
    return anchor - z_other.astype(jnp.float32) - factor * hinge + coef * product


def solution(mesh):
    placed = (P("dp", "feat"), P("dp", "feat"))
    in_line = mesh.shape["dp"] == 4 and mesh.shape["feat"] == 8
    return jax.shard_map(
        by_line if in_line else by_gather,
        mesh=mesh, in_specs=placed, out_specs=P("dp", "feat"), check_vma=False,
    )
```

time: 110 us -> 115 us (1.045)
  starting transfers between devices: 40.2 us -> 53 us
  other arithmetic: 5.08 us -> 0.67 us
  waiting for transfers between devices: 41.8 us -> 39.5 us
  Pallas kernels: 16.4 us -> 14.7 us
    ppermute x7 -> x9, starting transfers between devices: 16.9 us -> 25.6 us  [the longest x4 16.5 us: by_line(): lax.ppermute(x, 'dp', p)]
    ppermute x16 -> x20, waiting for transfers between devices: 22.4 us -> 30.8 us  [to_partner(): return lax.ppermute(x, 'feat', [(i, i ^ step) for i in range(8)])]
    ppermute x3, waiting for transfers between devices: 16.8 us -> 8.64 us  [by_line(): lax.ppermute(stats, 'dp', [(i, (i + k) % 4) for i in range(4)])]
    pallas_call x1 -> x0, Pallas kernels: 5.16 us -> none  [by_line(): pl.pallas_call(functools.partial(last_kernel, total), grid=(4,), out_shap...]
    ppermute x16 -> x20, starting transfers between devices: 17.9 us -> 22.9 us  [to_partner(): return lax.ppermute(x, 'feat', [(i, i ^ step) for i in range(8)])]
    pallas_call x11 -> x14, Pallas kernels: 11.2 us -> 14.7 us  [call(): pl.pallas_call(body, out_shape=[jax.ShapeDtypeStruct(s, t) for s, t in ou...]
    ppermute x7 -> x9, waiting for transfers between devices: 2.6 us -> 0.02 us  [the longest x4 0.01 us: by_line(): lax.ppermute(x, 'dp', p)]
    add x3 -> x0, other arithmetic: 2.05 us -> none  [the longest x1 1.75 us: by_line(): return held + coefficient(total) * pushed]
  transfers between devices with their start and end apart: 26 -> 32, of which waited for: 16 -> 21; matrix products, arithmetic and copies ran while one was open for 3% -> 1% of each run, Pallas kernels for 4% -> 5%
where the time goes in v6:
time: 115 us
  starting transfers between devices  53 us (46%)
  waiting for transfers between devices  39.5 us (34%)
  Pallas kernels  14.7 us (13%)
  local copies, waits for them, and re-layouts  6.66 us (6%)
    ppermute x20, waiting for transfers between devices, to_partner(): return lax.ppermute(x, 'feat', [(i, i ^ step) for i in range(8)])  30.8 us
    ppermute x20, starting transfers between devices, to_partner(): return lax.ppermute(x, 'feat', [(i, i ^ step) for i in range(8)])  22.9 us
    ppermute x4, starting transfers between devices, by_line(): lax.ppermute(x, 'dp', p)  16.5 us
    pallas_call x14, Pallas kernels, call(): pl.pallas_call(body, out_shape=[jax.ShapeDtypeStruct(s, t) for s, t in ou...  14.7 us
    ppermute x3, waiting for transfers between devices, by_line(): lax.ppermute(stats, 'dp', [(i, (i + k) % 4) for i in range(4)])  8.64 us
    unnamed x32, local copies, waits for them, and re-layouts  5.3 us
    ppermute x3, starting transfers between devices, by_line(): lax.ppermute(stats, 'dp', [(i, (i + k) % 4) for i in range(4)])  4.41 us
    ppermute x1, starting transfers between devices, by_line(): swapped = [lax.ppermute(z_anchor[:half], 'dp', across)]  3.2 us
  transfers between devices with their start and end apart: 32, of which 21 were waited for; matrix products, arithmetic and copies ran while one was open for 1% of the time, Pallas kernels for 5%

profile of v6, /device:TPU:9, one launch (start us, length us, event | category | flops | bytes accessed | tf_op | source)
XLA Modules:
  0.0 114.9 jit_solution(15012682108633036567)
XLA Ops:
  0.0 1.4 %fusion.9 = (bf16[256,1024]{1,0:T(8,128)(2,1)S(1)}, bf16[256,1024]{1,0:T(8,128)(2,1)S(1)}) fusion(bf16[512,1024]{1,0:T(8,128)(2,1)} %z.2), kind=kLoop, calls=%fused_computation.22 | loop fusion | bytes 2097152 | tf_op jit(solution)/shard_map/slice | solution.py:263
  1.4 3.2 %collective-permute-start.1 = (bf16[256,1024]{1,0:T(8,128)(2,1)S(1)}, bf16[256,1024]{1,0:T(8,128)(2,1)S(1)}, u32[]{:S(2)}, u32[]{:S(2)}) collective-permute-start(bf16[256,1024]{1,0:T(8,128)(2,1)S(1)} %get-tuple-element.86), channel_id=1, source_target_pairs={{8,16},{16,8},{9,17},{17,9},{10,18},{18,10},{11,19},{19,11},{12,20... | collective-permute-start | bytes 1572872 | tf_op jit(solution)/shard_map/ppermute | solution.py:255
  4.6 1.3 %collective-permute-start = (bf16[256,1024]{1,0:T(8,128)(2,1)S(1)}, bf16[256,1024]{1,0:T(8,128)(2,1)S(1)}, u32[]{:S(2)}, u32[]{:S(2)}) collective-permute-start(bf16[256,1024]{1,0:T(8,128)(2,1)S(1)} %get-tuple-element.86), channel_id=1, source_target_pairs={{0,8},{24,16},{1,9},{25,17},{2,10},{26,18},{3,11},{27,19},{4,12},{... | collective-permute-start | bytes 1572872 | tf_op jit(solution)/shard_map/ppermute | solution.py:254
  6.4 2.2 %collective-permute-start.4 = (f32[2,1024]{1,0:T(2,128)S(1)}, f32[2,1024]{1,0:T(2,128)S(1)}, u32[]{:S(2)}, u32[]{:S(2)}) collective-permute-start(f32[2,1024]{1,0:T(2,128)S(1)} %pad_maximum_fusion.3), channel_id=1, source_target_pairs={{0,24},{8,0},{16,8},{24,16},{1,25},{9,1},{17,9},{25,17},{2,26},{10... | collective-permute-start | bytes 24584 | tf_op jit(solution)/shard_map/ppermute | solution.py:261
  8.6 2.2 %collective-permute-start.2 = (f32[2,1024]{1,0:T(2,128)S(1)}, f32[2,1024]{1,0:T(2,128)S(1)}, u32[]{:S(2)}, u32[]{:S(2)}) collective-permute-start(f32[2,1024]{1,0:T(2,128)S(1)} %pad_maximum_fusion.3), channel_id=1, source_target_pairs={{0,8},{8,16},{16,24},{24,0},{1,9},{9,17},{17,25},{25,1},{2,10},{10... | collective-permute-start | bytes 24584 | tf_op jit(solution)/shard_map/ppermute | solution.py:261
  10.8 5.4 %collective-permute-done.4 = f32[2,1024]{1,0:T(2,128)S(1)} collective-permute-done((f32[2,1024]{1,0:T(2,128)S(1)}, f32[2,1024]{1,0:T(2,128)S(1)}, u32[]{:S(2)}, u32[]{:S(2)}) %collective-permute-start.4) | collective-permute-done | bytes 8224 | tf_op jit(solution)/shard_map/ppermute | solution.py:261
  16.2 2.7 %collective-permute-done.3 = f32[2,1024]{1,0:T(2,128)S(1)} collective-permute-done((f32[2,1024]{1,0:T(2,128)S(1)}, f32[2,1024]{1,0:T(2,128)S(1)}, u32[]{:S(2)}, u32[]{:S(2)}) %collective-permute-start.3) | collective-permute-done | bytes 8224 | tf_op jit(solution)/shard_map/ppermute | solution.py:261
  19.5 2.6 %collective-permute-start.10 = (bf16[256,1024]{1,0:T(8,128)(2,1)S(1)}, bf16[256,1024]{1,0:T(8,128)(2,1)S(1)}, u32[]{:S(2)}, u32[]{:S(2)}) collective-permute-start(bf16[256,1024]{1,0:T(8,128)(2,1)S(1)} %get-tuple-element.53), channel_id=1, source_target_pairs={{8,16},{16,8},{9,17},{17,9},{10,18},{18,10},{11,19},{19,11},{12,20... | collective-permute-start | bytes 1572872 | tf_op jit(solution)/shard_map/ppermute | solution.py:266
  22.1 1.3 %collective-permute-start.9 = (bf16[256,1024]{1,0:T(8,128)(2,1)S(1)}, bf16[256,1024]{1,0:T(8,128)(2,1)S(1)}, u32[]{:S(2)}, u32[]{:S(2)}) collective-permute-start(bf16[256,1024]{1,0:T(8,128)(2,1)S(1)} %get-tuple-element.53), channel_id=1, source_target_pairs={{0,8},{24,16},{1,9},{25,17},{2,10},{26,18},{3,11},{27,19},{4,12},{... | collective-permute-start | bytes 1572872 | tf_op jit(solution)/shard_map/ppermute | solution.py:265
  23.5 1.9 %shard_map.37 = (bf16[512,1024]{1,0:T(8,128)(2,1)S(1)}, bf16[512,1024]{1,0:T(8,128)(2,1)S(1)}, f32[1,1024]{1,0:T(1,128)S(1)}, f32[256,640]{1,0:T(8,128)S(1)}, bf16[256,640]{1,0:T(8,128)(2,1)S(1)}) custom-call(s32[8]{0:T(128)S(1)} %broadcast_xor_fusion.order, bf16[512,1024]{1,0:T(8,128)(2,1)S(1)} %copy-done, f32[1,1024]{1,0:T(1,128)S(1)} %get-tuple-element.84.mean), custom_call_target="tpu_custom_call" | custom-call | tf_op jit(solution)/shard_map/pallas_call | solution.py:17
  25.4 2.6 %collective-permute-start.5 = (bf16[256,640]{1,0:T(8,128)(2,1)S(1)}, bf16[256,640]{1,0:T(8,128)(2,1)S(1)}, u32[]{:S(2)}, u32[]{:S(2)}) collective-permute-start(bf16[256,640]{1,0:T(8,128)(2,1)S(1)} %get-tuple-element.47), channel_id=1, source_target_pairs={{0,1},{1,0},{2,3},{3,2},{4,5},{5,4},{6,7},{7,6},{8,9},{9,8},{10,11... | collective-permute-start | bytes 983048 | tf_op jit(solution)/shard_map/ppermute | solution.py:215
  29.4 1.3 %collective-permute-start.6 = (bf16[64,640]{1,0:T(8,128)(2,1)S(1)}, bf16[64,640]{1,0:T(8,128)(2,1)S(1)}, u32[]{:S(2)}, u32[]{:S(2)}) collective-permute-start(bf16[64,640]{1,0:T(8,128)(2,1)S(1)} %get-tuple-element.49), channel_id=1, source_target_pairs={{0,2},{1,3},{2,0},{3,1},{4,6},{5,7},{6,4},{7,5},{8,10},{9,11},{10,... | collective-permute-start | bytes 245768 | tf_op jit(solution)/shard_map/ppermute | solution.py:215
  34.3 1.8 %collective-permute-done.8.c = bf16[64,640]{1,0:T(8,128)(2,1)S(1)} collective-permute-done((bf16[64,640]{1,0:T(8,128)(2,1)S(1)}, bf16[64,640]{1,0:T(8,128)(2,1)S(1)}, u32[]{:S(2)}, u32[]{:S(2)}) %collective-permute-start.8) | collective-permute-done | bytes 81952 | tf_op jit(solution)/shard_map/ppermute | solution.py:215
  36.3 2.7 %shard_map.40 = (bf16[512,1024]{1,0:T(8,128)(2,1)S(1)}, bf16[512,1024]{1,0:T(8,128)(2,1)S(1)}, f32[1,1024]{1,0:T(1,128)S(1)}, f32[1,1024]{1,0:T(1,128)S(1)}, f32...) custom-call(s32[8]{0:T(128)S(1)} %broadcast_xor_fusion.order, ...), custom_call_target="tpu_custom_call" | custom-call | tf_op jit(solution)/shard_map/pallas_call | solution.py:17
  39.0 2.1 %collective-permute-start.11 = (bf16[256,1024]{1,0:T(8,128)(2,1)S(1)}, bf16[256,1024]{1,0:T(8,128)(2,1)S(1)}, u32[]{:S(2)}, u32[]{:S(2)}) collective-permute-start(bf16[256,1024]{1,0:T(8,128)(2,1)S(1)} %get-tuple-element.55), channel_id=1, source_target_pairs={{0,1},{1,0},{2,3},{3,2},{4,5},{5,4},{6,7},{7,6},{8,9},{9,8},{10,11... | collective-permute-start | bytes 1572872 | tf_op jit(solution)/shard_map/ppermute | solution.py:215
  45.4 2.1 %collective-permute-done.12.a = bf16[64,1024]{1,0:T(8,128)(2,1)S(1)} collective-permute-done((bf16[64,1024]{1,0:T(8,128)(2,1)S(1)}, bf16[64,1024]{1,0:T(8,128)(2,1)S(1)}, u32[]{:S(2)}, u32[]{:S(2)}) %collective-permute-start.12) | collective-permute-done | bytes 131104 | tf_op jit(solution)/shard_map/ppermute | solution.py:215
  48.3 2.7 %collective-permute-done.14.c = bf16[64,1024]{1,0:T(8,128)(2,1)S(1)} collective-permute-done((bf16[64,1024]{1,0:T(8,128)(2,1)S(1)}, bf16[64,1024]{1,0:T(8,128)(2,1)S(1)}, u32[]{:S(2)}, u32[]{:S(2)}) %collective-permute-start.14) | collective-permute-done | bytes 131104 | tf_op jit(solution)/shard_map/ppermute | solution.py:215
  51.1 1.5 %collective-permute-start.17 = (bf16[64,1664]{1,0:T(8,128)(2,1)S(1)}, bf16[64,1664]{1,0:T(8,128)(2,1)S(1)}, u32[]{:S(2)}, u32[]{:S(2)}) collective-permute-start(bf16[64,1664]{1,0:T(8,128)(2,1)S(1)} %pad_maximum_fusion.2), channel_id=1, source_target_pairs={{0,6},{1,7},{2,4},{3,5},{4,2},{5,3},{6,0},{7,1},{8,14},{9,15},{10,... | collective-permute-start | bytes 638984 | tf_op jit(solution)/shard_map/ppermute | solution.py:215
  53.8 3.4 %collective-permute-done.17 = bf16[64,1664]{1,0:T(8,128)(2,1)S(1)} collective-permute-done((bf16[64,1664]{1,0:T(8,128)(2,1)S(1)}, bf16[64,1664]{1,0:T(8,128)(2,1)S(1)}, u32[]{:S(2)}, u32[]{:S(2)}) %collective-permute-start.17) | collective-permute-done | bytes 213024 | tf_op jit(solution)/shard_map/ppermute | solution.py:215
  57.2 6.5 %collective-permute-done.16 = bf16[64,1664]{1,0:T(8,128)(2,1)S(1)} collective-permute-done((bf16[64,1664]{1,0:T(8,128)(2,1)S(1)}, bf16[64,1664]{1,0:T(8,128)(2,1)S(1)}, u32[]{:S(2)}, u32[]{:S(2)}) %collective-permute-start.16) | collective-permute-done | bytes 213024 | tf_op jit(solution)/shard_map/ppermute | solution.py:215
  64.7 2.0 %collective-permute-done.19.far = bf16[256,1664]{1,0:T(8,128)(2,1)S(1)} collective-permute-done((bf16[256,1664]{1,0:T(8,128)(2,1)S(1)}, bf16[256,1664]{1,0:T(8,128)(2,1)S(1)}, u32[]{:S(2)}, u32[]{:S(2)}) %collective-permute-start.19) | collective-permute-done | bytes 852000 | tf_op jit(solution)/shard_map/ppermute | solution.py:215
  67.4 1.8 %shard_map.44 = (bf16[512,512]{1,0:T(8,128)(2,1)}, bf16[512,512]{1,0:T(8,128)(2,1)}, bf16[512,512]{1,0:T(8,128)(2,1)S(1)}, bf16[512,512]{1,0:T(8,128)(2,1)S(1)}) custom-call(bf16[512,1664]{1,0:T(8,128)(2,1)S(1)} %shard_map.43.inner, bf16[512,1024]{1,0:T(8,128)(2,1)S(1)} %get-tuple-element.62.own, bf16[512,1024]{1,0:T(8,128)(2,1)S(1)} %get-tuple-element.63.near, ...), custom_call_target="tpu_custom_call" | custom-call | tf_op jit(solution)/shard_map/pallas_call | solution.py:17
  70.8 9.9 %collective-permute-start.24 = (bf16[512,512]{1,0:T(8,128)(2,1)}, bf16[512,512]{1,0:T(8,128)(2,1)S(1)}, u32[]{:S(2)}, u32[]{:S(2)}) collective-permute-start(bf16[512,512]{1,0:T(8,128)(2,1)} %get-tuple-element.68), channel_id=1, source_target_pairs={{8,0},{16,24},{9,1},{17,25},{10,2},{18,26},{11,3},{19,27},{12,4},{... | collective-permute-start | bytes 1572872 | tf_op jit(solution)/shard_map/ppermute | solution.py:292
  80.7 2.3 %collective-permute-start.25 = (bf16[512,512]{1,0:T(8,128)(2,1)}, bf16[512,512]{1,0:T(8,128)(2,1)}, u32[]{:S(2)}, u32[]{:S(2)}) collective-permute-start(bf16[512,512]{1,0:T(8,128)(2,1)} %get-tuple-element.69), channel_id=1, source_target_pairs={{8,16},{16,8},{9,17},{17,9},{10,18},{18,10},{11,19},{19,11},{12,20... | collective-permute-start | bytes 1572872 | tf_op jit(solution)/shard_map/ppermute | solution.py:292
  90.7 1.3 %collective-permute-start.30 = (bf16[512,512]{1,0:T(8,128)(2,1)}, bf16[512,512]{1,0:T(8,128)(2,1)S(1)}, u32[]{:S(2)}, u32[]{:S(2)}) collective-permute-start(bf16[512,512]{1,0:T(8,128)(2,1)} %copy-done.14), channel_id=1, source_target_pairs={{8,0},{16,24},{9,1},{17,25},{10,2},{18,26},{11,3},{19,27},{12,4},{... | collective-permute-start | bytes 1572872 | tf_op jit(solution)/shard_map/ppermute | solution.py:292
  92.0 1.4 %collective-permute-done.21.a = bf16[64,512]{1,0:T(8,128)(2,1)S(1)} collective-permute-done((bf16[64,512]{1,0:T(8,128)(2,1)S(1)}, bf16[64,512]{1,0:T(8,128)(2,1)S(1)}, u32[]{:S(2)}, u32[]{:S(2)}) %collective-permute-start.21) | collective-permute-done | bytes 65568 | tf_op jit(solution)/shard_map/ppermute | solution.py:215
  93.4 3.0 %collective-permute-start.31 = (bf16[512,512]{1,0:T(8,128)(2,1)S(1)}, bf16[512,512]{1,0:T(8,128)(2,1)S(1)}, u32[]{:S(2)}, u32[]{:S(2)}) collective-permute-start(bf16[512,512]{1,0:T(8,128)(2,1)S(1)} %copy-done.13), channel_id=1, source_target_pairs={{8,16},{16,8},{9,17},{17,9},{10,18},{18,10},{11,19},{19,11},{12,20... | collective-permute-start | bytes 1572872 | tf_op jit(solution)/shard_map/ppermute | solution.py:292
  97.0 2.1 %shard_map.48.held = f32[512,1024]{1,0:T(8,128)S(1)} custom-call(s32[1]{0:T(128)} %bitcast.middle, bf16[512,1664]{1,0:T(8,128)(2,1)S(1)} %shard_map.43.inner, bf16[512,1024]{1,0:T(8,128)(2,1)S(1)} %copy-done.2, bf16[512,1024]{1,0:T(8,128)(2,1)S(1)} %copy-done.4, bf16[512,1024]{1,0:T(8,128)(2,1)S(1)} %copy-done, bf16[512,1024]{1,0:T(8,128)(2,1)S(1)} %copy-done.9, ...), custom_call_target="tpu_custom_call" | custom-call | tf_op jit(solution)/shard_map/pallas_call | solution.py:17
  99.1 1.3 %collective-permute-done.23.c = bf16[64,512]{1,0:T(8,128)(2,1)S(1)} collective-permute-done((bf16[64,512]{1,0:T(8,128)(2,1)S(1)}, bf16[64,512]{1,0:T(8,128)(2,1)S(1)}, u32[]{:S(2)}, u32[]{:S(2)}) %collective-permute-start.23) | collective-permute-done | bytes 65568 | tf_op jit(solution)/shard_map/ppermute | solution.py:215
  103.2 1.5 %collective-permute-done.28 = bf16[64,512]{1,0:T(8,128)(2,1)S(1)} collective-permute-done((bf16[64,512]{1,0:T(8,128)(2,1)S(1)}, bf16[64,512]{1,0:T(8,128)(2,1)S(1)}, u32[]{:S(2)}, u32[]{:S(2)}) %collective-permute-start.28) | collective-permute-done | bytes 65568 | tf_op jit(solution)/shard_map/ppermute | solution.py:215
  105.5 4.0 %collective-permute-start.29 = (bf16[256,512]{1,0:T(8,128)(2,1)S(1)}, bf16[256,512]{1,0:T(8,128)(2,1)S(1)}, u32[]{:S(2)}, u32[]{:S(2)}) collective-permute-start(bf16[256,512]{1,0:T(8,128)(2,1)S(1)} %pad_maximum_fusion.1.near), channel_id=1, source_target_pairs={{0,1},{1,0},{2,3},{3,2},{4,5},{5,4},{6,7},{7,6},{8,9},{9,8},{10,11... | collective-permute-start | bytes 786440 | tf_op jit(solution)/shard_map/ppermute | solution.py:215
  111.3 3.6 %shard_map.50 = f32[512,1024]{1,0:T(8,128)} custom-call(s32[1]{0:T(128)} %bitcast.middle, bf16[512,512]{1,0:T(8,128)(2,1)S(1)} %shard_map.49.inner, bf16[512,1024]{1,0:T(8,128)(2,1)S(1)} %get-tuple-element.82.third, f32[512,1024]{1,0:T(8,128)S(1)} %shard_map.48.held, bf16[512,512]{1,0:T(8,128)(2,1)S(1)} %collective-permute-done.24.out_a, ...), custom_call_target="tpu_custom_call" | custom-call | tf_op jit(solution)/shard_map/pallas_call | solution.py:17
  (88 shorter events, 29.5 us)
Async XLA Ops:
  1.4 22.1 %collective-permute-start.1 = (bf16[256,1024]{1,0:T(8,128)(2,1)S(1)}, bf16[256,1024]{1,0:T(8,128)(2,1)S(1)}, u32[]{:S(2)}, u32[]{:S(2)}) collective-permute-start(bf16[256,1024]{1,0:T(8,128)(2,1)S(1)} %get-tuple-element.86), channel_id=1, source_target_pairs={{8,16},{16,8},{9,17},{17,9},{10,18},{18,10},{11,19},{19,11},{12,20... | collective-permute-start | bytes 1572872 | tf_op jit(solution)/shard_map/ppermute | solution.py:255
  4.6 18.9 %collective-permute-start = (bf16[256,1024]{1,0:T(8,128)(2,1)S(1)}, bf16[256,1024]{1,0:T(8,128)(2,1)S(1)}, u32[]{:S(2)}, u32[]{:S(2)}) collective-permute-start(bf16[256,1024]{1,0:T(8,128)(2,1)S(1)} %get-tuple-element.86), channel_id=1, source_target_pairs={{0,8},{24,16},{1,9},{25,17},{2,10},{26,18},{3,11},{27,19},{4,12},{... | collective-permute-start | bytes 1572872 | tf_op jit(solution)/shard_map/ppermute | solution.py:254
  6.4 9.8 %collective-permute-start.4 = (f32[2,1024]{1,0:T(2,128)S(1)}, f32[2,1024]{1,0:T(2,128)S(1)}, u32[]{:S(2)}, u32[]{:S(2)}) collective-permute-start(f32[2,1024]{1,0:T(2,128)S(1)} %pad_maximum_fusion.3), channel_id=1, source_target_pairs={{0,24},{8,0},{16,8},{24,16},{1,25},{9,1},{17,9},{25,17},{2,26},{10... | collective-permute-start | bytes 24584 | tf_op jit(solution)/shard_map/ppermute | solution.py:261
  8.6 10.3 %collective-permute-start.3 = (f32[2,1024]{1,0:T(2,128)S(1)}, f32[2,1024]{1,0:T(2,128)S(1)}, u32[]{:S(2)}, u32[]{:S(2)}) collective-permute-start(f32[2,1024]{1,0:T(2,128)S(1)} %pad_maximum_fusion.3), channel_id=1, source_target_pairs={{0,16},{8,24},{16,0},{24,8},{1,17},{9,25},{17,1},{25,9},{2,18},{10... | collective-permute-start | bytes 24584 | tf_op jit(solution)/shard_map/ppermute | solution.py:261
  8.6 10.9 %collective-permute-start.2 = (f32[2,1024]{1,0:T(2,128)S(1)}, f32[2,1024]{1,0:T(2,128)S(1)}, u32[]{:S(2)}, u32[]{:S(2)}) collective-permute-start(f32[2,1024]{1,0:T(2,128)S(1)} %pad_maximum_fusion.3), channel_id=1, source_target_pairs={{0,8},{8,16},{16,24},{24,0},{1,9},{9,17},{17,25},{25,1},{2,10},{10... | collective-permute-start | bytes 24584 | tf_op jit(solution)/shard_map/ppermute | solution.py:261
  19.5 16.8 %collective-permute-start.10 = (bf16[256,1024]{1,0:T(8,128)(2,1)S(1)}, bf16[256,1024]{1,0:T(8,128)(2,1)S(1)}, u32[]{:S(2)}, u32[]{:S(2)}) collective-permute-start(bf16[256,1024]{1,0:T(8,128)(2,1)S(1)} %get-tuple-element.53), channel_id=1, source_target_pairs={{8,16},{16,8},{9,17},{17,9},{10,18},{18,10},{11,19},{19,11},{12,20... | collective-permute-start | bytes 1572872 | tf_op jit(solution)/shard_map/ppermute | solution.py:266
  22.1 14.2 %collective-permute-start.9 = (bf16[256,1024]{1,0:T(8,128)(2,1)S(1)}, bf16[256,1024]{1,0:T(8,128)(2,1)S(1)}, u32[]{:S(2)}, u32[]{:S(2)}) collective-permute-start(bf16[256,1024]{1,0:T(8,128)(2,1)S(1)} %get-tuple-element.53), channel_id=1, source_target_pairs={{0,8},{24,16},{1,9},{25,17},{2,10},{26,18},{3,11},{27,19},{4,12},{... | collective-permute-start | bytes 1572872 | tf_op jit(solution)/shard_map/ppermute | solution.py:265
  25.4 3.8 %collective-permute-start.5 = (bf16[256,640]{1,0:T(8,128)(2,1)S(1)}, bf16[256,640]{1,0:T(8,128)(2,1)S(1)}, u32[]{:S(2)}, u32[]{:S(2)}) collective-permute-start(bf16[256,640]{1,0:T(8,128)(2,1)S(1)} %get-tuple-element.47), channel_id=1, source_target_pairs={{0,1},{1,0},{2,3},{3,2},{4,5},{5,4},{6,7},{7,6},{8,9},{9,8},{10,11... | collective-permute-start | bytes 983048 | tf_op jit(solution)/shard_map/ppermute | solution.py:215
  29.4 3.7 %collective-permute-start.6 = (bf16[64,640]{1,0:T(8,128)(2,1)S(1)}, bf16[64,640]{1,0:T(8,128)(2,1)S(1)}, u32[]{:S(2)}, u32[]{:S(2)}) collective-permute-start(bf16[64,640]{1,0:T(8,128)(2,1)S(1)} %get-tuple-element.49), channel_id=1, source_target_pairs={{0,2},{1,3},{2,0},{3,1},{4,6},{5,7},{6,4},{7,5},{8,10},{9,11},{10,... | collective-permute-start | bytes 245768 | tf_op jit(solution)/shard_map/ppermute | solution.py:215
  30.7 3.6 %collective-permute-start.7 = (bf16[64,640]{1,0:T(8,128)(2,1)S(1)}, bf16[64,640]{1,0:T(8,128)(2,1)S(1)}, u32[]{:S(2)}, u32[]{:S(2)}) collective-permute-start(bf16[64,640]{1,0:T(8,128)(2,1)S(1)} %get-tuple-element.50), channel_id=1, source_target_pairs={{0,4},{1,5},{2,6},{3,7},{4,0},{5,1},{6,2},{7,3},{8,12},{9,13},{10,... | collective-permute-start | bytes 245768 | tf_op jit(solution)/shard_map/ppermute | solution.py:215
  31.9 4.2 %collective-permute-start.8 = (bf16[64,640]{1,0:T(8,128)(2,1)S(1)}, bf16[64,640]{1,0:T(8,128)(2,1)S(1)}, u32[]{:S(2)}, u32[]{:S(2)}) collective-permute-start(bf16[64,640]{1,0:T(8,128)(2,1)S(1)} %get-tuple-element.51), channel_id=1, source_target_pairs={{0,6},{1,7},{2,4},{3,5},{4,2},{5,3},{6,0},{7,1},{8,14},{9,15},{10,... | collective-permute-start | bytes 245768 | tf_op jit(solution)/shard_map/ppermute | solution.py:215
  39.0 3.6 %collective-permute-start.11 = (bf16[256,1024]{1,0:T(8,128)(2,1)S(1)}, bf16[256,1024]{1,0:T(8,128)(2,1)S(1)}, u32[]{:S(2)}, u32[]{:S(2)}) collective-permute-start(bf16[256,1024]{1,0:T(8,128)(2,1)S(1)} %get-tuple-element.55), channel_id=1, source_target_pairs={{0,1},{1,0},{2,3},{3,2},{4,5},{5,4},{6,7},{7,6},{8,9},{9,8},{10,11... | collective-permute-start | bytes 1572872 | tf_op jit(solution)/shard_map/ppermute | solution.py:215
  41.0 22.8 %collective-permute-start.18 = (bf16[512,1024]{1,0:T(8,128)(2,1)S(1)}, bf16[512,1024]{1,0:T(8,128)(2,1)S(1)}, u32[]{:S(2)}, u32[]{:S(2)}) collective-permute-start(bf16[512,1024]{1,0:T(8,128)(2,1)S(1)} %copy-done), channel_id=1, source_target_pairs={{0,24},{24,0},{1,25},{25,1},{2,26},{26,2},{3,27},{27,3},{4,28},{28... | collective-permute-start | bytes 3145736 | tf_op jit(solution)/shard_map/ppermute | solution.py:264
  42.7 4.8 %collective-permute-start.12 = (bf16[64,1024]{1,0:T(8,128)(2,1)S(1)}, bf16[64,1024]{1,0:T(8,128)(2,1)S(1)}, u32[]{:S(2)}, u32[]{:S(2)}) collective-permute-start(bf16[64,1024]{1,0:T(8,128)(2,1)S(1)} %get-tuple-element.57), channel_id=1, source_target_pairs={{0,2},{1,3},{2,0},{3,1},{4,6},{5,7},{6,4},{7,5},{8,10},{9,11},{10,... | collective-permute-start | bytes 393224 | tf_op jit(solution)/shard_map/ppermute | solution.py:215
  43.9 4.4 %collective-permute-start.13 = (bf16[64,1024]{1,0:T(8,128)(2,1)S(1)}, bf16[64,1024]{1,0:T(8,128)(2,1)S(1)}, u32[]{:S(2)}, u32[]{:S(2)}) collective-permute-start(bf16[64,1024]{1,0:T(8,128)(2,1)S(1)} %get-tuple-element.58), channel_id=1, source_target_pairs={{0,4},{1,5},{2,6},{3,7},{4,0},{5,1},{6,2},{7,3},{8,12},{9,13},{10,... | collective-permute-start | bytes 393224 | tf_op jit(solution)/shard_map/ppermute | solution.py:215
  45.2 5.8 %collective-permute-start.14 = (bf16[64,1024]{1,0:T(8,128)(2,1)S(1)}, bf16[64,1024]{1,0:T(8,128)(2,1)S(1)}, u32[]{:S(2)}, u32[]{:S(2)}) collective-permute-start(bf16[64,1024]{1,0:T(8,128)(2,1)S(1)} %get-tuple-element.59), channel_id=1, source_target_pairs={{0,6},{1,7},{2,4},{3,5},{4,2},{5,3},{6,0},{7,1},{8,14},{9,15},{10,... | collective-permute-start | bytes 393224 | tf_op jit(solution)/shard_map/ppermute | solution.py:215
  51.1 6.1 %collective-permute-start.17 = (bf16[64,1664]{1,0:T(8,128)(2,1)S(1)}, bf16[64,1664]{1,0:T(8,128)(2,1)S(1)}, u32[]{:S(2)}, u32[]{:S(2)}) collective-permute-start(bf16[64,1664]{1,0:T(8,128)(2,1)S(1)} %pad_maximum_fusion.2), channel_id=1, source_target_pairs={{0,6},{1,7},{2,4},{3,5},{4,2},{5,3},{6,0},{7,1},{8,14},{9,15},{10,... | collective-permute-start | bytes 638984 | tf_op jit(solution)/shard_map/ppermute | solution.py:215
  52.6 11.2 %collective-permute-start.16 = (bf16[64,1664]{1,0:T(8,128)(2,1)S(1)}, bf16[64,1664]{1,0:T(8,128)(2,1)S(1)}, u32[]{:S(2)}, u32[]{:S(2)}) collective-permute-start(bf16[64,1664]{1,0:T(8,128)(2,1)S(1)} %pad_maximum_fusion.2), channel_id=1, source_target_pairs={{0,4},{1,5},{2,6},{3,7},{4,0},{5,1},{6,2},{7,3},{8,12},{9,13},{10,... | collective-permute-start | bytes 638984 | tf_op jit(solution)/shard_map/ppermute | solution.py:215
  53.8 10.0 %collective-permute-start.15 = (bf16[64,1664]{1,0:T(8,128)(2,1)S(1)}, bf16[64,1664]{1,0:T(8,128)(2,1)S(1)}, u32[]{:S(2)}, u32[]{:S(2)}) collective-permute-start(bf16[64,1664]{1,0:T(8,128)(2,1)S(1)} %pad_maximum_fusion.2), channel_id=1, source_target_pairs={{0,2},{1,3},{2,0},{3,1},{4,6},{5,7},{6,4},{7,5},{8,10},{9,11},{10,... | collective-permute-start | bytes 638984 | tf_op jit(solution)/shard_map/ppermute | solution.py:215
  63.8 2.9 %collective-permute-start.19 = (bf16[256,1664]{1,0:T(8,128)(2,1)S(1)}, bf16[256,1664]{1,0:T(8,128)(2,1)S(1)}, u32[]{:S(2)}, u32[]{:S(2)}) collective-permute-start(bf16[256,1664]{1,0:T(8,128)(2,1)S(1)} %pad_maximum_fusion.near), channel_id=1, source_target_pairs={{0,1},{1,0},{2,3},{3,2},{4,5},{5,4},{6,7},{7,6},{8,9},{9,8},{10,11... | collective-permute-start | bytes 2555912 | tf_op jit(solution)/shard_map/ppermute | solution.py:215
  70.8 29.7 %collective-permute-start.24 = (bf16[512,512]{1,0:T(8,128)(2,1)}, bf16[512,512]{1,0:T(8,128)(2,1)S(1)}, u32[]{:S(2)}, u32[]{:S(2)}) collective-permute-start(bf16[512,512]{1,0:T(8,128)(2,1)} %get-tuple-element.68), channel_id=1, source_target_pairs={{8,0},{16,24},{9,1},{17,25},{10,2},{18,26},{11,3},{19,27},{12,4},{... | collective-permute-start | bytes 1572872 | tf_op jit(solution)/shard_map/ppermute | solution.py:292
  80.7 19.8 %collective-permute-start.25 = (bf16[512,512]{1,0:T(8,128)(2,1)}, bf16[512,512]{1,0:T(8,128)(2,1)}, u32[]{:S(2)}, u32[]{:S(2)}) collective-permute-start(bf16[512,512]{1,0:T(8,128)(2,1)} %get-tuple-element.69), channel_id=1, source_target_pairs={{8,16},{16,8},{9,17},{17,9},{10,18},{18,10},{11,19},{19,11},{12,20... | collective-permute-start | bytes 1572872 | tf_op jit(solution)/shard_map/ppermute | solution.py:292
  87.6 2.2 %collective-permute-start.20 = (bf16[256,512]{1,0:T(8,128)(2,1)S(1)}, bf16[256,512]{1,0:T(8,128)(2,1)S(1)}, u32[]{:S(2)}, u32[]{:S(2)}) collective-permute-start(bf16[256,512]{1,0:T(8,128)(2,1)S(1)} %get-tuple-element.74), channel_id=1, source_target_pairs={{0,1},{1,0},{2,3},{3,2},{4,5},{5,4},{6,7},{7,6},{8,9},{9,8},{10,11... | collective-permute-start | bytes 786440 | tf_op jit(solution)/shard_map/ppermute | solution.py:215
  89.8 3.6 %collective-permute-start.21 = (bf16[64,512]{1,0:T(8,128)(2,1)S(1)}, bf16[64,512]{1,0:T(8,128)(2,1)S(1)}, u32[]{:S(2)}, u32[]{:S(2)}) collective-permute-start(bf16[64,512]{1,0:T(8,128)(2,1)S(1)} %get-tuple-element.76), channel_id=1, source_target_pairs={{0,2},{1,3},{2,0},{3,1},{4,6},{5,7},{6,4},{7,5},{8,10},{9,11},{10,... | collective-permute-start | bytes 196616 | tf_op jit(solution)/shard_map/ppermute | solution.py:215
  90.1 6.3 %collective-permute-start.22 = (bf16[64,512]{1,0:T(8,128)(2,1)S(1)}, bf16[64,512]{1,0:T(8,128)(2,1)S(1)}, u32[]{:S(2)}, u32[]{:S(2)}) collective-permute-start(bf16[64,512]{1,0:T(8,128)(2,1)S(1)} %get-tuple-element.77), channel_id=1, source_target_pairs={{0,4},{1,5},{2,6},{3,7},{4,0},{5,1},{6,2},{7,3},{8,12},{9,13},{10,... | collective-permute-start | bytes 196616 | tf_op jit(solution)/shard_map/ppermute | solution.py:215
  90.7 20.6 %collective-permute-start.30 = (bf16[512,512]{1,0:T(8,128)(2,1)}, bf16[512,512]{1,0:T(8,128)(2,1)S(1)}, u32[]{:S(2)}, u32[]{:S(2)}) collective-permute-start(bf16[512,512]{1,0:T(8,128)(2,1)} %copy-done.14), channel_id=1, source_target_pairs={{8,0},{16,24},{9,1},{17,25},{10,2},{18,26},{11,3},{19,27},{12,4},{... | collective-permute-start | bytes 1572872 | tf_op jit(solution)/shard_map/ppermute | solution.py:292
  93.4 17.9 %collective-permute-start.31 = (bf16[512,512]{1,0:T(8,128)(2,1)S(1)}, bf16[512,512]{1,0:T(8,128)(2,1)S(1)}, u32[]{:S(2)}, u32[]{:S(2)}) collective-permute-start(bf16[512,512]{1,0:T(8,128)(2,1)S(1)} %copy-done.13), channel_id=1, source_target_pairs={{8,16},{16,8},{9,17},{17,9},{10,18},{18,10},{11,19},{19,11},{12,20... | collective-permute-start | bytes 1572872 | tf_op jit(solution)/shard_map/ppermute | solution.py:292
  96.4 4.1 %collective-permute-start.23 = (bf16[64,512]{1,0:T(8,128)(2,1)S(1)}, bf16[64,512]{1,0:T(8,128)(2,1)S(1)}, u32[]{:S(2)}, u32[]{:S(2)}) collective-permute-start(bf16[64,512]{1,0:T(8,128)(2,1)S(1)} %get-tuple-element.78), channel_id=1, source_target_pairs={{0,6},{1,7},{2,4},{3,5},{4,2},{5,3},{6,0},{7,1},{8,14},{9,15},{10,... | collective-permute-start | bytes 196616 | tf_op jit(solution)/shard_map/ppermute | solution.py:215
  100.5 4.2 %collective-permute-start.28 = (bf16[64,512]{1,0:T(8,128)(2,1)S(1)}, bf16[64,512]{1,0:T(8,128)(2,1)S(1)}, u32[]{:S(2)}, u32[]{:S(2)}) collective-permute-start(bf16[64,512]{1,0:T(8,128)(2,1)S(1)} %shard_map.47), channel_id=1, source_target_pairs={{0,6},{1,7},{2,4},{3,5},{4,2},{5,3},{6,0},{7,1},{8,14},{9,15},{10,... | collective-permute-start | bytes 196616 | tf_op jit(solution)/shard_map/ppermute | solution.py:215
  101.1 4.1 %collective-permute-start.27 = (bf16[64,512]{1,0:T(8,128)(2,1)S(1)}, bf16[64,512]{1,0:T(8,128)(2,1)S(1)}, u32[]{:S(2)}, u32[]{:S(2)}) collective-permute-start(bf16[64,512]{1,0:T(8,128)(2,1)S(1)} %shard_map.47), channel_id=1, source_target_pairs={{0,4},{1,5},{2,6},{3,7},{4,0},{5,1},{6,2},{7,3},{8,12},{9,13},{10,... | collective-permute-start | bytes 196616 | tf_op jit(solution)/shard_map/ppermute | solution.py:215
  102.0 3.4 %collective-permute-start.26 = (bf16[64,512]{1,0:T(8,128)(2,1)S(1)}, bf16[64,512]{1,0:T(8,128)(2,1)S(1)}, u32[]{:S(2)}, u32[]{:S(2)}) collective-permute-start(bf16[64,512]{1,0:T(8,128)(2,1)S(1)} %shard_map.47), channel_id=1, source_target_pairs={{0,2},{1,3},{2,0},{3,1},{4,6},{5,7},{6,4},{7,5},{8,10},{9,11},{10,... | collective-permute-start | bytes 196616 | tf_op jit(solution)/shard_map/ppermute | solution.py:215
  105.5 5.2 %collective-permute-start.29 = (bf16[256,512]{1,0:T(8,128)(2,1)S(1)}, bf16[256,512]{1,0:T(8,128)(2,1)S(1)}, u32[]{:S(2)}, u32[]{:S(2)}) collective-permute-start(bf16[256,512]{1,0:T(8,128)(2,1)S(1)} %pad_maximum_fusion.1.near), channel_id=1, source_target_pairs={{0,1},{1,0},{2,3},{3,2},{4,5},{5,4},{6,7},{7,6},{8,9},{9,8},{10,11... | collective-permute-start | bytes 786440 | tf_op jit(solution)/shard_map/ppermute | solution.py:215
  (16 other events, 175.4 us)

commit v7 on v6

--- a/solution.py
+++ b/solution.py
@@ -42,15 +42,10 @@
     return jnp.dot(left, right, preferred_element_type=jnp.float32)
 
 
-def centered_into(out, pieces, mean, square):
-    at, total = 0, 0.0
-    for piece in pieces:
-        block = (piece[...].astype(jnp.float32) - mean).astype(jnp.bfloat16)
-        out[at:at + block.shape[0], :] = block
-        wide = block.astype(jnp.float32)
-        total = total + jnp.sum(wide * wide, axis=0, keepdims=True)
-        at += block.shape[0]
-    square[...] = total
+def centered_into(out, block, mean, square):
+    out[...] = (block[...].astype(jnp.float32) - mean).astype(jnp.bfloat16)
+    wide = out[...].astype(jnp.float32)
+    square[...] = jnp.sum(wide * wide, axis=0, keepdims=True)
 
 
 def high_low(n, like):
@@ -69,7 +64,7 @@
 def own_kernel(order, z, mean, own, turned, square, kept, sent):
     rows = z.shape[0]
     eighth, half = rows // 8, rows // 2
-    centered_into(own, [z], mean[...], square)
+    centered_into(own, z, mean[...], square)
     turn_into(turned, order, own)
     inner = gram(turned[...], own[...])
     wide = turned[...].astype(jnp.float32)
@@ -88,17 +83,25 @@
     sent[:, rows:] = high_low(norm[half:], (half, NORM)).astype(jnp.bfloat16)
 
 
-def first_kernel(order, turned, near_a, near_b, swapped_a, swapped_b, mean, *refs):
+def first_kernel(order, middle, turned, near_in, swapped_in, mean, *refs):
     near, swapped, near_square, swapped_square, kept, sent, turned_near = refs
     rows = near.shape[0]
     half = rows // 2
-    centered_into(near, [near_a, near_b], mean[...], near_square)
-    centered_into(swapped, [swapped_a, swapped_b], mean[...], swapped_square)
-    turn_into(turned_near, order, near)
-    for k, (left, right) in enumerate(((turned, near), (turned_near, swapped))):
-        inner = gram(left[...], right[...])
-        kept[:, k * rows:(k + 1) * rows] = inner[:half]
-        sent[:, k * rows:(k + 1) * rows] = inner[half:].astype(jnp.bfloat16)
+
+    @pl.when(middle[0] == 1)
+    def _():
+        centered_into(near, near_in, mean[...], near_square)
+        centered_into(swapped, swapped_in, mean[...], swapped_square)
+        turn_into(turned_near, order, near)
+        for k, (left, right) in enumerate(((turned, near), (turned_near, swapped))):
+            inner = gram(left[...], right[...])
+            kept[:, k * rows:(k + 1) * rows] = inner[:half]
+            sent[:, k * rows:(k + 1) * rows] = inner[half:].astype(jnp.bfloat16)
+
+    @pl.when(middle[0] == 0)
+    def _():
+        for ref in refs[:-1]:
+            ref[...] = jnp.zeros_like(ref)
 
 
 def second_kernel(middle, turned, swapped, swapped_square, end, mean, third, square, kept, sent):
@@ -111,7 +114,7 @@
 
     @pl.when(middle[0] == 0)
     def _():
-        centered_into(third, [end], mean[...], square)
+        centered_into(third, end, mean[...], square)
 
     inner = gram(turned[...], third[...])
     kept[...] = inner[:half]
@@ -148,18 +151,28 @@
         out[pl.ds(pl.multiple_of(order[4 + k] * eighth, eighth), eighth), :] = far[here, :]
 
 
-def middle_kernel(inner, own, near, swapped, own_square, near_square, swapped_square, *outs):
+def middle_kernel(
+    middle, inner, own, near, swapped, own_square, near_square, swapped_square, out, over
+):
     rows, width = own.shape
-    with_own, with_swapped = inner[:, :rows], inner[:, rows:2 * rows]
-    for k, (out, over) in enumerate((outs[:2], outs[2:])):
-        here = slice(k * width // 2, (k + 1) * width // 2)
-        outward = dot_t(with_own, own[:, here]) + dot(with_swapped, swapped[:, here])
-        square = own_square[:, here] + swapped_square[:, here]
-        outward = outward - near[:, here].astype(jnp.float32) * square
-        out[...] = outward.astype(jnp.bfloat16)
-        across = dot_t(with_swapped, near[:, here])
-        across = across - swapped[:, here].astype(jnp.float32) * near_square[:, here]
-        over[...] = across.astype(jnp.bfloat16)
+
+    @pl.when(middle[0] == 1)
+    def _():
+        with_own, with_swapped = inner[:, :rows], inner[:, rows:]
+        for k in range(2):
+            here = slice(k * width // 2, (k + 1) * width // 2)
+            outward = dot_t(with_own, own[:, here]) + dot(with_swapped, swapped[:, here])
+            square = own_square[:, here] + swapped_square[:, here]
+            outward = outward - near[:, here].astype(jnp.float32) * square
+            out[:, here] = outward.astype(jnp.bfloat16)
+            across = dot_t(with_swapped, near[:, here])
+            across = across - swapped[:, here].astype(jnp.float32) * near_square[:, here]
+            over[:, here] = across.astype(jnp.bfloat16)
+
+    @pl.when(middle[0] == 0)
+    def _():
+        out[...] = jnp.zeros_like(out)
+        over[...] = jnp.zeros_like(over)
 
 
 def coefficient(total):
@@ -167,11 +180,11 @@
 
 
 def held_kernel(
-    total, middle, inner, own, near, z, other,
+    total, middle, first, with_own, own, near, z, other,
     own_square, near_square, third_square, mean, spread, held,
 ):
     rows, width = own.shape
-    norm = jnp.sum(inner[:, 3 * rows:].astype(jnp.float32), axis=1, keepdims=True)
+    norm = jnp.sum(with_own[:, rows:].astype(jnp.float32), axis=1, keepdims=True)
     for k in range(4):
         here = slice(k * width // 4, (k + 1) * width // 4)
         anchor = z[:, here].astype(jnp.float32)
@@ -180,7 +193,7 @@
         hinge = jnp.where(deviation < 1.0, centered / deviation, 0.0)
         plain = anchor - other[:, here].astype(jnp.float32) - total / (4.0 * (total - 1)) * hinge
         square = own_square[:, here] + third_square[:, here]
-        product = dot(inner[:, 2 * rows:3 * rows], own[:, here])
+        product = dot(with_own[:, :rows], own[:, here])
         product = product + own[:, here].astype(jnp.float32) * (norm - square)
         held[:, here] = plain + coefficient(total) * product
 
@@ -188,27 +201,22 @@
     def _():
         for k in range(4):
             here = slice(k * width // 4, (k + 1) * width // 4)
-            product = dot(inner[:, :rows], near[:, here])
+            product = dot(first[:, :rows], near[:, here])
             product = product - own[:, here].astype(jnp.float32) * near_square[:, here]
             held[:, here] = held[:, here] + coefficient(total) * product
 
 
-def last_kernel(total, middle, inner, third, held, out_a, over_a, out_b, over_b, result):
+def last_kernel(total, middle, inner, third, held, out, over, result):
     width = third.shape[1]
-    for here, out, over in (
-        (slice(0, width // 2), out_a, over_a), (slice(width // 2, width), out_b, over_b)
-    ):
-        product = dot(inner[...], third[:, here])
-
-        @pl.when(middle[0] == 1)
-        def _():
-            sums = product + over[...].astype(jnp.float32)
-            result[:, here] = held[:, here] + coefficient(total) * sums
-
-        @pl.when(middle[0] == 0)
-        def _():
-            sums = product + out[...].astype(jnp.float32)
-            result[:, here] = held[:, here] + coefficient(total) * sums
+
+    def put(arrived):
+        for k in range(4):
+            here = slice(k * width // 4, (k + 1) * width // 4)
+            product = dot(inner[...], third[:, here]) + arrived[:, here].astype(jnp.float32)
+            result[:, here] = held[:, here] + coefficient(total) * product
+
+    pl.when(middle[0] == 1)(lambda: put(over))
+    pl.when(middle[0] == 0)(lambda: put(out))
 
 
 def to_partner(x, step):
@@ -230,10 +238,13 @@
     )[0]
 
 
-def gather_rows(x, order, *others):
-    near = after(jnp.concatenate([x] + [to_partner(x, 2 * k) for k in (1, 2, 3)]), *others)
-    far = to_partner(near, 1)
-    shape = (8 * x.shape[0], x.shape[1])
+def gather_chips(x):
+    return jnp.concatenate([x] + [to_partner(x, 2 * k) for k in (1, 2, 3)])
+
+
+def gather_cores(near, order, *others):
+    far = after(to_partner(near, 1), *others)
+    shape = (2 * near.shape[0], near.shape[1])
     return kernel_call(place_kernel, [(shape, jnp.bfloat16)], smem=1)(order, near, far)[0]
 
 
@@ -251,23 +262,24 @@
     half = rows // 2
     flat, block = ((1, width), jnp.float32), ((rows, width), jnp.bfloat16)
 
-    near = [lax.ppermute(z_anchor[:half], "dp", inward)]
-    swapped = [lax.ppermute(z_anchor[:half], "dp", across)]
-    anchor = z_anchor.astype(jnp.float32)
-    sums = jnp.sum(anchor, axis=0, keepdims=True)
-    apart = anchor - sums / rows
-    stats = jnp.concatenate([sums, jnp.sum(apart * apart, axis=0, keepdims=True)])
+    base = z_anchor[:1].astype(jnp.float32)
+    apart = z_anchor.astype(jnp.float32) - base
+    stats = jnp.concatenate(
+        [jnp.sum(apart, axis=0, keepdims=True), jnp.sum(apart * apart, axis=0, keepdims=True)]
+    )
+    away = stats[:1] / rows
+    stats = jnp.concatenate([base + away, stats[1:] - stats[:1] * away])
     all_stats = [stats] + [
         lax.ppermute(stats, "dp", [(i, (i + k) % 4) for i in range(4)]) for k in (1, 2, 3)
     ]
-    later = after(z_anchor[half:], *all_stats)
-    end = lax.ppermute(after(z_anchor, *all_stats, near[0], swapped[0]), "dp", [(0, 3), (3, 0)])
-    near.append(lax.ppermute(later, "dp", inward))
-    swapped.append(lax.ppermute(later, "dp", across))
-    mean = (all_stats[0][:1] + all_stats[1][:1] + all_stats[2][:1] + all_stats[3][:1]) / total
+    ahead = after(z_anchor, stats)
+    near = lax.ppermute(ahead, "dp", inward)
+    swapped = lax.ppermute(ahead, "dp", across)
+    end = lax.ppermute(ahead, "dp", [(0, 3), (3, 0)])
+    mean = (all_stats[0][:1] + all_stats[1][:1] + all_stats[2][:1] + all_stats[3][:1]) / 4
     spread = 0.0
     for one in all_stats:
-        shift = one[:1] / rows - mean
+        shift = one[:1] - mean
         spread = spread + (one[1:] + rows * shift * shift)
 
     def summands(n):
@@ -275,21 +287,20 @@
 
     own, turned, own_square, kept, sent = kernel_call(
         own_kernel, [block, block, flat, *summands(rows + NORM)], smem=1, scratch=12
-    )(order, after(z_anchor, near[0], swapped[0]), mean)
-    with_own = scatter(*halve(kept, sent, rows), last=rows)
+    )(order, z_anchor, mean)
+    with_own = gather_chips(scatter(*halve(kept, sent, rows), last=rows))
     near, swapped, near_square, swapped_square, kept, sent, _ = kernel_call(
         first_kernel,
         [block, block, flat, flat, *summands(2 * rows), block],
-        smem=1, scratch=12,
-    )(order, after(turned, with_own), *near, *swapped, mean)
-    first = scatter(*halve(kept, sent))
-    first = gather_rows(jnp.concatenate([first, with_own], axis=1), order, end)
-
-    part = ((rows, width // 2), jnp.bfloat16)
-    ready = kernel_call(middle_kernel, [part] * 4, scratch=12)(
-        first, own, near, swapped, own_square, near_square, swapped_square
-    )
-    pushed = [lax.ppermute(x, "dp", p) for x, p in zip(ready, (outward, across) * 2)]
+        smem=2, scratch=12,
+    )(order, middle, after(turned, with_own), near, swapped, mean)
+    with_own = gather_cores(with_own, order)
+    first = gather_cores(gather_chips(scatter(*halve(kept, sent))), order, end)
+
+    ready = kernel_call(middle_kernel, [block, block], smem=1, scratch=12)(
+        middle, first, own, near, swapped, own_square, near_square, swapped_square
+    )
+    pushed = [lax.ppermute(x, "dp", p) for x, p in zip(ready, (outward, across))]
 
     third, third_square, kept, sent = kernel_call(
         second_kernel, [block, flat, *summands(rows)], smem=1, scratch=12
@@ -297,10 +308,11 @@
     halved = halve(kept, sent)
     result = ((rows, width), jnp.float32)
     held = kernel_call(functools.partial(held_kernel, total), [result], smem=1, scratch=12)(
-        middle, first, own, near, z_anchor, z_other,
+        middle, first, with_own, own, near, z_anchor, z_other,
         own_square, near_square, after(third_square, halved[0]), mean, spread,
     )[0]
-    second = gather_rows(after(scatter(*halved), *pushed[:2], held), order)
+    second = gather_chips(after(scatter(*halved), held))
+    second = gather_cores(second, order, *pushed)
     return kernel_call(functools.partial(last_kernel, total), [result], smem=1, scratch=12)(
         middle, second, third, held, *pushed
     )[0]

time: 115 us -> 99.6 us (0.87); the launches traced: 115 us -> 97.8 us
  starting transfers between devices: 53 us -> 42.5 us
  local copies, waits for them, and re-layouts: 6.66 us -> 1.25 us
  waiting for transfers between devices: 39.5 us -> 35.3 us
  other arithmetic: 0.67 us -> 3.82 us
    ppermute x4 -> x2, starting transfers between devices: 16.5 us -> 7.4 us  [by_line(): lax.ppermute(x, 'dp', p)]
    ppermute x3, waiting for transfers between devices: 8.64 us -> 0.01 us  [by_line(): lax.ppermute(stats, 'dp', [(i, (i + k) % 4) for i in range(4)])]
    ppermute x5 -> x3, starting transfers between devices: 9.12 us -> 3.99 us  [the longest x1 1.99 us: by_line(): swapped = lax.ppermute(ahead, 'dp', across)]
    ppermute x5 -> x3, waiting for transfers between devices: 0.01 us -> 4.59 us  [the longest x1 3.29 us: by_line(): near = lax.ppermute(ahead, 'dp', inward)]
    ppermute x20 -> x24, starting transfers between devices: 22.9 us -> 27.3 us  [to_partner(): return lax.ppermute(x, 'feat', [(i, i ^ step) for i in range(8)])]
    ppermute x20 -> x24, waiting for transfers between devices: 30.8 us -> 26.6 us  [to_partner(): return lax.ppermute(x, 'feat', [(i, i ^ step) for i in range(8)])]
    ppermute x4 -> x2, waiting for transfers between devices: 0.01 us -> 4.17 us  [by_line(): lax.ppermute(x, 'dp', p)]
    unnamed x32 -> x9, local copies, waits for them, and re-layouts: 5.3 us -> 1.25 us
  transfers between devices with their start and end apart: 32 -> 32, of which waited for: 21 -> 25; matrix products, arithmetic and copies ran while one was open for 1% -> 1% of each run, Pallas kernels for 5% -> 8%
where the time goes in v7:
time: 99.6 us; the launch traced here: 97.8 us
  starting transfers between devices  42.5 us (43%)
  waiting for transfers between devices  35.3 us (35%)
  Pallas kernels  14.7 us (15%)
  other arithmetic  3.82 us (4%)
  local copies, waits for them, and re-layouts  1.25 us (1%)
    ppermute x24, starting transfers between devices, to_partner(): return lax.ppermute(x, 'feat', [(i, i ^ step) for i in range(8)])  27.3 us
    ppermute x24, waiting for transfers between devices, to_partner(): return lax.ppermute(x, 'feat', [(i, i ^ step) for i in range(8)])  26.6 us
    pallas_call x15, Pallas kernels, call(): pl.pallas_call(body, out_shape=[jax.ShapeDtypeStruct(s, t) for s, t in ou...  14.7 us
    ppermute x2, starting transfers between devices, by_line(): lax.ppermute(x, 'dp', p)  7.4 us
    ppermute x2, waiting for transfers between devices, by_line(): lax.ppermute(x, 'dp', p)  4.17 us
    ppermute x3, starting transfers between devices, by_line(): lax.ppermute(stats, 'dp', [(i, (i + k) % 4) for i in range(4)])  3.83 us
    ppermute x1, waiting for transfers between devices, by_line(): near = lax.ppermute(ahead, 'dp', inward)  3.29 us
  transfers between devices with their start and end apart: 32, of which 25 were waited for; matrix products, arithmetic and copies ran while one was open for 1% of the time, Pallas kernels for 8%

profile of v7, /device:TPU:9, one launch (start us, length us, event | category | flops | bytes accessed | tf_op | source)
XLA Modules:
  0.0 97.8 jit_solution(10192127787829157788)
XLA Ops:
  0.7 1.6 %multiply_reduce_fusion = (f32[1024]{0:T(1024)S(1)}, f32[1024]{0:T(1024)S(1)}) fusion(bf16[512,1024]{1,0:T(8,128)(2,1)} %z.3, f32[1024]{0:T(1024)S(1)} %bitcast.6), kind=kLoop, calls=%fused_computation | loop fusion | flops 2619392 | bytes 1060864 | tf_op jit(solution)/shard_map/reduce_sum | solution.py:268
  3.1 1.3 %collective-permute-start = (f32[2,1024]{1,0:T(2,128)S(1)}, f32[2,1024]{1,0:T(2,128)S(1)}, u32[]{:S(2)}, u32[]{:S(2)}) collective-permute-start(f32[2,1024]{1,0:T(2,128)S(1)} %pad_maximum_fusion.2), channel_id=1, source_target_pairs={{0,8},{8,16},{16,24},{24,0},{1,9},{9,17},{17,25},{25,1},{2,10},{10... | collective-permute-start | bytes 24584 | tf_op jit(solution)/shard_map/ppermute | solution.py:273
  5.5 1.4 %collective-permute-start.2 = (f32[2,1024]{1,0:T(2,128)S(1)}, f32[2,1024]{1,0:T(2,128)S(1)}, u32[]{:S(2)}, u32[]{:S(2)}) collective-permute-start(f32[2,1024]{1,0:T(2,128)S(1)} %pad_maximum_fusion.2), channel_id=1, source_target_pairs={{0,24},{8,0},{16,8},{24,16},{1,25},{9,1},{17,9},{25,17},{2,26},{10... | collective-permute-start | bytes 24584 | tf_op jit(solution)/shard_map/ppermute | solution.py:273
  6.9 1.3 %collective-permute-start.10 = (bf16[512,1024]{1,0:T(8,128)(2,1)}, bf16[512,1024]{1,0:T(8,128)(2,1)}, u32[]{:S(2)}, u32[]{:S(2)}) collective-permute-start(bf16[512,1024]{1,0:T(8,128)(2,1)} %z.3), channel_id=1, source_target_pairs={{0,8},{24,16},{1,9},{25,17},{2,10},{26,18},{3,11},{27,19},{4,12},{... | collective-permute-start | bytes 3145736 | tf_op jit(solution)/shard_map/ppermute | solution.py:276
  8.2 2.0 %collective-permute-start.11 = (bf16[512,1024]{1,0:T(8,128)(2,1)}, bf16[512,1024]{1,0:T(8,128)(2,1)}, u32[]{:S(2)}, u32[]{:S(2)}) collective-permute-start(bf16[512,1024]{1,0:T(8,128)(2,1)} %z.3), channel_id=1, source_target_pairs={{8,16},{16,8},{9,17},{17,9},{10,18},{18,10},{11,19},{19,11},{12,20... | collective-permute-start | bytes 3145736 | tf_op jit(solution)/shard_map/ppermute | solution.py:277
  12.1 1.7 %shard_map.37 = (bf16[512,1024]{1,0:T(8,128)(2,1)S(1)}, bf16[512,1024]{1,0:T(8,128)(2,1)S(1)}, f32[1,1024]{1,0:T(1,128)S(1)}, f32[256,640]{1,0:T(8,128)S(1)}, bf16[256,640]{1,0:T(8,128)(2,1)S(1)}) custom-call(s32[8]{0:T(128)S(1)} %broadcast_xor_fusion.order, bf16[512,1024]{1,0:T(8,128)(2,1)S(1)} %copy-done, f32[1,1024]{1,0:T(1,128)S(1)} %get-tuple-element.80.mean), custom_call_target="tpu_custom_call" | custom-call | tf_op jit(solution)/shard_map/pallas_call | solution.py:17
  13.8 1.6 %collective-permute-start.3 = (bf16[256,640]{1,0:T(8,128)(2,1)S(1)}, bf16[256,640]{1,0:T(8,128)(2,1)S(1)}, u32[]{:S(2)}, u32[]{:S(2)}) collective-permute-start(bf16[256,640]{1,0:T(8,128)(2,1)S(1)} %get-tuple-element.43), channel_id=1, source_target_pairs={{0,1},{1,0},{2,3},{3,2},{4,5},{5,4},{6,7},{7,6},{8,9},{9,8},{10,11... | collective-permute-start | bytes 983048 | tf_op jit(solution)/shard_map/ppermute | solution.py:223
  15.4 1.3 %collective-permute-done.3.got = bf16[256,640]{1,0:T(8,128)(2,1)S(1)} collective-permute-done((bf16[256,640]{1,0:T(8,128)(2,1)S(1)}, bf16[256,640]{1,0:T(8,128)(2,1)S(1)}, u32[]{:S(2)}, u32[]{:S(2)}) %collective-permute-start.3) | collective-permute-done | bytes 327712 | tf_op jit(solution)/shard_map/ppermute | solution.py:223
  16.8 1.4 %collective-permute-start.4 = (bf16[64,640]{1,0:T(8,128)(2,1)S(1)}, bf16[64,640]{1,0:T(8,128)(2,1)S(1)}, u32[]{:S(2)}, u32[]{:S(2)}) collective-permute-start(bf16[64,640]{1,0:T(8,128)(2,1)S(1)} %get-tuple-element.45), channel_id=1, source_target_pairs={{0,2},{1,3},{2,0},{3,1},{4,6},{5,7},{6,4},{7,5},{8,10},{9,11},{10,... | collective-permute-start | bytes 245768 | tf_op jit(solution)/shard_map/ppermute | solution.py:223
  20.6 1.3 %collective-permute-done.5.b = bf16[64,640]{1,0:T(8,128)(2,1)S(1)} collective-permute-done((bf16[64,640]{1,0:T(8,128)(2,1)S(1)}, bf16[64,640]{1,0:T(8,128)(2,1)S(1)}, u32[]{:S(2)}, u32[]{:S(2)}) %collective-permute-start.5) | collective-permute-done | bytes 81952 | tf_op jit(solution)/shard_map/ppermute | solution.py:223
  21.9 1.7 %collective-permute-done.6.c = bf16[64,640]{1,0:T(8,128)(2,1)S(1)} collective-permute-done((bf16[64,640]{1,0:T(8,128)(2,1)S(1)}, bf16[64,640]{1,0:T(8,128)(2,1)S(1)}, u32[]{:S(2)}, u32[]{:S(2)}) %collective-permute-start.6) | collective-permute-done | bytes 81952 | tf_op jit(solution)/shard_map/ppermute | solution.py:223
  24.7 1.7 %collective-permute-start.9 = (bf16[64,640]{1,0:T(8,128)(2,1)S(1)}, bf16[64,640]{1,0:T(8,128)(2,1)S(1)}, u32[]{:S(2)}, u32[]{:S(2)}) collective-permute-start(bf16[64,640]{1,0:T(8,128)(2,1)S(1)} %shard_map.39), channel_id=1, source_target_pairs={{0,6},{1,7},{2,4},{3,5},{4,2},{5,3},{6,0},{7,1},{8,14},{9,15},{10,... | collective-permute-start | bytes 245768 | tf_op jit(solution)/shard_map/ppermute | solution.py:223
  28.9 3.3 %collective-permute-done.10.near_in = bf16[512,1024]{1,0:T(8,128)(2,1)} collective-permute-done((bf16[512,1024]{1,0:T(8,128)(2,1)}, bf16[512,1024]{1,0:T(8,128)(2,1)}, u32[]{:S(2)}, u32[]{:S(2)}) %collective-permute-start.10) | collective-permute-done | bytes 1048608 | tf_op jit(solution)/shard_map/ppermute | solution.py:276
  32.2 1.3 %collective-permute-done.11.swapped_in = bf16[512,1024]{1,0:T(8,128)(2,1)} collective-permute-done((bf16[512,1024]{1,0:T(8,128)(2,1)}, bf16[512,1024]{1,0:T(8,128)(2,1)}, u32[]{:S(2)}, u32[]{:S(2)}) %collective-permute-start.11) | collective-permute-done | bytes 1048608 | tf_op jit(solution)/shard_map/ppermute | solution.py:277
  33.5 3.8 %shard_map.40 = (bf16[512,1024]{1,0:T(8,128)(2,1)S(1)}, bf16[512,1024]{1,0:T(8,128)(2,1)S(1)}, f32[1,1024]{1,0:T(1,128)S(1)}, f32[1,1024]{1,0:T(1,128)S(1)}, f32...) custom-call(s32[8]{0:T(128)S(1)} %broadcast_xor_fusion.order, s32[1]{0:T(128)} %bitcast.middle, ...), custom_call_target="tpu_custom_call" | custom-call | tf_op jit(solution)/shard_map/pallas_call | solution.py:17
  37.3 2.4 %collective-permute-start.12 = (bf16[256,1024]{1,0:T(8,128)(2,1)S(1)}, bf16[256,1024]{1,0:T(8,128)(2,1)S(1)}, u32[]{:S(2)}, u32[]{:S(2)}) collective-permute-start(bf16[256,1024]{1,0:T(8,128)(2,1)S(1)} %get-tuple-element.51), channel_id=1, source_target_pairs={{0,1},{1,0},{2,3},{3,2},{4,5},{5,4},{6,7},{7,6},{8,9},{9,8},{10,11... | collective-permute-start | bytes 1572872 | tf_op jit(solution)/shard_map/ppermute | solution.py:223
  41.4 1.3 %collective-permute-start.13 = (bf16[64,1024]{1,0:T(8,128)(2,1)S(1)}, bf16[64,1024]{1,0:T(8,128)(2,1)S(1)}, u32[]{:S(2)}, u32[]{:S(2)}) collective-permute-start(bf16[64,1024]{1,0:T(8,128)(2,1)S(1)} %get-tuple-element.53), channel_id=1, source_target_pairs={{0,2},{1,3},{2,0},{3,1},{4,6},{5,7},{6,4},{7,5},{8,10},{9,11},{10,... | collective-permute-start | bytes 393224 | tf_op jit(solution)/shard_map/ppermute | solution.py:223
  44.2 2.1 %collective-permute-done.13.a = bf16[64,1024]{1,0:T(8,128)(2,1)S(1)} collective-permute-done((bf16[64,1024]{1,0:T(8,128)(2,1)S(1)}, bf16[64,1024]{1,0:T(8,128)(2,1)S(1)}, u32[]{:S(2)}, u32[]{:S(2)}) %collective-permute-start.13) | collective-permute-done | bytes 131104 | tf_op jit(solution)/shard_map/ppermute | solution.py:223
  47.1 2.7 %collective-permute-done.15.c = bf16[64,1024]{1,0:T(8,128)(2,1)S(1)} collective-permute-done((bf16[64,1024]{1,0:T(8,128)(2,1)S(1)}, bf16[64,1024]{1,0:T(8,128)(2,1)S(1)}, u32[]{:S(2)}, u32[]{:S(2)}) %collective-permute-start.15) | collective-permute-done | bytes 131104 | tf_op jit(solution)/shard_map/ppermute | solution.py:223
  49.9 1.5 %collective-permute-start.16 = (bf16[64,1024]{1,0:T(8,128)(2,1)S(1)}, bf16[64,1024]{1,0:T(8,128)(2,1)S(1)}, u32[]{:S(2)}, u32[]{:S(2)}) collective-permute-start(bf16[64,1024]{1,0:T(8,128)(2,1)S(1)} %shard_map.42), channel_id=1, source_target_pairs={{0,2},{1,3},{2,0},{3,1},{4,6},{5,7},{6,4},{7,5},{8,10},{9,11},{10,... | collective-permute-start | bytes 393224 | tf_op jit(solution)/shard_map/ppermute | solution.py:223
  53.7 2.4 %collective-permute-done.17 = bf16[64,1024]{1,0:T(8,128)(2,1)S(1)} collective-permute-done((bf16[64,1024]{1,0:T(8,128)(2,1)S(1)}, bf16[64,1024]{1,0:T(8,128)(2,1)S(1)}, u32[]{:S(2)}, u32[]{:S(2)}) %collective-permute-start.17) | collective-permute-done | bytes 131104 | tf_op jit(solution)/shard_map/ppermute | solution.py:223
  57.3 2.8 %collective-permute-start.19 = (bf16[256,1024]{1,0:T(8,128)(2,1)S(1)}, bf16[256,1024]{1,0:T(8,128)(2,1)S(1)}, u32[]{:S(2)}, u32[]{:S(2)}) collective-permute-start(bf16[256,1024]{1,0:T(8,128)(2,1)S(1)} %pad_maximum_fusion.near), channel_id=1, source_target_pairs={{0,1},{1,0},{2,3},{3,2},{4,5},{5,4},{6,7},{7,6},{8,9},{9,8},{10,11... | collective-permute-start | bytes 1572872 | tf_op jit(solution)/shard_map/ppermute | solution.py:223
  60.2 1.5 %collective-permute-done.19.far = bf16[256,1024]{1,0:T(8,128)(2,1)S(1)} collective-permute-done((bf16[256,1024]{1,0:T(8,128)(2,1)S(1)}, bf16[256,1024]{1,0:T(8,128)(2,1)S(1)}, u32[]{:S(2)}, u32[]{:S(2)}) %collective-permute-start.19) | collective-permute-done | bytes 524320 | tf_op jit(solution)/shard_map/ppermute | solution.py:223
  62.3 1.8 %shard_map.44 = (bf16[512,1024]{1,0:T(8,128)(2,1)S(1)}, bf16[512,1024]{1,0:T(8,128)(2,1)S(1)}) custom-call(s32[1]{0:T(128)} %bitcast.middle, bf16[512,1024]{1,0:T(8,128)(2,1)S(1)} %shard_map.43.inner.first, bf16[512,1024]{1,0:T(8,128)(2,1)S(1)} %get-tuple-element.57.own, bf16[512,1024]{1,0:T(8,128)(2,1)S(1)} %get-tuple-element.58.near, ...), custom_call_target="tpu_custom_call" | custom-call | tf_op jit(solution)/shard_map/pallas_call | solution.py:17
  64.2 5.3 %collective-permute-start.30 = (bf16[512,1024]{1,0:T(8,128)(2,1)S(1)}, bf16[512,1024]{1,0:T(8,128)(2,1)S(1)}, u32[]{:S(2)}, u32[]{:S(2)}) collective-permute-start(bf16[512,1024]{1,0:T(8,128)(2,1)S(1)} %get-tuple-element.63), channel_id=1, source_target_pairs={{8,0},{16,24},{9,1},{17,25},{10,2},{18,26},{11,3},{19,27},{12,4},{... | collective-permute-start | bytes 3145736 | tf_op jit(solution)/shard_map/ppermute | solution.py:303
  69.5 2.1 %collective-permute-start.31 = (bf16[512,1024]{1,0:T(8,128)(2,1)S(1)}, bf16[512,1024]{1,0:T(8,128)(2,1)S(1)}, u32[]{:S(2)}, u32[]{:S(2)}) collective-permute-start(bf16[512,1024]{1,0:T(8,128)(2,1)S(1)} %get-tuple-element.64), channel_id=1, source_target_pairs={{8,16},{16,8},{9,17},{17,9},{10,18},{18,10},{11,19},{19,11},{12,20... | collective-permute-start | bytes 3145736 | tf_op jit(solution)/shard_map/ppermute | solution.py:303
  74.9 1.4 %collective-permute-start.22 = (bf16[64,512]{1,0:T(8,128)(2,1)S(1)}, bf16[64,512]{1,0:T(8,128)(2,1)S(1)}, u32[]{:S(2)}, u32[]{:S(2)}) collective-permute-start(bf16[64,512]{1,0:T(8,128)(2,1)S(1)} %get-tuple-element.69), channel_id=1, source_target_pairs={{0,2},{1,3},{2,0},{3,1},{4,6},{5,7},{6,4},{7,5},{8,10},{9,11},{10,... | collective-permute-start | bytes 196616 | tf_op jit(solution)/shard_map/ppermute | solution.py:223
  78.2 2.1 %shard_map.49.held = f32[512,1024]{1,0:T(8,128)S(1)} custom-call(s32[1]{0:T(128)} %bitcast.middle, bf16[512,1024]{1,0:T(8,128)(2,1)S(1)} %shard_map.43.inner.first, bf16[512,640]{1,0:T(8,128)(2,1)S(1)} %shard_map.48.with_own, bf16[512,1024]{1,0:T(8,128)(2,1)S(1)} %get-tuple-element.57.own, bf16[512,1024]{1,0:T(8,128)(2,1)S(1)} %get-tuple-element.58.near, ...), custom_call_target="tpu_custom_call" | custom-call | tf_op jit(solution)/shard_map/pallas_call | solution.py:17
  85.2 1.7 %collective-permute-done.28 = bf16[64,512]{1,0:T(8,128)(2,1)S(1)} collective-permute-done((bf16[64,512]{1,0:T(8,128)(2,1)S(1)}, bf16[64,512]{1,0:T(8,128)(2,1)S(1)}, u32[]{:S(2)}, u32[]{:S(2)}) %collective-permute-start.28) | collective-permute-done | bytes 65568 | tf_op jit(solution)/shard_map/ppermute | solution.py:223
  87.0 2.8 %collective-permute-start.29 = (bf16[256,512]{1,0:T(8,128)(2,1)S(1)}, bf16[256,512]{1,0:T(8,128)(2,1)S(1)}, u32[]{:S(2)}, u32[]{:S(2)}) collective-permute-start(bf16[256,512]{1,0:T(8,128)(2,1)S(1)} %constant_dynamic-update-slice_fusion.near), channel_id=1, source_target_pairs={{0,1},{1,0},{2,3},{3,2},{4,5},{5,4},{6,7},{7,6},{8,9},{9,8},{10,11... | collective-permute-start | bytes 786440 | tf_op jit(solution)/shard_map/ppermute | solution.py:223
  91.1 4.0 %collective-permute-done.31.over = bf16[512,1024]{1,0:T(8,128)(2,1)S(1)} collective-permute-done((bf16[512,1024]{1,0:T(8,128)(2,1)S(1)}, bf16[512,1024]{1,0:T(8,128)(2,1)S(1)}, u32[]{:S(2)}, u32[]{:S(2)}) %collective-permute-start.31) | collective-permute-done | bytes 1048608 | tf_op jit(solution)/shard_map/ppermute | solution.py:303
  95.7 2.1 %shard_map.51 = f32[512,1024]{1,0:T(8,128)} custom-call(s32[1]{0:T(128)} %bitcast.middle, bf16[512,512]{1,0:T(8,128)(2,1)S(1)} %shard_map.50.inner, bf16[512,1024]{1,0:T(8,128)(2,1)S(1)} %get-tuple-element.76.third, f32[512,1024]{1,0:T(8,128)S(1)} %shard_map.49.held, bf16[512,1024]{1,0:T(8,128)(2,1)S(1)} %collective-permute-done.30.out, ...), custom_call_target="tpu_custom_call" | custom-call | tf_op jit(solution)/shard_map/pallas_call | solution.py:17
  (65 shorter events, 30.9 us)
Async XLA Ops:
  3.1 7.8 %collective-permute-start = (f32[2,1024]{1,0:T(2,128)S(1)}, f32[2,1024]{1,0:T(2,128)S(1)}, u32[]{:S(2)}, u32[]{:S(2)}) collective-permute-start(f32[2,1024]{1,0:T(2,128)S(1)} %pad_maximum_fusion.2), channel_id=1, source_target_pairs={{0,8},{8,16},{16,24},{24,0},{1,9},{9,17},{17,25},{25,1},{2,10},{10... | collective-permute-start | bytes 24584 | tf_op jit(solution)/shard_map/ppermute | solution.py:273
  4.4 6.4 %collective-permute-start.1 = (f32[2,1024]{1,0:T(2,128)S(1)}, f32[2,1024]{1,0:T(2,128)S(1)}, u32[]{:S(2)}, u32[]{:S(2)}) collective-permute-start(f32[2,1024]{1,0:T(2,128)S(1)} %pad_maximum_fusion.2), channel_id=1, source_target_pairs={{0,16},{8,24},{16,0},{24,8},{1,17},{9,25},{17,1},{25,9},{2,18},{10... | collective-permute-start | bytes 24584 | tf_op jit(solution)/shard_map/ppermute | solution.py:273
  5.5 5.3 %collective-permute-start.2 = (f32[2,1024]{1,0:T(2,128)S(1)}, f32[2,1024]{1,0:T(2,128)S(1)}, u32[]{:S(2)}, u32[]{:S(2)}) collective-permute-start(f32[2,1024]{1,0:T(2,128)S(1)} %pad_maximum_fusion.2), channel_id=1, source_target_pairs={{0,24},{8,0},{16,8},{24,16},{1,25},{9,1},{17,9},{25,17},{2,26},{10... | collective-permute-start | bytes 24584 | tf_op jit(solution)/shard_map/ppermute | solution.py:273
  6.9 25.3 %collective-permute-start.10 = (bf16[512,1024]{1,0:T(8,128)(2,1)}, bf16[512,1024]{1,0:T(8,128)(2,1)}, u32[]{:S(2)}, u32[]{:S(2)}) collective-permute-start(bf16[512,1024]{1,0:T(8,128)(2,1)} %z.3), channel_id=1, source_target_pairs={{0,8},{24,16},{1,9},{25,17},{2,10},{26,18},{3,11},{27,19},{4,12},{... | collective-permute-start | bytes 3145736 | tf_op jit(solution)/shard_map/ppermute | solution.py:276
  8.2 25.3 %collective-permute-start.11 = (bf16[512,1024]{1,0:T(8,128)(2,1)}, bf16[512,1024]{1,0:T(8,128)(2,1)}, u32[]{:S(2)}, u32[]{:S(2)}) collective-permute-start(bf16[512,1024]{1,0:T(8,128)(2,1)} %z.3), channel_id=1, source_target_pairs={{8,16},{16,8},{9,17},{17,9},{10,18},{18,10},{11,19},{19,11},{12,20... | collective-permute-start | bytes 3145736 | tf_op jit(solution)/shard_map/ppermute | solution.py:277
  13.8 2.8 %collective-permute-start.3 = (bf16[256,640]{1,0:T(8,128)(2,1)S(1)}, bf16[256,640]{1,0:T(8,128)(2,1)S(1)}, u32[]{:S(2)}, u32[]{:S(2)}) collective-permute-start(bf16[256,640]{1,0:T(8,128)(2,1)S(1)} %get-tuple-element.43), channel_id=1, source_target_pairs={{0,1},{1,0},{2,3},{3,2},{4,5},{5,4},{6,7},{7,6},{8,9},{9,8},{10,11... | collective-permute-start | bytes 983048 | tf_op jit(solution)/shard_map/ppermute | solution.py:223
  16.8 3.8 %collective-permute-start.4 = (bf16[64,640]{1,0:T(8,128)(2,1)S(1)}, bf16[64,640]{1,0:T(8,128)(2,1)S(1)}, u32[]{:S(2)}, u32[]{:S(2)}) collective-permute-start(bf16[64,640]{1,0:T(8,128)(2,1)S(1)} %get-tuple-element.45), channel_id=1, source_target_pairs={{0,2},{1,3},{2,0},{3,1},{4,6},{5,7},{6,4},{7,5},{8,10},{9,11},{10,... | collective-permute-start | bytes 245768 | tf_op jit(solution)/shard_map/ppermute | solution.py:223
  18.2 3.7 %collective-permute-start.5 = (bf16[64,640]{1,0:T(8,128)(2,1)S(1)}, bf16[64,640]{1,0:T(8,128)(2,1)S(1)}, u32[]{:S(2)}, u32[]{:S(2)}) collective-permute-start(bf16[64,640]{1,0:T(8,128)(2,1)S(1)} %get-tuple-element.46), channel_id=1, source_target_pairs={{0,4},{1,5},{2,6},{3,7},{4,0},{5,1},{6,2},{7,3},{8,12},{9,13},{10,... | collective-permute-start | bytes 245768 | tf_op jit(solution)/shard_map/ppermute | solution.py:223
  19.4 4.2 %collective-permute-start.6 = (bf16[64,640]{1,0:T(8,128)(2,1)S(1)}, bf16[64,640]{1,0:T(8,128)(2,1)S(1)}, u32[]{:S(2)}, u32[]{:S(2)}) collective-permute-start(bf16[64,640]{1,0:T(8,128)(2,1)S(1)} %get-tuple-element.47), channel_id=1, source_target_pairs={{0,6},{1,7},{2,4},{3,5},{4,2},{5,3},{6,0},{7,1},{8,14},{9,15},{10,... | collective-permute-start | bytes 245768 | tf_op jit(solution)/shard_map/ppermute | solution.py:223
  23.7 3.8 %collective-permute-start.7 = (bf16[64,640]{1,0:T(8,128)(2,1)S(1)}, bf16[64,640]{1,0:T(8,128)(2,1)S(1)}, u32[]{:S(2)}, u32[]{:S(2)}) collective-permute-start(bf16[64,640]{1,0:T(8,128)(2,1)S(1)} %shard_map.39), channel_id=1, source_target_pairs={{0,2},{1,3},{2,0},{3,1},{4,6},{5,7},{6,4},{7,5},{8,10},{9,11},{10,... | collective-permute-start | bytes 245768 | tf_op jit(solution)/shard_map/ppermute | solution.py:223
  24.4 3.7 %collective-permute-start.8 = (bf16[64,640]{1,0:T(8,128)(2,1)S(1)}, bf16[64,640]{1,0:T(8,128)(2,1)S(1)}, u32[]{:S(2)}, u32[]{:S(2)}) collective-permute-start(bf16[64,640]{1,0:T(8,128)(2,1)S(1)} %shard_map.39), channel_id=1, source_target_pairs={{0,4},{1,5},{2,6},{3,7},{4,0},{5,1},{6,2},{7,3},{8,12},{9,13},{10,... | collective-permute-start | bytes 245768 | tf_op jit(solution)/shard_map/ppermute | solution.py:223
  24.7 4.2 %collective-permute-start.9 = (bf16[64,640]{1,0:T(8,128)(2,1)S(1)}, bf16[64,640]{1,0:T(8,128)(2,1)S(1)}, u32[]{:S(2)}, u32[]{:S(2)}) collective-permute-start(bf16[64,640]{1,0:T(8,128)(2,1)S(1)} %shard_map.39), channel_id=1, source_target_pairs={{0,6},{1,7},{2,4},{3,5},{4,2},{5,3},{6,0},{7,1},{8,14},{9,15},{10,... | collective-permute-start | bytes 245768 | tf_op jit(solution)/shard_map/ppermute | solution.py:223
  37.3 4.0 %collective-permute-start.12 = (bf16[256,1024]{1,0:T(8,128)(2,1)S(1)}, bf16[256,1024]{1,0:T(8,128)(2,1)S(1)}, u32[]{:S(2)}, u32[]{:S(2)}) collective-permute-start(bf16[256,1024]{1,0:T(8,128)(2,1)S(1)} %get-tuple-element.51), channel_id=1, source_target_pairs={{0,1},{1,0},{2,3},{3,2},{4,5},{5,4},{6,7},{7,6},{8,9},{9,8},{10,11... | collective-permute-start | bytes 1572872 | tf_op jit(solution)/shard_map/ppermute | solution.py:223
  39.8 20.5 %collective-permute-start.20 = (bf16[512,1024]{1,0:T(8,128)(2,1)S(1)}, bf16[512,1024]{1,0:T(8,128)(2,1)S(1)}, u32[]{:S(2)}, u32[]{:S(2)}) collective-permute-start(bf16[512,1024]{1,0:T(8,128)(2,1)S(1)} %copy-done.1), channel_id=1, source_target_pairs={{0,24},{24,0},{1,25},{25,1},{2,26},{26,2},{3,27},{27,3},{4,28},{28... | collective-permute-start | bytes 3145736 | tf_op jit(solution)/shard_map/ppermute | solution.py:278
  41.4 4.8 %collective-permute-start.13 = (bf16[64,1024]{1,0:T(8,128)(2,1)S(1)}, bf16[64,1024]{1,0:T(8,128)(2,1)S(1)}, u32[]{:S(2)}, u32[]{:S(2)}) collective-permute-start(bf16[64,1024]{1,0:T(8,128)(2,1)S(1)} %get-tuple-element.53), channel_id=1, source_target_pairs={{0,2},{1,3},{2,0},{3,1},{4,6},{5,7},{6,4},{7,5},{8,10},{9,11},{10,... | collective-permute-start | bytes 393224 | tf_op jit(solution)/shard_map/ppermute | solution.py:223
  42.7 4.4 %collective-permute-start.14 = (bf16[64,1024]{1,0:T(8,128)(2,1)S(1)}, bf16[64,1024]{1,0:T(8,128)(2,1)S(1)}, u32[]{:S(2)}, u32[]{:S(2)}) collective-permute-start(bf16[64,1024]{1,0:T(8,128)(2,1)S(1)} %get-tuple-element.54), channel_id=1, source_target_pairs={{0,4},{1,5},{2,6},{3,7},{4,0},{5,1},{6,2},{7,3},{8,12},{9,13},{10,... | collective-permute-start | bytes 393224 | tf_op jit(solution)/shard_map/ppermute | solution.py:223
  44.0 5.8 %collective-permute-start.15 = (bf16[64,1024]{1,0:T(8,128)(2,1)S(1)}, bf16[64,1024]{1,0:T(8,128)(2,1)S(1)}, u32[]{:S(2)}, u32[]{:S(2)}) collective-permute-start(bf16[64,1024]{1,0:T(8,128)(2,1)S(1)} %get-tuple-element.55), channel_id=1, source_target_pairs={{0,6},{1,7},{2,4},{3,5},{4,2},{5,3},{6,0},{7,1},{8,14},{9,15},{10,... | collective-permute-start | bytes 393224 | tf_op jit(solution)/shard_map/ppermute | solution.py:223
  49.9 3.9 %collective-permute-start.16 = (bf16[64,1024]{1,0:T(8,128)(2,1)S(1)}, bf16[64,1024]{1,0:T(8,128)(2,1)S(1)}, u32[]{:S(2)}, u32[]{:S(2)}) collective-permute-start(bf16[64,1024]{1,0:T(8,128)(2,1)S(1)} %shard_map.42), channel_id=1, source_target_pairs={{0,2},{1,3},{2,0},{3,1},{4,6},{5,7},{6,4},{7,5},{8,10},{9,11},{10,... | collective-permute-start | bytes 393224 | tf_op jit(solution)/shard_map/ppermute | solution.py:223
  51.3 4.8 %collective-permute-start.17 = (bf16[64,1024]{1,0:T(8,128)(2,1)S(1)}, bf16[64,1024]{1,0:T(8,128)(2,1)S(1)}, u32[]{:S(2)}, u32[]{:S(2)}) collective-permute-start(bf16[64,1024]{1,0:T(8,128)(2,1)S(1)} %shard_map.42), channel_id=1, source_target_pairs={{0,4},{1,5},{2,6},{3,7},{4,0},{5,1},{6,2},{7,3},{8,12},{9,13},{10,... | collective-permute-start | bytes 393224 | tf_op jit(solution)/shard_map/ppermute | solution.py:223
  51.6 5.7 %collective-permute-start.18 = (bf16[64,1024]{1,0:T(8,128)(2,1)S(1)}, bf16[64,1024]{1,0:T(8,128)(2,1)S(1)}, u32[]{:S(2)}, u32[]{:S(2)}) collective-permute-start(bf16[64,1024]{1,0:T(8,128)(2,1)S(1)} %shard_map.42), channel_id=1, source_target_pairs={{0,6},{1,7},{2,4},{3,5},{4,2},{5,3},{6,0},{7,1},{8,14},{9,15},{10,... | collective-permute-start | bytes 393224 | tf_op jit(solution)/shard_map/ppermute | solution.py:223
  57.3 4.4 %collective-permute-start.19 = (bf16[256,1024]{1,0:T(8,128)(2,1)S(1)}, bf16[256,1024]{1,0:T(8,128)(2,1)S(1)}, u32[]{:S(2)}, u32[]{:S(2)}) collective-permute-start(bf16[256,1024]{1,0:T(8,128)(2,1)S(1)} %pad_maximum_fusion.near), channel_id=1, source_target_pairs={{0,1},{1,0},{2,3},{3,2},{4,5},{5,4},{6,7},{7,6},{8,9},{9,8},{10,11... | collective-permute-start | bytes 1572872 | tf_op jit(solution)/shard_map/ppermute | solution.py:223
  60.2 17.0 %collective-permute-start.25 = (bf16[256,640]{1,0:T(8,128)(2,1)S(1)}, bf16[256,640]{1,0:T(8,128)(2,1)S(1)}, u32[]{:S(2)}, u32[]{:S(2)}) collective-permute-start(bf16[256,640]{1,0:T(8,128)(2,1)S(1)} %pad_maximum_fusion.1.near), channel_id=1, source_target_pairs={{0,1},{1,0},{2,3},{3,2},{4,5},{5,4},{6,7},{7,6},{8,9},{9,8},{10,11... | collective-permute-start | bytes 983048 | tf_op jit(solution)/shard_map/ppermute | solution.py:223
  64.2 27.0 %collective-permute-start.30 = (bf16[512,1024]{1,0:T(8,128)(2,1)S(1)}, bf16[512,1024]{1,0:T(8,128)(2,1)S(1)}, u32[]{:S(2)}, u32[]{:S(2)}) collective-permute-start(bf16[512,1024]{1,0:T(8,128)(2,1)S(1)} %get-tuple-element.63), channel_id=1, source_target_pairs={{8,0},{16,24},{9,1},{17,25},{10,2},{18,26},{11,3},{19,27},{12,4},{... | collective-permute-start | bytes 3145736 | tf_op jit(solution)/shard_map/ppermute | solution.py:303
  69.5 25.6 %collective-permute-start.31 = (bf16[512,1024]{1,0:T(8,128)(2,1)S(1)}, bf16[512,1024]{1,0:T(8,128)(2,1)S(1)}, u32[]{:S(2)}, u32[]{:S(2)}) collective-permute-start(bf16[512,1024]{1,0:T(8,128)(2,1)S(1)} %get-tuple-element.64), channel_id=1, source_target_pairs={{8,16},{16,8},{9,17},{17,9},{10,18},{18,10},{11,19},{19,11},{12,20... | collective-permute-start | bytes 3145736 | tf_op jit(solution)/shard_map/ppermute | solution.py:303
  72.4 2.4 %collective-permute-start.21 = (bf16[256,512]{1,0:T(8,128)(2,1)S(1)}, bf16[256,512]{1,0:T(8,128)(2,1)S(1)}, u32[]{:S(2)}, u32[]{:S(2)}) collective-permute-start(bf16[256,512]{1,0:T(8,128)(2,1)S(1)} %get-tuple-element.67), channel_id=1, source_target_pairs={{0,1},{1,0},{2,3},{3,2},{4,5},{5,4},{6,7},{7,6},{8,9},{9,8},{10,11... | collective-permute-start | bytes 786440 | tf_op jit(solution)/shard_map/ppermute | solution.py:223
  74.9 5.5 %collective-permute-start.22 = (bf16[64,512]{1,0:T(8,128)(2,1)S(1)}, bf16[64,512]{1,0:T(8,128)(2,1)S(1)}, u32[]{:S(2)}, u32[]{:S(2)}) collective-permute-start(bf16[64,512]{1,0:T(8,128)(2,1)S(1)} %get-tuple-element.69), channel_id=1, source_target_pairs={{0,2},{1,3},{2,0},{3,1},{4,6},{5,7},{6,4},{7,5},{8,10},{9,11},{10,... | collective-permute-start | bytes 196616 | tf_op jit(solution)/shard_map/ppermute | solution.py:223
  76.3 4.1 %collective-permute-start.23 = (bf16[64,512]{1,0:T(8,128)(2,1)S(1)}, bf16[64,512]{1,0:T(8,128)(2,1)S(1)}, u32[]{:S(2)}, u32[]{:S(2)}) collective-permute-start(bf16[64,512]{1,0:T(8,128)(2,1)S(1)} %get-tuple-element.70), channel_id=1, source_target_pairs={{0,4},{1,5},{2,6},{3,7},{4,0},{5,1},{6,2},{7,3},{8,12},{9,13},{10,... | collective-permute-start | bytes 196616 | tf_op jit(solution)/shard_map/ppermute | solution.py:223
  77.1 4.0 %collective-permute-start.24 = (bf16[64,512]{1,0:T(8,128)(2,1)S(1)}, bf16[64,512]{1,0:T(8,128)(2,1)S(1)}, u32[]{:S(2)}, u32[]{:S(2)}) collective-permute-start(bf16[64,512]{1,0:T(8,128)(2,1)S(1)} %get-tuple-element.71), channel_id=1, source_target_pairs={{0,6},{1,7},{2,4},{3,5},{4,2},{5,3},{6,0},{7,1},{8,14},{9,15},{10,... | collective-permute-start | bytes 196616 | tf_op jit(solution)/shard_map/ppermute | solution.py:223
  81.2 3.5 %collective-permute-start.26 = (bf16[64,512]{1,0:T(8,128)(2,1)S(1)}, bf16[64,512]{1,0:T(8,128)(2,1)S(1)}, u32[]{:S(2)}, u32[]{:S(2)}) collective-permute-start(bf16[64,512]{1,0:T(8,128)(2,1)S(1)} %shard_map.47), channel_id=1, source_target_pairs={{0,2},{1,3},{2,0},{3,1},{4,6},{5,7},{6,4},{7,5},{8,10},{9,11},{10,... | collective-permute-start | bytes 196616 | tf_op jit(solution)/shard_map/ppermute | solution.py:223
  81.8 3.4 %collective-permute-start.27 = (bf16[64,512]{1,0:T(8,128)(2,1)S(1)}, bf16[64,512]{1,0:T(8,128)(2,1)S(1)}, u32[]{:S(2)}, u32[]{:S(2)}) collective-permute-start(bf16[64,512]{1,0:T(8,128)(2,1)S(1)} %shard_map.47), channel_id=1, source_target_pairs={{0,4},{1,5},{2,6},{3,7},{4,0},{5,1},{6,2},{7,3},{8,12},{9,13},{10,... | collective-permute-start | bytes 196616 | tf_op jit(solution)/shard_map/ppermute | solution.py:223
  82.7 4.3 %collective-permute-start.28 = (bf16[64,512]{1,0:T(8,128)(2,1)S(1)}, bf16[64,512]{1,0:T(8,128)(2,1)S(1)}, u32[]{:S(2)}, u32[]{:S(2)}) collective-permute-start(bf16[64,512]{1,0:T(8,128)(2,1)S(1)} %shard_map.47), channel_id=1, source_target_pairs={{0,6},{1,7},{2,4},{3,5},{4,2},{5,3},{6,0},{7,1},{8,14},{9,15},{10,... | collective-permute-start | bytes 196616 | tf_op jit(solution)/shard_map/ppermute | solution.py:223
  87.0 4.0 %collective-permute-start.29 = (bf16[256,512]{1,0:T(8,128)(2,1)S(1)}, bf16[256,512]{1,0:T(8,128)(2,1)S(1)}, u32[]{:S(2)}, u32[]{:S(2)}) collective-permute-start(bf16[256,512]{1,0:T(8,128)(2,1)S(1)} %constant_dynamic-update-slice_fusion.near), channel_id=1, source_target_pairs={{0,1},{1,0},{2,3},{3,2},{4,5},{5,4},{6,7},{7,6},{8,9},{9,8},{10,11... | collective-permute-start | bytes 786440 | tf_op jit(solution)/shard_map/ppermute | solution.py:223
  (3 other events, 26.1 us)

commit v8 on v7

--- a/solution.py
+++ b/solution.py
@@ -83,40 +83,43 @@
     sent[:, rows:] = high_low(norm[half:], (half, NORM)).astype(jnp.bfloat16)
 
 
-def first_kernel(order, middle, turned, near_in, swapped_in, mean, *refs):
-    near, swapped, near_square, swapped_square, kept, sent, turned_near = refs
-    rows = near.shape[0]
+def first_kernel(order, turned, beside_in, opposite_in, mean, *refs):
+    beside, beside_square, kept, sent, opposite, turned_beside, unused = refs
+    rows = beside.shape[0]
     half = rows // 2
+
+    def put(left, right, k):
+        inner = gram(left[...], right[...])
+        kept[:, k * rows:(k + 1) * rows] = inner[:half]
+        sent[:, k * rows:(k + 1) * rows] = inner[half:].astype(jnp.bfloat16)
+
+    centered_into(beside, beside_in, mean[...], beside_square)
+    put(turned, beside, 0)
+    centered_into(opposite, opposite_in, mean[...], unused)
+    turn_into(turned_beside, order, beside)
+    put(turned_beside, opposite, 1)
+
+
+def first_end_kernel(turned, beside_in, mean, beside, beside_square, kept, sent):
+    half = beside.shape[0] // 2
+    centered_into(beside, beside_in, mean[...], beside_square)
+    inner = gram(turned[...], beside[...])
+    kept[...] = inner[:half]
+    sent[...] = inner[half:].astype(jnp.bfloat16)
+
+
+def second_kernel(middle, turned, swapped, end, mean, opposite, square, kept, sent):
+    half = opposite.shape[0] // 2
 
     @pl.when(middle[0] == 1)
     def _():
-        centered_into(near, near_in, mean[...], near_square)
-        centered_into(swapped, swapped_in, mean[...], swapped_square)
-        turn_into(turned_near, order, near)
-        for k, (left, right) in enumerate(((turned, near), (turned_near, swapped))):
-            inner = gram(left[...], right[...])
-            kept[:, k * rows:(k + 1) * rows] = inner[:half]
-            sent[:, k * rows:(k + 1) * rows] = inner[half:].astype(jnp.bfloat16)
+        centered_into(opposite, swapped, mean[...], square)
 
     @pl.when(middle[0] == 0)
     def _():
-        for ref in refs[:-1]:
-            ref[...] = jnp.zeros_like(ref)
-
-
-def second_kernel(middle, turned, swapped, swapped_square, end, mean, third, square, kept, sent):
-    half = third.shape[0] // 2
-
-    @pl.when(middle[0] == 1)
-    def _():
-        third[...] = swapped[...]
-        square[...] = swapped_square[...]
-
-    @pl.when(middle[0] == 0)
-    def _():
-        centered_into(third, end, mean[...], square)
-
-    inner = gram(turned[...], third[...])
+        centered_into(opposite, end, mean[...], square)
+
+    inner = gram(turned[...], opposite[...])
     kept[...] = inner[:half]
     sent[...] = inner[half:].astype(jnp.bfloat16)
 
@@ -151,37 +154,13 @@
         out[pl.ds(pl.multiple_of(order[4 + k] * eighth, eighth), eighth), :] = far[here, :]
 
 
-def middle_kernel(
-    middle, inner, own, near, swapped, own_square, near_square, swapped_square, out, over
-):
-    rows, width = own.shape
-
-    @pl.when(middle[0] == 1)
-    def _():
-        with_own, with_swapped = inner[:, :rows], inner[:, rows:]
-        for k in range(2):
-            here = slice(k * width // 2, (k + 1) * width // 2)
-            outward = dot_t(with_own, own[:, here]) + dot(with_swapped, swapped[:, here])
-            square = own_square[:, here] + swapped_square[:, here]
-            outward = outward - near[:, here].astype(jnp.float32) * square
-            out[:, here] = outward.astype(jnp.bfloat16)
-            across = dot_t(with_swapped, near[:, here])
-            across = across - swapped[:, here].astype(jnp.float32) * near_square[:, here]
-            over[:, here] = across.astype(jnp.bfloat16)
-
-    @pl.when(middle[0] == 0)
-    def _():
-        out[...] = jnp.zeros_like(out)
-        over[...] = jnp.zeros_like(over)
-
-
 def coefficient(total):
     return 2.0 * total / (25.0 * (total - 1)) / (total - 1)
 
 
 def held_kernel(
-    total, middle, first, with_own, own, near, z, other,
-    own_square, near_square, third_square, mean, spread, held,
+    total, first, with_own, own, beside, z, other,
+    own_square, beside_square, opposite_square, mean, spread, held,
 ):
     rows, width = own.shape
     norm = jnp.sum(with_own[:, rows:].astype(jnp.float32), axis=1, keepdims=True)
@@ -192,31 +171,28 @@
         centered = anchor - mean[:, here]
         hinge = jnp.where(deviation < 1.0, centered / deviation, 0.0)
         plain = anchor - other[:, here].astype(jnp.float32) - total / (4.0 * (total - 1)) * hinge
-        square = own_square[:, here] + third_square[:, here]
+        square = own_square[:, here] + beside_square[:, here] + opposite_square[:, here]
         product = dot(with_own[:, :rows], own[:, here])
+        product = product + dot(first[:, :rows], beside[:, here])
         product = product + own[:, here].astype(jnp.float32) * (norm - square)
         held[:, here] = plain + coefficient(total) * product
 
-    @pl.when(middle[0] == 1)
-    def _():
+
+def last_kernel(total, middle, first, second, opposite, own, held, mean, out, over, result):
+    rows, width = own.shape
+
+    def put(arrived, product_of):
         for k in range(4):
             here = slice(k * width // 4, (k + 1) * width // 4)
-            product = dot(first[:, :rows], near[:, here])
-            product = product - own[:, here].astype(jnp.float32) * near_square[:, here]
-            held[:, here] = held[:, here] + coefficient(total) * product
-
-
-def last_kernel(total, middle, inner, third, held, out, over, result):
-    width = third.shape[1]
-
-    def put(arrived):
-        for k in range(4):
-            here = slice(k * width // 4, (k + 1) * width // 4)
-            product = dot(inner[...], third[:, here]) + arrived[:, here].astype(jnp.float32)
+            block = (arrived[:, here].astype(jnp.float32) - mean[:, here]).astype(jnp.bfloat16)
+            wide = block.astype(jnp.float32)
+            square = jnp.sum(wide * wide, axis=0, keepdims=True)
+            product = dot(second[...], opposite[:, here]) + product_of(first[:, rows:], block)
+            product = product - own[:, here].astype(jnp.float32) * square
             result[:, here] = held[:, here] + coefficient(total) * product
 
-    pl.when(middle[0] == 1)(lambda: put(over))
-    pl.when(middle[0] == 0)(lambda: put(out))
+    pl.when(middle[0] == 1)(lambda: put(over, dot_t))
+    pl.when(middle[0] == 0)(lambda: put(out, dot))
 
 
 def to_partner(x, step):
@@ -258,7 +234,7 @@
     plane = lax.axis_index("dp")
     middle = ((plane == 1) | (plane == 2)).astype(jnp.int32).reshape(1)
     order = lax.axis_index("feat") ^ jnp.array([0, 2, 4, 6, 1, 3, 5, 7], jnp.int32)
-    inward, across, outward = [(0, 1), (3, 2)], [(1, 2), (2, 1)], [(1, 0), (2, 3)]
+    across, outward = [(1, 2), (2, 1)], [(1, 0), (2, 3)]
     half = rows // 2
     flat, block = ((1, width), jnp.float32), ((rows, width), jnp.bfloat16)
 
@@ -273,7 +249,7 @@
         lax.ppermute(stats, "dp", [(i, (i + k) % 4) for i in range(4)]) for k in (1, 2, 3)
     ]
     ahead = after(z_anchor, stats)
-    near = lax.ppermute(ahead, "dp", inward)
+    beside_in = lax.ppermute(ahead, "dp", [(i, i ^ 1) for i in range(4)])
     swapped = lax.ppermute(ahead, "dp", across)
     end = lax.ppermute(ahead, "dp", [(0, 3), (3, 0)])
     mean = (all_stats[0][:1] + all_stats[1][:1] + all_stats[2][:1] + all_stats[3][:1]) / 4
@@ -289,32 +265,46 @@
         own_kernel, [block, block, flat, *summands(rows + NORM)], smem=1, scratch=12
     )(order, z_anchor, mean)
     with_own = gather_chips(scatter(*halve(kept, sent, rows), last=rows))
-    near, swapped, near_square, swapped_square, kept, sent, _ = kernel_call(
-        first_kernel,
-        [block, block, flat, flat, *summands(2 * rows), block],
-        smem=2, scratch=12,
-    )(order, middle, after(turned, with_own), near, swapped, mean)
+
+    def on_middle(order, turned, beside_in, swapped, mean):
+        beside, square, kept, sent, *_ = kernel_call(
+            first_kernel,
+            [block, flat, *summands(2 * rows), block, block, flat], smem=1, scratch=12,
+        )(order, turned, beside_in, swapped, mean)
+        return beside, square, scatter(*halve(kept, sent))
+
+    def on_end(order, turned, beside_in, swapped, mean):
+        beside, square, kept, sent = kernel_call(
+            first_end_kernel, [block, flat, *summands(rows)], scratch=12
+        )(turned, beside_in, mean)
+        first = scatter(*halve(kept, sent))
+        return beside, square, jnp.concatenate([first, jnp.zeros_like(first)], axis=1)
+
+    beside, beside_square, first = lax.cond(
+        middle[0] == 1, on_middle, on_end,
+        order, after(turned, with_own), beside_in, swapped, mean,
+    )
     with_own = gather_cores(with_own, order)
-    first = gather_cores(gather_chips(scatter(*halve(kept, sent))), order, end)
-
-    ready = kernel_call(middle_kernel, [block, block], smem=1, scratch=12)(
-        middle, first, own, near, swapped, own_square, near_square, swapped_square
-    )
-    pushed = [lax.ppermute(x, "dp", p) for x, p in zip(ready, (outward, across))]
-
-    third, third_square, kept, sent = kernel_call(
+    handed = [lax.ppermute(first[:, rows:], "dp", p) for p in (outward, across)]
+    out = lax.ppermute(after(swapped, first), "dp", outward)
+    over = lax.ppermute(after(beside_in, first), "dp", across)
+    first = jnp.concatenate([first[:, :rows], handed[0] + handed[1]], axis=1)
+    first = gather_chips(first)
+
+    opposite, opposite_square, kept, sent = kernel_call(
         second_kernel, [block, flat, *summands(rows)], smem=1, scratch=12
-    )(middle, after(turned, *ready), swapped, swapped_square, end, mean)
+    )(middle, after(turned, first), swapped, end, mean)
+    first = gather_cores(first, order)
     halved = halve(kept, sent)
     result = ((rows, width), jnp.float32)
-    held = kernel_call(functools.partial(held_kernel, total), [result], smem=1, scratch=12)(
-        middle, first, with_own, own, near, z_anchor, z_other,
-        own_square, near_square, after(third_square, halved[0]), mean, spread,
+    held = kernel_call(functools.partial(held_kernel, total), [result], scratch=12)(
+        first, with_own, own, beside, z_anchor, z_other,
+        own_square, beside_square, after(opposite_square, halved[0]), mean, spread,
     )[0]
-    second = gather_chips(after(scatter(*halved), held))
-    second = gather_cores(second, order, *pushed)
+    second = after(gather_chips(after(scatter(*halved), held)), out, over)
+    second = gather_cores(second, order)
     return kernel_call(functools.partial(last_kernel, total), [result], smem=1, scratch=12)(
-        middle, second, third, held, *pushed
+        middle, first, second, opposite, own, held, mean, out, over
     )[0]
 
 

time: 99.6 us -> 126 us (1.27); the launches traced: 97.8 us -> 125 us
  waiting for transfers between devices: 35.3 us -> 58.1 us
  Pallas kernels: 14.7 us -> 18.4 us
  starting transfers between devices: 42.5 us -> 43.9 us
    ppermute x1, waiting for transfers between devices: 1.3 us -> 23.9 us  [by_line(): swapped = lax.ppermute(ahead, 'dp', across)]
    ppermute x24, waiting for transfers between devices: 26.6 us -> 31.5 us  [to_partner(): return lax.ppermute(x, 'feat', [(i, i ^ step) for i in range(8)])]
    ppermute x3 -> x5, waiting for transfers between devices: 7.45 us -> 2.8 us  [the longest x2 2.79 us: by_line(): handed = [lax.ppermute(first[:, rows:], 'dp', p) for p in (outward, across)]]
    pallas_call x15 -> x14, Pallas kernels: 14.7 us -> 18.4 us  [call(): pl.pallas_call(body, out_shape=[jax.ShapeDtypeStruct(s, t) for s, t in ou...]
    ppermute x3, starting transfers between devices: 3.83 us -> 5.62 us  [by_line(): lax.ppermute(stats, 'dp', [(i, (i + k) % 4) for i in range(4)])]
    ppermute x3 -> x5, starting transfers between devices: 8.68 us -> 7.16 us  [the longest x2 3.63 us: by_line(): handed = [lax.ppermute(first[:, rows:], 'dp', p) for p in (outward, across)]]
  transfers between devices with their start and end apart: 32 -> 34, of which waited for: 25 -> 20; matrix products, arithmetic and copies ran while one was open for 1% -> 1% of each run, Pallas kernels for 8% -> 12%
where the time goes in v8:
time: 126 us; the launch traced here: 125 us
  waiting for transfers between devices  58.1 us (46%)
  starting transfers between devices  43.9 us (35%)
  Pallas kernels  18.4 us (15%)
  other arithmetic  3.87 us (3%)
    ppermute x24, waiting for transfers between devices, to_partner(): return lax.ppermute(x, 'feat', [(i, i ^ step) for i in range(8)])  31.5 us
    ppermute x24, starting transfers between devices, to_partner(): return lax.ppermute(x, 'feat', [(i, i ^ step) for i in range(8)])  28.2 us
    ppermute x1, waiting for transfers between devices, by_line(): swapped = lax.ppermute(ahead, 'dp', across)  23.9 us
    pallas_call x14, Pallas kernels, call(): pl.pallas_call(body, out_shape=[jax.ShapeDtypeStruct(s, t) for s, t in ou...  18.4 us
    ppermute x3, starting transfers between devices, by_line(): lax.ppermute(stats, 'dp', [(i, (i + k) % 4) for i in range(4)])  5.62 us
    ppermute x2, starting transfers between devices, by_line(): handed = [lax.ppermute(first[:, rows:], 'dp', p) for p in (outward, across)]  3.63 us
    ppermute x2, waiting for transfers between devices, by_line(): handed = [lax.ppermute(first[:, rows:], 'dp', p) for p in (outward, across)]  2.79 us
  transfers between devices with their start and end apart: 34, of which 20 were waited for; matrix products, arithmetic and copies ran while one was open for 1% of the time, Pallas kernels for 12%

profile of v8, /device:TPU:9, one launch (start us, length us, event | category | flops | bytes accessed | tf_op | source)
XLA Modules:
  0.0 125.5 jit_solution(4985558609056976262)
XLA Ops:
  0.7 1.6 %multiply_reduce_fusion = (f32[1024]{0:T(1024)S(1)}, f32[1024]{0:T(1024)S(1)}) fusion(bf16[512,1024]{1,0:T(8,128)(2,1)} %z.3, f32[1024]{0:T(1024)S(1)} %bitcast.6), kind=kLoop, calls=%fused_computation | loop fusion | flops 2619392 | bytes 1060864 | tf_op jit(solution)/shard_map/reduce_sum | solution.py:244
  3.1 1.5 %collective-permute-start.8 = (f32[2,1024]{1,0:T(2,128)S(1)}, f32[2,1024]{1,0:T(2,128)S(1)}, u32[]{:S(2)}, u32[]{:S(2)}) collective-permute-start(f32[2,1024]{1,0:T(2,128)S(1)} %pad_maximum_fusion.4), channel_id=1, source_target_pairs={{0,8},{8,16},{16,24},{24,0},{1,9},{9,17},{17,25},{25,1},{2,10},{10... | collective-permute-start | bytes 24584 | tf_op jit(solution)/shard_map/ppermute | solution.py:249
  4.6 4.1 %collective-permute-start.9 = (f32[2,1024]{1,0:T(2,128)S(1)}, f32[2,1024]{1,0:T(2,128)S(1)}, u32[]{:S(2)}, u32[]{:S(2)}) collective-permute-start(f32[2,1024]{1,0:T(2,128)S(1)} %pad_maximum_fusion.4), channel_id=1, source_target_pairs={{0,16},{8,24},{16,0},{24,8},{1,17},{9,25},{17,1},{25,9},{2,18},{10... | collective-permute-start | bytes 24584 | tf_op jit(solution)/shard_map/ppermute | solution.py:249
  8.7 2.2 %collective-permute-start.19 = (bf16[512,1024]{1,0:T(8,128)(2,1)}, bf16[512,1024]{1,0:T(8,128)(2,1)}, u32[]{:S(2)}, u32[]{:S(2)}) collective-permute-start(bf16[512,1024]{1,0:T(8,128)(2,1)} %z.3), channel_id=1, source_target_pairs={{8,16},{16,8},{9,17},{17,9},{10,18},{18,10},{11,19},{19,11},{12,20... | collective-permute-start | bytes 3145736 | tf_op jit(solution)/shard_map/ppermute | solution.py:253
  11.6 3.0 %shard_map.37 = (bf16[512,1024]{1,0:T(8,128)(2,1)S(1)}, bf16[512,1024]{1,0:T(8,128)(2,1)}, f32[1,1024]{1,0:T(1,128)S(1)}, f32[256,640]{1,0:T(8,128)S(1)}, bf16[256,640]{1,0:T(8,128)(2,1)S(1)}) custom-call(s32[8]{0:T(128)S(1)} %broadcast_xor_fusion.order, bf16[512,1024]{1,0:T(8,128)(2,1)} %z.3, f32[1,1024]{1,0:T(1,128)S(1)} %get-tuple-element.106.mean), custom_call_target="tpu_custom_call" | custom-call | tf_op jit(solution)/shard_map/pallas_call | solution.py:17
  14.6 1.8 %collective-permute-start.11 = (bf16[256,640]{1,0:T(8,128)(2,1)S(1)}, bf16[256,640]{1,0:T(8,128)(2,1)S(1)}, u32[]{:S(2)}, u32[]{:S(2)}) collective-permute-start(bf16[256,640]{1,0:T(8,128)(2,1)S(1)} %get-tuple-element.75), channel_id=1, source_target_pairs={{0,1},{1,0},{2,3},{3,2},{4,5},{5,4},{6,7},{7,6},{8,9},{9,8},{10,11... | collective-permute-start | bytes 983048 | tf_op jit(solution)/shard_map/ppermute | solution.py:199
  17.8 1.3 %collective-permute-start.12 = (bf16[64,640]{1,0:T(8,128)(2,1)S(1)}, bf16[64,640]{1,0:T(8,128)(2,1)S(1)}, u32[]{:S(2)}, u32[]{:S(2)}) collective-permute-start(bf16[64,640]{1,0:T(8,128)(2,1)S(1)} %get-tuple-element.77), channel_id=1, source_target_pairs={{0,2},{1,3},{2,0},{3,1},{4,6},{5,7},{6,4},{7,5},{8,10},{9,11},{10,... | collective-permute-start | bytes 245768 | tf_op jit(solution)/shard_map/ppermute | solution.py:199
  22.8 1.7 %collective-permute-done.14.c = bf16[64,640]{1,0:T(8,128)(2,1)S(1)} collective-permute-done((bf16[64,640]{1,0:T(8,128)(2,1)S(1)}, bf16[64,640]{1,0:T(8,128)(2,1)S(1)}, u32[]{:S(2)}, u32[]{:S(2)}) %collective-permute-start.14) | collective-permute-done | bytes 81952 | tf_op jit(solution)/shard_map/ppermute | solution.py:199
  25.6 2.8 %collective-permute-done.15 = bf16[64,640]{1,0:T(8,128)(2,1)S(1)} collective-permute-done((bf16[64,640]{1,0:T(8,128)(2,1)S(1)}, bf16[64,640]{1,0:T(8,128)(2,1)S(1)}, u32[]{:S(2)}, u32[]{:S(2)}) %collective-permute-start.15) | collective-permute-done | bytes 81952 | tf_op jit(solution)/shard_map/ppermute | solution.py:199
  29.0 3.6 %collective-permute-done.17 = bf16[64,640]{1,0:T(8,128)(2,1)S(1)} collective-permute-done((bf16[64,640]{1,0:T(8,128)(2,1)S(1)}, bf16[64,640]{1,0:T(8,128)(2,1)S(1)}, u32[]{:S(2)}, u32[]{:S(2)}) %collective-permute-start.17) | collective-permute-done | bytes 81952 | tf_op jit(solution)/shard_map/ppermute | solution.py:199
  32.6 23.9 %collective-permute-done.19.swapped = bf16[512,1024]{1,0:T(8,128)(2,1)} collective-permute-done((bf16[512,1024]{1,0:T(8,128)(2,1)}, bf16[512,1024]{1,0:T(8,128)(2,1)}, u32[]{:S(2)}, u32[]{:S(2)}) %collective-permute-start.19) | collective-permute-done | bytes 1048608 | tf_op jit(solution)/shard_map/ppermute | solution.py:253
  56.5 18.2 %conditional.1 = (bf16[512,1024]{1,0:T(8,128)(2,1)S(1)}, f32[1,1024]{1,0:T(1,128)S(1)}, bf16[64,1024]{1,0:T(8,128)(2,1)}, bf16[64,512]{1,0:T(8,128)(2,1)S(1)}, bf16[64,512]{1,0:T(8,128)(2,1)S(1)}) conditional(s32[]{:T(128)} %convert_element_type.13, (bf16[512,1024]{1,0:T(8,128)(2,1)}, bf16[512,1024]{1,0:T(8,128)(2,1)}, ...), branch_computations={%region_2.0_spmd, %region_3.0_spmd} | conditional | bytes 3932360 | solution.py:283
  56.5 4.2 %branch_1_fun.3 = (bf16[512,1024]{1,0:T(8,128)(2,1)S(1)}, f32[1,1024]{1,0:T(1,128)S(1)}, f32[256,1024]{1,0:T(8,128)S(1)}, bf16[256,1024]{1,0:T(8,128)(2,1)S(1)},...) custom-call(s32[8]{0:T(128)S(1)} %get-tuple-element.32.order, ...), custom_call_target="tpu_custom_call" | custom-call | tf_op jit(solution)/shard_map/cond/branch_1_fun/pallas_call | solution.py:17
  60.7 2.4 %collective-permute-start.4 = (bf16[256,1024]{1,0:T(8,128)(2,1)S(1)}, bf16[256,1024]{1,0:T(8,128)(2,1)S(1)}, u32[]{:S(2)}, u32[]{:S(2)}) collective-permute-start(bf16[256,1024]{1,0:T(8,128)(2,1)S(1)} %get-tuple-element.40), channel_id=1, source_target_pairs={{0,1},{1,0},{2,3},{3,2},{4,5},{5,4},{6,7},{7,6},{8,9},{9,8},{10,11... | collective-permute-start | bytes 1572872 | tf_op jit(solution)/shard_map/cond/branch_1_fun/ppermute | solution.py:199
  63.1 1.5 %collective-permute-done.4.got = bf16[256,1024]{1,0:T(8,128)(2,1)S(1)} collective-permute-done((bf16[256,1024]{1,0:T(8,128)(2,1)S(1)}, bf16[256,1024]{1,0:T(8,128)(2,1)S(1)}, u32[]{:S(2)}, u32[]{:S(2)}) %collective-permute-start.4) | collective-permute-done | bytes 524320 | tf_op jit(solution)/shard_map/cond/branch_1_fun/ppermute | solution.py:199
  64.8 1.3 %collective-permute-start.5 = (bf16[64,1024]{1,0:T(8,128)(2,1)S(1)}, bf16[64,1024]{1,0:T(8,128)(2,1)S(1)}, u32[]{:S(2)}, u32[]{:S(2)}) collective-permute-start(bf16[64,1024]{1,0:T(8,128)(2,1)S(1)} %get-tuple-element.42), channel_id=1, source_target_pairs={{0,2},{1,3},{2,0},{3,1},{4,6},{5,7},{6,4},{7,5},{8,10},{9,11},{10,... | collective-permute-start | bytes 393224 | tf_op jit(solution)/shard_map/cond/branch_1_fun/ppermute | solution.py:199
  67.5 2.1 %collective-permute-done.5.a = bf16[64,1024]{1,0:T(8,128)(2,1)S(1)} collective-permute-done((bf16[64,1024]{1,0:T(8,128)(2,1)S(1)}, bf16[64,1024]{1,0:T(8,128)(2,1)S(1)}, u32[]{:S(2)}, u32[]{:S(2)}) %collective-permute-start.5) | collective-permute-done | bytes 131104 | tf_op jit(solution)/shard_map/cond/branch_1_fun/ppermute | solution.py:199
  70.4 2.7 %collective-permute-done.7.c = bf16[64,1024]{1,0:T(8,128)(2,1)S(1)} collective-permute-done((bf16[64,1024]{1,0:T(8,128)(2,1)S(1)}, bf16[64,1024]{1,0:T(8,128)(2,1)S(1)}, u32[]{:S(2)}, u32[]{:S(2)}) %collective-permute-start.7) | collective-permute-done | bytes 131104 | tf_op jit(solution)/shard_map/cond/branch_1_fun/ppermute | solution.py:199
  74.7 1.4 %collective-permute-start.20 = (bf16[64,512]{1,0:T(8,128)(2,1)S(1)}, bf16[64,512]{1,0:T(8,128)(2,1)S(1)}, u32[]{:S(2)}, u32[]{:S(2)}) collective-permute-start(bf16[64,512]{1,0:T(8,128)(2,1)S(1)} %get-tuple-element.102), channel_id=1, source_target_pairs={{8,0},{16,24},{9,1},{17,25},{10,2},{18,26},{11,3},{19,27},{12,4},{... | collective-permute-start | bytes 196616 | tf_op jit(solution)/shard_map/ppermute | solution.py:288
  76.1 2.2 %collective-permute-start.21 = (bf16[64,512]{1,0:T(8,128)(2,1)S(1)}, bf16[64,512]{1,0:T(8,128)(2,1)S(1)}, u32[]{:S(2)}, u32[]{:S(2)}) collective-permute-start(bf16[64,512]{1,0:T(8,128)(2,1)S(1)} %get-tuple-element.102), channel_id=1, source_target_pairs={{8,16},{16,8},{9,17},{17,9},{10,18},{18,10},{11,19},{19,11},{12,20... | collective-permute-start | bytes 196616 | tf_op jit(solution)/shard_map/ppermute | solution.py:288
  78.4 2.8 %collective-permute-done.21 = bf16[64,512]{1,0:T(8,128)(2,1)S(1)} collective-permute-done((bf16[64,512]{1,0:T(8,128)(2,1)S(1)}, bf16[64,512]{1,0:T(8,128)(2,1)S(1)}, u32[]{:S(2)}, u32[]{:S(2)}) %collective-permute-start.21) | collective-permute-done | bytes 65568 | tf_op jit(solution)/shard_map/ppermute | solution.py:288
  81.2 1.5 %collective-permute-start.22 = (bf16[64,1024]{1,0:T(8,128)(2,1)S(1)}, bf16[64,1024]{1,0:T(8,128)(2,1)S(1)}, u32[]{:S(2)}, u32[]{:S(2)}) collective-permute-start(bf16[64,1024]{1,0:T(8,128)(2,1)S(1)} %pad_maximum_fusion.3), channel_id=1, source_target_pairs={{0,2},{1,3},{2,0},{3,1},{4,6},{5,7},{6,4},{7,5},{8,10},{9,11},{10,... | collective-permute-start | bytes 393224 | tf_op jit(solution)/shard_map/ppermute | solution.py:199
  82.7 1.3 %collective-permute-start.35 = (bf16[512,1024]{1,0:T(8,128)(2,1)}, bf16[512,1024]{1,0:T(8,128)(2,1)S(1)}, u32[]{:S(2)}, u32[]{:S(2)}) collective-permute-start(bf16[512,1024]{1,0:T(8,128)(2,1)} %collective-permute-done.19.swapped), channel_id=1, source_target_pairs={{8,0},{16,24},{9,1},{17,25},{10,2},{18,26},{11,3},{19,27},{12,4},{... | collective-permute-start | bytes 3145736 | tf_op jit(solution)/shard_map/ppermute | solution.py:289
  84.0 2.2 %collective-permute-start.36 = (bf16[512,1024]{1,0:T(8,128)(2,1)}, bf16[512,1024]{1,0:T(8,128)(2,1)S(1)}, u32[]{:S(2)}, u32[]{:S(2)}) collective-permute-start(bf16[512,1024]{1,0:T(8,128)(2,1)} %collective-permute-done.18), channel_id=1, source_target_pairs={{8,16},{16,8},{9,17},{17,9},{10,18},{18,10},{11,19},{19,11},{12,20... | collective-permute-start | bytes 3145736 | tf_op jit(solution)/shard_map/ppermute | solution.py:290
  87.6 4.0 %collective-permute-done.23 = bf16[64,1024]{1,0:T(8,128)(2,1)S(1)} collective-permute-done((bf16[64,1024]{1,0:T(8,128)(2,1)S(1)}, bf16[64,1024]{1,0:T(8,128)(2,1)S(1)}, u32[]{:S(2)}, u32[]{:S(2)}) %collective-permute-start.23) | collective-permute-done | bytes 131104 | tf_op jit(solution)/shard_map/ppermute | solution.py:199
  91.6 4.4 %collective-permute-start.25 = (bf16[256,1024]{1,0:T(8,128)(2,1)S(1)}, bf16[256,1024]{1,0:T(8,128)(2,1)S(1)}, u32[]{:S(2)}, u32[]{:S(2)}) collective-permute-start(bf16[256,1024]{1,0:T(8,128)(2,1)S(1)} %pad_maximum_fusion.near), channel_id=1, source_target_pairs={{0,1},{1,0},{2,3},{3,2},{4,5},{5,4},{6,7},{7,6},{8,9},{9,8},{10,11... | collective-permute-start | bytes 1572872 | tf_op jit(solution)/shard_map/ppermute | solution.py:199
  96.0 2.2 %shard_map.41 = (bf16[512,1024]{1,0:T(8,128)(2,1)S(1)}, f32[1,1024]{1,0:T(1,128)S(1)}, f32[256,512]{1,0:T(8,128)S(1)}, bf16[256,512]{1,0:T(8,128)(2,1)S(1)}) custom-call(s32[1]{0:T(128)} %bitcast.middle, bf16[512,1024]{1,0:T(8,128)(2,1)S(1)} %copy-done.1, bf16[512,1024]{1,0:T(8,128)(2,1)} %collective-permute-done.19.swapped, ...), custom_call_target="tpu_custom_call" | custom-call | tf_op jit(solution)/shard_map/pallas_call | solution.py:17
  101.4 2.1 %collective-permute-done.28.a = bf16[64,512]{1,0:T(8,128)(2,1)S(1)} collective-permute-done((bf16[64,512]{1,0:T(8,128)(2,1)S(1)}, bf16[64,512]{1,0:T(8,128)(2,1)S(1)}, u32[]{:S(2)}, u32[]{:S(2)}) %collective-permute-start.28) | collective-permute-done | bytes 65568 | tf_op jit(solution)/shard_map/ppermute | solution.py:199
  105.3 2.2 %collective-permute-done.30.c = bf16[64,512]{1,0:T(8,128)(2,1)S(1)} collective-permute-done((bf16[64,512]{1,0:T(8,128)(2,1)S(1)}, bf16[64,512]{1,0:T(8,128)(2,1)S(1)}, u32[]{:S(2)}, u32[]{:S(2)}) %collective-permute-start.30) | collective-permute-done | bytes 65568 | tf_op jit(solution)/shard_map/ppermute | solution.py:199
  108.2 3.1 %shard_map.45.held = f32[512,1024]{1,0:T(8,128)S(1)} custom-call(bf16[512,1024]{1,0:T(8,128)(2,1)S(1)} %shard_map.40.first, bf16[512,640]{1,0:T(8,128)(2,1)S(1)} %shard_map.44.with_own, bf16[512,1024]{1,0:T(8,128)(2,1)S(1)} %get-tuple-element.90.own, bf16[512,1024]{1,0:T(8,128)(2,1)S(1)} %get-tuple-element.91.beside, bf16[512,1024]{1,0:T(8,128)(2,1)} %z.3, ...), custom_call_target="tpu_custom_call" | custom-call | tf_op jit(solution)/shard_map/pallas_call | solution.py:17
  116.9 3.9 %collective-permute-start.37 = (bf16[256,512]{1,0:T(8,128)(2,1)S(1)}, bf16[256,512]{1,0:T(8,128)(2,1)S(1)}, u32[]{:S(2)}, u32[]{:S(2)}) collective-permute-start(bf16[256,512]{1,0:T(8,128)(2,1)S(1)} %pad_maximum_fusion.2.near), channel_id=1, source_target_pairs={{0,1},{1,0},{2,3},{3,2},{4,5},{5,4},{6,7},{7,6},{8,9},{9,8},{10,11... | collective-permute-start | bytes 786440 | tf_op jit(solution)/shard_map/ppermute | solution.py:199
  122.5 3.0 %shard_map.47 = f32[512,1024]{1,0:T(8,128)} custom-call(s32[1]{0:T(128)} %bitcast.middle, bf16[512,1024]{1,0:T(8,128)(2,1)S(1)} %shard_map.40.first, bf16[512,512]{1,0:T(8,128)(2,1)S(1)} %shard_map.46.second, bf16[512,1024]{1,0:T(8,128)(2,1)S(1)} %get-tuple-element.100.opposite, bf16[512,1024]{1,0:T(8,128)(2,1)S(1)} %get-tuple-element.90.own, ...), custom_call_target="tpu_custom_call" | custom-call | tf_op jit(solution)/shard_map/pallas_call | solution.py:17
  (71 shorter events, 27.2 us)
Async XLA Ops:
  3.1 8.5 %collective-permute-start.10 = (f32[2,1024]{1,0:T(2,128)S(1)}, f32[2,1024]{1,0:T(2,128)S(1)}, u32[]{:S(2)}, u32[]{:S(2)}) collective-permute-start(f32[2,1024]{1,0:T(2,128)S(1)} %pad_maximum_fusion.4), channel_id=1, source_target_pairs={{0,24},{8,0},{16,8},{24,16},{1,25},{9,1},{17,9},{25,17},{2,26},{10... | collective-permute-start | bytes 24584 | tf_op jit(solution)/shard_map/ppermute | solution.py:249
  3.1 8.4 %collective-permute-start.8 = (f32[2,1024]{1,0:T(2,128)S(1)}, f32[2,1024]{1,0:T(2,128)S(1)}, u32[]{:S(2)}, u32[]{:S(2)}) collective-permute-start(f32[2,1024]{1,0:T(2,128)S(1)} %pad_maximum_fusion.4), channel_id=1, source_target_pairs={{0,8},{8,16},{16,24},{24,0},{1,9},{9,17},{17,25},{25,1},{2,10},{10... | collective-permute-start | bytes 24584 | tf_op jit(solution)/shard_map/ppermute | solution.py:249
  4.6 7.0 %collective-permute-start.9 = (f32[2,1024]{1,0:T(2,128)S(1)}, f32[2,1024]{1,0:T(2,128)S(1)}, u32[]{:S(2)}, u32[]{:S(2)}) collective-permute-start(f32[2,1024]{1,0:T(2,128)S(1)} %pad_maximum_fusion.4), channel_id=1, source_target_pairs={{0,16},{8,24},{16,0},{24,8},{1,17},{9,25},{17,1},{25,9},{2,18},{10... | collective-permute-start | bytes 24584 | tf_op jit(solution)/shard_map/ppermute | solution.py:249
  8.7 23.9 %collective-permute-start.18 = (bf16[512,1024]{1,0:T(8,128)(2,1)}, bf16[512,1024]{1,0:T(8,128)(2,1)}, u32[]{:S(2)}, u32[]{:S(2)}) collective-permute-start(bf16[512,1024]{1,0:T(8,128)(2,1)} %z.3), channel_id=1, source_target_pairs={{0,8},{8,0},{16,24},{24,16},{1,9},{9,1},{17,25},{25,17},{2,10},{10... | collective-permute-start | bytes 3145736 | tf_op jit(solution)/shard_map/ppermute | solution.py:252
  8.7 47.8 %collective-permute-start.19 = (bf16[512,1024]{1,0:T(8,128)(2,1)}, bf16[512,1024]{1,0:T(8,128)(2,1)}, u32[]{:S(2)}, u32[]{:S(2)}) collective-permute-start(bf16[512,1024]{1,0:T(8,128)(2,1)} %z.3), channel_id=1, source_target_pairs={{8,16},{16,8},{9,17},{17,9},{10,18},{18,10},{11,19},{19,11},{12,20... | collective-permute-start | bytes 3145736 | tf_op jit(solution)/shard_map/ppermute | solution.py:253
  14.6 3.1 %collective-permute-start.11 = (bf16[256,640]{1,0:T(8,128)(2,1)S(1)}, bf16[256,640]{1,0:T(8,128)(2,1)S(1)}, u32[]{:S(2)}, u32[]{:S(2)}) collective-permute-start(bf16[256,640]{1,0:T(8,128)(2,1)S(1)} %get-tuple-element.75), channel_id=1, source_target_pairs={{0,1},{1,0},{2,3},{3,2},{4,5},{5,4},{6,7},{7,6},{8,9},{9,8},{10,11... | collective-permute-start | bytes 983048 | tf_op jit(solution)/shard_map/ppermute | solution.py:199
  17.8 3.8 %collective-permute-start.12 = (bf16[64,640]{1,0:T(8,128)(2,1)S(1)}, bf16[64,640]{1,0:T(8,128)(2,1)S(1)}, u32[]{:S(2)}, u32[]{:S(2)}) collective-permute-start(bf16[64,640]{1,0:T(8,128)(2,1)S(1)} %get-tuple-element.77), channel_id=1, source_target_pairs={{0,2},{1,3},{2,0},{3,1},{4,6},{5,7},{6,4},{7,5},{8,10},{9,11},{10,... | collective-permute-start | bytes 245768 | tf_op jit(solution)/shard_map/ppermute | solution.py:199
  19.1 3.7 %collective-permute-start.13 = (bf16[64,640]{1,0:T(8,128)(2,1)S(1)}, bf16[64,640]{1,0:T(8,128)(2,1)S(1)}, u32[]{:S(2)}, u32[]{:S(2)}) collective-permute-start(bf16[64,640]{1,0:T(8,128)(2,1)S(1)} %get-tuple-element.78), channel_id=1, source_target_pairs={{0,4},{1,5},{2,6},{3,7},{4,0},{5,1},{6,2},{7,3},{8,12},{9,13},{10,... | collective-permute-start | bytes 245768 | tf_op jit(solution)/shard_map/ppermute | solution.py:199
  20.3 4.2 %collective-permute-start.14 = (bf16[64,640]{1,0:T(8,128)(2,1)S(1)}, bf16[64,640]{1,0:T(8,128)(2,1)S(1)}, u32[]{:S(2)}, u32[]{:S(2)}) collective-permute-start(bf16[64,640]{1,0:T(8,128)(2,1)S(1)} %get-tuple-element.79), channel_id=1, source_target_pairs={{0,6},{1,7},{2,4},{3,5},{4,2},{5,3},{6,0},{7,1},{8,14},{9,15},{10,... | collective-permute-start | bytes 245768 | tf_op jit(solution)/shard_map/ppermute | solution.py:199
  21.6 74.4 %collective-permute-start.26 = (bf16[512,1024]{1,0:T(8,128)(2,1)}, bf16[512,1024]{1,0:T(8,128)(2,1)S(1)}, u32[]{:S(2)}, u32[]{:S(2)}) collective-permute-start(bf16[512,1024]{1,0:T(8,128)(2,1)} %z.3), channel_id=1, source_target_pairs={{0,24},{24,0},{1,25},{25,1},{2,26},{26,2},{3,27},{27,3},{4,28},{28... | collective-permute-start | bytes 3145736 | tf_op jit(solution)/shard_map/ppermute | solution.py:254
  24.6 3.8 %collective-permute-start.15 = (bf16[64,640]{1,0:T(8,128)(2,1)S(1)}, bf16[64,640]{1,0:T(8,128)(2,1)S(1)}, u32[]{:S(2)}, u32[]{:S(2)}) collective-permute-start(bf16[64,640]{1,0:T(8,128)(2,1)S(1)} %shard_map.39), channel_id=1, source_target_pairs={{0,2},{1,3},{2,0},{3,1},{4,6},{5,7},{6,4},{7,5},{8,10},{9,11},{10,... | collective-permute-start | bytes 245768 | tf_op jit(solution)/shard_map/ppermute | solution.py:199
  25.3 3.7 %collective-permute-start.16 = (bf16[64,640]{1,0:T(8,128)(2,1)S(1)}, bf16[64,640]{1,0:T(8,128)(2,1)S(1)}, u32[]{:S(2)}, u32[]{:S(2)}) collective-permute-start(bf16[64,640]{1,0:T(8,128)(2,1)S(1)} %shard_map.39), channel_id=1, source_target_pairs={{0,4},{1,5},{2,6},{3,7},{4,0},{5,1},{6,2},{7,3},{8,12},{9,13},{10,... | collective-permute-start | bytes 245768 | tf_op jit(solution)/shard_map/ppermute | solution.py:199
  28.4 4.2 %collective-permute-start.17 = (bf16[64,640]{1,0:T(8,128)(2,1)S(1)}, bf16[64,640]{1,0:T(8,128)(2,1)S(1)}, u32[]{:S(2)}, u32[]{:S(2)}) collective-permute-start(bf16[64,640]{1,0:T(8,128)(2,1)S(1)} %shard_map.39), channel_id=1, source_target_pairs={{0,6},{1,7},{2,4},{3,5},{4,2},{5,3},{6,0},{7,1},{8,14},{9,15},{10,... | collective-permute-start | bytes 245768 | tf_op jit(solution)/shard_map/ppermute | solution.py:199
  60.7 4.0 %collective-permute-start.4 = (bf16[256,1024]{1,0:T(8,128)(2,1)S(1)}, bf16[256,1024]{1,0:T(8,128)(2,1)S(1)}, u32[]{:S(2)}, u32[]{:S(2)}) collective-permute-start(bf16[256,1024]{1,0:T(8,128)(2,1)S(1)} %get-tuple-element.40), channel_id=1, source_target_pairs={{0,1},{1,0},{2,3},{3,2},{4,5},{5,4},{6,7},{7,6},{8,9},{9,8},{10,11... | collective-permute-start | bytes 1572872 | tf_op jit(solution)/shard_map/cond/branch_1_fun/ppermute | solution.py:199
  64.8 4.8 %collective-permute-start.5 = (bf16[64,1024]{1,0:T(8,128)(2,1)S(1)}, bf16[64,1024]{1,0:T(8,128)(2,1)S(1)}, u32[]{:S(2)}, u32[]{:S(2)}) collective-permute-start(bf16[64,1024]{1,0:T(8,128)(2,1)S(1)} %get-tuple-element.42), channel_id=1, source_target_pairs={{0,2},{1,3},{2,0},{3,1},{4,6},{5,7},{6,4},{7,5},{8,10},{9,11},{10,... | collective-permute-start | bytes 393224 | tf_op jit(solution)/shard_map/cond/branch_1_fun/ppermute | solution.py:199
  66.0 4.4 %collective-permute-start.6 = (bf16[64,1024]{1,0:T(8,128)(2,1)S(1)}, bf16[64,1024]{1,0:T(8,128)(2,1)S(1)}, u32[]{:S(2)}, u32[]{:S(2)}) collective-permute-start(bf16[64,1024]{1,0:T(8,128)(2,1)S(1)} %get-tuple-element.43), channel_id=1, source_target_pairs={{0,4},{1,5},{2,6},{3,7},{4,0},{5,1},{6,2},{7,3},{8,12},{9,13},{10,... | collective-permute-start | bytes 393224 | tf_op jit(solution)/shard_map/cond/branch_1_fun/ppermute | solution.py:199
  67.3 5.8 %collective-permute-start.7 = (bf16[64,1024]{1,0:T(8,128)(2,1)S(1)}, bf16[64,1024]{1,0:T(8,128)(2,1)S(1)}, u32[]{:S(2)}, u32[]{:S(2)}) collective-permute-start(bf16[64,1024]{1,0:T(8,128)(2,1)S(1)} %get-tuple-element.44), channel_id=1, source_target_pairs={{0,6},{1,7},{2,4},{3,5},{4,2},{5,3},{6,0},{7,1},{8,14},{9,15},{10,... | collective-permute-start | bytes 393224 | tf_op jit(solution)/shard_map/cond/branch_1_fun/ppermute | solution.py:199
  74.7 3.6 %collective-permute-start.20 = (bf16[64,512]{1,0:T(8,128)(2,1)S(1)}, bf16[64,512]{1,0:T(8,128)(2,1)S(1)}, u32[]{:S(2)}, u32[]{:S(2)}) collective-permute-start(bf16[64,512]{1,0:T(8,128)(2,1)S(1)} %get-tuple-element.102), channel_id=1, source_target_pairs={{8,0},{16,24},{9,1},{17,25},{10,2},{18,26},{11,3},{19,27},{12,4},{... | collective-permute-start | bytes 196616 | tf_op jit(solution)/shard_map/ppermute | solution.py:288
  76.1 5.0 %collective-permute-start.21 = (bf16[64,512]{1,0:T(8,128)(2,1)S(1)}, bf16[64,512]{1,0:T(8,128)(2,1)S(1)}, u32[]{:S(2)}, u32[]{:S(2)}) collective-permute-start(bf16[64,512]{1,0:T(8,128)(2,1)S(1)} %get-tuple-element.102), channel_id=1, source_target_pairs={{8,16},{16,8},{9,17},{17,9},{10,18},{18,10},{11,19},{19,11},{12,20... | collective-permute-start | bytes 196616 | tf_op jit(solution)/shard_map/ppermute | solution.py:288
  81.2 5.4 %collective-permute-start.22 = (bf16[64,1024]{1,0:T(8,128)(2,1)S(1)}, bf16[64,1024]{1,0:T(8,128)(2,1)S(1)}, u32[]{:S(2)}, u32[]{:S(2)}) collective-permute-start(bf16[64,1024]{1,0:T(8,128)(2,1)S(1)} %pad_maximum_fusion.3), channel_id=1, source_target_pairs={{0,2},{1,3},{2,0},{3,1},{4,6},{5,7},{6,4},{7,5},{8,10},{9,11},{10,... | collective-permute-start | bytes 393224 | tf_op jit(solution)/shard_map/ppermute | solution.py:199
  82.7 34.2 %collective-permute-start.35 = (bf16[512,1024]{1,0:T(8,128)(2,1)}, bf16[512,1024]{1,0:T(8,128)(2,1)S(1)}, u32[]{:S(2)}, u32[]{:S(2)}) collective-permute-start(bf16[512,1024]{1,0:T(8,128)(2,1)} %collective-permute-done.19.swapped), channel_id=1, source_target_pairs={{8,0},{16,24},{9,1},{17,25},{10,2},{18,26},{11,3},{19,27},{12,4},{... | collective-permute-start | bytes 3145736 | tf_op jit(solution)/shard_map/ppermute | solution.py:289
  84.0 32.9 %collective-permute-start.36 = (bf16[512,1024]{1,0:T(8,128)(2,1)}, bf16[512,1024]{1,0:T(8,128)(2,1)S(1)}, u32[]{:S(2)}, u32[]{:S(2)}) collective-permute-start(bf16[512,1024]{1,0:T(8,128)(2,1)} %collective-permute-done.18), channel_id=1, source_target_pairs={{8,16},{16,8},{9,17},{17,9},{10,18},{18,10},{11,19},{19,11},{12,20... | collective-permute-start | bytes 3145736 | tf_op jit(solution)/shard_map/ppermute | solution.py:290
  86.2 5.3 %collective-permute-start.23 = (bf16[64,1024]{1,0:T(8,128)(2,1)S(1)}, bf16[64,1024]{1,0:T(8,128)(2,1)S(1)}, u32[]{:S(2)}, u32[]{:S(2)}) collective-permute-start(bf16[64,1024]{1,0:T(8,128)(2,1)S(1)} %pad_maximum_fusion.3), channel_id=1, source_target_pairs={{0,4},{1,5},{2,6},{3,7},{4,0},{5,1},{6,2},{7,3},{8,12},{9,13},{10,... | collective-permute-start | bytes 393224 | tf_op jit(solution)/shard_map/ppermute | solution.py:199
  86.6 4.9 %collective-permute-start.24 = (bf16[64,1024]{1,0:T(8,128)(2,1)S(1)}, bf16[64,1024]{1,0:T(8,128)(2,1)S(1)}, u32[]{:S(2)}, u32[]{:S(2)}) collective-permute-start(bf16[64,1024]{1,0:T(8,128)(2,1)S(1)} %pad_maximum_fusion.3), channel_id=1, source_target_pairs={{0,6},{1,7},{2,4},{3,5},{4,2},{5,3},{6,0},{7,1},{8,14},{9,15},{10,... | collective-permute-start | bytes 393224 | tf_op jit(solution)/shard_map/ppermute | solution.py:199
  91.6 16.0 %collective-permute-start.25 = (bf16[256,1024]{1,0:T(8,128)(2,1)S(1)}, bf16[256,1024]{1,0:T(8,128)(2,1)S(1)}, u32[]{:S(2)}, u32[]{:S(2)}) collective-permute-start(bf16[256,1024]{1,0:T(8,128)(2,1)S(1)} %pad_maximum_fusion.near), channel_id=1, source_target_pairs={{0,1},{1,0},{2,3},{3,2},{4,5},{5,4},{6,7},{7,6},{8,9},{9,8},{10,11... | collective-permute-start | bytes 1572872 | tf_op jit(solution)/shard_map/ppermute | solution.py:199
  99.9 3.6 %collective-permute-start.28 = (bf16[64,512]{1,0:T(8,128)(2,1)S(1)}, bf16[64,512]{1,0:T(8,128)(2,1)S(1)}, u32[]{:S(2)}, u32[]{:S(2)}) collective-permute-start(bf16[64,512]{1,0:T(8,128)(2,1)S(1)} %get-tuple-element.87), channel_id=1, source_target_pairs={{0,2},{1,3},{2,0},{3,1},{4,6},{5,7},{6,4},{7,5},{8,10},{9,11},{10,... | collective-permute-start | bytes 196616 | tf_op jit(solution)/shard_map/ppermute | solution.py:199
  101.2 4.1 %collective-permute-start.29 = (bf16[64,512]{1,0:T(8,128)(2,1)S(1)}, bf16[64,512]{1,0:T(8,128)(2,1)S(1)}, u32[]{:S(2)}, u32[]{:S(2)}) collective-permute-start(bf16[64,512]{1,0:T(8,128)(2,1)S(1)} %get-tuple-element.88), channel_id=1, source_target_pairs={{0,4},{1,5},{2,6},{3,7},{4,0},{5,1},{6,2},{7,3},{8,12},{9,13},{10,... | collective-permute-start | bytes 196616 | tf_op jit(solution)/shard_map/ppermute | solution.py:199
  103.5 4.0 %collective-permute-start.30 = (bf16[64,512]{1,0:T(8,128)(2,1)S(1)}, bf16[64,512]{1,0:T(8,128)(2,1)S(1)}, u32[]{:S(2)}, u32[]{:S(2)}) collective-permute-start(bf16[64,512]{1,0:T(8,128)(2,1)S(1)} %get-tuple-element.89), channel_id=1, source_target_pairs={{0,6},{1,7},{2,4},{3,5},{4,2},{5,3},{6,0},{7,1},{8,14},{9,15},{10,... | collective-permute-start | bytes 196616 | tf_op jit(solution)/shard_map/ppermute | solution.py:199
  111.4 3.2 %collective-permute-start.32 = (bf16[64,512]{1,0:T(8,128)(2,1)S(1)}, bf16[64,512]{1,0:T(8,128)(2,1)S(1)}, u32[]{:S(2)}, u32[]{:S(2)}) collective-permute-start(bf16[64,512]{1,0:T(8,128)(2,1)S(1)} %shard_map.43), channel_id=1, source_target_pairs={{0,2},{1,3},{2,0},{3,1},{4,6},{5,7},{6,4},{7,5},{8,10},{9,11},{10,... | collective-permute-start | bytes 196616 | tf_op jit(solution)/shard_map/ppermute | solution.py:199
  112.6 3.1 %collective-permute-start.33 = (bf16[64,512]{1,0:T(8,128)(2,1)S(1)}, bf16[64,512]{1,0:T(8,128)(2,1)S(1)}, u32[]{:S(2)}, u32[]{:S(2)}) collective-permute-start(bf16[64,512]{1,0:T(8,128)(2,1)S(1)} %shard_map.43), channel_id=1, source_target_pairs={{0,4},{1,5},{2,6},{3,7},{4,0},{5,1},{6,2},{7,3},{8,12},{9,13},{10,... | collective-permute-start | bytes 196616 | tf_op jit(solution)/shard_map/ppermute | solution.py:199
  112.9 4.0 %collective-permute-start.34 = (bf16[64,512]{1,0:T(8,128)(2,1)S(1)}, bf16[64,512]{1,0:T(8,128)(2,1)S(1)}, u32[]{:S(2)}, u32[]{:S(2)}) collective-permute-start(bf16[64,512]{1,0:T(8,128)(2,1)S(1)} %shard_map.43), channel_id=1, source_target_pairs={{0,6},{1,7},{2,4},{3,5},{4,2},{5,3},{6,0},{7,1},{8,14},{9,15},{10,... | collective-permute-start | bytes 196616 | tf_op jit(solution)/shard_map/ppermute | solution.py:199
  116.9 5.0 %collective-permute-start.37 = (bf16[256,512]{1,0:T(8,128)(2,1)S(1)}, bf16[256,512]{1,0:T(8,128)(2,1)S(1)}, u32[]{:S(2)}, u32[]{:S(2)}) collective-permute-start(bf16[256,512]{1,0:T(8,128)(2,1)S(1)} %pad_maximum_fusion.2.near), channel_id=1, source_target_pairs={{0,1},{1,0},{2,3},{3,2},{4,5},{5,4},{6,7},{7,6},{8,9},{9,8},{10,11... | collective-permute-start | bytes 786440 | tf_op jit(solution)/shard_map/ppermute | solution.py:199
  (6 other events, 48.9 us)

commit v9 on v8

--- a/solution.py
+++ b/solution.py
@@ -83,45 +83,38 @@
     sent[:, rows:] = high_low(norm[half:], (half, NORM)).astype(jnp.bfloat16)
 
 
-def first_kernel(order, turned, beside_in, opposite_in, mean, *refs):
-    beside, beside_square, kept, sent, opposite, turned_beside, unused = refs
+def split_sum(inner, kept, sent, here):
+    half = kept.shape[0]
+    kept[:, here] = inner[:half]
+    sent[:, here] = inner[half:].astype(jnp.bfloat16)
+
+
+def middle_kernel(
+    order, turned, beside_in, opposite_in, mean,
+    beside, beside_square, opposite, opposite_square, kept, sent, turned_beside,
+):
     rows = beside.shape[0]
-    half = rows // 2
-
-    def put(left, right, k):
-        inner = gram(left[...], right[...])
-        kept[:, k * rows:(k + 1) * rows] = inner[:half]
-        sent[:, k * rows:(k + 1) * rows] = inner[half:].astype(jnp.bfloat16)
-
     centered_into(beside, beside_in, mean[...], beside_square)
-    put(turned, beside, 0)
-    centered_into(opposite, opposite_in, mean[...], unused)
+    split_sum(gram(turned[...], beside[...]), kept, sent, slice(0, rows))
+    centered_into(opposite, opposite_in, mean[...], opposite_square)
+    split_sum(gram(turned[...], opposite[...]), kept, sent, slice(rows, 2 * rows))
     turn_into(turned_beside, order, beside)
-    put(turned_beside, opposite, 1)
-
-
-def first_end_kernel(turned, beside_in, mean, beside, beside_square, kept, sent):
-    half = beside.shape[0] // 2
-    centered_into(beside, beside_in, mean[...], beside_square)
-    inner = gram(turned[...], beside[...])
-    kept[...] = inner[:half]
-    sent[...] = inner[half:].astype(jnp.bfloat16)
-
-
-def second_kernel(middle, turned, swapped, end, mean, opposite, square, kept, sent):
-    half = opposite.shape[0] // 2
-
-    @pl.when(middle[0] == 1)
-    def _():
-        centered_into(opposite, swapped, mean[...], square)
-
-    @pl.when(middle[0] == 0)
-    def _():
-        centered_into(opposite, end, mean[...], square)
-
-    inner = gram(turned[...], opposite[...])
-    kept[...] = inner[:half]
-    sent[...] = inner[half:].astype(jnp.bfloat16)
+    split_sum(gram(turned_beside[...], opposite[...]), kept, sent, slice(2 * rows, 3 * rows))
+
+
+def block_kernel(turned, block_in, mean, block, square, kept, sent):
+    centered_into(block, block_in, mean[...], square)
+    split_sum(gram(turned[...], block[...]), kept, sent, slice(None))
+
+
+def stats_kernel(z, out):
+    rows = z.shape[0]
+    base = z[:16, :].astype(jnp.float32)[:1]
+    apart = z[...].astype(jnp.float32) - base
+    total = jnp.sum(apart, axis=0, keepdims=True)
+    away = total / rows
+    out[:1, :] = base + away
+    out[1:, :] = jnp.sum(apart * apart, axis=0, keepdims=True) - total * away
 
 
 def with_norm(x, last):
@@ -159,7 +152,7 @@
 
 
 def held_kernel(
-    total, first, with_own, own, beside, z, other,
+    total, with_own, own, z, other,
     own_square, beside_square, opposite_square, mean, spread, held,
 ):
     rows, width = own.shape
@@ -173,12 +166,11 @@
         plain = anchor - other[:, here].astype(jnp.float32) - total / (4.0 * (total - 1)) * hinge
         square = own_square[:, here] + beside_square[:, here] + opposite_square[:, here]
         product = dot(with_own[:, :rows], own[:, here])
-        product = product + dot(first[:, :rows], beside[:, here])
         product = product + own[:, here].astype(jnp.float32) * (norm - square)
         held[:, here] = plain + coefficient(total) * product
 
 
-def last_kernel(total, middle, first, second, opposite, own, held, mean, out, over, result):
+def last_kernel(total, middle, inner, beside, opposite, own, held, mean, out, over, result):
     rows, width = own.shape
 
     def put(arrived, product_of):
@@ -187,7 +179,9 @@
             block = (arrived[:, here].astype(jnp.float32) - mean[:, here]).astype(jnp.bfloat16)
             wide = block.astype(jnp.float32)
             square = jnp.sum(wide * wide, axis=0, keepdims=True)
-            product = dot(second[...], opposite[:, here]) + product_of(first[:, rows:], block)
+            product = dot(inner[:, :rows], beside[:, here])
+            product = product + dot(inner[:, rows:2 * rows], opposite[:, here])
+            product = product + product_of(inner[:, 2 * rows:], block)
             product = product - own[:, here].astype(jnp.float32) * square
             result[:, here] = held[:, here] + coefficient(total) * product
 
@@ -238,20 +232,13 @@
     half = rows // 2
     flat, block = ((1, width), jnp.float32), ((rows, width), jnp.bfloat16)
 
-    base = z_anchor[:1].astype(jnp.float32)
-    apart = z_anchor.astype(jnp.float32) - base
-    stats = jnp.concatenate(
-        [jnp.sum(apart, axis=0, keepdims=True), jnp.sum(apart * apart, axis=0, keepdims=True)]
-    )
-    away = stats[:1] / rows
-    stats = jnp.concatenate([base + away, stats[1:] - stats[:1] * away])
+    stats = kernel_call(stats_kernel, [((2, width), jnp.float32)], scratch=12)(z_anchor)[0]
     all_stats = [stats] + [
         lax.ppermute(stats, "dp", [(i, (i + k) % 4) for i in range(4)]) for k in (1, 2, 3)
     ]
-    ahead = after(z_anchor, stats)
+    ahead = after(z_anchor, *all_stats)
     beside_in = lax.ppermute(ahead, "dp", [(i, i ^ 1) for i in range(4)])
     swapped = lax.ppermute(ahead, "dp", across)
-    end = lax.ppermute(ahead, "dp", [(0, 3), (3, 0)])
     mean = (all_stats[0][:1] + all_stats[1][:1] + all_stats[2][:1] + all_stats[3][:1]) / 4
     spread = 0.0
     for one in all_stats:
@@ -264,47 +251,60 @@
     own, turned, own_square, kept, sent = kernel_call(
         own_kernel, [block, block, flat, *summands(rows + NORM)], smem=1, scratch=12
     )(order, z_anchor, mean)
-    with_own = gather_chips(scatter(*halve(kept, sent, rows), last=rows))
-
-    def on_middle(order, turned, beside_in, swapped, mean):
-        beside, square, kept, sent, *_ = kernel_call(
-            first_kernel,
-            [block, flat, *summands(2 * rows), block, block, flat], smem=1, scratch=12,
+    with_own = gather_cores(gather_chips(scatter(*halve(kept, sent, rows), last=rows)), order)
+
+    end = lax.ppermute(after(z_anchor, beside_in, swapped, with_own), "dp", [(0, 3), (3, 0)])
+
+    def first_of_middle(order, turned, beside_in, swapped, mean):
+        *blocks, kept, sent, _ = kernel_call(
+            middle_kernel, [block, flat, block, flat, *summands(3 * rows), block],
+            smem=1, scratch=12,
         )(order, turned, beside_in, swapped, mean)
-        return beside, square, scatter(*halve(kept, sent))
-
-    def on_end(order, turned, beside_in, swapped, mean):
+        return *blocks, scatter(*halve(kept, sent))
+
+    def first_of_end(order, turned, beside_in, swapped, mean):
         beside, square, kept, sent = kernel_call(
-            first_end_kernel, [block, flat, *summands(rows)], scratch=12
+            block_kernel, [block, flat, *summands(rows)], scratch=12
         )(turned, beside_in, mean)
         first = scatter(*halve(kept, sent))
-        return beside, square, jnp.concatenate([first, jnp.zeros_like(first)], axis=1)
-
-    beside, beside_square, first = lax.cond(
-        middle[0] == 1, on_middle, on_end,
+        first = jnp.concatenate([first, jnp.zeros((rows // 8, 2 * rows), first.dtype)], axis=1)
+        return beside, square, swapped, jnp.zeros_like(square), first
+
+    beside, beside_square, opposite, opposite_square, first = lax.cond(
+        middle[0] == 1, first_of_middle, first_of_end,
         order, after(turned, with_own), beside_in, swapped, mean,
     )
-    with_own = gather_cores(with_own, order)
-    handed = [lax.ppermute(first[:, rows:], "dp", p) for p in (outward, across)]
-    out = lax.ppermute(after(swapped, first), "dp", outward)
-    over = lax.ppermute(after(beside_in, first), "dp", across)
-    first = jnp.concatenate([first[:, :rows], handed[0] + handed[1]], axis=1)
-    first = gather_chips(first)
-
-    opposite, opposite_square, kept, sent = kernel_call(
-        second_kernel, [block, flat, *summands(rows)], smem=1, scratch=12
-    )(middle, after(turned, first), swapped, end, mean)
-    first = gather_cores(first, order)
-    halved = halve(kept, sent)
+    handed = [lax.ppermute(first[:, 2 * rows:], "dp", p) for p in (outward, across)]
+    out = lax.ppermute(after(swapped, *handed), "dp", outward)
+    over = lax.ppermute(after(beside_in, *handed), "dp", across)
+    handed = handed[0] + handed[1]
     result = ((rows, width), jnp.float32)
-    held = kernel_call(functools.partial(held_kernel, total), [result], scratch=12)(
-        first, with_own, own, beside, z_anchor, z_other,
-        own_square, beside_square, after(opposite_square, halved[0]), mean, spread,
-    )[0]
-    second = after(gather_chips(after(scatter(*halved), held)), out, over)
-    second = gather_cores(second, order)
+
+    def hold(opposite_square):
+        return kernel_call(functools.partial(held_kernel, total), [result], scratch=12)(
+            with_own, own, z_anchor, z_other,
+            own_square, beside_square, opposite_square, mean, spread,
+        )[0]
+
+    def second_of_middle(turned, end, opposite, opposite_square, first, handed):
+        inner = jnp.concatenate([first[:, :2 * rows], handed], axis=1)
+        return opposite, gather_chips(inner), hold(opposite_square)
+
+    def second_of_end(turned, end, opposite, opposite_square, first, handed):
+        opposite, opposite_square, kept, sent = kernel_call(
+            block_kernel, [block, flat, *summands(rows)], scratch=12
+        )(turned, end, mean)
+        inner = scatter(*halve(kept, sent))
+        inner = jnp.concatenate([first[:, :rows], inner, handed], axis=1)
+        return opposite, gather_chips(inner), hold(opposite_square)
+
+    opposite, inner, held = lax.cond(
+        middle[0] == 1, second_of_middle, second_of_end,
+        turned, end, opposite, opposite_square, first, handed,
+    )
+    inner = gather_cores(inner, order, out, over)
     return kernel_call(functools.partial(last_kernel, total), [result], smem=1, scratch=12)(
-        middle, first, second, opposite, own, held, mean, out, over
+        middle, inner, beside, opposite, own, held, mean, out, over
     )[0]
 
 

time: 126 us -> 102 us (0.81)
  waiting for transfers between devices: 58.1 us -> 42.1 us
  starting transfers between devices: 43.9 us -> 36.7 us
  other arithmetic: 3.87 us -> 0.81 us
    ppermute x1, waiting for transfers between devices: 23.9 us -> 0.01 us  [by_line(): swapped = lax.ppermute(ahead, 'dp', across)]
    ppermute x5, waiting for transfers between devices: 2.8 us -> 15.8 us  [the longest x1 6.64 us: by_line(): out = lax.ppermute(after(swapped, *handed), 'dp', outward)]
    ppermute x24 -> x16, starting transfers between devices: 28.2 us -> 18.2 us  [to_partner(): return lax.ppermute(x, 'feat', [(i, i ^ step) for i in range(8)])]
    ppermute x24 -> x16, waiting for transfers between devices: 31.5 us -> 26.1 us  [to_partner(): return lax.ppermute(x, 'feat', [(i, i ^ step) for i in range(8)])]
    ppermute x5, starting transfers between devices: 7.88 us -> 9.86 us  [the longest x2 3.2 us: by_line(): lax.ppermute(first[:, 2 * rows:], 'dp', p)]
    reduce_sum x1 -> x0, other arithmetic: 1.59 us -> none  [by_line(): jnp.sum(apart * apart, axis=0, keepdims=True)]
    ppermute x1, starting transfers between devices: 2.18 us -> 3.66 us  [by_line(): swapped = lax.ppermute(ahead, 'dp', across)]
    pallas_call x14 -> x11, Pallas kernels: 18.4 us -> 19.2 us  [call(): pl.pallas_call(body, out_shape=[jax.ShapeDtypeStruct(s, t) for s, t in ou...]
  transfers between devices with their start and end apart: 34 -> 26, of which waited for: 20 -> 18; matrix products, arithmetic and copies ran while one was open for 1% -> 3% of each run, Pallas kernels for 12% -> 12%
where the time goes in v9:
time: 102 us; the launch traced here: 101 us
  waiting for transfers between devices  42.1 us (41%)
  starting transfers between devices  36.7 us (36%)
  Pallas kernels  19.2 us (19%)
  local copies, waits for them, and re-layouts  1.78 us (2%)
    ppermute x16, waiting for transfers between devices, to_partner(): return lax.ppermute(x, 'feat', [(i, i ^ step) for i in range(8)])  26.1 us
    pallas_call x11, Pallas kernels, call(): pl.pallas_call(body, out_shape=[jax.ShapeDtypeStruct(s, t) for s, t in ou...  19.2 us
    ppermute x16, starting transfers between devices, to_partner(): return lax.ppermute(x, 'feat', [(i, i ^ step) for i in range(8)])  18.2 us
    ppermute x1, waiting for transfers between devices, by_line(): out = lax.ppermute(after(swapped, *handed), 'dp', outward)  6.64 us
    ppermute x2, waiting for transfers between devices, by_line(): lax.ppermute(first[:, 2 * rows:], 'dp', p)  5.39 us
    ppermute x3, starting transfers between devices, by_line(): lax.ppermute(stats, 'dp', [(i, (i + k) % 4) for i in range(4)])  4.72 us
    ppermute x1, waiting for transfers between devices, by_line(): over = lax.ppermute(after(beside_in, *handed), 'dp', across)  3.75 us
    ppermute x1, starting transfers between devices, by_line(): swapped = lax.ppermute(ahead, 'dp', across)  3.66 us
  transfers between devices with their start and end apart: 26, of which 18 were waited for; matrix products, arithmetic and copies ran while one was open for 3% of the time, Pallas kernels for 12%

profile of v9, /device:TPU:9, one launch (start us, length us, event | category | flops | bytes accessed | tf_op | source)
XLA Modules:
  0.0 100.8 jit_solution(3514477917280009131)
XLA Ops:
  0.0 1.9 %shard_map.37 = f32[2,1024]{1,0:T(2,128)S(1)} custom-call(bf16[512,1024]{1,0:T(8,128)(2,1)} %z.3), custom_call_target="tpu_custom_call" | custom-call | tf_op jit(solution)/shard_map/pallas_call | solution.py:17
  2.0 2.5 %collective-permute-start.19 = (f32[2,1024]{1,0:T(2,128)S(1)}, f32[2,1024]{1,0:T(2,128)S(1)}, u32[]{:S(2)}, u32[]{:S(2)}) collective-permute-start(f32[2,1024]{1,0:T(2,128)S(1)} %shard_map.37), channel_id=1, source_target_pairs={{0,16},{8,24},{16,0},{24,8},{1,17},{9,25},{17,1},{25,9},{2,18},{10... | collective-permute-start | bytes 24584 | tf_op jit(solution)/shard_map/ppermute | solution.py:237
  4.4 2.2 %collective-permute-start.18 = (f32[2,1024]{1,0:T(2,128)S(1)}, f32[2,1024]{1,0:T(2,128)S(1)}, u32[]{:S(2)}, u32[]{:S(2)}) collective-permute-start(f32[2,1024]{1,0:T(2,128)S(1)} %shard_map.37), channel_id=1, source_target_pairs={{0,8},{8,16},{16,24},{24,0},{1,9},{9,17},{17,25},{25,1},{2,10},{10... | collective-permute-start | bytes 24584 | tf_op jit(solution)/shard_map/ppermute | solution.py:237
  7.4 3.7 %collective-permute-start.22 = (bf16[512,1024]{1,0:T(8,128)(2,1)}, bf16[512,1024]{1,0:T(8,128)(2,1)}, u32[]{:S(2)}, u32[]{:S(2)}) collective-permute-start(bf16[512,1024]{1,0:T(8,128)(2,1)} %z.3), channel_id=1, source_target_pairs={{8,16},{16,8},{9,17},{17,9},{10,18},{18,10},{11,19},{19,11},{12,20... | collective-permute-start | bytes 3145736 | tf_op jit(solution)/shard_map/ppermute | solution.py:241
  11.4 2.3 %shard_map.38 = (bf16[512,1024]{1,0:T(8,128)(2,1)}, bf16[512,1024]{1,0:T(8,128)(2,1)S(1)}, f32[1,1024]{1,0:T(1,128)S(1)}, f32[256,640]{1,0:T(8,128)S(1)}, bf16[256,640]{1,0:T(8,128)(2,1)S(1)}) custom-call(s32[8]{0:T(128)S(1)} %broadcast_xor_fusion.order, bf16[512,1024]{1,0:T(8,128)(2,1)S(1)} %copy-done, f32[1,1024]{1,0:T(1,128)S(1)} %get-tuple-element.180.mean), custom_call_target="tpu_custom_call" | custom-call | tf_op jit(solution)/shard_map/pallas_call | solution.py:17
  13.8 2.4 %collective-permute-start.23 = (bf16[256,640]{1,0:T(8,128)(2,1)S(1)}, bf16[256,640]{1,0:T(8,128)(2,1)S(1)}, u32[]{:S(2)}, u32[]{:S(2)}) collective-permute-start(bf16[256,640]{1,0:T(8,128)(2,1)S(1)} %get-tuple-element.158), channel_id=1, source_target_pairs={{0,1},{1,0},{2,3},{3,2},{4,5},{5,4},{6,7},{7,6},{8,9},{9,8},{10,11... | collective-permute-start | bytes 983048 | tf_op jit(solution)/shard_map/ppermute | solution.py:193
  16.2 1.3 %collective-permute-done.23.got = bf16[256,640]{1,0:T(8,128)(2,1)S(1)} collective-permute-done((bf16[256,640]{1,0:T(8,128)(2,1)S(1)}, bf16[256,640]{1,0:T(8,128)(2,1)S(1)}, u32[]{:S(2)}, u32[]{:S(2)}) %collective-permute-start.23) | collective-permute-done | bytes 327712 | tf_op jit(solution)/shard_map/ppermute | solution.py:193
  17.5 1.3 %collective-permute-start.24 = (bf16[64,640]{1,0:T(8,128)(2,1)S(1)}, bf16[64,640]{1,0:T(8,128)(2,1)S(1)}, u32[]{:S(2)}, u32[]{:S(2)}) collective-permute-start(bf16[64,640]{1,0:T(8,128)(2,1)S(1)} %get-tuple-element.160), channel_id=1, source_target_pairs={{0,2},{1,3},{2,0},{3,1},{4,6},{5,7},{6,4},{7,5},{8,10},{9,11},{10,... | collective-permute-start | bytes 245768 | tf_op jit(solution)/shard_map/ppermute | solution.py:193
  22.5 1.7 %collective-permute-done.26.c = bf16[64,640]{1,0:T(8,128)(2,1)S(1)} collective-permute-done((bf16[64,640]{1,0:T(8,128)(2,1)S(1)}, bf16[64,640]{1,0:T(8,128)(2,1)S(1)}, u32[]{:S(2)}, u32[]{:S(2)}) %collective-permute-start.26) | collective-permute-done | bytes 81952 | tf_op jit(solution)/shard_map/ppermute | solution.py:193
  27.1 1.6 %collective-permute-done.29 = bf16[64,640]{1,0:T(8,128)(2,1)S(1)} collective-permute-done((bf16[64,640]{1,0:T(8,128)(2,1)S(1)}, bf16[64,640]{1,0:T(8,128)(2,1)S(1)}, u32[]{:S(2)}, u32[]{:S(2)}) %collective-permute-start.29) | collective-permute-done | bytes 81952 | tf_op jit(solution)/shard_map/ppermute | solution.py:193
  29.9 3.1 %collective-permute-start.30 = (bf16[256,640]{1,0:T(8,128)(2,1)S(1)}, bf16[256,640]{1,0:T(8,128)(2,1)S(1)}, u32[]{:S(2)}, u32[]{:S(2)}) collective-permute-start(bf16[256,640]{1,0:T(8,128)(2,1)S(1)} %pad_maximum_fusion.4.near), channel_id=1, source_target_pairs={{0,1},{1,0},{2,3},{3,2},{4,5},{5,4},{6,7},{7,6},{8,9},{9,8},{10,11... | collective-permute-start | bytes 983048 | tf_op jit(solution)/shard_map/ppermute | solution.py:193
  33.1 1.3 %collective-permute-done.30.far = bf16[256,640]{1,0:T(8,128)(2,1)S(1)} collective-permute-done((bf16[256,640]{1,0:T(8,128)(2,1)S(1)}, bf16[256,640]{1,0:T(8,128)(2,1)S(1)}, u32[]{:S(2)}, u32[]{:S(2)}) %collective-permute-start.30) | collective-permute-done | bytes 327712 | tf_op jit(solution)/shard_map/ppermute | solution.py:193
  34.3 1.5 %shard_map.41 = bf16[512,640]{1,0:T(8,128)(2,1)} custom-call(s32[8]{0:T(128)S(1)} %broadcast_xor_fusion.order, bf16[256,640]{1,0:T(8,128)(2,1)S(1)} %pad_maximum_fusion.4.near, bf16[256,640]{1,0:T(8,128)(2,1)S(1)} %collective-permute-done.30.far), custom_call_target="tpu_custom_call" | custom-call | tf_op jit(solution)/shard_map/pallas_call | solution.py:17
  35.8 1.6 %collective-permute-start.31 = (bf16[512,1024]{1,0:T(8,128)(2,1)S(1)}, bf16[512,1024]{1,0:T(8,128)(2,1)}, u32[]{:S(2)}, u32[]{:S(2)}) collective-permute-start(bf16[512,1024]{1,0:T(8,128)(2,1)S(1)} %copy-done), channel_id=1, source_target_pairs={{0,24},{24,0},{1,25},{25,1},{2,26},{26,2},{3,27},{27,3},{4,28},{28... | collective-permute-start | bytes 3145736 | tf_op jit(solution)/shard_map/ppermute | solution.py:256
  37.5 20.5 %conditional.2 = (bf16[512,1024]{1,0:T(8,128)(2,1)}, f32[1,1024]{1,0:T(1,128)S(1)}, bf16[512,1024]{1,0:T(8,128)(2,1)}, f32[1,1024]{1,0:T(1,128)S(1)}, bf16[64,15...) conditional(s32[]{:T(128)} %convert_element_type.8, (bf16[512,1024]{1,0:T(8,128)(2,1)S(1)}, ...), branch_computations={%region_0.0_spmd, %region_1.0_spmd} | conditional | bytes 5636304 | solution.py:273
  37.5 4.2 %branch_1_fun.4 = (bf16[512,1024]{1,0:T(8,128)(2,1)}, f32[1,1024]{1,0:T(1,128)S(1)}, bf16[512,1024]{1,0:T(8,128)(2,1)}, f32[1,1024]{1,0:T(1,128)S(1)}, f32[256,1...) custom-call(s32[8]{0:T(128)S(1)} %get-tuple-element.84.order, ...), custom_call_target="tpu_custom_call" | custom-call | tf_op jit(solution)/shard_map/cond/branch_1_fun/pallas_call | solution.py:17
  42.9 1.9 %collective-permute-done.4.got = bf16[256,1536]{1,0:T(8,128)(2,1)S(1)} collective-permute-done((bf16[256,1536]{1,0:T(8,128)(2,1)S(1)}, bf16[256,1536]{1,0:T(8,128)(2,1)S(1)}, u32[]{:S(2)}, u32[]{:S(2)}) %collective-permute-start.4) | collective-permute-done | bytes 786464 | tf_op jit(solution)/shard_map/cond/branch_1_fun/ppermute | solution.py:193
  44.9 1.3 %collective-permute-start.5 = (bf16[64,1536]{1,0:T(8,128)(2,1)S(1)}, bf16[64,1536]{1,0:T(8,128)(2,1)S(1)}, u32[]{:S(2)}, u32[]{:S(2)}) collective-permute-start(bf16[64,1536]{1,0:T(8,128)(2,1)S(1)} %get-tuple-element.96), channel_id=1, source_target_pairs={{0,2},{1,3},{2,0},{3,1},{4,6},{5,7},{6,4},{7,5},{8,10},{9,11},{10,... | collective-permute-start | bytes 589832 | tf_op jit(solution)/shard_map/cond/branch_1_fun/ppermute | solution.py:193
  47.6 3.5 %collective-permute-done.5.a = bf16[64,1536]{1,0:T(8,128)(2,1)S(1)} collective-permute-done((bf16[64,1536]{1,0:T(8,128)(2,1)S(1)}, bf16[64,1536]{1,0:T(8,128)(2,1)S(1)}, u32[]{:S(2)}, u32[]{:S(2)}) %collective-permute-start.5) | collective-permute-done | bytes 196640 | tf_op jit(solution)/shard_map/cond/branch_1_fun/ppermute | solution.py:193
  52.0 4.3 %collective-permute-done.7.c = bf16[64,1536]{1,0:T(8,128)(2,1)S(1)} collective-permute-done((bf16[64,1536]{1,0:T(8,128)(2,1)S(1)}, bf16[64,1536]{1,0:T(8,128)(2,1)S(1)}, u32[]{:S(2)}, u32[]{:S(2)}) %collective-permute-start.7) | collective-permute-done | bytes 196640 | tf_op jit(solution)/shard_map/cond/branch_1_fun/ppermute | solution.py:193
  57.9 1.9 %collective-permute-start.33 = (bf16[64,512]{1,0:T(8,128)(2,1)S(1)}, bf16[64,512]{1,0:T(8,128)(2,1)S(1)}, u32[]{:S(2)}, u32[]{:S(2)}) collective-permute-start(bf16[64,512]{1,0:T(8,128)(2,1)S(1)} %get-tuple-element.166), channel_id=1, source_target_pairs={{8,16},{16,8},{9,17},{17,9},{10,18},{18,10},{11,19},{19,11},{12,20... | collective-permute-start | bytes 196616 | tf_op jit(solution)/shard_map/ppermute | solution.py:277
  59.8 1.3 %collective-permute-start.32 = (bf16[64,512]{1,0:T(8,128)(2,1)S(1)}, bf16[64,512]{1,0:T(8,128)(2,1)S(1)}, u32[]{:S(2)}, u32[]{:S(2)}) collective-permute-start(bf16[64,512]{1,0:T(8,128)(2,1)S(1)} %get-tuple-element.166), channel_id=1, source_target_pairs={{8,0},{16,24},{9,1},{17,25},{10,2},{18,26},{11,3},{19,27},{12,4},{... | collective-permute-start | bytes 196616 | tf_op jit(solution)/shard_map/ppermute | solution.py:277
  61.1 5.4 %collective-permute-done.33 = bf16[64,512]{1,0:T(8,128)(2,1)S(1)} collective-permute-done((bf16[64,512]{1,0:T(8,128)(2,1)S(1)}, bf16[64,512]{1,0:T(8,128)(2,1)S(1)}, u32[]{:S(2)}, u32[]{:S(2)}) %collective-permute-start.33) | collective-permute-done | bytes 65568 | tf_op jit(solution)/shard_map/ppermute | solution.py:277
  66.5 3.1 %collective-permute-start.35 = (bf16[512,1024]{1,0:T(8,128)(2,1)}, bf16[512,1024]{1,0:T(8,128)(2,1)S(1)}, u32[]{:S(2)}, u32[]{:S(2)}) collective-permute-start(bf16[512,1024]{1,0:T(8,128)(2,1)} %collective-permute-done.22), channel_id=1, source_target_pairs={{8,0},{16,24},{9,1},{17,25},{10,2},{18,26},{11,3},{19,27},{12,4},{... | collective-permute-start | bytes 3145736 | tf_op jit(solution)/shard_map/ppermute | solution.py:278
  69.6 1.9 %collective-permute-start.36 = (bf16[512,1024]{1,0:T(8,128)(2,1)}, bf16[512,1024]{1,0:T(8,128)(2,1)S(1)}, u32[]{:S(2)}, u32[]{:S(2)}) collective-permute-start(bf16[512,1024]{1,0:T(8,128)(2,1)} %collective-permute-done.21), channel_id=1, source_target_pairs={{8,16},{16,8},{9,17},{17,9},{10,18},{18,10},{11,19},{19,11},{12,20... | collective-permute-start | bytes 3145736 | tf_op jit(solution)/shard_map/ppermute | solution.py:279
  71.6 13.0 %conditional.3 = (bf16[512,1024]{1,0:T(8,128)(2,1)}, bf16[256,1536]{1,0:T(8,128)(2,1)S(1)}, f32[512,1024]{1,0:T(8,128)S(1)}) conditional(s32[]{:T(128)} %convert_element_type.8, (bf16[512,1024]{1,0:T(8,128)(2,1)}, bf16[512,1024]{1,0:T(8,128)(2,1)}, f32[1,1024]{1,0:T(1,128)S(1)}, bf16[64,1536]{1,0:T(8,128)(2,1)}, bf16[64,512]{1,0:T(8,128)(2,1)S(1)}, ...), branch_computations={%region_2.0_spmd, %region_3.0_spmd} | conditional | flops 5308416 | bytes 17301892 | solution.py:301
  72.6 1.6 %collective-permute-start.17 = (bf16[64,1536]{1,0:T(8,128)(2,1)S(1)}, bf16[64,1536]{1,0:T(8,128)(2,1)S(1)}, u32[]{:S(2)}, u32[]{:S(2)}) collective-permute-start(bf16[64,1536]{1,0:T(8,128)(2,1)S(1)} %pad_maximum_fusion.3), channel_id=1, source_target_pairs={{0,6},{1,7},{2,4},{3,5},{4,2},{5,3},{6,0},{7,1},{8,14},{9,15},{10,... | collective-permute-start | bytes 589832 | tf_op jit(solution)/shard_map/cond/branch_1_fun/ppermute | solution.py:193
  75.3 3.0 %branch_1_fun.7 = f32[512,1024]{1,0:T(8,128)S(1)} custom-call(bf16[512,640]{1,0:T(8,128)(2,1)} %get-tuple-element.122.with_own, bf16[512,1024]{1,0:T(8,128)(2,1)} %get-tuple-element.123.own, bf16[512,1024]{1,0:T(8,128)(2,1)S(1)} %get-tuple-element.124.z, bf16[512,1024]{1,0:T(8,128)(2,1)} %get-tuple-element.125.other, ...), custom_call_target="tpu_custom_call" | custom-call | tf_op jit(solution)/shard_map/cond/branch_1_fun/pallas_call | solution.py:17
  78.9 5.7 %collective-permute-done.16 = bf16[64,1536]{1,0:T(8,128)(2,1)S(1)} collective-permute-done((bf16[64,1536]{1,0:T(8,128)(2,1)S(1)}, bf16[64,1536]{1,0:T(8,128)(2,1)S(1)}, u32[]{:S(2)}, u32[]{:S(2)}) %collective-permute-start.16) | collective-permute-done | bytes 196640 | tf_op jit(solution)/shard_map/cond/branch_1_fun/ppermute | solution.py:193
  85.2 6.6 %collective-permute-done.35.out = bf16[512,1024]{1,0:T(8,128)(2,1)S(1)} collective-permute-done((bf16[512,1024]{1,0:T(8,128)(2,1)}, bf16[512,1024]{1,0:T(8,128)(2,1)S(1)}, u32[]{:S(2)}, u32[]{:S(2)}) %collective-permute-start.35) | collective-permute-done | bytes 1048608 | tf_op jit(solution)/shard_map/ppermute | solution.py:278
  91.9 3.8 %collective-permute-done.36.over = bf16[512,1024]{1,0:T(8,128)(2,1)S(1)} collective-permute-done((bf16[512,1024]{1,0:T(8,128)(2,1)}, bf16[512,1024]{1,0:T(8,128)(2,1)S(1)}, u32[]{:S(2)}, u32[]{:S(2)}) %collective-permute-start.36) | collective-permute-done | bytes 1048608 | tf_op jit(solution)/shard_map/ppermute | solution.py:279
  96.3 4.5 %shard_map.43 = f32[512,1024]{1,0:T(8,128)} custom-call(s32[1]{0:T(128)} %bitcast.middle, bf16[512,1536]{1,0:T(8,128)(2,1)S(1)} %shard_map.42.inner, bf16[512,1024]{1,0:T(8,128)(2,1)S(1)} %copy-done.6, bf16[512,1024]{1,0:T(8,128)(2,1)} %get-tuple-element.177.opposite, bf16[512,1024]{1,0:T(8,128)(2,1)S(1)} %copy-done.1, ...), custom_call_target="tpu_custom_call" | custom-call | tf_op jit(solution)/shard_map/pallas_call | solution.py:17
  (49 shorter events, 18.2 us)
Async XLA Ops:
  0.0 11.4 %copy-start = (bf16[512,1024]{1,0:T(8,128)(2,1)S(1)}, bf16[512,1024]{1,0:T(8,128)(2,1)}, u32[]{:S(2)}) copy-start(bf16[512,1024]{1,0:T(8,128)(2,1)} %z.3) | copy-start | bytes 3145732
  1.9 5.4 %collective-permute-start.20 = (f32[2,1024]{1,0:T(2,128)S(1)}, f32[2,1024]{1,0:T(2,128)S(1)}, u32[]{:S(2)}, u32[]{:S(2)}) collective-permute-start(f32[2,1024]{1,0:T(2,128)S(1)} %shard_map.37), channel_id=1, source_target_pairs={{0,24},{8,0},{16,8},{24,16},{1,25},{9,1},{17,9},{25,17},{2,26},{10... | collective-permute-start | bytes 24584 | tf_op jit(solution)/shard_map/ppermute | solution.py:237
  2.0 5.3 %collective-permute-start.19 = (f32[2,1024]{1,0:T(2,128)S(1)}, f32[2,1024]{1,0:T(2,128)S(1)}, u32[]{:S(2)}, u32[]{:S(2)}) collective-permute-start(f32[2,1024]{1,0:T(2,128)S(1)} %shard_map.37), channel_id=1, source_target_pairs={{0,16},{8,24},{16,0},{24,8},{1,17},{9,25},{17,1},{25,9},{2,18},{10... | collective-permute-start | bytes 24584 | tf_op jit(solution)/shard_map/ppermute | solution.py:237
  4.4 3.0 %collective-permute-start.18 = (f32[2,1024]{1,0:T(2,128)S(1)}, f32[2,1024]{1,0:T(2,128)S(1)}, u32[]{:S(2)}, u32[]{:S(2)}) collective-permute-start(f32[2,1024]{1,0:T(2,128)S(1)} %shard_map.37), channel_id=1, source_target_pairs={{0,8},{8,16},{16,24},{24,0},{1,9},{9,17},{17,25},{25,1},{2,10},{10... | collective-permute-start | bytes 24584 | tf_op jit(solution)/shard_map/ppermute | solution.py:237
  7.4 28.4 %collective-permute-start.22 = (bf16[512,1024]{1,0:T(8,128)(2,1)}, bf16[512,1024]{1,0:T(8,128)(2,1)}, u32[]{:S(2)}, u32[]{:S(2)}) collective-permute-start(bf16[512,1024]{1,0:T(8,128)(2,1)} %z.3), channel_id=1, source_target_pairs={{8,16},{16,8},{9,17},{17,9},{10,18},{18,10},{11,19},{19,11},{12,20... | collective-permute-start | bytes 3145736 | tf_op jit(solution)/shard_map/ppermute | solution.py:241
  11.1 24.7 %collective-permute-start.21 = (bf16[512,1024]{1,0:T(8,128)(2,1)}, bf16[512,1024]{1,0:T(8,128)(2,1)}, u32[]{:S(2)}, u32[]{:S(2)}) collective-permute-start(bf16[512,1024]{1,0:T(8,128)(2,1)} %z.3), channel_id=1, source_target_pairs={{0,8},{8,0},{16,24},{24,16},{1,9},{9,1},{17,25},{25,17},{2,10},{10... | collective-permute-start | bytes 3145736 | tf_op jit(solution)/shard_map/ppermute | solution.py:240
  13.8 23.7 %copy-start.3 = (bf16[512,1024]{1,0:T(8,128)(2,1)}, bf16[512,1024]{1,0:T(8,128)(2,1)S(1)}, u32[]{:S(2)}) copy-start(bf16[512,1024]{1,0:T(8,128)(2,1)S(1)} %get-tuple-element.164) | copy-start | bytes 3145732
  13.8 3.7 %collective-permute-start.23 = (bf16[256,640]{1,0:T(8,128)(2,1)S(1)}, bf16[256,640]{1,0:T(8,128)(2,1)S(1)}, u32[]{:S(2)}, u32[]{:S(2)}) collective-permute-start(bf16[256,640]{1,0:T(8,128)(2,1)S(1)} %get-tuple-element.158), channel_id=1, source_target_pairs={{0,1},{1,0},{2,3},{3,2},{4,5},{5,4},{6,7},{7,6},{8,9},{9,8},{10,11... | collective-permute-start | bytes 983048 | tf_op jit(solution)/shard_map/ppermute | solution.py:193
  17.5 3.8 %collective-permute-start.24 = (bf16[64,640]{1,0:T(8,128)(2,1)S(1)}, bf16[64,640]{1,0:T(8,128)(2,1)S(1)}, u32[]{:S(2)}, u32[]{:S(2)}) collective-permute-start(bf16[64,640]{1,0:T(8,128)(2,1)S(1)} %get-tuple-element.160), channel_id=1, source_target_pairs={{0,2},{1,3},{2,0},{3,1},{4,6},{5,7},{6,4},{7,5},{8,10},{9,11},{10,... | collective-permute-start | bytes 245768 | tf_op jit(solution)/shard_map/ppermute | solution.py:193
  18.8 3.7 %collective-permute-start.25 = (bf16[64,640]{1,0:T(8,128)(2,1)S(1)}, bf16[64,640]{1,0:T(8,128)(2,1)S(1)}, u32[]{:S(2)}, u32[]{:S(2)}) collective-permute-start(bf16[64,640]{1,0:T(8,128)(2,1)S(1)} %get-tuple-element.161), channel_id=1, source_target_pairs={{0,4},{1,5},{2,6},{3,7},{4,0},{5,1},{6,2},{7,3},{8,12},{9,13},{10,... | collective-permute-start | bytes 245768 | tf_op jit(solution)/shard_map/ppermute | solution.py:193
  20.1 4.2 %collective-permute-start.26 = (bf16[64,640]{1,0:T(8,128)(2,1)S(1)}, bf16[64,640]{1,0:T(8,128)(2,1)S(1)}, u32[]{:S(2)}, u32[]{:S(2)}) collective-permute-start(bf16[64,640]{1,0:T(8,128)(2,1)S(1)} %get-tuple-element.162), channel_id=1, source_target_pairs={{0,6},{1,7},{2,4},{3,5},{4,2},{5,3},{6,0},{7,1},{8,14},{9,15},{10,... | collective-permute-start | bytes 245768 | tf_op jit(solution)/shard_map/ppermute | solution.py:193
  24.4 4.4 %collective-permute-start.29 = (bf16[64,640]{1,0:T(8,128)(2,1)S(1)}, bf16[64,640]{1,0:T(8,128)(2,1)S(1)}, u32[]{:S(2)}, u32[]{:S(2)}) collective-permute-start(bf16[64,640]{1,0:T(8,128)(2,1)S(1)} %shard_map.40), channel_id=1, source_target_pairs={{0,6},{1,7},{2,4},{3,5},{4,2},{5,3},{6,0},{7,1},{8,14},{9,15},{10,... | collective-permute-start | bytes 245768 | tf_op jit(solution)/shard_map/ppermute | solution.py:193
  25.0 4.6 %collective-permute-start.28 = (bf16[64,640]{1,0:T(8,128)(2,1)S(1)}, bf16[64,640]{1,0:T(8,128)(2,1)S(1)}, u32[]{:S(2)}, u32[]{:S(2)}) collective-permute-start(bf16[64,640]{1,0:T(8,128)(2,1)S(1)} %shard_map.40), channel_id=1, source_target_pairs={{0,4},{1,5},{2,6},{3,7},{4,0},{5,1},{6,2},{7,3},{8,12},{9,13},{10,... | collective-permute-start | bytes 245768 | tf_op jit(solution)/shard_map/ppermute | solution.py:193
  26.2 3.7 %collective-permute-start.27 = (bf16[64,640]{1,0:T(8,128)(2,1)S(1)}, bf16[64,640]{1,0:T(8,128)(2,1)S(1)}, u32[]{:S(2)}, u32[]{:S(2)}) collective-permute-start(bf16[64,640]{1,0:T(8,128)(2,1)S(1)} %shard_map.40), channel_id=1, source_target_pairs={{0,2},{1,3},{2,0},{3,1},{4,6},{5,7},{6,4},{7,5},{8,10},{9,11},{10,... | collective-permute-start | bytes 245768 | tf_op jit(solution)/shard_map/ppermute | solution.py:193
  29.9 4.4 %collective-permute-start.30 = (bf16[256,640]{1,0:T(8,128)(2,1)S(1)}, bf16[256,640]{1,0:T(8,128)(2,1)S(1)}, u32[]{:S(2)}, u32[]{:S(2)}) collective-permute-start(bf16[256,640]{1,0:T(8,128)(2,1)S(1)} %pad_maximum_fusion.4.near), channel_id=1, source_target_pairs={{0,1},{1,0},{2,3},{3,2},{4,5},{5,4},{6,7},{7,6},{8,9},{9,8},{10,11... | collective-permute-start | bytes 983048 | tf_op jit(solution)/shard_map/ppermute | solution.py:193
  35.8 35.8 %collective-permute-start.31 = (bf16[512,1024]{1,0:T(8,128)(2,1)S(1)}, bf16[512,1024]{1,0:T(8,128)(2,1)}, u32[]{:S(2)}, u32[]{:S(2)}) collective-permute-start(bf16[512,1024]{1,0:T(8,128)(2,1)S(1)} %copy-done), channel_id=1, source_target_pairs={{0,24},{24,0},{1,25},{25,1},{2,26},{26,2},{3,27},{27,3},{4,28},{28... | collective-permute-start | bytes 3145736 | tf_op jit(solution)/shard_map/ppermute | solution.py:256
  41.6 3.1 %collective-permute-start.4 = (bf16[256,1536]{1,0:T(8,128)(2,1)S(1)}, bf16[256,1536]{1,0:T(8,128)(2,1)S(1)}, u32[]{:S(2)}, u32[]{:S(2)}) collective-permute-start(bf16[256,1536]{1,0:T(8,128)(2,1)S(1)} %get-tuple-element.94), channel_id=1, source_target_pairs={{0,1},{1,0},{2,3},{3,2},{4,5},{5,4},{6,7},{7,6},{8,9},{9,8},{10,11... | collective-permute-start | bytes 2359304 | tf_op jit(solution)/shard_map/cond/branch_1_fun/ppermute | solution.py:193
  44.9 6.2 %collective-permute-start.5 = (bf16[64,1536]{1,0:T(8,128)(2,1)S(1)}, bf16[64,1536]{1,0:T(8,128)(2,1)S(1)}, u32[]{:S(2)}, u32[]{:S(2)}) collective-permute-start(bf16[64,1536]{1,0:T(8,128)(2,1)S(1)} %get-tuple-element.96), channel_id=1, source_target_pairs={{0,2},{1,3},{2,0},{3,1},{4,6},{5,7},{6,4},{7,5},{8,10},{9,11},{10,... | collective-permute-start | bytes 589832 | tf_op jit(solution)/shard_map/cond/branch_1_fun/ppermute | solution.py:193
  46.2 5.8 %collective-permute-start.6 = (bf16[64,1536]{1,0:T(8,128)(2,1)S(1)}, bf16[64,1536]{1,0:T(8,128)(2,1)S(1)}, u32[]{:S(2)}, u32[]{:S(2)}) collective-permute-start(bf16[64,1536]{1,0:T(8,128)(2,1)S(1)} %get-tuple-element.97), channel_id=1, source_target_pairs={{0,4},{1,5},{2,6},{3,7},{4,0},{5,1},{6,2},{7,3},{8,12},{9,13},{10,... | collective-permute-start | bytes 589832 | tf_op jit(solution)/shard_map/cond/branch_1_fun/ppermute | solution.py:193
  47.4 8.9 %collective-permute-start.7 = (bf16[64,1536]{1,0:T(8,128)(2,1)S(1)}, bf16[64,1536]{1,0:T(8,128)(2,1)S(1)}, u32[]{:S(2)}, u32[]{:S(2)}) collective-permute-start(bf16[64,1536]{1,0:T(8,128)(2,1)S(1)} %get-tuple-element.98), channel_id=1, source_target_pairs={{0,6},{1,7},{2,4},{3,5},{4,2},{5,3},{6,0},{7,1},{8,14},{9,15},{10,... | collective-permute-start | bytes 589832 | tf_op jit(solution)/shard_map/cond/branch_1_fun/ppermute | solution.py:193
  57.9 8.6 %collective-permute-start.33 = (bf16[64,512]{1,0:T(8,128)(2,1)S(1)}, bf16[64,512]{1,0:T(8,128)(2,1)S(1)}, u32[]{:S(2)}, u32[]{:S(2)}) collective-permute-start(bf16[64,512]{1,0:T(8,128)(2,1)S(1)} %get-tuple-element.166), channel_id=1, source_target_pairs={{8,16},{16,8},{9,17},{17,9},{10,18},{18,10},{11,19},{19,11},{12,20... | collective-permute-start | bytes 196616 | tf_op jit(solution)/shard_map/ppermute | solution.py:277
  59.8 6.7 %collective-permute-start.32 = (bf16[64,512]{1,0:T(8,128)(2,1)S(1)}, bf16[64,512]{1,0:T(8,128)(2,1)S(1)}, u32[]{:S(2)}, u32[]{:S(2)}) collective-permute-start(bf16[64,512]{1,0:T(8,128)(2,1)S(1)} %get-tuple-element.166), channel_id=1, source_target_pairs={{8,0},{16,24},{9,1},{17,25},{10,2},{18,26},{11,3},{19,27},{12,4},{... | collective-permute-start | bytes 196616 | tf_op jit(solution)/shard_map/ppermute | solution.py:277
  66.5 25.3 %collective-permute-start.35 = (bf16[512,1024]{1,0:T(8,128)(2,1)}, bf16[512,1024]{1,0:T(8,128)(2,1)S(1)}, u32[]{:S(2)}, u32[]{:S(2)}) collective-permute-start(bf16[512,1024]{1,0:T(8,128)(2,1)} %collective-permute-done.22), channel_id=1, source_target_pairs={{8,0},{16,24},{9,1},{17,25},{10,2},{18,26},{11,3},{19,27},{12,4},{... | collective-permute-start | bytes 3145736 | tf_op jit(solution)/shard_map/ppermute | solution.py:278
  69.6 26.0 %collective-permute-start.36 = (bf16[512,1024]{1,0:T(8,128)(2,1)}, bf16[512,1024]{1,0:T(8,128)(2,1)S(1)}, u32[]{:S(2)}, u32[]{:S(2)}) collective-permute-start(bf16[512,1024]{1,0:T(8,128)(2,1)} %collective-permute-done.21), channel_id=1, source_target_pairs={{8,16},{16,8},{9,17},{17,9},{10,18},{18,10},{11,19},{19,11},{12,20... | collective-permute-start | bytes 3145736 | tf_op jit(solution)/shard_map/ppermute | solution.py:279
  72.6 6.3 %collective-permute-start.17 = (bf16[64,1536]{1,0:T(8,128)(2,1)S(1)}, bf16[64,1536]{1,0:T(8,128)(2,1)S(1)}, u32[]{:S(2)}, u32[]{:S(2)}) collective-permute-start(bf16[64,1536]{1,0:T(8,128)(2,1)S(1)} %pad_maximum_fusion.3), channel_id=1, source_target_pairs={{0,6},{1,7},{2,4},{3,5},{4,2},{5,3},{6,0},{7,1},{8,14},{9,15},{10,... | collective-permute-start | bytes 589832 | tf_op jit(solution)/shard_map/cond/branch_1_fun/ppermute | solution.py:193
  74.1 10.4 %collective-permute-start.16 = (bf16[64,1536]{1,0:T(8,128)(2,1)S(1)}, bf16[64,1536]{1,0:T(8,128)(2,1)S(1)}, u32[]{:S(2)}, u32[]{:S(2)}) collective-permute-start(bf16[64,1536]{1,0:T(8,128)(2,1)S(1)} %pad_maximum_fusion.3), channel_id=1, source_target_pairs={{0,4},{1,5},{2,6},{3,7},{4,0},{5,1},{6,2},{7,3},{8,12},{9,13},{10,... | collective-permute-start | bytes 589832 | tf_op jit(solution)/shard_map/cond/branch_1_fun/ppermute | solution.py:193
  75.0 9.5 %collective-permute-start.15 = (bf16[64,1536]{1,0:T(8,128)(2,1)S(1)}, bf16[64,1536]{1,0:T(8,128)(2,1)S(1)}, u32[]{:S(2)}, u32[]{:S(2)}) collective-permute-start(bf16[64,1536]{1,0:T(8,128)(2,1)S(1)} %pad_maximum_fusion.3), channel_id=1, source_target_pairs={{0,2},{1,3},{2,0},{3,1},{4,6},{5,7},{6,4},{7,5},{8,10},{9,11},{10,... | collective-permute-start | bytes 589832 | tf_op jit(solution)/shard_map/cond/branch_1_fun/ppermute | solution.py:193
  84.6 11.6 %copy-start.1 = (bf16[512,1024]{1,0:T(8,128)(2,1)S(1)}, bf16[512,1024]{1,0:T(8,128)(2,1)}, u32[]{:S(2)}) copy-start(bf16[512,1024]{1,0:T(8,128)(2,1)} %get-tuple-element.167.own) | copy-start | bytes 3145732
  84.7 11.6 %copy-start.6 = (bf16[512,1024]{1,0:T(8,128)(2,1)S(1)}, bf16[512,1024]{1,0:T(8,128)(2,1)}, u32[]{:S(2)}) copy-start(bf16[512,1024]{1,0:T(8,128)(2,1)} %get-tuple-element.176.beside) | copy-start | bytes 3145732
  84.7 11.0 %collective-permute-start.34 = (bf16[256,1536]{1,0:T(8,128)(2,1)S(1)}, bf16[256,1536]{1,0:T(8,128)(2,1)S(1)}, u32[]{:S(2)}, u32[]{:S(2)}) collective-permute-start(bf16[256,1536]{1,0:T(8,128)(2,1)S(1)} %get-tuple-element.172.near), channel_id=1, source_target_pairs={{0,1},{1,0},{2,3},{3,2},{4,5},{5,4},{6,7},{7,6},{8,9},{9,8},{10,11... | collective-permute-start | bytes 2359304 | tf_op jit(solution)/shard_map/ppermute | solution.py:193

commit v10 on v9

--- a/solution.py
+++ b/solution.py
@@ -90,16 +90,19 @@
 
 
 def middle_kernel(
-    order, turned, beside_in, opposite_in, mean,
+    order, beside_in, opposite_in, mean,
     beside, beside_square, opposite, opposite_square, kept, sent, turned_beside,
 ):
+    centered_into(beside, beside_in, mean[...], beside_square)
+    centered_into(opposite, opposite_in, mean[...], opposite_square)
+    turn_into(turned_beside, order, beside)
+    split_sum(gram(turned_beside[...], opposite[...]), kept, sent, slice(None))
+
+
+def both_kernel(turned, beside, opposite, kept, sent):
     rows = beside.shape[0]
-    centered_into(beside, beside_in, mean[...], beside_square)
     split_sum(gram(turned[...], beside[...]), kept, sent, slice(0, rows))
-    centered_into(opposite, opposite_in, mean[...], opposite_square)
     split_sum(gram(turned[...], opposite[...]), kept, sent, slice(rows, 2 * rows))
-    turn_into(turned_beside, order, beside)
-    split_sum(gram(turned_beside[...], opposite[...]), kept, sent, slice(2 * rows, 3 * rows))
 
 
 def block_kernel(turned, block_in, mean, block, square, kept, sent):
@@ -125,17 +128,17 @@
     return jnp.concatenate([x[:, :last], split], axis=1)
 
 
-def add_kernel(last, kept, got, mine, *out):
-    total = with_norm(kept[...] + got[...].astype(jnp.float32), last)
-    quarter = mine.shape[0]
-    mine[...] = total[:quarter]
-    for k, ref in enumerate(out, 1):
-        ref[...] = total[k * quarter:(k + 1) * quarter].astype(jnp.bfloat16)
-
-
-def total_kernel(last, mine, a, b, c, out):
-    total = mine[...] + a[...].astype(jnp.float32)
-    total = total + b[...].astype(jnp.float32) + c[...].astype(jnp.float32)
+def add_kernel(last, kept, got, out):
+    total = with_norm(kept[...] + got[...].astype(jnp.float32), last).astype(jnp.bfloat16)
+    quarter = out.shape[1]
+    for k in range(4):
+        out[k] = total[k * quarter:(k + 1) * quarter]
+
+
+def total_kernel(last, got, out):
+    total = got[0].astype(jnp.float32)
+    for k in range(1, 4):
+        total = total + got[k].astype(jnp.float32)
     out[...] = with_norm(total, last).astype(jnp.bfloat16)
 
 
@@ -189,31 +192,34 @@
     pl.when(middle[0] == 0)(lambda: put(out, dot))
 
 
-def to_partner(x, step):
-    return lax.ppermute(x, "feat", [(i, i ^ step) for i in range(8)])
-
-
-def halve(kept, sent, last=0):
+def to_other_core(x):
+    return lax.ppermute(x, "feat", [(i, i ^ 1) for i in range(8)])
+
+
+def over_chips(x):
+    return lax.all_to_all(
+        x, "feat", 0, 0, axis_index_groups=[[0, 2, 4, 6], [1, 3, 5, 7]], tiled=True
+    )
+
+
+def scatter_sum(kept, sent, last=0):
     half, n = kept.shape
     part = (half // 4, n)
-    return kernel_call(
-        functools.partial(add_kernel, last), [(part, jnp.float32)] + [(part, jnp.bfloat16)] * 3
-    )(kept, to_partner(sent, 1))
-
-
-def scatter(mine, *out, last=0):
-    got = [to_partner(x, 2 * k) for k, x in enumerate(out, 1)]
-    return kernel_call(functools.partial(total_kernel, last), [(mine.shape, jnp.bfloat16)])(
-        mine, *got
+    out = kernel_call(functools.partial(add_kernel, last), [((4, *part), jnp.bfloat16)])(
+        kept, to_other_core(sent)
     )[0]
+    return kernel_call(functools.partial(total_kernel, last), [(part, jnp.bfloat16)])(
+        over_chips(out)
+    )[0]
 
 
 def gather_chips(x):
-    return jnp.concatenate([x] + [to_partner(x, 2 * k) for k in (1, 2, 3)])
+    out = over_chips(jnp.broadcast_to(x[None], (4, *x.shape)))
+    return out.reshape(4 * x.shape[0], x.shape[1])
 
 
 def gather_cores(near, order, *others):
-    far = after(to_partner(near, 1), *others)
+    far = after(to_other_core(near), *others)
     shape = (2 * near.shape[0], near.shape[1])
     return kernel_call(place_kernel, [(shape, jnp.bfloat16)], smem=1)(order, near, far)[0]
 
@@ -227,7 +233,8 @@
     total = rows * 4
     plane = lax.axis_index("dp")
     middle = ((plane == 1) | (plane == 2)).astype(jnp.int32).reshape(1)
-    order = lax.axis_index("feat") ^ jnp.array([0, 2, 4, 6, 1, 3, 5, 7], jnp.int32)
+    core, chips = lax.axis_index("feat") % 2, jnp.array([0, 2, 4, 6], jnp.int32)
+    order = jnp.concatenate([chips + core, chips + 1 - core])
     across, outward = [(1, 2), (2, 1)], [(1, 0), (2, 3)]
     half = rows // 2
     flat, block = ((1, width), jnp.float32), ((rows, width), jnp.bfloat16)
@@ -236,7 +243,7 @@
     all_stats = [stats] + [
         lax.ppermute(stats, "dp", [(i, (i + k) % 4) for i in range(4)]) for k in (1, 2, 3)
     ]
-    ahead = after(z_anchor, *all_stats)
+    ahead = after(z_anchor, stats)
     beside_in = lax.ppermute(ahead, "dp", [(i, i ^ 1) for i in range(4)])
     swapped = lax.ppermute(ahead, "dp", across)
     mean = (all_stats[0][:1] + all_stats[1][:1] + all_stats[2][:1] + all_stats[3][:1]) / 4
@@ -251,30 +258,29 @@
     own, turned, own_square, kept, sent = kernel_call(
         own_kernel, [block, block, flat, *summands(rows + NORM)], smem=1, scratch=12
     )(order, z_anchor, mean)
-    with_own = gather_cores(gather_chips(scatter(*halve(kept, sent, rows), last=rows)), order)
-
-    end = lax.ppermute(after(z_anchor, beside_in, swapped, with_own), "dp", [(0, 3), (3, 0)])
-
-    def first_of_middle(order, turned, beside_in, swapped, mean):
+    near_own = gather_chips(scatter_sum(kept, sent, rows))
+
+    end = lax.ppermute(after(z_anchor, beside_in, swapped, near_own), "dp", [(0, 3), (3, 0)])
+    with_own = gather_cores(after(near_own, beside_in, swapped), order)
+
+    def first_of_middle(turned, beside_in, swapped, mean):
         *blocks, kept, sent, _ = kernel_call(
-            middle_kernel, [block, flat, block, flat, *summands(3 * rows), block],
+            middle_kernel, [block, flat, block, flat, *summands(rows), block],
             smem=1, scratch=12,
-        )(order, turned, beside_in, swapped, mean)
-        return *blocks, scatter(*halve(kept, sent))
-
-    def first_of_end(order, turned, beside_in, swapped, mean):
+        )(order, beside_in, swapped, mean)
+        return *blocks, scatter_sum(kept, sent)
+
+    def first_of_end(turned, beside_in, swapped, mean):
         beside, square, kept, sent = kernel_call(
             block_kernel, [block, flat, *summands(rows)], scratch=12
         )(turned, beside_in, mean)
-        first = scatter(*halve(kept, sent))
-        first = jnp.concatenate([first, jnp.zeros((rows // 8, 2 * rows), first.dtype)], axis=1)
-        return beside, square, swapped, jnp.zeros_like(square), first
+        return beside, square, swapped, jnp.zeros_like(square), scatter_sum(kept, sent)
 
     beside, beside_square, opposite, opposite_square, first = lax.cond(
         middle[0] == 1, first_of_middle, first_of_end,
-        order, after(turned, with_own), beside_in, swapped, mean,
-    )
-    handed = [lax.ppermute(first[:, 2 * rows:], "dp", p) for p in (outward, across)]
+        after(turned, near_own), beside_in, swapped, mean,
+    )
+    handed = [lax.ppermute(first, "dp", p) for p in (outward, across)]
     out = lax.ppermute(after(swapped, *handed), "dp", outward)
     over = lax.ppermute(after(beside_in, *handed), "dp", across)
     handed = handed[0] + handed[1]
@@ -287,15 +293,17 @@
         )[0]
 
     def second_of_middle(turned, end, opposite, opposite_square, first, handed):
-        inner = jnp.concatenate([first[:, :2 * rows], handed], axis=1)
+        kept, sent = kernel_call(both_kernel, summands(2 * rows), scratch=12)(
+            turned, beside, opposite
+        )
+        inner = jnp.concatenate([scatter_sum(kept, sent), handed], axis=1)
         return opposite, gather_chips(inner), hold(opposite_square)
 
     def second_of_end(turned, end, opposite, opposite_square, first, handed):
         opposite, opposite_square, kept, sent = kernel_call(
             block_kernel, [block, flat, *summands(rows)], scratch=12
         )(turned, end, mean)
-        inner = scatter(*halve(kept, sent))
-        inner = jnp.concatenate([first[:, :rows], inner, handed], axis=1)
+        inner = jnp.concatenate([first, scatter_sum(kept, sent), handed], axis=1)
         return opposite, gather_chips(inner), hold(opposite_square)
 
     opposite, inner, held = lax.cond(

time: 102 us -> 113 us (1.11)
  blocking collectives: 0 us -> 35 us
  waiting for transfers between devices: 42.1 us -> 17.6 us
  Pallas kernels: 19.2 us -> 24.6 us
  starting transfers between devices: 36.7 us -> 34 us
    all_to_all x0 -> x4, blocking collectives: none -> 35 us  [over_chips(): lax.all_to_all(x, 'feat', 0, 0, axis_index_groups=[[0, 2, 4, 6], [1, 3, 5...]
    ppermute x19 -> x8, waiting for transfers between devices: 31.5 us -> 11.2 us  [the longest x5 6.44 us: to_other_core(): return lax.ppermute(x, 'feat', [(i, i ^ 1) for i in range(8)])]
    ppermute x19 -> x8, starting transfers between devices: 23 us -> 16.2 us  [the longest x2 7.83 us: by_line(): handed = [lax.ppermute(first, 'dp', p) for p in (outward, across)]]
    ppermute x1, waiting for transfers between devices: 6.64 us -> 0.01 us  [by_line(): out = lax.ppermute(after(swapped, *handed), 'dp', outward)]
    all_to_all x0 -> x1, waiting for transfers between devices: none -> 5.91 us  [over_chips(): lax.all_to_all(x, 'feat', 0, 0, axis_index_groups=[[0, 2, 4, 6], [1, 3, 5...]
    pallas_call x11 -> x14, Pallas kernels: 19.2 us -> 24.6 us  [call(): pl.pallas_call(body, out_shape=[jax.ShapeDtypeStruct(s, t) for s, t in ou...]
    all_to_all x0 -> x1, starting transfers between devices: none -> 4.22 us  [over_chips(): lax.all_to_all(x, 'feat', 0, 0, axis_index_groups=[[0, 2, 4, 6], [1, 3, 5...]
    ppermute x1, waiting for transfers between devices: 3.75 us -> 0.01 us  [by_line(): over = lax.ppermute(after(beside_in, *handed), 'dp', across)]
  transfers between devices with their start and end apart: 26 -> 16, of which waited for: 18 -> 8; matrix products, arithmetic and copies ran while one was open for 3% -> 1% of each run, Pallas kernels for 12% -> 15%
where the time goes in v10:
time: 113 us; the launch traced here: 112 us
  blocking collectives  35 us (31%)
  starting transfers between devices  34 us (30%)
  Pallas kernels  24.6 us (22%)
  waiting for transfers between devices  17.6 us (16%)
    all_to_all x4, blocking collectives, over_chips(): lax.all_to_all(x, 'feat', 0, 0, axis_index_groups=[[0, 2, 4, 6], [1, 3, 5...  35 us
    pallas_call x14, Pallas kernels, call(): pl.pallas_call(body, out_shape=[jax.ShapeDtypeStruct(s, t) for s, t in ou...  24.6 us
    ppermute x2, starting transfers between devices, by_line(): handed = [lax.ppermute(first, 'dp', p) for p in (outward, across)]  7.83 us
    ppermute x5, starting transfers between devices, to_other_core(): return lax.ppermute(x, 'feat', [(i, i ^ 1) for i in range(8)])  6.72 us
    ppermute x5, waiting for transfers between devices, to_other_core(): return lax.ppermute(x, 'feat', [(i, i ^ 1) for i in range(8)])  6.44 us
    all_to_all x1, waiting for transfers between devices, over_chips(): lax.all_to_all(x, 'feat', 0, 0, axis_index_groups=[[0, 2, 4, 6], [1, 3, 5...  5.91 us
    ppermute x2, waiting for transfers between devices, by_line(): handed = [lax.ppermute(first, 'dp', p) for p in (outward, across)]  4.73 us
    ppermute x3, starting transfers between devices, by_line(): lax.ppermute(stats, 'dp', [(i, (i + k) % 4) for i in range(4)])  4.72 us
  transfers between devices with their start and end apart: 16, of which 8 were waited for; matrix products, arithmetic and copies ran while one was open for 1% of the time, Pallas kernels for 15%

profile of v10, /device:TPU:9, one launch (start us, length us, event | category | flops | bytes accessed | tf_op | source)
XLA Modules:
  0.0 112.5 jit_solution(7630304719722908552)
XLA Ops:
  0.0 1.8 %shard_map.37 = f32[2,1024]{1,0:T(2,128)S(1)} custom-call(bf16[512,1024]{1,0:T(8,128)(2,1)} %z.3), custom_call_target="tpu_custom_call" | custom-call | tf_op jit(solution)/shard_map/pallas_call | solution.py:17
  1.9 2.5 %collective-permute-start.5 = (f32[2,1024]{1,0:T(2,128)S(1)}, f32[2,1024]{1,0:T(2,128)S(1)}, u32[]{:S(2)}, u32[]{:S(2)}) collective-permute-start(f32[2,1024]{1,0:T(2,128)S(1)} %shard_map.37), channel_id=1, source_target_pairs={{0,16},{8,24},{16,0},{24,8},{1,17},{9,25},{17,1},{25,9},{2,18},{10... | collective-permute-start | bytes 24584 | tf_op jit(solution)/shard_map/ppermute | solution.py:244
  4.3 2.2 %collective-permute-start.4 = (f32[2,1024]{1,0:T(2,128)S(1)}, f32[2,1024]{1,0:T(2,128)S(1)}, u32[]{:S(2)}, u32[]{:S(2)}) collective-permute-start(f32[2,1024]{1,0:T(2,128)S(1)} %shard_map.37), channel_id=1, source_target_pairs={{0,8},{8,16},{16,24},{24,0},{1,9},{9,17},{17,25},{25,1},{2,10},{10... | collective-permute-start | bytes 24584 | tf_op jit(solution)/shard_map/ppermute | solution.py:244
  6.5 1.9 %collective-permute-start.8 = (bf16[512,1024]{1,0:T(8,128)(2,1)}, bf16[512,1024]{1,0:T(8,128)(2,1)}, u32[]{:S(2)}, u32[]{:S(2)}) collective-permute-start(bf16[512,1024]{1,0:T(8,128)(2,1)} %z.3), channel_id=1, source_target_pairs={{8,16},{16,8},{9,17},{17,9},{10,18},{18,10},{11,19},{19,11},{12,20... | collective-permute-start | bytes 3145736 | tf_op jit(solution)/shard_map/ppermute | solution.py:248
  8.7 3.4 %shard_map.38 = (bf16[512,1024]{1,0:T(8,128)(2,1)}, bf16[512,1024]{1,0:T(8,128)(2,1)}, f32[1,1024]{1,0:T(1,128)S(1)}, f32[256,640]{1,0:T(8,128)S(1)}, bf16[256,640]{1,0:T(8,128)(2,1)S(1)}) custom-call(s32[8]{0:T(128)S(1)} %pad_add_fusion.order, bf16[512,1024]{1,0:T(8,128)(2,1)} %z.3, f32[1,1024]{1,0:T(1,128)S(1)} %get-tuple-element.169.mean), custom_call_target="tpu_custom_call" | custom-call | tf_op jit(solution)/shard_map/pallas_call | solution.py:17
  12.1 1.5 %collective-permute-start.9 = (bf16[256,640]{1,0:T(8,128)(2,1)S(1)}, bf16[256,640]{1,0:T(8,128)(2,1)S(1)}, u32[]{:S(2)}, u32[]{:S(2)}) collective-permute-start(bf16[256,640]{1,0:T(8,128)(2,1)S(1)} %get-tuple-element.147), channel_id=1, source_target_pairs={{0,1},{1,0},{2,3},{3,2},{4,5},{5,4},{6,7},{7,6},{8,9},{9,8},{10,11... | collective-permute-start | bytes 983048 | tf_op jit(solution)/shard_map/ppermute | solution.py:196
  13.6 1.3 %collective-permute-done.9.got = bf16[256,640]{1,0:T(8,128)(2,1)S(1)} collective-permute-done((bf16[256,640]{1,0:T(8,128)(2,1)S(1)}, bf16[256,640]{1,0:T(8,128)(2,1)S(1)}, u32[]{:S(2)}, u32[]{:S(2)}) %collective-permute-start.9) | collective-permute-done | bytes 327712 | tf_op jit(solution)/shard_map/ppermute | solution.py:196
  15.0 8.9 %all_to_all.37.got = bf16[4,64,640]{2,1,0:T(8,128)(2,1)S(1)} all-to-all(bf16[4,64,640]{2,1,0:T(8,128)(2,1)S(1)} %shard_map.39), channel_id=1, replica_groups={{0,2,4,6},{1,3,5,7},{8,10,12,14},{9,11,13,15},{16,18,20,22},{17,19,21,2..., dimensions={0} | all-to-all | bytes 655360 | tf_op jit(solution)/shard_map/all_to_all | solution.py:200
  24.0 7.5 %all_to_all.38 = bf16[4,64,640]{2,1,0:T(8,128)(2,1)S(1)} all-to-all(bf16[4,64,640]{2,1,0:T(8,128)(2,1)S(1)} %broadcast_in_dim.6), channel_id=1, replica_groups={{0,2,4,6},{1,3,5,7},{8,10,12,14},{9,11,13,15},{16,18,20,22},{17,19,21,2..., dimensions={0} | all-to-all | bytes 655360 | tf_op jit(solution)/shard_map/all_to_all | solution.py:200
  32.0 1.7 %collective-permute-start.10 = (bf16[512,1024]{1,0:T(8,128)(2,1)}, bf16[512,1024]{1,0:T(8,128)(2,1)}, u32[]{:S(2)}, u32[]{:S(2)}) collective-permute-start(bf16[512,1024]{1,0:T(8,128)(2,1)} %z.3), channel_id=1, source_target_pairs={{0,24},{24,0},{1,25},{25,1},{2,26},{26,2},{3,27},{27,3},{4,28},{28... | collective-permute-start | bytes 3145736 | tf_op jit(solution)/shard_map/ppermute | solution.py:263
  33.6 2.6 %collective-permute-start.11 = (bf16[256,640]{1,0:T(8,128)(2,1)S(1)}, bf16[256,640]{1,0:T(8,128)(2,1)S(1)}, u32[]{:S(2)}, u32[]{:S(2)}) collective-permute-start(bf16[256,640]{1,0:T(8,128)(2,1)S(1)} %bitcast.4), channel_id=1, source_target_pairs={{0,1},{1,0},{2,3},{3,2},{4,5},{5,4},{6,7},{7,6},{8,9},{9,8},{10,11... | collective-permute-start | bytes 983048 | tf_op jit(solution)/shard_map/ppermute | solution.py:196
  36.2 13.6 %conditional.2 = (bf16[512,1024]{1,0:T(8,128)(2,1)}, f32[1,1024]{1,0:T(1,128)S(1)}, bf16[512,1024]{1,0:T(8,128)(2,1)}, f32[1,1024]{1,0:T(1,128)S(1)}, bf16[64,512]{1,0:T(8,128)(2,1)S(1)}) conditional(s32[]{:T(128)} %convert_element_type.8, (bf16[512,1024]{1,0:T(8,128)(2,1)}, bf16[512,1024]{1,0:T(8,128)(2,1)}, f32[1,1024]{1,0:T(1,128)S(1)}, ...), branch_computations={%region_0.1_spmd, %region_1.2_spmd} | conditional | bytes 3936372 | solution.py:279
  36.2 3.9 %branch_1_fun.7 = (bf16[512,1024]{1,0:T(8,128)(2,1)}, f32[1,1024]{1,0:T(1,128)S(1)}, bf16[512,1024]{1,0:T(8,128)(2,1)}, f32[1,1024]{1,0:T(1,128)S(1)}, f32[256,5...) custom-call(s32[8]{0:T(128)S(1)} %get-tuple-element.83.order, ...), custom_call_target="tpu_custom_call" | custom-call | tf_op jit(solution)/shard_map/cond/branch_1_fun/pallas_call | solution.py:17
  40.1 1.5 %collective-permute-done.1.got = bf16[256,512]{1,0:T(8,128)(2,1)S(1)} collective-permute-done((bf16[256,512]{1,0:T(8,128)(2,1)S(1)}, bf16[256,512]{1,0:T(8,128)(2,1)S(1)}, u32[]{:S(2)}, u32[]{:S(2)}) %collective-permute-start.1) | collective-permute-done | bytes 262176 | tf_op jit(solution)/shard_map/cond/branch_1_fun/ppermute | solution.py:196
  41.7 8.1 %all_to_all.34.got = bf16[4,64,512]{2,1,0:T(8,128)(2,1)S(1)} all-to-all(bf16[4,64,512]{2,1,0:T(8,128)(2,1)S(1)} %branch_1_fun.8), channel_id=1, replica_groups={{0,2,4,6},{1,3,5,7},{8,10,12,14},{9,11,13,15},{16,18,20,22},{17,19,21,2..., dimensions={0} | all-to-all | bytes 524288 | tf_op jit(solution)/shard_map/cond/branch_1_fun/all_to_all | solution.py:200
  49.8 3.4 %collective-permute-start.13 = (bf16[64,512]{1,0:T(8,128)(2,1)S(1)}, bf16[64,512]{1,0:T(8,128)(2,1)S(1)}, u32[]{:S(2)}, u32[]{:S(2)}) collective-permute-start(bf16[64,512]{1,0:T(8,128)(2,1)S(1)} %get-tuple-element.154), channel_id=1, source_target_pairs={{8,16},{16,8},{9,17},{17,9},{10,18},{18,10},{11,19},{19,11},{12,20... | collective-permute-start | bytes 196616 | tf_op jit(solution)/shard_map/ppermute | solution.py:283
  53.2 4.5 %collective-permute-start.12 = (bf16[64,512]{1,0:T(8,128)(2,1)S(1)}, bf16[64,512]{1,0:T(8,128)(2,1)S(1)}, u32[]{:S(2)}, u32[]{:S(2)}) collective-permute-start(bf16[64,512]{1,0:T(8,128)(2,1)S(1)} %get-tuple-element.154), channel_id=1, source_target_pairs={{8,0},{16,24},{9,1},{17,25},{10,2},{18,26},{11,3},{19,27},{12,4},{... | collective-permute-start | bytes 196616 | tf_op jit(solution)/shard_map/ppermute | solution.py:283
  57.7 4.7 %collective-permute-done.13 = bf16[64,512]{1,0:T(8,128)(2,1)S(1)} collective-permute-done((bf16[64,512]{1,0:T(8,128)(2,1)S(1)}, bf16[64,512]{1,0:T(8,128)(2,1)S(1)}, u32[]{:S(2)}, u32[]{:S(2)}) %collective-permute-start.13) | collective-permute-done | bytes 65568 | tf_op jit(solution)/shard_map/ppermute | solution.py:283
  62.4 3.2 %collective-permute-start.15 = (bf16[512,1024]{1,0:T(8,128)(2,1)}, bf16[512,1024]{1,0:T(8,128)(2,1)S(1)}, u32[]{:S(2)}, u32[]{:S(2)}) collective-permute-start(bf16[512,1024]{1,0:T(8,128)(2,1)} %collective-permute-done.8), channel_id=1, source_target_pairs={{8,0},{16,24},{9,1},{17,25},{10,2},{18,26},{11,3},{19,27},{12,4},{... | collective-permute-start | bytes 3145736 | tf_op jit(solution)/shard_map/ppermute | solution.py:284
  65.7 3.6 %collective-permute-start.16 = (bf16[512,1024]{1,0:T(8,128)(2,1)}, bf16[512,1024]{1,0:T(8,128)(2,1)S(1)}, u32[]{:S(2)}, u32[]{:S(2)}) collective-permute-start(bf16[512,1024]{1,0:T(8,128)(2,1)} %collective-permute-done.7), channel_id=1, source_target_pairs={{8,16},{16,8},{9,17},{17,9},{10,18},{18,10},{11,19},{19,11},{12,20... | collective-permute-start | bytes 3145736 | tf_op jit(solution)/shard_map/ppermute | solution.py:285
  69.4 1.4 %shard_map.41 = bf16[512,640]{1,0:T(8,128)(2,1)} custom-call(s32[8]{0:T(128)S(1)} %pad_add_fusion.order, bf16[256,640]{1,0:T(8,128)(2,1)S(1)} %bitcast.5, bf16[256,640]{1,0:T(8,128)(2,1)S(1)} %collective-permute-done.11.far), custom_call_target="tpu_custom_call" | custom-call | tf_op jit(solution)/shard_map/pallas_call | solution.py:17
  70.8 31.9 %conditional.3 = (bf16[512,1024]{1,0:T(8,128)(2,1)}, f32[512,1024]{1,0:T(8,128)}, bf16[256,1536]{1,0:T(8,128)(2,1)}) conditional(s32[]{:T(128)} %convert_element_type.8, (bf16[512,1024]{1,0:T(8,128)(2,1)}, bf16[512,1024]{1,0:T(8,128)(2,1)}, f32[1,1024]{1,0:T(1,128)S(1)}, bf16[512,640]{1,0:T(8,128)(2,1)}, bf16[512,1024]{1,0:T(8,128)(2,1)}, ...), branch_computations={%region_2.3_spmd, %region_3.4_spmd} | conditional | flops 589824 | bytes 11075708 | solution.py:309
  70.8 3.1 %branch_1_fun.11 = (f32[256,1024]{1,0:T(8,128)S(1)}, bf16[256,1024]{1,0:T(8,128)(2,1)S(1)}) custom-call(bf16[512,1024]{1,0:T(8,128)(2,1)} %get-tuple-element.119.turned, bf16[512,1024]{1,0:T(8,128)(2,1)} %get-tuple-element.120.beside, bf16[512,1024]{1,0:T(8,128)(2,1)} %get-tuple-element.185.opposite), custom_call_target="tpu_custom_call" | custom-call | tf_op jit(solution)/shard_map/cond/branch_1_fun/pallas_call | solution.py:17
  75.1 1.5 %collective-permute-done.3.got = bf16[256,1024]{1,0:T(8,128)(2,1)S(1)} collective-permute-done((bf16[256,1024]{1,0:T(8,128)(2,1)S(1)}, bf16[256,1024]{1,0:T(8,128)(2,1)S(1)}, u32[]{:S(2)}, u32[]{:S(2)}) %collective-permute-start.3) | collective-permute-done | bytes 524320 | tf_op jit(solution)/shard_map/cond/branch_1_fun/ppermute | solution.py:196
  76.7 10.5 %all_to_all.36.got = bf16[4,64,1024]{2,1,0:T(8,128)(2,1)S(1)} all-to-all(bf16[4,64,1024]{2,1,0:T(8,128)(2,1)S(1)} %branch_1_fun.12), channel_id=1, replica_groups={{0,2,4,6},{1,3,5,7},{8,10,12,14},{9,11,13,15},{16,18,20,22},{17,19,21,2..., dimensions={0} | all-to-all | bytes 1048576 | tf_op jit(solution)/shard_map/cond/branch_1_fun/all_to_all | solution.py:200
  88.2 4.2 %all-to-all-start.5 = ((bf16[4,64,1536]{2,1,0:T(8,128)(2,1)}), bf16[4,64,1536]{2,1,0:T(8,128)(2,1)}, u32[]{:S(2)}, u32[]{:S(2)}) async-start(bf16[4,64,1536]{2,1,0:T(8,128)(2,1)} %broadcast_in_dim.1), calls=%async_computation.5 | async-start | bytes 1572864 | tf_op jit(solution)/shard_map/cond/branch_1_fun/all_to_all | solution.py:200
  92.4 4.4 %branch_1_fun.10 = f32[512,1024]{1,0:T(8,128)} custom-call(bf16[512,640]{1,0:T(8,128)(2,1)} %get-tuple-element.110.with_own, bf16[512,1024]{1,0:T(8,128)(2,1)S(1)} %copy-done.2, bf16[512,1024]{1,0:T(8,128)(2,1)} %get-tuple-element.112.z, bf16[512,1024]{1,0:T(8,128)(2,1)} %get-tuple-element.113.other, f32[1,1024]{1,0:T(1,128)S(1)} %get-tuple-element.114.own_square, ...), custom_call_target="tpu_custom_call" | custom-call | tf_op jit(solution)/shard_map/cond/branch_1_fun/pallas_call | solution.py:17
  96.8 5.9 %all-to-all-done.5 = bf16[4,64,1536]{2,1,0:T(8,128)(2,1)} async-done(((bf16[4,64,1536]{2,1,0:T(8,128)(2,1)}), bf16[4,64,1536]{2,1,0:T(8,128)(2,1)}, u32[]{:S(2)}, u32[]{:S(2)}) %all-to-all-start.5) | async-done | bytes 786464 | tf_op jit(solution)/shard_map/cond/branch_1_fun/all_to_all | solution.py:200
  102.8 1.5 %collective-permute-start.14 = (bf16[256,1536]{1,0:T(8,128)(2,1)}, bf16[256,1536]{1,0:T(8,128)(2,1)S(1)}, u32[]{:S(2)}, u32[]{:S(2)}) collective-permute-start(bf16[256,1536]{1,0:T(8,128)(2,1)} %get-tuple-element.167.near), channel_id=1, source_target_pairs={{0,1},{1,0},{2,3},{3,2},{4,5},{5,4},{6,7},{7,6},{8,9},{9,8},{10,11... | collective-permute-start | bytes 2359304 | tf_op jit(solution)/shard_map/ppermute | solution.py:196
  104.3 2.1 %collective-permute-done.14.far = bf16[256,1536]{1,0:T(8,128)(2,1)S(1)} collective-permute-done((bf16[256,1536]{1,0:T(8,128)(2,1)}, bf16[256,1536]{1,0:T(8,128)(2,1)S(1)}, u32[]{:S(2)}, u32[]{:S(2)}) %collective-permute-start.14) | collective-permute-done | bytes 786464 | tf_op jit(solution)/shard_map/ppermute | solution.py:196
  106.4 1.2 %shard_map.42.inner = bf16[512,1536]{1,0:T(8,128)(2,1)S(1)} custom-call(s32[8]{0:T(128)S(1)} %pad_add_fusion.order, bf16[256,1536]{1,0:T(8,128)(2,1)} %get-tuple-element.167.near, bf16[256,1536]{1,0:T(8,128)(2,1)S(1)} %collective-permute-done.14.far), custom_call_target="tpu_custom_call" | custom-call | tf_op jit(solution)/shard_map/pallas_call | solution.py:17
  107.7 4.8 %shard_map.43 = f32[512,1024]{1,0:T(8,128)} custom-call(s32[1]{0:T(128)} %bitcast.2.middle, bf16[512,1536]{1,0:T(8,128)(2,1)S(1)} %shard_map.42.inner, bf16[512,1024]{1,0:T(8,128)(2,1)S(1)} %copy-done.4, bf16[512,1024]{1,0:T(8,128)(2,1)S(1)} %copy-done.3, bf16[512,1024]{1,0:T(8,128)(2,1)S(1)} %copy-done, f32[512,1024]{1,0:T(8,128)} %get-tuple-element.165.held, ...), custom_call_target="tpu_custom_call" | custom-call | tf_op jit(solution)/shard_map/pallas_call | solution.py:17
  (35 shorter events, 3.4 us)
Async XLA Ops:
  1.8 6.8 %collective-permute-start.6 = (f32[2,1024]{1,0:T(2,128)S(1)}, f32[2,1024]{1,0:T(2,128)S(1)}, u32[]{:S(2)}, u32[]{:S(2)}) collective-permute-start(f32[2,1024]{1,0:T(2,128)S(1)} %shard_map.37), channel_id=1, source_target_pairs={{0,24},{8,0},{16,8},{24,16},{1,25},{9,1},{17,9},{25,17},{2,26},{10... | collective-permute-start | bytes 24584 | tf_op jit(solution)/shard_map/ppermute | solution.py:244
  1.9 6.8 %collective-permute-start.5 = (f32[2,1024]{1,0:T(2,128)S(1)}, f32[2,1024]{1,0:T(2,128)S(1)}, u32[]{:S(2)}, u32[]{:S(2)}) collective-permute-start(f32[2,1024]{1,0:T(2,128)S(1)} %shard_map.37), channel_id=1, source_target_pairs={{0,16},{8,24},{16,0},{24,8},{1,17},{9,25},{17,1},{25,9},{2,18},{10... | collective-permute-start | bytes 24584 | tf_op jit(solution)/shard_map/ppermute | solution.py:244
  4.3 4.3 %collective-permute-start.4 = (f32[2,1024]{1,0:T(2,128)S(1)}, f32[2,1024]{1,0:T(2,128)S(1)}, u32[]{:S(2)}, u32[]{:S(2)}) collective-permute-start(f32[2,1024]{1,0:T(2,128)S(1)} %shard_map.37), channel_id=1, source_target_pairs={{0,8},{8,16},{16,24},{24,0},{1,9},{9,17},{17,25},{25,1},{2,10},{10... | collective-permute-start | bytes 24584 | tf_op jit(solution)/shard_map/ppermute | solution.py:244
  6.5 25.3 %collective-permute-start.8 = (bf16[512,1024]{1,0:T(8,128)(2,1)}, bf16[512,1024]{1,0:T(8,128)(2,1)}, u32[]{:S(2)}, u32[]{:S(2)}) collective-permute-start(bf16[512,1024]{1,0:T(8,128)(2,1)} %z.3), channel_id=1, source_target_pairs={{8,16},{16,8},{9,17},{17,9},{10,18},{18,10},{11,19},{19,11},{12,20... | collective-permute-start | bytes 3145736 | tf_op jit(solution)/shard_map/ppermute | solution.py:248
  8.5 23.5 %collective-permute-start.7 = (bf16[512,1024]{1,0:T(8,128)(2,1)}, bf16[512,1024]{1,0:T(8,128)(2,1)}, u32[]{:S(2)}, u32[]{:S(2)}) collective-permute-start(bf16[512,1024]{1,0:T(8,128)(2,1)} %z.3), channel_id=1, source_target_pairs={{0,8},{8,0},{16,24},{24,16},{1,9},{9,1},{17,25},{25,17},{2,10},{10... | collective-permute-start | bytes 3145736 | tf_op jit(solution)/shard_map/ppermute | solution.py:247
  12.1 2.8 %collective-permute-start.9 = (bf16[256,640]{1,0:T(8,128)(2,1)S(1)}, bf16[256,640]{1,0:T(8,128)(2,1)S(1)}, u32[]{:S(2)}, u32[]{:S(2)}) collective-permute-start(bf16[256,640]{1,0:T(8,128)(2,1)S(1)} %get-tuple-element.147), channel_id=1, source_target_pairs={{0,1},{1,0},{2,3},{3,2},{4,5},{5,4},{6,7},{7,6},{8,9},{9,8},{10,11... | collective-permute-start | bytes 983048 | tf_op jit(solution)/shard_map/ppermute | solution.py:196
  32.0 38.8 %collective-permute-start.10 = (bf16[512,1024]{1,0:T(8,128)(2,1)}, bf16[512,1024]{1,0:T(8,128)(2,1)}, u32[]{:S(2)}, u32[]{:S(2)}) collective-permute-start(bf16[512,1024]{1,0:T(8,128)(2,1)} %z.3), channel_id=1, source_target_pairs={{0,24},{24,0},{1,25},{25,1},{2,26},{26,2},{3,27},{27,3},{4,28},{28... | collective-permute-start | bytes 3145736 | tf_op jit(solution)/shard_map/ppermute | solution.py:263
  33.6 35.7 %collective-permute-start.11 = (bf16[256,640]{1,0:T(8,128)(2,1)S(1)}, bf16[256,640]{1,0:T(8,128)(2,1)S(1)}, u32[]{:S(2)}, u32[]{:S(2)}) collective-permute-start(bf16[256,640]{1,0:T(8,128)(2,1)S(1)} %bitcast.4), channel_id=1, source_target_pairs={{0,1},{1,0},{2,3},{3,2},{4,5},{5,4},{6,7},{7,6},{8,9},{9,8},{10,11... | collective-permute-start | bytes 983048 | tf_op jit(solution)/shard_map/ppermute | solution.py:196
  40.1 1.5 %collective-permute-start.1 = (bf16[256,512]{1,0:T(8,128)(2,1)S(1)}, bf16[256,512]{1,0:T(8,128)(2,1)S(1)}, u32[]{:S(2)}, u32[]{:S(2)}) collective-permute-start(bf16[256,512]{1,0:T(8,128)(2,1)S(1)} %get-tuple-element.92), channel_id=1, source_target_pairs={{0,1},{1,0},{2,3},{3,2},{4,5},{5,4},{6,7},{7,6},{8,9},{9,8},{10,11... | collective-permute-start | bytes 786440 | tf_op jit(solution)/shard_map/cond/branch_1_fun/ppermute | solution.py:196
  49.8 12.6 %collective-permute-start.13 = (bf16[64,512]{1,0:T(8,128)(2,1)S(1)}, bf16[64,512]{1,0:T(8,128)(2,1)S(1)}, u32[]{:S(2)}, u32[]{:S(2)}) collective-permute-start(bf16[64,512]{1,0:T(8,128)(2,1)S(1)} %get-tuple-element.154), channel_id=1, source_target_pairs={{8,16},{16,8},{9,17},{17,9},{10,18},{18,10},{11,19},{19,11},{12,20... | collective-permute-start | bytes 196616 | tf_op jit(solution)/shard_map/ppermute | solution.py:283
  53.2 9.2 %collective-permute-start.12 = (bf16[64,512]{1,0:T(8,128)(2,1)S(1)}, bf16[64,512]{1,0:T(8,128)(2,1)S(1)}, u32[]{:S(2)}, u32[]{:S(2)}) collective-permute-start(bf16[64,512]{1,0:T(8,128)(2,1)S(1)} %get-tuple-element.154), channel_id=1, source_target_pairs={{8,0},{16,24},{9,1},{17,25},{10,2},{18,26},{11,3},{19,27},{12,4},{... | collective-permute-start | bytes 196616 | tf_op jit(solution)/shard_map/ppermute | solution.py:283
  62.4 41.8 %collective-permute-start.15 = (bf16[512,1024]{1,0:T(8,128)(2,1)}, bf16[512,1024]{1,0:T(8,128)(2,1)S(1)}, u32[]{:S(2)}, u32[]{:S(2)}) collective-permute-start(bf16[512,1024]{1,0:T(8,128)(2,1)} %collective-permute-done.8), channel_id=1, source_target_pairs={{8,0},{16,24},{9,1},{17,25},{10,2},{18,26},{11,3},{19,27},{12,4},{... | collective-permute-start | bytes 3145736 | tf_op jit(solution)/shard_map/ppermute | solution.py:284
  65.7 38.6 %collective-permute-start.16 = (bf16[512,1024]{1,0:T(8,128)(2,1)}, bf16[512,1024]{1,0:T(8,128)(2,1)S(1)}, u32[]{:S(2)}, u32[]{:S(2)}) collective-permute-start(bf16[512,1024]{1,0:T(8,128)(2,1)} %collective-permute-done.7), channel_id=1, source_target_pairs={{8,16},{16,8},{9,17},{17,9},{10,18},{18,10},{11,19},{19,11},{12,20... | collective-permute-start | bytes 3145736 | tf_op jit(solution)/shard_map/ppermute | solution.py:285
  73.9 2.7 %collective-permute-start.3 = (bf16[256,1024]{1,0:T(8,128)(2,1)S(1)}, bf16[256,1024]{1,0:T(8,128)(2,1)S(1)}, u32[]{:S(2)}, u32[]{:S(2)}) collective-permute-start(bf16[256,1024]{1,0:T(8,128)(2,1)S(1)} %get-tuple-element.122), channel_id=1, source_target_pairs={{0,1},{1,0},{2,3},{3,2},{4,5},{5,4},{6,7},{7,6},{8,9},{9,8},{10,11... | collective-permute-start | bytes 1572872 | tf_op jit(solution)/shard_map/cond/branch_1_fun/ppermute | solution.py:196
  76.7 15.7 %copy-start.2 = (bf16[512,1024]{1,0:T(8,128)(2,1)S(1)}, bf16[512,1024]{1,0:T(8,128)(2,1)}, u32[]{:S(2)}) copy-start(bf16[512,1024]{1,0:T(8,128)(2,1)} %get-tuple-element.111.own) | copy-start | bytes 3145732 | tf_op jit(solution)/shard_map/cond
  88.2 14.6 %all-to-all-start.5 = ((bf16[4,64,1536]{2,1,0:T(8,128)(2,1)}), bf16[4,64,1536]{2,1,0:T(8,128)(2,1)}, u32[]{:S(2)}, u32[]{:S(2)}) async-start(bf16[4,64,1536]{2,1,0:T(8,128)(2,1)} %broadcast_in_dim.1), calls=%async_computation.5 | async-start | bytes 1572864 | tf_op jit(solution)/shard_map/cond/branch_1_fun/all_to_all | solution.py:200
  102.7 4.9 %copy-start = (bf16[512,1024]{1,0:T(8,128)(2,1)S(1)}, bf16[512,1024]{1,0:T(8,128)(2,1)}, u32[]{:S(2)}) copy-start(bf16[512,1024]{1,0:T(8,128)(2,1)} %get-tuple-element.150.own) | copy-start | bytes 3145732
  102.7 4.9 %copy-start.3 = (bf16[512,1024]{1,0:T(8,128)(2,1)S(1)}, bf16[512,1024]{1,0:T(8,128)(2,1)}, u32[]{:S(2)}) copy-start(bf16[512,1024]{1,0:T(8,128)(2,1)} %get-tuple-element.164.opposite) | copy-start | bytes 3145732
  102.7 4.9 %copy-start.4 = (bf16[512,1024]{1,0:T(8,128)(2,1)S(1)}, bf16[512,1024]{1,0:T(8,128)(2,1)}, u32[]{:S(2)}) copy-start(bf16[512,1024]{1,0:T(8,128)(2,1)} %get-tuple-element.156.beside) | copy-start | bytes 3145732
  102.8 3.6 %collective-permute-start.14 = (bf16[256,1536]{1,0:T(8,128)(2,1)}, bf16[256,1536]{1,0:T(8,128)(2,1)S(1)}, u32[]{:S(2)}, u32[]{:S(2)}) collective-permute-start(bf16[256,1536]{1,0:T(8,128)(2,1)} %get-tuple-element.167.near), channel_id=1, source_target_pairs={{0,1},{1,0},{2,3},{3,2},{4,5},{5,4},{6,7},{7,6},{8,9},{9,8},{10,11... | collective-permute-start | bytes 2359304 | tf_op jit(solution)/shard_map/ppermute | solution.py:196

commit v11 on v9

--- a/solution.py
+++ b/solution.py
@@ -90,16 +90,19 @@
 
 
 def middle_kernel(
-    order, turned, beside_in, opposite_in, mean,
+    order, beside_in, opposite_in, mean,
     beside, beside_square, opposite, opposite_square, kept, sent, turned_beside,
 ):
+    centered_into(beside, beside_in, mean[...], beside_square)
+    centered_into(opposite, opposite_in, mean[...], opposite_square)
+    turn_into(turned_beside, order, beside)
+    split_sum(gram(turned_beside[...], opposite[...]), kept, sent, slice(None))
+
+
+def both_kernel(turned, beside, opposite, kept, sent):
     rows = beside.shape[0]
-    centered_into(beside, beside_in, mean[...], beside_square)
     split_sum(gram(turned[...], beside[...]), kept, sent, slice(0, rows))
-    centered_into(opposite, opposite_in, mean[...], opposite_square)
     split_sum(gram(turned[...], opposite[...]), kept, sent, slice(rows, 2 * rows))
-    turn_into(turned_beside, order, beside)
-    split_sum(gram(turned_beside[...], opposite[...]), kept, sent, slice(2 * rows, 3 * rows))
 
 
 def block_kernel(turned, block_in, mean, block, square, kept, sent):
@@ -139,12 +142,29 @@
     out[...] = with_norm(total, last).astype(jnp.bfloat16)
 
 
-def place_kernel(order, near, far, out):
-    eighth = out.shape[0] // 8
-    for k in range(4):
-        here = slice(k * eighth, (k + 1) * eighth)
-        out[pl.ds(pl.multiple_of(order[k] * eighth, eighth), eighth), :] = near[here, :]
-        out[pl.ds(pl.multiple_of(order[4 + k] * eighth, eighth), eighth), :] = far[here, :]
+def place_kernel(order, near, far, *outs):
+    rows, width = outs[0].shape
+    eighth = rows // 8
+    for n, out in enumerate(outs):
+        columns = slice(n * width, (n + 1) * width)
+        for k in range(4):
+            here = slice(k * eighth, (k + 1) * eighth)
+            start = pl.multiple_of(order[k] * eighth, eighth)
+            out[pl.ds(start, eighth), :] = near[here, columns]
+            start = pl.multiple_of(order[4 + k] * eighth, eighth)
+            out[pl.ds(start, eighth), :] = far[here, columns]
+
+
+def push_kernel(inner, beside, opposite, beside_square, opposite_square, out, over):
+    width = beside.shape[1]
+    for k in range(2):
+        here = slice(k * width // 2, (k + 1) * width // 2)
+        outward = dot(inner[...], opposite[:, here])
+        outward = outward - beside[:, here].astype(jnp.float32) * opposite_square[:, here]
+        out[:, here] = outward.astype(jnp.bfloat16)
+        across = dot_t(inner[...], beside[:, here])
+        across = across - opposite[:, here].astype(jnp.float32) * beside_square[:, here]
+        over[:, here] = across.astype(jnp.bfloat16)
 
 
 def coefficient(total):
@@ -170,40 +190,35 @@
         held[:, here] = plain + coefficient(total) * product
 
 
-def last_kernel(total, middle, inner, beside, opposite, own, held, mean, out, over, result):
-    rows, width = own.shape
-
-    def put(arrived, product_of):
+def last_kernel(
+    total, middle, with_beside, with_opposite, beside, opposite, held, out, over, result
+):
+    width = beside.shape[1]
+
+    def put(arrived):
         for k in range(4):
             here = slice(k * width // 4, (k + 1) * width // 4)
-            block = (arrived[:, here].astype(jnp.float32) - mean[:, here]).astype(jnp.bfloat16)
-            wide = block.astype(jnp.float32)
-            square = jnp.sum(wide * wide, axis=0, keepdims=True)
-            product = dot(inner[:, :rows], beside[:, here])
-            product = product + dot(inner[:, rows:2 * rows], opposite[:, here])
-            product = product + product_of(inner[:, 2 * rows:], block)
-            product = product - own[:, here].astype(jnp.float32) * square
+            product = dot(with_beside[...], beside[:, here])
+            product = product + dot(with_opposite[...], opposite[:, here])
+            product = product + arrived[:, here].astype(jnp.float32)
             result[:, here] = held[:, here] + coefficient(total) * product
 
-    pl.when(middle[0] == 1)(lambda: put(over, dot_t))
-    pl.when(middle[0] == 0)(lambda: put(out, dot))
+    pl.when(middle[0] == 1)(lambda: put(over))
+    pl.when(middle[0] == 0)(lambda: put(out))
 
 
 def to_partner(x, step):
     return lax.ppermute(x, "feat", [(i, i ^ step) for i in range(8)])
 
 
-def halve(kept, sent, last=0):
+def scatter_sum(kept, sent, last=0):
     half, n = kept.shape
     part = (half // 4, n)
-    return kernel_call(
+    mine, *out = kernel_call(
         functools.partial(add_kernel, last), [(part, jnp.float32)] + [(part, jnp.bfloat16)] * 3
     )(kept, to_partner(sent, 1))
-
-
-def scatter(mine, *out, last=0):
     got = [to_partner(x, 2 * k) for k, x in enumerate(out, 1)]
-    return kernel_call(functools.partial(total_kernel, last), [(mine.shape, jnp.bfloat16)])(
+    return kernel_call(functools.partial(total_kernel, last), [(part, jnp.bfloat16)])(
         mine, *got
     )[0]
 
@@ -212,10 +227,11 @@
     return jnp.concatenate([x] + [to_partner(x, 2 * k) for k in (1, 2, 3)])
 
 
-def gather_cores(near, order, *others):
-    far = after(to_partner(near, 1), *others)
-    shape = (2 * near.shape[0], near.shape[1])
-    return kernel_call(place_kernel, [(shape, jnp.bfloat16)], smem=1)(order, near, far)[0]
+def gather_cores(near, order, parts=1):
+    shape = (2 * near.shape[0], near.shape[1] // parts)
+    return kernel_call(place_kernel, [(shape, jnp.bfloat16)] * parts, smem=1)(
+        order, near, to_partner(near, 1)
+    )
 
 
 def after(x, *others):
@@ -236,7 +252,7 @@
     all_stats = [stats] + [
         lax.ppermute(stats, "dp", [(i, (i + k) % 4) for i in range(4)]) for k in (1, 2, 3)
     ]
-    ahead = after(z_anchor, *all_stats)
+    ahead = after(z_anchor, stats)
     beside_in = lax.ppermute(ahead, "dp", [(i, i ^ 1) for i in range(4)])
     swapped = lax.ppermute(ahead, "dp", across)
     mean = (all_stats[0][:1] + all_stats[1][:1] + all_stats[2][:1] + all_stats[3][:1]) / 4
@@ -251,33 +267,35 @@
     own, turned, own_square, kept, sent = kernel_call(
         own_kernel, [block, block, flat, *summands(rows + NORM)], smem=1, scratch=12
     )(order, z_anchor, mean)
-    with_own = gather_cores(gather_chips(scatter(*halve(kept, sent, rows), last=rows)), order)
-
-    end = lax.ppermute(after(z_anchor, beside_in, swapped, with_own), "dp", [(0, 3), (3, 0)])
-
-    def first_of_middle(order, turned, beside_in, swapped, mean):
+    near_own = gather_chips(scatter_sum(kept, sent, rows))
+
+    end = lax.ppermute(after(z_anchor, beside_in, swapped, near_own), "dp", [(0, 3), (3, 0)])
+    with_own = gather_cores(after(near_own, beside_in, swapped), order)[0]
+
+    def first_of_middle(turned, beside_in, swapped):
         *blocks, kept, sent, _ = kernel_call(
-            middle_kernel, [block, flat, block, flat, *summands(3 * rows), block],
+            middle_kernel, [block, flat, block, flat, *summands(rows), block],
             smem=1, scratch=12,
-        )(order, turned, beside_in, swapped, mean)
-        return *blocks, scatter(*halve(kept, sent))
-
-    def first_of_end(order, turned, beside_in, swapped, mean):
+        )(order, beside_in, swapped, mean)
+        inner = gather_cores(gather_chips(scatter_sum(kept, sent)), order)[0]
+        beside, beside_square, opposite, opposite_square = blocks
+        out, over = kernel_call(push_kernel, [block, block], scratch=12)(
+            inner, beside, opposite, beside_square, opposite_square
+        )
+        return *blocks, inner, out, over
+
+    def first_of_end(turned, beside_in, swapped):
         beside, square, kept, sent = kernel_call(
             block_kernel, [block, flat, *summands(rows)], scratch=12
         )(turned, beside_in, mean)
-        first = scatter(*halve(kept, sent))
-        first = jnp.concatenate([first, jnp.zeros((rows // 8, 2 * rows), first.dtype)], axis=1)
-        return beside, square, swapped, jnp.zeros_like(square), first
-
-    beside, beside_square, opposite, opposite_square, first = lax.cond(
+        inner = gather_cores(gather_chips(scatter_sum(kept, sent)), order)[0]
+        return beside, square, swapped, jnp.zeros_like(square), inner, swapped, swapped
+
+    beside, beside_square, opposite, opposite_square, first, *ready = lax.cond(
         middle[0] == 1, first_of_middle, first_of_end,
-        order, after(turned, with_own), beside_in, swapped, mean,
-    )
-    handed = [lax.ppermute(first[:, 2 * rows:], "dp", p) for p in (outward, across)]
-    out = lax.ppermute(after(swapped, *handed), "dp", outward)
-    over = lax.ppermute(after(beside_in, *handed), "dp", across)
-    handed = handed[0] + handed[1]
+        after(turned, near_own), beside_in, swapped,
+    )
+    out, over = (lax.ppermute(x, "dp", p) for x, p in zip(ready, (outward, across)))
     result = ((rows, width), jnp.float32)
 
     def hold(opposite_square):
@@ -286,25 +304,26 @@
             own_square, beside_square, opposite_square, mean, spread,
         )[0]
 
-    def second_of_middle(turned, end, opposite, opposite_square, first, handed):
-        inner = jnp.concatenate([first[:, :2 * rows], handed], axis=1)
-        return opposite, gather_chips(inner), hold(opposite_square)
-
-    def second_of_end(turned, end, opposite, opposite_square, first, handed):
+    def second_of_middle(turned, end, opposite, opposite_square, first):
+        kept, sent = kernel_call(both_kernel, summands(2 * rows), scratch=12)(
+            turned, beside, opposite
+        )
+        inner = gather_cores(gather_chips(scatter_sum(kept, sent)), order, 2)
+        return opposite, *inner, hold(opposite_square)
+
+    def second_of_end(turned, end, opposite, opposite_square, first):
         opposite, opposite_square, kept, sent = kernel_call(
             block_kernel, [block, flat, *summands(rows)], scratch=12
         )(turned, end, mean)
-        inner = scatter(*halve(kept, sent))
-        inner = jnp.concatenate([first[:, :rows], inner, handed], axis=1)
-        return opposite, gather_chips(inner), hold(opposite_square)
-
-    opposite, inner, held = lax.cond(
+        inner = gather_cores(gather_chips(scatter_sum(kept, sent)), order)
+        return opposite, first, *inner, hold(opposite_square)
+
+    opposite, with_beside, with_opposite, held = lax.cond(
         middle[0] == 1, second_of_middle, second_of_end,
-        turned, end, opposite, opposite_square, first, handed,
-    )
-    inner = gather_cores(inner, order, out, over)
+        after(turned, *ready), end, opposite, opposite_square, first,
+    )
     return kernel_call(functools.partial(last_kernel, total), [result], smem=1, scratch=12)(
-        middle, inner, beside, opposite, own, held, mean, out, over
+        middle, with_beside, with_opposite, beside, opposite, held, out, over
     )[0]
 
 

time: 102 us -> 101 us (level)
  waiting for transfers between devices: 42.1 us -> 34.5 us
  Pallas kernels: 19.2 us -> 26.6 us
  starting transfers between devices: 36.7 us -> 38.5 us
  local copies, waits for them, and re-layouts: 1.78 us -> 0.02 us
    ppermute x5 -> x3, waiting for transfers between devices: 15.8 us -> 0.01 us  [the longest x2 0.01 us: by_line(): lax.ppermute(x, 'dp', p)]
    ppermute x16 -> x24, starting transfers between devices: 18.2 us -> 26.8 us  [to_partner(): return lax.ppermute(x, 'feat', [(i, i ^ step) for i in range(8)])]
    pallas_call x11 -> x16, Pallas kernels: 19.2 us -> 26.6 us  [call(): pl.pallas_call(body, out_shape=[jax.ShapeDtypeStruct(s, t) for s, t in ou...]
    ppermute x5 -> x3, starting transfers between devices: 9.86 us -> 4.92 us  [the longest x2 3.27 us: by_line(): lax.ppermute(x, 'dp', p)]
    ppermute x16 -> x24, waiting for transfers between devices: 26.1 us -> 30.7 us  [to_partner(): return lax.ppermute(x, 'feat', [(i, i ^ step) for i in range(8)])]
    ppermute x1, waiting for transfers between devices: 0.01 us -> 2.39 us  [by_line(): swapped = lax.ppermute(ahead, 'dp', across)]
    slice x2 -> x0, local copies, waits for them, and re-layouts: 1.76 us -> none  [the longest x1 0.91 us: second_of_middle(): inner = jnp.concatenate([first[:, :2 * rows], handed], axis=1)]
    ppermute x1, starting transfers between devices: 3.66 us -> 1.91 us  [by_line(): swapped = lax.ppermute(ahead, 'dp', across)]
  transfers between devices with their start and end apart: 26 -> 32, of which waited for: 18 -> 25; matrix products, arithmetic and copies ran while one was open for 3% -> 1% of each run, Pallas kernels for 12% -> 20%
where the time goes in v11:
time: 101 us
  starting transfers between devices  38.5 us (38%)
  waiting for transfers between devices  34.5 us (34%)
  Pallas kernels  26.6 us (26%)
    ppermute x24, waiting for transfers between devices, to_partner(): return lax.ppermute(x, 'feat', [(i, i ^ step) for i in range(8)])  30.7 us
    ppermute x24, starting transfers between devices, to_partner(): return lax.ppermute(x, 'feat', [(i, i ^ step) for i in range(8)])  26.8 us
    pallas_call x16, Pallas kernels, call(): pl.pallas_call(body, out_shape=[jax.ShapeDtypeStruct(s, t) for s, t in ou...  26.6 us
    ppermute x3, starting transfers between devices, by_line(): lax.ppermute(stats, 'dp', [(i, (i + k) % 4) for i in range(4)])  3.83 us
    ppermute x2, starting transfers between devices, by_line(): lax.ppermute(x, 'dp', p)  3.27 us
    ppermute x1, waiting for transfers between devices, by_line(): swapped = lax.ppermute(ahead, 'dp', across)  2.39 us
  transfers between devices with their start and end apart: 32, of which 25 were waited for; matrix products, arithmetic and copies ran while one was open for 1% of the time, Pallas kernels for 20%

profile of v11, /device:TPU:9, one launch (start us, length us, event | category | flops | bytes accessed | tf_op | source)
XLA Modules:
  0.0 100.8 jit_solution(3263654787950949290)
XLA Ops:
  0.0 1.9 %shard_map.37 = f32[2,1024]{1,0:T(2,128)S(1)} custom-call(bf16[512,1024]{1,0:T(8,128)(2,1)} %z.3), custom_call_target="tpu_custom_call" | custom-call | tf_op jit(solution)/shard_map/pallas_call | solution.py:17
  4.3 1.4 %collective-permute-start.34 = (f32[2,1024]{1,0:T(2,128)S(1)}, f32[2,1024]{1,0:T(2,128)S(1)}, u32[]{:S(2)}, u32[]{:S(2)}) collective-permute-start(f32[2,1024]{1,0:T(2,128)S(1)} %shard_map.37), channel_id=1, source_target_pairs={{0,24},{8,0},{16,8},{24,16},{1,25},{9,1},{17,9},{25,17},{2,26},{10... | collective-permute-start | bytes 24584 | tf_op jit(solution)/shard_map/ppermute | solution.py:253
  6.8 1.9 %collective-permute-start.43 = (bf16[512,1024]{1,0:T(8,128)(2,1)}, bf16[512,1024]{1,0:T(8,128)(2,1)S(1)}, u32[]{:S(2)}, u32[]{:S(2)}) collective-permute-start(bf16[512,1024]{1,0:T(8,128)(2,1)} %z.3), channel_id=1, source_target_pairs={{8,16},{16,8},{9,17},{17,9},{10,18},{18,10},{11,19},{19,11},{12,20... | collective-permute-start | bytes 3145736 | tf_op jit(solution)/shard_map/ppermute | solution.py:257
  9.5 3.4 %shard_map.38 = (bf16[512,1024]{1,0:T(8,128)(2,1)}, bf16[512,1024]{1,0:T(8,128)(2,1)}, f32[1,1024]{1,0:T(1,128)S(1)}, f32[256,640]{1,0:T(8,128)S(1)}, bf16[256,640]{1,0:T(8,128)(2,1)S(1)}) custom-call(s32[8]{0:T(128)S(1)} %broadcast_xor_fusion.order, bf16[512,1024]{1,0:T(8,128)(2,1)} %z.3, f32[1,1024]{1,0:T(1,128)S(1)} %get-tuple-element.194.mean), custom_call_target="tpu_custom_call" | custom-call | tf_op jit(solution)/shard_map/pallas_call | solution.py:17
  12.8 1.8 %collective-permute-start.35 = (bf16[256,640]{1,0:T(8,128)(2,1)S(1)}, bf16[256,640]{1,0:T(8,128)(2,1)S(1)}, u32[]{:S(2)}, u32[]{:S(2)}) collective-permute-start(bf16[256,640]{1,0:T(8,128)(2,1)S(1)} %get-tuple-element.170), channel_id=1, source_target_pairs={{0,1},{1,0},{2,3},{3,2},{4,5},{5,4},{6,7},{7,6},{8,9},{9,8},{10,11... | collective-permute-start | bytes 983048 | tf_op jit(solution)/shard_map/ppermute | solution.py:211
  21.0 1.7 %collective-permute-done.38.c = bf16[64,640]{1,0:T(8,128)(2,1)S(1)} collective-permute-done((bf16[64,640]{1,0:T(8,128)(2,1)S(1)}, bf16[64,640]{1,0:T(8,128)(2,1)S(1)}, u32[]{:S(2)}, u32[]{:S(2)}) %collective-permute-start.38) | collective-permute-done | bytes 81952 | tf_op jit(solution)/shard_map/ppermute | solution.py:211
  23.7 1.8 %collective-permute-start.41 = (bf16[64,640]{1,0:T(8,128)(2,1)S(1)}, bf16[64,640]{1,0:T(8,128)(2,1)S(1)}, u32[]{:S(2)}, u32[]{:S(2)}) collective-permute-start(bf16[64,640]{1,0:T(8,128)(2,1)S(1)} %shard_map.40), channel_id=1, source_target_pairs={{0,6},{1,7},{2,4},{3,5},{4,2},{5,3},{6,0},{7,1},{8,14},{9,15},{10,... | collective-permute-start | bytes 245768 | tf_op jit(solution)/shard_map/ppermute | solution.py:211
  28.0 1.4 %collective-permute-done.42 = bf16[512,1024]{1,0:T(8,128)(2,1)} collective-permute-done((bf16[512,1024]{1,0:T(8,128)(2,1)}, bf16[512,1024]{1,0:T(8,128)(2,1)}, u32[]{:S(2)}, u32[]{:S(2)}) %collective-permute-start.42) | collective-permute-done | bytes 1048608 | tf_op jit(solution)/shard_map/ppermute | solution.py:256
  29.4 2.4 %collective-permute-done.43 = bf16[512,1024]{1,0:T(8,128)(2,1)S(1)} collective-permute-done((bf16[512,1024]{1,0:T(8,128)(2,1)}, bf16[512,1024]{1,0:T(8,128)(2,1)S(1)}, u32[]{:S(2)}, u32[]{:S(2)}) %collective-permute-start.43) | collective-permute-done | bytes 1048608 | tf_op jit(solution)/shard_map/ppermute | solution.py:257
  31.8 1.6 %collective-permute-start.44 = (bf16[512,1024]{1,0:T(8,128)(2,1)S(1)}, bf16[512,1024]{1,0:T(8,128)(2,1)}, u32[]{:S(2)}, u32[]{:S(2)}) collective-permute-start(bf16[512,1024]{1,0:T(8,128)(2,1)S(1)} %copy-done), channel_id=1, source_target_pairs={{0,24},{24,0},{1,25},{25,1},{2,26},{26,2},{3,27},{27,3},{4,28},{28... | collective-permute-start | bytes 3145736 | tf_op jit(solution)/shard_map/ppermute | solution.py:272
  33.4 30.0 %conditional.2 = (bf16[512,1024]{1,0:T(8,128)(2,1)}, f32[1,1024]{1,0:T(1,128)}, bf16[512,1024]{1,0:T(8,128)(2,1)}, f32[1,1024]{1,0:T(1,128)}, bf16[512,512]{1,0:...) conditional(s32[]{:T(128)} %convert_element_type.8, (bf16[512,1024]{1,0:T(8,128)(2,1)}, ...), branch_computations={%region_0.0_spmd, %region_1.0_spmd} | conditional | flops 1048576 | bytes 10490236 | solution.py:294
  33.4 3.9 %branch_1_fun.10 = (bf16[512,1024]{1,0:T(8,128)(2,1)}, f32[1,1024]{1,0:T(1,128)}, bf16[512,1024]{1,0:T(8,128)(2,1)}, f32[1,1024]{1,0:T(1,128)}, f32[256,512]{1,0...) custom-call(s32[8]{0:T(128)S(1)} %get-tuple-element.86.order, ...), custom_call_target="tpu_custom_call" | custom-call | tf_op jit(solution)/shard_map/cond/branch_1_fun/pallas_call | solution.py:17
  37.4 2.7 %collective-permute-start.8 = (bf16[256,512]{1,0:T(8,128)(2,1)S(1)}, bf16[256,512]{1,0:T(8,128)(2,1)S(1)}, u32[]{:S(2)}, u32[]{:S(2)}) collective-permute-start(bf16[256,512]{1,0:T(8,128)(2,1)S(1)} %get-tuple-element.95), channel_id=1, source_target_pairs={{0,1},{1,0},{2,3},{3,2},{4,5},{5,4},{6,7},{7,6},{8,9},{9,8},{10,11... | collective-permute-start | bytes 786440 | tf_op jit(solution)/shard_map/cond/branch_1_fun/ppermute | solution.py:211
  44.5 2.1 %collective-permute-done.11.c = bf16[64,512]{1,0:T(8,128)(2,1)S(1)} collective-permute-done((bf16[64,512]{1,0:T(8,128)(2,1)S(1)}, bf16[64,512]{1,0:T(8,128)(2,1)S(1)}, u32[]{:S(2)}, u32[]{:S(2)}) %collective-permute-start.11) | collective-permute-done | bytes 65568 | tf_op jit(solution)/shard_map/cond/branch_1_fun/ppermute | solution.py:211
  47.9 1.5 %collective-permute-start.13 = (bf16[64,512]{1,0:T(8,128)(2,1)S(1)}, bf16[64,512]{1,0:T(8,128)(2,1)S(1)}, u32[]{:S(2)}, u32[]{:S(2)}) collective-permute-start(bf16[64,512]{1,0:T(8,128)(2,1)S(1)} %branch_1_fun.12), channel_id=1, source_target_pairs={{0,4},{1,5},{2,6},{3,7},{4,0},{5,1},{6,2},{7,3},{8,12},{9,13},{10,... | collective-permute-start | bytes 196616 | tf_op jit(solution)/shard_map/cond/branch_1_fun/ppermute | solution.py:211
  51.1 3.0 %collective-permute-done.14 = bf16[64,512]{1,0:T(8,128)(2,1)S(1)} collective-permute-done((bf16[64,512]{1,0:T(8,128)(2,1)S(1)}, bf16[64,512]{1,0:T(8,128)(2,1)S(1)}, u32[]{:S(2)}, u32[]{:S(2)}) %collective-permute-start.14) | collective-permute-done | bytes 65568 | tf_op jit(solution)/shard_map/cond/branch_1_fun/ppermute | solution.py:211
  54.1 2.7 %collective-permute-start.15 = (bf16[256,512]{1,0:T(8,128)(2,1)S(1)}, bf16[256,512]{1,0:T(8,128)(2,1)S(1)}, u32[]{:S(2)}, u32[]{:S(2)}) collective-permute-start(bf16[256,512]{1,0:T(8,128)(2,1)S(1)} %pad_maximum_fusion.1.near), channel_id=1, source_target_pairs={{0,1},{1,0},{2,3},{3,2},{4,5},{5,4},{6,7},{7,6},{8,9},{9,8},{10,11... | collective-permute-start | bytes 786440 | tf_op jit(solution)/shard_map/cond/branch_1_fun/ppermute | solution.py:211
  58.0 1.4 %branch_1_fun.13.inner = bf16[512,512]{1,0:T(8,128)(2,1)} custom-call(s32[8]{0:T(128)S(1)} %get-tuple-element.86.order, bf16[256,512]{1,0:T(8,128)(2,1)S(1)} %pad_maximum_fusion.1.near, bf16[256,512]{1,0:T(8,128)(2,1)S(1)} %collective-permute-done.15.far), custom_call_target="tpu_custom_call" | custom-call | tf_op jit(solution)/shard_map/cond/branch_1_fun/pallas_call | solution.py:17
  59.4 4.1 %branch_1_fun.14 = (bf16[512,1024]{1,0:T(8,128)(2,1)}, bf16[512,1024]{1,0:T(8,128)(2,1)}) custom-call(bf16[512,512]{1,0:T(8,128)(2,1)} %branch_1_fun.13.inner, bf16[512,1024]{1,0:T(8,128)(2,1)} %get-tuple-element.202.beside, bf16[512,1024]{1,0:T(8,128)(2,1)} %get-tuple-element.204.opposite, f32[1,1024]{1,0:T(1,128)} %get-tuple-element.203.beside_square, ...), custom_call_target="tpu_custom_call" | custom-call | tf_op jit(solution)/shard_map/cond/branch_1_fun/pallas_call | solution.py:17
  64.8 1.9 %collective-permute-start.47 = (bf16[512,1024]{1,0:T(8,128)(2,1)}, bf16[512,1024]{1,0:T(8,128)(2,1)S(1)}, u32[]{:S(2)}, u32[]{:S(2)}) collective-permute-start(bf16[512,1024]{1,0:T(8,128)(2,1)} %get-tuple-element.178), channel_id=1, source_target_pairs={{8,16},{16,8},{9,17},{17,9},{10,18},{18,10},{11,19},{19,11},{12,20... | collective-permute-start | bytes 3145736 | tf_op jit(solution)/shard_map/ppermute | solution.py:298
  69.3 27.2 %conditional.3 = (bf16[512,1024]{1,0:T(8,128)(2,1)}, bf16[512,512]{1,0:T(8,128)(2,1)}, bf16[512,512]{1,0:T(8,128)(2,1)S(1)}, f32[512,1024]{1,0:T(8,128)S(1)}) conditional(s32[]{:T(128)} %convert_element_type.8, (bf16[512,1024]{1,0:T(8,128)(2,1)}, bf16[512,1024]{1,0:T(8,128)(2,1)}, f32[1,1024]{1,0:T(1,128)S(1)}, s32[8]{0:T(128)S(1)}, ...), branch_computations={%region_2.0_spmd, %region_3.0_spmd} | conditional | flops 2097152 | bytes 16777624 | solution.py:321
  69.5 3.1 %branch_1_fun.15 = (f32[256,1024]{1,0:T(8,128)S(1)}, bf16[256,1024]{1,0:T(8,128)(2,1)S(1)}) custom-call(bf16[512,1024]{1,0:T(8,128)(2,1)} %get-tuple-element.124.turned, bf16[512,1024]{1,0:T(8,128)(2,1)} %get-tuple-element.125.beside, bf16[512,1024]{1,0:T(8,128)(2,1)} %get-tuple-element.213.opposite), custom_call_target="tpu_custom_call" | custom-call | tf_op jit(solution)/shard_map/cond/branch_1_fun/pallas_call | solution.py:17
  73.1 1.5 %collective-permute-done.24.got = bf16[256,1024]{1,0:T(8,128)(2,1)S(1)} collective-permute-done((bf16[256,1024]{1,0:T(8,128)(2,1)S(1)}, bf16[256,1024]{1,0:T(8,128)(2,1)S(1)}, u32[]{:S(2)}, u32[]{:S(2)}) %collective-permute-start.24) | collective-permute-done | bytes 524320 | tf_op jit(solution)/shard_map/cond/branch_1_fun/ppermute | solution.py:211
  75.9 1.6 %collective-permute-start.27 = (bf16[64,1024]{1,0:T(8,128)(2,1)S(1)}, bf16[64,1024]{1,0:T(8,128)(2,1)S(1)}, u32[]{:S(2)}, u32[]{:S(2)}) collective-permute-start(bf16[64,1024]{1,0:T(8,128)(2,1)S(1)} %get-tuple-element.131), channel_id=1, source_target_pairs={{0,6},{1,7},{2,4},{3,5},{4,2},{5,3},{6,0},{7,1},{8,14},{9,15},{10,... | collective-permute-start | bytes 393224 | tf_op jit(solution)/shard_map/cond/branch_1_fun/ppermute | solution.py:211
  77.5 2.1 %collective-permute-done.25.a = bf16[64,1024]{1,0:T(8,128)(2,1)S(1)} collective-permute-done((bf16[64,1024]{1,0:T(8,128)(2,1)S(1)}, bf16[64,1024]{1,0:T(8,128)(2,1)S(1)}, u32[]{:S(2)}, u32[]{:S(2)}) %collective-permute-start.25) | collective-permute-done | bytes 131104 | tf_op jit(solution)/shard_map/cond/branch_1_fun/ppermute | solution.py:211
  80.2 2.4 %collective-permute-done.27.c = bf16[64,1024]{1,0:T(8,128)(2,1)S(1)} collective-permute-done((bf16[64,1024]{1,0:T(8,128)(2,1)S(1)}, bf16[64,1024]{1,0:T(8,128)(2,1)S(1)}, u32[]{:S(2)}, u32[]{:S(2)}) %collective-permute-start.27) | collective-permute-done | bytes 131104 | tf_op jit(solution)/shard_map/cond/branch_1_fun/ppermute | solution.py:211
  85.4 1.5 %collective-permute-done.28 = bf16[64,1024]{1,0:T(8,128)(2,1)S(1)} collective-permute-done((bf16[64,1024]{1,0:T(8,128)(2,1)S(1)}, bf16[64,1024]{1,0:T(8,128)(2,1)S(1)}, u32[]{:S(2)}, u32[]{:S(2)}) %collective-permute-start.28) | collective-permute-done | bytes 131104 | tf_op jit(solution)/shard_map/cond/branch_1_fun/ppermute | solution.py:211
  87.5 3.3 %collective-permute-done.30 = bf16[64,1024]{1,0:T(8,128)(2,1)S(1)} collective-permute-done((bf16[64,1024]{1,0:T(8,128)(2,1)S(1)}, bf16[64,1024]{1,0:T(8,128)(2,1)S(1)}, u32[]{:S(2)}, u32[]{:S(2)}) %collective-permute-start.30) | collective-permute-done | bytes 131104 | tf_op jit(solution)/shard_map/cond/branch_1_fun/ppermute | solution.py:211
  90.9 2.2 %collective-permute-start.31 = (bf16[256,1024]{1,0:T(8,128)(2,1)S(1)}, bf16[256,1024]{1,0:T(8,128)(2,1)S(1)}, u32[]{:S(2)}, u32[]{:S(2)}) collective-permute-start(bf16[256,1024]{1,0:T(8,128)(2,1)S(1)} %pad_maximum_fusion.3.near), channel_id=1, source_target_pairs={{0,1},{1,0},{2,3},{3,2},{4,5},{5,4},{6,7},{7,6},{8,9},{9,8},{10,11... | collective-permute-start | bytes 1572872 | tf_op jit(solution)/shard_map/cond/branch_1_fun/ppermute | solution.py:211
  93.0 2.0 %branch_1_fun.19 = f32[512,1024]{1,0:T(8,128)S(1)} custom-call(bf16[512,640]{1,0:T(8,128)(2,1)S(1)} %get-tuple-element.134.with_own, bf16[512,1024]{1,0:T(8,128)(2,1)S(1)} %copy-done.4, bf16[512,1024]{1,0:T(8,128)(2,1)S(1)} %get-tuple-element.136.z, bf16[512,1024]{1,0:T(8,128)(2,1)S(1)} %copy-done.2, f32[1,1024]{1,0:T(1,128)S(1)} %get-tuple-element.138.own_square, ...), custom_call_target="tpu_custom_call" | custom-call | tf_op jit(solution)/shard_map/cond/branch_1_fun/pallas_call | solution.py:17
  95.0 1.4 %branch_1_fun.18 = (bf16[512,512]{1,0:T(8,128)(2,1)}, bf16[512,512]{1,0:T(8,128)(2,1)S(1)}) custom-call(s32[8]{0:T(128)S(1)} %get-tuple-element.123.order, bf16[256,1024]{1,0:T(8,128)(2,1)S(1)} %pad_maximum_fusion.3.near, bf16[256,1024]{1,0:T(8,128)(2,1)S(1)} %collective-permute-done.31.far), custom_call_target="tpu_custom_call" | custom-call | tf_op jit(solution)/shard_map/cond/branch_1_fun/pallas_call | solution.py:17
  96.5 4.3 %shard_map.42 = f32[512,1024]{1,0:T(8,128)} custom-call(s32[1]{0:T(128)} %bitcast.middle, bf16[512,512]{1,0:T(8,128)(2,1)} %get-tuple-element.189.with_beside, bf16[512,512]{1,0:T(8,128)(2,1)S(1)} %get-tuple-element.190.with_opposite, bf16[512,1024]{1,0:T(8,128)(2,1)} %get-tuple-element.186.beside, bf16[512,1024]{1,0:T(8,128)(2,1)} %get-tuple-element.191.opposite, ...), custom_call_target="tpu_custom_call" | custom-call | tf_op jit(solution)/shard_map/pallas_call | solution.py:17
  (61 shorter events, 32.3 us)
Async XLA Ops:
  1.9 7.5 %collective-permute-start.32 = (f32[2,1024]{1,0:T(2,128)S(1)}, f32[2,1024]{1,0:T(2,128)S(1)}, u32[]{:S(2)}, u32[]{:S(2)}) collective-permute-start(f32[2,1024]{1,0:T(2,128)S(1)} %shard_map.37), channel_id=1, source_target_pairs={{0,8},{8,16},{16,24},{24,0},{1,9},{9,17},{17,25},{25,1},{2,10},{10... | collective-permute-start | bytes 24584 | tf_op jit(solution)/shard_map/ppermute | solution.py:253
  3.3 6.1 %collective-permute-start.33 = (f32[2,1024]{1,0:T(2,128)S(1)}, f32[2,1024]{1,0:T(2,128)S(1)}, u32[]{:S(2)}, u32[]{:S(2)}) collective-permute-start(f32[2,1024]{1,0:T(2,128)S(1)} %shard_map.37), channel_id=1, source_target_pairs={{0,16},{8,24},{16,0},{24,8},{1,17},{9,25},{17,1},{25,9},{2,18},{10... | collective-permute-start | bytes 24584 | tf_op jit(solution)/shard_map/ppermute | solution.py:253
  4.3 5.1 %collective-permute-start.34 = (f32[2,1024]{1,0:T(2,128)S(1)}, f32[2,1024]{1,0:T(2,128)S(1)}, u32[]{:S(2)}, u32[]{:S(2)}) collective-permute-start(f32[2,1024]{1,0:T(2,128)S(1)} %shard_map.37), channel_id=1, source_target_pairs={{0,24},{8,0},{16,8},{24,16},{1,25},{9,1},{17,9},{25,17},{2,26},{10... | collective-permute-start | bytes 24584 | tf_op jit(solution)/shard_map/ppermute | solution.py:253
  5.7 23.6 %collective-permute-start.42 = (bf16[512,1024]{1,0:T(8,128)(2,1)}, bf16[512,1024]{1,0:T(8,128)(2,1)}, u32[]{:S(2)}, u32[]{:S(2)}) collective-permute-start(bf16[512,1024]{1,0:T(8,128)(2,1)} %z.3), channel_id=1, source_target_pairs={{0,8},{8,0},{16,24},{24,16},{1,9},{9,1},{17,25},{25,17},{2,10},{10... | collective-permute-start | bytes 3145736 | tf_op jit(solution)/shard_map/ppermute | solution.py:256
  6.8 24.9 %collective-permute-start.43 = (bf16[512,1024]{1,0:T(8,128)(2,1)}, bf16[512,1024]{1,0:T(8,128)(2,1)S(1)}, u32[]{:S(2)}, u32[]{:S(2)}) collective-permute-start(bf16[512,1024]{1,0:T(8,128)(2,1)} %z.3), channel_id=1, source_target_pairs={{8,16},{16,8},{9,17},{17,9},{10,18},{18,10},{11,19},{19,11},{12,20... | collective-permute-start | bytes 3145736 | tf_op jit(solution)/shard_map/ppermute | solution.py:257
  12.8 3.1 %collective-permute-start.35 = (bf16[256,640]{1,0:T(8,128)(2,1)S(1)}, bf16[256,640]{1,0:T(8,128)(2,1)S(1)}, u32[]{:S(2)}, u32[]{:S(2)}) collective-permute-start(bf16[256,640]{1,0:T(8,128)(2,1)S(1)} %get-tuple-element.170), channel_id=1, source_target_pairs={{0,1},{1,0},{2,3},{3,2},{4,5},{5,4},{6,7},{7,6},{8,9},{9,8},{10,11... | collective-permute-start | bytes 983048 | tf_op jit(solution)/shard_map/ppermute | solution.py:211
  16.0 3.8 %collective-permute-start.36 = (bf16[64,640]{1,0:T(8,128)(2,1)S(1)}, bf16[64,640]{1,0:T(8,128)(2,1)S(1)}, u32[]{:S(2)}, u32[]{:S(2)}) collective-permute-start(bf16[64,640]{1,0:T(8,128)(2,1)S(1)} %get-tuple-element.172), channel_id=1, source_target_pairs={{0,2},{1,3},{2,0},{3,1},{4,6},{5,7},{6,4},{7,5},{8,10},{9,11},{10,... | collective-permute-start | bytes 245768 | tf_op jit(solution)/shard_map/ppermute | solution.py:211
  17.3 3.7 %collective-permute-start.37 = (bf16[64,640]{1,0:T(8,128)(2,1)S(1)}, bf16[64,640]{1,0:T(8,128)(2,1)S(1)}, u32[]{:S(2)}, u32[]{:S(2)}) collective-permute-start(bf16[64,640]{1,0:T(8,128)(2,1)S(1)} %get-tuple-element.173), channel_id=1, source_target_pairs={{0,4},{1,5},{2,6},{3,7},{4,0},{5,1},{6,2},{7,3},{8,12},{9,13},{10,... | collective-permute-start | bytes 245768 | tf_op jit(solution)/shard_map/ppermute | solution.py:211
  18.5 4.2 %collective-permute-start.38 = (bf16[64,640]{1,0:T(8,128)(2,1)S(1)}, bf16[64,640]{1,0:T(8,128)(2,1)S(1)}, u32[]{:S(2)}, u32[]{:S(2)}) collective-permute-start(bf16[64,640]{1,0:T(8,128)(2,1)S(1)} %get-tuple-element.174), channel_id=1, source_target_pairs={{0,6},{1,7},{2,4},{3,5},{4,2},{5,3},{6,0},{7,1},{8,14},{9,15},{10,... | collective-permute-start | bytes 245768 | tf_op jit(solution)/shard_map/ppermute | solution.py:211
  22.8 3.8 %collective-permute-start.39 = (bf16[64,640]{1,0:T(8,128)(2,1)S(1)}, bf16[64,640]{1,0:T(8,128)(2,1)S(1)}, u32[]{:S(2)}, u32[]{:S(2)}) collective-permute-start(bf16[64,640]{1,0:T(8,128)(2,1)S(1)} %shard_map.40), channel_id=1, source_target_pairs={{0,2},{1,3},{2,0},{3,1},{4,6},{5,7},{6,4},{7,5},{8,10},{9,11},{10,... | collective-permute-start | bytes 245768 | tf_op jit(solution)/shard_map/ppermute | solution.py:211
  23.5 3.7 %collective-permute-start.40 = (bf16[64,640]{1,0:T(8,128)(2,1)S(1)}, bf16[64,640]{1,0:T(8,128)(2,1)S(1)}, u32[]{:S(2)}, u32[]{:S(2)}) collective-permute-start(bf16[64,640]{1,0:T(8,128)(2,1)S(1)} %shard_map.40), channel_id=1, source_target_pairs={{0,4},{1,5},{2,6},{3,7},{4,0},{5,1},{6,2},{7,3},{8,12},{9,13},{10,... | collective-permute-start | bytes 245768 | tf_op jit(solution)/shard_map/ppermute | solution.py:211
  23.7 4.2 %collective-permute-start.41 = (bf16[64,640]{1,0:T(8,128)(2,1)S(1)}, bf16[64,640]{1,0:T(8,128)(2,1)S(1)}, u32[]{:S(2)}, u32[]{:S(2)}) collective-permute-start(bf16[64,640]{1,0:T(8,128)(2,1)S(1)} %shard_map.40), channel_id=1, source_target_pairs={{0,6},{1,7},{2,4},{3,5},{4,2},{5,3},{6,0},{7,1},{8,14},{9,15},{10,... | collective-permute-start | bytes 245768 | tf_op jit(solution)/shard_map/ppermute | solution.py:211
  31.8 37.5 %collective-permute-start.44 = (bf16[512,1024]{1,0:T(8,128)(2,1)S(1)}, bf16[512,1024]{1,0:T(8,128)(2,1)}, u32[]{:S(2)}, u32[]{:S(2)}) collective-permute-start(bf16[512,1024]{1,0:T(8,128)(2,1)S(1)} %copy-done), channel_id=1, source_target_pairs={{0,24},{24,0},{1,25},{25,1},{2,26},{26,2},{3,27},{27,3},{4,28},{28... | collective-permute-start | bytes 3145736 | tf_op jit(solution)/shard_map/ppermute | solution.py:272
  37.4 3.9 %collective-permute-start.8 = (bf16[256,512]{1,0:T(8,128)(2,1)S(1)}, bf16[256,512]{1,0:T(8,128)(2,1)S(1)}, u32[]{:S(2)}, u32[]{:S(2)}) collective-permute-start(bf16[256,512]{1,0:T(8,128)(2,1)S(1)} %get-tuple-element.95), channel_id=1, source_target_pairs={{0,1},{1,0},{2,3},{3,2},{4,5},{5,4},{6,7},{7,6},{8,9},{9,8},{10,11... | collective-permute-start | bytes 786440 | tf_op jit(solution)/shard_map/cond/branch_1_fun/ppermute | solution.py:211
  41.3 3.2 %collective-permute-start.10 = (bf16[64,512]{1,0:T(8,128)(2,1)S(1)}, bf16[64,512]{1,0:T(8,128)(2,1)S(1)}, u32[]{:S(2)}, u32[]{:S(2)}) collective-permute-start(bf16[64,512]{1,0:T(8,128)(2,1)S(1)} %get-tuple-element.98), channel_id=1, source_target_pairs={{0,4},{1,5},{2,6},{3,7},{4,0},{5,1},{6,2},{7,3},{8,12},{9,13},{10,... | collective-permute-start | bytes 196616 | tf_op jit(solution)/shard_map/cond/branch_1_fun/ppermute | solution.py:211
  42.6 4.0 %collective-permute-start.11 = (bf16[64,512]{1,0:T(8,128)(2,1)S(1)}, bf16[64,512]{1,0:T(8,128)(2,1)S(1)}, u32[]{:S(2)}, u32[]{:S(2)}) collective-permute-start(bf16[64,512]{1,0:T(8,128)(2,1)S(1)} %get-tuple-element.99), channel_id=1, source_target_pairs={{0,6},{1,7},{2,4},{3,5},{4,2},{5,3},{6,0},{7,1},{8,14},{9,15},{10,... | collective-permute-start | bytes 196616 | tf_op jit(solution)/shard_map/cond/branch_1_fun/ppermute | solution.py:211
  43.7 4.0 %collective-permute-start.9 = (bf16[64,512]{1,0:T(8,128)(2,1)S(1)}, bf16[64,512]{1,0:T(8,128)(2,1)S(1)}, u32[]{:S(2)}, u32[]{:S(2)}) collective-permute-start(bf16[64,512]{1,0:T(8,128)(2,1)S(1)} %get-tuple-element.97), channel_id=1, source_target_pairs={{0,2},{1,3},{2,0},{3,1},{4,6},{5,7},{6,4},{7,5},{8,10},{9,11},{10,... | collective-permute-start | bytes 196616 | tf_op jit(solution)/shard_map/cond/branch_1_fun/ppermute | solution.py:211
  47.8 3.2 %collective-permute-start.12 = (bf16[64,512]{1,0:T(8,128)(2,1)S(1)}, bf16[64,512]{1,0:T(8,128)(2,1)S(1)}, u32[]{:S(2)}, u32[]{:S(2)}) collective-permute-start(bf16[64,512]{1,0:T(8,128)(2,1)S(1)} %branch_1_fun.12), channel_id=1, source_target_pairs={{0,2},{1,3},{2,0},{3,1},{4,6},{5,7},{6,4},{7,5},{8,10},{9,11},{10,... | collective-permute-start | bytes 196616 | tf_op jit(solution)/shard_map/cond/branch_1_fun/ppermute | solution.py:211
  47.9 3.2 %collective-permute-start.13 = (bf16[64,512]{1,0:T(8,128)(2,1)S(1)}, bf16[64,512]{1,0:T(8,128)(2,1)S(1)}, u32[]{:S(2)}, u32[]{:S(2)}) collective-permute-start(bf16[64,512]{1,0:T(8,128)(2,1)S(1)} %branch_1_fun.12), channel_id=1, source_target_pairs={{0,4},{1,5},{2,6},{3,7},{4,0},{5,1},{6,2},{7,3},{8,12},{9,13},{10,... | collective-permute-start | bytes 196616 | tf_op jit(solution)/shard_map/cond/branch_1_fun/ppermute | solution.py:211
  49.5 4.6 %collective-permute-start.14 = (bf16[64,512]{1,0:T(8,128)(2,1)S(1)}, bf16[64,512]{1,0:T(8,128)(2,1)S(1)}, u32[]{:S(2)}, u32[]{:S(2)}) collective-permute-start(bf16[64,512]{1,0:T(8,128)(2,1)S(1)} %branch_1_fun.12), channel_id=1, source_target_pairs={{0,6},{1,7},{2,4},{3,5},{4,2},{5,3},{6,0},{7,1},{8,14},{9,15},{10,... | collective-permute-start | bytes 196616 | tf_op jit(solution)/shard_map/cond/branch_1_fun/ppermute | solution.py:211
  54.1 3.9 %collective-permute-start.15 = (bf16[256,512]{1,0:T(8,128)(2,1)S(1)}, bf16[256,512]{1,0:T(8,128)(2,1)S(1)}, u32[]{:S(2)}, u32[]{:S(2)}) collective-permute-start(bf16[256,512]{1,0:T(8,128)(2,1)S(1)} %pad_maximum_fusion.1.near), channel_id=1, source_target_pairs={{0,1},{1,0},{2,3},{3,2},{4,5},{5,4},{6,7},{7,6},{8,9},{9,8},{10,11... | collective-permute-start | bytes 786440 | tf_op jit(solution)/shard_map/cond/branch_1_fun/ppermute | solution.py:211
  63.4 33.1 %collective-permute-start.46 = (bf16[512,1024]{1,0:T(8,128)(2,1)}, bf16[512,1024]{1,0:T(8,128)(2,1)S(1)}, u32[]{:S(2)}, u32[]{:S(2)}) collective-permute-start(bf16[512,1024]{1,0:T(8,128)(2,1)} %get-tuple-element.177), channel_id=1, source_target_pairs={{8,0},{16,24},{9,1},{17,25},{10,2},{18,26},{11,3},{19,27},{12,4},{... | collective-permute-start | bytes 3145736 | tf_op jit(solution)/shard_map/ppermute | solution.py:298
  64.8 31.7 %collective-permute-start.47 = (bf16[512,1024]{1,0:T(8,128)(2,1)}, bf16[512,1024]{1,0:T(8,128)(2,1)S(1)}, u32[]{:S(2)}, u32[]{:S(2)}) collective-permute-start(bf16[512,1024]{1,0:T(8,128)(2,1)} %get-tuple-element.178), channel_id=1, source_target_pairs={{8,16},{16,8},{9,17},{17,9},{10,18},{18,10},{11,19},{19,11},{12,20... | collective-permute-start | bytes 3145736 | tf_op jit(solution)/shard_map/ppermute | solution.py:298
  66.7 2.0 %collective-permute-start.45 = (bf16[256,640]{1,0:T(8,128)(2,1)S(1)}, bf16[256,640]{1,0:T(8,128)(2,1)S(1)}, u32[]{:S(2)}, u32[]{:S(2)}) collective-permute-start(bf16[256,640]{1,0:T(8,128)(2,1)S(1)} %pad_maximum_fusion.4.near), channel_id=1, source_target_pairs={{0,1},{1,0},{2,3},{3,2},{4,5},{5,4},{6,7},{7,6},{8,9},{9,8},{10,11... | collective-permute-start | bytes 983048 | tf_op jit(solution)/shard_map/ppermute | solution.py:211
  72.7 2.0 %collective-permute-start.24 = (bf16[256,1024]{1,0:T(8,128)(2,1)S(1)}, bf16[256,1024]{1,0:T(8,128)(2,1)S(1)}, u32[]{:S(2)}, u32[]{:S(2)}) collective-permute-start(bf16[256,1024]{1,0:T(8,128)(2,1)S(1)} %get-tuple-element.127), channel_id=1, source_target_pairs={{0,1},{1,0},{2,3},{3,2},{4,5},{5,4},{6,7},{7,6},{8,9},{9,8},{10,11... | collective-permute-start | bytes 1572872 | tf_op jit(solution)/shard_map/cond/branch_1_fun/ppermute | solution.py:211
  74.8 4.8 %collective-permute-start.25 = (bf16[64,1024]{1,0:T(8,128)(2,1)S(1)}, bf16[64,1024]{1,0:T(8,128)(2,1)S(1)}, u32[]{:S(2)}, u32[]{:S(2)}) collective-permute-start(bf16[64,1024]{1,0:T(8,128)(2,1)S(1)} %get-tuple-element.129), channel_id=1, source_target_pairs={{0,2},{1,3},{2,0},{3,1},{4,6},{5,7},{6,4},{7,5},{8,10},{9,11},{10,... | collective-permute-start | bytes 393224 | tf_op jit(solution)/shard_map/cond/branch_1_fun/ppermute | solution.py:211
  75.6 4.6 %collective-permute-start.26 = (bf16[64,1024]{1,0:T(8,128)(2,1)S(1)}, bf16[64,1024]{1,0:T(8,128)(2,1)S(1)}, u32[]{:S(2)}, u32[]{:S(2)}) collective-permute-start(bf16[64,1024]{1,0:T(8,128)(2,1)S(1)} %get-tuple-element.130), channel_id=1, source_target_pairs={{0,4},{1,5},{2,6},{3,7},{4,0},{5,1},{6,2},{7,3},{8,12},{9,13},{10,... | collective-permute-start | bytes 393224 | tf_op jit(solution)/shard_map/cond/branch_1_fun/ppermute | solution.py:211
  75.9 6.7 %collective-permute-start.27 = (bf16[64,1024]{1,0:T(8,128)(2,1)S(1)}, bf16[64,1024]{1,0:T(8,128)(2,1)S(1)}, u32[]{:S(2)}, u32[]{:S(2)}) collective-permute-start(bf16[64,1024]{1,0:T(8,128)(2,1)S(1)} %get-tuple-element.131), channel_id=1, source_target_pairs={{0,6},{1,7},{2,4},{3,5},{4,2},{5,3},{6,0},{7,1},{8,14},{9,15},{10,... | collective-permute-start | bytes 393224 | tf_op jit(solution)/shard_map/cond/branch_1_fun/ppermute | solution.py:211
  82.6 4.2 %collective-permute-start.28 = (bf16[64,1024]{1,0:T(8,128)(2,1)S(1)}, bf16[64,1024]{1,0:T(8,128)(2,1)S(1)}, u32[]{:S(2)}, u32[]{:S(2)}) collective-permute-start(bf16[64,1024]{1,0:T(8,128)(2,1)S(1)} %branch_1_fun.17), channel_id=1, source_target_pairs={{0,2},{1,3},{2,0},{3,1},{4,6},{5,7},{6,4},{7,5},{8,10},{9,11},{10,... | collective-permute-start | bytes 393224 | tf_op jit(solution)/shard_map/cond/branch_1_fun/ppermute | solution.py:211
  83.4 4.1 %collective-permute-start.29 = (bf16[64,1024]{1,0:T(8,128)(2,1)S(1)}, bf16[64,1024]{1,0:T(8,128)(2,1)S(1)}, u32[]{:S(2)}, u32[]{:S(2)}) collective-permute-start(bf16[64,1024]{1,0:T(8,128)(2,1)S(1)} %branch_1_fun.17), channel_id=1, source_target_pairs={{0,4},{1,5},{2,6},{3,7},{4,0},{5,1},{6,2},{7,3},{8,12},{9,13},{10,... | collective-permute-start | bytes 393224 | tf_op jit(solution)/shard_map/cond/branch_1_fun/ppermute | solution.py:211
  84.4 6.4 %collective-permute-start.30 = (bf16[64,1024]{1,0:T(8,128)(2,1)S(1)}, bf16[64,1024]{1,0:T(8,128)(2,1)S(1)}, u32[]{:S(2)}, u32[]{:S(2)}) collective-permute-start(bf16[64,1024]{1,0:T(8,128)(2,1)S(1)} %branch_1_fun.17), channel_id=1, source_target_pairs={{0,6},{1,7},{2,4},{3,5},{4,2},{5,3},{6,0},{7,1},{8,14},{9,15},{10,... | collective-permute-start | bytes 393224 | tf_op jit(solution)/shard_map/cond/branch_1_fun/ppermute | solution.py:211
  90.9 4.2 %collective-permute-start.31 = (bf16[256,1024]{1,0:T(8,128)(2,1)S(1)}, bf16[256,1024]{1,0:T(8,128)(2,1)S(1)}, u32[]{:S(2)}, u32[]{:S(2)}) collective-permute-start(bf16[256,1024]{1,0:T(8,128)(2,1)S(1)} %pad_maximum_fusion.3.near), channel_id=1, source_target_pairs={{0,1},{1,0},{2,3},{3,2},{4,5},{5,4},{6,7},{7,6},{8,9},{9,8},{10,11... | collective-permute-start | bytes 1572872 | tf_op jit(solution)/shard_map/cond/branch_1_fun/ppermute | solution.py:211
  (3 other events, 72.5 us)

commit v12 on v9

--- a/solution.py
+++ b/solution.py
@@ -89,22 +89,41 @@
     sent[:, here] = inner[half:].astype(jnp.bfloat16)
 
 
-def middle_kernel(
-    order, turned, beside_in, opposite_in, mean,
+def first_kernel(
+    order, middle, turned, beside_in, opposite_in, mean,
     beside, beside_square, opposite, opposite_square, kept, sent, turned_beside,
 ):
-    rows = beside.shape[0]
     centered_into(beside, beside_in, mean[...], beside_square)
-    split_sum(gram(turned[...], beside[...]), kept, sent, slice(0, rows))
-    centered_into(opposite, opposite_in, mean[...], opposite_square)
-    split_sum(gram(turned[...], opposite[...]), kept, sent, slice(rows, 2 * rows))
-    turn_into(turned_beside, order, beside)
-    split_sum(gram(turned_beside[...], opposite[...]), kept, sent, slice(2 * rows, 3 * rows))
-
-
-def block_kernel(turned, block_in, mean, block, square, kept, sent):
-    centered_into(block, block_in, mean[...], square)
-    split_sum(gram(turned[...], block[...]), kept, sent, slice(None))
+
+    @pl.when(middle[0] == 1)
+    def _():
+        centered_into(opposite, opposite_in, mean[...], opposite_square)
+        turn_into(turned_beside, order, beside)
+        split_sum(gram(turned_beside[...], opposite[...]), kept, sent, slice(None))
+
+    @pl.when(middle[0] == 0)
+    def _():
+        split_sum(gram(turned[...], beside[...]), kept, sent, slice(None))
+
+
+def second_kernel(
+    middle, turned, beside, swapped, swapped_square, end, mean, opposite, square, kept, sent
+):
+    rows = opposite.shape[0]
+
+    @pl.when(middle[0] == 1)
+    def _():
+        opposite[...] = swapped[...]
+        square[...] = swapped_square[...]
+        split_sum(gram(turned[...], beside[...]), kept, sent, slice(rows, 2 * rows))
+
+    @pl.when(middle[0] == 0)
+    def _():
+        centered_into(opposite, end, mean[...], square)
+        kept[:, rows:] = jnp.zeros_like(kept[:, rows:])
+        sent[:, rows:] = jnp.zeros_like(sent[:, rows:])
+
+    split_sum(gram(turned[...], opposite[...]), kept, sent, slice(0, rows))
 
 
 def stats_kernel(z, out):
@@ -145,6 +164,21 @@
         here = slice(k * eighth, (k + 1) * eighth)
         out[pl.ds(pl.multiple_of(order[k] * eighth, eighth), eighth), :] = near[here, :]
         out[pl.ds(pl.multiple_of(order[4 + k] * eighth, eighth), eighth), :] = far[here, :]
+
+
+def push_kernel(middle, inner, beside, opposite, beside_square, opposite_square, out, over):
+    width = beside.shape[1]
+
+    @pl.when(middle[0] == 1)
+    def _():
+        for k in range(2):
+            here = slice(k * width // 2, (k + 1) * width // 2)
+            outward = dot(inner[...], opposite[:, here])
+            outward = outward - beside[:, here].astype(jnp.float32) * opposite_square[:, here]
+            out[:, here] = outward.astype(jnp.bfloat16)
+            across = dot_t(inner[...], beside[:, here])
+            across = across - opposite[:, here].astype(jnp.float32) * beside_square[:, here]
+            over[:, here] = across.astype(jnp.bfloat16)
 
 
 def coefficient(total):
@@ -170,23 +204,19 @@
         held[:, here] = plain + coefficient(total) * product
 
 
-def last_kernel(total, middle, inner, beside, opposite, own, held, mean, out, over, result):
-    rows, width = own.shape
-
-    def put(arrived, product_of):
+def last_kernel(total, middle, first, second, beside, opposite, held, out, over, result):
+    rows, width = beside.shape
+
+    def put(with_beside, arrived):
         for k in range(4):
             here = slice(k * width // 4, (k + 1) * width // 4)
-            block = (arrived[:, here].astype(jnp.float32) - mean[:, here]).astype(jnp.bfloat16)
-            wide = block.astype(jnp.float32)
-            square = jnp.sum(wide * wide, axis=0, keepdims=True)
-            product = dot(inner[:, :rows], beside[:, here])
-            product = product + dot(inner[:, rows:2 * rows], opposite[:, here])
-            product = product + product_of(inner[:, 2 * rows:], block)
-            product = product - own[:, here].astype(jnp.float32) * square
+            product = dot(with_beside, beside[:, here])
+            product = product + dot(second[:, :rows], opposite[:, here])
+            product = product + arrived[:, here].astype(jnp.float32)
             result[:, here] = held[:, here] + coefficient(total) * product
 
-    pl.when(middle[0] == 1)(lambda: put(over, dot_t))
-    pl.when(middle[0] == 0)(lambda: put(out, dot))
+    pl.when(middle[0] == 1)(lambda: put(second[:, rows:], over))
+    pl.when(middle[0] == 0)(lambda: put(first[...], out))
 
 
 def to_partner(x, step):
@@ -236,7 +266,7 @@
     all_stats = [stats] + [
         lax.ppermute(stats, "dp", [(i, (i + k) % 4) for i in range(4)]) for k in (1, 2, 3)
     ]
-    ahead = after(z_anchor, *all_stats)
+    ahead = after(z_anchor, stats)
     beside_in = lax.ppermute(ahead, "dp", [(i, i ^ 1) for i in range(4)])
     swapped = lax.ppermute(ahead, "dp", across)
     mean = (all_stats[0][:1] + all_stats[1][:1] + all_stats[2][:1] + all_stats[3][:1]) / 4
@@ -251,60 +281,32 @@
     own, turned, own_square, kept, sent = kernel_call(
         own_kernel, [block, block, flat, *summands(rows + NORM)], smem=1, scratch=12
     )(order, z_anchor, mean)
-    with_own = gather_cores(gather_chips(scatter(*halve(kept, sent, rows), last=rows)), order)
-
-    end = lax.ppermute(after(z_anchor, beside_in, swapped, with_own), "dp", [(0, 3), (3, 0)])
-
-    def first_of_middle(order, turned, beside_in, swapped, mean):
-        *blocks, kept, sent, _ = kernel_call(
-            middle_kernel, [block, flat, block, flat, *summands(3 * rows), block],
-            smem=1, scratch=12,
-        )(order, turned, beside_in, swapped, mean)
-        return *blocks, scatter(*halve(kept, sent))
-
-    def first_of_end(order, turned, beside_in, swapped, mean):
-        beside, square, kept, sent = kernel_call(
-            block_kernel, [block, flat, *summands(rows)], scratch=12
-        )(turned, beside_in, mean)
-        first = scatter(*halve(kept, sent))
-        first = jnp.concatenate([first, jnp.zeros((rows // 8, 2 * rows), first.dtype)], axis=1)
-        return beside, square, swapped, jnp.zeros_like(square), first
-
-    beside, beside_square, opposite, opposite_square, first = lax.cond(
-        middle[0] == 1, first_of_middle, first_of_end,
-        order, after(turned, with_own), beside_in, swapped, mean,
+    near_own = gather_chips(scatter(*halve(kept, sent, rows), last=rows))
+    end = lax.ppermute(after(z_anchor, beside_in, swapped, near_own), "dp", [(0, 3), (3, 0)])
+
+    beside, beside_square, swapped, swapped_square, kept, sent, _ = kernel_call(
+        first_kernel, [block, flat, block, flat, *summands(rows), block], smem=2, scratch=12
+    )(order, middle, after(turned, near_own), beside_in, swapped, mean)
+    with_own = gather_cores(near_own, order)
+    first = gather_cores(gather_chips(scatter(*halve(kept, sent))), order, end)
+    ready = kernel_call(push_kernel, [block, block], smem=1, scratch=12)(
+        middle, first, beside, swapped, beside_square, swapped_square
     )
-    handed = [lax.ppermute(first[:, 2 * rows:], "dp", p) for p in (outward, across)]
-    out = lax.ppermute(after(swapped, *handed), "dp", outward)
-    over = lax.ppermute(after(beside_in, *handed), "dp", across)
-    handed = handed[0] + handed[1]
+    pushed = [lax.ppermute(x, "dp", p) for x, p in zip(ready, (outward, across))]
+
+    opposite, opposite_square, kept, sent = kernel_call(
+        second_kernel, [block, flat, *summands(2 * rows)], smem=1, scratch=12
+    )(middle, after(turned, *ready), beside, swapped, swapped_square, end, mean)
+    halved = halve(kept, sent)
     result = ((rows, width), jnp.float32)
-
-    def hold(opposite_square):
-        return kernel_call(functools.partial(held_kernel, total), [result], scratch=12)(
-            with_own, own, z_anchor, z_other,
-            own_square, beside_square, opposite_square, mean, spread,
-        )[0]
-
-    def second_of_middle(turned, end, opposite, opposite_square, first, handed):
-        inner = jnp.concatenate([first[:, :2 * rows], handed], axis=1)
-        return opposite, gather_chips(inner), hold(opposite_square)
-
-    def second_of_end(turned, end, opposite, opposite_square, first, handed):
-        opposite, opposite_square, kept, sent = kernel_call(
-            block_kernel, [block, flat, *summands(rows)], scratch=12
-        )(turned, end, mean)
-        inner = scatter(*halve(kept, sent))
-        inner = jnp.concatenate([first[:, :rows], inner, handed], axis=1)
-        return opposite, gather_chips(inner), hold(opposite_square)
-
-    opposite, inner, held = lax.cond(
-        middle[0] == 1, second_of_middle, second_of_end,
-        turned, end, opposite, opposite_square, first, handed,
-    )
-    inner = gather_cores(inner, order, out, over)
+    held = kernel_call(functools.partial(held_kernel, total), [result], scratch=12)(
+        with_own, own, z_anchor, z_other,
+        own_square, beside_square, after(opposite_square, halved[0]), mean, spread,
+    )[0]
+    second = gather_chips(after(scatter(*halved), held))
+    second = gather_cores(after(second, *pushed), order)
     return kernel_call(functools.partial(last_kernel, total), [result], smem=1, scratch=12)(
-        middle, inner, beside, opposite, own, held, mean, out, over
+        middle, first, second, beside, opposite, held, *pushed
     )[0]
 
 

time: 102 us -> 93.5 us (0.917)
  waiting for transfers between devices: 42.1 us -> 30.8 us
  starting transfers between devices: 36.7 us -> 42 us
  local copies, waits for them, and re-layouts: 1.78 us -> 0.01 us
    ppermute x5 -> x3, waiting for transfers between devices: 15.8 us -> 0.01 us  [the longest x2 0.01 us: by_line(): lax.ppermute(x, 'dp', p)]
    ppermute x16 -> x24, starting transfers between devices: 18.2 us -> 29.9 us  [to_partner(): return lax.ppermute(x, 'feat', [(i, i ^ step) for i in range(8)])]
    ppermute x5 -> x3, starting transfers between devices: 9.86 us -> 5.27 us  [the longest x2 3.64 us: by_line(): lax.ppermute(x, 'dp', p)]
    ppermute x1, waiting for transfers between devices: 0.01 us -> 2.5 us  [by_line(): swapped = lax.ppermute(ahead, 'dp', across)]
    ppermute x1, waiting for transfers between devices: 0.01 us -> 2.32 us  [by_line(): beside_in = lax.ppermute(ahead, 'dp', [(i, i ^ 1) for i in range(4)])]
    slice x2 -> x0, local copies, waits for them, and re-layouts: 1.76 us -> none  [the longest x1 0.91 us: second_of_middle(): inner = jnp.concatenate([first[:, :2 * rows], handed], axis=1)]
    ppermute x1, starting transfers between devices: 3.66 us -> 1.91 us  [by_line(): swapped = lax.ppermute(ahead, 'dp', across)]
    pallas_call x11 -> x16, Pallas kernels: 19.2 us -> 18.9 us  [call(): pl.pallas_call(body, out_shape=[jax.ShapeDtypeStruct(s, t) for s, t in ou...]
  transfers between devices with their start and end apart: 26 -> 32, of which waited for: 18 -> 23; matrix products, arithmetic and copies ran while one was open for 3% -> 1% of each run, Pallas kernels for 12% -> 13%
where the time goes in v12:
time: 93.5 us; the launch traced here: 92.7 us
  starting transfers between devices  42 us (45%)
  waiting for transfers between devices  30.8 us (33%)
  Pallas kernels  18.9 us (20%)
    ppermute x24, starting transfers between devices, to_partner(): return lax.ppermute(x, 'feat', [(i, i ^ step) for i in range(8)])  29.9 us
    ppermute x24, waiting for transfers between devices, to_partner(): return lax.ppermute(x, 'feat', [(i, i ^ step) for i in range(8)])  26 us
    pallas_call x16, Pallas kernels, call(): pl.pallas_call(body, out_shape=[jax.ShapeDtypeStruct(s, t) for s, t in ou...  18.9 us
    ppermute x3, starting transfers between devices, by_line(): lax.ppermute(stats, 'dp', [(i, (i + k) % 4) for i in range(4)])  3.83 us
    ppermute x2, starting transfers between devices, by_line(): lax.ppermute(x, 'dp', p)  3.64 us
    ppermute x1, waiting for transfers between devices, by_line(): swapped = lax.ppermute(ahead, 'dp', across)  2.5 us
    ppermute x1, waiting for transfers between devices, by_line(): beside_in = lax.ppermute(ahead, 'dp', [(i, i ^ 1) for i in range(4)])  2.32 us
    ppermute x1, starting transfers between devices, by_line(): swapped = lax.ppermute(ahead, 'dp', across)  1.91 us
  transfers between devices with their start and end apart: 32, of which 23 were waited for; matrix products, arithmetic and copies ran while one was open for 1% of the time, Pallas kernels for 13%

profile of v12, /device:TPU:9, one launch (start us, length us, event | category | flops | bytes accessed | tf_op | source)
XLA Modules:
  0.0 92.7 jit_solution(335141062591584915)
XLA Ops:
  0.0 1.8 %shard_map.37 = f32[2,1024]{1,0:T(2,128)S(1)} custom-call(bf16[512,1024]{1,0:T(8,128)(2,1)} %z.5), custom_call_target="tpu_custom_call" | custom-call | tf_op jit(solution)/shard_map/pallas_call | solution.py:17
  1.8 1.3 %collective-permute-start = (f32[2,1024]{1,0:T(2,128)S(1)}, f32[2,1024]{1,0:T(2,128)S(1)}, u32[]{:S(2)}, u32[]{:S(2)}) collective-permute-start(f32[2,1024]{1,0:T(2,128)S(1)} %shard_map.37), channel_id=1, source_target_pairs={{0,8},{8,16},{16,24},{24,0},{1,9},{9,17},{17,25},{25,1},{2,10},{10... | collective-permute-start | bytes 24584 | tf_op jit(solution)/shard_map/ppermute | solution.py:267
  4.3 1.4 %collective-permute-start.2 = (f32[2,1024]{1,0:T(2,128)S(1)}, f32[2,1024]{1,0:T(2,128)S(1)}, u32[]{:S(2)}, u32[]{:S(2)}) collective-permute-start(f32[2,1024]{1,0:T(2,128)S(1)} %shard_map.37), channel_id=1, source_target_pairs={{0,24},{8,0},{16,8},{24,16},{1,25},{9,1},{17,9},{25,17},{2,26},{10... | collective-permute-start | bytes 24584 | tf_op jit(solution)/shard_map/ppermute | solution.py:267
  6.7 1.9 %collective-permute-start.11 = (bf16[512,1024]{1,0:T(8,128)(2,1)}, bf16[512,1024]{1,0:T(8,128)(2,1)}, u32[]{:S(2)}, u32[]{:S(2)}) collective-permute-start(bf16[512,1024]{1,0:T(8,128)(2,1)} %z.5), channel_id=1, source_target_pairs={{8,16},{16,8},{9,17},{17,9},{10,18},{18,10},{11,19},{19,11},{12,20... | collective-permute-start | bytes 3145736 | tf_op jit(solution)/shard_map/ppermute | solution.py:271
  9.4 2.4 %shard_map.38 = (bf16[512,1024]{1,0:T(8,128)(2,1)S(1)}, bf16[512,1024]{1,0:T(8,128)(2,1)S(1)}, f32[1,1024]{1,0:T(1,128)S(1)}, f32[256,640]{1,0:T(8,128)S(1)}, bf16[256,640]{1,0:T(8,128)(2,1)S(1)}) custom-call(s32[8]{0:T(128)S(1)} %broadcast_xor_fusion.order, bf16[512,1024]{1,0:T(8,128)(2,1)} %z.5, f32[1,1024]{1,0:T(1,128)S(1)} %get-tuple-element.80.mean), custom_call_target="tpu_custom_call" | custom-call | tf_op jit(solution)/shard_map/pallas_call | solution.py:17
  11.7 1.9 %collective-permute-start.3 = (bf16[256,640]{1,0:T(8,128)(2,1)S(1)}, bf16[256,640]{1,0:T(8,128)(2,1)S(1)}, u32[]{:S(2)}, u32[]{:S(2)}) collective-permute-start(bf16[256,640]{1,0:T(8,128)(2,1)S(1)} %get-tuple-element.44), channel_id=1, source_target_pairs={{0,1},{1,0},{2,3},{3,2},{4,5},{5,4},{6,7},{7,6},{8,9},{9,8},{10,11... | collective-permute-start | bytes 983048 | tf_op jit(solution)/shard_map/ppermute | solution.py:223
  15.0 1.3 %collective-permute-start.4 = (bf16[64,640]{1,0:T(8,128)(2,1)S(1)}, bf16[64,640]{1,0:T(8,128)(2,1)S(1)}, u32[]{:S(2)}, u32[]{:S(2)}) collective-permute-start(bf16[64,640]{1,0:T(8,128)(2,1)S(1)} %get-tuple-element.46), channel_id=1, source_target_pairs={{0,2},{1,3},{2,0},{3,1},{4,6},{5,7},{6,4},{7,5},{8,10},{9,11},{10,... | collective-permute-start | bytes 245768 | tf_op jit(solution)/shard_map/ppermute | solution.py:223
  19.9 1.7 %collective-permute-done.6.c = bf16[64,640]{1,0:T(8,128)(2,1)S(1)} collective-permute-done((bf16[64,640]{1,0:T(8,128)(2,1)S(1)}, bf16[64,640]{1,0:T(8,128)(2,1)S(1)}, u32[]{:S(2)}, u32[]{:S(2)}) %collective-permute-start.6) | collective-permute-done | bytes 81952 | tf_op jit(solution)/shard_map/ppermute | solution.py:223
  22.7 1.8 %collective-permute-start.9 = (bf16[64,640]{1,0:T(8,128)(2,1)S(1)}, bf16[64,640]{1,0:T(8,128)(2,1)S(1)}, u32[]{:S(2)}, u32[]{:S(2)}) collective-permute-start(bf16[64,640]{1,0:T(8,128)(2,1)S(1)} %shard_map.40), channel_id=1, source_target_pairs={{0,6},{1,7},{2,4},{3,5},{4,2},{5,3},{6,0},{7,1},{8,14},{9,15},{10,... | collective-permute-start | bytes 245768 | tf_op jit(solution)/shard_map/ppermute | solution.py:223
  27.0 2.3 %collective-permute-done.10.beside_in = bf16[512,1024]{1,0:T(8,128)(2,1)S(1)} collective-permute-done((bf16[512,1024]{1,0:T(8,128)(2,1)}, bf16[512,1024]{1,0:T(8,128)(2,1)S(1)}, u32[]{:S(2)}, u32[]{:S(2)}) %collective-permute-start.10) | collective-permute-done | bytes 1048608 | tf_op jit(solution)/shard_map/ppermute | solution.py:270
  29.3 2.5 %collective-permute-done.11.opposite_in = bf16[512,1024]{1,0:T(8,128)(2,1)} collective-permute-done((bf16[512,1024]{1,0:T(8,128)(2,1)}, bf16[512,1024]{1,0:T(8,128)(2,1)}, u32[]{:S(2)}, u32[]{:S(2)}) %collective-permute-start.11) | collective-permute-done | bytes 1048608 | tf_op jit(solution)/shard_map/ppermute | solution.py:271
  31.8 1.6 %collective-permute-start.20 = (bf16[512,1024]{1,0:T(8,128)(2,1)}, bf16[512,1024]{1,0:T(8,128)(2,1)}, u32[]{:S(2)}, u32[]{:S(2)}) collective-permute-start(bf16[512,1024]{1,0:T(8,128)(2,1)} %z.5), channel_id=1, source_target_pairs={{0,24},{24,0},{1,25},{25,1},{2,26},{26,2},{3,27},{27,3},{4,28},{28... | collective-permute-start | bytes 3145736 | tf_op jit(solution)/shard_map/ppermute | solution.py:285
  33.4 3.2 %shard_map.41 = (bf16[512,1024]{1,0:T(8,128)(2,1)S(1)}, f32[1,1024]{1,0:T(1,128)S(1)}, bf16[512,1024]{1,0:T(8,128)(2,1)S(1)}, f32[1,1024]{1,0:T(1,128)S(1)}, f32...) custom-call(s32[8]{0:T(128)S(1)} %broadcast_xor_fusion.order, s32[1]{0:T(128)} %bitcast.middle, ...), custom_call_target="tpu_custom_call" | custom-call | tf_op jit(solution)/shard_map/pallas_call | solution.py:17
  36.6 2.7 %collective-permute-start.12 = (bf16[256,512]{1,0:T(8,128)(2,1)S(1)}, bf16[256,512]{1,0:T(8,128)(2,1)S(1)}, u32[]{:S(2)}, u32[]{:S(2)}) collective-permute-start(bf16[256,512]{1,0:T(8,128)(2,1)S(1)} %get-tuple-element.52), channel_id=1, source_target_pairs={{0,1},{1,0},{2,3},{3,2},{4,5},{5,4},{6,7},{7,6},{8,9},{9,8},{10,11... | collective-permute-start | bytes 786440 | tf_op jit(solution)/shard_map/ppermute | solution.py:223
  40.5 1.3 %collective-permute-start.13 = (bf16[64,512]{1,0:T(8,128)(2,1)S(1)}, bf16[64,512]{1,0:T(8,128)(2,1)S(1)}, u32[]{:S(2)}, u32[]{:S(2)}) collective-permute-start(bf16[64,512]{1,0:T(8,128)(2,1)S(1)} %get-tuple-element.54), channel_id=1, source_target_pairs={{0,2},{1,3},{2,0},{3,1},{4,6},{5,7},{6,4},{7,5},{8,10},{9,11},{10,... | collective-permute-start | bytes 196616 | tf_op jit(solution)/shard_map/ppermute | solution.py:223
  44.9 2.1 %collective-permute-done.15.c = bf16[64,512]{1,0:T(8,128)(2,1)S(1)} collective-permute-done((bf16[64,512]{1,0:T(8,128)(2,1)S(1)}, bf16[64,512]{1,0:T(8,128)(2,1)S(1)}, u32[]{:S(2)}, u32[]{:S(2)}) %collective-permute-start.15) | collective-permute-done | bytes 65568 | tf_op jit(solution)/shard_map/ppermute | solution.py:223
  47.8 2.0 %collective-permute-start.18 = (bf16[64,512]{1,0:T(8,128)(2,1)S(1)}, bf16[64,512]{1,0:T(8,128)(2,1)S(1)}, u32[]{:S(2)}, u32[]{:S(2)}) collective-permute-start(bf16[64,512]{1,0:T(8,128)(2,1)S(1)} %shard_map.43), channel_id=1, source_target_pairs={{0,6},{1,7},{2,4},{3,5},{4,2},{5,3},{6,0},{7,1},{8,14},{9,15},{10,... | collective-permute-start | bytes 196616 | tf_op jit(solution)/shard_map/ppermute | solution.py:223
  51.9 3.7 %collective-permute-start.19 = (bf16[256,512]{1,0:T(8,128)(2,1)S(1)}, bf16[256,512]{1,0:T(8,128)(2,1)S(1)}, u32[]{:S(2)}, u32[]{:S(2)}) collective-permute-start(bf16[256,512]{1,0:T(8,128)(2,1)S(1)} %pad_maximum_fusion.2.near), channel_id=1, source_target_pairs={{0,1},{1,0},{2,3},{3,2},{4,5},{5,4},{6,7},{7,6},{8,9},{9,8},{10,11... | collective-permute-start | bytes 786440 | tf_op jit(solution)/shard_map/ppermute | solution.py:223
  58.6 1.4 %collective-permute-start.29 = (bf16[512,1024]{1,0:T(8,128)(2,1)S(1)}, bf16[512,1024]{1,0:T(8,128)(2,1)S(1)}, u32[]{:S(2)}, u32[]{:S(2)}) collective-permute-start(bf16[512,1024]{1,0:T(8,128)(2,1)S(1)} %get-tuple-element.63), channel_id=1, source_target_pairs={{8,0},{16,24},{9,1},{17,25},{10,2},{18,26},{11,3},{19,27},{12,4},{... | collective-permute-start | bytes 3145736 | tf_op jit(solution)/shard_map/ppermute | solution.py:295
  59.9 2.3 %collective-permute-start.30 = (bf16[512,1024]{1,0:T(8,128)(2,1)S(1)}, bf16[512,1024]{1,0:T(8,128)(2,1)S(1)}, u32[]{:S(2)}, u32[]{:S(2)}) collective-permute-start(bf16[512,1024]{1,0:T(8,128)(2,1)S(1)} %get-tuple-element.64), channel_id=1, source_target_pairs={{8,16},{16,8},{9,17},{17,9},{10,18},{18,10},{11,19},{19,11},{12,20... | collective-permute-start | bytes 3145736 | tf_op jit(solution)/shard_map/ppermute | solution.py:295
  62.2 2.8 %shard_map.46 = (bf16[512,1024]{1,0:T(8,128)(2,1)S(1)}, f32[1,1024]{1,0:T(1,128)S(1)}, f32[256,1024]{1,0:T(8,128)S(1)}, bf16[256,1024]{1,0:T(8,128)(2,1)S(1)}) custom-call(s32[1]{0:T(128)} %bitcast.middle, bf16[512,1024]{1,0:T(8,128)(2,1)S(1)} %get-tuple-element.65.turned, bf16[512,1024]{1,0:T(8,128)(2,1)S(1)} %get-tuple-element.59.beside, ...), custom_call_target="tpu_custom_call" | custom-call | tf_op jit(solution)/shard_map/pallas_call | solution.py:17
  65.1 2.4 %collective-permute-start.21 = (bf16[256,1024]{1,0:T(8,128)(2,1)S(1)}, bf16[256,1024]{1,0:T(8,128)(2,1)S(1)}, u32[]{:S(2)}, u32[]{:S(2)}) collective-permute-start(bf16[256,1024]{1,0:T(8,128)(2,1)S(1)} %get-tuple-element.67), channel_id=1, source_target_pairs={{0,1},{1,0},{2,3},{3,2},{4,5},{5,4},{6,7},{7,6},{8,9},{9,8},{10,11... | collective-permute-start | bytes 1572872 | tf_op jit(solution)/shard_map/ppermute | solution.py:223
  67.6 1.5 %collective-permute-done.21.got = bf16[256,1024]{1,0:T(8,128)(2,1)S(1)} collective-permute-done((bf16[256,1024]{1,0:T(8,128)(2,1)S(1)}, bf16[256,1024]{1,0:T(8,128)(2,1)S(1)}, u32[]{:S(2)}, u32[]{:S(2)}) %collective-permute-start.21) | collective-permute-done | bytes 524320 | tf_op jit(solution)/shard_map/ppermute | solution.py:223
  69.1 1.3 %collective-permute-start.22 = (bf16[64,1024]{1,0:T(8,128)(2,1)S(1)}, bf16[64,1024]{1,0:T(8,128)(2,1)S(1)}, u32[]{:S(2)}, u32[]{:S(2)}) collective-permute-start(bf16[64,1024]{1,0:T(8,128)(2,1)S(1)} %get-tuple-element.69), channel_id=1, source_target_pairs={{0,2},{1,3},{2,0},{3,1},{4,6},{5,7},{6,4},{7,5},{8,10},{9,11},{10,... | collective-permute-start | bytes 393224 | tf_op jit(solution)/shard_map/ppermute | solution.py:223
  72.5 2.5 %shard_map.50.held = f32[512,1024]{1,0:T(8,128)S(1)} custom-call(bf16[512,640]{1,0:T(8,128)(2,1)S(1)} %shard_map.49.with_own, bf16[512,1024]{1,0:T(8,128)(2,1)S(1)} %get-tuple-element.72.own, bf16[512,1024]{1,0:T(8,128)(2,1)} %z.5, bf16[512,1024]{1,0:T(8,128)(2,1)S(1)} %copy-done, f32[1,1024]{1,0:T(1,128)S(1)} %get-tuple-element.73.own_square, ...), custom_call_target="tpu_custom_call" | custom-call | tf_op jit(solution)/shard_map/pallas_call | solution.py:17
  75.0 2.5 %collective-permute-done.24.c = bf16[64,1024]{1,0:T(8,128)(2,1)S(1)} collective-permute-done((bf16[64,1024]{1,0:T(8,128)(2,1)S(1)}, bf16[64,1024]{1,0:T(8,128)(2,1)S(1)}, u32[]{:S(2)}, u32[]{:S(2)}) %collective-permute-start.24) | collective-permute-done | bytes 131104 | tf_op jit(solution)/shard_map/ppermute | solution.py:223
  77.6 1.5 %collective-permute-start.26 = (bf16[64,1024]{1,0:T(8,128)(2,1)S(1)}, bf16[64,1024]{1,0:T(8,128)(2,1)S(1)}, u32[]{:S(2)}, u32[]{:S(2)}) collective-permute-start(bf16[64,1024]{1,0:T(8,128)(2,1)S(1)} %shard_map.48), channel_id=1, source_target_pairs={{0,2},{1,3},{2,0},{3,1},{4,6},{5,7},{6,4},{7,5},{8,10},{9,11},{10,... | collective-permute-start | bytes 393224 | tf_op jit(solution)/shard_map/ppermute | solution.py:223
  80.3 1.4 %collective-permute-done.26 = bf16[64,1024]{1,0:T(8,128)(2,1)S(1)} collective-permute-done((bf16[64,1024]{1,0:T(8,128)(2,1)S(1)}, bf16[64,1024]{1,0:T(8,128)(2,1)S(1)}, u32[]{:S(2)}, u32[]{:S(2)}) %collective-permute-start.26) | collective-permute-done | bytes 131104 | tf_op jit(solution)/shard_map/ppermute | solution.py:223
  81.7 2.1 %collective-permute-done.27 = bf16[64,1024]{1,0:T(8,128)(2,1)S(1)} collective-permute-done((bf16[64,1024]{1,0:T(8,128)(2,1)S(1)}, bf16[64,1024]{1,0:T(8,128)(2,1)S(1)}, u32[]{:S(2)}, u32[]{:S(2)}) %collective-permute-start.27) | collective-permute-done | bytes 131104 | tf_op jit(solution)/shard_map/ppermute | solution.py:223
  85.0 2.8 %collective-permute-start.31 = (bf16[256,1024]{1,0:T(8,128)(2,1)S(1)}, bf16[256,1024]{1,0:T(8,128)(2,1)S(1)}, u32[]{:S(2)}, u32[]{:S(2)}) collective-permute-start(bf16[256,1024]{1,0:T(8,128)(2,1)S(1)} %pad_maximum_fusion.near), channel_id=1, source_target_pairs={{0,1},{1,0},{2,3},{3,2},{4,5},{5,4},{6,7},{7,6},{8,9},{9,8},{10,11... | collective-permute-start | bytes 1572872 | tf_op jit(solution)/shard_map/ppermute | solution.py:223
  87.9 1.5 %collective-permute-done.31.far = bf16[256,1024]{1,0:T(8,128)(2,1)S(1)} collective-permute-done((bf16[256,1024]{1,0:T(8,128)(2,1)S(1)}, bf16[256,1024]{1,0:T(8,128)(2,1)S(1)}, u32[]{:S(2)}, u32[]{:S(2)}) %collective-permute-start.31) | collective-permute-done | bytes 524320 | tf_op jit(solution)/shard_map/ppermute | solution.py:223
  90.0 2.6 %shard_map.52 = f32[512,1024]{1,0:T(8,128)} custom-call(s32[1]{0:T(128)} %bitcast.middle, bf16[512,512]{1,0:T(8,128)(2,1)S(1)} %shard_map.44.inner.first, bf16[512,1024]{1,0:T(8,128)(2,1)S(1)} %shard_map.51.second, bf16[512,1024]{1,0:T(8,128)(2,1)S(1)} %get-tuple-element.59.beside, bf16[512,1024]{1,0:T(8,128)(2,1)S(1)} %get-tuple-element.78.opposite, ...), custom_call_target="tpu_custom_call" | custom-call | tf_op jit(solution)/shard_map/pallas_call | solution.py:17
  (55 shorter events, 26.9 us)
Async XLA Ops:
  1.8 7.5 %collective-permute-start = (f32[2,1024]{1,0:T(2,128)S(1)}, f32[2,1024]{1,0:T(2,128)S(1)}, u32[]{:S(2)}, u32[]{:S(2)}) collective-permute-start(f32[2,1024]{1,0:T(2,128)S(1)} %shard_map.37), channel_id=1, source_target_pairs={{0,8},{8,16},{16,24},{24,0},{1,9},{9,17},{17,25},{25,1},{2,10},{10... | collective-permute-start | bytes 24584 | tf_op jit(solution)/shard_map/ppermute | solution.py:267
  3.2 6.1 %collective-permute-start.1 = (f32[2,1024]{1,0:T(2,128)S(1)}, f32[2,1024]{1,0:T(2,128)S(1)}, u32[]{:S(2)}, u32[]{:S(2)}) collective-permute-start(f32[2,1024]{1,0:T(2,128)S(1)} %shard_map.37), channel_id=1, source_target_pairs={{0,16},{8,24},{16,0},{24,8},{1,17},{9,25},{17,1},{25,9},{2,18},{10... | collective-permute-start | bytes 24584 | tf_op jit(solution)/shard_map/ppermute | solution.py:267
  4.3 5.1 %collective-permute-start.2 = (f32[2,1024]{1,0:T(2,128)S(1)}, f32[2,1024]{1,0:T(2,128)S(1)}, u32[]{:S(2)}, u32[]{:S(2)}) collective-permute-start(f32[2,1024]{1,0:T(2,128)S(1)} %shard_map.37), channel_id=1, source_target_pairs={{0,24},{8,0},{16,8},{24,16},{1,25},{9,1},{17,9},{25,17},{2,26},{10... | collective-permute-start | bytes 24584 | tf_op jit(solution)/shard_map/ppermute | solution.py:267
  5.6 23.6 %collective-permute-start.10 = (bf16[512,1024]{1,0:T(8,128)(2,1)}, bf16[512,1024]{1,0:T(8,128)(2,1)S(1)}, u32[]{:S(2)}, u32[]{:S(2)}) collective-permute-start(bf16[512,1024]{1,0:T(8,128)(2,1)} %z.5), channel_id=1, source_target_pairs={{0,8},{8,0},{16,24},{24,16},{1,9},{9,1},{17,25},{25,17},{2,10},{10... | collective-permute-start | bytes 3145736 | tf_op jit(solution)/shard_map/ppermute | solution.py:270
  6.7 25.1 %collective-permute-start.11 = (bf16[512,1024]{1,0:T(8,128)(2,1)}, bf16[512,1024]{1,0:T(8,128)(2,1)}, u32[]{:S(2)}, u32[]{:S(2)}) collective-permute-start(bf16[512,1024]{1,0:T(8,128)(2,1)} %z.5), channel_id=1, source_target_pairs={{8,16},{16,8},{9,17},{17,9},{10,18},{18,10},{11,19},{19,11},{12,20... | collective-permute-start | bytes 3145736 | tf_op jit(solution)/shard_map/ppermute | solution.py:271
  11.7 3.1 %collective-permute-start.3 = (bf16[256,640]{1,0:T(8,128)(2,1)S(1)}, bf16[256,640]{1,0:T(8,128)(2,1)S(1)}, u32[]{:S(2)}, u32[]{:S(2)}) collective-permute-start(bf16[256,640]{1,0:T(8,128)(2,1)S(1)} %get-tuple-element.44), channel_id=1, source_target_pairs={{0,1},{1,0},{2,3},{3,2},{4,5},{5,4},{6,7},{7,6},{8,9},{9,8},{10,11... | collective-permute-start | bytes 983048 | tf_op jit(solution)/shard_map/ppermute | solution.py:223
  15.0 3.8 %collective-permute-start.4 = (bf16[64,640]{1,0:T(8,128)(2,1)S(1)}, bf16[64,640]{1,0:T(8,128)(2,1)S(1)}, u32[]{:S(2)}, u32[]{:S(2)}) collective-permute-start(bf16[64,640]{1,0:T(8,128)(2,1)S(1)} %get-tuple-element.46), channel_id=1, source_target_pairs={{0,2},{1,3},{2,0},{3,1},{4,6},{5,7},{6,4},{7,5},{8,10},{9,11},{10,... | collective-permute-start | bytes 245768 | tf_op jit(solution)/shard_map/ppermute | solution.py:223
  16.3 3.7 %collective-permute-start.5 = (bf16[64,640]{1,0:T(8,128)(2,1)S(1)}, bf16[64,640]{1,0:T(8,128)(2,1)S(1)}, u32[]{:S(2)}, u32[]{:S(2)}) collective-permute-start(bf16[64,640]{1,0:T(8,128)(2,1)S(1)} %get-tuple-element.47), channel_id=1, source_target_pairs={{0,4},{1,5},{2,6},{3,7},{4,0},{5,1},{6,2},{7,3},{8,12},{9,13},{10,... | collective-permute-start | bytes 245768 | tf_op jit(solution)/shard_map/ppermute | solution.py:223
  17.5 4.2 %collective-permute-start.6 = (bf16[64,640]{1,0:T(8,128)(2,1)S(1)}, bf16[64,640]{1,0:T(8,128)(2,1)S(1)}, u32[]{:S(2)}, u32[]{:S(2)}) collective-permute-start(bf16[64,640]{1,0:T(8,128)(2,1)S(1)} %get-tuple-element.48), channel_id=1, source_target_pairs={{0,6},{1,7},{2,4},{3,5},{4,2},{5,3},{6,0},{7,1},{8,14},{9,15},{10,... | collective-permute-start | bytes 245768 | tf_op jit(solution)/shard_map/ppermute | solution.py:223
  21.8 3.8 %collective-permute-start.7 = (bf16[64,640]{1,0:T(8,128)(2,1)S(1)}, bf16[64,640]{1,0:T(8,128)(2,1)S(1)}, u32[]{:S(2)}, u32[]{:S(2)}) collective-permute-start(bf16[64,640]{1,0:T(8,128)(2,1)S(1)} %shard_map.40), channel_id=1, source_target_pairs={{0,2},{1,3},{2,0},{3,1},{4,6},{5,7},{6,4},{7,5},{8,10},{9,11},{10,... | collective-permute-start | bytes 245768 | tf_op jit(solution)/shard_map/ppermute | solution.py:223
  22.4 3.7 %collective-permute-start.8 = (bf16[64,640]{1,0:T(8,128)(2,1)S(1)}, bf16[64,640]{1,0:T(8,128)(2,1)S(1)}, u32[]{:S(2)}, u32[]{:S(2)}) collective-permute-start(bf16[64,640]{1,0:T(8,128)(2,1)S(1)} %shard_map.40), channel_id=1, source_target_pairs={{0,4},{1,5},{2,6},{3,7},{4,0},{5,1},{6,2},{7,3},{8,12},{9,13},{10,... | collective-permute-start | bytes 245768 | tf_op jit(solution)/shard_map/ppermute | solution.py:223
  22.7 4.2 %collective-permute-start.9 = (bf16[64,640]{1,0:T(8,128)(2,1)S(1)}, bf16[64,640]{1,0:T(8,128)(2,1)S(1)}, u32[]{:S(2)}, u32[]{:S(2)}) collective-permute-start(bf16[64,640]{1,0:T(8,128)(2,1)S(1)} %shard_map.40), channel_id=1, source_target_pairs={{0,6},{1,7},{2,4},{3,5},{4,2},{5,3},{6,0},{7,1},{8,14},{9,15},{10,... | collective-permute-start | bytes 245768 | tf_op jit(solution)/shard_map/ppermute | solution.py:223
  31.8 25.0 %collective-permute-start.20 = (bf16[512,1024]{1,0:T(8,128)(2,1)}, bf16[512,1024]{1,0:T(8,128)(2,1)}, u32[]{:S(2)}, u32[]{:S(2)}) collective-permute-start(bf16[512,1024]{1,0:T(8,128)(2,1)} %z.5), channel_id=1, source_target_pairs={{0,24},{24,0},{1,25},{25,1},{2,26},{26,2},{3,27},{27,3},{4,28},{28... | collective-permute-start | bytes 3145736 | tf_op jit(solution)/shard_map/ppermute | solution.py:285
  36.6 3.9 %collective-permute-start.12 = (bf16[256,512]{1,0:T(8,128)(2,1)S(1)}, bf16[256,512]{1,0:T(8,128)(2,1)S(1)}, u32[]{:S(2)}, u32[]{:S(2)}) collective-permute-start(bf16[256,512]{1,0:T(8,128)(2,1)S(1)} %get-tuple-element.52), channel_id=1, source_target_pairs={{0,1},{1,0},{2,3},{3,2},{4,5},{5,4},{6,7},{7,6},{8,9},{9,8},{10,11... | collective-permute-start | bytes 786440 | tf_op jit(solution)/shard_map/ppermute | solution.py:223
  40.5 3.2 %collective-permute-start.13 = (bf16[64,512]{1,0:T(8,128)(2,1)S(1)}, bf16[64,512]{1,0:T(8,128)(2,1)S(1)}, u32[]{:S(2)}, u32[]{:S(2)}) collective-permute-start(bf16[64,512]{1,0:T(8,128)(2,1)S(1)} %get-tuple-element.54), channel_id=1, source_target_pairs={{0,2},{1,3},{2,0},{3,1},{4,6},{5,7},{6,4},{7,5},{8,10},{9,11},{10,... | collective-permute-start | bytes 196616 | tf_op jit(solution)/shard_map/ppermute | solution.py:223
  41.8 3.1 %collective-permute-start.14 = (bf16[64,512]{1,0:T(8,128)(2,1)S(1)}, bf16[64,512]{1,0:T(8,128)(2,1)S(1)}, u32[]{:S(2)}, u32[]{:S(2)}) collective-permute-start(bf16[64,512]{1,0:T(8,128)(2,1)S(1)} %get-tuple-element.55), channel_id=1, source_target_pairs={{0,4},{1,5},{2,6},{3,7},{4,0},{5,1},{6,2},{7,3},{8,12},{9,13},{10,... | collective-permute-start | bytes 196616 | tf_op jit(solution)/shard_map/ppermute | solution.py:223
  43.1 4.0 %collective-permute-start.15 = (bf16[64,512]{1,0:T(8,128)(2,1)S(1)}, bf16[64,512]{1,0:T(8,128)(2,1)S(1)}, u32[]{:S(2)}, u32[]{:S(2)}) collective-permute-start(bf16[64,512]{1,0:T(8,128)(2,1)S(1)} %get-tuple-element.56), channel_id=1, source_target_pairs={{0,6},{1,7},{2,4},{3,5},{4,2},{5,3},{6,0},{7,1},{8,14},{9,15},{10,... | collective-permute-start | bytes 196616 | tf_op jit(solution)/shard_map/ppermute | solution.py:223
  47.1 3.2 %collective-permute-start.16 = (bf16[64,512]{1,0:T(8,128)(2,1)S(1)}, bf16[64,512]{1,0:T(8,128)(2,1)S(1)}, u32[]{:S(2)}, u32[]{:S(2)}) collective-permute-start(bf16[64,512]{1,0:T(8,128)(2,1)S(1)} %shard_map.43), channel_id=1, source_target_pairs={{0,2},{1,3},{2,0},{3,1},{4,6},{5,7},{6,4},{7,5},{8,10},{9,11},{10,... | collective-permute-start | bytes 196616 | tf_op jit(solution)/shard_map/ppermute | solution.py:223
  47.5 3.1 %collective-permute-start.17 = (bf16[64,512]{1,0:T(8,128)(2,1)S(1)}, bf16[64,512]{1,0:T(8,128)(2,1)S(1)}, u32[]{:S(2)}, u32[]{:S(2)}) collective-permute-start(bf16[64,512]{1,0:T(8,128)(2,1)S(1)} %shard_map.43), channel_id=1, source_target_pairs={{0,4},{1,5},{2,6},{3,7},{4,0},{5,1},{6,2},{7,3},{8,12},{9,13},{10,... | collective-permute-start | bytes 196616 | tf_op jit(solution)/shard_map/ppermute | solution.py:223
  47.8 4.0 %collective-permute-start.18 = (bf16[64,512]{1,0:T(8,128)(2,1)S(1)}, bf16[64,512]{1,0:T(8,128)(2,1)S(1)}, u32[]{:S(2)}, u32[]{:S(2)}) collective-permute-start(bf16[64,512]{1,0:T(8,128)(2,1)S(1)} %shard_map.43), channel_id=1, source_target_pairs={{0,6},{1,7},{2,4},{3,5},{4,2},{5,3},{6,0},{7,1},{8,14},{9,15},{10,... | collective-permute-start | bytes 196616 | tf_op jit(solution)/shard_map/ppermute | solution.py:223
  51.9 4.9 %collective-permute-start.19 = (bf16[256,512]{1,0:T(8,128)(2,1)S(1)}, bf16[256,512]{1,0:T(8,128)(2,1)S(1)}, u32[]{:S(2)}, u32[]{:S(2)}) collective-permute-start(bf16[256,512]{1,0:T(8,128)(2,1)S(1)} %pad_maximum_fusion.2.near), channel_id=1, source_target_pairs={{0,1},{1,0},{2,3},{3,2},{4,5},{5,4},{6,7},{7,6},{8,9},{9,8},{10,11... | collective-permute-start | bytes 786440 | tf_op jit(solution)/shard_map/ppermute | solution.py:223
  58.6 26.4 %collective-permute-start.29 = (bf16[512,1024]{1,0:T(8,128)(2,1)S(1)}, bf16[512,1024]{1,0:T(8,128)(2,1)S(1)}, u32[]{:S(2)}, u32[]{:S(2)}) collective-permute-start(bf16[512,1024]{1,0:T(8,128)(2,1)S(1)} %get-tuple-element.63), channel_id=1, source_target_pairs={{8,0},{16,24},{9,1},{17,25},{10,2},{18,26},{11,3},{19,27},{12,4},{... | collective-permute-start | bytes 3145736 | tf_op jit(solution)/shard_map/ppermute | solution.py:295
  59.9 25.1 %collective-permute-start.30 = (bf16[512,1024]{1,0:T(8,128)(2,1)S(1)}, bf16[512,1024]{1,0:T(8,128)(2,1)S(1)}, u32[]{:S(2)}, u32[]{:S(2)}) collective-permute-start(bf16[512,1024]{1,0:T(8,128)(2,1)S(1)} %get-tuple-element.64), channel_id=1, source_target_pairs={{8,16},{16,8},{9,17},{17,9},{10,18},{18,10},{11,19},{19,11},{12,20... | collective-permute-start | bytes 3145736 | tf_op jit(solution)/shard_map/ppermute | solution.py:295
  65.1 4.0 %collective-permute-start.21 = (bf16[256,1024]{1,0:T(8,128)(2,1)S(1)}, bf16[256,1024]{1,0:T(8,128)(2,1)S(1)}, u32[]{:S(2)}, u32[]{:S(2)}) collective-permute-start(bf16[256,1024]{1,0:T(8,128)(2,1)S(1)} %get-tuple-element.67), channel_id=1, source_target_pairs={{0,1},{1,0},{2,3},{3,2},{4,5},{5,4},{6,7},{7,6},{8,9},{9,8},{10,11... | collective-permute-start | bytes 1572872 | tf_op jit(solution)/shard_map/ppermute | solution.py:223
  67.5 4.2 %collective-permute-start.25 = (bf16[256,640]{1,0:T(8,128)(2,1)S(1)}, bf16[256,640]{1,0:T(8,128)(2,1)S(1)}, u32[]{:S(2)}, u32[]{:S(2)}) collective-permute-start(bf16[256,640]{1,0:T(8,128)(2,1)S(1)} %pad_maximum_fusion.1.near), channel_id=1, source_target_pairs={{0,1},{1,0},{2,3},{3,2},{4,5},{5,4},{6,7},{7,6},{8,9},{9,8},{10,11... | collective-permute-start | bytes 983048 | tf_op jit(solution)/shard_map/ppermute | solution.py:223
  69.1 5.9 %collective-permute-start.22 = (bf16[64,1024]{1,0:T(8,128)(2,1)S(1)}, bf16[64,1024]{1,0:T(8,128)(2,1)S(1)}, u32[]{:S(2)}, u32[]{:S(2)}) collective-permute-start(bf16[64,1024]{1,0:T(8,128)(2,1)S(1)} %get-tuple-element.69), channel_id=1, source_target_pairs={{0,2},{1,3},{2,0},{3,1},{4,6},{5,7},{6,4},{7,5},{8,10},{9,11},{10,... | collective-permute-start | bytes 393224 | tf_op jit(solution)/shard_map/ppermute | solution.py:223
  70.4 4.6 %collective-permute-start.23 = (bf16[64,1024]{1,0:T(8,128)(2,1)S(1)}, bf16[64,1024]{1,0:T(8,128)(2,1)S(1)}, u32[]{:S(2)}, u32[]{:S(2)}) collective-permute-start(bf16[64,1024]{1,0:T(8,128)(2,1)S(1)} %get-tuple-element.70), channel_id=1, source_target_pairs={{0,4},{1,5},{2,6},{3,7},{4,0},{5,1},{6,2},{7,3},{8,12},{9,13},{10,... | collective-permute-start | bytes 393224 | tf_op jit(solution)/shard_map/ppermute | solution.py:223
  71.7 5.8 %collective-permute-start.24 = (bf16[64,1024]{1,0:T(8,128)(2,1)S(1)}, bf16[64,1024]{1,0:T(8,128)(2,1)S(1)}, u32[]{:S(2)}, u32[]{:S(2)}) collective-permute-start(bf16[64,1024]{1,0:T(8,128)(2,1)S(1)} %get-tuple-element.71), channel_id=1, source_target_pairs={{0,6},{1,7},{2,4},{3,5},{4,2},{5,3},{6,0},{7,1},{8,14},{9,15},{10,... | collective-permute-start | bytes 393224 | tf_op jit(solution)/shard_map/ppermute | solution.py:223
  77.6 4.2 %collective-permute-start.26 = (bf16[64,1024]{1,0:T(8,128)(2,1)S(1)}, bf16[64,1024]{1,0:T(8,128)(2,1)S(1)}, u32[]{:S(2)}, u32[]{:S(2)}) collective-permute-start(bf16[64,1024]{1,0:T(8,128)(2,1)S(1)} %shard_map.48), channel_id=1, source_target_pairs={{0,2},{1,3},{2,0},{3,1},{4,6},{5,7},{6,4},{7,5},{8,10},{9,11},{10,... | collective-permute-start | bytes 393224 | tf_op jit(solution)/shard_map/ppermute | solution.py:223
  79.0 4.8 %collective-permute-start.27 = (bf16[64,1024]{1,0:T(8,128)(2,1)S(1)}, bf16[64,1024]{1,0:T(8,128)(2,1)S(1)}, u32[]{:S(2)}, u32[]{:S(2)}) collective-permute-start(bf16[64,1024]{1,0:T(8,128)(2,1)S(1)} %shard_map.48), channel_id=1, source_target_pairs={{0,4},{1,5},{2,6},{3,7},{4,0},{5,1},{6,2},{7,3},{8,12},{9,13},{10,... | collective-permute-start | bytes 393224 | tf_op jit(solution)/shard_map/ppermute | solution.py:223
  79.3 5.7 %collective-permute-start.28 = (bf16[64,1024]{1,0:T(8,128)(2,1)S(1)}, bf16[64,1024]{1,0:T(8,128)(2,1)S(1)}, u32[]{:S(2)}, u32[]{:S(2)}) collective-permute-start(bf16[64,1024]{1,0:T(8,128)(2,1)S(1)} %shard_map.48), channel_id=1, source_target_pairs={{0,6},{1,7},{2,4},{3,5},{4,2},{5,3},{6,0},{7,1},{8,14},{9,15},{10,... | collective-permute-start | bytes 393224 | tf_op jit(solution)/shard_map/ppermute | solution.py:223
  85.0 4.4 %collective-permute-start.31 = (bf16[256,1024]{1,0:T(8,128)(2,1)S(1)}, bf16[256,1024]{1,0:T(8,128)(2,1)S(1)}, u32[]{:S(2)}, u32[]{:S(2)}) collective-permute-start(bf16[256,1024]{1,0:T(8,128)(2,1)S(1)} %pad_maximum_fusion.near), channel_id=1, source_target_pairs={{0,1},{1,0},{2,3},{3,2},{4,5},{5,4},{6,7},{7,6},{8,9},{9,8},{10,11... | collective-permute-start | bytes 1572872 | tf_op jit(solution)/shard_map/ppermute | solution.py:223
  (1 other events, 7.4 us)

commit v13 on v12

--- a/solution.py
+++ b/solution.py
@@ -11,7 +11,7 @@
 NORM = 128
 
 
-def kernel_call(body, outs, smem=0, scratch=4):
+def kernel_call(body, outs, smem=0, scratch=4, temps=()):
     def call(*args):
         space = [pltpu.SMEM] * smem + [pltpu.VMEM] * (len(args) - smem)
         return pl.pallas_call(
@@ -19,6 +19,7 @@
             out_shape=[jax.ShapeDtypeStruct(s, t) for s, t in outs],
             in_specs=[pl.BlockSpec(memory_space=m) for m in space],
             out_specs=[pl.BlockSpec(memory_space=pltpu.VMEM) for _ in outs],
+            scratch_shapes=[pltpu.VMEM(s, t) for s, t in temps],
             compiler_params=pltpu.CompilerParams(vmem_limit_bytes=scratch * 1024 * 1024),
             cost_estimate=pl.CostEstimate(flops=0, bytes_accessed=0, transcendentals=0),
         )(*args)
@@ -106,24 +107,17 @@
         split_sum(gram(turned[...], beside[...]), kept, sent, slice(None))
 
 
-def second_kernel(
-    middle, turned, beside, swapped, swapped_square, end, mean, opposite, square, kept, sent
-):
-    rows = opposite.shape[0]
-
+def second_kernel(middle, turned, swapped, swapped_square, end, mean, opposite, square, kept, sent):
     @pl.when(middle[0] == 1)
     def _():
         opposite[...] = swapped[...]
         square[...] = swapped_square[...]
-        split_sum(gram(turned[...], beside[...]), kept, sent, slice(rows, 2 * rows))
 
     @pl.when(middle[0] == 0)
     def _():
         centered_into(opposite, end, mean[...], square)
-        kept[:, rows:] = jnp.zeros_like(kept[:, rows:])
-        sent[:, rows:] = jnp.zeros_like(sent[:, rows:])
-
-    split_sum(gram(turned[...], opposite[...]), kept, sent, slice(0, rows))
+
+    split_sum(gram(turned[...], opposite[...]), kept, sent, slice(None))
 
 
 def stats_kernel(z, out):
@@ -158,7 +152,7 @@
     out[...] = with_norm(total, last).astype(jnp.bfloat16)
 
 
-def place_kernel(order, near, far, out):
+def place_into(out, order, near, far):
     eighth = out.shape[0] // 8
     for k in range(4):
         here = slice(k * eighth, (k + 1) * eighth)
@@ -166,7 +160,14 @@
         out[pl.ds(pl.multiple_of(order[4 + k] * eighth, eighth), eighth), :] = far[here, :]
 
 
-def push_kernel(middle, inner, beside, opposite, beside_square, opposite_square, out, over):
+def place_kernel(order, near, far, out):
+    place_into(out, order, near, far)
+
+
+def push_kernel(
+    order, middle, near, far, beside, opposite, beside_square, opposite_square, inner, out, over
+):
+    place_into(inner, order, near, far)
     width = beside.shape[1]
 
     @pl.when(middle[0] == 1)
@@ -204,19 +205,22 @@
         held[:, here] = plain + coefficient(total) * product
 
 
-def last_kernel(total, middle, first, second, beside, opposite, held, out, over, result):
+def last_kernel(
+    total, order, middle, first, near, far, beside, opposite, held, out, over, result, second
+):
     rows, width = beside.shape
-
-    def put(with_beside, arrived):
+    place_into(second, order, near, far)
+
+    def put(product_of, with_beside, arrived):
         for k in range(4):
             here = slice(k * width // 4, (k + 1) * width // 4)
-            product = dot(with_beside, beside[:, here])
+            product = product_of(with_beside, beside[:, here])
             product = product + dot(second[:, :rows], opposite[:, here])
             product = product + arrived[:, here].astype(jnp.float32)
             result[:, here] = held[:, here] + coefficient(total) * product
 
-    pl.when(middle[0] == 1)(lambda: put(second[:, rows:], over))
-    pl.when(middle[0] == 0)(lambda: put(first[...], out))
+    pl.when(middle[0] == 1)(lambda: put(dot_t, second[:, rows:], over))
+    pl.when(middle[0] == 0)(lambda: put(dot, first[...], out))
 
 
 def to_partner(x, step):
@@ -242,10 +246,11 @@
     return jnp.concatenate([x] + [to_partner(x, 2 * k) for k in (1, 2, 3)])
 
 
-def gather_cores(near, order, *others):
-    far = after(to_partner(near, 1), *others)
+def gather_cores(near, order):
     shape = (2 * near.shape[0], near.shape[1])
-    return kernel_call(place_kernel, [(shape, jnp.bfloat16)], smem=1)(order, near, far)[0]
+    return kernel_call(place_kernel, [(shape, jnp.bfloat16)], smem=1)(
+        order, near, to_partner(near, 1)
+    )[0]
 
 
 def after(x, *others):
@@ -267,8 +272,8 @@
         lax.ppermute(stats, "dp", [(i, (i + k) % 4) for i in range(4)]) for k in (1, 2, 3)
     ]
     ahead = after(z_anchor, stats)
+    swapped = lax.ppermute(ahead, "dp", across)
     beside_in = lax.ppermute(ahead, "dp", [(i, i ^ 1) for i in range(4)])
-    swapped = lax.ppermute(ahead, "dp", across)
     mean = (all_stats[0][:1] + all_stats[1][:1] + all_stats[2][:1] + all_stats[3][:1]) / 4
     spread = 0.0
     for one in all_stats:
@@ -281,32 +286,38 @@
     own, turned, own_square, kept, sent = kernel_call(
         own_kernel, [block, block, flat, *summands(rows + NORM)], smem=1, scratch=12
     )(order, z_anchor, mean)
-    near_own = gather_chips(scatter(*halve(kept, sent, rows), last=rows))
-    end = lax.ppermute(after(z_anchor, beside_in, swapped, near_own), "dp", [(0, 3), (3, 0)])
-
-    beside, beside_square, swapped, swapped_square, kept, sent, _ = kernel_call(
-        first_kernel, [block, flat, block, flat, *summands(rows), block], smem=2, scratch=12
-    )(order, middle, after(turned, near_own), beside_in, swapped, mean)
-    with_own = gather_cores(near_own, order)
-    first = gather_cores(gather_chips(scatter(*halve(kept, sent))), order, end)
-    ready = kernel_call(push_kernel, [block, block], smem=1, scratch=12)(
-        middle, first, beside, swapped, beside_square, swapped_square
-    )
+    with_own = gather_chips(scatter(*halve(kept, sent, rows), last=rows))
+    with_own = gather_cores(with_own, order)
+    end = lax.ppermute(after(z_anchor, beside_in, swapped, with_own), "dp", [(0, 3), (3, 0)])
+
+    beside, beside_square, swapped, swapped_square, kept, sent = kernel_call(
+        first_kernel, [block, flat, block, flat, *summands(rows)],
+        smem=2, scratch=12, temps=[block],
+    )(order, middle, after(turned, with_own), beside_in, swapped, mean)
+    first = scatter(*halve(kept, sent))
+    crossed = lax.ppermute(first, "dp", [(0, 1), (3, 2)])
+    near = gather_chips(first)
+    first, *ready = kernel_call(
+        push_kernel, [((rows, rows), jnp.bfloat16), block, block], smem=2, scratch=12
+    )(order, middle, near, to_partner(near, 1), beside, swapped, beside_square, swapped_square)
     pushed = [lax.ppermute(x, "dp", p) for x, p in zip(ready, (outward, across))]
 
     opposite, opposite_square, kept, sent = kernel_call(
-        second_kernel, [block, flat, *summands(2 * rows)], smem=1, scratch=12
-    )(middle, after(turned, *ready), beside, swapped, swapped_square, end, mean)
+        second_kernel, [block, flat, *summands(rows)], smem=1, scratch=12
+    )(middle, after(turned, *ready), swapped, swapped_square, end, mean)
     halved = halve(kept, sent)
     result = ((rows, width), jnp.float32)
     held = kernel_call(functools.partial(held_kernel, total), [result], scratch=12)(
         with_own, own, z_anchor, z_other,
         own_square, beside_square, after(opposite_square, halved[0]), mean, spread,
     )[0]
-    second = gather_chips(after(scatter(*halved), held))
-    second = gather_cores(after(second, *pushed), order)
-    return kernel_call(functools.partial(last_kernel, total), [result], smem=1, scratch=12)(
-        middle, first, second, beside, opposite, held, *pushed
+    second = jnp.concatenate([scatter(*halved), crossed], axis=1)
+    near = after(gather_chips(after(second, held)), *pushed)
+    return kernel_call(
+        functools.partial(last_kernel, total), [result],
+        smem=2, scratch=12, temps=[((rows, 2 * rows), jnp.bfloat16)],
+    )(
+        order, middle, first, near, to_partner(near, 1), beside, opposite, held, *pushed
     )[0]
 
 

time: 93.5 us -> 95.1 us (1.017)
  the two profiles are of different devices: /device:TPU:9 before, /device:TPU:0 now
where the time goes in v13:
time: 95.1 us; the launch traced here: 94.7 us
  starting transfers between devices  40.7 us (43%)
  waiting for transfers between devices  37.7 us (40%)
  Pallas kernels  15.2 us (16%)
    ppermute x24, waiting for transfers between devices, to_partner(): return lax.ppermute(x, 'feat', [(i, i ^ step) for i in range(8)])  28.7 us
    ppermute x24, starting transfers between devices, to_partner(): return lax.ppermute(x, 'feat', [(i, i ^ step) for i in range(8)])  21.8 us
    pallas_call x14, Pallas kernels, call(): pl.pallas_call(body, out_shape=[jax.ShapeDtypeStruct(s, t) for s, t in ou...  15.2 us
    ppermute x1, waiting for transfers between devices, by_line(): lax.ppermute(after(z_anchor, beside_in, swapped, with_own), 'dp', [(0, 3)...  6.22 us
    ppermute x3, starting transfers between devices, by_line(): lax.ppermute(stats, 'dp', [(i, (i + k) % 4) for i in range(4)])  6.11 us
    ppermute x1, starting transfers between devices, by_line(): lax.ppermute(after(z_anchor, beside_in, swapped, with_own), 'dp', [(0, 3)...  4.83 us
    ppermute x1, starting transfers between devices, by_line(): beside_in = lax.ppermute(ahead, 'dp', [(i, i ^ 1) for i in range(4)])  3.74 us
    ppermute x2, waiting for transfers between devices, by_line(): lax.ppermute(x, 'dp', p)  2.84 us
  transfers between devices with their start and end apart: 33, of which 23 were waited for; matrix products, arithmetic and copies ran while one was open for 1% of the time, Pallas kernels for 8%

profile of v13, /device:TPU:0, one launch (start us, length us, event | category | flops | bytes accessed | tf_op | source)
XLA Modules:
  0.0 94.7 jit_solution(6505306924303838209)
XLA Ops:
  0.0 1.8 %shard_map.37 = f32[2,1024]{1,0:T(2,128)S(1)} custom-call(bf16[512,1024]{1,0:T(8,128)(2,1)} %z.5), custom_call_target="tpu_custom_call" | custom-call | tf_op jit(solution)/shard_map/pallas_call | solution.py:17
  1.8 5.1 %collective-permute-start.2 = (f32[2,1024]{1,0:T(2,128)S(1)}, f32[2,1024]{1,0:T(2,128)S(1)}, u32[]{:S(2)}, u32[]{:S(2)}) collective-permute-start(f32[2,1024]{1,0:T(2,128)S(1)} %shard_map.37), channel_id=1, source_target_pairs={{0,24},{8,0},{16,8},{24,16},{1,25},{9,1},{17,9},{25,17},{2,26},{10... | collective-permute-start | bytes 24584 | tf_op jit(solution)/shard_map/ppermute | solution.py:272
  8.7 3.7 %collective-permute-start.11 = (bf16[512,1024]{1,0:T(8,128)(2,1)}, bf16[512,1024]{1,0:T(8,128)(2,1)}, u32[]{:S(2)}, u32[]{:S(2)}) collective-permute-start(bf16[512,1024]{1,0:T(8,128)(2,1)} %z.5), channel_id=1, source_target_pairs={{0,8},{8,0},{16,24},{24,16},{1,9},{9,1},{17,25},{25,17},{2,10},{10... | collective-permute-start | bytes 3145736 | tf_op jit(solution)/shard_map/ppermute | solution.py:276
  13.1 2.4 %shard_map.38 = (bf16[512,1024]{1,0:T(8,128)(2,1)S(1)}, bf16[512,1024]{1,0:T(8,128)(2,1)S(1)}, f32[1,1024]{1,0:T(1,128)S(1)}, f32[256,640]{1,0:T(8,128)S(1)}, bf16[256,640]{1,0:T(8,128)(2,1)S(1)}) custom-call(s32[8]{0:T(128)S(1)} %broadcast_xor_fusion.order, bf16[512,1024]{1,0:T(8,128)(2,1)} %z.5, f32[1,1024]{1,0:T(1,128)S(1)} %get-tuple-element.80.mean), custom_call_target="tpu_custom_call" | custom-call | tf_op jit(solution)/shard_map/pallas_call | solution.py:17
  15.6 1.6 %collective-permute-done.3.got = bf16[256,640]{1,0:T(8,128)(2,1)S(1)} collective-permute-done((bf16[256,640]{1,0:T(8,128)(2,1)S(1)}, bf16[256,640]{1,0:T(8,128)(2,1)S(1)}, u32[]{:S(2)}, u32[]{:S(2)}) %collective-permute-start.3) | collective-permute-done | bytes 327712 | tf_op jit(solution)/shard_map/ppermute | solution.py:227
  17.3 1.6 %collective-permute-start.4 = (bf16[64,640]{1,0:T(8,128)(2,1)S(1)}, bf16[64,640]{1,0:T(8,128)(2,1)S(1)}, u32[]{:S(2)}, u32[]{:S(2)}) collective-permute-start(bf16[64,640]{1,0:T(8,128)(2,1)S(1)} %get-tuple-element.46), channel_id=1, source_target_pairs={{0,2},{1,3},{2,0},{3,1},{4,6},{5,7},{6,4},{7,5},{8,10},{9,11},{10,... | collective-permute-start | bytes 245768 | tf_op jit(solution)/shard_map/ppermute | solution.py:227
  18.9 1.5 %collective-permute-start.5 = (bf16[64,640]{1,0:T(8,128)(2,1)S(1)}, bf16[64,640]{1,0:T(8,128)(2,1)S(1)}, u32[]{:S(2)}, u32[]{:S(2)}) collective-permute-start(bf16[64,640]{1,0:T(8,128)(2,1)S(1)} %get-tuple-element.47), channel_id=1, source_target_pairs={{0,4},{1,5},{2,6},{3,7},{4,0},{5,1},{6,2},{7,3},{8,12},{9,13},{10,... | collective-permute-start | bytes 245768 | tf_op jit(solution)/shard_map/ppermute | solution.py:227
  21.9 2.3 %collective-permute-done.5.b = bf16[64,640]{1,0:T(8,128)(2,1)S(1)} collective-permute-done((bf16[64,640]{1,0:T(8,128)(2,1)S(1)}, bf16[64,640]{1,0:T(8,128)(2,1)S(1)}, u32[]{:S(2)}, u32[]{:S(2)}) %collective-permute-start.5) | collective-permute-done | bytes 81952 | tf_op jit(solution)/shard_map/ppermute | solution.py:227
  24.1 1.6 %collective-permute-done.6.c = bf16[64,640]{1,0:T(8,128)(2,1)S(1)} collective-permute-done((bf16[64,640]{1,0:T(8,128)(2,1)S(1)}, bf16[64,640]{1,0:T(8,128)(2,1)S(1)}, u32[]{:S(2)}, u32[]{:S(2)}) %collective-permute-start.6) | collective-permute-done | bytes 81952 | tf_op jit(solution)/shard_map/ppermute | solution.py:227
  27.9 1.5 %collective-permute-start.7 = (bf16[64,640]{1,0:T(8,128)(2,1)S(1)}, bf16[64,640]{1,0:T(8,128)(2,1)S(1)}, u32[]{:S(2)}, u32[]{:S(2)}) collective-permute-start(bf16[64,640]{1,0:T(8,128)(2,1)S(1)} %shard_map.40), channel_id=1, source_target_pairs={{0,2},{1,3},{2,0},{3,1},{4,6},{5,7},{6,4},{7,5},{8,10},{9,11},{10,... | collective-permute-start | bytes 245768 | tf_op jit(solution)/shard_map/ppermute | solution.py:227
  29.4 2.0 %collective-permute-done.9 = bf16[64,640]{1,0:T(8,128)(2,1)S(1)} collective-permute-done((bf16[64,640]{1,0:T(8,128)(2,1)S(1)}, bf16[64,640]{1,0:T(8,128)(2,1)S(1)}, u32[]{:S(2)}, u32[]{:S(2)}) %collective-permute-start.9) | collective-permute-done | bytes 81952 | tf_op jit(solution)/shard_map/ppermute | solution.py:227
  32.5 1.7 %collective-permute-done.10.far = bf16[256,640]{1,0:T(8,128)(2,1)} collective-permute-done((bf16[256,640]{1,0:T(8,128)(2,1)S(1)}, bf16[256,640]{1,0:T(8,128)(2,1)}, u32[]{:S(2)}, u32[]{:S(2)}) %collective-permute-start.10) | collective-permute-done | bytes 327712 | tf_op jit(solution)/shard_map/ppermute | solution.py:227
  35.3 2.2 %shard_map.42 = (bf16[512,1024]{1,0:T(8,128)(2,1)S(1)}, f32[1,1024]{1,0:T(1,128)S(1)}, bf16[512,1024]{1,0:T(8,128)(2,1)S(1)}, f32[1,1024]{1,0:T(1,128)S(1)}, f32...) custom-call(s32[8]{0:T(128)S(1)} %broadcast_xor_fusion.order, s32[1]{0:T(128)} %bitcast.middle, ...), custom_call_target="tpu_custom_call" | custom-call | tf_op jit(solution)/shard_map/pallas_call | solution.py:17
  37.7 4.8 %collective-permute-start.21 = (bf16[512,1024]{1,0:T(8,128)(2,1)}, bf16[512,1024]{1,0:T(8,128)(2,1)S(1)}, u32[]{:S(2)}, u32[]{:S(2)}) collective-permute-start(bf16[512,1024]{1,0:T(8,128)(2,1)} %z.5), channel_id=1, source_target_pairs={{0,24},{24,0},{1,25},{25,1},{2,26},{26,2},{3,27},{27,3},{4,28},{28... | collective-permute-start | bytes 3145736 | tf_op jit(solution)/shard_map/ppermute | solution.py:291
  42.6 1.6 %collective-permute-start.14 = (bf16[64,512]{1,0:T(8,128)(2,1)S(1)}, bf16[64,512]{1,0:T(8,128)(2,1)S(1)}, u32[]{:S(2)}, u32[]{:S(2)}) collective-permute-start(bf16[64,512]{1,0:T(8,128)(2,1)S(1)} %get-tuple-element.54), channel_id=1, source_target_pairs={{0,2},{1,3},{2,0},{3,1},{4,6},{5,7},{6,4},{7,5},{8,10},{9,11},{10,... | collective-permute-start | bytes 196616 | tf_op jit(solution)/shard_map/ppermute | solution.py:227
  46.9 2.2 %collective-permute-done.15.b = bf16[64,512]{1,0:T(8,128)(2,1)S(1)} collective-permute-done((bf16[64,512]{1,0:T(8,128)(2,1)S(1)}, bf16[64,512]{1,0:T(8,128)(2,1)S(1)}, u32[]{:S(2)}, u32[]{:S(2)}) %collective-permute-start.15) | collective-permute-done | bytes 65568 | tf_op jit(solution)/shard_map/ppermute | solution.py:227
  52.3 1.5 %collective-permute-start.17 = (bf16[64,512]{1,0:T(8,128)(2,1)S(1)}, bf16[64,512]{1,0:T(8,128)(2,1)S(1)}, u32[]{:S(2)}, u32[]{:S(2)}) collective-permute-start(bf16[64,512]{1,0:T(8,128)(2,1)S(1)} %shard_map.44), channel_id=1, source_target_pairs={{0,2},{1,3},{2,0},{3,1},{4,6},{5,7},{6,4},{7,5},{8,10},{9,11},{10,... | collective-permute-start | bytes 196616 | tf_op jit(solution)/shard_map/ppermute | solution.py:227
  53.8 1.7 %collective-permute-done.19 = bf16[64,512]{1,0:T(8,128)(2,1)S(1)} collective-permute-done((bf16[64,512]{1,0:T(8,128)(2,1)S(1)}, bf16[64,512]{1,0:T(8,128)(2,1)S(1)}, u32[]{:S(2)}, u32[]{:S(2)}) %collective-permute-start.19) | collective-permute-done | bytes 65568 | tf_op jit(solution)/shard_map/ppermute | solution.py:227
  56.6 1.5 %collective-permute-done.20.far = bf16[256,512]{1,0:T(8,128)(2,1)S(1)} collective-permute-done((bf16[256,512]{1,0:T(8,128)(2,1)S(1)}, bf16[256,512]{1,0:T(8,128)(2,1)S(1)}, u32[]{:S(2)}, u32[]{:S(2)}) %collective-permute-start.20) | collective-permute-done | bytes 262176 | tf_op jit(solution)/shard_map/ppermute | solution.py:227
  58.8 1.4 %collective-permute-start.30 = (bf16[512,1024]{1,0:T(8,128)(2,1)S(1)}, bf16[512,1024]{1,0:T(8,128)(2,1)S(1)}, u32[]{:S(2)}, u32[]{:S(2)}) collective-permute-start(bf16[512,1024]{1,0:T(8,128)(2,1)S(1)} %get-tuple-element.62), channel_id=1, source_target_pairs={{8,0},{16,24},{9,1},{17,25},{10,2},{18,26},{11,3},{19,27},{12,4},{... | collective-permute-start | bytes 3145736 | tf_op jit(solution)/shard_map/ppermute | solution.py:303
  60.9 6.2 %collective-permute-done.21.end = bf16[512,1024]{1,0:T(8,128)(2,1)S(1)} collective-permute-done((bf16[512,1024]{1,0:T(8,128)(2,1)}, bf16[512,1024]{1,0:T(8,128)(2,1)S(1)}, u32[]{:S(2)}, u32[]{:S(2)}) %collective-permute-start.21) | collective-permute-done | bytes 1048608 | tf_op jit(solution)/shard_map/ppermute | solution.py:291
  68.2 1.5 %collective-permute-done.22.got = bf16[256,512]{1,0:T(8,128)(2,1)S(1)} collective-permute-done((bf16[256,512]{1,0:T(8,128)(2,1)S(1)}, bf16[256,512]{1,0:T(8,128)(2,1)S(1)}, u32[]{:S(2)}, u32[]{:S(2)}) %collective-permute-start.22) | collective-permute-done | bytes 262176 | tf_op jit(solution)/shard_map/ppermute | solution.py:227
  69.8 1.6 %collective-permute-start.23 = (bf16[64,512]{1,0:T(8,128)(2,1)S(1)}, bf16[64,512]{1,0:T(8,128)(2,1)S(1)}, u32[]{:S(2)}, u32[]{:S(2)}) collective-permute-start(bf16[64,512]{1,0:T(8,128)(2,1)S(1)} %get-tuple-element.69), channel_id=1, source_target_pairs={{0,2},{1,3},{2,0},{3,1},{4,6},{5,7},{6,4},{7,5},{8,10},{9,11},{10,... | collective-permute-start | bytes 196616 | tf_op jit(solution)/shard_map/ppermute | solution.py:227
  71.3 1.3 %collective-permute-start.24 = (bf16[64,512]{1,0:T(8,128)(2,1)S(1)}, bf16[64,512]{1,0:T(8,128)(2,1)S(1)}, u32[]{:S(2)}, u32[]{:S(2)}) collective-permute-start(bf16[64,512]{1,0:T(8,128)(2,1)S(1)} %get-tuple-element.70), channel_id=1, source_target_pairs={{0,4},{1,5},{2,6},{3,7},{4,0},{5,1},{6,2},{7,3},{8,12},{9,13},{10,... | collective-permute-start | bytes 196616 | tf_op jit(solution)/shard_map/ppermute | solution.py:227
  74.1 1.3 %collective-permute-start.26 = (bf16[64,512]{1,0:T(8,128)(2,1)S(1)}, bf16[64,512]{1,0:T(8,128)(2,1)S(1)}, u32[]{:S(2)}, u32[]{:S(2)}) collective-permute-start(bf16[64,512]{1,0:T(8,128)(2,1)S(1)} %shard_map.44), channel_id=1, source_target_pairs={{0,8},{24,16},{1,9},{25,17},{2,10},{26,18},{3,11},{27,19},{4,12},{... | collective-permute-start | bytes 196616 | tf_op jit(solution)/shard_map/ppermute | solution.py:298
  75.4 2.6 %shard_map.49.held = f32[512,1024]{1,0:T(8,128)S(1)} custom-call(bf16[512,640]{1,0:T(8,128)(2,1)S(1)} %shard_map.41.with_own, bf16[512,1024]{1,0:T(8,128)(2,1)S(1)} %get-tuple-element.72.own, bf16[512,1024]{1,0:T(8,128)(2,1)} %z.5, bf16[512,1024]{1,0:T(8,128)(2,1)S(1)} %copy-done, f32[1,1024]{1,0:T(1,128)S(1)} %get-tuple-element.73.own_square, ...), custom_call_target="tpu_custom_call" | custom-call | tf_op jit(solution)/shard_map/pallas_call | solution.py:17
  78.1 2.4 %collective-permute-start.29 = (bf16[64,1024]{1,0:T(8,128)(2,1)S(1)}, bf16[64,1024]{1,0:T(8,128)(2,1)S(1)}, u32[]{:S(2)}, u32[]{:S(2)}) collective-permute-start(bf16[64,1024]{1,0:T(8,128)(2,1)S(1)} %pad_maximum_fusion.3), channel_id=1, source_target_pairs={{0,6},{1,7},{2,4},{3,5},{4,2},{5,3},{6,0},{7,1},{8,14},{9,15},{10,... | collective-permute-start | bytes 393224 | tf_op jit(solution)/shard_map/ppermute | solution.py:227
  81.6 3.3 %collective-permute-done.29 = bf16[64,1024]{1,0:T(8,128)(2,1)S(1)} collective-permute-done((bf16[64,1024]{1,0:T(8,128)(2,1)S(1)}, bf16[64,1024]{1,0:T(8,128)(2,1)S(1)}, u32[]{:S(2)}, u32[]{:S(2)}) %collective-permute-start.29) | collective-permute-done | bytes 131104 | tf_op jit(solution)/shard_map/ppermute | solution.py:227
  85.0 1.6 %collective-permute-done.28 = bf16[64,1024]{1,0:T(8,128)(2,1)S(1)} collective-permute-done((bf16[64,1024]{1,0:T(8,128)(2,1)S(1)}, bf16[64,1024]{1,0:T(8,128)(2,1)S(1)}, u32[]{:S(2)}, u32[]{:S(2)}) %collective-permute-start.28) | collective-permute-done | bytes 131104 | tf_op jit(solution)/shard_map/ppermute | solution.py:227
  86.7 2.8 %collective-permute-done.30.out = bf16[512,1024]{1,0:T(8,128)(2,1)S(1)} collective-permute-done((bf16[512,1024]{1,0:T(8,128)(2,1)S(1)}, bf16[512,1024]{1,0:T(8,128)(2,1)S(1)}, u32[]{:S(2)}, u32[]{:S(2)}) %collective-permute-start.30) | collective-permute-done | bytes 1048608 | tf_op jit(solution)/shard_map/ppermute | solution.py:303
  89.5 1.9 %collective-permute-done.32.far = bf16[256,1024]{1,0:T(8,128)(2,1)S(1)} collective-permute-done((bf16[256,1024]{1,0:T(8,128)(2,1)S(1)}, bf16[256,1024]{1,0:T(8,128)(2,1)S(1)}, u32[]{:S(2)}, u32[]{:S(2)}) %collective-permute-start.32) | collective-permute-done | bytes 524320 | tf_op jit(solution)/shard_map/ppermute | solution.py:227
  91.4 3.2 %shard_map.50 = f32[512,1024]{1,0:T(8,128)} custom-call(s32[8]{0:T(128)S(1)} %broadcast_xor_fusion.order, s32[1]{0:T(128)} %bitcast.middle, bf16[512,512]{1,0:T(8,128)(2,1)S(1)} %get-tuple-element.61.first, bf16[256,1024]{1,0:T(8,128)(2,1)S(1)} %pad_maximum_fusion.near, bf16[256,1024]{1,0:T(8,128)(2,1)S(1)} %collective-permute-done.32.far, ...), custom_call_target="tpu_custom_call" | custom-call | tf_op jit(solution)/shard_map/pallas_call | solution.py:17
  (56 shorter events, 21.0 us)
Async XLA Ops:
  1.8 11.2 %collective-permute-start.2 = (f32[2,1024]{1,0:T(2,128)S(1)}, f32[2,1024]{1,0:T(2,128)S(1)}, u32[]{:S(2)}, u32[]{:S(2)}) collective-permute-start(f32[2,1024]{1,0:T(2,128)S(1)} %shard_map.37), channel_id=1, source_target_pairs={{0,24},{8,0},{16,8},{24,16},{1,25},{9,1},{17,9},{25,17},{2,26},{10... | collective-permute-start | bytes 24584 | tf_op jit(solution)/shard_map/ppermute | solution.py:272
  6.9 6.1 %collective-permute-start.1 = (f32[2,1024]{1,0:T(2,128)S(1)}, f32[2,1024]{1,0:T(2,128)S(1)}, u32[]{:S(2)}, u32[]{:S(2)}) collective-permute-start(f32[2,1024]{1,0:T(2,128)S(1)} %shard_map.37), channel_id=1, source_target_pairs={{0,16},{8,24},{16,0},{24,8},{1,17},{9,25},{17,1},{25,9},{2,18},{10... | collective-permute-start | bytes 24584 | tf_op jit(solution)/shard_map/ppermute | solution.py:272
  6.9 6.1 %collective-permute-start = (f32[2,1024]{1,0:T(2,128)S(1)}, f32[2,1024]{1,0:T(2,128)S(1)}, u32[]{:S(2)}, u32[]{:S(2)}) collective-permute-start(f32[2,1024]{1,0:T(2,128)S(1)} %shard_map.37), channel_id=1, source_target_pairs={{0,8},{8,16},{16,24},{24,0},{1,9},{9,17},{17,25},{25,1},{2,10},{10... | collective-permute-start | bytes 24584 | tf_op jit(solution)/shard_map/ppermute | solution.py:272
  7.9 27.3 %collective-permute-start.12 = (bf16[512,1024]{1,0:T(8,128)(2,1)}, bf16[512,1024]{1,0:T(8,128)(2,1)S(1)}, u32[]{:S(2)}, u32[]{:S(2)}) collective-permute-start(bf16[512,1024]{1,0:T(8,128)(2,1)} %z.5), channel_id=1, source_target_pairs={{8,16},{16,8},{9,17},{17,9},{10,18},{18,10},{11,19},{19,11},{12,20... | collective-permute-start | bytes 3145736 | tf_op jit(solution)/shard_map/ppermute | solution.py:275
  8.7 26.6 %collective-permute-start.11 = (bf16[512,1024]{1,0:T(8,128)(2,1)}, bf16[512,1024]{1,0:T(8,128)(2,1)}, u32[]{:S(2)}, u32[]{:S(2)}) collective-permute-start(bf16[512,1024]{1,0:T(8,128)(2,1)} %z.5), channel_id=1, source_target_pairs={{0,8},{8,0},{16,24},{24,16},{1,9},{9,1},{17,25},{25,17},{2,10},{10... | collective-permute-start | bytes 3145736 | tf_op jit(solution)/shard_map/ppermute | solution.py:276
  15.5 1.7 %collective-permute-start.3 = (bf16[256,640]{1,0:T(8,128)(2,1)S(1)}, bf16[256,640]{1,0:T(8,128)(2,1)S(1)}, u32[]{:S(2)}, u32[]{:S(2)}) collective-permute-start(bf16[256,640]{1,0:T(8,128)(2,1)S(1)} %get-tuple-element.44), channel_id=1, source_target_pairs={{0,1},{1,0},{2,3},{3,2},{4,5},{5,4},{6,7},{7,6},{8,9},{9,8},{10,11... | collective-permute-start | bytes 983048 | tf_op jit(solution)/shard_map/ppermute | solution.py:227
  17.3 4.6 %collective-permute-start.4 = (bf16[64,640]{1,0:T(8,128)(2,1)S(1)}, bf16[64,640]{1,0:T(8,128)(2,1)S(1)}, u32[]{:S(2)}, u32[]{:S(2)}) collective-permute-start(bf16[64,640]{1,0:T(8,128)(2,1)S(1)} %get-tuple-element.46), channel_id=1, source_target_pairs={{0,2},{1,3},{2,0},{3,1},{4,6},{5,7},{6,4},{7,5},{8,10},{9,11},{10,... | collective-permute-start | bytes 245768 | tf_op jit(solution)/shard_map/ppermute | solution.py:227
  18.9 5.3 %collective-permute-start.5 = (bf16[64,640]{1,0:T(8,128)(2,1)S(1)}, bf16[64,640]{1,0:T(8,128)(2,1)S(1)}, u32[]{:S(2)}, u32[]{:S(2)}) collective-permute-start(bf16[64,640]{1,0:T(8,128)(2,1)S(1)} %get-tuple-element.47), channel_id=1, source_target_pairs={{0,4},{1,5},{2,6},{3,7},{4,0},{5,1},{6,2},{7,3},{8,12},{9,13},{10,... | collective-permute-start | bytes 245768 | tf_op jit(solution)/shard_map/ppermute | solution.py:227
  20.4 5.3 %collective-permute-start.6 = (bf16[64,640]{1,0:T(8,128)(2,1)S(1)}, bf16[64,640]{1,0:T(8,128)(2,1)S(1)}, u32[]{:S(2)}, u32[]{:S(2)}) collective-permute-start(bf16[64,640]{1,0:T(8,128)(2,1)S(1)} %get-tuple-element.48), channel_id=1, source_target_pairs={{0,6},{1,7},{2,4},{3,5},{4,2},{5,3},{6,0},{7,1},{8,14},{9,15},{10,... | collective-permute-start | bytes 245768 | tf_op jit(solution)/shard_map/ppermute | solution.py:227
  25.8 5.5 %collective-permute-start.9 = (bf16[64,640]{1,0:T(8,128)(2,1)S(1)}, bf16[64,640]{1,0:T(8,128)(2,1)S(1)}, u32[]{:S(2)}, u32[]{:S(2)}) collective-permute-start(bf16[64,640]{1,0:T(8,128)(2,1)S(1)} %shard_map.40), channel_id=1, source_target_pairs={{0,6},{1,7},{2,4},{3,5},{4,2},{5,3},{6,0},{7,1},{8,14},{9,15},{10,... | collective-permute-start | bytes 245768 | tf_op jit(solution)/shard_map/ppermute | solution.py:227
  26.7 5.3 %collective-permute-start.8 = (bf16[64,640]{1,0:T(8,128)(2,1)S(1)}, bf16[64,640]{1,0:T(8,128)(2,1)S(1)}, u32[]{:S(2)}, u32[]{:S(2)}) collective-permute-start(bf16[64,640]{1,0:T(8,128)(2,1)S(1)} %shard_map.40), channel_id=1, source_target_pairs={{0,4},{1,5},{2,6},{3,7},{4,0},{5,1},{6,2},{7,3},{8,12},{9,13},{10,... | collective-permute-start | bytes 245768 | tf_op jit(solution)/shard_map/ppermute | solution.py:227
  27.9 4.4 %collective-permute-start.7 = (bf16[64,640]{1,0:T(8,128)(2,1)S(1)}, bf16[64,640]{1,0:T(8,128)(2,1)S(1)}, u32[]{:S(2)}, u32[]{:S(2)}) collective-permute-start(bf16[64,640]{1,0:T(8,128)(2,1)S(1)} %shard_map.40), channel_id=1, source_target_pairs={{0,2},{1,3},{2,0},{3,1},{4,6},{5,7},{6,4},{7,5},{8,10},{9,11},{10,... | collective-permute-start | bytes 245768 | tf_op jit(solution)/shard_map/ppermute | solution.py:227
  32.4 1.8 %collective-permute-start.10 = (bf16[256,640]{1,0:T(8,128)(2,1)S(1)}, bf16[256,640]{1,0:T(8,128)(2,1)}, u32[]{:S(2)}, u32[]{:S(2)}) collective-permute-start(bf16[256,640]{1,0:T(8,128)(2,1)S(1)} %pad_maximum_fusion.1.near), channel_id=1, source_target_pairs={{0,1},{1,0},{2,3},{3,2},{4,5},{5,4},{6,7},{7,6},{8,9},{9,8},{10,11... | collective-permute-start | bytes 983048 | tf_op jit(solution)/shard_map/ppermute | solution.py:227
  37.5 5.0 %collective-permute-start.13 = (bf16[256,512]{1,0:T(8,128)(2,1)S(1)}, bf16[256,512]{1,0:T(8,128)(2,1)S(1)}, u32[]{:S(2)}, u32[]{:S(2)}) collective-permute-start(bf16[256,512]{1,0:T(8,128)(2,1)S(1)} %get-tuple-element.52), channel_id=1, source_target_pairs={{0,1},{1,0},{2,3},{3,2},{4,5},{5,4},{6,7},{7,6},{8,9},{9,8},{10,11... | collective-permute-start | bytes 786440 | tf_op jit(solution)/shard_map/ppermute | solution.py:227
  37.7 29.5 %collective-permute-start.21 = (bf16[512,1024]{1,0:T(8,128)(2,1)}, bf16[512,1024]{1,0:T(8,128)(2,1)S(1)}, u32[]{:S(2)}, u32[]{:S(2)}) collective-permute-start(bf16[512,1024]{1,0:T(8,128)(2,1)} %z.5), channel_id=1, source_target_pairs={{0,24},{24,0},{1,25},{25,1},{2,26},{26,2},{3,27},{27,3},{4,28},{28... | collective-permute-start | bytes 3145736 | tf_op jit(solution)/shard_map/ppermute | solution.py:291
  42.6 4.3 %collective-permute-start.14 = (bf16[64,512]{1,0:T(8,128)(2,1)S(1)}, bf16[64,512]{1,0:T(8,128)(2,1)S(1)}, u32[]{:S(2)}, u32[]{:S(2)}) collective-permute-start(bf16[64,512]{1,0:T(8,128)(2,1)S(1)} %get-tuple-element.54), channel_id=1, source_target_pairs={{0,2},{1,3},{2,0},{3,1},{4,6},{5,7},{6,4},{7,5},{8,10},{9,11},{10,... | collective-permute-start | bytes 196616 | tf_op jit(solution)/shard_map/ppermute | solution.py:227
  44.1 5.0 %collective-permute-start.15 = (bf16[64,512]{1,0:T(8,128)(2,1)S(1)}, bf16[64,512]{1,0:T(8,128)(2,1)S(1)}, u32[]{:S(2)}, u32[]{:S(2)}) collective-permute-start(bf16[64,512]{1,0:T(8,128)(2,1)S(1)} %get-tuple-element.55), channel_id=1, source_target_pairs={{0,4},{1,5},{2,6},{3,7},{4,0},{5,1},{6,2},{7,3},{8,12},{9,13},{10,... | collective-permute-start | bytes 196616 | tf_op jit(solution)/shard_map/ppermute | solution.py:227
  45.0 5.2 %collective-permute-start.16 = (bf16[64,512]{1,0:T(8,128)(2,1)S(1)}, bf16[64,512]{1,0:T(8,128)(2,1)S(1)}, u32[]{:S(2)}, u32[]{:S(2)}) collective-permute-start(bf16[64,512]{1,0:T(8,128)(2,1)S(1)} %get-tuple-element.56), channel_id=1, source_target_pairs={{0,6},{1,7},{2,4},{3,5},{4,2},{5,3},{6,0},{7,1},{8,14},{9,15},{10,... | collective-permute-start | bytes 196616 | tf_op jit(solution)/shard_map/ppermute | solution.py:227
  50.2 5.3 %collective-permute-start.19 = (bf16[64,512]{1,0:T(8,128)(2,1)S(1)}, bf16[64,512]{1,0:T(8,128)(2,1)S(1)}, u32[]{:S(2)}, u32[]{:S(2)}) collective-permute-start(bf16[64,512]{1,0:T(8,128)(2,1)S(1)} %shard_map.44), channel_id=1, source_target_pairs={{0,6},{1,7},{2,4},{3,5},{4,2},{5,3},{6,0},{7,1},{8,14},{9,15},{10,... | collective-permute-start | bytes 196616 | tf_op jit(solution)/shard_map/ppermute | solution.py:227
  51.4 4.7 %collective-permute-start.18 = (bf16[64,512]{1,0:T(8,128)(2,1)S(1)}, bf16[64,512]{1,0:T(8,128)(2,1)S(1)}, u32[]{:S(2)}, u32[]{:S(2)}) collective-permute-start(bf16[64,512]{1,0:T(8,128)(2,1)S(1)} %shard_map.44), channel_id=1, source_target_pairs={{0,4},{1,5},{2,6},{3,7},{4,0},{5,1},{6,2},{7,3},{8,12},{9,13},{10,... | collective-permute-start | bytes 196616 | tf_op jit(solution)/shard_map/ppermute | solution.py:227
  52.3 4.3 %collective-permute-start.17 = (bf16[64,512]{1,0:T(8,128)(2,1)S(1)}, bf16[64,512]{1,0:T(8,128)(2,1)S(1)}, u32[]{:S(2)}, u32[]{:S(2)}) collective-permute-start(bf16[64,512]{1,0:T(8,128)(2,1)S(1)} %shard_map.44), channel_id=1, source_target_pairs={{0,2},{1,3},{2,0},{3,1},{4,6},{5,7},{6,4},{7,5},{8,10},{9,11},{10,... | collective-permute-start | bytes 196616 | tf_op jit(solution)/shard_map/ppermute | solution.py:227
  56.6 1.6 %collective-permute-start.20 = (bf16[256,512]{1,0:T(8,128)(2,1)S(1)}, bf16[256,512]{1,0:T(8,128)(2,1)S(1)}, u32[]{:S(2)}, u32[]{:S(2)}) collective-permute-start(bf16[256,512]{1,0:T(8,128)(2,1)S(1)} %pad_maximum_fusion.2.near), channel_id=1, source_target_pairs={{0,1},{1,0},{2,3},{3,2},{4,5},{5,4},{6,7},{7,6},{8,9},{9,8},{10,11... | collective-permute-start | bytes 786440 | tf_op jit(solution)/shard_map/ppermute | solution.py:227
  58.8 30.7 %collective-permute-start.30 = (bf16[512,1024]{1,0:T(8,128)(2,1)S(1)}, bf16[512,1024]{1,0:T(8,128)(2,1)S(1)}, u32[]{:S(2)}, u32[]{:S(2)}) collective-permute-start(bf16[512,1024]{1,0:T(8,128)(2,1)S(1)} %get-tuple-element.62), channel_id=1, source_target_pairs={{8,0},{16,24},{9,1},{17,25},{10,2},{18,26},{11,3},{19,27},{12,4},{... | collective-permute-start | bytes 3145736 | tf_op jit(solution)/shard_map/ppermute | solution.py:303
  60.2 29.3 %collective-permute-start.31 = (bf16[512,1024]{1,0:T(8,128)(2,1)S(1)}, bf16[512,1024]{1,0:T(8,128)(2,1)S(1)}, u32[]{:S(2)}, u32[]{:S(2)}) collective-permute-start(bf16[512,1024]{1,0:T(8,128)(2,1)S(1)} %get-tuple-element.63), channel_id=1, source_target_pairs={{8,16},{16,8},{9,17},{17,9},{10,18},{18,10},{11,19},{19,11},{12,20... | collective-permute-start | bytes 3145736 | tf_op jit(solution)/shard_map/ppermute | solution.py:303
  69.8 4.3 %collective-permute-start.23 = (bf16[64,512]{1,0:T(8,128)(2,1)S(1)}, bf16[64,512]{1,0:T(8,128)(2,1)S(1)}, u32[]{:S(2)}, u32[]{:S(2)}) collective-permute-start(bf16[64,512]{1,0:T(8,128)(2,1)S(1)} %get-tuple-element.69), channel_id=1, source_target_pairs={{0,2},{1,3},{2,0},{3,1},{4,6},{5,7},{6,4},{7,5},{8,10},{9,11},{10,... | collective-permute-start | bytes 196616 | tf_op jit(solution)/shard_map/ppermute | solution.py:227
  71.3 6.6 %collective-permute-start.24 = (bf16[64,512]{1,0:T(8,128)(2,1)S(1)}, bf16[64,512]{1,0:T(8,128)(2,1)S(1)}, u32[]{:S(2)}, u32[]{:S(2)}) collective-permute-start(bf16[64,512]{1,0:T(8,128)(2,1)S(1)} %get-tuple-element.70), channel_id=1, source_target_pairs={{0,4},{1,5},{2,6},{3,7},{4,0},{5,1},{6,2},{7,3},{8,12},{9,13},{10,... | collective-permute-start | bytes 196616 | tf_op jit(solution)/shard_map/ppermute | solution.py:227
  72.6 5.4 %collective-permute-start.25 = (bf16[64,512]{1,0:T(8,128)(2,1)S(1)}, bf16[64,512]{1,0:T(8,128)(2,1)S(1)}, u32[]{:S(2)}, u32[]{:S(2)}) collective-permute-start(bf16[64,512]{1,0:T(8,128)(2,1)S(1)} %get-tuple-element.71), channel_id=1, source_target_pairs={{0,6},{1,7},{2,4},{3,5},{4,2},{5,3},{6,0},{7,1},{8,14},{9,15},{10,... | collective-permute-start | bytes 196616 | tf_op jit(solution)/shard_map/ppermute | solution.py:227
  74.1 3.9 %collective-permute-start.26 = (bf16[64,512]{1,0:T(8,128)(2,1)S(1)}, bf16[64,512]{1,0:T(8,128)(2,1)S(1)}, u32[]{:S(2)}, u32[]{:S(2)}) collective-permute-start(bf16[64,512]{1,0:T(8,128)(2,1)S(1)} %shard_map.44), channel_id=1, source_target_pairs={{0,8},{24,16},{1,9},{25,17},{2,10},{26,18},{3,11},{27,19},{4,12},{... | collective-permute-start | bytes 196616 | tf_op jit(solution)/shard_map/ppermute | solution.py:298
  78.1 6.9 %collective-permute-start.29 = (bf16[64,1024]{1,0:T(8,128)(2,1)S(1)}, bf16[64,1024]{1,0:T(8,128)(2,1)S(1)}, u32[]{:S(2)}, u32[]{:S(2)}) collective-permute-start(bf16[64,1024]{1,0:T(8,128)(2,1)S(1)} %pad_maximum_fusion.3), channel_id=1, source_target_pairs={{0,6},{1,7},{2,4},{3,5},{4,2},{5,3},{6,0},{7,1},{8,14},{9,15},{10,... | collective-permute-start | bytes 393224 | tf_op jit(solution)/shard_map/ppermute | solution.py:227
  80.5 6.0 %collective-permute-start.28 = (bf16[64,1024]{1,0:T(8,128)(2,1)S(1)}, bf16[64,1024]{1,0:T(8,128)(2,1)S(1)}, u32[]{:S(2)}, u32[]{:S(2)}) collective-permute-start(bf16[64,1024]{1,0:T(8,128)(2,1)S(1)} %pad_maximum_fusion.3), channel_id=1, source_target_pairs={{0,4},{1,5},{2,6},{3,7},{4,0},{5,1},{6,2},{7,3},{8,12},{9,13},{10,... | collective-permute-start | bytes 393224 | tf_op jit(solution)/shard_map/ppermute | solution.py:227
  81.2 5.4 %collective-permute-start.27 = (bf16[64,1024]{1,0:T(8,128)(2,1)S(1)}, bf16[64,1024]{1,0:T(8,128)(2,1)S(1)}, u32[]{:S(2)}, u32[]{:S(2)}) collective-permute-start(bf16[64,1024]{1,0:T(8,128)(2,1)S(1)} %pad_maximum_fusion.3), channel_id=1, source_target_pairs={{0,2},{1,3},{2,0},{3,1},{4,6},{5,7},{6,4},{7,5},{8,10},{9,11},{10,... | collective-permute-start | bytes 393224 | tf_op jit(solution)/shard_map/ppermute | solution.py:227
  89.5 1.9 %collective-permute-start.32 = (bf16[256,1024]{1,0:T(8,128)(2,1)S(1)}, bf16[256,1024]{1,0:T(8,128)(2,1)S(1)}, u32[]{:S(2)}, u32[]{:S(2)}) collective-permute-start(bf16[256,1024]{1,0:T(8,128)(2,1)S(1)} %pad_maximum_fusion.near), channel_id=1, source_target_pairs={{0,1},{1,0},{2,3},{3,2},{4,5},{5,4},{6,7},{7,6},{8,9},{9,8},{10,11... | collective-permute-start | bytes 1572872 | tf_op jit(solution)/shard_map/ppermute | solution.py:227
  (2 other events, 18.3 us)

commit v14 on v13

--- a/solution.py
+++ b/solution.py
@@ -160,18 +160,14 @@
         out[pl.ds(pl.multiple_of(order[4 + k] * eighth, eighth), eighth), :] = far[here, :]
 
 
-def place_kernel(order, near, far, out):
-    place_into(out, order, near, far)
-
-
 def push_kernel(
-    order, middle, near, far, beside, opposite, beside_square, opposite_square, inner, out, over
+    order, middle, near, far, beside, opposite, beside_square, opposite_square, out, over, inner
 ):
-    place_into(inner, order, near, far)
     width = beside.shape[1]
 
     @pl.when(middle[0] == 1)
     def _():
+        place_into(inner, order, near, far)
         for k in range(2):
             here = slice(k * width // 2, (k + 1) * width // 2)
             outward = dot(inner[...], opposite[:, here])
@@ -187,10 +183,11 @@
 
 
 def held_kernel(
-    total, with_own, own, z, other,
-    own_square, beside_square, opposite_square, mean, spread, held,
+    total, order, near, far, own, z, other,
+    own_square, beside_square, opposite_square, mean, spread, held, with_own,
 ):
     rows, width = own.shape
+    place_into(with_own, order, near, far)
     norm = jnp.sum(with_own[:, rows:].astype(jnp.float32), axis=1, keepdims=True)
     for k in range(4):
         here = slice(k * width // 4, (k + 1) * width // 4)
@@ -206,21 +203,21 @@
 
 
 def last_kernel(
-    total, order, middle, first, near, far, beside, opposite, held, out, over, result, second
+    total, order, middle, near, far, beside, opposite, held, out, over, result, second
 ):
     rows, width = beside.shape
     place_into(second, order, near, far)
 
-    def put(product_of, with_beside, arrived):
+    def put(product_of, arrived):
         for k in range(4):
             here = slice(k * width // 4, (k + 1) * width // 4)
-            product = product_of(with_beside, beside[:, here])
+            product = product_of(second[:, rows:], beside[:, here])
             product = product + dot(second[:, :rows], opposite[:, here])
             product = product + arrived[:, here].astype(jnp.float32)
             result[:, here] = held[:, here] + coefficient(total) * product
 
-    pl.when(middle[0] == 1)(lambda: put(dot_t, second[:, rows:], over))
-    pl.when(middle[0] == 0)(lambda: put(dot, first[...], out))
+    pl.when(middle[0] == 1)(lambda: put(dot_t, over))
+    pl.when(middle[0] == 0)(lambda: put(dot, out))
 
 
 def to_partner(x, step):
@@ -242,15 +239,16 @@
     )[0]
 
 
+def pile_kernel(*refs):
+    *pieces, out = refs
+    rows = pieces[0].shape[0]
+    for k, piece in enumerate(pieces):
+        out[k * rows:(k + 1) * rows, :] = piece[...]
+
+
 def gather_chips(x):
-    return jnp.concatenate([x] + [to_partner(x, 2 * k) for k in (1, 2, 3)])
-
-
-def gather_cores(near, order):
-    shape = (2 * near.shape[0], near.shape[1])
-    return kernel_call(place_kernel, [(shape, jnp.bfloat16)], smem=1)(
-        order, near, to_partner(near, 1)
-    )[0]
+    pile = [((4 * x.shape[0], x.shape[1]), x.dtype)]
+    return kernel_call(pile_kernel, pile)(x, *(to_partner(x, 2 * k) for k in (1, 2, 3)))[0]
 
 
 def after(x, *others):
@@ -272,8 +270,8 @@
         lax.ppermute(stats, "dp", [(i, (i + k) % 4) for i in range(4)]) for k in (1, 2, 3)
     ]
     ahead = after(z_anchor, stats)
+    beside_in = lax.ppermute(ahead, "dp", [(i, i ^ 1) for i in range(4)])
     swapped = lax.ppermute(ahead, "dp", across)
-    beside_in = lax.ppermute(ahead, "dp", [(i, i ^ 1) for i in range(4)])
     mean = (all_stats[0][:1] + all_stats[1][:1] + all_stats[2][:1] + all_stats[3][:1]) / 4
     spread = 0.0
     for one in all_stats:
@@ -286,20 +284,26 @@
     own, turned, own_square, kept, sent = kernel_call(
         own_kernel, [block, block, flat, *summands(rows + NORM)], smem=1, scratch=12
     )(order, z_anchor, mean)
-    with_own = gather_chips(scatter(*halve(kept, sent, rows), last=rows))
-    with_own = gather_cores(with_own, order)
-    end = lax.ppermute(after(z_anchor, beside_in, swapped, with_own), "dp", [(0, 3), (3, 0)])
+    near_own = gather_chips(scatter(*halve(kept, sent, rows), last=rows))
+    end = lax.ppermute(after(z_anchor, beside_in, swapped, near_own), "dp", [(0, 3), (3, 0)])
 
     beside, beside_square, swapped, swapped_square, kept, sent = kernel_call(
         first_kernel, [block, flat, block, flat, *summands(rows)],
         smem=2, scratch=12, temps=[block],
-    )(order, middle, after(turned, with_own), beside_in, swapped, mean)
+    )(order, middle, after(turned, near_own), beside_in, swapped, mean)
     first = scatter(*halve(kept, sent))
     crossed = lax.ppermute(first, "dp", [(0, 1), (3, 2)])
-    near = gather_chips(first)
-    first, *ready = kernel_call(
-        push_kernel, [((rows, rows), jnp.bfloat16), block, block], smem=2, scratch=12
-    )(order, middle, near, to_partner(near, 1), beside, swapped, beside_square, swapped_square)
+
+    def gather(x):
+        near = gather_chips(x)
+        return near, to_partner(near, 1)
+
+    near, far = lax.cond(
+        middle[0] == 1, gather, lambda x: (jnp.zeros((half, rows), x.dtype),) * 2, first
+    )
+    ready = kernel_call(
+        push_kernel, [block, block], smem=2, scratch=12, temps=[((rows, rows), jnp.bfloat16)]
+    )(order, middle, near, far, beside, swapped, beside_square, swapped_square)
     pushed = [lax.ppermute(x, "dp", p) for x, p in zip(ready, (outward, across))]
 
     opposite, opposite_square, kept, sent = kernel_call(
@@ -307,17 +311,21 @@
     )(middle, after(turned, *ready), swapped, swapped_square, end, mean)
     halved = halve(kept, sent)
     result = ((rows, width), jnp.float32)
-    held = kernel_call(functools.partial(held_kernel, total), [result], scratch=12)(
-        with_own, own, z_anchor, z_other,
+    held = kernel_call(
+        functools.partial(held_kernel, total), [result],
+        smem=1, scratch=12, temps=[((rows, rows + NORM), jnp.bfloat16)],
+    )(
+        order, near_own, to_partner(near_own, 1), own, z_anchor, z_other,
         own_square, beside_square, after(opposite_square, halved[0]), mean, spread,
     )[0]
+    crossed = jnp.where(middle == 1, crossed, first)
     second = jnp.concatenate([scatter(*halved), crossed], axis=1)
     near = after(gather_chips(after(second, held)), *pushed)
     return kernel_call(
         functools.partial(last_kernel, total), [result],
         smem=2, scratch=12, temps=[((rows, 2 * rows), jnp.bfloat16)],
     )(
-        order, middle, first, near, to_partner(near, 1), beside, opposite, held, *pushed
+        order, middle, near, to_partner(near, 1), beside, opposite, held, *pushed
     )[0]
 
 

time: 95.1 us -> 120 us (1.26)
  the two profiles are of different devices: /device:TPU:0 before, /device:TPU:9 now
where the time goes in v14:
time: 120 us; the launch traced here: 119 us
  waiting for transfers between devices  53.5 us (45%)
  starting transfers between devices  38 us (32%)
  Pallas kernels  20.1 us (17%)
  local copies, waits for them, and re-layouts  6.6 us (6%)
    ppermute x24, waiting for transfers between devices, to_partner(): return lax.ppermute(x, 'feat', [(i, i ^ step) for i in range(8)])  25.2 us
    ppermute x24, starting transfers between devices, to_partner(): return lax.ppermute(x, 'feat', [(i, i ^ step) for i in range(8)])  24.2 us
    ppermute x3, waiting for transfers between devices, by_line(): lax.ppermute(stats, 'dp', [(i, (i + k) % 4) for i in range(4)])  21.3 us
    pallas_call x16, Pallas kernels, call(): pl.pallas_call(body, out_shape=[jax.ShapeDtypeStruct(s, t) for s, t in ou...  20.1 us
    unnamed x28, local copies, waits for them, and re-layouts  6.6 us
    ppermute x2, starting transfers between devices, by_line(): lax.ppermute(x, 'dp', p)  4.76 us
    ppermute x1, starting transfers between devices, by_line(): swapped = lax.ppermute(ahead, 'dp', across)  4.48 us
    ppermute x2, waiting for transfers between devices, by_line(): lax.ppermute(x, 'dp', p)  3.94 us
  transfers between devices with their start and end apart: 33, of which 26 were waited for; matrix products, arithmetic and copies ran while one was open for 1% of the time, Pallas kernels for 13%

profile of v14, /device:TPU:9, one launch (start us, length us, event | category | flops | bytes accessed | tf_op | source)
XLA Modules:
  0.0 119.1 jit_solution(4635647091057846380)
XLA Ops:
  0.0 1.8 %shard_map.37 = f32[2,1024]{1,0:T(2,128)S(1)} custom-call(bf16[512,1024]{1,0:T(8,128)(2,1)} %z.5), custom_call_target="tpu_custom_call" | custom-call | tf_op jit(solution)/shard_map/pallas_call | solution.py:17
  1.9 4.5 %collective-permute-start.15 = (bf16[512,1024]{1,0:T(8,128)(2,1)}, bf16[512,1024]{1,0:T(8,128)(2,1)S(1)}, u32[]{:S(2)}, u32[]{:S(2)}) collective-permute-start(bf16[512,1024]{1,0:T(8,128)(2,1)} %z.5), channel_id=1, source_target_pairs={{8,16},{16,8},{9,17},{17,9},{10,18},{18,10},{11,19},{19,11},{12,20... | collective-permute-start | bytes 3145736 | tf_op jit(solution)/shard_map/ppermute | solution.py:274
  8.6 20.0 %collective-permute-done.4 = f32[2,1024]{1,0:T(2,128)S(1)} collective-permute-done((f32[2,1024]{1,0:T(2,128)S(1)}, f32[2,1024]{1,0:T(2,128)S(1)}, u32[]{:S(2)}, u32[]{:S(2)}) %collective-permute-start.4) | collective-permute-done | bytes 8224 | tf_op jit(solution)/shard_map/ppermute | solution.py:270
  29.9 2.4 %shard_map.38 = (bf16[512,1024]{1,0:T(8,128)(2,1)S(1)}, bf16[512,1024]{1,0:T(8,128)(2,1)S(1)}, f32[1,1024]{1,0:T(1,128)S(1)}, f32[256,640]{1,0:T(8,128)S(1)}, bf16[256,640]{1,0:T(8,128)(2,1)S(1)}) custom-call(s32[8]{0:T(128)S(1)} %broadcast_xor_fusion.order, bf16[512,1024]{1,0:T(8,128)(2,1)} %z.5, f32[1,1024]{1,0:T(1,128)S(1)} %get-tuple-element.83.mean), custom_call_target="tpu_custom_call" | custom-call | tf_op jit(solution)/shard_map/pallas_call | solution.py:17
  32.3 1.6 %collective-permute-start.7 = (bf16[256,640]{1,0:T(8,128)(2,1)S(1)}, bf16[256,640]{1,0:T(8,128)(2,1)S(1)}, u32[]{:S(2)}, u32[]{:S(2)}) collective-permute-start(bf16[256,640]{1,0:T(8,128)(2,1)S(1)} %get-tuple-element.46), channel_id=1, source_target_pairs={{0,1},{1,0},{2,3},{3,2},{4,5},{5,4},{6,7},{7,6},{8,9},{9,8},{10,11... | collective-permute-start | bytes 983048 | tf_op jit(solution)/shard_map/ppermute | solution.py:224
  35.3 2.2 %collective-permute-start.10 = (bf16[64,640]{1,0:T(8,128)(2,1)S(1)}, bf16[64,640]{1,0:T(8,128)(2,1)S(1)}, u32[]{:S(2)}, u32[]{:S(2)}) collective-permute-start(bf16[64,640]{1,0:T(8,128)(2,1)S(1)} %get-tuple-element.50), channel_id=1, source_target_pairs={{0,6},{1,7},{2,4},{3,5},{4,2},{5,3},{6,0},{7,1},{8,14},{9,15},{10,... | collective-permute-start | bytes 245768 | tf_op jit(solution)/shard_map/ppermute | solution.py:224
  38.0 1.9 %collective-permute-done.10.c = bf16[64,640]{1,0:T(8,128)(2,1)S(1)} collective-permute-done((bf16[64,640]{1,0:T(8,128)(2,1)S(1)}, bf16[64,640]{1,0:T(8,128)(2,1)S(1)}, u32[]{:S(2)}, u32[]{:S(2)}) %collective-permute-start.10) | collective-permute-done | bytes 81952 | tf_op jit(solution)/shard_map/ppermute | solution.py:224
  39.9 2.0 %collective-permute-done.8.a = bf16[64,640]{1,0:T(8,128)(2,1)S(1)} collective-permute-done((bf16[64,640]{1,0:T(8,128)(2,1)S(1)}, bf16[64,640]{1,0:T(8,128)(2,1)S(1)}, u32[]{:S(2)}, u32[]{:S(2)}) %collective-permute-start.8) | collective-permute-done | bytes 81952 | tf_op jit(solution)/shard_map/ppermute | solution.py:224
  45.4 1.4 %collective-permute-done.12.refs_2_ = bf16[64,640]{1,0:T(8,128)(2,1)S(1)} collective-permute-done((bf16[64,640]{1,0:T(8,128)(2,1)S(1)}, bf16[64,640]{1,0:T(8,128)(2,1)S(1)}, u32[]{:S(2)}, u32[]{:S(2)}) %collective-permute-start.12) | collective-permute-done | bytes 81952 | tf_op jit(solution)/shard_map/ppermute | solution.py:224
  46.9 2.0 %collective-permute-done.13.refs_3_ = bf16[64,640]{1,0:T(8,128)(2,1)S(1)} collective-permute-done((bf16[64,640]{1,0:T(8,128)(2,1)S(1)}, bf16[64,640]{1,0:T(8,128)(2,1)S(1)}, u32[]{:S(2)}, u32[]{:S(2)}) %collective-permute-start.13) | collective-permute-done | bytes 81952 | tf_op jit(solution)/shard_map/ppermute | solution.py:224
  50.9 1.6 %collective-permute-start.20 = (bf16[512,1024]{1,0:T(8,128)(2,1)}, bf16[512,1024]{1,0:T(8,128)(2,1)}, u32[]{:S(2)}, u32[]{:S(2)}) collective-permute-start(bf16[512,1024]{1,0:T(8,128)(2,1)} %z.5), channel_id=1, source_target_pairs={{0,24},{24,0},{1,25},{25,1},{2,26},{26,2},{3,27},{27,3},{4,28},{28... | collective-permute-start | bytes 3145736 | tf_op jit(solution)/shard_map/ppermute | solution.py:288
  55.0 1.5 %shard_map.42 = (bf16[512,1024]{1,0:T(8,128)(2,1)S(1)}, f32[1,1024]{1,0:T(1,128)S(1)}, bf16[512,1024]{1,0:T(8,128)(2,1)S(1)}, f32[1,1024]{1,0:T(1,128)S(1)}, f32...) custom-call(s32[8]{0:T(128)S(1)} %broadcast_xor_fusion.order, s32[1]{0:T(128)} %bitcast.middle, ...), custom_call_target="tpu_custom_call" | custom-call | tf_op jit(solution)/shard_map/pallas_call | solution.py:17
  56.5 2.6 %collective-permute-start.16 = (bf16[256,512]{1,0:T(8,128)(2,1)S(1)}, bf16[256,512]{1,0:T(8,128)(2,1)S(1)}, u32[]{:S(2)}, u32[]{:S(2)}) collective-permute-start(bf16[256,512]{1,0:T(8,128)(2,1)S(1)} %get-tuple-element.54), channel_id=1, source_target_pairs={{0,1},{1,0},{2,3},{3,2},{4,5},{5,4},{6,7},{7,6},{8,9},{9,8},{10,11... | collective-permute-start | bytes 786440 | tf_op jit(solution)/shard_map/ppermute | solution.py:224
  62.4 1.9 %collective-permute-start.19 = (bf16[64,512]{1,0:T(8,128)(2,1)}, bf16[64,512]{1,0:T(8,128)(2,1)}, u32[]{:S(2)}, u32[]{:S(2)}) collective-permute-start(bf16[64,512]{1,0:T(8,128)(2,1)} %get-tuple-element.58), channel_id=1, source_target_pairs={{0,6},{1,7},{2,4},{3,5},{4,2},{5,3},{6,0},{7,1},{8,14},{9,15},{10,... | collective-permute-start | bytes 196616 | tf_op jit(solution)/shard_map/ppermute | solution.py:224
  65.5 1.4 %collective-permute-done.19.c = bf16[64,512]{1,0:T(8,128)(2,1)} collective-permute-done((bf16[64,512]{1,0:T(8,128)(2,1)}, bf16[64,512]{1,0:T(8,128)(2,1)}, u32[]{:S(2)}, u32[]{:S(2)}) %collective-permute-start.19) | collective-permute-done | bytes 65568 | tf_op jit(solution)/shard_map/ppermute | solution.py:224
  67.8 1.5 %shard_map.44 = bf16[64,512]{1,0:T(8,128)(2,1)} custom-call(f32[64,512]{1,0:T(8,128)S(1)} %copy-done.8, bf16[64,512]{1,0:T(8,128)(2,1)S(1)} %collective-permute-done.17.a, bf16[64,512]{1,0:T(8,128)(2,1)} %collective-permute-done.18.b, bf16[64,512]{1,0:T(8,128)(2,1)} %collective-permute-done.19.c), custom_call_target="tpu_custom_call" | custom-call | tf_op jit(solution)/shard_map/pallas_call | solution.py:17
  69.3 13.1 %conditional.1 = (bf16[256,512]{1,0:T(8,128)(2,1)}, bf16[256,512]{1,0:T(8,128)(2,1)}) conditional(s32[]{:T(128)} %convert_element_type.7, () %tuple.20, bf16[64,512]{1,0:T(8,128)(2,1)} %shard_map.44), branch_computations={%region_0.0_spmd, %region_1.0_spmd} | conditional | bytes 1835184 | solution.py:301
  73.8 2.3 %collective-permute-done.2.refs_3_ = bf16[64,512]{1,0:T(8,128)(2,1)S(1)} collective-permute-done((bf16[64,512]{1,0:T(8,128)(2,1)}, bf16[64,512]{1,0:T(8,128)(2,1)S(1)}, u32[]{:S(2)}, u32[]{:S(2)}) %collective-permute-start.2) | collective-permute-done | bytes 65568 | tf_op jit(solution)/shard_map/cond/branch_1_fun/ppermute | solution.py:224
  76.1 1.6 %branch_1_fun.1 = bf16[256,512]{1,0:T(8,128)(2,1)} custom-call(bf16[64,512]{1,0:T(8,128)(2,1)} %refs_0_, bf16[64,512]{1,0:T(8,128)(2,1)S(1)} %collective-permute-done.refs_1_, bf16[64,512]{1,0:T(8,128)(2,1)S(1)} %collective-permute-done.1.refs_2_, bf16[64,512]{1,0:T(8,128)(2,1)S(1)} %collective-permute-done.2.refs_3_), custom_call_target="tpu_custom_call" | custom-call | tf_op jit(solution)/shard_map/cond/branch_1_fun/pallas_call | solution.py:17
  77.7 3.2 %collective-permute-start.3 = (bf16[256,512]{1,0:T(8,128)(2,1)}, bf16[256,512]{1,0:T(8,128)(2,1)}, u32[]{:S(2)}, u32[]{:S(2)}) collective-permute-start(bf16[256,512]{1,0:T(8,128)(2,1)} %branch_1_fun.1), channel_id=1, source_target_pairs={{0,1},{1,0},{2,3},{3,2},{4,5},{5,4},{6,7},{7,6},{8,9},{9,8},{10,11... | collective-permute-start | bytes 786440 | tf_op jit(solution)/shard_map/cond/branch_1_fun/ppermute | solution.py:224
  80.9 1.5 %collective-permute-done.3 = bf16[256,512]{1,0:T(8,128)(2,1)} collective-permute-done((bf16[256,512]{1,0:T(8,128)(2,1)}, bf16[256,512]{1,0:T(8,128)(2,1)}, u32[]{:S(2)}, u32[]{:S(2)}) %collective-permute-start.3) | collective-permute-done | bytes 262176 | tf_op jit(solution)/shard_map/cond/branch_1_fun/ppermute | solution.py:224
  83.0 2.3 %shard_map.45 = (bf16[512,1024]{1,0:T(8,128)(2,1)S(1)}, bf16[512,1024]{1,0:T(8,128)(2,1)S(1)}) custom-call(s32[8]{0:T(128)S(1)} %copy-done.10, s32[1]{0:T(128)} %bitcast.middle, bf16[256,512]{1,0:T(8,128)(2,1)} %get-tuple-element.59.near, bf16[256,512]{1,0:T(8,128)(2,1)} %get-tuple-element.60.far, bf16[512,1024]{1,0:T(8,128)(2,1)S(1)} %get-tuple-element.61.beside, ...), custom_call_target="tpu_custom_call" | custom-call | tf_op jit(solution)/shard_map/pallas_call | solution.py:17
  85.4 1.5 %collective-permute-start.30 = (bf16[512,1024]{1,0:T(8,128)(2,1)S(1)}, bf16[512,1024]{1,0:T(8,128)(2,1)S(1)}, u32[]{:S(2)}, u32[]{:S(2)}) collective-permute-start(bf16[512,1024]{1,0:T(8,128)(2,1)S(1)} %get-tuple-element.65), channel_id=1, source_target_pairs={{8,0},{16,24},{9,1},{17,25},{10,2},{18,26},{11,3},{19,27},{12,4},{... | collective-permute-start | bytes 3145736 | tf_op jit(solution)/shard_map/ppermute | solution.py:307
  86.9 3.3 %collective-permute-start.31 = (bf16[512,1024]{1,0:T(8,128)(2,1)S(1)}, bf16[512,1024]{1,0:T(8,128)(2,1)S(1)}, u32[]{:S(2)}, u32[]{:S(2)}) collective-permute-start(bf16[512,1024]{1,0:T(8,128)(2,1)S(1)} %get-tuple-element.66), channel_id=1, source_target_pairs={{8,16},{16,8},{9,17},{17,9},{10,18},{18,10},{11,19},{19,11},{12,20... | collective-permute-start | bytes 3145736 | tf_op jit(solution)/shard_map/ppermute | solution.py:307
  90.9 2.0 %shard_map.46 = (bf16[512,1024]{1,0:T(8,128)(2,1)S(1)}, f32[1,1024]{1,0:T(1,128)S(1)}, f32[256,512]{1,0:T(8,128)S(1)}, bf16[256,512]{1,0:T(8,128)(2,1)S(1)}) custom-call(s32[1]{0:T(128)} %bitcast.middle, bf16[512,1024]{1,0:T(8,128)(2,1)S(1)} %get-tuple-element.67.turned, bf16[512,1024]{1,0:T(8,128)(2,1)S(1)} %get-tuple-element.62.opposite.swapped, ...), custom_call_target="tpu_custom_call" | custom-call | tf_op jit(solution)/shard_map/pallas_call | solution.py:17
  95.4 3.1 %collective-permute-done.25 = bf16[64,512]{1,0:T(8,128)(2,1)S(1)} collective-permute-done((bf16[64,512]{1,0:T(8,128)(2,1)}, bf16[64,512]{1,0:T(8,128)(2,1)S(1)}, u32[]{:S(2)}, u32[]{:S(2)}) %collective-permute-start.25) | collective-permute-done | bytes 65568 | tf_op jit(solution)/shard_map/ppermute | solution.py:295
  99.1 2.6 %shard_map.49.held = f32[512,1024]{1,0:T(8,128)S(1)} custom-call(s32[8]{0:T(128)S(1)} %copy-done.11, bf16[256,640]{1,0:T(8,128)(2,1)S(1)} %shard_map.41.near, bf16[256,640]{1,0:T(8,128)(2,1)S(1)} %collective-permute-done.26.far, bf16[512,1024]{1,0:T(8,128)(2,1)S(1)} %copy-done.6, bf16[512,1024]{1,0:T(8,128)(2,1)} %z.5, bf16[512,1024]{1,0:T(8,128)(2,1)S(1)} %copy-done.4, ...), custom_call_target="tpu_custom_call" | custom-call | tf_op jit(solution)/shard_map/pallas_call | solution.py:17
  105.3 1.5 %collective-permute-done.27.refs_1_ = bf16[64,1024]{1,0:T(8,128)(2,1)S(1)} collective-permute-done((bf16[64,1024]{1,0:T(8,128)(2,1)S(1)}, bf16[64,1024]{1,0:T(8,128)(2,1)S(1)}, u32[]{:S(2)}, u32[]{:S(2)}) %collective-permute-start.27) | collective-permute-done | bytes 131104 | tf_op jit(solution)/shard_map/ppermute | solution.py:224
  107.2 2.0 %collective-permute-done.29.refs_3_ = bf16[64,1024]{1,0:T(8,128)(2,1)S(1)} collective-permute-done((bf16[64,1024]{1,0:T(8,128)(2,1)S(1)}, bf16[64,1024]{1,0:T(8,128)(2,1)S(1)}, u32[]{:S(2)}, u32[]{:S(2)}) %collective-permute-start.29) | collective-permute-done | bytes 131104 | tf_op jit(solution)/shard_map/ppermute | solution.py:224
  109.3 3.9 %collective-permute-done.31.over = bf16[512,1024]{1,0:T(8,128)(2,1)S(1)} collective-permute-done((bf16[512,1024]{1,0:T(8,128)(2,1)S(1)}, bf16[512,1024]{1,0:T(8,128)(2,1)S(1)}, u32[]{:S(2)}, u32[]{:S(2)}) %collective-permute-start.31) | collective-permute-done | bytes 1048608 | tf_op jit(solution)/shard_map/ppermute | solution.py:307
  114.4 1.5 %collective-permute-done.32.far = bf16[256,1024]{1,0:T(8,128)(2,1)S(1)} collective-permute-done((bf16[256,1024]{1,0:T(8,128)(2,1)S(1)}, bf16[256,1024]{1,0:T(8,128)(2,1)S(1)}, u32[]{:S(2)}, u32[]{:S(2)}) %collective-permute-start.32) | collective-permute-done | bytes 524320 | tf_op jit(solution)/shard_map/ppermute | solution.py:224
  115.9 3.2 %shard_map.51 = f32[512,1024]{1,0:T(8,128)} custom-call(s32[8]{0:T(128)S(1)} %copy-done.11, s32[1]{0:T(128)} %bitcast.middle, bf16[256,1024]{1,0:T(8,128)(2,1)S(1)} %shard_map.50.near, bf16[256,1024]{1,0:T(8,128)(2,1)S(1)} %collective-permute-done.32.far, bf16[512,1024]{1,0:T(8,128)(2,1)S(1)} %get-tuple-element.61.beside, ...), custom_call_target="tpu_custom_call" | custom-call | tf_op jit(solution)/shard_map/pallas_call | solution.py:17
  (83 shorter events, 32.8 us)
Async XLA Ops:
  1.8 47.1 %collective-permute-start.14 = (bf16[512,1024]{1,0:T(8,128)(2,1)}, bf16[512,1024]{1,0:T(8,128)(2,1)S(1)}, u32[]{:S(2)}, u32[]{:S(2)}) collective-permute-start(bf16[512,1024]{1,0:T(8,128)(2,1)} %z.5), channel_id=1, source_target_pairs={{0,8},{8,0},{16,24},{24,16},{1,9},{9,1},{17,25},{25,17},{2,10},{10... | collective-permute-start | bytes 3145736 | tf_op jit(solution)/shard_map/ppermute | solution.py:273
  1.9 48.0 %collective-permute-start.15 = (bf16[512,1024]{1,0:T(8,128)(2,1)}, bf16[512,1024]{1,0:T(8,128)(2,1)S(1)}, u32[]{:S(2)}, u32[]{:S(2)}) collective-permute-start(bf16[512,1024]{1,0:T(8,128)(2,1)} %z.5), channel_id=1, source_target_pairs={{8,16},{16,8},{9,17},{17,9},{10,18},{18,10},{11,19},{19,11},{12,20... | collective-permute-start | bytes 3145736 | tf_op jit(solution)/shard_map/ppermute | solution.py:274
  6.4 22.2 %collective-permute-start.4 = (f32[2,1024]{1,0:T(2,128)S(1)}, f32[2,1024]{1,0:T(2,128)S(1)}, u32[]{:S(2)}, u32[]{:S(2)}) collective-permute-start(f32[2,1024]{1,0:T(2,128)S(1)} %shard_map.37), channel_id=1, source_target_pairs={{0,8},{8,16},{16,24},{24,0},{1,9},{9,17},{17,25},{25,1},{2,10},{10... | collective-permute-start | bytes 24584 | tf_op jit(solution)/shard_map/ppermute | solution.py:270
  6.4 22.3 %collective-permute-start.5 = (f32[2,1024]{1,0:T(2,128)S(1)}, f32[2,1024]{1,0:T(2,128)S(1)}, u32[]{:S(2)}, u32[]{:S(2)}) collective-permute-start(f32[2,1024]{1,0:T(2,128)S(1)} %shard_map.37), channel_id=1, source_target_pairs={{0,16},{8,24},{16,0},{24,8},{1,17},{9,25},{17,1},{25,9},{2,18},{10... | collective-permute-start | bytes 24584 | tf_op jit(solution)/shard_map/ppermute | solution.py:270
  6.5 23.3 %collective-permute-start.6 = (f32[2,1024]{1,0:T(2,128)S(1)}, f32[2,1024]{1,0:T(2,128)S(1)}, u32[]{:S(2)}, u32[]{:S(2)}) collective-permute-start(f32[2,1024]{1,0:T(2,128)S(1)} %shard_map.37), channel_id=1, source_target_pairs={{0,24},{8,0},{16,8},{24,16},{1,25},{9,1},{17,9},{25,17},{2,26},{10... | collective-permute-start | bytes 24584 | tf_op jit(solution)/shard_map/ppermute | solution.py:270
  32.3 2.9 %collective-permute-start.7 = (bf16[256,640]{1,0:T(8,128)(2,1)S(1)}, bf16[256,640]{1,0:T(8,128)(2,1)S(1)}, u32[]{:S(2)}, u32[]{:S(2)}) collective-permute-start(bf16[256,640]{1,0:T(8,128)(2,1)S(1)} %get-tuple-element.46), channel_id=1, source_target_pairs={{0,1},{1,0},{2,3},{3,2},{4,5},{5,4},{6,7},{7,6},{8,9},{9,8},{10,11... | collective-permute-start | bytes 983048 | tf_op jit(solution)/shard_map/ppermute | solution.py:224
  35.3 4.6 %collective-permute-start.10 = (bf16[64,640]{1,0:T(8,128)(2,1)S(1)}, bf16[64,640]{1,0:T(8,128)(2,1)S(1)}, u32[]{:S(2)}, u32[]{:S(2)}) collective-permute-start(bf16[64,640]{1,0:T(8,128)(2,1)S(1)} %get-tuple-element.50), channel_id=1, source_target_pairs={{0,6},{1,7},{2,4},{3,5},{4,2},{5,3},{6,0},{7,1},{8,14},{9,15},{10,... | collective-permute-start | bytes 245768 | tf_op jit(solution)/shard_map/ppermute | solution.py:224
  37.5 4.4 %collective-permute-start.8 = (bf16[64,640]{1,0:T(8,128)(2,1)S(1)}, bf16[64,640]{1,0:T(8,128)(2,1)S(1)}, u32[]{:S(2)}, u32[]{:S(2)}) collective-permute-start(bf16[64,640]{1,0:T(8,128)(2,1)S(1)} %get-tuple-element.48), channel_id=1, source_target_pairs={{0,2},{1,3},{2,0},{3,1},{4,6},{5,7},{6,4},{7,5},{8,10},{9,11},{10,... | collective-permute-start | bytes 245768 | tf_op jit(solution)/shard_map/ppermute | solution.py:224
  37.8 4.2 %collective-permute-start.9 = (bf16[64,640]{1,0:T(8,128)(2,1)S(1)}, bf16[64,640]{1,0:T(8,128)(2,1)S(1)}, u32[]{:S(2)}, u32[]{:S(2)}) collective-permute-start(bf16[64,640]{1,0:T(8,128)(2,1)S(1)} %get-tuple-element.49), channel_id=1, source_target_pairs={{0,4},{1,5},{2,6},{3,7},{4,0},{5,1},{6,2},{7,3},{8,12},{9,13},{10,... | collective-permute-start | bytes 245768 | tf_op jit(solution)/shard_map/ppermute | solution.py:224
  42.1 3.4 %collective-permute-start.11 = (bf16[64,640]{1,0:T(8,128)(2,1)S(1)}, bf16[64,640]{1,0:T(8,128)(2,1)S(1)}, u32[]{:S(2)}, u32[]{:S(2)}) collective-permute-start(bf16[64,640]{1,0:T(8,128)(2,1)S(1)} %shard_map.40.refs_0_), channel_id=1, source_target_pairs={{0,2},{1,3},{2,0},{3,1},{4,6},{5,7},{6,4},{7,5},{8,10},{9,11},{10,... | collective-permute-start | bytes 245768 | tf_op jit(solution)/shard_map/ppermute | solution.py:224
  43.3 3.6 %collective-permute-start.12 = (bf16[64,640]{1,0:T(8,128)(2,1)S(1)}, bf16[64,640]{1,0:T(8,128)(2,1)S(1)}, u32[]{:S(2)}, u32[]{:S(2)}) collective-permute-start(bf16[64,640]{1,0:T(8,128)(2,1)S(1)} %shard_map.40.refs_0_), channel_id=1, source_target_pairs={{0,4},{1,5},{2,6},{3,7},{4,0},{5,1},{6,2},{7,3},{8,12},{9,13},{10,... | collective-permute-start | bytes 245768 | tf_op jit(solution)/shard_map/ppermute | solution.py:224
  44.6 4.3 %collective-permute-start.13 = (bf16[64,640]{1,0:T(8,128)(2,1)S(1)}, bf16[64,640]{1,0:T(8,128)(2,1)S(1)}, u32[]{:S(2)}, u32[]{:S(2)}) collective-permute-start(bf16[64,640]{1,0:T(8,128)(2,1)S(1)} %shard_map.40.refs_0_), channel_id=1, source_target_pairs={{0,6},{1,7},{2,4},{3,5},{4,2},{5,3},{6,0},{7,1},{8,14},{9,15},{10,... | collective-permute-start | bytes 245768 | tf_op jit(solution)/shard_map/ppermute | solution.py:224
  50.9 40.0 %collective-permute-start.20 = (bf16[512,1024]{1,0:T(8,128)(2,1)}, bf16[512,1024]{1,0:T(8,128)(2,1)}, u32[]{:S(2)}, u32[]{:S(2)}) collective-permute-start(bf16[512,1024]{1,0:T(8,128)(2,1)} %z.5), channel_id=1, source_target_pairs={{0,24},{24,0},{1,25},{25,1},{2,26},{26,2},{3,27},{27,3},{4,28},{28... | collective-permute-start | bytes 3145736 | tf_op jit(solution)/shard_map/ppermute | solution.py:288
  56.5 3.8 %collective-permute-start.16 = (bf16[256,512]{1,0:T(8,128)(2,1)S(1)}, bf16[256,512]{1,0:T(8,128)(2,1)S(1)}, u32[]{:S(2)}, u32[]{:S(2)}) collective-permute-start(bf16[256,512]{1,0:T(8,128)(2,1)S(1)} %get-tuple-element.54), channel_id=1, source_target_pairs={{0,1},{1,0},{2,3},{3,2},{4,5},{5,4},{6,7},{7,6},{8,9},{9,8},{10,11... | collective-permute-start | bytes 786440 | tf_op jit(solution)/shard_map/ppermute | solution.py:224
  61.6 3.3 %collective-permute-start.17 = (bf16[64,512]{1,0:T(8,128)(2,1)}, bf16[64,512]{1,0:T(8,128)(2,1)S(1)}, u32[]{:S(2)}, u32[]{:S(2)}) collective-permute-start(bf16[64,512]{1,0:T(8,128)(2,1)} %get-tuple-element.56), channel_id=1, source_target_pairs={{0,2},{1,3},{2,0},{3,1},{4,6},{5,7},{6,4},{7,5},{8,10},{9,11},{10,... | collective-permute-start | bytes 196616 | tf_op jit(solution)/shard_map/ppermute | solution.py:224
  61.9 3.6 %collective-permute-start.18 = (bf16[64,512]{1,0:T(8,128)(2,1)}, bf16[64,512]{1,0:T(8,128)(2,1)}, u32[]{:S(2)}, u32[]{:S(2)}) collective-permute-start(bf16[64,512]{1,0:T(8,128)(2,1)} %get-tuple-element.57), channel_id=1, source_target_pairs={{0,4},{1,5},{2,6},{3,7},{4,0},{5,1},{6,2},{7,3},{8,12},{9,13},{10,... | collective-permute-start | bytes 196616 | tf_op jit(solution)/shard_map/ppermute | solution.py:224
  62.4 4.5 %collective-permute-start.19 = (bf16[64,512]{1,0:T(8,128)(2,1)}, bf16[64,512]{1,0:T(8,128)(2,1)}, u32[]{:S(2)}, u32[]{:S(2)}) collective-permute-start(bf16[64,512]{1,0:T(8,128)(2,1)} %get-tuple-element.58), channel_id=1, source_target_pairs={{0,6},{1,7},{2,4},{3,5},{4,2},{5,3},{6,0},{7,1},{8,14},{9,15},{10,... | collective-permute-start | bytes 196616 | tf_op jit(solution)/shard_map/ppermute | solution.py:224
  69.3 3.3 %collective-permute-start = (bf16[64,512]{1,0:T(8,128)(2,1)}, bf16[64,512]{1,0:T(8,128)(2,1)S(1)}, u32[]{:S(2)}, u32[]{:S(2)}) collective-permute-start(bf16[64,512]{1,0:T(8,128)(2,1)} %refs_0_), channel_id=1, source_target_pairs={{0,2},{1,3},{2,0},{3,1},{4,6},{5,7},{6,4},{7,5},{8,10},{9,11},{10,... | collective-permute-start | bytes 196616 | tf_op jit(solution)/shard_map/cond/branch_1_fun/ppermute | solution.py:224
  70.5 3.3 %collective-permute-start.1 = (bf16[64,512]{1,0:T(8,128)(2,1)}, bf16[64,512]{1,0:T(8,128)(2,1)S(1)}, u32[]{:S(2)}, u32[]{:S(2)}) collective-permute-start(bf16[64,512]{1,0:T(8,128)(2,1)} %refs_0_), channel_id=1, source_target_pairs={{0,4},{1,5},{2,6},{3,7},{4,0},{5,1},{6,2},{7,3},{8,12},{9,13},{10,... | collective-permute-start | bytes 196616 | tf_op jit(solution)/shard_map/cond/branch_1_fun/ppermute | solution.py:224
  71.3 4.8 %collective-permute-start.2 = (bf16[64,512]{1,0:T(8,128)(2,1)}, bf16[64,512]{1,0:T(8,128)(2,1)S(1)}, u32[]{:S(2)}, u32[]{:S(2)}) collective-permute-start(bf16[64,512]{1,0:T(8,128)(2,1)} %refs_0_), channel_id=1, source_target_pairs={{0,6},{1,7},{2,4},{3,5},{4,2},{5,3},{6,0},{7,1},{8,14},{9,15},{10,... | collective-permute-start | bytes 196616 | tf_op jit(solution)/shard_map/cond/branch_1_fun/ppermute | solution.py:224
  77.7 4.7 %collective-permute-start.3 = (bf16[256,512]{1,0:T(8,128)(2,1)}, bf16[256,512]{1,0:T(8,128)(2,1)}, u32[]{:S(2)}, u32[]{:S(2)}) collective-permute-start(bf16[256,512]{1,0:T(8,128)(2,1)} %branch_1_fun.1), channel_id=1, source_target_pairs={{0,1},{1,0},{2,3},{3,2},{4,5},{5,4},{6,7},{7,6},{8,9},{9,8},{10,11... | collective-permute-start | bytes 786440 | tf_op jit(solution)/shard_map/cond/branch_1_fun/ppermute | solution.py:224
  85.4 23.9 %collective-permute-start.30 = (bf16[512,1024]{1,0:T(8,128)(2,1)S(1)}, bf16[512,1024]{1,0:T(8,128)(2,1)S(1)}, u32[]{:S(2)}, u32[]{:S(2)}) collective-permute-start(bf16[512,1024]{1,0:T(8,128)(2,1)S(1)} %get-tuple-element.65), channel_id=1, source_target_pairs={{8,0},{16,24},{9,1},{17,25},{10,2},{18,26},{11,3},{19,27},{12,4},{... | collective-permute-start | bytes 3145736 | tf_op jit(solution)/shard_map/ppermute | solution.py:307
  86.9 26.3 %collective-permute-start.31 = (bf16[512,1024]{1,0:T(8,128)(2,1)S(1)}, bf16[512,1024]{1,0:T(8,128)(2,1)S(1)}, u32[]{:S(2)}, u32[]{:S(2)}) collective-permute-start(bf16[512,1024]{1,0:T(8,128)(2,1)S(1)} %get-tuple-element.66), channel_id=1, source_target_pairs={{8,16},{16,8},{9,17},{17,9},{10,18},{18,10},{11,19},{19,11},{12,20... | collective-permute-start | bytes 3145736 | tf_op jit(solution)/shard_map/ppermute | solution.py:307
  90.2 4.8 %collective-permute-start.26 = (bf16[256,640]{1,0:T(8,128)(2,1)S(1)}, bf16[256,640]{1,0:T(8,128)(2,1)S(1)}, u32[]{:S(2)}, u32[]{:S(2)}) collective-permute-start(bf16[256,640]{1,0:T(8,128)(2,1)S(1)} %shard_map.41.near), channel_id=1, source_target_pairs={{0,1},{1,0},{2,3},{3,2},{4,5},{5,4},{6,7},{7,6},{8,9},{9,8},{10,11... | collective-permute-start | bytes 983048 | tf_op jit(solution)/shard_map/ppermute | solution.py:224
  93.0 5.5 %collective-permute-start.25 = (bf16[64,512]{1,0:T(8,128)(2,1)}, bf16[64,512]{1,0:T(8,128)(2,1)S(1)}, u32[]{:S(2)}, u32[]{:S(2)}) collective-permute-start(bf16[64,512]{1,0:T(8,128)(2,1)} %shard_map.44), channel_id=1, source_target_pairs={{0,8},{24,16},{1,9},{25,17},{2,10},{26,18},{3,11},{27,19},{4,12},{... | collective-permute-start | bytes 196616 | tf_op jit(solution)/shard_map/ppermute | solution.py:295
  94.6 7.1 %collective-permute-start.22 = (bf16[64,512]{1,0:T(8,128)(2,1)S(1)}, bf16[64,512]{1,0:T(8,128)(2,1)S(1)}, u32[]{:S(2)}, u32[]{:S(2)}) collective-permute-start(bf16[64,512]{1,0:T(8,128)(2,1)S(1)} %get-tuple-element.72), channel_id=1, source_target_pairs={{0,2},{1,3},{2,0},{3,1},{4,6},{5,7},{6,4},{7,5},{8,10},{9,11},{10,... | collective-permute-start | bytes 196616 | tf_op jit(solution)/shard_map/ppermute | solution.py:224
  94.9 6.8 %collective-permute-start.23 = (bf16[64,512]{1,0:T(8,128)(2,1)S(1)}, bf16[64,512]{1,0:T(8,128)(2,1)S(1)}, u32[]{:S(2)}, u32[]{:S(2)}) collective-permute-start(bf16[64,512]{1,0:T(8,128)(2,1)S(1)} %get-tuple-element.73), channel_id=1, source_target_pairs={{0,4},{1,5},{2,6},{3,7},{4,0},{5,1},{6,2},{7,3},{8,12},{9,13},{10,... | collective-permute-start | bytes 196616 | tf_op jit(solution)/shard_map/ppermute | solution.py:224
  98.5 4.0 %collective-permute-start.24 = (bf16[64,512]{1,0:T(8,128)(2,1)S(1)}, bf16[64,512]{1,0:T(8,128)(2,1)S(1)}, u32[]{:S(2)}, u32[]{:S(2)}) collective-permute-start(bf16[64,512]{1,0:T(8,128)(2,1)S(1)} %get-tuple-element.74), channel_id=1, source_target_pairs={{0,6},{1,7},{2,4},{3,5},{4,2},{5,3},{6,0},{7,1},{8,14},{9,15},{10,... | collective-permute-start | bytes 196616 | tf_op jit(solution)/shard_map/ppermute | solution.py:224
  102.6 4.2 %collective-permute-start.27 = (bf16[64,1024]{1,0:T(8,128)(2,1)S(1)}, bf16[64,1024]{1,0:T(8,128)(2,1)S(1)}, u32[]{:S(2)}, u32[]{:S(2)}) collective-permute-start(bf16[64,1024]{1,0:T(8,128)(2,1)S(1)} %pad_maximum_fusion.refs_0_), channel_id=1, source_target_pairs={{0,2},{1,3},{2,0},{3,1},{4,6},{5,7},{6,4},{7,5},{8,10},{9,11},{10,... | collective-permute-start | bytes 393224 | tf_op jit(solution)/shard_map/ppermute | solution.py:224
  103.0 4.1 %collective-permute-start.28 = (bf16[64,1024]{1,0:T(8,128)(2,1)S(1)}, bf16[64,1024]{1,0:T(8,128)(2,1)S(1)}, u32[]{:S(2)}, u32[]{:S(2)}) collective-permute-start(bf16[64,1024]{1,0:T(8,128)(2,1)S(1)} %pad_maximum_fusion.refs_0_), channel_id=1, source_target_pairs={{0,4},{1,5},{2,6},{3,7},{4,0},{5,1},{6,2},{7,3},{8,12},{9,13},{10,... | collective-permute-start | bytes 393224 | tf_op jit(solution)/shard_map/ppermute | solution.py:224
  104.0 5.2 %collective-permute-start.29 = (bf16[64,1024]{1,0:T(8,128)(2,1)S(1)}, bf16[64,1024]{1,0:T(8,128)(2,1)S(1)}, u32[]{:S(2)}, u32[]{:S(2)}) collective-permute-start(bf16[64,1024]{1,0:T(8,128)(2,1)S(1)} %pad_maximum_fusion.refs_0_), channel_id=1, source_target_pairs={{0,6},{1,7},{2,4},{3,5},{4,2},{5,3},{6,0},{7,1},{8,14},{9,15},{10,... | collective-permute-start | bytes 393224 | tf_op jit(solution)/shard_map/ppermute | solution.py:224
  113.2 2.7 %collective-permute-start.32 = (bf16[256,1024]{1,0:T(8,128)(2,1)S(1)}, bf16[256,1024]{1,0:T(8,128)(2,1)S(1)}, u32[]{:S(2)}, u32[]{:S(2)}) collective-permute-start(bf16[256,1024]{1,0:T(8,128)(2,1)S(1)} %shard_map.50.near), channel_id=1, source_target_pairs={{0,1},{1,0},{2,3},{3,2},{4,5},{5,4},{6,7},{7,6},{8,9},{9,8},{10,11... | collective-permute-start | bytes 1572872 | tf_op jit(solution)/shard_map/ppermute | solution.py:224
  (15 other events, 146.2 us)

commit v15 on v14

--- a/solution.py
+++ b/solution.py
@@ -269,7 +269,7 @@
     all_stats = [stats] + [
         lax.ppermute(stats, "dp", [(i, (i + k) % 4) for i in range(4)]) for k in (1, 2, 3)
     ]
-    ahead = after(z_anchor, stats)
+    ahead = after(z_anchor, *all_stats)
     beside_in = lax.ppermute(ahead, "dp", [(i, i ^ 1) for i in range(4)])
     swapped = lax.ppermute(ahead, "dp", across)
     mean = (all_stats[0][:1] + all_stats[1][:1] + all_stats[2][:1] + all_stats[3][:1]) / 4
@@ -293,23 +293,19 @@
     )(order, middle, after(turned, near_own), beside_in, swapped, mean)
     first = scatter(*halve(kept, sent))
     crossed = lax.ppermute(first, "dp", [(0, 1), (3, 2)])
-
-    def gather(x):
-        near = gather_chips(x)
-        return near, to_partner(near, 1)
-
-    near, far = lax.cond(
-        middle[0] == 1, gather, lambda x: (jnp.zeros((half, rows), x.dtype),) * 2, first
-    )
+    near = gather_chips(first)
     ready = kernel_call(
         push_kernel, [block, block], smem=2, scratch=12, temps=[((rows, rows), jnp.bfloat16)]
-    )(order, middle, near, far, beside, swapped, beside_square, swapped_square)
-    pushed = [lax.ppermute(x, "dp", p) for x, p in zip(ready, (outward, across))]
+    )(order, middle, near, to_partner(near, 1), beside, swapped, beside_square, swapped_square)
+    out, over = ready
+    pushed = [
+        lax.ppermute(out, "dp", outward), lax.ppermute(after(over, end), "dp", across)
+    ]
 
     opposite, opposite_square, kept, sent = kernel_call(
         second_kernel, [block, flat, *summands(rows)], smem=1, scratch=12
     )(middle, after(turned, *ready), swapped, swapped_square, end, mean)
-    halved = halve(kept, sent)
+    halved = halve(kept, after(sent, crossed))
     result = ((rows, width), jnp.float32)
     held = kernel_call(
         functools.partial(held_kernel, total), [result],

time: 120 us -> 94.7 us (0.79)
  waiting for transfers between devices: 53.5 us -> 29.1 us
  starting transfers between devices: 38 us -> 47.2 us
  local copies, waits for them, and re-layouts: 6.6 us -> 0.02 us
  Pallas kernels: 20.1 us -> 15.9 us
    ppermute x3, waiting for transfers between devices: 21.3 us -> 1.11 us  [by_line(): lax.ppermute(stats, 'dp', [(i, (i + k) % 4) for i in range(4)])]
    unnamed x28 -> x6, local copies, waits for them, and re-layouts: 6.6 us -> 0.02 us
    ppermute x24, starting transfers between devices: 24.2 us -> 30.3 us  [to_partner(): return lax.ppermute(x, 'feat', [(i, i ^ step) for i in range(8)])]
    pallas_call x16, Pallas kernels: 20.1 us -> 15.9 us  [call(): pl.pallas_call(body, out_shape=[jax.ShapeDtypeStruct(s, t) for s, t in ou...]
    ppermute x2, waiting for transfers between devices: 3.94 us -> 1.07 us  [the longest x1 1.07 us: by_line(): lax.ppermute(after(over, end), 'dp', across)]
    ppermute x3, starting transfers between devices: 1.51 us -> 3.83 us  [by_line(): lax.ppermute(stats, 'dp', [(i, (i + k) % 4) for i in range(4)])]
    ppermute x1, waiting for transfers between devices: 3.09 us -> 1.24 us  [by_line(): crossed = lax.ppermute(first, 'dp', [(0, 1), (3, 2)])]
    ppermute x1, starting transfers between devices: 0.07 us -> 1.69 us  [by_line(): beside_in = lax.ppermute(ahead, 'dp', [(i, i ^ 1) for i in range(4)])]
  transfers between devices with their start and end apart: 33 -> 33, of which waited for: 26 -> 26; matrix products, arithmetic and copies ran while one was open for 1% -> 1% of each run, Pallas kernels for 13% -> 12%
where the time goes in v15:
time: 94.7 us; the launch traced here: 93.1 us
  starting transfers between devices  47.2 us (50%)
  waiting for transfers between devices  29.1 us (31%)
  Pallas kernels  15.9 us (17%)
    ppermute x24, starting transfers between devices, to_partner(): return lax.ppermute(x, 'feat', [(i, i ^ step) for i in range(8)])  30.3 us
    ppermute x24, waiting for transfers between devices, to_partner(): return lax.ppermute(x, 'feat', [(i, i ^ step) for i in range(8)])  24.1 us
    pallas_call x16, Pallas kernels, call(): pl.pallas_call(body, out_shape=[jax.ShapeDtypeStruct(s, t) for s, t in ou...  15.9 us
    ppermute x3, starting transfers between devices, by_line(): lax.ppermute(stats, 'dp', [(i, (i + k) % 4) for i in range(4)])  3.83 us
    ppermute x1, starting transfers between devices, by_line(): swapped = lax.ppermute(ahead, 'dp', across)  3.57 us
    ppermute x1, starting transfers between devices, by_line(): lax.ppermute(after(over, end), 'dp', across)  3.02 us
  transfers between devices with their start and end apart: 33, of which 26 were waited for; matrix products, arithmetic and copies ran while one was open for 1% of the time, Pallas kernels for 12%

profile of v15, /device:TPU:9, one launch (start us, length us, event | category | flops | bytes accessed | tf_op | source)
XLA Modules:
  0.0 93.1 jit_solution(9788068863642739975)
XLA Ops:
  0.0 1.8 %shard_map.37 = f32[2,1024]{1,0:T(2,128)S(1)} custom-call(bf16[512,1024]{1,0:T(8,128)(2,1)} %z.5), custom_call_target="tpu_custom_call" | custom-call | tf_op jit(solution)/shard_map/pallas_call | solution.py:17
  1.8 1.3 %collective-permute-start = (f32[2,1024]{1,0:T(2,128)S(1)}, f32[2,1024]{1,0:T(2,128)S(1)}, u32[]{:S(2)}, u32[]{:S(2)}) collective-permute-start(f32[2,1024]{1,0:T(2,128)S(1)} %shard_map.37), channel_id=1, source_target_pairs={{0,8},{8,16},{16,24},{24,0},{1,9},{9,17},{17,25},{25,1},{2,10},{10... | collective-permute-start | bytes 24584 | tf_op jit(solution)/shard_map/ppermute | solution.py:270
  4.3 1.4 %collective-permute-start.2 = (f32[2,1024]{1,0:T(2,128)S(1)}, f32[2,1024]{1,0:T(2,128)S(1)}, u32[]{:S(2)}, u32[]{:S(2)}) collective-permute-start(f32[2,1024]{1,0:T(2,128)S(1)} %shard_map.37), channel_id=1, source_target_pairs={{0,24},{8,0},{16,8},{24,16},{1,25},{9,1},{17,9},{25,17},{2,26},{10... | collective-permute-start | bytes 24584 | tf_op jit(solution)/shard_map/ppermute | solution.py:270
  6.8 1.7 %collective-permute-start.10 = (bf16[512,1024]{1,0:T(8,128)(2,1)}, bf16[512,1024]{1,0:T(8,128)(2,1)S(1)}, u32[]{:S(2)}, u32[]{:S(2)}) collective-permute-start(bf16[512,1024]{1,0:T(8,128)(2,1)} %z.5), channel_id=1, source_target_pairs={{0,8},{8,0},{16,24},{24,16},{1,9},{9,1},{17,25},{25,17},{2,10},{10... | collective-permute-start | bytes 3145736 | tf_op jit(solution)/shard_map/ppermute | solution.py:273
  8.4 3.6 %collective-permute-start.11 = (bf16[512,1024]{1,0:T(8,128)(2,1)}, bf16[512,1024]{1,0:T(8,128)(2,1)S(1)}, u32[]{:S(2)}, u32[]{:S(2)}) collective-permute-start(bf16[512,1024]{1,0:T(8,128)(2,1)} %z.5), channel_id=1, source_target_pairs={{8,16},{16,8},{9,17},{17,9},{10,18},{18,10},{11,19},{19,11},{12,20... | collective-permute-start | bytes 3145736 | tf_op jit(solution)/shard_map/ppermute | solution.py:274
  12.7 2.4 %shard_map.38 = (bf16[512,1024]{1,0:T(8,128)(2,1)S(1)}, bf16[512,1024]{1,0:T(8,128)(2,1)S(1)}, f32[1,1024]{1,0:T(1,128)S(1)}, f32[256,640]{1,0:T(8,128)S(1)}, bf16[256,640]{1,0:T(8,128)(2,1)S(1)}) custom-call(s32[8]{0:T(128)S(1)} %broadcast_xor_fusion.order, bf16[512,1024]{1,0:T(8,128)(2,1)} %z.5, f32[1,1024]{1,0:T(1,128)S(1)} %get-tuple-element.82.mean), custom_call_target="tpu_custom_call" | custom-call | tf_op jit(solution)/shard_map/pallas_call | solution.py:17
  15.1 3.0 %collective-permute-start.3 = (bf16[256,640]{1,0:T(8,128)(2,1)S(1)}, bf16[256,640]{1,0:T(8,128)(2,1)S(1)}, u32[]{:S(2)}, u32[]{:S(2)}) collective-permute-start(bf16[256,640]{1,0:T(8,128)(2,1)S(1)} %get-tuple-element.45), channel_id=1, source_target_pairs={{0,1},{1,0},{2,3},{3,2},{4,5},{5,4},{6,7},{7,6},{8,9},{9,8},{10,11... | collective-permute-start | bytes 983048 | tf_op jit(solution)/shard_map/ppermute | solution.py:224
  19.5 1.3 %collective-permute-start.4 = (bf16[64,640]{1,0:T(8,128)(2,1)S(1)}, bf16[64,640]{1,0:T(8,128)(2,1)S(1)}, u32[]{:S(2)}, u32[]{:S(2)}) collective-permute-start(bf16[64,640]{1,0:T(8,128)(2,1)S(1)} %get-tuple-element.47), channel_id=1, source_target_pairs={{0,2},{1,3},{2,0},{3,1},{4,6},{5,7},{6,4},{7,5},{8,10},{9,11},{10,... | collective-permute-start | bytes 245768 | tf_op jit(solution)/shard_map/ppermute | solution.py:224
  24.4 1.9 %collective-permute-done.6.c = bf16[64,640]{1,0:T(8,128)(2,1)S(1)} collective-permute-done((bf16[64,640]{1,0:T(8,128)(2,1)S(1)}, bf16[64,640]{1,0:T(8,128)(2,1)S(1)}, u32[]{:S(2)}, u32[]{:S(2)}) %collective-permute-start.6) | collective-permute-done | bytes 81952 | tf_op jit(solution)/shard_map/ppermute | solution.py:224
  27.3 1.8 %collective-permute-start.9 = (bf16[64,640]{1,0:T(8,128)(2,1)S(1)}, bf16[64,640]{1,0:T(8,128)(2,1)S(1)}, u32[]{:S(2)}, u32[]{:S(2)}) collective-permute-start(bf16[64,640]{1,0:T(8,128)(2,1)S(1)} %shard_map.40.refs_0_), channel_id=1, source_target_pairs={{0,6},{1,7},{2,4},{3,5},{4,2},{5,3},{6,0},{7,1},{8,14},{9,15},{10,... | collective-permute-start | bytes 245768 | tf_op jit(solution)/shard_map/ppermute | solution.py:224
  31.5 1.5 %collective-permute-done.11.opposite_in = bf16[512,1024]{1,0:T(8,128)(2,1)S(1)} collective-permute-done((bf16[512,1024]{1,0:T(8,128)(2,1)}, bf16[512,1024]{1,0:T(8,128)(2,1)S(1)}, u32[]{:S(2)}, u32[]{:S(2)}) %collective-permute-start.11) | collective-permute-done | bytes 1048608 | tf_op jit(solution)/shard_map/ppermute | solution.py:274
  33.0 1.6 %collective-permute-start.20 = (bf16[512,1024]{1,0:T(8,128)(2,1)}, bf16[512,1024]{1,0:T(8,128)(2,1)}, u32[]{:S(2)}, u32[]{:S(2)}) collective-permute-start(bf16[512,1024]{1,0:T(8,128)(2,1)} %z.5), channel_id=1, source_target_pairs={{0,24},{24,0},{1,25},{25,1},{2,26},{26,2},{3,27},{27,3},{4,28},{28... | collective-permute-start | bytes 3145736 | tf_op jit(solution)/shard_map/ppermute | solution.py:288
  34.7 1.5 %shard_map.42 = (bf16[512,1024]{1,0:T(8,128)(2,1)S(1)}, f32[1,1024]{1,0:T(1,128)S(1)}, bf16[512,1024]{1,0:T(8,128)(2,1)S(1)}, f32[1,1024]{1,0:T(1,128)S(1)}, f32...) custom-call(s32[8]{0:T(128)S(1)} %broadcast_xor_fusion.order, s32[1]{0:T(128)} %bitcast.middle, ...), custom_call_target="tpu_custom_call" | custom-call | tf_op jit(solution)/shard_map/pallas_call | solution.py:17
  36.2 3.4 %collective-permute-start.12 = (bf16[256,512]{1,0:T(8,128)(2,1)S(1)}, bf16[256,512]{1,0:T(8,128)(2,1)S(1)}, u32[]{:S(2)}, u32[]{:S(2)}) collective-permute-start(bf16[256,512]{1,0:T(8,128)(2,1)S(1)} %get-tuple-element.53), channel_id=1, source_target_pairs={{0,1},{1,0},{2,3},{3,2},{4,5},{5,4},{6,7},{7,6},{8,9},{9,8},{10,11... | collective-permute-start | bytes 786440 | tf_op jit(solution)/shard_map/ppermute | solution.py:224
  40.8 1.3 %collective-permute-start.13 = (bf16[64,512]{1,0:T(8,128)(2,1)S(1)}, bf16[64,512]{1,0:T(8,128)(2,1)S(1)}, u32[]{:S(2)}, u32[]{:S(2)}) collective-permute-start(bf16[64,512]{1,0:T(8,128)(2,1)S(1)} %get-tuple-element.55), channel_id=1, source_target_pairs={{0,2},{1,3},{2,0},{3,1},{4,6},{5,7},{6,4},{7,5},{8,10},{9,11},{10,... | collective-permute-start | bytes 196616 | tf_op jit(solution)/shard_map/ppermute | solution.py:224
  45.2 2.1 %collective-permute-done.15.c = bf16[64,512]{1,0:T(8,128)(2,1)S(1)} collective-permute-done((bf16[64,512]{1,0:T(8,128)(2,1)S(1)}, bf16[64,512]{1,0:T(8,128)(2,1)S(1)}, u32[]{:S(2)}, u32[]{:S(2)}) %collective-permute-start.15) | collective-permute-done | bytes 65568 | tf_op jit(solution)/shard_map/ppermute | solution.py:224
  48.1 2.0 %collective-permute-start.18 = (bf16[64,512]{1,0:T(8,128)(2,1)S(1)}, bf16[64,512]{1,0:T(8,128)(2,1)S(1)}, u32[]{:S(2)}, u32[]{:S(2)}) collective-permute-start(bf16[64,512]{1,0:T(8,128)(2,1)S(1)} %shard_map.44.refs_0_), channel_id=1, source_target_pairs={{0,6},{1,7},{2,4},{3,5},{4,2},{5,3},{6,0},{7,1},{8,14},{9,15},{10,... | collective-permute-start | bytes 196616 | tf_op jit(solution)/shard_map/ppermute | solution.py:224
  52.1 3.7 %collective-permute-start.19 = (bf16[256,512]{1,0:T(8,128)(2,1)S(1)}, bf16[256,512]{1,0:T(8,128)(2,1)S(1)}, u32[]{:S(2)}, u32[]{:S(2)}) collective-permute-start(bf16[256,512]{1,0:T(8,128)(2,1)S(1)} %shard_map.45.near), channel_id=1, source_target_pairs={{0,1},{1,0},{2,3},{3,2},{4,5},{5,4},{6,7},{7,6},{8,9},{9,8},{10,11... | collective-permute-start | bytes 786440 | tf_op jit(solution)/shard_map/ppermute | solution.py:224
  57.0 1.8 %shard_map.46 = (bf16[512,1024]{1,0:T(8,128)(2,1)S(1)}, bf16[512,1024]{1,0:T(8,128)(2,1)S(1)}) custom-call(s32[8]{0:T(128)S(1)} %broadcast_xor_fusion.order, s32[1]{0:T(128)} %bitcast.middle, bf16[256,512]{1,0:T(8,128)(2,1)S(1)} %shard_map.45.near, bf16[256,512]{1,0:T(8,128)(2,1)S(1)} %collective-permute-done.19.far, ...), custom_call_target="tpu_custom_call" | custom-call | tf_op jit(solution)/shard_map/pallas_call | solution.py:17
  58.8 1.8 %collective-permute-start.30 = (bf16[512,1024]{1,0:T(8,128)(2,1)S(1)}, bf16[512,1024]{1,0:T(8,128)(2,1)S(1)}, u32[]{:S(2)}, u32[]{:S(2)}) collective-permute-start(bf16[512,1024]{1,0:T(8,128)(2,1)S(1)} %get-tuple-element.62), channel_id=1, source_target_pairs={{8,0},{16,24},{9,1},{17,25},{10,2},{18,26},{11,3},{19,27},{12,4},{... | collective-permute-start | bytes 3145736 | tf_op jit(solution)/shard_map/ppermute | solution.py:302
  60.7 3.0 %collective-permute-start.31 = (bf16[512,1024]{1,0:T(8,128)(2,1)S(1)}, bf16[512,1024]{1,0:T(8,128)(2,1)S(1)}, u32[]{:S(2)}, u32[]{:S(2)}) collective-permute-start(bf16[512,1024]{1,0:T(8,128)(2,1)S(1)} %get-tuple-element.78), channel_id=1, source_target_pairs={{8,16},{16,8},{9,17},{17,9},{10,18},{18,10},{11,19},{19,11},{12,20... | collective-permute-start | bytes 3145736 | tf_op jit(solution)/shard_map/ppermute | solution.py:302
  63.7 1.3 %collective-permute-start.21 = (bf16[64,512]{1,0:T(8,128)(2,1)S(1)}, bf16[64,512]{1,0:T(8,128)(2,1)S(1)}, u32[]{:S(2)}, u32[]{:S(2)}) collective-permute-start(bf16[64,512]{1,0:T(8,128)(2,1)S(1)} %shard_map.44.refs_0_), channel_id=1, source_target_pairs={{0,8},{24,16},{1,9},{25,17},{2,10},{26,18},{3,11},{27,19},{4,12},{... | collective-permute-start | bytes 196616 | tf_op jit(solution)/shard_map/ppermute | solution.py:295
  65.7 2.0 %shard_map.47 = (bf16[512,1024]{1,0:T(8,128)(2,1)S(1)}, f32[1,1024]{1,0:T(1,128)S(1)}, f32[256,512]{1,0:T(8,128)S(1)}, bf16[256,512]{1,0:T(8,128)(2,1)S(1)}) custom-call(s32[1]{0:T(128)} %bitcast.middle, bf16[512,1024]{1,0:T(8,128)(2,1)S(1)} %get-tuple-element.64.turned, bf16[512,1024]{1,0:T(8,128)(2,1)S(1)} %get-tuple-element.59.opposite.swapped, ...), custom_call_target="tpu_custom_call" | custom-call | tf_op jit(solution)/shard_map/pallas_call | solution.py:17
  69.0 1.5 %collective-permute-start.22 = (bf16[256,512]{1,0:T(8,128)(2,1)S(1)}, bf16[256,512]{1,0:T(8,128)(2,1)S(1)}, u32[]{:S(2)}, u32[]{:S(2)}) collective-permute-start(bf16[256,512]{1,0:T(8,128)(2,1)S(1)} %get-tuple-element.68), channel_id=1, source_target_pairs={{0,1},{1,0},{2,3},{3,2},{4,5},{5,4},{6,7},{7,6},{8,9},{9,8},{10,11... | collective-permute-start | bytes 786440 | tf_op jit(solution)/shard_map/ppermute | solution.py:224
  71.7 1.3 %collective-permute-start.23 = (bf16[64,512]{1,0:T(8,128)(2,1)S(1)}, bf16[64,512]{1,0:T(8,128)(2,1)S(1)}, u32[]{:S(2)}, u32[]{:S(2)}) collective-permute-start(bf16[64,512]{1,0:T(8,128)(2,1)S(1)} %get-tuple-element.70), channel_id=1, source_target_pairs={{0,2},{1,3},{2,0},{3,1},{4,6},{5,7},{6,4},{7,5},{8,10},{9,11},{10,... | collective-permute-start | bytes 196616 | tf_op jit(solution)/shard_map/ppermute | solution.py:224
  74.5 2.6 %shard_map.50.held = f32[512,1024]{1,0:T(8,128)S(1)} custom-call(s32[8]{0:T(128)S(1)} %broadcast_xor_fusion.order, bf16[256,640]{1,0:T(8,128)(2,1)S(1)} %shard_map.41.near, bf16[256,640]{1,0:T(8,128)(2,1)S(1)} %collective-permute-done.26.far, bf16[512,1024]{1,0:T(8,128)(2,1)S(1)} %copy-done.2, bf16[512,1024]{1,0:T(8,128)(2,1)} %z.5, ...), custom_call_target="tpu_custom_call" | custom-call | tf_op jit(solution)/shard_map/pallas_call | solution.py:17
  79.7 1.4 %collective-permute-start.29 = (bf16[64,1024]{1,0:T(8,128)(2,1)S(1)}, bf16[64,1024]{1,0:T(8,128)(2,1)S(1)}, u32[]{:S(2)}, u32[]{:S(2)}) collective-permute-start(bf16[64,1024]{1,0:T(8,128)(2,1)S(1)} %pad_maximum_fusion.refs_0_), channel_id=1, source_target_pairs={{0,6},{1,7},{2,4},{3,5},{4,2},{5,3},{6,0},{7,1},{8,14},{9,15},{10,... | collective-permute-start | bytes 393224 | tf_op jit(solution)/shard_map/ppermute | solution.py:224
  81.0 1.5 %collective-permute-done.27.refs_1_ = bf16[64,1024]{1,0:T(8,128)(2,1)S(1)} collective-permute-done((bf16[64,1024]{1,0:T(8,128)(2,1)S(1)}, bf16[64,1024]{1,0:T(8,128)(2,1)S(1)}, u32[]{:S(2)}, u32[]{:S(2)}) %collective-permute-start.27) | collective-permute-done | bytes 131104 | tf_op jit(solution)/shard_map/ppermute | solution.py:224
  82.8 2.6 %collective-permute-done.29.refs_3_ = bf16[64,1024]{1,0:T(8,128)(2,1)S(1)} collective-permute-done((bf16[64,1024]{1,0:T(8,128)(2,1)S(1)}, bf16[64,1024]{1,0:T(8,128)(2,1)S(1)}, u32[]{:S(2)}, u32[]{:S(2)}) %collective-permute-start.29) | collective-permute-done | bytes 131104 | tf_op jit(solution)/shard_map/ppermute | solution.py:224
  86.6 1.7 %collective-permute-start.32 = (bf16[256,1024]{1,0:T(8,128)(2,1)S(1)}, bf16[256,1024]{1,0:T(8,128)(2,1)S(1)}, u32[]{:S(2)}, u32[]{:S(2)}) collective-permute-start(bf16[256,1024]{1,0:T(8,128)(2,1)S(1)} %shard_map.51.near), channel_id=1, source_target_pairs={{0,1},{1,0},{2,3},{3,2},{4,5},{5,4},{6,7},{7,6},{8,9},{9,8},{10,11... | collective-permute-start | bytes 1572872 | tf_op jit(solution)/shard_map/ppermute | solution.py:224
  88.3 1.5 %collective-permute-done.32.far = bf16[256,1024]{1,0:T(8,128)(2,1)S(1)} collective-permute-done((bf16[256,1024]{1,0:T(8,128)(2,1)S(1)}, bf16[256,1024]{1,0:T(8,128)(2,1)S(1)}, u32[]{:S(2)}, u32[]{:S(2)}) %collective-permute-start.32) | collective-permute-done | bytes 524320 | tf_op jit(solution)/shard_map/ppermute | solution.py:224
  89.9 3.2 %shard_map.52 = f32[512,1024]{1,0:T(8,128)} custom-call(s32[8]{0:T(128)S(1)} %broadcast_xor_fusion.order, s32[1]{0:T(128)} %bitcast.middle, bf16[256,1024]{1,0:T(8,128)(2,1)S(1)} %shard_map.51.near, bf16[256,1024]{1,0:T(8,128)(2,1)S(1)} %collective-permute-done.32.far, bf16[512,1024]{1,0:T(8,128)(2,1)S(1)} %get-tuple-element.58.beside, ...), custom_call_target="tpu_custom_call" | custom-call | tf_op jit(solution)/shard_map/pallas_call | solution.py:17
  (60 shorter events, 28.2 us)
Async XLA Ops:
  1.8 3.8 %collective-permute-start = (f32[2,1024]{1,0:T(2,128)S(1)}, f32[2,1024]{1,0:T(2,128)S(1)}, u32[]{:S(2)}, u32[]{:S(2)}) collective-permute-start(f32[2,1024]{1,0:T(2,128)S(1)} %shard_map.37), channel_id=1, source_target_pairs={{0,8},{8,16},{16,24},{24,0},{1,9},{9,17},{17,25},{25,1},{2,10},{10... | collective-permute-start | bytes 24584 | tf_op jit(solution)/shard_map/ppermute | solution.py:270
  3.2 3.4 %collective-permute-start.1 = (f32[2,1024]{1,0:T(2,128)S(1)}, f32[2,1024]{1,0:T(2,128)S(1)}, u32[]{:S(2)}, u32[]{:S(2)}) collective-permute-start(f32[2,1024]{1,0:T(2,128)S(1)} %shard_map.37), channel_id=1, source_target_pairs={{0,16},{8,24},{16,0},{24,8},{1,17},{9,25},{17,1},{25,9},{2,18},{10... | collective-permute-start | bytes 24584 | tf_op jit(solution)/shard_map/ppermute | solution.py:270
  6.8 24.7 %collective-permute-start.10 = (bf16[512,1024]{1,0:T(8,128)(2,1)}, bf16[512,1024]{1,0:T(8,128)(2,1)S(1)}, u32[]{:S(2)}, u32[]{:S(2)}) collective-permute-start(bf16[512,1024]{1,0:T(8,128)(2,1)} %z.5), channel_id=1, source_target_pairs={{0,8},{8,0},{16,24},{24,16},{1,9},{9,1},{17,25},{25,17},{2,10},{10... | collective-permute-start | bytes 3145736 | tf_op jit(solution)/shard_map/ppermute | solution.py:273
  8.4 24.6 %collective-permute-start.11 = (bf16[512,1024]{1,0:T(8,128)(2,1)}, bf16[512,1024]{1,0:T(8,128)(2,1)S(1)}, u32[]{:S(2)}, u32[]{:S(2)}) collective-permute-start(bf16[512,1024]{1,0:T(8,128)(2,1)} %z.5), channel_id=1, source_target_pairs={{8,16},{16,8},{9,17},{17,9},{10,18},{18,10},{11,19},{19,11},{12,20... | collective-permute-start | bytes 3145736 | tf_op jit(solution)/shard_map/ppermute | solution.py:274
  15.1 4.3 %collective-permute-start.3 = (bf16[256,640]{1,0:T(8,128)(2,1)S(1)}, bf16[256,640]{1,0:T(8,128)(2,1)S(1)}, u32[]{:S(2)}, u32[]{:S(2)}) collective-permute-start(bf16[256,640]{1,0:T(8,128)(2,1)S(1)} %get-tuple-element.45), channel_id=1, source_target_pairs={{0,1},{1,0},{2,3},{3,2},{4,5},{5,4},{6,7},{7,6},{8,9},{9,8},{10,11... | collective-permute-start | bytes 983048 | tf_op jit(solution)/shard_map/ppermute | solution.py:224
  19.5 3.7 %collective-permute-start.4 = (bf16[64,640]{1,0:T(8,128)(2,1)S(1)}, bf16[64,640]{1,0:T(8,128)(2,1)S(1)}, u32[]{:S(2)}, u32[]{:S(2)}) collective-permute-start(bf16[64,640]{1,0:T(8,128)(2,1)S(1)} %get-tuple-element.47), channel_id=1, source_target_pairs={{0,2},{1,3},{2,0},{3,1},{4,6},{5,7},{6,4},{7,5},{8,10},{9,11},{10,... | collective-permute-start | bytes 245768 | tf_op jit(solution)/shard_map/ppermute | solution.py:224
  20.8 3.6 %collective-permute-start.5 = (bf16[64,640]{1,0:T(8,128)(2,1)S(1)}, bf16[64,640]{1,0:T(8,128)(2,1)S(1)}, u32[]{:S(2)}, u32[]{:S(2)}) collective-permute-start(bf16[64,640]{1,0:T(8,128)(2,1)S(1)} %get-tuple-element.48), channel_id=1, source_target_pairs={{0,4},{1,5},{2,6},{3,7},{4,0},{5,1},{6,2},{7,3},{8,12},{9,13},{10,... | collective-permute-start | bytes 245768 | tf_op jit(solution)/shard_map/ppermute | solution.py:224
  22.0 4.2 %collective-permute-start.6 = (bf16[64,640]{1,0:T(8,128)(2,1)S(1)}, bf16[64,640]{1,0:T(8,128)(2,1)S(1)}, u32[]{:S(2)}, u32[]{:S(2)}) collective-permute-start(bf16[64,640]{1,0:T(8,128)(2,1)S(1)} %get-tuple-element.49), channel_id=1, source_target_pairs={{0,6},{1,7},{2,4},{3,5},{4,2},{5,3},{6,0},{7,1},{8,14},{9,15},{10,... | collective-permute-start | bytes 245768 | tf_op jit(solution)/shard_map/ppermute | solution.py:224
  26.4 3.7 %collective-permute-start.7 = (bf16[64,640]{1,0:T(8,128)(2,1)S(1)}, bf16[64,640]{1,0:T(8,128)(2,1)S(1)}, u32[]{:S(2)}, u32[]{:S(2)}) collective-permute-start(bf16[64,640]{1,0:T(8,128)(2,1)S(1)} %shard_map.40.refs_0_), channel_id=1, source_target_pairs={{0,2},{1,3},{2,0},{3,1},{4,6},{5,7},{6,4},{7,5},{8,10},{9,11},{10,... | collective-permute-start | bytes 245768 | tf_op jit(solution)/shard_map/ppermute | solution.py:224
  27.0 3.6 %collective-permute-start.8 = (bf16[64,640]{1,0:T(8,128)(2,1)S(1)}, bf16[64,640]{1,0:T(8,128)(2,1)S(1)}, u32[]{:S(2)}, u32[]{:S(2)}) collective-permute-start(bf16[64,640]{1,0:T(8,128)(2,1)S(1)} %shard_map.40.refs_0_), channel_id=1, source_target_pairs={{0,4},{1,5},{2,6},{3,7},{4,0},{5,1},{6,2},{7,3},{8,12},{9,13},{10,... | collective-permute-start | bytes 245768 | tf_op jit(solution)/shard_map/ppermute | solution.py:224
  27.3 4.2 %collective-permute-start.9 = (bf16[64,640]{1,0:T(8,128)(2,1)S(1)}, bf16[64,640]{1,0:T(8,128)(2,1)S(1)}, u32[]{:S(2)}, u32[]{:S(2)}) collective-permute-start(bf16[64,640]{1,0:T(8,128)(2,1)S(1)} %shard_map.40.refs_0_), channel_id=1, source_target_pairs={{0,6},{1,7},{2,4},{3,5},{4,2},{5,3},{6,0},{7,1},{8,14},{9,15},{10,... | collective-permute-start | bytes 245768 | tf_op jit(solution)/shard_map/ppermute | solution.py:224
  33.0 27.6 %collective-permute-start.20 = (bf16[512,1024]{1,0:T(8,128)(2,1)}, bf16[512,1024]{1,0:T(8,128)(2,1)}, u32[]{:S(2)}, u32[]{:S(2)}) collective-permute-start(bf16[512,1024]{1,0:T(8,128)(2,1)} %z.5), channel_id=1, source_target_pairs={{0,24},{24,0},{1,25},{25,1},{2,26},{26,2},{3,27},{27,3},{4,28},{28... | collective-permute-start | bytes 3145736 | tf_op jit(solution)/shard_map/ppermute | solution.py:288
  36.2 4.5 %collective-permute-start.12 = (bf16[256,512]{1,0:T(8,128)(2,1)S(1)}, bf16[256,512]{1,0:T(8,128)(2,1)S(1)}, u32[]{:S(2)}, u32[]{:S(2)}) collective-permute-start(bf16[256,512]{1,0:T(8,128)(2,1)S(1)} %get-tuple-element.53), channel_id=1, source_target_pairs={{0,1},{1,0},{2,3},{3,2},{4,5},{5,4},{6,7},{7,6},{8,9},{9,8},{10,11... | collective-permute-start | bytes 786440 | tf_op jit(solution)/shard_map/ppermute | solution.py:224
  40.8 3.2 %collective-permute-start.13 = (bf16[64,512]{1,0:T(8,128)(2,1)S(1)}, bf16[64,512]{1,0:T(8,128)(2,1)S(1)}, u32[]{:S(2)}, u32[]{:S(2)}) collective-permute-start(bf16[64,512]{1,0:T(8,128)(2,1)S(1)} %get-tuple-element.55), channel_id=1, source_target_pairs={{0,2},{1,3},{2,0},{3,1},{4,6},{5,7},{6,4},{7,5},{8,10},{9,11},{10,... | collective-permute-start | bytes 196616 | tf_op jit(solution)/shard_map/ppermute | solution.py:224
  42.1 3.1 %collective-permute-start.14 = (bf16[64,512]{1,0:T(8,128)(2,1)S(1)}, bf16[64,512]{1,0:T(8,128)(2,1)S(1)}, u32[]{:S(2)}, u32[]{:S(2)}) collective-permute-start(bf16[64,512]{1,0:T(8,128)(2,1)S(1)} %get-tuple-element.56), channel_id=1, source_target_pairs={{0,4},{1,5},{2,6},{3,7},{4,0},{5,1},{6,2},{7,3},{8,12},{9,13},{10,... | collective-permute-start | bytes 196616 | tf_op jit(solution)/shard_map/ppermute | solution.py:224
  43.3 4.0 %collective-permute-start.15 = (bf16[64,512]{1,0:T(8,128)(2,1)S(1)}, bf16[64,512]{1,0:T(8,128)(2,1)S(1)}, u32[]{:S(2)}, u32[]{:S(2)}) collective-permute-start(bf16[64,512]{1,0:T(8,128)(2,1)S(1)} %get-tuple-element.57), channel_id=1, source_target_pairs={{0,6},{1,7},{2,4},{3,5},{4,2},{5,3},{6,0},{7,1},{8,14},{9,15},{10,... | collective-permute-start | bytes 196616 | tf_op jit(solution)/shard_map/ppermute | solution.py:224
  47.4 3.2 %collective-permute-start.16 = (bf16[64,512]{1,0:T(8,128)(2,1)S(1)}, bf16[64,512]{1,0:T(8,128)(2,1)S(1)}, u32[]{:S(2)}, u32[]{:S(2)}) collective-permute-start(bf16[64,512]{1,0:T(8,128)(2,1)S(1)} %shard_map.44.refs_0_), channel_id=1, source_target_pairs={{0,2},{1,3},{2,0},{3,1},{4,6},{5,7},{6,4},{7,5},{8,10},{9,11},{10,... | collective-permute-start | bytes 196616 | tf_op jit(solution)/shard_map/ppermute | solution.py:224
  47.8 3.1 %collective-permute-start.17 = (bf16[64,512]{1,0:T(8,128)(2,1)S(1)}, bf16[64,512]{1,0:T(8,128)(2,1)S(1)}, u32[]{:S(2)}, u32[]{:S(2)}) collective-permute-start(bf16[64,512]{1,0:T(8,128)(2,1)S(1)} %shard_map.44.refs_0_), channel_id=1, source_target_pairs={{0,4},{1,5},{2,6},{3,7},{4,0},{5,1},{6,2},{7,3},{8,12},{9,13},{10,... | collective-permute-start | bytes 196616 | tf_op jit(solution)/shard_map/ppermute | solution.py:224
  48.1 4.0 %collective-permute-start.18 = (bf16[64,512]{1,0:T(8,128)(2,1)S(1)}, bf16[64,512]{1,0:T(8,128)(2,1)S(1)}, u32[]{:S(2)}, u32[]{:S(2)}) collective-permute-start(bf16[64,512]{1,0:T(8,128)(2,1)S(1)} %shard_map.44.refs_0_), channel_id=1, source_target_pairs={{0,6},{1,7},{2,4},{3,5},{4,2},{5,3},{6,0},{7,1},{8,14},{9,15},{10,... | collective-permute-start | bytes 196616 | tf_op jit(solution)/shard_map/ppermute | solution.py:224
  52.1 4.9 %collective-permute-start.19 = (bf16[256,512]{1,0:T(8,128)(2,1)S(1)}, bf16[256,512]{1,0:T(8,128)(2,1)S(1)}, u32[]{:S(2)}, u32[]{:S(2)}) collective-permute-start(bf16[256,512]{1,0:T(8,128)(2,1)S(1)} %shard_map.45.near), channel_id=1, source_target_pairs={{0,1},{1,0},{2,3},{3,2},{4,5},{5,4},{6,7},{7,6},{8,9},{9,8},{10,11... | collective-permute-start | bytes 786440 | tf_op jit(solution)/shard_map/ppermute | solution.py:224
  58.8 26.7 %collective-permute-start.30 = (bf16[512,1024]{1,0:T(8,128)(2,1)S(1)}, bf16[512,1024]{1,0:T(8,128)(2,1)S(1)}, u32[]{:S(2)}, u32[]{:S(2)}) collective-permute-start(bf16[512,1024]{1,0:T(8,128)(2,1)S(1)} %get-tuple-element.62), channel_id=1, source_target_pairs={{8,0},{16,24},{9,1},{17,25},{10,2},{18,26},{11,3},{19,27},{12,4},{... | collective-permute-start | bytes 3145736 | tf_op jit(solution)/shard_map/ppermute | solution.py:302
  60.7 25.9 %collective-permute-start.31 = (bf16[512,1024]{1,0:T(8,128)(2,1)S(1)}, bf16[512,1024]{1,0:T(8,128)(2,1)S(1)}, u32[]{:S(2)}, u32[]{:S(2)}) collective-permute-start(bf16[512,1024]{1,0:T(8,128)(2,1)S(1)} %get-tuple-element.78), channel_id=1, source_target_pairs={{8,16},{16,8},{9,17},{17,9},{10,18},{18,10},{11,19},{19,11},{12,20... | collective-permute-start | bytes 3145736 | tf_op jit(solution)/shard_map/ppermute | solution.py:302
  63.7 5.3 %collective-permute-start.21 = (bf16[64,512]{1,0:T(8,128)(2,1)S(1)}, bf16[64,512]{1,0:T(8,128)(2,1)S(1)}, u32[]{:S(2)}, u32[]{:S(2)}) collective-permute-start(bf16[64,512]{1,0:T(8,128)(2,1)S(1)} %shard_map.44.refs_0_), channel_id=1, source_target_pairs={{0,8},{24,16},{1,9},{25,17},{2,10},{26,18},{3,11},{27,19},{4,12},{... | collective-permute-start | bytes 196616 | tf_op jit(solution)/shard_map/ppermute | solution.py:295
  65.0 9.2 %collective-permute-start.26 = (bf16[256,640]{1,0:T(8,128)(2,1)S(1)}, bf16[256,640]{1,0:T(8,128)(2,1)S(1)}, u32[]{:S(2)}, u32[]{:S(2)}) collective-permute-start(bf16[256,640]{1,0:T(8,128)(2,1)S(1)} %shard_map.41.near), channel_id=1, source_target_pairs={{0,1},{1,0},{2,3},{3,2},{4,5},{5,4},{6,7},{7,6},{8,9},{9,8},{10,11... | collective-permute-start | bytes 983048 | tf_op jit(solution)/shard_map/ppermute | solution.py:224
  69.0 2.7 %collective-permute-start.22 = (bf16[256,512]{1,0:T(8,128)(2,1)S(1)}, bf16[256,512]{1,0:T(8,128)(2,1)S(1)}, u32[]{:S(2)}, u32[]{:S(2)}) collective-permute-start(bf16[256,512]{1,0:T(8,128)(2,1)S(1)} %get-tuple-element.68), channel_id=1, source_target_pairs={{0,1},{1,0},{2,3},{3,2},{4,5},{5,4},{6,7},{7,6},{8,9},{9,8},{10,11... | collective-permute-start | bytes 786440 | tf_op jit(solution)/shard_map/ppermute | solution.py:224
  71.7 5.3 %collective-permute-start.23 = (bf16[64,512]{1,0:T(8,128)(2,1)S(1)}, bf16[64,512]{1,0:T(8,128)(2,1)S(1)}, u32[]{:S(2)}, u32[]{:S(2)}) collective-permute-start(bf16[64,512]{1,0:T(8,128)(2,1)S(1)} %get-tuple-element.70), channel_id=1, source_target_pairs={{0,2},{1,3},{2,0},{3,1},{4,6},{5,7},{6,4},{7,5},{8,10},{9,11},{10,... | collective-permute-start | bytes 196616 | tf_op jit(solution)/shard_map/ppermute | solution.py:224
  73.0 4.1 %collective-permute-start.24 = (bf16[64,512]{1,0:T(8,128)(2,1)S(1)}, bf16[64,512]{1,0:T(8,128)(2,1)S(1)}, u32[]{:S(2)}, u32[]{:S(2)}) collective-permute-start(bf16[64,512]{1,0:T(8,128)(2,1)S(1)} %get-tuple-element.71), channel_id=1, source_target_pairs={{0,4},{1,5},{2,6},{3,7},{4,0},{5,1},{6,2},{7,3},{8,12},{9,13},{10,... | collective-permute-start | bytes 196616 | tf_op jit(solution)/shard_map/ppermute | solution.py:224
  74.2 4.0 %collective-permute-start.25 = (bf16[64,512]{1,0:T(8,128)(2,1)S(1)}, bf16[64,512]{1,0:T(8,128)(2,1)S(1)}, u32[]{:S(2)}, u32[]{:S(2)}) collective-permute-start(bf16[64,512]{1,0:T(8,128)(2,1)S(1)} %get-tuple-element.72), channel_id=1, source_target_pairs={{0,6},{1,7},{2,4},{3,5},{4,2},{5,3},{6,0},{7,1},{8,14},{9,15},{10,... | collective-permute-start | bytes 196616 | tf_op jit(solution)/shard_map/ppermute | solution.py:224
  78.3 4.2 %collective-permute-start.27 = (bf16[64,1024]{1,0:T(8,128)(2,1)S(1)}, bf16[64,1024]{1,0:T(8,128)(2,1)S(1)}, u32[]{:S(2)}, u32[]{:S(2)}) collective-permute-start(bf16[64,1024]{1,0:T(8,128)(2,1)S(1)} %pad_maximum_fusion.refs_0_), channel_id=1, source_target_pairs={{0,2},{1,3},{2,0},{3,1},{4,6},{5,7},{6,4},{7,5},{8,10},{9,11},{10,... | collective-permute-start | bytes 393224 | tf_op jit(solution)/shard_map/ppermute | solution.py:224
  78.7 4.1 %collective-permute-start.28 = (bf16[64,1024]{1,0:T(8,128)(2,1)S(1)}, bf16[64,1024]{1,0:T(8,128)(2,1)S(1)}, u32[]{:S(2)}, u32[]{:S(2)}) collective-permute-start(bf16[64,1024]{1,0:T(8,128)(2,1)S(1)} %pad_maximum_fusion.refs_0_), channel_id=1, source_target_pairs={{0,4},{1,5},{2,6},{3,7},{4,0},{5,1},{6,2},{7,3},{8,12},{9,13},{10,... | collective-permute-start | bytes 393224 | tf_op jit(solution)/shard_map/ppermute | solution.py:224
  79.7 5.8 %collective-permute-start.29 = (bf16[64,1024]{1,0:T(8,128)(2,1)S(1)}, bf16[64,1024]{1,0:T(8,128)(2,1)S(1)}, u32[]{:S(2)}, u32[]{:S(2)}) collective-permute-start(bf16[64,1024]{1,0:T(8,128)(2,1)S(1)} %pad_maximum_fusion.refs_0_), channel_id=1, source_target_pairs={{0,6},{1,7},{2,4},{3,5},{4,2},{5,3},{6,0},{7,1},{8,14},{9,15},{10,... | collective-permute-start | bytes 393224 | tf_op jit(solution)/shard_map/ppermute | solution.py:224
  86.6 3.2 %collective-permute-start.32 = (bf16[256,1024]{1,0:T(8,128)(2,1)S(1)}, bf16[256,1024]{1,0:T(8,128)(2,1)S(1)}, u32[]{:S(2)}, u32[]{:S(2)}) collective-permute-start(bf16[256,1024]{1,0:T(8,128)(2,1)S(1)} %shard_map.51.near), channel_id=1, source_target_pairs={{0,1},{1,0},{2,3},{3,2},{4,5},{5,4},{6,7},{7,6},{8,9},{9,8},{10,11... | collective-permute-start | bytes 1572872 | tf_op jit(solution)/shard_map/ppermute | solution.py:224
  (4 other events, 51.7 us)

commit v16 on v15

--- a/solution.py
+++ b/solution.py
@@ -107,17 +107,27 @@
         split_sum(gram(turned[...], beside[...]), kept, sent, slice(None))
 
 
-def second_kernel(middle, turned, swapped, swapped_square, end, mean, opposite, square, kept, sent):
+def early_kernel(middle, turned, beside, opposite, kept, sent):
+    rows = beside.shape[0]
+
     @pl.when(middle[0] == 1)
     def _():
-        opposite[...] = swapped[...]
-        square[...] = swapped_square[...]
+        split_sum(gram(turned[...], opposite[...]), kept, sent, slice(0, rows))
+        split_sum(gram(turned[...], beside[...]), kept, sent, slice(rows, 2 * rows))
+
+
+def late_kernel(middle, turned, sent_early, end_in, mean, end, square, kept, sent):
+    rows = end.shape[0]
+
+    @pl.when(middle[0] == 1)
+    def _():
+        sent[...] = sent_early[...]
 
     @pl.when(middle[0] == 0)
     def _():
-        centered_into(opposite, end, mean[...], square)
-
-    split_sum(gram(turned[...], opposite[...]), kept, sent, slice(None))
+        centered_into(end, end_in, mean[...], square)
+        split_sum(gram(turned[...], end[...]), kept, sent, slice(0, rows))
+        sent[:, rows:] = jnp.zeros_like(sent[:, rows:])
 
 
 def stats_kernel(z, out):
@@ -146,10 +156,44 @@
         ref[...] = total[k * quarter:(k + 1) * quarter].astype(jnp.bfloat16)
 
 
+def add_either_kernel(middle, kept_early, kept, got, mine, *out):
+    quarter, rows = mine.shape[0], kept.shape[1]
+
+    def put(total, here):
+        mine[:, here] = total[:quarter]
+        for k, ref in enumerate(out, 1):
+            ref[:, here] = total[k * quarter:(k + 1) * quarter].astype(jnp.bfloat16)
+
+    @pl.when(middle[0] == 1)
+    def _():
+        put(kept_early[...] + got[...].astype(jnp.float32), slice(None))
+
+    @pl.when(middle[0] == 0)
+    def _():
+        put(kept[...] + got[:, :rows].astype(jnp.float32), slice(0, rows))
+        put(jnp.zeros((4 * quarter, rows), jnp.float32), slice(rows, 2 * rows))
+
+
 def total_kernel(last, mine, a, b, c, out):
     total = mine[...] + a[...].astype(jnp.float32)
     total = total + b[...].astype(jnp.float32) + c[...].astype(jnp.float32)
     out[...] = with_norm(total, last).astype(jnp.bfloat16)
+
+
+def total_either_kernel(middle, first, mine, a, b, c, out):
+    rows = first.shape[1]
+
+    def put(here):
+        total = mine[:, here] + a[:, here].astype(jnp.float32)
+        total = total + b[:, here].astype(jnp.float32) + c[:, here].astype(jnp.float32)
+        out[:, here] = total.astype(jnp.bfloat16)
+
+    put(slice(0, rows))
+    pl.when(middle[0] == 1)(lambda: put(slice(rows, 2 * rows)))
+
+    @pl.when(middle[0] == 0)
+    def _():
+        out[:, rows:] = first[...]
 
 
 def place_into(out, order, near, far):
@@ -183,8 +227,8 @@
 
 
 def held_kernel(
-    total, order, near, far, own, z, other,
-    own_square, beside_square, opposite_square, mean, spread, held, with_own,
+    total, order, middle, near, far, own, z, other,
+    own_square, beside_square, swapped_square, end_square, mean, spread, held, with_own,
 ):
     rows, width = own.shape
     place_into(with_own, order, near, far)
@@ -196,28 +240,29 @@
         centered = anchor - mean[:, here]
         hinge = jnp.where(deviation < 1.0, centered / deviation, 0.0)
         plain = anchor - other[:, here].astype(jnp.float32) - total / (4.0 * (total - 1)) * hinge
-        square = own_square[:, here] + beside_square[:, here] + opposite_square[:, here]
+        opposite = jnp.where(middle[0] == 1, swapped_square[:, here], end_square[:, here])
+        square = own_square[:, here] + beside_square[:, here] + opposite
         product = dot(with_own[:, :rows], own[:, here])
         product = product + own[:, here].astype(jnp.float32) * (norm - square)
         held[:, here] = plain + coefficient(total) * product
 
 
 def last_kernel(
-    total, order, middle, near, far, beside, opposite, held, out, over, result, second
+    total, order, middle, near, far, beside, swapped, end, held, out, over, result, second
 ):
     rows, width = beside.shape
     place_into(second, order, near, far)
 
-    def put(product_of, arrived):
+    def put(opposite, arrived):
         for k in range(4):
             here = slice(k * width // 4, (k + 1) * width // 4)
-            product = product_of(second[:, rows:], beside[:, here])
+            product = dot(second[:, rows:], beside[:, here])
             product = product + dot(second[:, :rows], opposite[:, here])
             product = product + arrived[:, here].astype(jnp.float32)
             result[:, here] = held[:, here] + coefficient(total) * product
 
-    pl.when(middle[0] == 1)(lambda: put(dot_t, over))
-    pl.when(middle[0] == 0)(lambda: put(dot, out))
+    pl.when(middle[0] == 1)(lambda: put(swapped, over))
+    pl.when(middle[0] == 0)(lambda: put(end, out))
 
 
 def to_partner(x, step):
@@ -292,8 +337,10 @@
         smem=2, scratch=12, temps=[block],
     )(order, middle, after(turned, near_own), beside_in, swapped, mean)
     first = scatter(*halve(kept, sent))
-    crossed = lax.ppermute(first, "dp", [(0, 1), (3, 2)])
-    near = gather_chips(first)
+    kept_early, sent_early = kernel_call(
+        early_kernel, summands(2 * rows), smem=1, scratch=12
+    )(middle, after(turned, first), beside, swapped)
+    near = after(gather_chips(first), sent_early)
     ready = kernel_call(
         push_kernel, [block, block], smem=2, scratch=12, temps=[((rows, rows), jnp.bfloat16)]
     )(order, middle, near, to_partner(near, 1), beside, swapped, beside_square, swapped_square)
@@ -302,26 +349,31 @@
         lax.ppermute(out, "dp", outward), lax.ppermute(after(over, end), "dp", across)
     ]
 
-    opposite, opposite_square, kept, sent = kernel_call(
-        second_kernel, [block, flat, *summands(rows)], smem=1, scratch=12
-    )(middle, after(turned, *ready), swapped, swapped_square, end, mean)
-    halved = halve(kept, after(sent, crossed))
+    end, end_square, kept, sent = kernel_call(
+        late_kernel, [block, flat, summands(rows)[0], summands(2 * rows)[1]], smem=1, scratch=12
+    )(middle, after(turned, *ready), sent_early, end, mean)
+    eighth = (rows // 8, 2 * rows)
+    halved = kernel_call(
+        add_either_kernel, [(eighth, jnp.float32)] + [(eighth, jnp.bfloat16)] * 3, smem=1
+    )(middle, kept_early, kept, to_partner(sent, 1))
     result = ((rows, width), jnp.float32)
     held = kernel_call(
         functools.partial(held_kernel, total), [result],
-        smem=1, scratch=12, temps=[((rows, rows + NORM), jnp.bfloat16)],
+        smem=2, scratch=12, temps=[((rows, rows + NORM), jnp.bfloat16)],
     )(
-        order, near_own, to_partner(near_own, 1), own, z_anchor, z_other,
-        own_square, beside_square, after(opposite_square, halved[0]), mean, spread,
+        order, middle, near_own, to_partner(near_own, 1), own, z_anchor, z_other,
+        own_square, beside_square, swapped_square, after(end_square, halved[0]), mean, spread,
     )[0]
-    crossed = jnp.where(middle == 1, crossed, first)
-    second = jnp.concatenate([scatter(*halved), crossed], axis=1)
+    got = [to_partner(x, 2 * k) for k, x in enumerate(halved[1:], 1)]
+    second = kernel_call(total_either_kernel, [(eighth, jnp.bfloat16)], smem=1)(
+        middle, first, halved[0], *got
+    )[0]
     near = after(gather_chips(after(second, held)), *pushed)
     return kernel_call(
         functools.partial(last_kernel, total), [result],
         smem=2, scratch=12, temps=[((rows, 2 * rows), jnp.bfloat16)],
     )(
-        order, middle, near, to_partner(near, 1), beside, opposite, held, *pushed
+        order, middle, near, to_partner(near, 1), beside, swapped, end, held, *pushed
     )[0]
 
 

time: 94.7 us -> 94.7 us (level); the launches traced: 93.1 us -> 94.4 us
  starting transfers between devices: 47.2 us -> 42.4 us
  waiting for transfers between devices: 29.1 us -> 33.9 us
  Pallas kernels: 15.9 us -> 17.2 us
    ppermute x1, waiting for transfers between devices: 1.07 us -> 4.01 us  [by_line(): lax.ppermute(after(over, end), 'dp', across)]
    ppermute x24, starting transfers between devices: 30.3 us -> 28.1 us  [to_partner(): return lax.ppermute(x, 'feat', [(i, i ^ step) for i in range(8)])]
    ppermute x1, starting transfers between devices: 3.57 us -> 1.91 us  [by_line(): swapped = lax.ppermute(ahead, 'dp', across)]
    ppermute x1 -> x0, starting transfers between devices: 1.29 us -> none  [by_line(): crossed = lax.ppermute(first, 'dp', [(0, 1), (3, 2)])]
    pallas_call x16 -> x17, Pallas kernels: 15.9 us -> 17.2 us  [call(): pl.pallas_call(body, out_shape=[jax.ShapeDtypeStruct(s, t) for s, t in ou...]
    ppermute x1, waiting for transfers between devices: 1.52 us -> 2.79 us  [by_line(): swapped = lax.ppermute(ahead, 'dp', across)]
    ppermute x1 -> x0, waiting for transfers between devices: 1.24 us -> none  [by_line(): crossed = lax.ppermute(first, 'dp', [(0, 1), (3, 2)])]
    ppermute x24, waiting for transfers between devices: 24.1 us -> 25.2 us  [to_partner(): return lax.ppermute(x, 'feat', [(i, i ^ step) for i in range(8)])]
  transfers between devices with their start and end apart: 33 -> 32, of which waited for: 26 -> 25; matrix products, arithmetic and copies ran while one was open for 1% -> 1% of each run, Pallas kernels for 12% -> 13%
where the time goes in v16:
time: 94.7 us; the launch traced here: 94.4 us
  starting transfers between devices  42.4 us (45%)
  waiting for transfers between devices  33.9 us (36%)
  Pallas kernels  17.2 us (18%)
    ppermute x24, starting transfers between devices, to_partner(): return lax.ppermute(x, 'feat', [(i, i ^ step) for i in range(8)])  28.1 us
    ppermute x24, waiting for transfers between devices, to_partner(): return lax.ppermute(x, 'feat', [(i, i ^ step) for i in range(8)])  25.2 us
    pallas_call x17, Pallas kernels, call(): pl.pallas_call(body, out_shape=[jax.ShapeDtypeStruct(s, t) for s, t in ou...  17.2 us
    ppermute x3, starting transfers between devices, by_line(): lax.ppermute(stats, 'dp', [(i, (i + k) % 4) for i in range(4)])  4.72 us
    ppermute x1, waiting for transfers between devices, by_line(): lax.ppermute(after(over, end), 'dp', across)  4.01 us
    ppermute x1, waiting for transfers between devices, by_line(): swapped = lax.ppermute(ahead, 'dp', across)  2.79 us
    ppermute x1, starting transfers between devices, by_line(): beside_in = lax.ppermute(ahead, 'dp', [(i, i ^ 1) for i in range(4)])  2.33 us
    ppermute x1, starting transfers between devices, by_line(): lax.ppermute(after(over, end), 'dp', across)  2.32 us
  transfers between devices with their start and end apart: 32, of which 25 were waited for; matrix products, arithmetic and copies ran while one was open for 1% of the time, Pallas kernels for 13%

profile of v16, /device:TPU:9, one launch (start us, length us, event | category | flops | bytes accessed | tf_op | source)
XLA Modules:
  0.0 94.4 jit_solution(17611453287932789258)
XLA Ops:
  0.0 1.8 %shard_map.37 = f32[2,1024]{1,0:T(2,128)S(1)} custom-call(bf16[512,1024]{1,0:T(8,128)(2,1)} %z.5), custom_call_target="tpu_custom_call" | custom-call | tf_op jit(solution)/shard_map/pallas_call | solution.py:17
  1.9 2.5 %collective-permute-start.1 = (f32[2,1024]{1,0:T(2,128)S(1)}, f32[2,1024]{1,0:T(2,128)S(1)}, u32[]{:S(2)}, u32[]{:S(2)}) collective-permute-start(f32[2,1024]{1,0:T(2,128)S(1)} %shard_map.37), channel_id=1, source_target_pairs={{0,16},{8,24},{16,0},{24,8},{1,17},{9,25},{17,1},{25,9},{2,18},{10... | collective-permute-start | bytes 24584 | tf_op jit(solution)/shard_map/ppermute | solution.py:315
  4.3 2.2 %collective-permute-start = (f32[2,1024]{1,0:T(2,128)S(1)}, f32[2,1024]{1,0:T(2,128)S(1)}, u32[]{:S(2)}, u32[]{:S(2)}) collective-permute-start(f32[2,1024]{1,0:T(2,128)S(1)} %shard_map.37), channel_id=1, source_target_pairs={{0,8},{8,16},{16,24},{24,0},{1,9},{9,17},{17,25},{25,1},{2,10},{10... | collective-permute-start | bytes 24584 | tf_op jit(solution)/shard_map/ppermute | solution.py:315
  7.3 2.3 %collective-permute-start.10 = (bf16[512,1024]{1,0:T(8,128)(2,1)}, bf16[512,1024]{1,0:T(8,128)(2,1)S(1)}, u32[]{:S(2)}, u32[]{:S(2)}) collective-permute-start(bf16[512,1024]{1,0:T(8,128)(2,1)} %z.5), channel_id=1, source_target_pairs={{0,8},{8,0},{16,24},{24,16},{1,9},{9,1},{17,25},{25,17},{2,10},{10... | collective-permute-start | bytes 3145736 | tf_op jit(solution)/shard_map/ppermute | solution.py:318
  9.7 1.9 %collective-permute-start.11 = (bf16[512,1024]{1,0:T(8,128)(2,1)}, bf16[512,1024]{1,0:T(8,128)(2,1)}, u32[]{:S(2)}, u32[]{:S(2)}) collective-permute-start(bf16[512,1024]{1,0:T(8,128)(2,1)} %z.5), channel_id=1, source_target_pairs={{8,16},{16,8},{9,17},{17,9},{10,18},{18,10},{11,19},{19,11},{12,20... | collective-permute-start | bytes 3145736 | tf_op jit(solution)/shard_map/ppermute | solution.py:319
  12.3 2.4 %shard_map.38 = (bf16[512,1024]{1,0:T(8,128)(2,1)S(1)}, bf16[512,1024]{1,0:T(8,128)(2,1)S(1)}, f32[1,1024]{1,0:T(1,128)S(1)}, f32[256,640]{1,0:T(8,128)S(1)}, bf16[256,640]{1,0:T(8,128)(2,1)S(1)}) custom-call(s32[8]{0:T(128)S(1)} %broadcast_xor_fusion.order, bf16[512,1024]{1,0:T(8,128)(2,1)} %z.5, f32[1,1024]{1,0:T(1,128)S(1)} %get-tuple-element.88.mean), custom_call_target="tpu_custom_call" | custom-call | tf_op jit(solution)/shard_map/pallas_call | solution.py:17
  14.7 2.4 %collective-permute-start.3 = (bf16[256,640]{1,0:T(8,128)(2,1)S(1)}, bf16[256,640]{1,0:T(8,128)(2,1)S(1)}, u32[]{:S(2)}, u32[]{:S(2)}) collective-permute-start(bf16[256,640]{1,0:T(8,128)(2,1)S(1)} %get-tuple-element.48), channel_id=1, source_target_pairs={{0,1},{1,0},{2,3},{3,2},{4,5},{5,4},{6,7},{7,6},{8,9},{9,8},{10,11... | collective-permute-start | bytes 983048 | tf_op jit(solution)/shard_map/ppermute | solution.py:269
  18.5 1.3 %collective-permute-start.4 = (bf16[64,640]{1,0:T(8,128)(2,1)S(1)}, bf16[64,640]{1,0:T(8,128)(2,1)S(1)}, u32[]{:S(2)}, u32[]{:S(2)}) collective-permute-start(bf16[64,640]{1,0:T(8,128)(2,1)S(1)} %get-tuple-element.50), channel_id=1, source_target_pairs={{0,2},{1,3},{2,0},{3,1},{4,6},{5,7},{6,4},{7,5},{8,10},{9,11},{10,... | collective-permute-start | bytes 245768 | tf_op jit(solution)/shard_map/ppermute | solution.py:269
  23.5 1.7 %collective-permute-done.6.c = bf16[64,640]{1,0:T(8,128)(2,1)S(1)} collective-permute-done((bf16[64,640]{1,0:T(8,128)(2,1)S(1)}, bf16[64,640]{1,0:T(8,128)(2,1)S(1)}, u32[]{:S(2)}, u32[]{:S(2)}) %collective-permute-start.6) | collective-permute-done | bytes 81952 | tf_op jit(solution)/shard_map/ppermute | solution.py:269
  26.3 1.8 %collective-permute-start.9 = (bf16[64,640]{1,0:T(8,128)(2,1)S(1)}, bf16[64,640]{1,0:T(8,128)(2,1)S(1)}, u32[]{:S(2)}, u32[]{:S(2)}) collective-permute-start(bf16[64,640]{1,0:T(8,128)(2,1)S(1)} %shard_map.40.refs_0_), channel_id=1, source_target_pairs={{0,6},{1,7},{2,4},{3,5},{4,2},{5,3},{6,0},{7,1},{8,14},{9,15},{10,... | collective-permute-start | bytes 245768 | tf_op jit(solution)/shard_map/ppermute | solution.py:269
  31.3 2.8 %collective-permute-done.11.opposite_in = bf16[512,1024]{1,0:T(8,128)(2,1)} collective-permute-done((bf16[512,1024]{1,0:T(8,128)(2,1)}, bf16[512,1024]{1,0:T(8,128)(2,1)}, u32[]{:S(2)}, u32[]{:S(2)}) %collective-permute-start.11) | collective-permute-done | bytes 1048608 | tf_op jit(solution)/shard_map/ppermute | solution.py:319
  34.1 1.6 %collective-permute-start.20 = (bf16[512,1024]{1,0:T(8,128)(2,1)}, bf16[512,1024]{1,0:T(8,128)(2,1)}, u32[]{:S(2)}, u32[]{:S(2)}) collective-permute-start(bf16[512,1024]{1,0:T(8,128)(2,1)} %z.5), channel_id=1, source_target_pairs={{0,24},{24,0},{1,25},{25,1},{2,26},{26,2},{3,27},{27,3},{4,28},{28... | collective-permute-start | bytes 3145736 | tf_op jit(solution)/shard_map/ppermute | solution.py:333
  35.8 2.2 %shard_map.42 = (bf16[512,1024]{1,0:T(8,128)(2,1)S(1)}, f32[1,1024]{1,0:T(1,128)S(1)}, bf16[512,1024]{1,0:T(8,128)(2,1)S(1)}, f32[1,1024]{1,0:T(1,128)S(1)}, f32...) custom-call(s32[8]{0:T(128)S(1)} %broadcast_xor_fusion.order, s32[1]{0:T(128)} %bitcast.middle, ...), custom_call_target="tpu_custom_call" | custom-call | tf_op jit(solution)/shard_map/pallas_call | solution.py:17
  38.0 3.4 %collective-permute-start.12 = (bf16[256,512]{1,0:T(8,128)(2,1)S(1)}, bf16[256,512]{1,0:T(8,128)(2,1)S(1)}, u32[]{:S(2)}, u32[]{:S(2)}) collective-permute-start(bf16[256,512]{1,0:T(8,128)(2,1)S(1)} %get-tuple-element.56), channel_id=1, source_target_pairs={{0,1},{1,0},{2,3},{3,2},{4,5},{5,4},{6,7},{7,6},{8,9},{9,8},{10,11... | collective-permute-start | bytes 786440 | tf_op jit(solution)/shard_map/ppermute | solution.py:269
  42.6 1.3 %collective-permute-start.13 = (bf16[64,512]{1,0:T(8,128)(2,1)S(1)}, bf16[64,512]{1,0:T(8,128)(2,1)S(1)}, u32[]{:S(2)}, u32[]{:S(2)}) collective-permute-start(bf16[64,512]{1,0:T(8,128)(2,1)S(1)} %get-tuple-element.58), channel_id=1, source_target_pairs={{0,2},{1,3},{2,0},{3,1},{4,6},{5,7},{6,4},{7,5},{8,10},{9,11},{10,... | collective-permute-start | bytes 196616 | tf_op jit(solution)/shard_map/ppermute | solution.py:269
  47.0 2.1 %collective-permute-done.15.c = bf16[64,512]{1,0:T(8,128)(2,1)S(1)} collective-permute-done((bf16[64,512]{1,0:T(8,128)(2,1)S(1)}, bf16[64,512]{1,0:T(8,128)(2,1)S(1)}, u32[]{:S(2)}, u32[]{:S(2)}) %collective-permute-start.15) | collective-permute-done | bytes 65568 | tf_op jit(solution)/shard_map/ppermute | solution.py:269
  49.9 2.0 %collective-permute-start.18 = (bf16[64,512]{1,0:T(8,128)(2,1)S(1)}, bf16[64,512]{1,0:T(8,128)(2,1)S(1)}, u32[]{:S(2)}, u32[]{:S(2)}) collective-permute-start(bf16[64,512]{1,0:T(8,128)(2,1)S(1)} %shard_map.44.refs_0_.first), channel_id=1, source_target_pairs={{0,6},{1,7},{2,4},{3,5},{4,2},{5,3},{6,0},{7,1},{8,14},{9,15},{10,... | collective-permute-start | bytes 196616 | tf_op jit(solution)/shard_map/ppermute | solution.py:269
  51.9 1.3 %shard_map.45 = (f32[256,1024]{1,0:T(8,128)S(1)}, bf16[256,1024]{1,0:T(8,128)(2,1)S(1)}) custom-call(s32[1]{0:T(128)} %bitcast.middle, bf16[512,1024]{1,0:T(8,128)(2,1)S(1)} %get-tuple-element.71.turned, bf16[512,1024]{1,0:T(8,128)(2,1)S(1)} %get-tuple-element.62.beside, bf16[512,1024]{1,0:T(8,128)(2,1)S(1)} %get-tuple-element.63.opposite.swapped), custom_call_target="tpu_custom_call" | custom-call | tf_op jit(solution)/shard_map/pallas_call | solution.py:17
  53.9 3.7 %collective-permute-start.19 = (bf16[256,512]{1,0:T(8,128)(2,1)S(1)}, bf16[256,512]{1,0:T(8,128)(2,1)S(1)}, u32[]{:S(2)}, u32[]{:S(2)}) collective-permute-start(bf16[256,512]{1,0:T(8,128)(2,1)S(1)} %shard_map.46.near), channel_id=1, source_target_pairs={{0,1},{1,0},{2,3},{3,2},{4,5},{5,4},{6,7},{7,6},{8,9},{9,8},{10,11... | collective-permute-start | bytes 786440 | tf_op jit(solution)/shard_map/ppermute | solution.py:269
  58.8 1.8 %shard_map.47 = (bf16[512,1024]{1,0:T(8,128)(2,1)S(1)}, bf16[512,1024]{1,0:T(8,128)(2,1)S(1)}) custom-call(s32[8]{0:T(128)S(1)} %broadcast_xor_fusion.order, s32[1]{0:T(128)} %bitcast.middle, bf16[256,512]{1,0:T(8,128)(2,1)S(1)} %shard_map.46.near, bf16[256,512]{1,0:T(8,128)(2,1)S(1)} %collective-permute-done.19.far, ...), custom_call_target="tpu_custom_call" | custom-call | tf_op jit(solution)/shard_map/pallas_call | solution.py:17
  60.6 1.4 %collective-permute-start.29 = (bf16[512,1024]{1,0:T(8,128)(2,1)S(1)}, bf16[512,1024]{1,0:T(8,128)(2,1)S(1)}, u32[]{:S(2)}, u32[]{:S(2)}) collective-permute-start(bf16[512,1024]{1,0:T(8,128)(2,1)S(1)} %get-tuple-element.69), channel_id=1, source_target_pairs={{8,0},{16,24},{9,1},{17,25},{10,2},{18,26},{11,3},{19,27},{12,4},{... | collective-permute-start | bytes 3145736 | tf_op jit(solution)/shard_map/ppermute | solution.py:349
  62.0 2.3 %collective-permute-start.30 = (bf16[512,1024]{1,0:T(8,128)(2,1)S(1)}, bf16[512,1024]{1,0:T(8,128)(2,1)S(1)}, u32[]{:S(2)}, u32[]{:S(2)}) collective-permute-start(bf16[512,1024]{1,0:T(8,128)(2,1)S(1)} %get-tuple-element.84), channel_id=1, source_target_pairs={{8,16},{16,8},{9,17},{17,9},{10,18},{18,10},{11,19},{19,11},{12,20... | collective-permute-start | bytes 3145736 | tf_op jit(solution)/shard_map/ppermute | solution.py:349
  66.7 1.5 %collective-permute-done.21.got = bf16[256,1024]{1,0:T(8,128)(2,1)S(1)} collective-permute-done((bf16[256,1024]{1,0:T(8,128)(2,1)S(1)}, bf16[256,1024]{1,0:T(8,128)(2,1)S(1)}, u32[]{:S(2)}, u32[]{:S(2)}) %collective-permute-start.21) | collective-permute-done | bytes 524320 | tf_op jit(solution)/shard_map/ppermute | solution.py:269
  68.2 1.3 %collective-permute-start.22 = (bf16[64,1024]{1,0:T(8,128)(2,1)S(1)}, bf16[64,1024]{1,0:T(8,128)(2,1)S(1)}, u32[]{:S(2)}, u32[]{:S(2)}) collective-permute-start(bf16[64,1024]{1,0:T(8,128)(2,1)S(1)} %get-tuple-element.76), channel_id=1, source_target_pairs={{0,2},{1,3},{2,0},{3,1},{4,6},{5,7},{6,4},{7,5},{8,10},{9,11},{10,... | collective-permute-start | bytes 393224 | tf_op jit(solution)/shard_map/ppermute | solution.py:269
  70.9 2.6 %shard_map.51.held = f32[512,1024]{1,0:T(8,128)S(1)} custom-call(s32[8]{0:T(128)S(1)} %broadcast_xor_fusion.order, s32[1]{0:T(128)} %bitcast.middle, bf16[256,640]{1,0:T(8,128)(2,1)S(1)} %shard_map.41.near, bf16[256,640]{1,0:T(8,128)(2,1)S(1)} %collective-permute-done.25.far, bf16[512,1024]{1,0:T(8,128)(2,1)S(1)} %get-tuple-element.79.own, ...), custom_call_target="tpu_custom_call" | custom-call | tf_op jit(solution)/shard_map/pallas_call | solution.py:17
  73.9 2.7 %collective-permute-done.24.c = bf16[64,1024]{1,0:T(8,128)(2,1)S(1)} collective-permute-done((bf16[64,1024]{1,0:T(8,128)(2,1)S(1)}, bf16[64,1024]{1,0:T(8,128)(2,1)S(1)}, u32[]{:S(2)}, u32[]{:S(2)}) %collective-permute-start.24) | collective-permute-done | bytes 131104 | tf_op jit(solution)/shard_map/ppermute | solution.py:269
  76.6 1.5 %collective-permute-start.26 = (bf16[64,1024]{1,0:T(8,128)(2,1)S(1)}, bf16[64,1024]{1,0:T(8,128)(2,1)S(1)}, u32[]{:S(2)}, u32[]{:S(2)}) collective-permute-start(bf16[64,1024]{1,0:T(8,128)(2,1)S(1)} %shard_map.50.refs_0_), channel_id=1, source_target_pairs={{0,2},{1,3},{2,0},{3,1},{4,6},{5,7},{6,4},{7,5},{8,10},{9,11},{10,... | collective-permute-start | bytes 393224 | tf_op jit(solution)/shard_map/ppermute | solution.py:269
  79.4 1.4 %collective-permute-done.26.refs_1_ = bf16[64,1024]{1,0:T(8,128)(2,1)S(1)} collective-permute-done((bf16[64,1024]{1,0:T(8,128)(2,1)S(1)}, bf16[64,1024]{1,0:T(8,128)(2,1)S(1)}, u32[]{:S(2)}, u32[]{:S(2)}) %collective-permute-start.26) | collective-permute-done | bytes 131104 | tf_op jit(solution)/shard_map/ppermute | solution.py:269
  80.8 2.1 %collective-permute-done.27.refs_2_ = bf16[64,1024]{1,0:T(8,128)(2,1)S(1)} collective-permute-done((bf16[64,1024]{1,0:T(8,128)(2,1)S(1)}, bf16[64,1024]{1,0:T(8,128)(2,1)S(1)}, u32[]{:S(2)}, u32[]{:S(2)}) %collective-permute-start.27) | collective-permute-done | bytes 131104 | tf_op jit(solution)/shard_map/ppermute | solution.py:269
  84.4 4.0 %collective-permute-done.30.over = bf16[512,1024]{1,0:T(8,128)(2,1)S(1)} collective-permute-done((bf16[512,1024]{1,0:T(8,128)(2,1)S(1)}, bf16[512,1024]{1,0:T(8,128)(2,1)S(1)}, u32[]{:S(2)}, u32[]{:S(2)}) %collective-permute-start.30) | collective-permute-done | bytes 1048608 | tf_op jit(solution)/shard_map/ppermute | solution.py:349
  89.6 1.5 %collective-permute-done.31.far = bf16[256,1024]{1,0:T(8,128)(2,1)S(1)} collective-permute-done((bf16[256,1024]{1,0:T(8,128)(2,1)S(1)}, bf16[256,1024]{1,0:T(8,128)(2,1)S(1)}, u32[]{:S(2)}, u32[]{:S(2)}) %collective-permute-start.31) | collective-permute-done | bytes 524320 | tf_op jit(solution)/shard_map/ppermute | solution.py:269
  91.1 3.3 %shard_map.53 = f32[512,1024]{1,0:T(8,128)} custom-call(s32[8]{0:T(128)S(1)} %broadcast_xor_fusion.order, s32[1]{0:T(128)} %bitcast.middle, bf16[256,1024]{1,0:T(8,128)(2,1)S(1)} %shard_map.52.near, bf16[256,1024]{1,0:T(8,128)(2,1)S(1)} %collective-permute-done.31.far, bf16[512,1024]{1,0:T(8,128)(2,1)S(1)} %get-tuple-element.62.beside, ...), custom_call_target="tpu_custom_call" | custom-call | tf_op jit(solution)/shard_map/pallas_call | solution.py:17
  (53 shorter events, 26.1 us)
Async XLA Ops:
  1.8 4.7 %collective-permute-start.2 = (f32[2,1024]{1,0:T(2,128)S(1)}, f32[2,1024]{1,0:T(2,128)S(1)}, u32[]{:S(2)}, u32[]{:S(2)}) collective-permute-start(f32[2,1024]{1,0:T(2,128)S(1)} %shard_map.37), channel_id=1, source_target_pairs={{0,24},{8,0},{16,8},{24,16},{1,25},{9,1},{17,9},{25,17},{2,26},{10... | collective-permute-start | bytes 24584 | tf_op jit(solution)/shard_map/ppermute | solution.py:315
  1.9 4.7 %collective-permute-start.1 = (f32[2,1024]{1,0:T(2,128)S(1)}, f32[2,1024]{1,0:T(2,128)S(1)}, u32[]{:S(2)}, u32[]{:S(2)}) collective-permute-start(f32[2,1024]{1,0:T(2,128)S(1)} %shard_map.37), channel_id=1, source_target_pairs={{0,16},{8,24},{16,0},{24,8},{1,17},{9,25},{17,1},{25,9},{2,18},{10... | collective-permute-start | bytes 24584 | tf_op jit(solution)/shard_map/ppermute | solution.py:315
  4.3 3.0 %collective-permute-start = (f32[2,1024]{1,0:T(2,128)S(1)}, f32[2,1024]{1,0:T(2,128)S(1)}, u32[]{:S(2)}, u32[]{:S(2)}) collective-permute-start(f32[2,1024]{1,0:T(2,128)S(1)} %shard_map.37), channel_id=1, source_target_pairs={{0,8},{8,16},{16,24},{24,0},{1,9},{9,17},{17,25},{25,1},{2,10},{10... | collective-permute-start | bytes 24584 | tf_op jit(solution)/shard_map/ppermute | solution.py:315
  7.3 24.0 %collective-permute-start.10 = (bf16[512,1024]{1,0:T(8,128)(2,1)}, bf16[512,1024]{1,0:T(8,128)(2,1)S(1)}, u32[]{:S(2)}, u32[]{:S(2)}) collective-permute-start(bf16[512,1024]{1,0:T(8,128)(2,1)} %z.5), channel_id=1, source_target_pairs={{0,8},{8,0},{16,24},{24,16},{1,9},{9,1},{17,25},{25,17},{2,10},{10... | collective-permute-start | bytes 3145736 | tf_op jit(solution)/shard_map/ppermute | solution.py:318
  9.7 24.5 %collective-permute-start.11 = (bf16[512,1024]{1,0:T(8,128)(2,1)}, bf16[512,1024]{1,0:T(8,128)(2,1)}, u32[]{:S(2)}, u32[]{:S(2)}) collective-permute-start(bf16[512,1024]{1,0:T(8,128)(2,1)} %z.5), channel_id=1, source_target_pairs={{8,16},{16,8},{9,17},{17,9},{10,18},{18,10},{11,19},{19,11},{12,20... | collective-permute-start | bytes 3145736 | tf_op jit(solution)/shard_map/ppermute | solution.py:319
  14.7 3.7 %collective-permute-start.3 = (bf16[256,640]{1,0:T(8,128)(2,1)S(1)}, bf16[256,640]{1,0:T(8,128)(2,1)S(1)}, u32[]{:S(2)}, u32[]{:S(2)}) collective-permute-start(bf16[256,640]{1,0:T(8,128)(2,1)S(1)} %get-tuple-element.48), channel_id=1, source_target_pairs={{0,1},{1,0},{2,3},{3,2},{4,5},{5,4},{6,7},{7,6},{8,9},{9,8},{10,11... | collective-permute-start | bytes 983048 | tf_op jit(solution)/shard_map/ppermute | solution.py:269
  18.5 3.8 %collective-permute-start.4 = (bf16[64,640]{1,0:T(8,128)(2,1)S(1)}, bf16[64,640]{1,0:T(8,128)(2,1)S(1)}, u32[]{:S(2)}, u32[]{:S(2)}) collective-permute-start(bf16[64,640]{1,0:T(8,128)(2,1)S(1)} %get-tuple-element.50), channel_id=1, source_target_pairs={{0,2},{1,3},{2,0},{3,1},{4,6},{5,7},{6,4},{7,5},{8,10},{9,11},{10,... | collective-permute-start | bytes 245768 | tf_op jit(solution)/shard_map/ppermute | solution.py:269
  19.8 3.7 %collective-permute-start.5 = (bf16[64,640]{1,0:T(8,128)(2,1)S(1)}, bf16[64,640]{1,0:T(8,128)(2,1)S(1)}, u32[]{:S(2)}, u32[]{:S(2)}) collective-permute-start(bf16[64,640]{1,0:T(8,128)(2,1)S(1)} %get-tuple-element.51), channel_id=1, source_target_pairs={{0,4},{1,5},{2,6},{3,7},{4,0},{5,1},{6,2},{7,3},{8,12},{9,13},{10,... | collective-permute-start | bytes 245768 | tf_op jit(solution)/shard_map/ppermute | solution.py:269
  21.0 4.2 %collective-permute-start.6 = (bf16[64,640]{1,0:T(8,128)(2,1)S(1)}, bf16[64,640]{1,0:T(8,128)(2,1)S(1)}, u32[]{:S(2)}, u32[]{:S(2)}) collective-permute-start(bf16[64,640]{1,0:T(8,128)(2,1)S(1)} %get-tuple-element.52), channel_id=1, source_target_pairs={{0,6},{1,7},{2,4},{3,5},{4,2},{5,3},{6,0},{7,1},{8,14},{9,15},{10,... | collective-permute-start | bytes 245768 | tf_op jit(solution)/shard_map/ppermute | solution.py:269
  25.3 3.8 %collective-permute-start.7 = (bf16[64,640]{1,0:T(8,128)(2,1)S(1)}, bf16[64,640]{1,0:T(8,128)(2,1)S(1)}, u32[]{:S(2)}, u32[]{:S(2)}) collective-permute-start(bf16[64,640]{1,0:T(8,128)(2,1)S(1)} %shard_map.40.refs_0_), channel_id=1, source_target_pairs={{0,2},{1,3},{2,0},{3,1},{4,6},{5,7},{6,4},{7,5},{8,10},{9,11},{10,... | collective-permute-start | bytes 245768 | tf_op jit(solution)/shard_map/ppermute | solution.py:269
  26.0 3.7 %collective-permute-start.8 = (bf16[64,640]{1,0:T(8,128)(2,1)S(1)}, bf16[64,640]{1,0:T(8,128)(2,1)S(1)}, u32[]{:S(2)}, u32[]{:S(2)}) collective-permute-start(bf16[64,640]{1,0:T(8,128)(2,1)S(1)} %shard_map.40.refs_0_), channel_id=1, source_target_pairs={{0,4},{1,5},{2,6},{3,7},{4,0},{5,1},{6,2},{7,3},{8,12},{9,13},{10,... | collective-permute-start | bytes 245768 | tf_op jit(solution)/shard_map/ppermute | solution.py:269
  26.3 4.2 %collective-permute-start.9 = (bf16[64,640]{1,0:T(8,128)(2,1)S(1)}, bf16[64,640]{1,0:T(8,128)(2,1)S(1)}, u32[]{:S(2)}, u32[]{:S(2)}) collective-permute-start(bf16[64,640]{1,0:T(8,128)(2,1)S(1)} %shard_map.40.refs_0_), channel_id=1, source_target_pairs={{0,6},{1,7},{2,4},{3,5},{4,2},{5,3},{6,0},{7,1},{8,14},{9,15},{10,... | collective-permute-start | bytes 245768 | tf_op jit(solution)/shard_map/ppermute | solution.py:269
  34.1 27.8 %collective-permute-start.20 = (bf16[512,1024]{1,0:T(8,128)(2,1)}, bf16[512,1024]{1,0:T(8,128)(2,1)}, u32[]{:S(2)}, u32[]{:S(2)}) collective-permute-start(bf16[512,1024]{1,0:T(8,128)(2,1)} %z.5), channel_id=1, source_target_pairs={{0,24},{24,0},{1,25},{25,1},{2,26},{26,2},{3,27},{27,3},{4,28},{28... | collective-permute-start | bytes 3145736 | tf_op jit(solution)/shard_map/ppermute | solution.py:333
  38.0 4.5 %collective-permute-start.12 = (bf16[256,512]{1,0:T(8,128)(2,1)S(1)}, bf16[256,512]{1,0:T(8,128)(2,1)S(1)}, u32[]{:S(2)}, u32[]{:S(2)}) collective-permute-start(bf16[256,512]{1,0:T(8,128)(2,1)S(1)} %get-tuple-element.56), channel_id=1, source_target_pairs={{0,1},{1,0},{2,3},{3,2},{4,5},{5,4},{6,7},{7,6},{8,9},{9,8},{10,11... | collective-permute-start | bytes 786440 | tf_op jit(solution)/shard_map/ppermute | solution.py:269
  42.6 3.2 %collective-permute-start.13 = (bf16[64,512]{1,0:T(8,128)(2,1)S(1)}, bf16[64,512]{1,0:T(8,128)(2,1)S(1)}, u32[]{:S(2)}, u32[]{:S(2)}) collective-permute-start(bf16[64,512]{1,0:T(8,128)(2,1)S(1)} %get-tuple-element.58), channel_id=1, source_target_pairs={{0,2},{1,3},{2,0},{3,1},{4,6},{5,7},{6,4},{7,5},{8,10},{9,11},{10,... | collective-permute-start | bytes 196616 | tf_op jit(solution)/shard_map/ppermute | solution.py:269
  43.9 3.1 %collective-permute-start.14 = (bf16[64,512]{1,0:T(8,128)(2,1)S(1)}, bf16[64,512]{1,0:T(8,128)(2,1)S(1)}, u32[]{:S(2)}, u32[]{:S(2)}) collective-permute-start(bf16[64,512]{1,0:T(8,128)(2,1)S(1)} %get-tuple-element.59), channel_id=1, source_target_pairs={{0,4},{1,5},{2,6},{3,7},{4,0},{5,1},{6,2},{7,3},{8,12},{9,13},{10,... | collective-permute-start | bytes 196616 | tf_op jit(solution)/shard_map/ppermute | solution.py:269
  45.1 4.0 %collective-permute-start.15 = (bf16[64,512]{1,0:T(8,128)(2,1)S(1)}, bf16[64,512]{1,0:T(8,128)(2,1)S(1)}, u32[]{:S(2)}, u32[]{:S(2)}) collective-permute-start(bf16[64,512]{1,0:T(8,128)(2,1)S(1)} %get-tuple-element.60), channel_id=1, source_target_pairs={{0,6},{1,7},{2,4},{3,5},{4,2},{5,3},{6,0},{7,1},{8,14},{9,15},{10,... | collective-permute-start | bytes 196616 | tf_op jit(solution)/shard_map/ppermute | solution.py:269
  49.1 4.0 %collective-permute-start.16 = (bf16[64,512]{1,0:T(8,128)(2,1)S(1)}, bf16[64,512]{1,0:T(8,128)(2,1)S(1)}, u32[]{:S(2)}, u32[]{:S(2)}) collective-permute-start(bf16[64,512]{1,0:T(8,128)(2,1)S(1)} %shard_map.44.refs_0_.first), channel_id=1, source_target_pairs={{0,2},{1,3},{2,0},{3,1},{4,6},{5,7},{6,4},{7,5},{8,10},{9,11},{10,... | collective-permute-start | bytes 196616 | tf_op jit(solution)/shard_map/ppermute | solution.py:269
  49.6 3.6 %collective-permute-start.17 = (bf16[64,512]{1,0:T(8,128)(2,1)S(1)}, bf16[64,512]{1,0:T(8,128)(2,1)S(1)}, u32[]{:S(2)}, u32[]{:S(2)}) collective-permute-start(bf16[64,512]{1,0:T(8,128)(2,1)S(1)} %shard_map.44.refs_0_.first), channel_id=1, source_target_pairs={{0,4},{1,5},{2,6},{3,7},{4,0},{5,1},{6,2},{7,3},{8,12},{9,13},{10,... | collective-permute-start | bytes 196616 | tf_op jit(solution)/shard_map/ppermute | solution.py:269
  49.9 4.0 %collective-permute-start.18 = (bf16[64,512]{1,0:T(8,128)(2,1)S(1)}, bf16[64,512]{1,0:T(8,128)(2,1)S(1)}, u32[]{:S(2)}, u32[]{:S(2)}) collective-permute-start(bf16[64,512]{1,0:T(8,128)(2,1)S(1)} %shard_map.44.refs_0_.first), channel_id=1, source_target_pairs={{0,6},{1,7},{2,4},{3,5},{4,2},{5,3},{6,0},{7,1},{8,14},{9,15},{10,... | collective-permute-start | bytes 196616 | tf_op jit(solution)/shard_map/ppermute | solution.py:269
  53.9 4.9 %collective-permute-start.19 = (bf16[256,512]{1,0:T(8,128)(2,1)S(1)}, bf16[256,512]{1,0:T(8,128)(2,1)S(1)}, u32[]{:S(2)}, u32[]{:S(2)}) collective-permute-start(bf16[256,512]{1,0:T(8,128)(2,1)S(1)} %shard_map.46.near), channel_id=1, source_target_pairs={{0,1},{1,0},{2,3},{3,2},{4,5},{5,4},{6,7},{7,6},{8,9},{9,8},{10,11... | collective-permute-start | bytes 786440 | tf_op jit(solution)/shard_map/ppermute | solution.py:269
  60.6 23.8 %collective-permute-start.29 = (bf16[512,1024]{1,0:T(8,128)(2,1)S(1)}, bf16[512,1024]{1,0:T(8,128)(2,1)S(1)}, u32[]{:S(2)}, u32[]{:S(2)}) collective-permute-start(bf16[512,1024]{1,0:T(8,128)(2,1)S(1)} %get-tuple-element.69), channel_id=1, source_target_pairs={{8,0},{16,24},{9,1},{17,25},{10,2},{18,26},{11,3},{19,27},{12,4},{... | collective-permute-start | bytes 3145736 | tf_op jit(solution)/shard_map/ppermute | solution.py:349
  62.0 26.4 %collective-permute-start.30 = (bf16[512,1024]{1,0:T(8,128)(2,1)S(1)}, bf16[512,1024]{1,0:T(8,128)(2,1)S(1)}, u32[]{:S(2)}, u32[]{:S(2)}) collective-permute-start(bf16[512,1024]{1,0:T(8,128)(2,1)S(1)} %get-tuple-element.84), channel_id=1, source_target_pairs={{8,16},{16,8},{9,17},{17,9},{10,18},{18,10},{11,19},{19,11},{12,20... | collective-permute-start | bytes 3145736 | tf_op jit(solution)/shard_map/ppermute | solution.py:349
  65.6 2.5 %collective-permute-start.21 = (bf16[256,1024]{1,0:T(8,128)(2,1)S(1)}, bf16[256,1024]{1,0:T(8,128)(2,1)S(1)}, u32[]{:S(2)}, u32[]{:S(2)}) collective-permute-start(bf16[256,1024]{1,0:T(8,128)(2,1)S(1)} %get-tuple-element.74), channel_id=1, source_target_pairs={{0,1},{1,0},{2,3},{3,2},{4,5},{5,4},{6,7},{7,6},{8,9},{9,8},{10,11... | collective-permute-start | bytes 1572872 | tf_op jit(solution)/shard_map/ppermute | solution.py:269
  66.6 4.2 %collective-permute-start.25 = (bf16[256,640]{1,0:T(8,128)(2,1)S(1)}, bf16[256,640]{1,0:T(8,128)(2,1)S(1)}, u32[]{:S(2)}, u32[]{:S(2)}) collective-permute-start(bf16[256,640]{1,0:T(8,128)(2,1)S(1)} %shard_map.41.near), channel_id=1, source_target_pairs={{0,1},{1,0},{2,3},{3,2},{4,5},{5,4},{6,7},{7,6},{8,9},{9,8},{10,11... | collective-permute-start | bytes 983048 | tf_op jit(solution)/shard_map/ppermute | solution.py:269
  68.2 5.3 %collective-permute-start.22 = (bf16[64,1024]{1,0:T(8,128)(2,1)S(1)}, bf16[64,1024]{1,0:T(8,128)(2,1)S(1)}, u32[]{:S(2)}, u32[]{:S(2)}) collective-permute-start(bf16[64,1024]{1,0:T(8,128)(2,1)S(1)} %get-tuple-element.76), channel_id=1, source_target_pairs={{0,2},{1,3},{2,0},{3,1},{4,6},{5,7},{6,4},{7,5},{8,10},{9,11},{10,... | collective-permute-start | bytes 393224 | tf_op jit(solution)/shard_map/ppermute | solution.py:269
  69.5 4.4 %collective-permute-start.23 = (bf16[64,1024]{1,0:T(8,128)(2,1)S(1)}, bf16[64,1024]{1,0:T(8,128)(2,1)S(1)}, u32[]{:S(2)}, u32[]{:S(2)}) collective-permute-start(bf16[64,1024]{1,0:T(8,128)(2,1)S(1)} %get-tuple-element.77), channel_id=1, source_target_pairs={{0,4},{1,5},{2,6},{3,7},{4,0},{5,1},{6,2},{7,3},{8,12},{9,13},{10,... | collective-permute-start | bytes 393224 | tf_op jit(solution)/shard_map/ppermute | solution.py:269
  70.7 5.8 %collective-permute-start.24 = (bf16[64,1024]{1,0:T(8,128)(2,1)S(1)}, bf16[64,1024]{1,0:T(8,128)(2,1)S(1)}, u32[]{:S(2)}, u32[]{:S(2)}) collective-permute-start(bf16[64,1024]{1,0:T(8,128)(2,1)S(1)} %get-tuple-element.78), channel_id=1, source_target_pairs={{0,6},{1,7},{2,4},{3,5},{4,2},{5,3},{6,0},{7,1},{8,14},{9,15},{10,... | collective-permute-start | bytes 393224 | tf_op jit(solution)/shard_map/ppermute | solution.py:269
  76.6 4.2 %collective-permute-start.26 = (bf16[64,1024]{1,0:T(8,128)(2,1)S(1)}, bf16[64,1024]{1,0:T(8,128)(2,1)S(1)}, u32[]{:S(2)}, u32[]{:S(2)}) collective-permute-start(bf16[64,1024]{1,0:T(8,128)(2,1)S(1)} %shard_map.50.refs_0_), channel_id=1, source_target_pairs={{0,2},{1,3},{2,0},{3,1},{4,6},{5,7},{6,4},{7,5},{8,10},{9,11},{10,... | collective-permute-start | bytes 393224 | tf_op jit(solution)/shard_map/ppermute | solution.py:269
  78.1 4.8 %collective-permute-start.27 = (bf16[64,1024]{1,0:T(8,128)(2,1)S(1)}, bf16[64,1024]{1,0:T(8,128)(2,1)S(1)}, u32[]{:S(2)}, u32[]{:S(2)}) collective-permute-start(bf16[64,1024]{1,0:T(8,128)(2,1)S(1)} %shard_map.50.refs_0_), channel_id=1, source_target_pairs={{0,4},{1,5},{2,6},{3,7},{4,0},{5,1},{6,2},{7,3},{8,12},{9,13},{10,... | collective-permute-start | bytes 393224 | tf_op jit(solution)/shard_map/ppermute | solution.py:269
  78.4 5.7 %collective-permute-start.28 = (bf16[64,1024]{1,0:T(8,128)(2,1)S(1)}, bf16[64,1024]{1,0:T(8,128)(2,1)S(1)}, u32[]{:S(2)}, u32[]{:S(2)}) collective-permute-start(bf16[64,1024]{1,0:T(8,128)(2,1)S(1)} %shard_map.50.refs_0_), channel_id=1, source_target_pairs={{0,6},{1,7},{2,4},{3,5},{4,2},{5,3},{6,0},{7,1},{8,14},{9,15},{10,... | collective-permute-start | bytes 393224 | tf_op jit(solution)/shard_map/ppermute | solution.py:269
  88.4 2.7 %collective-permute-start.31 = (bf16[256,1024]{1,0:T(8,128)(2,1)S(1)}, bf16[256,1024]{1,0:T(8,128)(2,1)S(1)}, u32[]{:S(2)}, u32[]{:S(2)}) collective-permute-start(bf16[256,1024]{1,0:T(8,128)(2,1)S(1)} %shard_map.52.near), channel_id=1, source_target_pairs={{0,1},{1,0},{2,3},{3,2},{4,5},{5,4},{6,7},{7,6},{8,9},{9,8},{10,11... | collective-permute-start | bytes 1572872 | tf_op jit(solution)/shard_map/ppermute | solution.py:269
  (1 other events, 9.0 us)

commit v17 on v16

--- a/solution.py
+++ b/solution.py
@@ -314,7 +314,7 @@
     all_stats = [stats] + [
         lax.ppermute(stats, "dp", [(i, (i + k) % 4) for i in range(4)]) for k in (1, 2, 3)
     ]
-    ahead = after(z_anchor, *all_stats)
+    ahead = after(z_anchor, stats)
     beside_in = lax.ppermute(ahead, "dp", [(i, i ^ 1) for i in range(4)])
     swapped = lax.ppermute(ahead, "dp", across)
     mean = (all_stats[0][:1] + all_stats[1][:1] + all_stats[2][:1] + all_stats[3][:1]) / 4
@@ -329,8 +329,9 @@
     own, turned, own_square, kept, sent = kernel_call(
         own_kernel, [block, block, flat, *summands(rows + NORM)], smem=1, scratch=12
     )(order, z_anchor, mean)
-    near_own = gather_chips(scatter(*halve(kept, sent, rows), last=rows))
-    end = lax.ppermute(after(z_anchor, beside_in, swapped, near_own), "dp", [(0, 3), (3, 0)])
+    near_own = scatter(*halve(kept, sent, rows), last=rows)
+    near_own = jnp.concatenate([near_own] + [to_partner(near_own, 2 * k) for k in (1, 2, 3)])
+    end = lax.ppermute(after(z_anchor, swapped, near_own), "dp", [(0, 3), (3, 0)])
 
     beside, beside_square, swapped, swapped_square, kept, sent = kernel_call(
         first_kernel, [block, flat, block, flat, *summands(rows)],

time: 94.7 us -> 114 us (1.20)
  starting transfers between devices: 42.4 us -> 62.9 us
  waiting for transfers between devices: 33.9 us -> 32.7 us
    ppermute x24, starting transfers between devices: 28.1 us -> 48.9 us  [to_partner(): return lax.ppermute(x, 'feat', [(i, i ^ step) for i in range(8)])]
    ppermute x1, starting transfers between devices: 2.33 us -> 0.01 us  [by_line(): beside_in = lax.ppermute(ahead, 'dp', [(i, i ^ 1) for i in range(4)])]
    ppermute x1, starting transfers between devices: 1.91 us -> 3.08 us  [by_line(): swapped = lax.ppermute(ahead, 'dp', across)]
    pallas_call x17 -> x16, Pallas kernels: 17.2 us -> 17.2 us  [call(): pl.pallas_call(body, out_shape=[jax.ShapeDtypeStruct(s, t) for s, t in ou...]
  transfers between devices with their start and end apart: 32 -> 32, of which waited for: 25 -> 22; matrix products, arithmetic and copies ran while one was open for 1% -> 1% of each run, Pallas kernels for 13% -> 11%
where the time goes in v17:
time: 114 us
  starting transfers between devices  62.9 us (55%)
  waiting for transfers between devices  32.7 us (29%)
  Pallas kernels  17.2 us (15%)
    ppermute x24, starting transfers between devices, to_partner(): return lax.ppermute(x, 'feat', [(i, i ^ step) for i in range(8)])  48.9 us
    ppermute x24, waiting for transfers between devices, to_partner(): return lax.ppermute(x, 'feat', [(i, i ^ step) for i in range(8)])  25.6 us
    pallas_call x16, Pallas kernels, call(): pl.pallas_call(body, out_shape=[jax.ShapeDtypeStruct(s, t) for s, t in ou...  17.2 us
    ppermute x3, starting transfers between devices, by_line(): lax.ppermute(stats, 'dp', [(i, (i + k) % 4) for i in range(4)])  4.72 us
    ppermute x1, waiting for transfers between devices, by_line(): lax.ppermute(after(over, end), 'dp', across)  3.62 us
    ppermute x1, waiting for transfers between devices, by_line(): swapped = lax.ppermute(ahead, 'dp', across)  3.53 us
    ppermute x1, starting transfers between devices, by_line(): lax.ppermute(after(over, end), 'dp', across)  3.22 us
    ppermute x1, starting transfers between devices, by_line(): swapped = lax.ppermute(ahead, 'dp', across)  3.08 us
  transfers between devices with their start and end apart: 32, of which 22 were waited for; matrix products, arithmetic and copies ran while one was open for 1% of the time, Pallas kernels for 11%

profile of v17, /device:TPU:9, one launch (start us, length us, event | category | flops | bytes accessed | tf_op | source)
XLA Modules:
  0.0 113.7 jit_solution(11607695392555861036)
XLA Ops:
  0.0 1.8 %shard_map.37 = f32[2,1024]{1,0:T(2,128)S(1)} custom-call(bf16[512,1024]{1,0:T(8,128)(2,1)} %z.5), custom_call_target="tpu_custom_call" | custom-call | tf_op jit(solution)/shard_map/pallas_call | solution.py:17
  1.9 2.5 %collective-permute-start.1 = (f32[2,1024]{1,0:T(2,128)S(1)}, f32[2,1024]{1,0:T(2,128)S(1)}, u32[]{:S(2)}, u32[]{:S(2)}) collective-permute-start(f32[2,1024]{1,0:T(2,128)S(1)} %shard_map.37), channel_id=1, source_target_pairs={{0,16},{8,24},{16,0},{24,8},{1,17},{9,25},{17,1},{25,9},{2,18},{10... | collective-permute-start | bytes 24584 | tf_op jit(solution)/shard_map/ppermute | solution.py:315
  4.3 2.2 %collective-permute-start = (f32[2,1024]{1,0:T(2,128)S(1)}, f32[2,1024]{1,0:T(2,128)S(1)}, u32[]{:S(2)}, u32[]{:S(2)}) collective-permute-start(f32[2,1024]{1,0:T(2,128)S(1)} %shard_map.37), channel_id=1, source_target_pairs={{0,8},{8,16},{16,24},{24,0},{1,9},{9,17},{17,25},{25,1},{2,10},{10... | collective-permute-start | bytes 24584 | tf_op jit(solution)/shard_map/ppermute | solution.py:315
  6.5 3.1 %collective-permute-start.11 = (bf16[512,1024]{1,0:T(8,128)(2,1)}, bf16[512,1024]{1,0:T(8,128)(2,1)}, u32[]{:S(2)}, u32[]{:S(2)}) collective-permute-start(bf16[512,1024]{1,0:T(8,128)(2,1)} %z.5), channel_id=1, source_target_pairs={{8,16},{16,8},{9,17},{17,9},{10,18},{18,10},{11,19},{19,11},{12,20... | collective-permute-start | bytes 3145736 | tf_op jit(solution)/shard_map/ppermute | solution.py:319
  10.4 2.4 %shard_map.38 = (bf16[512,1024]{1,0:T(8,128)(2,1)S(1)}, bf16[512,1024]{1,0:T(8,128)(2,1)S(1)}, f32[1,1024]{1,0:T(1,128)S(1)}, f32[256,640]{1,0:T(8,128)S(1)}, bf16[256,640]{1,0:T(8,128)(2,1)S(1)}) custom-call(s32[8]{0:T(128)S(1)} %broadcast_xor_fusion.order, bf16[512,1024]{1,0:T(8,128)(2,1)} %z.5, f32[1,1024]{1,0:T(1,128)S(1)} %get-tuple-element.88.mean), custom_call_target="tpu_custom_call" | custom-call | tf_op jit(solution)/shard_map/pallas_call | solution.py:17
  12.7 1.9 %collective-permute-start.3 = (bf16[256,640]{1,0:T(8,128)(2,1)S(1)}, bf16[256,640]{1,0:T(8,128)(2,1)S(1)}, u32[]{:S(2)}, u32[]{:S(2)}) collective-permute-start(bf16[256,640]{1,0:T(8,128)(2,1)S(1)} %get-tuple-element.48), channel_id=1, source_target_pairs={{0,1},{1,0},{2,3},{3,2},{4,5},{5,4},{6,7},{7,6},{8,9},{9,8},{10,11... | collective-permute-start | bytes 983048 | tf_op jit(solution)/shard_map/ppermute | solution.py:269
  16.0 1.3 %collective-permute-start.4 = (bf16[64,640]{1,0:T(8,128)(2,1)S(1)}, bf16[64,640]{1,0:T(8,128)(2,1)S(1)}, u32[]{:S(2)}, u32[]{:S(2)}) collective-permute-start(bf16[64,640]{1,0:T(8,128)(2,1)S(1)} %get-tuple-element.50), channel_id=1, source_target_pairs={{0,2},{1,3},{2,0},{3,1},{4,6},{5,7},{6,4},{7,5},{8,10},{9,11},{10,... | collective-permute-start | bytes 245768 | tf_op jit(solution)/shard_map/ppermute | solution.py:269
  20.9 1.7 %collective-permute-done.6.c = bf16[64,640]{1,0:T(8,128)(2,1)S(1)} collective-permute-done((bf16[64,640]{1,0:T(8,128)(2,1)S(1)}, bf16[64,640]{1,0:T(8,128)(2,1)S(1)}, u32[]{:S(2)}, u32[]{:S(2)}) %collective-permute-start.6) | collective-permute-done | bytes 81952 | tf_op jit(solution)/shard_map/ppermute | solution.py:269
  25.5 1.6 %collective-permute-done.9 = bf16[64,640]{1,0:T(8,128)(2,1)S(1)} collective-permute-done((bf16[64,640]{1,0:T(8,128)(2,1)S(1)}, bf16[64,640]{1,0:T(8,128)(2,1)S(1)}, u32[]{:S(2)}, u32[]{:S(2)}) %collective-permute-start.9) | collective-permute-done | bytes 81952 | tf_op jit(solution)/shard_map/ppermute | solution.py:269
  28.4 3.5 %collective-permute-done.11.opposite_in = bf16[512,1024]{1,0:T(8,128)(2,1)} collective-permute-done((bf16[512,1024]{1,0:T(8,128)(2,1)}, bf16[512,1024]{1,0:T(8,128)(2,1)}, u32[]{:S(2)}, u32[]{:S(2)}) %collective-permute-start.11) | collective-permute-done | bytes 1048608 | tf_op jit(solution)/shard_map/ppermute | solution.py:319
  31.9 1.6 %collective-permute-start.20 = (bf16[512,1024]{1,0:T(8,128)(2,1)}, bf16[512,1024]{1,0:T(8,128)(2,1)}, u32[]{:S(2)}, u32[]{:S(2)}) collective-permute-start(bf16[512,1024]{1,0:T(8,128)(2,1)} %z.5), channel_id=1, source_target_pairs={{0,24},{24,0},{1,25},{25,1},{2,26},{26,2},{3,27},{27,3},{4,28},{28... | collective-permute-start | bytes 3145736 | tf_op jit(solution)/shard_map/ppermute | solution.py:334
  33.5 2.2 %shard_map.41 = (bf16[512,1024]{1,0:T(8,128)(2,1)S(1)}, f32[1,1024]{1,0:T(1,128)S(1)}, bf16[512,1024]{1,0:T(8,128)(2,1)S(1)}, f32[1,1024]{1,0:T(1,128)S(1)}, f32...) custom-call(s32[8]{0:T(128)S(1)} %broadcast_xor_fusion.order, s32[1]{0:T(128)} %bitcast.middle, ...), custom_call_target="tpu_custom_call" | custom-call | tf_op jit(solution)/shard_map/pallas_call | solution.py:17
  35.7 25.0 %collective-permute-start.12 = (bf16[256,512]{1,0:T(8,128)(2,1)S(1)}, bf16[256,512]{1,0:T(8,128)(2,1)S(1)}, u32[]{:S(2)}, u32[]{:S(2)}) collective-permute-start(bf16[256,512]{1,0:T(8,128)(2,1)S(1)} %get-tuple-element.56), channel_id=1, source_target_pairs={{0,1},{1,0},{2,3},{3,2},{4,5},{5,4},{6,7},{7,6},{8,9},{9,8},{10,11... | collective-permute-start | bytes 786440 | tf_op jit(solution)/shard_map/ppermute | solution.py:269
  62.2 2.3 %collective-permute-start.14 = (bf16[64,512]{1,0:T(8,128)(2,1)S(1)}, bf16[64,512]{1,0:T(8,128)(2,1)S(1)}, u32[]{:S(2)}, u32[]{:S(2)}) collective-permute-start(bf16[64,512]{1,0:T(8,128)(2,1)S(1)} %get-tuple-element.59), channel_id=1, source_target_pairs={{0,4},{1,5},{2,6},{3,7},{4,0},{5,1},{6,2},{7,3},{8,12},{9,13},{10,... | collective-permute-start | bytes 196616 | tf_op jit(solution)/shard_map/ppermute | solution.py:269
  66.2 2.2 %collective-permute-done.15.c = bf16[64,512]{1,0:T(8,128)(2,1)S(1)} collective-permute-done((bf16[64,512]{1,0:T(8,128)(2,1)S(1)}, bf16[64,512]{1,0:T(8,128)(2,1)S(1)}, u32[]{:S(2)}, u32[]{:S(2)}) %collective-permute-start.15) | collective-permute-done | bytes 65568 | tf_op jit(solution)/shard_map/ppermute | solution.py:269
  69.2 2.1 %collective-permute-start.18 = (bf16[64,512]{1,0:T(8,128)(2,1)S(1)}, bf16[64,512]{1,0:T(8,128)(2,1)S(1)}, u32[]{:S(2)}, u32[]{:S(2)}) collective-permute-start(bf16[64,512]{1,0:T(8,128)(2,1)S(1)} %shard_map.43.refs_0_.first), channel_id=1, source_target_pairs={{0,6},{1,7},{2,4},{3,5},{4,2},{5,3},{6,0},{7,1},{8,14},{9,15},{10,... | collective-permute-start | bytes 196616 | tf_op jit(solution)/shard_map/ppermute | solution.py:269
  71.2 1.3 %shard_map.44 = (f32[256,1024]{1,0:T(8,128)S(1)}, bf16[256,1024]{1,0:T(8,128)(2,1)S(1)}) custom-call(s32[1]{0:T(128)} %bitcast.middle, bf16[512,1024]{1,0:T(8,128)(2,1)S(1)} %get-tuple-element.71.turned, bf16[512,1024]{1,0:T(8,128)(2,1)S(1)} %get-tuple-element.62.beside, bf16[512,1024]{1,0:T(8,128)(2,1)S(1)} %get-tuple-element.63.opposite.swapped), custom_call_target="tpu_custom_call" | custom-call | tf_op jit(solution)/shard_map/pallas_call | solution.py:17
  73.2 3.8 %collective-permute-start.19 = (bf16[256,512]{1,0:T(8,128)(2,1)S(1)}, bf16[256,512]{1,0:T(8,128)(2,1)S(1)}, u32[]{:S(2)}, u32[]{:S(2)}) collective-permute-start(bf16[256,512]{1,0:T(8,128)(2,1)S(1)} %shard_map.45.near), channel_id=1, source_target_pairs={{0,1},{1,0},{2,3},{3,2},{4,5},{5,4},{6,7},{7,6},{8,9},{9,8},{10,11... | collective-permute-start | bytes 786440 | tf_op jit(solution)/shard_map/ppermute | solution.py:269
  78.1 1.8 %shard_map.46 = (bf16[512,1024]{1,0:T(8,128)(2,1)S(1)}, bf16[512,1024]{1,0:T(8,128)(2,1)S(1)}) custom-call(s32[8]{0:T(128)S(1)} %broadcast_xor_fusion.order, s32[1]{0:T(128)} %bitcast.middle, bf16[256,512]{1,0:T(8,128)(2,1)S(1)} %shard_map.45.near, bf16[256,512]{1,0:T(8,128)(2,1)S(1)} %collective-permute-done.19.far, ...), custom_call_target="tpu_custom_call" | custom-call | tf_op jit(solution)/shard_map/pallas_call | solution.py:17
  79.9 1.4 %collective-permute-start.29 = (bf16[512,1024]{1,0:T(8,128)(2,1)S(1)}, bf16[512,1024]{1,0:T(8,128)(2,1)S(1)}, u32[]{:S(2)}, u32[]{:S(2)}) collective-permute-start(bf16[512,1024]{1,0:T(8,128)(2,1)S(1)} %get-tuple-element.69), channel_id=1, source_target_pairs={{8,0},{16,24},{9,1},{17,25},{10,2},{18,26},{11,3},{19,27},{12,4},{... | collective-permute-start | bytes 3145736 | tf_op jit(solution)/shard_map/ppermute | solution.py:350
  81.3 3.2 %collective-permute-start.30 = (bf16[512,1024]{1,0:T(8,128)(2,1)S(1)}, bf16[512,1024]{1,0:T(8,128)(2,1)S(1)}, u32[]{:S(2)}, u32[]{:S(2)}) collective-permute-start(bf16[512,1024]{1,0:T(8,128)(2,1)S(1)} %get-tuple-element.84), channel_id=1, source_target_pairs={{8,16},{16,8},{9,17},{17,9},{10,18},{18,10},{11,19},{19,11},{12,20... | collective-permute-start | bytes 3145736 | tf_op jit(solution)/shard_map/ppermute | solution.py:350
  84.6 1.3 %shard_map.47 = (bf16[512,1024]{1,0:T(8,128)(2,1)S(1)}, f32[1,1024]{1,0:T(1,128)S(1)}, f32[256,512]{1,0:T(8,128)S(1)}, bf16[256,1024]{1,0:T(8,128)(2,1)S(1)}) custom-call(s32[1]{0:T(128)} %bitcast.middle, bf16[512,1024]{1,0:T(8,128)(2,1)S(1)} %get-tuple-element.71.turned, bf16[256,1024]{1,0:T(8,128)(2,1)S(1)} %get-tuple-element.65.sent_early, ...), custom_call_target="tpu_custom_call" | custom-call | tf_op jit(solution)/shard_map/pallas_call | solution.py:17
  86.6 1.5 %collective-permute-done.21.got = bf16[256,1024]{1,0:T(8,128)(2,1)S(1)} collective-permute-done((bf16[256,1024]{1,0:T(8,128)(2,1)S(1)}, bf16[256,1024]{1,0:T(8,128)(2,1)S(1)}, u32[]{:S(2)}, u32[]{:S(2)}) %collective-permute-start.21) | collective-permute-done | bytes 524320 | tf_op jit(solution)/shard_map/ppermute | solution.py:269
  88.2 1.3 %collective-permute-start.22 = (bf16[64,1024]{1,0:T(8,128)(2,1)S(1)}, bf16[64,1024]{1,0:T(8,128)(2,1)S(1)}, u32[]{:S(2)}, u32[]{:S(2)}) collective-permute-start(bf16[64,1024]{1,0:T(8,128)(2,1)S(1)} %get-tuple-element.76), channel_id=1, source_target_pairs={{0,2},{1,3},{2,0},{3,1},{4,6},{5,7},{6,4},{7,5},{8,10},{9,11},{10,... | collective-permute-start | bytes 393224 | tf_op jit(solution)/shard_map/ppermute | solution.py:269
  90.9 2.6 %shard_map.50.held = f32[512,1024]{1,0:T(8,128)S(1)} custom-call(s32[8]{0:T(128)S(1)} %broadcast_xor_fusion.order, s32[1]{0:T(128)} %bitcast.middle, bf16[256,640]{1,0:T(8,128)(2,1)S(1)} %pad_maximum_fusion.near, bf16[256,640]{1,0:T(8,128)(2,1)S(1)} %collective-permute-done.25.far, bf16[512,1024]{1,0:T(8,128)(2,1)S(1)} %get-tuple-element.79.own, ...), custom_call_target="tpu_custom_call" | custom-call | tf_op jit(solution)/shard_map/pallas_call | solution.py:17
  93.9 2.7 %collective-permute-done.24.c = bf16[64,1024]{1,0:T(8,128)(2,1)S(1)} collective-permute-done((bf16[64,1024]{1,0:T(8,128)(2,1)S(1)}, bf16[64,1024]{1,0:T(8,128)(2,1)S(1)}, u32[]{:S(2)}, u32[]{:S(2)}) %collective-permute-start.24) | collective-permute-done | bytes 131104 | tf_op jit(solution)/shard_map/ppermute | solution.py:269
  96.6 1.5 %collective-permute-start.26 = (bf16[64,1024]{1,0:T(8,128)(2,1)S(1)}, bf16[64,1024]{1,0:T(8,128)(2,1)S(1)}, u32[]{:S(2)}, u32[]{:S(2)}) collective-permute-start(bf16[64,1024]{1,0:T(8,128)(2,1)S(1)} %shard_map.49.refs_0_), channel_id=1, source_target_pairs={{0,2},{1,3},{2,0},{3,1},{4,6},{5,7},{6,4},{7,5},{8,10},{9,11},{10,... | collective-permute-start | bytes 393224 | tf_op jit(solution)/shard_map/ppermute | solution.py:269
  99.3 1.5 %collective-permute-done.26.refs_1_ = bf16[64,1024]{1,0:T(8,128)(2,1)S(1)} collective-permute-done((bf16[64,1024]{1,0:T(8,128)(2,1)S(1)}, bf16[64,1024]{1,0:T(8,128)(2,1)S(1)}, u32[]{:S(2)}, u32[]{:S(2)}) %collective-permute-start.26) | collective-permute-done | bytes 131104 | tf_op jit(solution)/shard_map/ppermute | solution.py:269
  100.8 2.0 %collective-permute-done.27.refs_2_ = bf16[64,1024]{1,0:T(8,128)(2,1)S(1)} collective-permute-done((bf16[64,1024]{1,0:T(8,128)(2,1)S(1)}, bf16[64,1024]{1,0:T(8,128)(2,1)S(1)}, u32[]{:S(2)}, u32[]{:S(2)}) %collective-permute-start.27) | collective-permute-done | bytes 131104 | tf_op jit(solution)/shard_map/ppermute | solution.py:269
  104.1 3.6 %collective-permute-done.30.over = bf16[512,1024]{1,0:T(8,128)(2,1)S(1)} collective-permute-done((bf16[512,1024]{1,0:T(8,128)(2,1)S(1)}, bf16[512,1024]{1,0:T(8,128)(2,1)S(1)}, u32[]{:S(2)}, u32[]{:S(2)}) %collective-permute-start.30) | collective-permute-done | bytes 1048608 | tf_op jit(solution)/shard_map/ppermute | solution.py:350
  108.9 1.5 %collective-permute-done.31.far = bf16[256,1024]{1,0:T(8,128)(2,1)S(1)} collective-permute-done((bf16[256,1024]{1,0:T(8,128)(2,1)S(1)}, bf16[256,1024]{1,0:T(8,128)(2,1)S(1)}, u32[]{:S(2)}, u32[]{:S(2)}) %collective-permute-start.31) | collective-permute-done | bytes 524320 | tf_op jit(solution)/shard_map/ppermute | solution.py:269
  110.5 3.3 %shard_map.52 = f32[512,1024]{1,0:T(8,128)} custom-call(s32[8]{0:T(128)S(1)} %broadcast_xor_fusion.order, s32[1]{0:T(128)} %bitcast.middle, bf16[256,1024]{1,0:T(8,128)(2,1)S(1)} %shard_map.51.near, bf16[256,1024]{1,0:T(8,128)(2,1)S(1)} %collective-permute-done.31.far, bf16[512,1024]{1,0:T(8,128)(2,1)S(1)} %get-tuple-element.62.beside, ...), custom_call_target="tpu_custom_call" | custom-call | tf_op jit(solution)/shard_map/pallas_call | solution.py:17
  (53 shorter events, 22.1 us)
Async XLA Ops:
  1.8 8.5 %collective-permute-start.2 = (f32[2,1024]{1,0:T(2,128)S(1)}, f32[2,1024]{1,0:T(2,128)S(1)}, u32[]{:S(2)}, u32[]{:S(2)}) collective-permute-start(f32[2,1024]{1,0:T(2,128)S(1)} %shard_map.37), channel_id=1, source_target_pairs={{0,24},{8,0},{16,8},{24,16},{1,25},{9,1},{17,9},{25,17},{2,26},{10... | collective-permute-start | bytes 24584 | tf_op jit(solution)/shard_map/ppermute | solution.py:315
  1.9 8.4 %collective-permute-start.1 = (f32[2,1024]{1,0:T(2,128)S(1)}, f32[2,1024]{1,0:T(2,128)S(1)}, u32[]{:S(2)}, u32[]{:S(2)}) collective-permute-start(f32[2,1024]{1,0:T(2,128)S(1)} %shard_map.37), channel_id=1, source_target_pairs={{0,16},{8,24},{16,0},{24,8},{1,17},{9,25},{17,1},{25,9},{2,18},{10... | collective-permute-start | bytes 24584 | tf_op jit(solution)/shard_map/ppermute | solution.py:315
  4.3 6.0 %collective-permute-start = (f32[2,1024]{1,0:T(2,128)S(1)}, f32[2,1024]{1,0:T(2,128)S(1)}, u32[]{:S(2)}, u32[]{:S(2)}) collective-permute-start(f32[2,1024]{1,0:T(2,128)S(1)} %shard_map.37), channel_id=1, source_target_pairs={{0,8},{8,16},{16,24},{24,0},{1,9},{9,17},{17,25},{25,1},{2,10},{10... | collective-permute-start | bytes 24584 | tf_op jit(solution)/shard_map/ppermute | solution.py:315
  6.5 27.0 %collective-permute-start.10 = (bf16[512,1024]{1,0:T(8,128)(2,1)}, bf16[512,1024]{1,0:T(8,128)(2,1)S(1)}, u32[]{:S(2)}, u32[]{:S(2)}) collective-permute-start(bf16[512,1024]{1,0:T(8,128)(2,1)} %z.5), channel_id=1, source_target_pairs={{0,8},{8,0},{16,24},{24,16},{1,9},{9,1},{17,25},{25,17},{2,10},{10... | collective-permute-start | bytes 3145736 | tf_op jit(solution)/shard_map/ppermute | solution.py:318
  6.5 25.3 %collective-permute-start.11 = (bf16[512,1024]{1,0:T(8,128)(2,1)}, bf16[512,1024]{1,0:T(8,128)(2,1)}, u32[]{:S(2)}, u32[]{:S(2)}) collective-permute-start(bf16[512,1024]{1,0:T(8,128)(2,1)} %z.5), channel_id=1, source_target_pairs={{8,16},{16,8},{9,17},{17,9},{10,18},{18,10},{11,19},{19,11},{12,20... | collective-permute-start | bytes 3145736 | tf_op jit(solution)/shard_map/ppermute | solution.py:319
  12.7 3.1 %collective-permute-start.3 = (bf16[256,640]{1,0:T(8,128)(2,1)S(1)}, bf16[256,640]{1,0:T(8,128)(2,1)S(1)}, u32[]{:S(2)}, u32[]{:S(2)}) collective-permute-start(bf16[256,640]{1,0:T(8,128)(2,1)S(1)} %get-tuple-element.48), channel_id=1, source_target_pairs={{0,1},{1,0},{2,3},{3,2},{4,5},{5,4},{6,7},{7,6},{8,9},{9,8},{10,11... | collective-permute-start | bytes 983048 | tf_op jit(solution)/shard_map/ppermute | solution.py:269
  16.0 3.8 %collective-permute-start.4 = (bf16[64,640]{1,0:T(8,128)(2,1)S(1)}, bf16[64,640]{1,0:T(8,128)(2,1)S(1)}, u32[]{:S(2)}, u32[]{:S(2)}) collective-permute-start(bf16[64,640]{1,0:T(8,128)(2,1)S(1)} %get-tuple-element.50), channel_id=1, source_target_pairs={{0,2},{1,3},{2,0},{3,1},{4,6},{5,7},{6,4},{7,5},{8,10},{9,11},{10,... | collective-permute-start | bytes 245768 | tf_op jit(solution)/shard_map/ppermute | solution.py:269
  17.3 3.7 %collective-permute-start.5 = (bf16[64,640]{1,0:T(8,128)(2,1)S(1)}, bf16[64,640]{1,0:T(8,128)(2,1)S(1)}, u32[]{:S(2)}, u32[]{:S(2)}) collective-permute-start(bf16[64,640]{1,0:T(8,128)(2,1)S(1)} %get-tuple-element.51), channel_id=1, source_target_pairs={{0,4},{1,5},{2,6},{3,7},{4,0},{5,1},{6,2},{7,3},{8,12},{9,13},{10,... | collective-permute-start | bytes 245768 | tf_op jit(solution)/shard_map/ppermute | solution.py:269
  18.5 4.2 %collective-permute-start.6 = (bf16[64,640]{1,0:T(8,128)(2,1)S(1)}, bf16[64,640]{1,0:T(8,128)(2,1)S(1)}, u32[]{:S(2)}, u32[]{:S(2)}) collective-permute-start(bf16[64,640]{1,0:T(8,128)(2,1)S(1)} %get-tuple-element.52), channel_id=1, source_target_pairs={{0,6},{1,7},{2,4},{3,5},{4,2},{5,3},{6,0},{7,1},{8,14},{9,15},{10,... | collective-permute-start | bytes 245768 | tf_op jit(solution)/shard_map/ppermute | solution.py:269
  22.8 4.4 %collective-permute-start.9 = (bf16[64,640]{1,0:T(8,128)(2,1)S(1)}, bf16[64,640]{1,0:T(8,128)(2,1)S(1)}, u32[]{:S(2)}, u32[]{:S(2)}) collective-permute-start(bf16[64,640]{1,0:T(8,128)(2,1)S(1)} %shard_map.40), channel_id=1, source_target_pairs={{0,6},{1,7},{2,4},{3,5},{4,2},{5,3},{6,0},{7,1},{8,14},{9,15},{10,... | collective-permute-start | bytes 245768 | tf_op jit(solution)/shard_map/ppermute | solution.py:269
  23.4 4.6 %collective-permute-start.8 = (bf16[64,640]{1,0:T(8,128)(2,1)S(1)}, bf16[64,640]{1,0:T(8,128)(2,1)S(1)}, u32[]{:S(2)}, u32[]{:S(2)}) collective-permute-start(bf16[64,640]{1,0:T(8,128)(2,1)S(1)} %shard_map.40), channel_id=1, source_target_pairs={{0,4},{1,5},{2,6},{3,7},{4,0},{5,1},{6,2},{7,3},{8,12},{9,13},{10,... | collective-permute-start | bytes 245768 | tf_op jit(solution)/shard_map/ppermute | solution.py:269
  24.6 3.7 %collective-permute-start.7 = (bf16[64,640]{1,0:T(8,128)(2,1)S(1)}, bf16[64,640]{1,0:T(8,128)(2,1)S(1)}, u32[]{:S(2)}, u32[]{:S(2)}) collective-permute-start(bf16[64,640]{1,0:T(8,128)(2,1)S(1)} %shard_map.40), channel_id=1, source_target_pairs={{0,2},{1,3},{2,0},{3,1},{4,6},{5,7},{6,4},{7,5},{8,10},{9,11},{10,... | collective-permute-start | bytes 245768 | tf_op jit(solution)/shard_map/ppermute | solution.py:269
  31.9 49.4 %collective-permute-start.20 = (bf16[512,1024]{1,0:T(8,128)(2,1)}, bf16[512,1024]{1,0:T(8,128)(2,1)}, u32[]{:S(2)}, u32[]{:S(2)}) collective-permute-start(bf16[512,1024]{1,0:T(8,128)(2,1)} %z.5), channel_id=1, source_target_pairs={{0,24},{24,0},{1,25},{25,1},{2,26},{26,2},{3,27},{27,3},{4,28},{28... | collective-permute-start | bytes 3145736 | tf_op jit(solution)/shard_map/ppermute | solution.py:334
  35.7 26.1 %collective-permute-start.12 = (bf16[256,512]{1,0:T(8,128)(2,1)S(1)}, bf16[256,512]{1,0:T(8,128)(2,1)S(1)}, u32[]{:S(2)}, u32[]{:S(2)}) collective-permute-start(bf16[256,512]{1,0:T(8,128)(2,1)S(1)} %get-tuple-element.56), channel_id=1, source_target_pairs={{0,1},{1,0},{2,3},{3,2},{4,5},{5,4},{6,7},{7,6},{8,9},{9,8},{10,11... | collective-permute-start | bytes 786440 | tf_op jit(solution)/shard_map/ppermute | solution.py:269
  61.9 3.2 %collective-permute-start.13 = (bf16[64,512]{1,0:T(8,128)(2,1)S(1)}, bf16[64,512]{1,0:T(8,128)(2,1)S(1)}, u32[]{:S(2)}, u32[]{:S(2)}) collective-permute-start(bf16[64,512]{1,0:T(8,128)(2,1)S(1)} %get-tuple-element.58), channel_id=1, source_target_pairs={{0,2},{1,3},{2,0},{3,1},{4,6},{5,7},{6,4},{7,5},{8,10},{9,11},{10,... | collective-permute-start | bytes 196616 | tf_op jit(solution)/shard_map/ppermute | solution.py:269
  62.2 4.1 %collective-permute-start.14 = (bf16[64,512]{1,0:T(8,128)(2,1)S(1)}, bf16[64,512]{1,0:T(8,128)(2,1)S(1)}, u32[]{:S(2)}, u32[]{:S(2)}) collective-permute-start(bf16[64,512]{1,0:T(8,128)(2,1)S(1)} %get-tuple-element.59), channel_id=1, source_target_pairs={{0,4},{1,5},{2,6},{3,7},{4,0},{5,1},{6,2},{7,3},{8,12},{9,13},{10,... | collective-permute-start | bytes 196616 | tf_op jit(solution)/shard_map/ppermute | solution.py:269
  64.5 4.0 %collective-permute-start.15 = (bf16[64,512]{1,0:T(8,128)(2,1)S(1)}, bf16[64,512]{1,0:T(8,128)(2,1)S(1)}, u32[]{:S(2)}, u32[]{:S(2)}) collective-permute-start(bf16[64,512]{1,0:T(8,128)(2,1)S(1)} %get-tuple-element.60), channel_id=1, source_target_pairs={{0,6},{1,7},{2,4},{3,5},{4,2},{5,3},{6,0},{7,1},{8,14},{9,15},{10,... | collective-permute-start | bytes 196616 | tf_op jit(solution)/shard_map/ppermute | solution.py:269
  68.5 4.0 %collective-permute-start.16 = (bf16[64,512]{1,0:T(8,128)(2,1)S(1)}, bf16[64,512]{1,0:T(8,128)(2,1)S(1)}, u32[]{:S(2)}, u32[]{:S(2)}) collective-permute-start(bf16[64,512]{1,0:T(8,128)(2,1)S(1)} %shard_map.43.refs_0_.first), channel_id=1, source_target_pairs={{0,2},{1,3},{2,0},{3,1},{4,6},{5,7},{6,4},{7,5},{8,10},{9,11},{10,... | collective-permute-start | bytes 196616 | tf_op jit(solution)/shard_map/ppermute | solution.py:269
  68.9 3.6 %collective-permute-start.17 = (bf16[64,512]{1,0:T(8,128)(2,1)S(1)}, bf16[64,512]{1,0:T(8,128)(2,1)S(1)}, u32[]{:S(2)}, u32[]{:S(2)}) collective-permute-start(bf16[64,512]{1,0:T(8,128)(2,1)S(1)} %shard_map.43.refs_0_.first), channel_id=1, source_target_pairs={{0,4},{1,5},{2,6},{3,7},{4,0},{5,1},{6,2},{7,3},{8,12},{9,13},{10,... | collective-permute-start | bytes 196616 | tf_op jit(solution)/shard_map/ppermute | solution.py:269
  69.2 4.0 %collective-permute-start.18 = (bf16[64,512]{1,0:T(8,128)(2,1)S(1)}, bf16[64,512]{1,0:T(8,128)(2,1)S(1)}, u32[]{:S(2)}, u32[]{:S(2)}) collective-permute-start(bf16[64,512]{1,0:T(8,128)(2,1)S(1)} %shard_map.43.refs_0_.first), channel_id=1, source_target_pairs={{0,6},{1,7},{2,4},{3,5},{4,2},{5,3},{6,0},{7,1},{8,14},{9,15},{10,... | collective-permute-start | bytes 196616 | tf_op jit(solution)/shard_map/ppermute | solution.py:269
  73.2 4.9 %collective-permute-start.19 = (bf16[256,512]{1,0:T(8,128)(2,1)S(1)}, bf16[256,512]{1,0:T(8,128)(2,1)S(1)}, u32[]{:S(2)}, u32[]{:S(2)}) collective-permute-start(bf16[256,512]{1,0:T(8,128)(2,1)S(1)} %shard_map.45.near), channel_id=1, source_target_pairs={{0,1},{1,0},{2,3},{3,2},{4,5},{5,4},{6,7},{7,6},{8,9},{9,8},{10,11... | collective-permute-start | bytes 786440 | tf_op jit(solution)/shard_map/ppermute | solution.py:269
  79.9 24.2 %collective-permute-start.29 = (bf16[512,1024]{1,0:T(8,128)(2,1)S(1)}, bf16[512,1024]{1,0:T(8,128)(2,1)S(1)}, u32[]{:S(2)}, u32[]{:S(2)}) collective-permute-start(bf16[512,1024]{1,0:T(8,128)(2,1)S(1)} %get-tuple-element.69), channel_id=1, source_target_pairs={{8,0},{16,24},{9,1},{17,25},{10,2},{18,26},{11,3},{19,27},{12,4},{... | collective-permute-start | bytes 3145736 | tf_op jit(solution)/shard_map/ppermute | solution.py:350
  81.3 26.4 %collective-permute-start.30 = (bf16[512,1024]{1,0:T(8,128)(2,1)S(1)}, bf16[512,1024]{1,0:T(8,128)(2,1)S(1)}, u32[]{:S(2)}, u32[]{:S(2)}) collective-permute-start(bf16[512,1024]{1,0:T(8,128)(2,1)S(1)} %get-tuple-element.84), channel_id=1, source_target_pairs={{8,16},{16,8},{9,17},{17,9},{10,18},{18,10},{11,19},{19,11},{12,20... | collective-permute-start | bytes 3145736 | tf_op jit(solution)/shard_map/ppermute | solution.py:350
  85.8 2.3 %collective-permute-start.21 = (bf16[256,1024]{1,0:T(8,128)(2,1)S(1)}, bf16[256,1024]{1,0:T(8,128)(2,1)S(1)}, u32[]{:S(2)}, u32[]{:S(2)}) collective-permute-start(bf16[256,1024]{1,0:T(8,128)(2,1)S(1)} %get-tuple-element.74), channel_id=1, source_target_pairs={{0,1},{1,0},{2,3},{3,2},{4,5},{5,4},{6,7},{7,6},{8,9},{9,8},{10,11... | collective-permute-start | bytes 1572872 | tf_op jit(solution)/shard_map/ppermute | solution.py:269
  86.6 4.2 %collective-permute-start.25 = (bf16[256,640]{1,0:T(8,128)(2,1)S(1)}, bf16[256,640]{1,0:T(8,128)(2,1)S(1)}, u32[]{:S(2)}, u32[]{:S(2)}) collective-permute-start(bf16[256,640]{1,0:T(8,128)(2,1)S(1)} %pad_maximum_fusion.near), channel_id=1, source_target_pairs={{0,1},{1,0},{2,3},{3,2},{4,5},{5,4},{6,7},{7,6},{8,9},{9,8},{10,11... | collective-permute-start | bytes 983048 | tf_op jit(solution)/shard_map/ppermute | solution.py:269
  88.2 5.3 %collective-permute-start.22 = (bf16[64,1024]{1,0:T(8,128)(2,1)S(1)}, bf16[64,1024]{1,0:T(8,128)(2,1)S(1)}, u32[]{:S(2)}, u32[]{:S(2)}) collective-permute-start(bf16[64,1024]{1,0:T(8,128)(2,1)S(1)} %get-tuple-element.76), channel_id=1, source_target_pairs={{0,2},{1,3},{2,0},{3,1},{4,6},{5,7},{6,4},{7,5},{8,10},{9,11},{10,... | collective-permute-start | bytes 393224 | tf_op jit(solution)/shard_map/ppermute | solution.py:269
  89.5 4.4 %collective-permute-start.23 = (bf16[64,1024]{1,0:T(8,128)(2,1)S(1)}, bf16[64,1024]{1,0:T(8,128)(2,1)S(1)}, u32[]{:S(2)}, u32[]{:S(2)}) collective-permute-start(bf16[64,1024]{1,0:T(8,128)(2,1)S(1)} %get-tuple-element.77), channel_id=1, source_target_pairs={{0,4},{1,5},{2,6},{3,7},{4,0},{5,1},{6,2},{7,3},{8,12},{9,13},{10,... | collective-permute-start | bytes 393224 | tf_op jit(solution)/shard_map/ppermute | solution.py:269
  90.7 5.8 %collective-permute-start.24 = (bf16[64,1024]{1,0:T(8,128)(2,1)S(1)}, bf16[64,1024]{1,0:T(8,128)(2,1)S(1)}, u32[]{:S(2)}, u32[]{:S(2)}) collective-permute-start(bf16[64,1024]{1,0:T(8,128)(2,1)S(1)} %get-tuple-element.78), channel_id=1, source_target_pairs={{0,6},{1,7},{2,4},{3,5},{4,2},{5,3},{6,0},{7,1},{8,14},{9,15},{10,... | collective-permute-start | bytes 393224 | tf_op jit(solution)/shard_map/ppermute | solution.py:269
  96.6 4.2 %collective-permute-start.26 = (bf16[64,1024]{1,0:T(8,128)(2,1)S(1)}, bf16[64,1024]{1,0:T(8,128)(2,1)S(1)}, u32[]{:S(2)}, u32[]{:S(2)}) collective-permute-start(bf16[64,1024]{1,0:T(8,128)(2,1)S(1)} %shard_map.49.refs_0_), channel_id=1, source_target_pairs={{0,2},{1,3},{2,0},{3,1},{4,6},{5,7},{6,4},{7,5},{8,10},{9,11},{10,... | collective-permute-start | bytes 393224 | tf_op jit(solution)/shard_map/ppermute | solution.py:269
  98.1 4.8 %collective-permute-start.27 = (bf16[64,1024]{1,0:T(8,128)(2,1)S(1)}, bf16[64,1024]{1,0:T(8,128)(2,1)S(1)}, u32[]{:S(2)}, u32[]{:S(2)}) collective-permute-start(bf16[64,1024]{1,0:T(8,128)(2,1)S(1)} %shard_map.49.refs_0_), channel_id=1, source_target_pairs={{0,4},{1,5},{2,6},{3,7},{4,0},{5,1},{6,2},{7,3},{8,12},{9,13},{10,... | collective-permute-start | bytes 393224 | tf_op jit(solution)/shard_map/ppermute | solution.py:269
  98.4 5.7 %collective-permute-start.28 = (bf16[64,1024]{1,0:T(8,128)(2,1)S(1)}, bf16[64,1024]{1,0:T(8,128)(2,1)S(1)}, u32[]{:S(2)}, u32[]{:S(2)}) collective-permute-start(bf16[64,1024]{1,0:T(8,128)(2,1)S(1)} %shard_map.49.refs_0_), channel_id=1, source_target_pairs={{0,6},{1,7},{2,4},{3,5},{4,2},{5,3},{6,0},{7,1},{8,14},{9,15},{10,... | collective-permute-start | bytes 393224 | tf_op jit(solution)/shard_map/ppermute | solution.py:269
  107.7 2.7 %collective-permute-start.31 = (bf16[256,1024]{1,0:T(8,128)(2,1)S(1)}, bf16[256,1024]{1,0:T(8,128)(2,1)S(1)}, u32[]{:S(2)}, u32[]{:S(2)}) collective-permute-start(bf16[256,1024]{1,0:T(8,128)(2,1)S(1)} %shard_map.51.near), channel_id=1, source_target_pairs={{0,1},{1,0},{2,3},{3,2},{4,5},{5,4},{6,7},{7,6},{8,9},{9,8},{10,11... | collective-permute-start | bytes 1572872 | tf_op jit(solution)/shard_map/ppermute | solution.py:269
  (1 other events, 9.6 us)

commit v18 on v17

--- a/solution.py
+++ b/solution.py
@@ -331,7 +331,7 @@
     )(order, z_anchor, mean)
     near_own = scatter(*halve(kept, sent, rows), last=rows)
     near_own = jnp.concatenate([near_own] + [to_partner(near_own, 2 * k) for k in (1, 2, 3)])
-    end = lax.ppermute(after(z_anchor, swapped, near_own), "dp", [(0, 3), (3, 0)])
+    end = lax.ppermute(after(z_anchor, beside_in, swapped, near_own), "dp", [(0, 3), (3, 0)])
 
     beside, beside_square, swapped, swapped_square, kept, sent = kernel_call(
         first_kernel, [block, flat, block, flat, *summands(rows)],

time: 114 us -> 91.7 us (0.80)
  starting transfers between devices: 62.9 us -> 40.7 us
    ppermute x24, starting transfers between devices: 48.9 us -> 26.7 us  [to_partner(): return lax.ppermute(x, 'feat', [(i, i ^ step) for i in range(8)])]
    ppermute x1, waiting for transfers between devices: 3.53 us -> 1.89 us  [by_line(): swapped = lax.ppermute(ahead, 'dp', across)]
    ppermute x1, waiting for transfers between devices: 0.01 us -> 1.64 us  [by_line(): beside_in = lax.ppermute(ahead, 'dp', [(i, i ^ 1) for i in range(4)])]
  transfers between devices with their start and end apart: 32 -> 32, of which waited for: 22 -> 23; matrix products, arithmetic and copies ran while one was open for 1% -> 1% of each run, Pallas kernels for 11% -> 13%
where the time goes in v18:
time: 91.7 us; the launch traced here: 91.3 us
  starting transfers between devices  40.7 us (44%)
  waiting for transfers between devices  32.5 us (35%)
  Pallas kernels  17.2 us (19%)
    ppermute x24, starting transfers between devices, to_partner(): return lax.ppermute(x, 'feat', [(i, i ^ step) for i in range(8)])  26.7 us
    ppermute x24, waiting for transfers between devices, to_partner(): return lax.ppermute(x, 'feat', [(i, i ^ step) for i in range(8)])  25.6 us
    pallas_call x16, Pallas kernels, call(): pl.pallas_call(body, out_shape=[jax.ShapeDtypeStruct(s, t) for s, t in ou...  17.2 us
    ppermute x3, starting transfers between devices, by_line(): lax.ppermute(stats, 'dp', [(i, (i + k) % 4) for i in range(4)])  4.72 us
    ppermute x1, waiting for transfers between devices, by_line(): lax.ppermute(after(over, end), 'dp', across)  3.39 us
    ppermute x1, starting transfers between devices, by_line(): lax.ppermute(after(over, end), 'dp', across)  3.14 us
    ppermute x1, starting transfers between devices, by_line(): swapped = lax.ppermute(ahead, 'dp', across)  3.08 us
    ppermute x1, waiting for transfers between devices, by_line(): swapped = lax.ppermute(ahead, 'dp', across)  1.89 us
  transfers between devices with their start and end apart: 32, of which 23 were waited for; matrix products, arithmetic and copies ran while one was open for 1% of the time, Pallas kernels for 13%

profile of v18, /device:TPU:9, one launch (start us, length us, event | category | flops | bytes accessed | tf_op | source)
XLA Modules:
  0.0 91.3 jit_solution(14612090513041381190)
XLA Ops:
  0.0 1.8 %shard_map.37 = f32[2,1024]{1,0:T(2,128)S(1)} custom-call(bf16[512,1024]{1,0:T(8,128)(2,1)} %z.5), custom_call_target="tpu_custom_call" | custom-call | tf_op jit(solution)/shard_map/pallas_call | solution.py:17
  1.9 2.5 %collective-permute-start.1 = (f32[2,1024]{1,0:T(2,128)S(1)}, f32[2,1024]{1,0:T(2,128)S(1)}, u32[]{:S(2)}, u32[]{:S(2)}) collective-permute-start(f32[2,1024]{1,0:T(2,128)S(1)} %shard_map.37), channel_id=1, source_target_pairs={{0,16},{8,24},{16,0},{24,8},{1,17},{9,25},{17,1},{25,9},{2,18},{10... | collective-permute-start | bytes 24584 | tf_op jit(solution)/shard_map/ppermute | solution.py:315
  4.3 2.2 %collective-permute-start = (f32[2,1024]{1,0:T(2,128)S(1)}, f32[2,1024]{1,0:T(2,128)S(1)}, u32[]{:S(2)}, u32[]{:S(2)}) collective-permute-start(f32[2,1024]{1,0:T(2,128)S(1)} %shard_map.37), channel_id=1, source_target_pairs={{0,8},{8,16},{16,24},{24,0},{1,9},{9,17},{17,25},{25,1},{2,10},{10... | collective-permute-start | bytes 24584 | tf_op jit(solution)/shard_map/ppermute | solution.py:315
  6.5 3.1 %collective-permute-start.11 = (bf16[512,1024]{1,0:T(8,128)(2,1)}, bf16[512,1024]{1,0:T(8,128)(2,1)}, u32[]{:S(2)}, u32[]{:S(2)}) collective-permute-start(bf16[512,1024]{1,0:T(8,128)(2,1)} %z.5), channel_id=1, source_target_pairs={{8,16},{16,8},{9,17},{17,9},{10,18},{18,10},{11,19},{19,11},{12,20... | collective-permute-start | bytes 3145736 | tf_op jit(solution)/shard_map/ppermute | solution.py:319
  10.4 2.4 %shard_map.38 = (bf16[512,1024]{1,0:T(8,128)(2,1)S(1)}, bf16[512,1024]{1,0:T(8,128)(2,1)S(1)}, f32[1,1024]{1,0:T(1,128)S(1)}, f32[256,640]{1,0:T(8,128)S(1)}, bf16[256,640]{1,0:T(8,128)(2,1)S(1)}) custom-call(s32[8]{0:T(128)S(1)} %broadcast_xor_fusion.order, bf16[512,1024]{1,0:T(8,128)(2,1)} %z.5, f32[1,1024]{1,0:T(1,128)S(1)} %get-tuple-element.88.mean), custom_call_target="tpu_custom_call" | custom-call | tf_op jit(solution)/shard_map/pallas_call | solution.py:17
  12.7 1.9 %collective-permute-start.3 = (bf16[256,640]{1,0:T(8,128)(2,1)S(1)}, bf16[256,640]{1,0:T(8,128)(2,1)S(1)}, u32[]{:S(2)}, u32[]{:S(2)}) collective-permute-start(bf16[256,640]{1,0:T(8,128)(2,1)S(1)} %get-tuple-element.48), channel_id=1, source_target_pairs={{0,1},{1,0},{2,3},{3,2},{4,5},{5,4},{6,7},{7,6},{8,9},{9,8},{10,11... | collective-permute-start | bytes 983048 | tf_op jit(solution)/shard_map/ppermute | solution.py:269
  16.0 1.3 %collective-permute-start.4 = (bf16[64,640]{1,0:T(8,128)(2,1)S(1)}, bf16[64,640]{1,0:T(8,128)(2,1)S(1)}, u32[]{:S(2)}, u32[]{:S(2)}) collective-permute-start(bf16[64,640]{1,0:T(8,128)(2,1)S(1)} %get-tuple-element.50), channel_id=1, source_target_pairs={{0,2},{1,3},{2,0},{3,1},{4,6},{5,7},{6,4},{7,5},{8,10},{9,11},{10,... | collective-permute-start | bytes 245768 | tf_op jit(solution)/shard_map/ppermute | solution.py:269
  20.9 1.7 %collective-permute-done.6.c = bf16[64,640]{1,0:T(8,128)(2,1)S(1)} collective-permute-done((bf16[64,640]{1,0:T(8,128)(2,1)S(1)}, bf16[64,640]{1,0:T(8,128)(2,1)S(1)}, u32[]{:S(2)}, u32[]{:S(2)}) %collective-permute-start.6) | collective-permute-done | bytes 81952 | tf_op jit(solution)/shard_map/ppermute | solution.py:269
  25.5 1.6 %collective-permute-done.9 = bf16[64,640]{1,0:T(8,128)(2,1)S(1)} collective-permute-done((bf16[64,640]{1,0:T(8,128)(2,1)S(1)}, bf16[64,640]{1,0:T(8,128)(2,1)S(1)}, u32[]{:S(2)}, u32[]{:S(2)}) %collective-permute-start.9) | collective-permute-done | bytes 81952 | tf_op jit(solution)/shard_map/ppermute | solution.py:269
  28.4 1.6 %collective-permute-done.10.beside_in = bf16[512,1024]{1,0:T(8,128)(2,1)S(1)} collective-permute-done((bf16[512,1024]{1,0:T(8,128)(2,1)}, bf16[512,1024]{1,0:T(8,128)(2,1)S(1)}, u32[]{:S(2)}, u32[]{:S(2)}) %collective-permute-start.10) | collective-permute-done | bytes 1048608 | tf_op jit(solution)/shard_map/ppermute | solution.py:318
  30.0 1.9 %collective-permute-done.11.opposite_in = bf16[512,1024]{1,0:T(8,128)(2,1)} collective-permute-done((bf16[512,1024]{1,0:T(8,128)(2,1)}, bf16[512,1024]{1,0:T(8,128)(2,1)}, u32[]{:S(2)}, u32[]{:S(2)}) %collective-permute-start.11) | collective-permute-done | bytes 1048608 | tf_op jit(solution)/shard_map/ppermute | solution.py:319
  31.9 1.6 %collective-permute-start.20 = (bf16[512,1024]{1,0:T(8,128)(2,1)}, bf16[512,1024]{1,0:T(8,128)(2,1)}, u32[]{:S(2)}, u32[]{:S(2)}) collective-permute-start(bf16[512,1024]{1,0:T(8,128)(2,1)} %z.5), channel_id=1, source_target_pairs={{0,24},{24,0},{1,25},{25,1},{2,26},{26,2},{3,27},{27,3},{4,28},{28... | collective-permute-start | bytes 3145736 | tf_op jit(solution)/shard_map/ppermute | solution.py:334
  33.5 2.2 %shard_map.41 = (bf16[512,1024]{1,0:T(8,128)(2,1)S(1)}, f32[1,1024]{1,0:T(1,128)S(1)}, bf16[512,1024]{1,0:T(8,128)(2,1)S(1)}, f32[1,1024]{1,0:T(1,128)S(1)}, f32...) custom-call(s32[8]{0:T(128)S(1)} %broadcast_xor_fusion.order, s32[1]{0:T(128)} %bitcast.middle, ...), custom_call_target="tpu_custom_call" | custom-call | tf_op jit(solution)/shard_map/pallas_call | solution.py:17
  35.7 2.5 %collective-permute-start.12 = (bf16[256,512]{1,0:T(8,128)(2,1)S(1)}, bf16[256,512]{1,0:T(8,128)(2,1)S(1)}, u32[]{:S(2)}, u32[]{:S(2)}) collective-permute-start(bf16[256,512]{1,0:T(8,128)(2,1)S(1)} %get-tuple-element.56), channel_id=1, source_target_pairs={{0,1},{1,0},{2,3},{3,2},{4,5},{5,4},{6,7},{7,6},{8,9},{9,8},{10,11... | collective-permute-start | bytes 786440 | tf_op jit(solution)/shard_map/ppermute | solution.py:269
  39.5 1.3 %collective-permute-start.13 = (bf16[64,512]{1,0:T(8,128)(2,1)S(1)}, bf16[64,512]{1,0:T(8,128)(2,1)S(1)}, u32[]{:S(2)}, u32[]{:S(2)}) collective-permute-start(bf16[64,512]{1,0:T(8,128)(2,1)S(1)} %get-tuple-element.58), channel_id=1, source_target_pairs={{0,2},{1,3},{2,0},{3,1},{4,6},{5,7},{6,4},{7,5},{8,10},{9,11},{10,... | collective-permute-start | bytes 196616 | tf_op jit(solution)/shard_map/ppermute | solution.py:269
  43.9 2.1 %collective-permute-done.15.c = bf16[64,512]{1,0:T(8,128)(2,1)S(1)} collective-permute-done((bf16[64,512]{1,0:T(8,128)(2,1)S(1)}, bf16[64,512]{1,0:T(8,128)(2,1)S(1)}, u32[]{:S(2)}, u32[]{:S(2)}) %collective-permute-start.15) | collective-permute-done | bytes 65568 | tf_op jit(solution)/shard_map/ppermute | solution.py:269
  46.7 2.0 %collective-permute-start.18 = (bf16[64,512]{1,0:T(8,128)(2,1)S(1)}, bf16[64,512]{1,0:T(8,128)(2,1)S(1)}, u32[]{:S(2)}, u32[]{:S(2)}) collective-permute-start(bf16[64,512]{1,0:T(8,128)(2,1)S(1)} %shard_map.43.refs_0_.first), channel_id=1, source_target_pairs={{0,6},{1,7},{2,4},{3,5},{4,2},{5,3},{6,0},{7,1},{8,14},{9,15},{10,... | collective-permute-start | bytes 196616 | tf_op jit(solution)/shard_map/ppermute | solution.py:269
  48.7 1.3 %shard_map.44 = (f32[256,1024]{1,0:T(8,128)S(1)}, bf16[256,1024]{1,0:T(8,128)(2,1)S(1)}) custom-call(s32[1]{0:T(128)} %bitcast.middle, bf16[512,1024]{1,0:T(8,128)(2,1)S(1)} %get-tuple-element.71.turned, bf16[512,1024]{1,0:T(8,128)(2,1)S(1)} %get-tuple-element.62.beside, bf16[512,1024]{1,0:T(8,128)(2,1)S(1)} %get-tuple-element.63.opposite.swapped), custom_call_target="tpu_custom_call" | custom-call | tf_op jit(solution)/shard_map/pallas_call | solution.py:17
  50.8 3.7 %collective-permute-start.19 = (bf16[256,512]{1,0:T(8,128)(2,1)S(1)}, bf16[256,512]{1,0:T(8,128)(2,1)S(1)}, u32[]{:S(2)}, u32[]{:S(2)}) collective-permute-start(bf16[256,512]{1,0:T(8,128)(2,1)S(1)} %shard_map.45.near), channel_id=1, source_target_pairs={{0,1},{1,0},{2,3},{3,2},{4,5},{5,4},{6,7},{7,6},{8,9},{9,8},{10,11... | collective-permute-start | bytes 786440 | tf_op jit(solution)/shard_map/ppermute | solution.py:269
  55.6 1.8 %shard_map.46 = (bf16[512,1024]{1,0:T(8,128)(2,1)S(1)}, bf16[512,1024]{1,0:T(8,128)(2,1)S(1)}) custom-call(s32[8]{0:T(128)S(1)} %broadcast_xor_fusion.order, s32[1]{0:T(128)} %bitcast.middle, bf16[256,512]{1,0:T(8,128)(2,1)S(1)} %shard_map.45.near, bf16[256,512]{1,0:T(8,128)(2,1)S(1)} %collective-permute-done.19.far, ...), custom_call_target="tpu_custom_call" | custom-call | tf_op jit(solution)/shard_map/pallas_call | solution.py:17
  57.5 1.4 %collective-permute-start.29 = (bf16[512,1024]{1,0:T(8,128)(2,1)S(1)}, bf16[512,1024]{1,0:T(8,128)(2,1)S(1)}, u32[]{:S(2)}, u32[]{:S(2)}) collective-permute-start(bf16[512,1024]{1,0:T(8,128)(2,1)S(1)} %get-tuple-element.69), channel_id=1, source_target_pairs={{8,0},{16,24},{9,1},{17,25},{10,2},{18,26},{11,3},{19,27},{12,4},{... | collective-permute-start | bytes 3145736 | tf_op jit(solution)/shard_map/ppermute | solution.py:350
  58.9 3.1 %collective-permute-start.30 = (bf16[512,1024]{1,0:T(8,128)(2,1)S(1)}, bf16[512,1024]{1,0:T(8,128)(2,1)S(1)}, u32[]{:S(2)}, u32[]{:S(2)}) collective-permute-start(bf16[512,1024]{1,0:T(8,128)(2,1)S(1)} %get-tuple-element.84), channel_id=1, source_target_pairs={{8,16},{16,8},{9,17},{17,9},{10,18},{18,10},{11,19},{19,11},{12,20... | collective-permute-start | bytes 3145736 | tf_op jit(solution)/shard_map/ppermute | solution.py:350
  64.2 1.5 %collective-permute-done.21.got = bf16[256,1024]{1,0:T(8,128)(2,1)S(1)} collective-permute-done((bf16[256,1024]{1,0:T(8,128)(2,1)S(1)}, bf16[256,1024]{1,0:T(8,128)(2,1)S(1)}, u32[]{:S(2)}, u32[]{:S(2)}) %collective-permute-start.21) | collective-permute-done | bytes 524320 | tf_op jit(solution)/shard_map/ppermute | solution.py:269
  68.4 2.6 %shard_map.50.held = f32[512,1024]{1,0:T(8,128)S(1)} custom-call(s32[8]{0:T(128)S(1)} %broadcast_xor_fusion.order, s32[1]{0:T(128)} %bitcast.middle, bf16[256,640]{1,0:T(8,128)(2,1)S(1)} %pad_maximum_fusion.near, bf16[256,640]{1,0:T(8,128)(2,1)S(1)} %collective-permute-done.25.far, bf16[512,1024]{1,0:T(8,128)(2,1)S(1)} %get-tuple-element.79.own, ...), custom_call_target="tpu_custom_call" | custom-call | tf_op jit(solution)/shard_map/pallas_call | solution.py:17
  71.4 2.7 %collective-permute-done.24.c = bf16[64,1024]{1,0:T(8,128)(2,1)S(1)} collective-permute-done((bf16[64,1024]{1,0:T(8,128)(2,1)S(1)}, bf16[64,1024]{1,0:T(8,128)(2,1)S(1)}, u32[]{:S(2)}, u32[]{:S(2)}) %collective-permute-start.24) | collective-permute-done | bytes 131104 | tf_op jit(solution)/shard_map/ppermute | solution.py:269
  74.1 1.5 %collective-permute-start.26 = (bf16[64,1024]{1,0:T(8,128)(2,1)S(1)}, bf16[64,1024]{1,0:T(8,128)(2,1)S(1)}, u32[]{:S(2)}, u32[]{:S(2)}) collective-permute-start(bf16[64,1024]{1,0:T(8,128)(2,1)S(1)} %shard_map.49.refs_0_), channel_id=1, source_target_pairs={{0,2},{1,3},{2,0},{3,1},{4,6},{5,7},{6,4},{7,5},{8,10},{9,11},{10,... | collective-permute-start | bytes 393224 | tf_op jit(solution)/shard_map/ppermute | solution.py:269
  76.9 1.4 %collective-permute-done.26.refs_1_ = bf16[64,1024]{1,0:T(8,128)(2,1)S(1)} collective-permute-done((bf16[64,1024]{1,0:T(8,128)(2,1)S(1)}, bf16[64,1024]{1,0:T(8,128)(2,1)S(1)}, u32[]{:S(2)}, u32[]{:S(2)}) %collective-permute-start.26) | collective-permute-done | bytes 131104 | tf_op jit(solution)/shard_map/ppermute | solution.py:269
  78.3 2.1 %collective-permute-done.27.refs_2_ = bf16[64,1024]{1,0:T(8,128)(2,1)S(1)} collective-permute-done((bf16[64,1024]{1,0:T(8,128)(2,1)S(1)}, bf16[64,1024]{1,0:T(8,128)(2,1)S(1)}, u32[]{:S(2)}, u32[]{:S(2)}) %collective-permute-start.27) | collective-permute-done | bytes 131104 | tf_op jit(solution)/shard_map/ppermute | solution.py:269
  81.6 3.4 %collective-permute-done.30.over = bf16[512,1024]{1,0:T(8,128)(2,1)S(1)} collective-permute-done((bf16[512,1024]{1,0:T(8,128)(2,1)S(1)}, bf16[512,1024]{1,0:T(8,128)(2,1)S(1)}, u32[]{:S(2)}, u32[]{:S(2)}) %collective-permute-start.30) | collective-permute-done | bytes 1048608 | tf_op jit(solution)/shard_map/ppermute | solution.py:350
  85.0 1.5 %collective-permute-start.31 = (bf16[256,1024]{1,0:T(8,128)(2,1)S(1)}, bf16[256,1024]{1,0:T(8,128)(2,1)S(1)}, u32[]{:S(2)}, u32[]{:S(2)}) collective-permute-start(bf16[256,1024]{1,0:T(8,128)(2,1)S(1)} %shard_map.51.near), channel_id=1, source_target_pairs={{0,1},{1,0},{2,3},{3,2},{4,5},{5,4},{6,7},{7,6},{8,9},{9,8},{10,11... | collective-permute-start | bytes 1572872 | tf_op jit(solution)/shard_map/ppermute | solution.py:269
  86.5 1.5 %collective-permute-done.31.far = bf16[256,1024]{1,0:T(8,128)(2,1)S(1)} collective-permute-done((bf16[256,1024]{1,0:T(8,128)(2,1)S(1)}, bf16[256,1024]{1,0:T(8,128)(2,1)S(1)}, u32[]{:S(2)}, u32[]{:S(2)}) %collective-permute-start.31) | collective-permute-done | bytes 524320 | tf_op jit(solution)/shard_map/ppermute | solution.py:269
  88.1 3.3 %shard_map.52 = f32[512,1024]{1,0:T(8,128)} custom-call(s32[8]{0:T(128)S(1)} %broadcast_xor_fusion.order, s32[1]{0:T(128)} %bitcast.middle, bf16[256,1024]{1,0:T(8,128)(2,1)S(1)} %shard_map.51.near, bf16[256,1024]{1,0:T(8,128)(2,1)S(1)} %collective-permute-done.31.far, bf16[512,1024]{1,0:T(8,128)(2,1)S(1)} %get-tuple-element.62.beside, ...), custom_call_target="tpu_custom_call" | custom-call | tf_op jit(solution)/shard_map/pallas_call | solution.py:17
  (53 shorter events, 24.6 us)
Async XLA Ops:
  1.8 8.5 %collective-permute-start.2 = (f32[2,1024]{1,0:T(2,128)S(1)}, f32[2,1024]{1,0:T(2,128)S(1)}, u32[]{:S(2)}, u32[]{:S(2)}) collective-permute-start(f32[2,1024]{1,0:T(2,128)S(1)} %shard_map.37), channel_id=1, source_target_pairs={{0,24},{8,0},{16,8},{24,16},{1,25},{9,1},{17,9},{25,17},{2,26},{10... | collective-permute-start | bytes 24584 | tf_op jit(solution)/shard_map/ppermute | solution.py:315
  1.9 8.4 %collective-permute-start.1 = (f32[2,1024]{1,0:T(2,128)S(1)}, f32[2,1024]{1,0:T(2,128)S(1)}, u32[]{:S(2)}, u32[]{:S(2)}) collective-permute-start(f32[2,1024]{1,0:T(2,128)S(1)} %shard_map.37), channel_id=1, source_target_pairs={{0,16},{8,24},{16,0},{24,8},{1,17},{9,25},{17,1},{25,9},{2,18},{10... | collective-permute-start | bytes 24584 | tf_op jit(solution)/shard_map/ppermute | solution.py:315
  4.3 6.0 %collective-permute-start = (f32[2,1024]{1,0:T(2,128)S(1)}, f32[2,1024]{1,0:T(2,128)S(1)}, u32[]{:S(2)}, u32[]{:S(2)}) collective-permute-start(f32[2,1024]{1,0:T(2,128)S(1)} %shard_map.37), channel_id=1, source_target_pairs={{0,8},{8,16},{16,24},{24,0},{1,9},{9,17},{17,25},{25,1},{2,10},{10... | collective-permute-start | bytes 24584 | tf_op jit(solution)/shard_map/ppermute | solution.py:315
  6.5 23.4 %collective-permute-start.10 = (bf16[512,1024]{1,0:T(8,128)(2,1)}, bf16[512,1024]{1,0:T(8,128)(2,1)S(1)}, u32[]{:S(2)}, u32[]{:S(2)}) collective-permute-start(bf16[512,1024]{1,0:T(8,128)(2,1)} %z.5), channel_id=1, source_target_pairs={{0,8},{8,0},{16,24},{24,16},{1,9},{9,1},{17,25},{25,17},{2,10},{10... | collective-permute-start | bytes 3145736 | tf_op jit(solution)/shard_map/ppermute | solution.py:318
  6.5 25.3 %collective-permute-start.11 = (bf16[512,1024]{1,0:T(8,128)(2,1)}, bf16[512,1024]{1,0:T(8,128)(2,1)}, u32[]{:S(2)}, u32[]{:S(2)}) collective-permute-start(bf16[512,1024]{1,0:T(8,128)(2,1)} %z.5), channel_id=1, source_target_pairs={{8,16},{16,8},{9,17},{17,9},{10,18},{18,10},{11,19},{19,11},{12,20... | collective-permute-start | bytes 3145736 | tf_op jit(solution)/shard_map/ppermute | solution.py:319
  12.7 3.1 %collective-permute-start.3 = (bf16[256,640]{1,0:T(8,128)(2,1)S(1)}, bf16[256,640]{1,0:T(8,128)(2,1)S(1)}, u32[]{:S(2)}, u32[]{:S(2)}) collective-permute-start(bf16[256,640]{1,0:T(8,128)(2,1)S(1)} %get-tuple-element.48), channel_id=1, source_target_pairs={{0,1},{1,0},{2,3},{3,2},{4,5},{5,4},{6,7},{7,6},{8,9},{9,8},{10,11... | collective-permute-start | bytes 983048 | tf_op jit(solution)/shard_map/ppermute | solution.py:269
  16.0 3.8 %collective-permute-start.4 = (bf16[64,640]{1,0:T(8,128)(2,1)S(1)}, bf16[64,640]{1,0:T(8,128)(2,1)S(1)}, u32[]{:S(2)}, u32[]{:S(2)}) collective-permute-start(bf16[64,640]{1,0:T(8,128)(2,1)S(1)} %get-tuple-element.50), channel_id=1, source_target_pairs={{0,2},{1,3},{2,0},{3,1},{4,6},{5,7},{6,4},{7,5},{8,10},{9,11},{10,... | collective-permute-start | bytes 245768 | tf_op jit(solution)/shard_map/ppermute | solution.py:269
  17.3 3.7 %collective-permute-start.5 = (bf16[64,640]{1,0:T(8,128)(2,1)S(1)}, bf16[64,640]{1,0:T(8,128)(2,1)S(1)}, u32[]{:S(2)}, u32[]{:S(2)}) collective-permute-start(bf16[64,640]{1,0:T(8,128)(2,1)S(1)} %get-tuple-element.51), channel_id=1, source_target_pairs={{0,4},{1,5},{2,6},{3,7},{4,0},{5,1},{6,2},{7,3},{8,12},{9,13},{10,... | collective-permute-start | bytes 245768 | tf_op jit(solution)/shard_map/ppermute | solution.py:269
  18.5 4.2 %collective-permute-start.6 = (bf16[64,640]{1,0:T(8,128)(2,1)S(1)}, bf16[64,640]{1,0:T(8,128)(2,1)S(1)}, u32[]{:S(2)}, u32[]{:S(2)}) collective-permute-start(bf16[64,640]{1,0:T(8,128)(2,1)S(1)} %get-tuple-element.52), channel_id=1, source_target_pairs={{0,6},{1,7},{2,4},{3,5},{4,2},{5,3},{6,0},{7,1},{8,14},{9,15},{10,... | collective-permute-start | bytes 245768 | tf_op jit(solution)/shard_map/ppermute | solution.py:269
  22.8 4.4 %collective-permute-start.9 = (bf16[64,640]{1,0:T(8,128)(2,1)S(1)}, bf16[64,640]{1,0:T(8,128)(2,1)S(1)}, u32[]{:S(2)}, u32[]{:S(2)}) collective-permute-start(bf16[64,640]{1,0:T(8,128)(2,1)S(1)} %shard_map.40), channel_id=1, source_target_pairs={{0,6},{1,7},{2,4},{3,5},{4,2},{5,3},{6,0},{7,1},{8,14},{9,15},{10,... | collective-permute-start | bytes 245768 | tf_op jit(solution)/shard_map/ppermute | solution.py:269
  23.4 4.6 %collective-permute-start.8 = (bf16[64,640]{1,0:T(8,128)(2,1)S(1)}, bf16[64,640]{1,0:T(8,128)(2,1)S(1)}, u32[]{:S(2)}, u32[]{:S(2)}) collective-permute-start(bf16[64,640]{1,0:T(8,128)(2,1)S(1)} %shard_map.40), channel_id=1, source_target_pairs={{0,4},{1,5},{2,6},{3,7},{4,0},{5,1},{6,2},{7,3},{8,12},{9,13},{10,... | collective-permute-start | bytes 245768 | tf_op jit(solution)/shard_map/ppermute | solution.py:269
  24.6 3.7 %collective-permute-start.7 = (bf16[64,640]{1,0:T(8,128)(2,1)S(1)}, bf16[64,640]{1,0:T(8,128)(2,1)S(1)}, u32[]{:S(2)}, u32[]{:S(2)}) collective-permute-start(bf16[64,640]{1,0:T(8,128)(2,1)S(1)} %shard_map.40), channel_id=1, source_target_pairs={{0,2},{1,3},{2,0},{3,1},{4,6},{5,7},{6,4},{7,5},{8,10},{9,11},{10,... | collective-permute-start | bytes 245768 | tf_op jit(solution)/shard_map/ppermute | solution.py:269
  31.9 27.0 %collective-permute-start.20 = (bf16[512,1024]{1,0:T(8,128)(2,1)}, bf16[512,1024]{1,0:T(8,128)(2,1)}, u32[]{:S(2)}, u32[]{:S(2)}) collective-permute-start(bf16[512,1024]{1,0:T(8,128)(2,1)} %z.5), channel_id=1, source_target_pairs={{0,24},{24,0},{1,25},{25,1},{2,26},{26,2},{3,27},{27,3},{4,28},{28... | collective-permute-start | bytes 3145736 | tf_op jit(solution)/shard_map/ppermute | solution.py:334
  35.7 3.7 %collective-permute-start.12 = (bf16[256,512]{1,0:T(8,128)(2,1)S(1)}, bf16[256,512]{1,0:T(8,128)(2,1)S(1)}, u32[]{:S(2)}, u32[]{:S(2)}) collective-permute-start(bf16[256,512]{1,0:T(8,128)(2,1)S(1)} %get-tuple-element.56), channel_id=1, source_target_pairs={{0,1},{1,0},{2,3},{3,2},{4,5},{5,4},{6,7},{7,6},{8,9},{9,8},{10,11... | collective-permute-start | bytes 786440 | tf_op jit(solution)/shard_map/ppermute | solution.py:269
  39.5 3.2 %collective-permute-start.13 = (bf16[64,512]{1,0:T(8,128)(2,1)S(1)}, bf16[64,512]{1,0:T(8,128)(2,1)S(1)}, u32[]{:S(2)}, u32[]{:S(2)}) collective-permute-start(bf16[64,512]{1,0:T(8,128)(2,1)S(1)} %get-tuple-element.58), channel_id=1, source_target_pairs={{0,2},{1,3},{2,0},{3,1},{4,6},{5,7},{6,4},{7,5},{8,10},{9,11},{10,... | collective-permute-start | bytes 196616 | tf_op jit(solution)/shard_map/ppermute | solution.py:269
  40.7 3.1 %collective-permute-start.14 = (bf16[64,512]{1,0:T(8,128)(2,1)S(1)}, bf16[64,512]{1,0:T(8,128)(2,1)S(1)}, u32[]{:S(2)}, u32[]{:S(2)}) collective-permute-start(bf16[64,512]{1,0:T(8,128)(2,1)S(1)} %get-tuple-element.59), channel_id=1, source_target_pairs={{0,4},{1,5},{2,6},{3,7},{4,0},{5,1},{6,2},{7,3},{8,12},{9,13},{10,... | collective-permute-start | bytes 196616 | tf_op jit(solution)/shard_map/ppermute | solution.py:269
  42.0 4.0 %collective-permute-start.15 = (bf16[64,512]{1,0:T(8,128)(2,1)S(1)}, bf16[64,512]{1,0:T(8,128)(2,1)S(1)}, u32[]{:S(2)}, u32[]{:S(2)}) collective-permute-start(bf16[64,512]{1,0:T(8,128)(2,1)S(1)} %get-tuple-element.60), channel_id=1, source_target_pairs={{0,6},{1,7},{2,4},{3,5},{4,2},{5,3},{6,0},{7,1},{8,14},{9,15},{10,... | collective-permute-start | bytes 196616 | tf_op jit(solution)/shard_map/ppermute | solution.py:269
  46.0 4.0 %collective-permute-start.16 = (bf16[64,512]{1,0:T(8,128)(2,1)S(1)}, bf16[64,512]{1,0:T(8,128)(2,1)S(1)}, u32[]{:S(2)}, u32[]{:S(2)}) collective-permute-start(bf16[64,512]{1,0:T(8,128)(2,1)S(1)} %shard_map.43.refs_0_.first), channel_id=1, source_target_pairs={{0,2},{1,3},{2,0},{3,1},{4,6},{5,7},{6,4},{7,5},{8,10},{9,11},{10,... | collective-permute-start | bytes 196616 | tf_op jit(solution)/shard_map/ppermute | solution.py:269
  46.5 3.6 %collective-permute-start.17 = (bf16[64,512]{1,0:T(8,128)(2,1)S(1)}, bf16[64,512]{1,0:T(8,128)(2,1)S(1)}, u32[]{:S(2)}, u32[]{:S(2)}) collective-permute-start(bf16[64,512]{1,0:T(8,128)(2,1)S(1)} %shard_map.43.refs_0_.first), channel_id=1, source_target_pairs={{0,4},{1,5},{2,6},{3,7},{4,0},{5,1},{6,2},{7,3},{8,12},{9,13},{10,... | collective-permute-start | bytes 196616 | tf_op jit(solution)/shard_map/ppermute | solution.py:269
  46.7 4.0 %collective-permute-start.18 = (bf16[64,512]{1,0:T(8,128)(2,1)S(1)}, bf16[64,512]{1,0:T(8,128)(2,1)S(1)}, u32[]{:S(2)}, u32[]{:S(2)}) collective-permute-start(bf16[64,512]{1,0:T(8,128)(2,1)S(1)} %shard_map.43.refs_0_.first), channel_id=1, source_target_pairs={{0,6},{1,7},{2,4},{3,5},{4,2},{5,3},{6,0},{7,1},{8,14},{9,15},{10,... | collective-permute-start | bytes 196616 | tf_op jit(solution)/shard_map/ppermute | solution.py:269
  50.8 4.9 %collective-permute-start.19 = (bf16[256,512]{1,0:T(8,128)(2,1)S(1)}, bf16[256,512]{1,0:T(8,128)(2,1)S(1)}, u32[]{:S(2)}, u32[]{:S(2)}) collective-permute-start(bf16[256,512]{1,0:T(8,128)(2,1)S(1)} %shard_map.45.near), channel_id=1, source_target_pairs={{0,1},{1,0},{2,3},{3,2},{4,5},{5,4},{6,7},{7,6},{8,9},{9,8},{10,11... | collective-permute-start | bytes 786440 | tf_op jit(solution)/shard_map/ppermute | solution.py:269
  57.5 24.2 %collective-permute-start.29 = (bf16[512,1024]{1,0:T(8,128)(2,1)S(1)}, bf16[512,1024]{1,0:T(8,128)(2,1)S(1)}, u32[]{:S(2)}, u32[]{:S(2)}) collective-permute-start(bf16[512,1024]{1,0:T(8,128)(2,1)S(1)} %get-tuple-element.69), channel_id=1, source_target_pairs={{8,0},{16,24},{9,1},{17,25},{10,2},{18,26},{11,3},{19,27},{12,4},{... | collective-permute-start | bytes 3145736 | tf_op jit(solution)/shard_map/ppermute | solution.py:350
  58.9 26.1 %collective-permute-start.30 = (bf16[512,1024]{1,0:T(8,128)(2,1)S(1)}, bf16[512,1024]{1,0:T(8,128)(2,1)S(1)}, u32[]{:S(2)}, u32[]{:S(2)}) collective-permute-start(bf16[512,1024]{1,0:T(8,128)(2,1)S(1)} %get-tuple-element.84), channel_id=1, source_target_pairs={{8,16},{16,8},{9,17},{17,9},{10,18},{18,10},{11,19},{19,11},{12,20... | collective-permute-start | bytes 3145736 | tf_op jit(solution)/shard_map/ppermute | solution.py:350
  63.4 2.3 %collective-permute-start.21 = (bf16[256,1024]{1,0:T(8,128)(2,1)S(1)}, bf16[256,1024]{1,0:T(8,128)(2,1)S(1)}, u32[]{:S(2)}, u32[]{:S(2)}) collective-permute-start(bf16[256,1024]{1,0:T(8,128)(2,1)S(1)} %get-tuple-element.74), channel_id=1, source_target_pairs={{0,1},{1,0},{2,3},{3,2},{4,5},{5,4},{6,7},{7,6},{8,9},{9,8},{10,11... | collective-permute-start | bytes 1572872 | tf_op jit(solution)/shard_map/ppermute | solution.py:269
  64.1 4.2 %collective-permute-start.25 = (bf16[256,640]{1,0:T(8,128)(2,1)S(1)}, bf16[256,640]{1,0:T(8,128)(2,1)S(1)}, u32[]{:S(2)}, u32[]{:S(2)}) collective-permute-start(bf16[256,640]{1,0:T(8,128)(2,1)S(1)} %pad_maximum_fusion.near), channel_id=1, source_target_pairs={{0,1},{1,0},{2,3},{3,2},{4,5},{5,4},{6,7},{7,6},{8,9},{9,8},{10,11... | collective-permute-start | bytes 983048 | tf_op jit(solution)/shard_map/ppermute | solution.py:269
  65.7 5.3 %collective-permute-start.22 = (bf16[64,1024]{1,0:T(8,128)(2,1)S(1)}, bf16[64,1024]{1,0:T(8,128)(2,1)S(1)}, u32[]{:S(2)}, u32[]{:S(2)}) collective-permute-start(bf16[64,1024]{1,0:T(8,128)(2,1)S(1)} %get-tuple-element.76), channel_id=1, source_target_pairs={{0,2},{1,3},{2,0},{3,1},{4,6},{5,7},{6,4},{7,5},{8,10},{9,11},{10,... | collective-permute-start | bytes 393224 | tf_op jit(solution)/shard_map/ppermute | solution.py:269
  67.0 4.4 %collective-permute-start.23 = (bf16[64,1024]{1,0:T(8,128)(2,1)S(1)}, bf16[64,1024]{1,0:T(8,128)(2,1)S(1)}, u32[]{:S(2)}, u32[]{:S(2)}) collective-permute-start(bf16[64,1024]{1,0:T(8,128)(2,1)S(1)} %get-tuple-element.77), channel_id=1, source_target_pairs={{0,4},{1,5},{2,6},{3,7},{4,0},{5,1},{6,2},{7,3},{8,12},{9,13},{10,... | collective-permute-start | bytes 393224 | tf_op jit(solution)/shard_map/ppermute | solution.py:269
  68.2 5.8 %collective-permute-start.24 = (bf16[64,1024]{1,0:T(8,128)(2,1)S(1)}, bf16[64,1024]{1,0:T(8,128)(2,1)S(1)}, u32[]{:S(2)}, u32[]{:S(2)}) collective-permute-start(bf16[64,1024]{1,0:T(8,128)(2,1)S(1)} %get-tuple-element.78), channel_id=1, source_target_pairs={{0,6},{1,7},{2,4},{3,5},{4,2},{5,3},{6,0},{7,1},{8,14},{9,15},{10,... | collective-permute-start | bytes 393224 | tf_op jit(solution)/shard_map/ppermute | solution.py:269
  74.1 4.2 %collective-permute-start.26 = (bf16[64,1024]{1,0:T(8,128)(2,1)S(1)}, bf16[64,1024]{1,0:T(8,128)(2,1)S(1)}, u32[]{:S(2)}, u32[]{:S(2)}) collective-permute-start(bf16[64,1024]{1,0:T(8,128)(2,1)S(1)} %shard_map.49.refs_0_), channel_id=1, source_target_pairs={{0,2},{1,3},{2,0},{3,1},{4,6},{5,7},{6,4},{7,5},{8,10},{9,11},{10,... | collective-permute-start | bytes 393224 | tf_op jit(solution)/shard_map/ppermute | solution.py:269
  75.6 4.8 %collective-permute-start.27 = (bf16[64,1024]{1,0:T(8,128)(2,1)S(1)}, bf16[64,1024]{1,0:T(8,128)(2,1)S(1)}, u32[]{:S(2)}, u32[]{:S(2)}) collective-permute-start(bf16[64,1024]{1,0:T(8,128)(2,1)S(1)} %shard_map.49.refs_0_), channel_id=1, source_target_pairs={{0,4},{1,5},{2,6},{3,7},{4,0},{5,1},{6,2},{7,3},{8,12},{9,13},{10,... | collective-permute-start | bytes 393224 | tf_op jit(solution)/shard_map/ppermute | solution.py:269
  75.9 5.7 %collective-permute-start.28 = (bf16[64,1024]{1,0:T(8,128)(2,1)S(1)}, bf16[64,1024]{1,0:T(8,128)(2,1)S(1)}, u32[]{:S(2)}, u32[]{:S(2)}) collective-permute-start(bf16[64,1024]{1,0:T(8,128)(2,1)S(1)} %shard_map.49.refs_0_), channel_id=1, source_target_pairs={{0,6},{1,7},{2,4},{3,5},{4,2},{5,3},{6,0},{7,1},{8,14},{9,15},{10,... | collective-permute-start | bytes 393224 | tf_op jit(solution)/shard_map/ppermute | solution.py:269
  85.0 3.1 %collective-permute-start.31 = (bf16[256,1024]{1,0:T(8,128)(2,1)S(1)}, bf16[256,1024]{1,0:T(8,128)(2,1)S(1)}, u32[]{:S(2)}, u32[]{:S(2)}) collective-permute-start(bf16[256,1024]{1,0:T(8,128)(2,1)S(1)} %shard_map.51.near), channel_id=1, source_target_pairs={{0,1},{1,0},{2,3},{3,2},{4,5},{5,4},{6,7},{7,6},{8,9},{9,8},{10,11... | collective-permute-start | bytes 1572872 | tf_op jit(solution)/shard_map/ppermute | solution.py:269
  (1 other events, 9.5 us)

commit v19 on v18

--- a/solution.py
+++ b/solution.py
@@ -11,15 +11,16 @@
 NORM = 128
 
 
-def kernel_call(body, outs, smem=0, scratch=4, temps=()):
+def kernel_call(body, outs, smem=0, scratch=4, temps=(), sems=0):
     def call(*args):
         space = [pltpu.SMEM] * smem + [pltpu.VMEM] * (len(args) - smem)
         return pl.pallas_call(
             body,
             out_shape=[jax.ShapeDtypeStruct(s, t) for s, t in outs],
             in_specs=[pl.BlockSpec(memory_space=m) for m in space],
-            out_specs=[pl.BlockSpec(memory_space=pltpu.VMEM) for _ in outs],
-            scratch_shapes=[pltpu.VMEM(s, t) for s, t in temps],
+            out_specs=[pl.BlockSpec(memory_space=pl.ANY if sems else pltpu.VMEM) for _ in outs],
+            scratch_shapes=[pltpu.VMEM(s, t) for s, t in temps]
+            + ([pltpu.SemaphoreType.DMA((sems,))] if sems else []),
             compiler_params=pltpu.CompilerParams(vmem_limit_bytes=scratch * 1024 * 1024),
             cost_estimate=pl.CostEstimate(flops=0, bytes_accessed=0, transcendentals=0),
         )(*args)
@@ -248,7 +249,7 @@
 
 
 def last_kernel(
-    total, order, middle, near, far, beside, swapped, end, held, out, over, result, second
+    total, order, middle, near, far, beside, swapped, end, held, out, over, result, second, made, sem
 ):
     rows, width = beside.shape
     place_into(second, order, near, far)
@@ -259,10 +260,17 @@
             product = dot(second[:, rows:], beside[:, here])
             product = product + dot(second[:, :rows], opposite[:, here])
             product = product + arrived[:, here].astype(jnp.float32)
-            result[:, here] = held[:, here] + coefficient(total) * product
+            made[:, here] = held[:, here] + coefficient(total) * product
+            to_result(k).start()
+
+    def to_result(k):
+        here = slice(k * width // 4, (k + 1) * width // 4)
+        return pltpu.make_async_copy(made.at[:, here], result.at[:, here], sem.at[k])
 
     pl.when(middle[0] == 1)(lambda: put(swapped, over))
     pl.when(middle[0] == 0)(lambda: put(end, out))
+    for k in range(4):
+        to_result(k).wait()
 
 
 def to_partner(x, step):
@@ -369,10 +377,10 @@
     second = kernel_call(total_either_kernel, [(eighth, jnp.bfloat16)], smem=1)(
         middle, first, halved[0], *got
     )[0]
-    near = after(gather_chips(after(second, held)), *pushed)
+    near = after(gather_chips(after(second, held)), pushed[0])
     return kernel_call(
         functools.partial(last_kernel, total), [result],
-        smem=2, scratch=12, temps=[((rows, 2 * rows), jnp.bfloat16)],
+        smem=2, scratch=12, temps=[((rows, 2 * rows), jnp.bfloat16), result], sems=4,
     )(
         order, middle, near, to_partner(near, 1), beside, swapped, end, held, *pushed
     )[0]

time: 91.7 us -> 91.3 us (level)
    ppermute x24, waiting for transfers between devices: 25.6 us -> 21.8 us  [to_partner(): return lax.ppermute(x, 'feat', [(i, i ^ step) for i in range(8)])]
    ppermute x1, waiting for transfers between devices: 0.01 us -> 1.89 us  [by_line(): lax.ppermute(out, 'dp', outward)]
    ppermute x1, waiting for transfers between devices: 3.39 us -> 4.87 us  [by_line(): lax.ppermute(after(over, end), 'dp', across)]
  transfers between devices with their start and end apart: 32 -> 32, of which waited for: 23 -> 22; matrix products, arithmetic and copies ran while one was open for 1% -> 1% of each run, Pallas kernels for 13% -> 13%
where the time goes in v19:
time: 91.3 us; the launch traced here: 90.3 us
  starting transfers between devices  40.2 us (44%)
  waiting for transfers between devices  32.1 us (35%)
  Pallas kernels  17 us (19%)
    ppermute x24, starting transfers between devices, to_partner(): return lax.ppermute(x, 'feat', [(i, i ^ step) for i in range(8)])  26.6 us
    ppermute x24, waiting for transfers between devices, to_partner(): return lax.ppermute(x, 'feat', [(i, i ^ step) for i in range(8)])  21.8 us
    pallas_call x16, Pallas kernels, call(): pl.pallas_call(body, out_shape=[jax.ShapeDtypeStruct(s, t) for s, t in ou...  17 us
    ppermute x1, waiting for transfers between devices, by_line(): lax.ppermute(after(over, end), 'dp', across)  4.87 us
    ppermute x3, starting transfers between devices, by_line(): lax.ppermute(stats, 'dp', [(i, (i + k) % 4) for i in range(4)])  4.72 us
    ppermute x1, starting transfers between devices, by_line(): swapped = lax.ppermute(ahead, 'dp', across)  3.08 us
    ppermute x1, starting transfers between devices, by_line(): lax.ppermute(after(over, end), 'dp', across)  2.77 us
    ppermute x1, waiting for transfers between devices, by_line(): lax.ppermute(out, 'dp', outward)  1.89 us
  transfers between devices with their start and end apart: 32, of which 22 were waited for; matrix products, arithmetic and copies ran while one was open for 1% of the time, Pallas kernels for 13%

profile of v19, /device:TPU:9, one launch (start us, length us, event | category | flops | bytes accessed | tf_op | source)
XLA Modules:
  0.0 90.3 jit_solution(15911896021521189481)
XLA Ops:
  0.0 1.8 %shard_map.37 = f32[2,1024]{1,0:T(2,128)S(1)} custom-call(bf16[512,1024]{1,0:T(8,128)(2,1)} %z.5), custom_call_target="tpu_custom_call" | custom-call | tf_op jit(solution)/shard_map/pallas_call | solution.py:17
  1.9 2.5 %collective-permute-start.1 = (f32[2,1024]{1,0:T(2,128)S(1)}, f32[2,1024]{1,0:T(2,128)S(1)}, u32[]{:S(2)}, u32[]{:S(2)}) collective-permute-start(f32[2,1024]{1,0:T(2,128)S(1)} %shard_map.37), channel_id=1, source_target_pairs={{0,16},{8,24},{16,0},{24,8},{1,17},{9,25},{17,1},{25,9},{2,18},{10... | collective-permute-start | bytes 24584 | tf_op jit(solution)/shard_map/ppermute | solution.py:323
  4.3 2.2 %collective-permute-start = (f32[2,1024]{1,0:T(2,128)S(1)}, f32[2,1024]{1,0:T(2,128)S(1)}, u32[]{:S(2)}, u32[]{:S(2)}) collective-permute-start(f32[2,1024]{1,0:T(2,128)S(1)} %shard_map.37), channel_id=1, source_target_pairs={{0,8},{8,16},{16,24},{24,0},{1,9},{9,17},{17,25},{25,1},{2,10},{10... | collective-permute-start | bytes 24584 | tf_op jit(solution)/shard_map/ppermute | solution.py:323
  6.5 3.1 %collective-permute-start.11 = (bf16[512,1024]{1,0:T(8,128)(2,1)}, bf16[512,1024]{1,0:T(8,128)(2,1)}, u32[]{:S(2)}, u32[]{:S(2)}) collective-permute-start(bf16[512,1024]{1,0:T(8,128)(2,1)} %z.5), channel_id=1, source_target_pairs={{8,16},{16,8},{9,17},{17,9},{10,18},{18,10},{11,19},{19,11},{12,20... | collective-permute-start | bytes 3145736 | tf_op jit(solution)/shard_map/ppermute | solution.py:327
  10.4 2.4 %shard_map.38 = (bf16[512,1024]{1,0:T(8,128)(2,1)S(1)}, bf16[512,1024]{1,0:T(8,128)(2,1)S(1)}, f32[1,1024]{1,0:T(1,128)S(1)}, f32[256,640]{1,0:T(8,128)S(1)}, bf16[256,640]{1,0:T(8,128)(2,1)S(1)}) custom-call(s32[8]{0:T(128)S(1)} %broadcast_xor_fusion.order, bf16[512,1024]{1,0:T(8,128)(2,1)} %z.5, f32[1,1024]{1,0:T(1,128)S(1)} %get-tuple-element.88.mean), custom_call_target="tpu_custom_call" | custom-call | tf_op jit(solution)/shard_map/pallas_call | solution.py:17
  12.7 1.9 %collective-permute-start.3 = (bf16[256,640]{1,0:T(8,128)(2,1)S(1)}, bf16[256,640]{1,0:T(8,128)(2,1)S(1)}, u32[]{:S(2)}, u32[]{:S(2)}) collective-permute-start(bf16[256,640]{1,0:T(8,128)(2,1)S(1)} %get-tuple-element.48), channel_id=1, source_target_pairs={{0,1},{1,0},{2,3},{3,2},{4,5},{5,4},{6,7},{7,6},{8,9},{9,8},{10,11... | collective-permute-start | bytes 983048 | tf_op jit(solution)/shard_map/ppermute | solution.py:277
  16.0 1.3 %collective-permute-start.4 = (bf16[64,640]{1,0:T(8,128)(2,1)S(1)}, bf16[64,640]{1,0:T(8,128)(2,1)S(1)}, u32[]{:S(2)}, u32[]{:S(2)}) collective-permute-start(bf16[64,640]{1,0:T(8,128)(2,1)S(1)} %get-tuple-element.50), channel_id=1, source_target_pairs={{0,2},{1,3},{2,0},{3,1},{4,6},{5,7},{6,4},{7,5},{8,10},{9,11},{10,... | collective-permute-start | bytes 245768 | tf_op jit(solution)/shard_map/ppermute | solution.py:277
  20.9 1.7 %collective-permute-done.6.c = bf16[64,640]{1,0:T(8,128)(2,1)S(1)} collective-permute-done((bf16[64,640]{1,0:T(8,128)(2,1)S(1)}, bf16[64,640]{1,0:T(8,128)(2,1)S(1)}, u32[]{:S(2)}, u32[]{:S(2)}) %collective-permute-start.6) | collective-permute-done | bytes 81952 | tf_op jit(solution)/shard_map/ppermute | solution.py:277
  25.5 1.6 %collective-permute-done.9 = bf16[64,640]{1,0:T(8,128)(2,1)S(1)} collective-permute-done((bf16[64,640]{1,0:T(8,128)(2,1)S(1)}, bf16[64,640]{1,0:T(8,128)(2,1)S(1)}, u32[]{:S(2)}, u32[]{:S(2)}) %collective-permute-start.9) | collective-permute-done | bytes 81952 | tf_op jit(solution)/shard_map/ppermute | solution.py:277
  28.4 1.6 %collective-permute-done.10.beside_in = bf16[512,1024]{1,0:T(8,128)(2,1)S(1)} collective-permute-done((bf16[512,1024]{1,0:T(8,128)(2,1)}, bf16[512,1024]{1,0:T(8,128)(2,1)S(1)}, u32[]{:S(2)}, u32[]{:S(2)}) %collective-permute-start.10) | collective-permute-done | bytes 1048608 | tf_op jit(solution)/shard_map/ppermute | solution.py:326
  30.0 1.9 %collective-permute-done.11.opposite_in = bf16[512,1024]{1,0:T(8,128)(2,1)} collective-permute-done((bf16[512,1024]{1,0:T(8,128)(2,1)}, bf16[512,1024]{1,0:T(8,128)(2,1)}, u32[]{:S(2)}, u32[]{:S(2)}) %collective-permute-start.11) | collective-permute-done | bytes 1048608 | tf_op jit(solution)/shard_map/ppermute | solution.py:327
  31.9 1.6 %collective-permute-start.20 = (bf16[512,1024]{1,0:T(8,128)(2,1)}, bf16[512,1024]{1,0:T(8,128)(2,1)}, u32[]{:S(2)}, u32[]{:S(2)}) collective-permute-start(bf16[512,1024]{1,0:T(8,128)(2,1)} %z.5), channel_id=1, source_target_pairs={{0,24},{24,0},{1,25},{25,1},{2,26},{26,2},{3,27},{27,3},{4,28},{28... | collective-permute-start | bytes 3145736 | tf_op jit(solution)/shard_map/ppermute | solution.py:342
  33.5 2.2 %shard_map.41 = (bf16[512,1024]{1,0:T(8,128)(2,1)S(1)}, f32[1,1024]{1,0:T(1,128)S(1)}, bf16[512,1024]{1,0:T(8,128)(2,1)S(1)}, f32[1,1024]{1,0:T(1,128)S(1)}, f32...) custom-call(s32[8]{0:T(128)S(1)} %broadcast_xor_fusion.order, s32[1]{0:T(128)} %bitcast.middle, ...), custom_call_target="tpu_custom_call" | custom-call | tf_op jit(solution)/shard_map/pallas_call | solution.py:17
  35.7 2.5 %collective-permute-start.12 = (bf16[256,512]{1,0:T(8,128)(2,1)S(1)}, bf16[256,512]{1,0:T(8,128)(2,1)S(1)}, u32[]{:S(2)}, u32[]{:S(2)}) collective-permute-start(bf16[256,512]{1,0:T(8,128)(2,1)S(1)} %get-tuple-element.56), channel_id=1, source_target_pairs={{0,1},{1,0},{2,3},{3,2},{4,5},{5,4},{6,7},{7,6},{8,9},{9,8},{10,11... | collective-permute-start | bytes 786440 | tf_op jit(solution)/shard_map/ppermute | solution.py:277
  39.5 1.3 %collective-permute-start.13 = (bf16[64,512]{1,0:T(8,128)(2,1)S(1)}, bf16[64,512]{1,0:T(8,128)(2,1)S(1)}, u32[]{:S(2)}, u32[]{:S(2)}) collective-permute-start(bf16[64,512]{1,0:T(8,128)(2,1)S(1)} %get-tuple-element.58), channel_id=1, source_target_pairs={{0,2},{1,3},{2,0},{3,1},{4,6},{5,7},{6,4},{7,5},{8,10},{9,11},{10,... | collective-permute-start | bytes 196616 | tf_op jit(solution)/shard_map/ppermute | solution.py:277
  43.9 2.1 %collective-permute-done.15.c = bf16[64,512]{1,0:T(8,128)(2,1)S(1)} collective-permute-done((bf16[64,512]{1,0:T(8,128)(2,1)S(1)}, bf16[64,512]{1,0:T(8,128)(2,1)S(1)}, u32[]{:S(2)}, u32[]{:S(2)}) %collective-permute-start.15) | collective-permute-done | bytes 65568 | tf_op jit(solution)/shard_map/ppermute | solution.py:277
  46.7 2.0 %collective-permute-start.18 = (bf16[64,512]{1,0:T(8,128)(2,1)S(1)}, bf16[64,512]{1,0:T(8,128)(2,1)S(1)}, u32[]{:S(2)}, u32[]{:S(2)}) collective-permute-start(bf16[64,512]{1,0:T(8,128)(2,1)S(1)} %shard_map.43.refs_0_.first), channel_id=1, source_target_pairs={{0,6},{1,7},{2,4},{3,5},{4,2},{5,3},{6,0},{7,1},{8,14},{9,15},{10,... | collective-permute-start | bytes 196616 | tf_op jit(solution)/shard_map/ppermute | solution.py:277
  48.7 1.3 %shard_map.44 = (f32[256,1024]{1,0:T(8,128)S(1)}, bf16[256,1024]{1,0:T(8,128)(2,1)S(1)}) custom-call(s32[1]{0:T(128)} %bitcast.middle, bf16[512,1024]{1,0:T(8,128)(2,1)S(1)} %get-tuple-element.71.turned, bf16[512,1024]{1,0:T(8,128)(2,1)S(1)} %get-tuple-element.62.beside, bf16[512,1024]{1,0:T(8,128)(2,1)S(1)} %get-tuple-element.63.opposite.swapped), custom_call_target="tpu_custom_call" | custom-call | tf_op jit(solution)/shard_map/pallas_call | solution.py:17
  50.8 3.7 %collective-permute-start.19 = (bf16[256,512]{1,0:T(8,128)(2,1)S(1)}, bf16[256,512]{1,0:T(8,128)(2,1)S(1)}, u32[]{:S(2)}, u32[]{:S(2)}) collective-permute-start(bf16[256,512]{1,0:T(8,128)(2,1)S(1)} %shard_map.45.near), channel_id=1, source_target_pairs={{0,1},{1,0},{2,3},{3,2},{4,5},{5,4},{6,7},{7,6},{8,9},{9,8},{10,11... | collective-permute-start | bytes 786440 | tf_op jit(solution)/shard_map/ppermute | solution.py:277
  55.6 1.8 %shard_map.46 = (bf16[512,1024]{1,0:T(8,128)(2,1)S(1)}, bf16[512,1024]{1,0:T(8,128)(2,1)S(1)}) custom-call(s32[8]{0:T(128)S(1)} %broadcast_xor_fusion.order, s32[1]{0:T(128)} %bitcast.middle, bf16[256,512]{1,0:T(8,128)(2,1)S(1)} %shard_map.45.near, bf16[256,512]{1,0:T(8,128)(2,1)S(1)} %collective-permute-done.19.far, ...), custom_call_target="tpu_custom_call" | custom-call | tf_op jit(solution)/shard_map/pallas_call | solution.py:17
  57.5 1.4 %collective-permute-start.29 = (bf16[512,1024]{1,0:T(8,128)(2,1)S(1)}, bf16[512,1024]{1,0:T(8,128)(2,1)S(1)}, u32[]{:S(2)}, u32[]{:S(2)}) collective-permute-start(bf16[512,1024]{1,0:T(8,128)(2,1)S(1)} %get-tuple-element.69), channel_id=1, source_target_pairs={{8,0},{16,24},{9,1},{17,25},{10,2},{18,26},{11,3},{19,27},{12,4},{... | collective-permute-start | bytes 3145736 | tf_op jit(solution)/shard_map/ppermute | solution.py:358
  58.9 1.4 %shard_map.47 = (bf16[512,1024]{1,0:T(8,128)(2,1)S(1)}, f32[1,1024]{1,0:T(1,128)S(1)}, f32[256,512]{1,0:T(8,128)S(1)}, bf16[256,1024]{1,0:T(8,128)(2,1)S(1)}) custom-call(s32[1]{0:T(128)} %bitcast.middle, bf16[512,1024]{1,0:T(8,128)(2,1)S(1)} %get-tuple-element.71.turned, bf16[256,1024]{1,0:T(8,128)(2,1)S(1)} %get-tuple-element.65.sent_early, ...), custom_call_target="tpu_custom_call" | custom-call | tf_op jit(solution)/shard_map/pallas_call | solution.py:17
  61.1 2.8 %collective-permute-start.31 = (bf16[512,1024]{1,0:T(8,128)(2,1)S(1)}, bf16[512,1024]{1,0:T(8,128)(2,1)S(1)}, u32[]{:S(2)}, u32[]{:S(2)}) collective-permute-start(bf16[512,1024]{1,0:T(8,128)(2,1)S(1)} %get-tuple-element.86), channel_id=1, source_target_pairs={{8,16},{16,8},{9,17},{17,9},{10,18},{18,10},{11,19},{19,11},{12,20... | collective-permute-start | bytes 3145736 | tf_op jit(solution)/shard_map/ppermute | solution.py:358
  66.7 2.6 %shard_map.50.held = f32[512,1024]{1,0:T(8,128)S(1)} custom-call(s32[8]{0:T(128)S(1)} %broadcast_xor_fusion.order, s32[1]{0:T(128)} %bitcast.middle, bf16[256,640]{1,0:T(8,128)(2,1)S(1)} %pad_maximum_fusion.near, bf16[256,640]{1,0:T(8,128)(2,1)S(1)} %collective-permute-done.25.far, bf16[512,1024]{1,0:T(8,128)(2,1)S(1)} %get-tuple-element.79.own, ...), custom_call_target="tpu_custom_call" | custom-call | tf_op jit(solution)/shard_map/pallas_call | solution.py:17
  69.4 2.7 %collective-permute-done.24.c = bf16[64,1024]{1,0:T(8,128)(2,1)S(1)} collective-permute-done((bf16[64,1024]{1,0:T(8,128)(2,1)S(1)}, bf16[64,1024]{1,0:T(8,128)(2,1)S(1)}, u32[]{:S(2)}, u32[]{:S(2)}) %collective-permute-start.24) | collective-permute-done | bytes 131104 | tf_op jit(solution)/shard_map/ppermute | solution.py:277
  72.1 1.4 %collective-permute-start.26 = (bf16[64,1024]{1,0:T(8,128)(2,1)S(1)}, bf16[64,1024]{1,0:T(8,128)(2,1)S(1)}, u32[]{:S(2)}, u32[]{:S(2)}) collective-permute-start(bf16[64,1024]{1,0:T(8,128)(2,1)S(1)} %shard_map.49.refs_0_), channel_id=1, source_target_pairs={{0,2},{1,3},{2,0},{3,1},{4,6},{5,7},{6,4},{7,5},{8,10},{9,11},{10,... | collective-permute-start | bytes 393224 | tf_op jit(solution)/shard_map/ppermute | solution.py:277
  74.8 1.5 %collective-permute-done.26.refs_1_ = bf16[64,1024]{1,0:T(8,128)(2,1)S(1)} collective-permute-done((bf16[64,1024]{1,0:T(8,128)(2,1)S(1)}, bf16[64,1024]{1,0:T(8,128)(2,1)S(1)}, u32[]{:S(2)}, u32[]{:S(2)}) %collective-permute-start.26) | collective-permute-done | bytes 131104 | tf_op jit(solution)/shard_map/ppermute | solution.py:277
  76.3 2.6 %collective-permute-done.27.refs_2_ = bf16[64,1024]{1,0:T(8,128)(2,1)S(1)} collective-permute-done((bf16[64,1024]{1,0:T(8,128)(2,1)S(1)}, bf16[64,1024]{1,0:T(8,128)(2,1)S(1)}, u32[]{:S(2)}, u32[]{:S(2)}) %collective-permute-start.27) | collective-permute-done | bytes 131104 | tf_op jit(solution)/shard_map/ppermute | solution.py:277
  79.1 1.9 %collective-permute-done.29.out = bf16[512,1024]{1,0:T(8,128)(2,1)S(1)} collective-permute-done((bf16[512,1024]{1,0:T(8,128)(2,1)S(1)}, bf16[512,1024]{1,0:T(8,128)(2,1)S(1)}, u32[]{:S(2)}, u32[]{:S(2)}) %collective-permute-start.29) | collective-permute-done | bytes 1048608 | tf_op jit(solution)/shard_map/ppermute | solution.py:358
  81.0 1.4 %collective-permute-start.30 = (bf16[256,1024]{1,0:T(8,128)(2,1)S(1)}, bf16[256,1024]{1,0:T(8,128)(2,1)S(1)}, u32[]{:S(2)}, u32[]{:S(2)}) collective-permute-start(bf16[256,1024]{1,0:T(8,128)(2,1)S(1)} %shard_map.51.near), channel_id=1, source_target_pairs={{0,1},{1,0},{2,3},{3,2},{4,5},{5,4},{6,7},{7,6},{8,9},{9,8},{10,11... | collective-permute-start | bytes 1572872 | tf_op jit(solution)/shard_map/ppermute | solution.py:277
  82.4 4.9 %collective-permute-done.31.over = bf16[512,1024]{1,0:T(8,128)(2,1)S(1)} collective-permute-done((bf16[512,1024]{1,0:T(8,128)(2,1)S(1)}, bf16[512,1024]{1,0:T(8,128)(2,1)S(1)}, u32[]{:S(2)}, u32[]{:S(2)}) %collective-permute-start.31) | collective-permute-done | bytes 1048608 | tf_op jit(solution)/shard_map/ppermute | solution.py:358
  87.3 3.0 %shard_map.52 = f32[512,1024]{1,0:T(8,128)} custom-call(s32[8]{0:T(128)S(1)} %broadcast_xor_fusion.order, s32[1]{0:T(128)} %bitcast.middle, bf16[256,1024]{1,0:T(8,128)(2,1)S(1)} %shard_map.51.near, bf16[256,1024]{1,0:T(8,128)(2,1)S(1)} %collective-permute-done.30.far, bf16[512,1024]{1,0:T(8,128)(2,1)S(1)} %get-tuple-element.62.beside, ...), custom_call_target="tpu_custom_call" | custom-call | tf_op jit(solution)/shard_map/pallas_call | solution.py:17
  (53 shorter events, 22.0 us)
Async XLA Ops:
  1.8 8.5 %collective-permute-start.2 = (f32[2,1024]{1,0:T(2,128)S(1)}, f32[2,1024]{1,0:T(2,128)S(1)}, u32[]{:S(2)}, u32[]{:S(2)}) collective-permute-start(f32[2,1024]{1,0:T(2,128)S(1)} %shard_map.37), channel_id=1, source_target_pairs={{0,24},{8,0},{16,8},{24,16},{1,25},{9,1},{17,9},{25,17},{2,26},{10... | collective-permute-start | bytes 24584 | tf_op jit(solution)/shard_map/ppermute | solution.py:323
  1.9 8.4 %collective-permute-start.1 = (f32[2,1024]{1,0:T(2,128)S(1)}, f32[2,1024]{1,0:T(2,128)S(1)}, u32[]{:S(2)}, u32[]{:S(2)}) collective-permute-start(f32[2,1024]{1,0:T(2,128)S(1)} %shard_map.37), channel_id=1, source_target_pairs={{0,16},{8,24},{16,0},{24,8},{1,17},{9,25},{17,1},{25,9},{2,18},{10... | collective-permute-start | bytes 24584 | tf_op jit(solution)/shard_map/ppermute | solution.py:323
  4.3 6.0 %collective-permute-start = (f32[2,1024]{1,0:T(2,128)S(1)}, f32[2,1024]{1,0:T(2,128)S(1)}, u32[]{:S(2)}, u32[]{:S(2)}) collective-permute-start(f32[2,1024]{1,0:T(2,128)S(1)} %shard_map.37), channel_id=1, source_target_pairs={{0,8},{8,16},{16,24},{24,0},{1,9},{9,17},{17,25},{25,1},{2,10},{10... | collective-permute-start | bytes 24584 | tf_op jit(solution)/shard_map/ppermute | solution.py:323
  6.5 23.4 %collective-permute-start.10 = (bf16[512,1024]{1,0:T(8,128)(2,1)}, bf16[512,1024]{1,0:T(8,128)(2,1)S(1)}, u32[]{:S(2)}, u32[]{:S(2)}) collective-permute-start(bf16[512,1024]{1,0:T(8,128)(2,1)} %z.5), channel_id=1, source_target_pairs={{0,8},{8,0},{16,24},{24,16},{1,9},{9,1},{17,25},{25,17},{2,10},{10... | collective-permute-start | bytes 3145736 | tf_op jit(solution)/shard_map/ppermute | solution.py:326
  6.5 25.3 %collective-permute-start.11 = (bf16[512,1024]{1,0:T(8,128)(2,1)}, bf16[512,1024]{1,0:T(8,128)(2,1)}, u32[]{:S(2)}, u32[]{:S(2)}) collective-permute-start(bf16[512,1024]{1,0:T(8,128)(2,1)} %z.5), channel_id=1, source_target_pairs={{8,16},{16,8},{9,17},{17,9},{10,18},{18,10},{11,19},{19,11},{12,20... | collective-permute-start | bytes 3145736 | tf_op jit(solution)/shard_map/ppermute | solution.py:327
  12.7 3.1 %collective-permute-start.3 = (bf16[256,640]{1,0:T(8,128)(2,1)S(1)}, bf16[256,640]{1,0:T(8,128)(2,1)S(1)}, u32[]{:S(2)}, u32[]{:S(2)}) collective-permute-start(bf16[256,640]{1,0:T(8,128)(2,1)S(1)} %get-tuple-element.48), channel_id=1, source_target_pairs={{0,1},{1,0},{2,3},{3,2},{4,5},{5,4},{6,7},{7,6},{8,9},{9,8},{10,11... | collective-permute-start | bytes 983048 | tf_op jit(solution)/shard_map/ppermute | solution.py:277
  16.0 3.8 %collective-permute-start.4 = (bf16[64,640]{1,0:T(8,128)(2,1)S(1)}, bf16[64,640]{1,0:T(8,128)(2,1)S(1)}, u32[]{:S(2)}, u32[]{:S(2)}) collective-permute-start(bf16[64,640]{1,0:T(8,128)(2,1)S(1)} %get-tuple-element.50), channel_id=1, source_target_pairs={{0,2},{1,3},{2,0},{3,1},{4,6},{5,7},{6,4},{7,5},{8,10},{9,11},{10,... | collective-permute-start | bytes 245768 | tf_op jit(solution)/shard_map/ppermute | solution.py:277
  17.3 3.7 %collective-permute-start.5 = (bf16[64,640]{1,0:T(8,128)(2,1)S(1)}, bf16[64,640]{1,0:T(8,128)(2,1)S(1)}, u32[]{:S(2)}, u32[]{:S(2)}) collective-permute-start(bf16[64,640]{1,0:T(8,128)(2,1)S(1)} %get-tuple-element.51), channel_id=1, source_target_pairs={{0,4},{1,5},{2,6},{3,7},{4,0},{5,1},{6,2},{7,3},{8,12},{9,13},{10,... | collective-permute-start | bytes 245768 | tf_op jit(solution)/shard_map/ppermute | solution.py:277
  18.5 4.2 %collective-permute-start.6 = (bf16[64,640]{1,0:T(8,128)(2,1)S(1)}, bf16[64,640]{1,0:T(8,128)(2,1)S(1)}, u32[]{:S(2)}, u32[]{:S(2)}) collective-permute-start(bf16[64,640]{1,0:T(8,128)(2,1)S(1)} %get-tuple-element.52), channel_id=1, source_target_pairs={{0,6},{1,7},{2,4},{3,5},{4,2},{5,3},{6,0},{7,1},{8,14},{9,15},{10,... | collective-permute-start | bytes 245768 | tf_op jit(solution)/shard_map/ppermute | solution.py:277
  22.8 4.4 %collective-permute-start.9 = (bf16[64,640]{1,0:T(8,128)(2,1)S(1)}, bf16[64,640]{1,0:T(8,128)(2,1)S(1)}, u32[]{:S(2)}, u32[]{:S(2)}) collective-permute-start(bf16[64,640]{1,0:T(8,128)(2,1)S(1)} %shard_map.40), channel_id=1, source_target_pairs={{0,6},{1,7},{2,4},{3,5},{4,2},{5,3},{6,0},{7,1},{8,14},{9,15},{10,... | collective-permute-start | bytes 245768 | tf_op jit(solution)/shard_map/ppermute | solution.py:277
  23.4 4.6 %collective-permute-start.8 = (bf16[64,640]{1,0:T(8,128)(2,1)S(1)}, bf16[64,640]{1,0:T(8,128)(2,1)S(1)}, u32[]{:S(2)}, u32[]{:S(2)}) collective-permute-start(bf16[64,640]{1,0:T(8,128)(2,1)S(1)} %shard_map.40), channel_id=1, source_target_pairs={{0,4},{1,5},{2,6},{3,7},{4,0},{5,1},{6,2},{7,3},{8,12},{9,13},{10,... | collective-permute-start | bytes 245768 | tf_op jit(solution)/shard_map/ppermute | solution.py:277
  24.6 3.7 %collective-permute-start.7 = (bf16[64,640]{1,0:T(8,128)(2,1)S(1)}, bf16[64,640]{1,0:T(8,128)(2,1)S(1)}, u32[]{:S(2)}, u32[]{:S(2)}) collective-permute-start(bf16[64,640]{1,0:T(8,128)(2,1)S(1)} %shard_map.40), channel_id=1, source_target_pairs={{0,2},{1,3},{2,0},{3,1},{4,6},{5,7},{6,4},{7,5},{8,10},{9,11},{10,... | collective-permute-start | bytes 245768 | tf_op jit(solution)/shard_map/ppermute | solution.py:277
  31.9 27.0 %collective-permute-start.20 = (bf16[512,1024]{1,0:T(8,128)(2,1)}, bf16[512,1024]{1,0:T(8,128)(2,1)}, u32[]{:S(2)}, u32[]{:S(2)}) collective-permute-start(bf16[512,1024]{1,0:T(8,128)(2,1)} %z.5), channel_id=1, source_target_pairs={{0,24},{24,0},{1,25},{25,1},{2,26},{26,2},{3,27},{27,3},{4,28},{28... | collective-permute-start | bytes 3145736 | tf_op jit(solution)/shard_map/ppermute | solution.py:342
  35.7 3.7 %collective-permute-start.12 = (bf16[256,512]{1,0:T(8,128)(2,1)S(1)}, bf16[256,512]{1,0:T(8,128)(2,1)S(1)}, u32[]{:S(2)}, u32[]{:S(2)}) collective-permute-start(bf16[256,512]{1,0:T(8,128)(2,1)S(1)} %get-tuple-element.56), channel_id=1, source_target_pairs={{0,1},{1,0},{2,3},{3,2},{4,5},{5,4},{6,7},{7,6},{8,9},{9,8},{10,11... | collective-permute-start | bytes 786440 | tf_op jit(solution)/shard_map/ppermute | solution.py:277
  39.5 3.2 %collective-permute-start.13 = (bf16[64,512]{1,0:T(8,128)(2,1)S(1)}, bf16[64,512]{1,0:T(8,128)(2,1)S(1)}, u32[]{:S(2)}, u32[]{:S(2)}) collective-permute-start(bf16[64,512]{1,0:T(8,128)(2,1)S(1)} %get-tuple-element.58), channel_id=1, source_target_pairs={{0,2},{1,3},{2,0},{3,1},{4,6},{5,7},{6,4},{7,5},{8,10},{9,11},{10,... | collective-permute-start | bytes 196616 | tf_op jit(solution)/shard_map/ppermute | solution.py:277
  40.7 3.1 %collective-permute-start.14 = (bf16[64,512]{1,0:T(8,128)(2,1)S(1)}, bf16[64,512]{1,0:T(8,128)(2,1)S(1)}, u32[]{:S(2)}, u32[]{:S(2)}) collective-permute-start(bf16[64,512]{1,0:T(8,128)(2,1)S(1)} %get-tuple-element.59), channel_id=1, source_target_pairs={{0,4},{1,5},{2,6},{3,7},{4,0},{5,1},{6,2},{7,3},{8,12},{9,13},{10,... | collective-permute-start | bytes 196616 | tf_op jit(solution)/shard_map/ppermute | solution.py:277
  42.0 4.0 %collective-permute-start.15 = (bf16[64,512]{1,0:T(8,128)(2,1)S(1)}, bf16[64,512]{1,0:T(8,128)(2,1)S(1)}, u32[]{:S(2)}, u32[]{:S(2)}) collective-permute-start(bf16[64,512]{1,0:T(8,128)(2,1)S(1)} %get-tuple-element.60), channel_id=1, source_target_pairs={{0,6},{1,7},{2,4},{3,5},{4,2},{5,3},{6,0},{7,1},{8,14},{9,15},{10,... | collective-permute-start | bytes 196616 | tf_op jit(solution)/shard_map/ppermute | solution.py:277
  46.0 4.0 %collective-permute-start.16 = (bf16[64,512]{1,0:T(8,128)(2,1)S(1)}, bf16[64,512]{1,0:T(8,128)(2,1)S(1)}, u32[]{:S(2)}, u32[]{:S(2)}) collective-permute-start(bf16[64,512]{1,0:T(8,128)(2,1)S(1)} %shard_map.43.refs_0_.first), channel_id=1, source_target_pairs={{0,2},{1,3},{2,0},{3,1},{4,6},{5,7},{6,4},{7,5},{8,10},{9,11},{10,... | collective-permute-start | bytes 196616 | tf_op jit(solution)/shard_map/ppermute | solution.py:277
  46.4 3.6 %collective-permute-start.17 = (bf16[64,512]{1,0:T(8,128)(2,1)S(1)}, bf16[64,512]{1,0:T(8,128)(2,1)S(1)}, u32[]{:S(2)}, u32[]{:S(2)}) collective-permute-start(bf16[64,512]{1,0:T(8,128)(2,1)S(1)} %shard_map.43.refs_0_.first), channel_id=1, source_target_pairs={{0,4},{1,5},{2,6},{3,7},{4,0},{5,1},{6,2},{7,3},{8,12},{9,13},{10,... | collective-permute-start | bytes 196616 | tf_op jit(solution)/shard_map/ppermute | solution.py:277
  46.7 4.0 %collective-permute-start.18 = (bf16[64,512]{1,0:T(8,128)(2,1)S(1)}, bf16[64,512]{1,0:T(8,128)(2,1)S(1)}, u32[]{:S(2)}, u32[]{:S(2)}) collective-permute-start(bf16[64,512]{1,0:T(8,128)(2,1)S(1)} %shard_map.43.refs_0_.first), channel_id=1, source_target_pairs={{0,6},{1,7},{2,4},{3,5},{4,2},{5,3},{6,0},{7,1},{8,14},{9,15},{10,... | collective-permute-start | bytes 196616 | tf_op jit(solution)/shard_map/ppermute | solution.py:277
  50.8 4.9 %collective-permute-start.19 = (bf16[256,512]{1,0:T(8,128)(2,1)S(1)}, bf16[256,512]{1,0:T(8,128)(2,1)S(1)}, u32[]{:S(2)}, u32[]{:S(2)}) collective-permute-start(bf16[256,512]{1,0:T(8,128)(2,1)S(1)} %shard_map.45.near), channel_id=1, source_target_pairs={{0,1},{1,0},{2,3},{3,2},{4,5},{5,4},{6,7},{7,6},{8,9},{9,8},{10,11... | collective-permute-start | bytes 786440 | tf_op jit(solution)/shard_map/ppermute | solution.py:277
  57.5 23.5 %collective-permute-start.29 = (bf16[512,1024]{1,0:T(8,128)(2,1)S(1)}, bf16[512,1024]{1,0:T(8,128)(2,1)S(1)}, u32[]{:S(2)}, u32[]{:S(2)}) collective-permute-start(bf16[512,1024]{1,0:T(8,128)(2,1)S(1)} %get-tuple-element.69), channel_id=1, source_target_pairs={{8,0},{16,24},{9,1},{17,25},{10,2},{18,26},{11,3},{19,27},{12,4},{... | collective-permute-start | bytes 3145736 | tf_op jit(solution)/shard_map/ppermute | solution.py:358
  60.3 3.6 %collective-permute-start.21 = (bf16[256,1024]{1,0:T(8,128)(2,1)S(1)}, bf16[256,1024]{1,0:T(8,128)(2,1)S(1)}, u32[]{:S(2)}, u32[]{:S(2)}) collective-permute-start(bf16[256,1024]{1,0:T(8,128)(2,1)S(1)} %get-tuple-element.74), channel_id=1, source_target_pairs={{0,1},{1,0},{2,3},{3,2},{4,5},{5,4},{6,7},{7,6},{8,9},{9,8},{10,11... | collective-permute-start | bytes 1572872 | tf_op jit(solution)/shard_map/ppermute | solution.py:277
  61.0 5.5 %collective-permute-start.25 = (bf16[256,640]{1,0:T(8,128)(2,1)S(1)}, bf16[256,640]{1,0:T(8,128)(2,1)S(1)}, u32[]{:S(2)}, u32[]{:S(2)}) collective-permute-start(bf16[256,640]{1,0:T(8,128)(2,1)S(1)} %pad_maximum_fusion.near), channel_id=1, source_target_pairs={{0,1},{1,0},{2,3},{3,2},{4,5},{5,4},{6,7},{7,6},{8,9},{9,8},{10,11... | collective-permute-start | bytes 983048 | tf_op jit(solution)/shard_map/ppermute | solution.py:277
  61.1 26.2 %collective-permute-start.31 = (bf16[512,1024]{1,0:T(8,128)(2,1)S(1)}, bf16[512,1024]{1,0:T(8,128)(2,1)S(1)}, u32[]{:S(2)}, u32[]{:S(2)}) collective-permute-start(bf16[512,1024]{1,0:T(8,128)(2,1)S(1)} %get-tuple-element.86), channel_id=1, source_target_pairs={{8,16},{16,8},{9,17},{17,9},{10,18},{18,10},{11,19},{19,11},{12,20... | collective-permute-start | bytes 3145736 | tf_op jit(solution)/shard_map/ppermute | solution.py:358
  64.0 5.3 %collective-permute-start.22 = (bf16[64,1024]{1,0:T(8,128)(2,1)S(1)}, bf16[64,1024]{1,0:T(8,128)(2,1)S(1)}, u32[]{:S(2)}, u32[]{:S(2)}) collective-permute-start(bf16[64,1024]{1,0:T(8,128)(2,1)S(1)} %get-tuple-element.76), channel_id=1, source_target_pairs={{0,2},{1,3},{2,0},{3,1},{4,6},{5,7},{6,4},{7,5},{8,10},{9,11},{10,... | collective-permute-start | bytes 393224 | tf_op jit(solution)/shard_map/ppermute | solution.py:277
  65.3 4.1 %collective-permute-start.23 = (bf16[64,1024]{1,0:T(8,128)(2,1)S(1)}, bf16[64,1024]{1,0:T(8,128)(2,1)S(1)}, u32[]{:S(2)}, u32[]{:S(2)}) collective-permute-start(bf16[64,1024]{1,0:T(8,128)(2,1)S(1)} %get-tuple-element.77), channel_id=1, source_target_pairs={{0,4},{1,5},{2,6},{3,7},{4,0},{5,1},{6,2},{7,3},{8,12},{9,13},{10,... | collective-permute-start | bytes 393224 | tf_op jit(solution)/shard_map/ppermute | solution.py:277
  66.5 5.5 %collective-permute-start.24 = (bf16[64,1024]{1,0:T(8,128)(2,1)S(1)}, bf16[64,1024]{1,0:T(8,128)(2,1)S(1)}, u32[]{:S(2)}, u32[]{:S(2)}) collective-permute-start(bf16[64,1024]{1,0:T(8,128)(2,1)S(1)} %get-tuple-element.78), channel_id=1, source_target_pairs={{0,6},{1,7},{2,4},{3,5},{4,2},{5,3},{6,0},{7,1},{8,14},{9,15},{10,... | collective-permute-start | bytes 393224 | tf_op jit(solution)/shard_map/ppermute | solution.py:277
  72.1 4.2 %collective-permute-start.26 = (bf16[64,1024]{1,0:T(8,128)(2,1)S(1)}, bf16[64,1024]{1,0:T(8,128)(2,1)S(1)}, u32[]{:S(2)}, u32[]{:S(2)}) collective-permute-start(bf16[64,1024]{1,0:T(8,128)(2,1)S(1)} %shard_map.49.refs_0_), channel_id=1, source_target_pairs={{0,2},{1,3},{2,0},{3,1},{4,6},{5,7},{6,4},{7,5},{8,10},{9,11},{10,... | collective-permute-start | bytes 393224 | tf_op jit(solution)/shard_map/ppermute | solution.py:277
  73.6 5.4 %collective-permute-start.27 = (bf16[64,1024]{1,0:T(8,128)(2,1)S(1)}, bf16[64,1024]{1,0:T(8,128)(2,1)S(1)}, u32[]{:S(2)}, u32[]{:S(2)}) collective-permute-start(bf16[64,1024]{1,0:T(8,128)(2,1)S(1)} %shard_map.49.refs_0_), channel_id=1, source_target_pairs={{0,4},{1,5},{2,6},{3,7},{4,0},{5,1},{6,2},{7,3},{8,12},{9,13},{10,... | collective-permute-start | bytes 393224 | tf_op jit(solution)/shard_map/ppermute | solution.py:277
  73.8 5.3 %collective-permute-start.28 = (bf16[64,1024]{1,0:T(8,128)(2,1)S(1)}, bf16[64,1024]{1,0:T(8,128)(2,1)S(1)}, u32[]{:S(2)}, u32[]{:S(2)}) collective-permute-start(bf16[64,1024]{1,0:T(8,128)(2,1)S(1)} %shard_map.49.refs_0_), channel_id=1, source_target_pairs={{0,6},{1,7},{2,4},{3,5},{4,2},{5,3},{6,0},{7,1},{8,14},{9,15},{10,... | collective-permute-start | bytes 393224 | tf_op jit(solution)/shard_map/ppermute | solution.py:277
  81.0 6.3 %collective-permute-start.30 = (bf16[256,1024]{1,0:T(8,128)(2,1)S(1)}, bf16[256,1024]{1,0:T(8,128)(2,1)S(1)}, u32[]{:S(2)}, u32[]{:S(2)}) collective-permute-start(bf16[256,1024]{1,0:T(8,128)(2,1)S(1)} %shard_map.51.near), channel_id=1, source_target_pairs={{0,1},{1,0},{2,3},{3,2},{4,5},{5,4},{6,7},{7,6},{8,9},{9,8},{10,11... | collective-permute-start | bytes 1572872 | tf_op jit(solution)/shard_map/ppermute | solution.py:277
  (1 other events, 7.8 us)

commit v20 on v19

--- a/solution.py
+++ b/solution.py
@@ -11,14 +11,16 @@
 NORM = 128
 
 
-def kernel_call(body, outs, smem=0, scratch=4, temps=(), sems=0):
+def kernel_call(body, outs, smem=0, scratch=4, temps=(), sems=0, out=pltpu.VMEM, outside=None):
     def call(*args):
         space = [pltpu.SMEM] * smem + [pltpu.VMEM] * (len(args) - smem)
+        if outside is not None:
+            space[outside] = pl.ANY
         return pl.pallas_call(
             body,
             out_shape=[jax.ShapeDtypeStruct(s, t) for s, t in outs],
             in_specs=[pl.BlockSpec(memory_space=m) for m in space],
-            out_specs=[pl.BlockSpec(memory_space=pl.ANY if sems else pltpu.VMEM) for _ in outs],
+            out_specs=[pl.BlockSpec(memory_space=out) for _ in outs],
             scratch_shapes=[pltpu.VMEM(s, t) for s, t in temps]
             + ([pltpu.SemaphoreType.DMA((sems,))] if sems else []),
             compiler_params=pltpu.CompilerParams(vmem_limit_bytes=scratch * 1024 * 1024),
@@ -48,6 +50,28 @@
     out[...] = (block[...].astype(jnp.float32) - mean).astype(jnp.bfloat16)
     wide = out[...].astype(jnp.float32)
     square[...] = jnp.sum(wide * wide, axis=0, keepdims=True)
+
+
+def pieces_in(source, landed, sem):
+    rows = landed.shape[0] // 4
+    return [
+        pltpu.make_async_copy(
+            source.at[k * rows:(k + 1) * rows], landed.at[k * rows:(k + 1) * rows], sem.at[k]
+        )
+        for k in range(4)
+    ]
+
+
+def centered_pieces(out, copies, landed, mean, square):
+    rows, total = landed.shape[0] // 4, 0.0
+    for k, copy in enumerate(copies):
+        copy.wait()
+        here = slice(k * rows, (k + 1) * rows)
+        block = (landed[here, :].astype(jnp.float32) - mean).astype(jnp.bfloat16)
+        out[here, :] = block
+        wide = block.astype(jnp.float32)
+        total = total + jnp.sum(wide * wide, axis=0, keepdims=True)
+    square[...] = total
 
 
 def high_low(n, like):
@@ -93,18 +117,22 @@
 
 def first_kernel(
     order, middle, turned, beside_in, opposite_in, mean,
-    beside, beside_square, opposite, opposite_square, kept, sent, turned_beside,
+    beside, beside_square, opposite, opposite_square, kept, sent, turned_beside, landed, sem,
 ):
-    centered_into(beside, beside_in, mean[...], beside_square)
+    copies = pieces_in(opposite_in, landed, sem)
 
     @pl.when(middle[0] == 1)
     def _():
-        centered_into(opposite, opposite_in, mean[...], opposite_square)
+        for copy in copies:
+            copy.start()
+        centered_into(beside, beside_in, mean[...], beside_square)
         turn_into(turned_beside, order, beside)
+        centered_pieces(opposite, copies, landed, mean[...], opposite_square)
         split_sum(gram(turned_beside[...], opposite[...]), kept, sent, slice(None))
 
     @pl.when(middle[0] == 0)
     def _():
+        centered_into(beside, beside_in, mean[...], beside_square)
         split_sum(gram(turned[...], beside[...]), kept, sent, slice(None))
 
 
@@ -117,7 +145,9 @@
         split_sum(gram(turned[...], beside[...]), kept, sent, slice(rows, 2 * rows))
 
 
-def late_kernel(middle, turned, sent_early, end_in, mean, end, square, kept, sent):
+def late_kernel(
+    middle, turned, sent_early, end_in, mean, end, square, kept, sent, landed, sem
+):
     rows = end.shape[0]
 
     @pl.when(middle[0] == 1)
@@ -126,7 +156,10 @@
 
     @pl.when(middle[0] == 0)
     def _():
-        centered_into(end, end_in, mean[...], square)
+        copies = pieces_in(end_in, landed, sem)
+        for copy in copies:
+            copy.start()
+        centered_pieces(end, copies, landed, mean[...], square)
         split_sum(gram(turned[...], end[...]), kept, sent, slice(0, rows))
         sent[:, rows:] = jnp.zeros_like(sent[:, rows:])
 
@@ -343,23 +376,25 @@
 
     beside, beside_square, swapped, swapped_square, kept, sent = kernel_call(
         first_kernel, [block, flat, block, flat, *summands(rows)],
-        smem=2, scratch=12, temps=[block],
+        smem=2, scratch=12, temps=[block, block], sems=4, outside=4,
     )(order, middle, after(turned, near_own), beside_in, swapped, mean)
     first = scatter(*halve(kept, sent))
     kept_early, sent_early = kernel_call(
         early_kernel, summands(2 * rows), smem=1, scratch=12
     )(middle, after(turned, first), beside, swapped)
+    far_own = to_partner(near_own, 1)
     near = after(gather_chips(first), sent_early)
     ready = kernel_call(
         push_kernel, [block, block], smem=2, scratch=12, temps=[((rows, rows), jnp.bfloat16)]
-    )(order, middle, near, to_partner(near, 1), beside, swapped, beside_square, swapped_square)
+    )(order, middle, near, after(to_partner(near, 1), far_own), beside, swapped, beside_square, swapped_square)
     out, over = ready
     pushed = [
         lax.ppermute(out, "dp", outward), lax.ppermute(after(over, end), "dp", across)
     ]
 
     end, end_square, kept, sent = kernel_call(
-        late_kernel, [block, flat, summands(rows)[0], summands(2 * rows)[1]], smem=1, scratch=12
+        late_kernel, [block, flat, summands(rows)[0], summands(2 * rows)[1]],
+        smem=1, scratch=12, temps=[block], sems=4, outside=3,
     )(middle, after(turned, *ready), sent_early, end, mean)
     eighth = (rows // 8, 2 * rows)
     halved = kernel_call(
@@ -370,7 +405,7 @@
         functools.partial(held_kernel, total), [result],
         smem=2, scratch=12, temps=[((rows, rows + NORM), jnp.bfloat16)],
     )(
-        order, middle, near_own, to_partner(near_own, 1), own, z_anchor, z_other,
+        order, middle, near_own, far_own, own, z_anchor, z_other,
         own_square, beside_square, swapped_square, after(end_square, halved[0]), mean, spread,
     )[0]
     got = [to_partner(x, 2 * k) for k, x in enumerate(halved[1:], 1)]
@@ -380,7 +415,7 @@
     near = after(gather_chips(after(second, held)), pushed[0])
     return kernel_call(
         functools.partial(last_kernel, total), [result],
-        smem=2, scratch=12, temps=[((rows, 2 * rows), jnp.bfloat16), result], sems=4,
+        smem=2, scratch=12, temps=[((rows, 2 * rows), jnp.bfloat16), result], sems=4, out=pl.ANY,
     )(
         order, middle, near, to_partner(near, 1), beside, swapped, end, held, *pushed
     )[0]

time: 91.3 us -> 92.5 us (1.013)
  waiting for transfers between devices: 32.1 us -> 34.2 us
    ppermute x1, waiting for transfers between devices: 1.89 us -> 4.9 us  [by_line(): swapped = lax.ppermute(ahead, 'dp', across)]
    ppermute x1, waiting for transfers between devices: 1.89 us -> 4.06 us  [by_line(): lax.ppermute(out, 'dp', outward)]
    ppermute x1, waiting for transfers between devices: 1.64 us -> 0.1 us  [by_line(): beside_in = lax.ppermute(ahead, 'dp', [(i, i ^ 1) for i in range(4)])]
    ppermute x1, starting transfers between devices: 1.44 us -> 2.94 us  [by_line(): lax.ppermute(out, 'dp', outward)]
    ppermute x1, starting transfers between devices: 3.08 us -> 1.91 us  [by_line(): swapped = lax.ppermute(ahead, 'dp', across)]
  transfers between devices with their start and end apart: 32 -> 32, of which waited for: 22 -> 21; matrix products, arithmetic and copies ran while one was open for 1% -> 1% of each run, Pallas kernels for 13% -> 13%
where the time goes in v20:
time: 92.5 us; the launch traced here: 91.4 us
  starting transfers between devices  39.9 us (43%)
  waiting for transfers between devices  34.2 us (37%)
  Pallas kernels  16.3 us (18%)
    ppermute x24, starting transfers between devices, to_partner(): return lax.ppermute(x, 'feat', [(i, i ^ step) for i in range(8)])  26.8 us
    ppermute x24, waiting for transfers between devices, to_partner(): return lax.ppermute(x, 'feat', [(i, i ^ step) for i in range(8)])  21.1 us
    pallas_call x16, Pallas kernels, call(): pl.pallas_call(body, out_shape=[jax.ShapeDtypeStruct(s, t) for s, t in ou...  16.3 us
    ppermute x1, waiting for transfers between devices, by_line(): swapped = lax.ppermute(ahead, 'dp', across)  4.9 us
    ppermute x3, starting transfers between devices, by_line(): lax.ppermute(stats, 'dp', [(i, (i + k) % 4) for i in range(4)])  4.72 us
    ppermute x1, waiting for transfers between devices, by_line(): lax.ppermute(out, 'dp', outward)  4.06 us
    ppermute x1, waiting for transfers between devices, by_line(): lax.ppermute(after(over, end), 'dp', across)  4.04 us
    ppermute x1, starting transfers between devices, by_line(): lax.ppermute(out, 'dp', outward)  2.94 us
  transfers between devices with their start and end apart: 32, of which 21 were waited for; matrix products, arithmetic and copies ran while one was open for 1% of the time, Pallas kernels for 13%

profile of v20, /device:TPU:9, one launch (start us, length us, event | category | flops | bytes accessed | tf_op | source)
XLA Modules:
  0.0 91.4 jit_solution(7982122563764083375)
XLA Ops:
  0.0 1.8 %shard_map.37 = f32[2,1024]{1,0:T(2,128)S(1)} custom-call(bf16[512,1024]{1,0:T(8,128)(2,1)} %z.5), custom_call_target="tpu_custom_call" | custom-call | tf_op jit(solution)/shard_map/pallas_call | solution.py:19
  1.9 2.5 %collective-permute-start.1 = (f32[2,1024]{1,0:T(2,128)S(1)}, f32[2,1024]{1,0:T(2,128)S(1)}, u32[]{:S(2)}, u32[]{:S(2)}) collective-permute-start(f32[2,1024]{1,0:T(2,128)S(1)} %shard_map.37), channel_id=1, source_target_pairs={{0,16},{8,24},{16,0},{24,8},{1,17},{9,25},{17,1},{25,9},{2,18},{10... | collective-permute-start | bytes 24584 | tf_op jit(solution)/shard_map/ppermute | solution.py:356
  4.3 2.2 %collective-permute-start = (f32[2,1024]{1,0:T(2,128)S(1)}, f32[2,1024]{1,0:T(2,128)S(1)}, u32[]{:S(2)}, u32[]{:S(2)}) collective-permute-start(f32[2,1024]{1,0:T(2,128)S(1)} %shard_map.37), channel_id=1, source_target_pairs={{0,8},{8,16},{16,24},{24,0},{1,9},{9,17},{17,25},{25,1},{2,10},{10... | collective-permute-start | bytes 24584 | tf_op jit(solution)/shard_map/ppermute | solution.py:356
  6.5 1.9 %collective-permute-start.11 = (bf16[512,1024]{1,0:T(8,128)(2,1)}, bf16[512,1024]{1,0:T(8,128)(2,1)S(1)}, u32[]{:S(2)}, u32[]{:S(2)}) collective-permute-start(bf16[512,1024]{1,0:T(8,128)(2,1)} %z.5), channel_id=1, source_target_pairs={{8,16},{16,8},{9,17},{17,9},{10,18},{18,10},{11,19},{19,11},{12,20... | collective-permute-start | bytes 3145736 | tf_op jit(solution)/shard_map/ppermute | solution.py:360
  9.3 2.4 %shard_map.38 = (bf16[512,1024]{1,0:T(8,128)(2,1)S(1)}, bf16[512,1024]{1,0:T(8,128)(2,1)S(1)}, f32[1,1024]{1,0:T(1,128)S(1)}, f32[256,640]{1,0:T(8,128)S(1)}, bf16[256,640]{1,0:T(8,128)(2,1)S(1)}) custom-call(s32[8]{0:T(128)S(1)} %broadcast_xor_fusion.order, bf16[512,1024]{1,0:T(8,128)(2,1)} %z.5, f32[1,1024]{1,0:T(1,128)S(1)} %get-tuple-element.90.mean), custom_call_target="tpu_custom_call" | custom-call | tf_op jit(solution)/shard_map/pallas_call | solution.py:19
  11.6 1.6 %collective-permute-start.3 = (bf16[256,640]{1,0:T(8,128)(2,1)S(1)}, bf16[256,640]{1,0:T(8,128)(2,1)S(1)}, u32[]{:S(2)}, u32[]{:S(2)}) collective-permute-start(bf16[256,640]{1,0:T(8,128)(2,1)S(1)} %get-tuple-element.49), channel_id=1, source_target_pairs={{0,1},{1,0},{2,3},{3,2},{4,5},{5,4},{6,7},{7,6},{8,9},{9,8},{10,11... | collective-permute-start | bytes 983048 | tf_op jit(solution)/shard_map/ppermute | solution.py:310
  13.2 1.3 %collective-permute-done.3.got = bf16[256,640]{1,0:T(8,128)(2,1)S(1)} collective-permute-done((bf16[256,640]{1,0:T(8,128)(2,1)S(1)}, bf16[256,640]{1,0:T(8,128)(2,1)S(1)}, u32[]{:S(2)}, u32[]{:S(2)}) %collective-permute-start.3) | collective-permute-done | bytes 327712 | tf_op jit(solution)/shard_map/ppermute | solution.py:310
  14.6 1.3 %collective-permute-start.4 = (bf16[64,640]{1,0:T(8,128)(2,1)S(1)}, bf16[64,640]{1,0:T(8,128)(2,1)S(1)}, u32[]{:S(2)}, u32[]{:S(2)}) collective-permute-start(bf16[64,640]{1,0:T(8,128)(2,1)S(1)} %get-tuple-element.51), channel_id=1, source_target_pairs={{0,2},{1,3},{2,0},{3,1},{4,6},{5,7},{6,4},{7,5},{8,10},{9,11},{10,... | collective-permute-start | bytes 245768 | tf_op jit(solution)/shard_map/ppermute | solution.py:310
  19.6 1.7 %collective-permute-done.6.c = bf16[64,640]{1,0:T(8,128)(2,1)S(1)} collective-permute-done((bf16[64,640]{1,0:T(8,128)(2,1)S(1)}, bf16[64,640]{1,0:T(8,128)(2,1)S(1)}, u32[]{:S(2)}, u32[]{:S(2)}) %collective-permute-start.6) | collective-permute-done | bytes 81952 | tf_op jit(solution)/shard_map/ppermute | solution.py:310
  24.2 1.6 %collective-permute-done.9 = bf16[64,640]{1,0:T(8,128)(2,1)S(1)} collective-permute-done((bf16[64,640]{1,0:T(8,128)(2,1)S(1)}, bf16[64,640]{1,0:T(8,128)(2,1)S(1)}, u32[]{:S(2)}, u32[]{:S(2)}) %collective-permute-start.9) | collective-permute-done | bytes 81952 | tf_op jit(solution)/shard_map/ppermute | solution.py:310
  27.0 4.9 %collective-permute-done.11.opposite_in = bf16[512,1024]{1,0:T(8,128)(2,1)S(1)} collective-permute-done((bf16[512,1024]{1,0:T(8,128)(2,1)}, bf16[512,1024]{1,0:T(8,128)(2,1)S(1)}, u32[]{:S(2)}, u32[]{:S(2)}) %collective-permute-start.11) | collective-permute-done | bytes 1048608 | tf_op jit(solution)/shard_map/ppermute | solution.py:360
  32.0 1.6 %collective-permute-start.21 = (bf16[512,1024]{1,0:T(8,128)(2,1)}, bf16[512,1024]{1,0:T(8,128)(2,1)}, u32[]{:S(2)}, u32[]{:S(2)}) collective-permute-start(bf16[512,1024]{1,0:T(8,128)(2,1)} %z.5), channel_id=1, source_target_pairs={{0,24},{24,0},{1,25},{25,1},{2,26},{26,2},{3,27},{27,3},{4,28},{28... | collective-permute-start | bytes 3145736 | tf_op jit(solution)/shard_map/ppermute | solution.py:375
  33.6 2.7 %shard_map.41 = (bf16[512,1024]{1,0:T(8,128)(2,1)S(1)}, f32[1,1024]{1,0:T(1,128)S(1)}, bf16[512,1024]{1,0:T(8,128)(2,1)S(1)}, f32[1,1024]{1,0:T(1,128)S(1)}, f32...) custom-call(s32[8]{0:T(128)S(1)} %broadcast_xor_fusion.order, s32[1]{0:T(128)} %bitcast.middle, ...), custom_call_target="tpu_custom_call" | custom-call | tf_op jit(solution)/shard_map/pallas_call | solution.py:19
  36.3 2.5 %collective-permute-start.12 = (bf16[256,512]{1,0:T(8,128)(2,1)S(1)}, bf16[256,512]{1,0:T(8,128)(2,1)S(1)}, u32[]{:S(2)}, u32[]{:S(2)}) collective-permute-start(bf16[256,512]{1,0:T(8,128)(2,1)S(1)} %get-tuple-element.57), channel_id=1, source_target_pairs={{0,1},{1,0},{2,3},{3,2},{4,5},{5,4},{6,7},{7,6},{8,9},{9,8},{10,11... | collective-permute-start | bytes 786440 | tf_op jit(solution)/shard_map/ppermute | solution.py:310
  40.1 1.3 %collective-permute-start.13 = (bf16[64,512]{1,0:T(8,128)(2,1)S(1)}, bf16[64,512]{1,0:T(8,128)(2,1)S(1)}, u32[]{:S(2)}, u32[]{:S(2)}) collective-permute-start(bf16[64,512]{1,0:T(8,128)(2,1)S(1)} %get-tuple-element.59), channel_id=1, source_target_pairs={{0,2},{1,3},{2,0},{3,1},{4,6},{5,7},{6,4},{7,5},{8,10},{9,11},{10,... | collective-permute-start | bytes 196616 | tf_op jit(solution)/shard_map/ppermute | solution.py:310
  41.4 1.2 %collective-permute-start.14 = (bf16[64,512]{1,0:T(8,128)(2,1)S(1)}, bf16[64,512]{1,0:T(8,128)(2,1)S(1)}, u32[]{:S(2)}, u32[]{:S(2)}) collective-permute-start(bf16[64,512]{1,0:T(8,128)(2,1)S(1)} %get-tuple-element.60), channel_id=1, source_target_pairs={{0,4},{1,5},{2,6},{3,7},{4,0},{5,1},{6,2},{7,3},{8,12},{9,13},{10,... | collective-permute-start | bytes 196616 | tf_op jit(solution)/shard_map/ppermute | solution.py:310
  44.5 2.1 %collective-permute-done.15.c = bf16[64,512]{1,0:T(8,128)(2,1)S(1)} collective-permute-done((bf16[64,512]{1,0:T(8,128)(2,1)S(1)}, bf16[64,512]{1,0:T(8,128)(2,1)S(1)}, u32[]{:S(2)}, u32[]{:S(2)}) %collective-permute-start.15) | collective-permute-done | bytes 65568 | tf_op jit(solution)/shard_map/ppermute | solution.py:310
  49.4 2.9 %collective-permute-start.20 = (bf16[256,640]{1,0:T(8,128)(2,1)S(1)}, bf16[256,640]{1,0:T(8,128)(2,1)S(1)}, u32[]{:S(2)}, u32[]{:S(2)}) collective-permute-start(bf16[256,640]{1,0:T(8,128)(2,1)S(1)} %pad_maximum_fusion.near), channel_id=1, source_target_pairs={{0,1},{1,0},{2,3},{3,2},{4,5},{5,4},{6,7},{7,6},{8,9},{9,8},{10,11... | collective-permute-start | bytes 983048 | tf_op jit(solution)/shard_map/ppermute | solution.py:310
  52.3 1.3 %shard_map.44 = (f32[256,1024]{1,0:T(8,128)S(1)}, bf16[256,1024]{1,0:T(8,128)(2,1)S(1)}) custom-call(s32[1]{0:T(128)} %bitcast.middle, bf16[512,1024]{1,0:T(8,128)(2,1)S(1)} %get-tuple-element.73.turned, bf16[512,1024]{1,0:T(8,128)(2,1)S(1)} %get-tuple-element.63.beside, bf16[512,1024]{1,0:T(8,128)(2,1)S(1)} %get-tuple-element.64.opposite.swapped), custom_call_target="tpu_custom_call" | custom-call | tf_op jit(solution)/shard_map/pallas_call | solution.py:19
  53.6 1.5 %collective-permute-start.19 = (bf16[256,512]{1,0:T(8,128)(2,1)S(1)}, bf16[256,512]{1,0:T(8,128)(2,1)S(1)}, u32[]{:S(2)}, u32[]{:S(2)}) collective-permute-start(bf16[256,512]{1,0:T(8,128)(2,1)S(1)} %shard_map.45.near), channel_id=1, source_target_pairs={{0,1},{1,0},{2,3},{3,2},{4,5},{5,4},{6,7},{7,6},{8,9},{9,8},{10,11... | collective-permute-start | bytes 786440 | tf_op jit(solution)/shard_map/ppermute | solution.py:310
  56.3 1.8 %shard_map.46 = (bf16[512,1024]{1,0:T(8,128)(2,1)S(1)}, bf16[512,1024]{1,0:T(8,128)(2,1)S(1)}) custom-call(s32[8]{0:T(128)S(1)} %broadcast_xor_fusion.order, s32[1]{0:T(128)} %bitcast.middle, bf16[256,512]{1,0:T(8,128)(2,1)S(1)} %shard_map.45.near, bf16[256,512]{1,0:T(8,128)(2,1)S(1)} %collective-permute-done.19.far, ...), custom_call_target="tpu_custom_call" | custom-call | tf_op jit(solution)/shard_map/pallas_call | solution.py:19
  58.1 2.9 %collective-permute-start.29 = (bf16[512,1024]{1,0:T(8,128)(2,1)S(1)}, bf16[512,1024]{1,0:T(8,128)(2,1)S(1)}, u32[]{:S(2)}, u32[]{:S(2)}) collective-permute-start(bf16[512,1024]{1,0:T(8,128)(2,1)S(1)} %get-tuple-element.71), channel_id=1, source_target_pairs={{8,0},{16,24},{9,1},{17,25},{10,2},{18,26},{11,3},{19,27},{12,4},{... | collective-permute-start | bytes 3145736 | tf_op jit(solution)/shard_map/ppermute | solution.py:392
  61.9 1.9 %collective-permute-start.31 = (bf16[512,1024]{1,0:T(8,128)(2,1)S(1)}, bf16[512,1024]{1,0:T(8,128)(2,1)S(1)}, u32[]{:S(2)}, u32[]{:S(2)}) collective-permute-start(bf16[512,1024]{1,0:T(8,128)(2,1)S(1)} %get-tuple-element.88), channel_id=1, source_target_pairs={{8,16},{16,8},{9,17},{17,9},{10,18},{18,10},{11,19},{19,11},{12,20... | collective-permute-start | bytes 3145736 | tf_op jit(solution)/shard_map/ppermute | solution.py:392
  63.9 1.3 %collective-permute-start.23 = (bf16[64,1024]{1,0:T(8,128)(2,1)S(1)}, bf16[64,1024]{1,0:T(8,128)(2,1)S(1)}, u32[]{:S(2)}, u32[]{:S(2)}) collective-permute-start(bf16[64,1024]{1,0:T(8,128)(2,1)S(1)} %get-tuple-element.78), channel_id=1, source_target_pairs={{0,2},{1,3},{2,0},{3,1},{4,6},{5,7},{6,4},{7,5},{8,10},{9,11},{10,... | collective-permute-start | bytes 393224 | tf_op jit(solution)/shard_map/ppermute | solution.py:310
  66.7 2.6 %shard_map.50.held = f32[512,1024]{1,0:T(8,128)S(1)} custom-call(s32[8]{0:T(128)S(1)} %broadcast_xor_fusion.order, s32[1]{0:T(128)} %bitcast.middle, bf16[256,640]{1,0:T(8,128)(2,1)S(1)} %pad_maximum_fusion.near, bf16[256,640]{1,0:T(8,128)(2,1)S(1)} %collective-permute-done.20.far, bf16[512,1024]{1,0:T(8,128)(2,1)S(1)} %get-tuple-element.81.own, ...), custom_call_target="tpu_custom_call" | custom-call | tf_op jit(solution)/shard_map/pallas_call | solution.py:19
  69.9 1.3 %collective-permute-done.25.c = bf16[64,1024]{1,0:T(8,128)(2,1)S(1)} collective-permute-done((bf16[64,1024]{1,0:T(8,128)(2,1)S(1)}, bf16[64,1024]{1,0:T(8,128)(2,1)S(1)}, u32[]{:S(2)}, u32[]{:S(2)}) %collective-permute-start.25) | collective-permute-done | bytes 131104 | tf_op jit(solution)/shard_map/ppermute | solution.py:310
  71.3 2.4 %collective-permute-start.28 = (bf16[64,1024]{1,0:T(8,128)(2,1)S(1)}, bf16[64,1024]{1,0:T(8,128)(2,1)S(1)}, u32[]{:S(2)}, u32[]{:S(2)}) collective-permute-start(bf16[64,1024]{1,0:T(8,128)(2,1)S(1)} %shard_map.49.refs_0_), channel_id=1, source_target_pairs={{0,6},{1,7},{2,4},{3,5},{4,2},{5,3},{6,0},{7,1},{8,14},{9,15},{10,... | collective-permute-start | bytes 393224 | tf_op jit(solution)/shard_map/ppermute | solution.py:310
  74.1 2.0 %collective-permute-done.28.refs_3_ = bf16[64,1024]{1,0:T(8,128)(2,1)S(1)} collective-permute-done((bf16[64,1024]{1,0:T(8,128)(2,1)S(1)}, bf16[64,1024]{1,0:T(8,128)(2,1)S(1)}, u32[]{:S(2)}, u32[]{:S(2)}) %collective-permute-start.28) | collective-permute-done | bytes 131104 | tf_op jit(solution)/shard_map/ppermute | solution.py:310
  76.1 1.7 %collective-permute-done.27.refs_2_ = bf16[64,1024]{1,0:T(8,128)(2,1)S(1)} collective-permute-done((bf16[64,1024]{1,0:T(8,128)(2,1)S(1)}, bf16[64,1024]{1,0:T(8,128)(2,1)S(1)}, u32[]{:S(2)}, u32[]{:S(2)}) %collective-permute-start.27) | collective-permute-done | bytes 131104 | tf_op jit(solution)/shard_map/ppermute | solution.py:310
  79.1 4.1 %collective-permute-done.29.out = bf16[512,1024]{1,0:T(8,128)(2,1)S(1)} collective-permute-done((bf16[512,1024]{1,0:T(8,128)(2,1)S(1)}, bf16[512,1024]{1,0:T(8,128)(2,1)S(1)}, u32[]{:S(2)}, u32[]{:S(2)}) %collective-permute-start.29) | collective-permute-done | bytes 1048608 | tf_op jit(solution)/shard_map/ppermute | solution.py:392
  84.4 4.0 %collective-permute-done.31.over = bf16[512,1024]{1,0:T(8,128)(2,1)S(1)} collective-permute-done((bf16[512,1024]{1,0:T(8,128)(2,1)S(1)}, bf16[512,1024]{1,0:T(8,128)(2,1)S(1)}, u32[]{:S(2)}, u32[]{:S(2)}) %collective-permute-start.31) | collective-permute-done | bytes 1048608 | tf_op jit(solution)/shard_map/ppermute | solution.py:392
  88.4 3.0 %shard_map.52 = f32[512,1024]{1,0:T(8,128)} custom-call(s32[8]{0:T(128)S(1)} %broadcast_xor_fusion.order, s32[1]{0:T(128)} %bitcast.middle, bf16[256,1024]{1,0:T(8,128)(2,1)S(1)} %shard_map.51.near, bf16[256,1024]{1,0:T(8,128)(2,1)S(1)} %collective-permute-done.30.far, bf16[512,1024]{1,0:T(8,128)(2,1)S(1)} %get-tuple-element.63.beside, ...), custom_call_target="tpu_custom_call" | custom-call | tf_op jit(solution)/shard_map/pallas_call | solution.py:19
  (53 shorter events, 21.7 us)
Async XLA Ops:
  1.8 7.4 %collective-permute-start.2 = (f32[2,1024]{1,0:T(2,128)S(1)}, f32[2,1024]{1,0:T(2,128)S(1)}, u32[]{:S(2)}, u32[]{:S(2)}) collective-permute-start(f32[2,1024]{1,0:T(2,128)S(1)} %shard_map.37), channel_id=1, source_target_pairs={{0,24},{8,0},{16,8},{24,16},{1,25},{9,1},{17,9},{25,17},{2,26},{10... | collective-permute-start | bytes 24584 | tf_op jit(solution)/shard_map/ppermute | solution.py:356
  1.9 7.3 %collective-permute-start.1 = (f32[2,1024]{1,0:T(2,128)S(1)}, f32[2,1024]{1,0:T(2,128)S(1)}, u32[]{:S(2)}, u32[]{:S(2)}) collective-permute-start(f32[2,1024]{1,0:T(2,128)S(1)} %shard_map.37), channel_id=1, source_target_pairs={{0,16},{8,24},{16,0},{24,8},{1,17},{9,25},{17,1},{25,9},{2,18},{10... | collective-permute-start | bytes 24584 | tf_op jit(solution)/shard_map/ppermute | solution.py:356
  4.3 4.9 %collective-permute-start = (f32[2,1024]{1,0:T(2,128)S(1)}, f32[2,1024]{1,0:T(2,128)S(1)}, u32[]{:S(2)}, u32[]{:S(2)}) collective-permute-start(f32[2,1024]{1,0:T(2,128)S(1)} %shard_map.37), channel_id=1, source_target_pairs={{0,8},{8,16},{16,24},{24,0},{1,9},{9,17},{17,25},{25,1},{2,10},{10... | collective-permute-start | bytes 24584 | tf_op jit(solution)/shard_map/ppermute | solution.py:356
  6.5 25.3 %collective-permute-start.11 = (bf16[512,1024]{1,0:T(8,128)(2,1)}, bf16[512,1024]{1,0:T(8,128)(2,1)S(1)}, u32[]{:S(2)}, u32[]{:S(2)}) collective-permute-start(bf16[512,1024]{1,0:T(8,128)(2,1)} %z.5), channel_id=1, source_target_pairs={{8,16},{16,8},{9,17},{17,9},{10,18},{18,10},{11,19},{19,11},{12,20... | collective-permute-start | bytes 3145736 | tf_op jit(solution)/shard_map/ppermute | solution.py:360
  8.5 23.5 %collective-permute-start.10 = (bf16[512,1024]{1,0:T(8,128)(2,1)}, bf16[512,1024]{1,0:T(8,128)(2,1)}, u32[]{:S(2)}, u32[]{:S(2)}) collective-permute-start(bf16[512,1024]{1,0:T(8,128)(2,1)} %z.5), channel_id=1, source_target_pairs={{0,8},{8,0},{16,24},{24,16},{1,9},{9,1},{17,25},{25,17},{2,10},{10... | collective-permute-start | bytes 3145736 | tf_op jit(solution)/shard_map/ppermute | solution.py:359
  11.6 2.8 %collective-permute-start.3 = (bf16[256,640]{1,0:T(8,128)(2,1)S(1)}, bf16[256,640]{1,0:T(8,128)(2,1)S(1)}, u32[]{:S(2)}, u32[]{:S(2)}) collective-permute-start(bf16[256,640]{1,0:T(8,128)(2,1)S(1)} %get-tuple-element.49), channel_id=1, source_target_pairs={{0,1},{1,0},{2,3},{3,2},{4,5},{5,4},{6,7},{7,6},{8,9},{9,8},{10,11... | collective-permute-start | bytes 983048 | tf_op jit(solution)/shard_map/ppermute | solution.py:310
  14.6 3.8 %collective-permute-start.4 = (bf16[64,640]{1,0:T(8,128)(2,1)S(1)}, bf16[64,640]{1,0:T(8,128)(2,1)S(1)}, u32[]{:S(2)}, u32[]{:S(2)}) collective-permute-start(bf16[64,640]{1,0:T(8,128)(2,1)S(1)} %get-tuple-element.51), channel_id=1, source_target_pairs={{0,2},{1,3},{2,0},{3,1},{4,6},{5,7},{6,4},{7,5},{8,10},{9,11},{10,... | collective-permute-start | bytes 245768 | tf_op jit(solution)/shard_map/ppermute | solution.py:310
  15.9 3.7 %collective-permute-start.5 = (bf16[64,640]{1,0:T(8,128)(2,1)S(1)}, bf16[64,640]{1,0:T(8,128)(2,1)S(1)}, u32[]{:S(2)}, u32[]{:S(2)}) collective-permute-start(bf16[64,640]{1,0:T(8,128)(2,1)S(1)} %get-tuple-element.52), channel_id=1, source_target_pairs={{0,4},{1,5},{2,6},{3,7},{4,0},{5,1},{6,2},{7,3},{8,12},{9,13},{10,... | collective-permute-start | bytes 245768 | tf_op jit(solution)/shard_map/ppermute | solution.py:310
  17.1 4.2 %collective-permute-start.6 = (bf16[64,640]{1,0:T(8,128)(2,1)S(1)}, bf16[64,640]{1,0:T(8,128)(2,1)S(1)}, u32[]{:S(2)}, u32[]{:S(2)}) collective-permute-start(bf16[64,640]{1,0:T(8,128)(2,1)S(1)} %get-tuple-element.53), channel_id=1, source_target_pairs={{0,6},{1,7},{2,4},{3,5},{4,2},{5,3},{6,0},{7,1},{8,14},{9,15},{10,... | collective-permute-start | bytes 245768 | tf_op jit(solution)/shard_map/ppermute | solution.py:310
  21.4 4.4 %collective-permute-start.9 = (bf16[64,640]{1,0:T(8,128)(2,1)S(1)}, bf16[64,640]{1,0:T(8,128)(2,1)S(1)}, u32[]{:S(2)}, u32[]{:S(2)}) collective-permute-start(bf16[64,640]{1,0:T(8,128)(2,1)S(1)} %shard_map.40), channel_id=1, source_target_pairs={{0,6},{1,7},{2,4},{3,5},{4,2},{5,3},{6,0},{7,1},{8,14},{9,15},{10,... | collective-permute-start | bytes 245768 | tf_op jit(solution)/shard_map/ppermute | solution.py:310
  22.1 4.6 %collective-permute-start.8 = (bf16[64,640]{1,0:T(8,128)(2,1)S(1)}, bf16[64,640]{1,0:T(8,128)(2,1)S(1)}, u32[]{:S(2)}, u32[]{:S(2)}) collective-permute-start(bf16[64,640]{1,0:T(8,128)(2,1)S(1)} %shard_map.40), channel_id=1, source_target_pairs={{0,4},{1,5},{2,6},{3,7},{4,0},{5,1},{6,2},{7,3},{8,12},{9,13},{10,... | collective-permute-start | bytes 245768 | tf_op jit(solution)/shard_map/ppermute | solution.py:310
  23.3 3.7 %collective-permute-start.7 = (bf16[64,640]{1,0:T(8,128)(2,1)S(1)}, bf16[64,640]{1,0:T(8,128)(2,1)S(1)}, u32[]{:S(2)}, u32[]{:S(2)}) collective-permute-start(bf16[64,640]{1,0:T(8,128)(2,1)S(1)} %shard_map.40), channel_id=1, source_target_pairs={{0,2},{1,3},{2,0},{3,1},{4,6},{5,7},{6,4},{7,5},{8,10},{9,11},{10,... | collective-permute-start | bytes 245768 | tf_op jit(solution)/shard_map/ppermute | solution.py:310
  32.0 29.1 %collective-permute-start.21 = (bf16[512,1024]{1,0:T(8,128)(2,1)}, bf16[512,1024]{1,0:T(8,128)(2,1)}, u32[]{:S(2)}, u32[]{:S(2)}) collective-permute-start(bf16[512,1024]{1,0:T(8,128)(2,1)} %z.5), channel_id=1, source_target_pairs={{0,24},{24,0},{1,25},{25,1},{2,26},{26,2},{3,27},{27,3},{4,28},{28... | collective-permute-start | bytes 3145736 | tf_op jit(solution)/shard_map/ppermute | solution.py:375
  36.3 3.7 %collective-permute-start.12 = (bf16[256,512]{1,0:T(8,128)(2,1)S(1)}, bf16[256,512]{1,0:T(8,128)(2,1)S(1)}, u32[]{:S(2)}, u32[]{:S(2)}) collective-permute-start(bf16[256,512]{1,0:T(8,128)(2,1)S(1)} %get-tuple-element.57), channel_id=1, source_target_pairs={{0,1},{1,0},{2,3},{3,2},{4,5},{5,4},{6,7},{7,6},{8,9},{9,8},{10,11... | collective-permute-start | bytes 786440 | tf_op jit(solution)/shard_map/ppermute | solution.py:310
  40.1 3.2 %collective-permute-start.13 = (bf16[64,512]{1,0:T(8,128)(2,1)S(1)}, bf16[64,512]{1,0:T(8,128)(2,1)S(1)}, u32[]{:S(2)}, u32[]{:S(2)}) collective-permute-start(bf16[64,512]{1,0:T(8,128)(2,1)S(1)} %get-tuple-element.59), channel_id=1, source_target_pairs={{0,2},{1,3},{2,0},{3,1},{4,6},{5,7},{6,4},{7,5},{8,10},{9,11},{10,... | collective-permute-start | bytes 196616 | tf_op jit(solution)/shard_map/ppermute | solution.py:310
  41.4 3.1 %collective-permute-start.14 = (bf16[64,512]{1,0:T(8,128)(2,1)S(1)}, bf16[64,512]{1,0:T(8,128)(2,1)S(1)}, u32[]{:S(2)}, u32[]{:S(2)}) collective-permute-start(bf16[64,512]{1,0:T(8,128)(2,1)S(1)} %get-tuple-element.60), channel_id=1, source_target_pairs={{0,4},{1,5},{2,6},{3,7},{4,0},{5,1},{6,2},{7,3},{8,12},{9,13},{10,... | collective-permute-start | bytes 196616 | tf_op jit(solution)/shard_map/ppermute | solution.py:310
  42.6 4.0 %collective-permute-start.15 = (bf16[64,512]{1,0:T(8,128)(2,1)S(1)}, bf16[64,512]{1,0:T(8,128)(2,1)S(1)}, u32[]{:S(2)}, u32[]{:S(2)}) collective-permute-start(bf16[64,512]{1,0:T(8,128)(2,1)S(1)} %get-tuple-element.61), channel_id=1, source_target_pairs={{0,6},{1,7},{2,4},{3,5},{4,2},{5,3},{6,0},{7,1},{8,14},{9,15},{10,... | collective-permute-start | bytes 196616 | tf_op jit(solution)/shard_map/ppermute | solution.py:310
  46.6 6.9 %collective-permute-start.18 = (bf16[64,512]{1,0:T(8,128)(2,1)S(1)}, bf16[64,512]{1,0:T(8,128)(2,1)S(1)}, u32[]{:S(2)}, u32[]{:S(2)}) collective-permute-start(bf16[64,512]{1,0:T(8,128)(2,1)S(1)} %shard_map.43.refs_0_.first), channel_id=1, source_target_pairs={{0,6},{1,7},{2,4},{3,5},{4,2},{5,3},{6,0},{7,1},{8,14},{9,15},{10,... | collective-permute-start | bytes 196616 | tf_op jit(solution)/shard_map/ppermute | solution.py:310
  47.1 6.5 %collective-permute-start.17 = (bf16[64,512]{1,0:T(8,128)(2,1)S(1)}, bf16[64,512]{1,0:T(8,128)(2,1)S(1)}, u32[]{:S(2)}, u32[]{:S(2)}) collective-permute-start(bf16[64,512]{1,0:T(8,128)(2,1)S(1)} %shard_map.43.refs_0_.first), channel_id=1, source_target_pairs={{0,4},{1,5},{2,6},{3,7},{4,0},{5,1},{6,2},{7,3},{8,12},{9,13},{10,... | collective-permute-start | bytes 196616 | tf_op jit(solution)/shard_map/ppermute | solution.py:310
  48.2 5.4 %collective-permute-start.16 = (bf16[64,512]{1,0:T(8,128)(2,1)S(1)}, bf16[64,512]{1,0:T(8,128)(2,1)S(1)}, u32[]{:S(2)}, u32[]{:S(2)}) collective-permute-start(bf16[64,512]{1,0:T(8,128)(2,1)S(1)} %shard_map.43.refs_0_.first), channel_id=1, source_target_pairs={{0,2},{1,3},{2,0},{3,1},{4,6},{5,7},{6,4},{7,5},{8,10},{9,11},{10,... | collective-permute-start | bytes 196616 | tf_op jit(solution)/shard_map/ppermute | solution.py:310
  49.4 5.8 %collective-permute-start.20 = (bf16[256,640]{1,0:T(8,128)(2,1)S(1)}, bf16[256,640]{1,0:T(8,128)(2,1)S(1)}, u32[]{:S(2)}, u32[]{:S(2)}) collective-permute-start(bf16[256,640]{1,0:T(8,128)(2,1)S(1)} %pad_maximum_fusion.near), channel_id=1, source_target_pairs={{0,1},{1,0},{2,3},{3,2},{4,5},{5,4},{6,7},{7,6},{8,9},{9,8},{10,11... | collective-permute-start | bytes 983048 | tf_op jit(solution)/shard_map/ppermute | solution.py:310
  53.6 2.7 %collective-permute-start.19 = (bf16[256,512]{1,0:T(8,128)(2,1)S(1)}, bf16[256,512]{1,0:T(8,128)(2,1)S(1)}, u32[]{:S(2)}, u32[]{:S(2)}) collective-permute-start(bf16[256,512]{1,0:T(8,128)(2,1)S(1)} %shard_map.45.near), channel_id=1, source_target_pairs={{0,1},{1,0},{2,3},{3,2},{4,5},{5,4},{6,7},{7,6},{8,9},{9,8},{10,11... | collective-permute-start | bytes 786440 | tf_op jit(solution)/shard_map/ppermute | solution.py:310
  58.1 25.0 %collective-permute-start.29 = (bf16[512,1024]{1,0:T(8,128)(2,1)S(1)}, bf16[512,1024]{1,0:T(8,128)(2,1)S(1)}, u32[]{:S(2)}, u32[]{:S(2)}) collective-permute-start(bf16[512,1024]{1,0:T(8,128)(2,1)S(1)} %get-tuple-element.71), channel_id=1, source_target_pairs={{8,0},{16,24},{9,1},{17,25},{10,2},{18,26},{11,3},{19,27},{12,4},{... | collective-permute-start | bytes 3145736 | tf_op jit(solution)/shard_map/ppermute | solution.py:392
  61.2 2.6 %collective-permute-start.22 = (bf16[256,1024]{1,0:T(8,128)(2,1)S(1)}, bf16[256,1024]{1,0:T(8,128)(2,1)S(1)}, u32[]{:S(2)}, u32[]{:S(2)}) collective-permute-start(bf16[256,1024]{1,0:T(8,128)(2,1)S(1)} %get-tuple-element.76), channel_id=1, source_target_pairs={{0,1},{1,0},{2,3},{3,2},{4,5},{5,4},{6,7},{7,6},{8,9},{9,8},{10,11... | collective-permute-start | bytes 1572872 | tf_op jit(solution)/shard_map/ppermute | solution.py:310
  61.9 26.5 %collective-permute-start.31 = (bf16[512,1024]{1,0:T(8,128)(2,1)S(1)}, bf16[512,1024]{1,0:T(8,128)(2,1)S(1)}, u32[]{:S(2)}, u32[]{:S(2)}) collective-permute-start(bf16[512,1024]{1,0:T(8,128)(2,1)S(1)} %get-tuple-element.88), channel_id=1, source_target_pairs={{8,16},{16,8},{9,17},{17,9},{10,18},{18,10},{11,19},{19,11},{12,20... | collective-permute-start | bytes 3145736 | tf_op jit(solution)/shard_map/ppermute | solution.py:392
  63.9 5.3 %collective-permute-start.23 = (bf16[64,1024]{1,0:T(8,128)(2,1)S(1)}, bf16[64,1024]{1,0:T(8,128)(2,1)S(1)}, u32[]{:S(2)}, u32[]{:S(2)}) collective-permute-start(bf16[64,1024]{1,0:T(8,128)(2,1)S(1)} %get-tuple-element.78), channel_id=1, source_target_pairs={{0,2},{1,3},{2,0},{3,1},{4,6},{5,7},{6,4},{7,5},{8,10},{9,11},{10,... | collective-permute-start | bytes 393224 | tf_op jit(solution)/shard_map/ppermute | solution.py:310
  65.2 4.7 %collective-permute-start.24 = (bf16[64,1024]{1,0:T(8,128)(2,1)S(1)}, bf16[64,1024]{1,0:T(8,128)(2,1)S(1)}, u32[]{:S(2)}, u32[]{:S(2)}) collective-permute-start(bf16[64,1024]{1,0:T(8,128)(2,1)S(1)} %get-tuple-element.79), channel_id=1, source_target_pairs={{0,4},{1,5},{2,6},{3,7},{4,0},{5,1},{6,2},{7,3},{8,12},{9,13},{10,... | collective-permute-start | bytes 393224 | tf_op jit(solution)/shard_map/ppermute | solution.py:310
  65.5 5.8 %collective-permute-start.25 = (bf16[64,1024]{1,0:T(8,128)(2,1)S(1)}, bf16[64,1024]{1,0:T(8,128)(2,1)S(1)}, u32[]{:S(2)}, u32[]{:S(2)}) collective-permute-start(bf16[64,1024]{1,0:T(8,128)(2,1)S(1)} %get-tuple-element.80), channel_id=1, source_target_pairs={{0,6},{1,7},{2,4},{3,5},{4,2},{5,3},{6,0},{7,1},{8,14},{9,15},{10,... | collective-permute-start | bytes 393224 | tf_op jit(solution)/shard_map/ppermute | solution.py:310
  71.3 4.8 %collective-permute-start.28 = (bf16[64,1024]{1,0:T(8,128)(2,1)S(1)}, bf16[64,1024]{1,0:T(8,128)(2,1)S(1)}, u32[]{:S(2)}, u32[]{:S(2)}) collective-permute-start(bf16[64,1024]{1,0:T(8,128)(2,1)S(1)} %shard_map.49.refs_0_), channel_id=1, source_target_pairs={{0,6},{1,7},{2,4},{3,5},{4,2},{5,3},{6,0},{7,1},{8,14},{9,15},{10,... | collective-permute-start | bytes 393224 | tf_op jit(solution)/shard_map/ppermute | solution.py:310
  73.7 4.1 %collective-permute-start.27 = (bf16[64,1024]{1,0:T(8,128)(2,1)S(1)}, bf16[64,1024]{1,0:T(8,128)(2,1)S(1)}, u32[]{:S(2)}, u32[]{:S(2)}) collective-permute-start(bf16[64,1024]{1,0:T(8,128)(2,1)S(1)} %shard_map.49.refs_0_), channel_id=1, source_target_pairs={{0,4},{1,5},{2,6},{3,7},{4,0},{5,1},{6,2},{7,3},{8,12},{9,13},{10,... | collective-permute-start | bytes 393224 | tf_op jit(solution)/shard_map/ppermute | solution.py:310
  74.0 5.1 %collective-permute-start.26 = (bf16[64,1024]{1,0:T(8,128)(2,1)S(1)}, bf16[64,1024]{1,0:T(8,128)(2,1)S(1)}, u32[]{:S(2)}, u32[]{:S(2)}) collective-permute-start(bf16[64,1024]{1,0:T(8,128)(2,1)S(1)} %shard_map.49.refs_0_), channel_id=1, source_target_pairs={{0,2},{1,3},{2,0},{3,1},{4,6},{5,7},{6,4},{7,5},{8,10},{9,11},{10,... | collective-permute-start | bytes 393224 | tf_op jit(solution)/shard_map/ppermute | solution.py:310
  83.2 5.2 %collective-permute-start.30 = (bf16[256,1024]{1,0:T(8,128)(2,1)S(1)}, bf16[256,1024]{1,0:T(8,128)(2,1)S(1)}, u32[]{:S(2)}, u32[]{:S(2)}) collective-permute-start(bf16[256,1024]{1,0:T(8,128)(2,1)S(1)} %shard_map.51.near), channel_id=1, source_target_pairs={{0,1},{1,0},{2,3},{3,2},{4,5},{5,4},{6,7},{7,6},{8,9},{9,8},{10,11... | collective-permute-start | bytes 1572872 | tf_op jit(solution)/shard_map/ppermute | solution.py:310
  (1 other events, 5.6 us)

commit v21 on v19

--- a/solution.py
+++ b/solution.py
@@ -377,7 +377,7 @@
     second = kernel_call(total_either_kernel, [(eighth, jnp.bfloat16)], smem=1)(
         middle, first, halved[0], *got
     )[0]
-    near = after(gather_chips(after(second, held)), pushed[0])
+    near = after(gather_chips(after(second, held)), pushed[1])
     return kernel_call(
         functools.partial(last_kernel, total), [result],
         smem=2, scratch=12, temps=[((rows, 2 * rows), jnp.bfloat16), result], sems=4,

time: 91.3 us -> 94.6 us (1.036)
  the two profiles are of different devices: /device:TPU:9 before, /device:TPU:0 now
where the time goes in v21:
time: 94.6 us; the launch traced here: 94.2 us
  waiting for transfers between devices  39.7 us (42%)
  starting transfers between devices  38.5 us (41%)
  Pallas kernels  15.1 us (16%)
    ppermute x24, waiting for transfers between devices, to_partner(): return lax.ppermute(x, 'feat', [(i, i ^ step) for i in range(8)])  28.4 us
    ppermute x24, starting transfers between devices, to_partner(): return lax.ppermute(x, 'feat', [(i, i ^ step) for i in range(8)])  22.2 us
    pallas_call x16, Pallas kernels, call(): pl.pallas_call(body, out_shape=[jax.ShapeDtypeStruct(s, t) for s, t in ou...  15.1 us
    ppermute x1, waiting for transfers between devices, by_line(): lax.ppermute(out, 'dp', outward)  7.2 us
    ppermute x3, starting transfers between devices, by_line(): lax.ppermute(stats, 'dp', [(i, (i + k) % 4) for i in range(4)])  6.11 us
    ppermute x1, starting transfers between devices, by_line(): lax.ppermute(after(z_anchor, beside_in, swapped, near_own), 'dp', [(0, 3)...  4.09 us
    ppermute x1, waiting for transfers between devices, by_line(): lax.ppermute(after(z_anchor, beside_in, swapped, near_own), 'dp', [(0, 3)...  2.88 us
    ppermute x1, starting transfers between devices, by_line(): beside_in = lax.ppermute(ahead, 'dp', [(i, i ^ 1) for i in range(4)])  2.48 us
  transfers between devices with their start and end apart: 32, of which 22 were waited for; matrix products, arithmetic and copies ran while one was open for 1% of the time, Pallas kernels for 11%

profile of v21, /device:TPU:0, one launch (start us, length us, event | category | flops | bytes accessed | tf_op | source)
XLA Modules:
  0.0 94.2 jit_solution(18406198326252546805)
XLA Ops:
  0.0 1.8 %shard_map.37 = f32[2,1024]{1,0:T(2,128)S(1)} custom-call(bf16[512,1024]{1,0:T(8,128)(2,1)} %z.5), custom_call_target="tpu_custom_call" | custom-call | tf_op jit(solution)/shard_map/pallas_call | solution.py:17
  1.8 5.1 %collective-permute-start.2 = (f32[2,1024]{1,0:T(2,128)S(1)}, f32[2,1024]{1,0:T(2,128)S(1)}, u32[]{:S(2)}, u32[]{:S(2)}) collective-permute-start(f32[2,1024]{1,0:T(2,128)S(1)} %shard_map.37), channel_id=1, source_target_pairs={{0,24},{8,0},{16,8},{24,16},{1,25},{9,1},{17,9},{25,17},{2,26},{10... | collective-permute-start | bytes 24584 | tf_op jit(solution)/shard_map/ppermute | solution.py:323
  7.9 2.5 %collective-permute-start.10 = (bf16[512,1024]{1,0:T(8,128)(2,1)}, bf16[512,1024]{1,0:T(8,128)(2,1)S(1)}, u32[]{:S(2)}, u32[]{:S(2)}) collective-permute-start(bf16[512,1024]{1,0:T(8,128)(2,1)} %z.5), channel_id=1, source_target_pairs={{0,8},{8,0},{16,24},{24,16},{1,9},{9,1},{17,25},{25,17},{2,10},{10... | collective-permute-start | bytes 3145736 | tf_op jit(solution)/shard_map/ppermute | solution.py:326
  10.4 1.6 %collective-permute-start.11 = (bf16[512,1024]{1,0:T(8,128)(2,1)}, bf16[512,1024]{1,0:T(8,128)(2,1)}, u32[]{:S(2)}, u32[]{:S(2)}) collective-permute-start(bf16[512,1024]{1,0:T(8,128)(2,1)} %z.5), channel_id=1, source_target_pairs={{8,16},{16,8},{9,17},{17,9},{10,18},{18,10},{11,19},{19,11},{12,20... | collective-permute-start | bytes 3145736 | tf_op jit(solution)/shard_map/ppermute | solution.py:327
  12.8 2.4 %shard_map.38 = (bf16[512,1024]{1,0:T(8,128)(2,1)S(1)}, bf16[512,1024]{1,0:T(8,128)(2,1)S(1)}, f32[1,1024]{1,0:T(1,128)S(1)}, f32[256,640]{1,0:T(8,128)S(1)}, bf16[256,640]{1,0:T(8,128)(2,1)S(1)}) custom-call(s32[8]{0:T(128)S(1)} %broadcast_xor_fusion.order, bf16[512,1024]{1,0:T(8,128)(2,1)} %z.5, f32[1,1024]{1,0:T(1,128)S(1)} %get-tuple-element.88.mean), custom_call_target="tpu_custom_call" | custom-call | tf_op jit(solution)/shard_map/pallas_call | solution.py:17
  15.2 1.6 %collective-permute-done.3.got = bf16[256,640]{1,0:T(8,128)(2,1)S(1)} collective-permute-done((bf16[256,640]{1,0:T(8,128)(2,1)S(1)}, bf16[256,640]{1,0:T(8,128)(2,1)S(1)}, u32[]{:S(2)}, u32[]{:S(2)}) %collective-permute-start.3) | collective-permute-done | bytes 327712 | tf_op jit(solution)/shard_map/ppermute | solution.py:277
  17.0 1.6 %collective-permute-start.4 = (bf16[64,640]{1,0:T(8,128)(2,1)S(1)}, bf16[64,640]{1,0:T(8,128)(2,1)S(1)}, u32[]{:S(2)}, u32[]{:S(2)}) collective-permute-start(bf16[64,640]{1,0:T(8,128)(2,1)S(1)} %get-tuple-element.50), channel_id=1, source_target_pairs={{0,2},{1,3},{2,0},{3,1},{4,6},{5,7},{6,4},{7,5},{8,10},{9,11},{10,... | collective-permute-start | bytes 245768 | tf_op jit(solution)/shard_map/ppermute | solution.py:277
  18.5 1.5 %collective-permute-start.5 = (bf16[64,640]{1,0:T(8,128)(2,1)S(1)}, bf16[64,640]{1,0:T(8,128)(2,1)S(1)}, u32[]{:S(2)}, u32[]{:S(2)}) collective-permute-start(bf16[64,640]{1,0:T(8,128)(2,1)S(1)} %get-tuple-element.51), channel_id=1, source_target_pairs={{0,4},{1,5},{2,6},{3,7},{4,0},{5,1},{6,2},{7,3},{8,12},{9,13},{10,... | collective-permute-start | bytes 245768 | tf_op jit(solution)/shard_map/ppermute | solution.py:277
  21.5 2.3 %collective-permute-done.5.b = bf16[64,640]{1,0:T(8,128)(2,1)S(1)} collective-permute-done((bf16[64,640]{1,0:T(8,128)(2,1)S(1)}, bf16[64,640]{1,0:T(8,128)(2,1)S(1)}, u32[]{:S(2)}, u32[]{:S(2)}) %collective-permute-start.5) | collective-permute-done | bytes 81952 | tf_op jit(solution)/shard_map/ppermute | solution.py:277
  23.8 1.6 %collective-permute-done.6.c = bf16[64,640]{1,0:T(8,128)(2,1)S(1)} collective-permute-done((bf16[64,640]{1,0:T(8,128)(2,1)S(1)}, bf16[64,640]{1,0:T(8,128)(2,1)S(1)}, u32[]{:S(2)}, u32[]{:S(2)}) %collective-permute-start.6) | collective-permute-done | bytes 81952 | tf_op jit(solution)/shard_map/ppermute | solution.py:277
  27.6 1.5 %collective-permute-start.7 = (bf16[64,640]{1,0:T(8,128)(2,1)S(1)}, bf16[64,640]{1,0:T(8,128)(2,1)S(1)}, u32[]{:S(2)}, u32[]{:S(2)}) collective-permute-start(bf16[64,640]{1,0:T(8,128)(2,1)S(1)} %shard_map.40), channel_id=1, source_target_pairs={{0,2},{1,3},{2,0},{3,1},{4,6},{5,7},{6,4},{7,5},{8,10},{9,11},{10,... | collective-permute-start | bytes 245768 | tf_op jit(solution)/shard_map/ppermute | solution.py:277
  29.1 2.0 %collective-permute-done.9 = bf16[64,640]{1,0:T(8,128)(2,1)S(1)} collective-permute-done((bf16[64,640]{1,0:T(8,128)(2,1)S(1)}, bf16[64,640]{1,0:T(8,128)(2,1)S(1)}, u32[]{:S(2)}, u32[]{:S(2)}) %collective-permute-start.9) | collective-permute-done | bytes 81952 | tf_op jit(solution)/shard_map/ppermute | solution.py:277
  33.2 4.1 %collective-permute-start.20 = (bf16[512,1024]{1,0:T(8,128)(2,1)}, bf16[512,1024]{1,0:T(8,128)(2,1)}, u32[]{:S(2)}, u32[]{:S(2)}) collective-permute-start(bf16[512,1024]{1,0:T(8,128)(2,1)} %z.5), channel_id=1, source_target_pairs={{0,24},{24,0},{1,25},{25,1},{2,26},{26,2},{3,27},{27,3},{4,28},{28... | collective-permute-start | bytes 3145736 | tf_op jit(solution)/shard_map/ppermute | solution.py:342
  37.3 2.2 %shard_map.41 = (bf16[512,1024]{1,0:T(8,128)(2,1)S(1)}, f32[1,1024]{1,0:T(1,128)S(1)}, bf16[512,1024]{1,0:T(8,128)(2,1)S(1)}, f32[1,1024]{1,0:T(1,128)S(1)}, f32...) custom-call(s32[8]{0:T(128)S(1)} %broadcast_xor_fusion.order, s32[1]{0:T(128)} %bitcast.middle, ...), custom_call_target="tpu_custom_call" | custom-call | tf_op jit(solution)/shard_map/pallas_call | solution.py:17
  39.6 1.5 %collective-permute-done.12.got = bf16[256,512]{1,0:T(8,128)(2,1)S(1)} collective-permute-done((bf16[256,512]{1,0:T(8,128)(2,1)S(1)}, bf16[256,512]{1,0:T(8,128)(2,1)S(1)}, u32[]{:S(2)}, u32[]{:S(2)}) %collective-permute-start.12) | collective-permute-done | bytes 262176 | tf_op jit(solution)/shard_map/ppermute | solution.py:277
  41.2 1.6 %collective-permute-start.13 = (bf16[64,512]{1,0:T(8,128)(2,1)S(1)}, bf16[64,512]{1,0:T(8,128)(2,1)S(1)}, u32[]{:S(2)}, u32[]{:S(2)}) collective-permute-start(bf16[64,512]{1,0:T(8,128)(2,1)S(1)} %get-tuple-element.58), channel_id=1, source_target_pairs={{0,2},{1,3},{2,0},{3,1},{4,6},{5,7},{6,4},{7,5},{8,10},{9,11},{10,... | collective-permute-start | bytes 196616 | tf_op jit(solution)/shard_map/ppermute | solution.py:277
  42.7 1.5 %collective-permute-start.14 = (bf16[64,512]{1,0:T(8,128)(2,1)S(1)}, bf16[64,512]{1,0:T(8,128)(2,1)S(1)}, u32[]{:S(2)}, u32[]{:S(2)}) collective-permute-start(bf16[64,512]{1,0:T(8,128)(2,1)S(1)} %get-tuple-element.59), channel_id=1, source_target_pairs={{0,4},{1,5},{2,6},{3,7},{4,0},{5,1},{6,2},{7,3},{8,12},{9,13},{10,... | collective-permute-start | bytes 196616 | tf_op jit(solution)/shard_map/ppermute | solution.py:277
  45.5 1.5 %collective-permute-done.14.b = bf16[64,512]{1,0:T(8,128)(2,1)S(1)} collective-permute-done((bf16[64,512]{1,0:T(8,128)(2,1)S(1)}, bf16[64,512]{1,0:T(8,128)(2,1)S(1)}, u32[]{:S(2)}, u32[]{:S(2)}) %collective-permute-start.14) | collective-permute-done | bytes 65568 | tf_op jit(solution)/shard_map/ppermute | solution.py:277
  47.0 2.4 %collective-permute-done.15.c = bf16[64,512]{1,0:T(8,128)(2,1)S(1)} collective-permute-done((bf16[64,512]{1,0:T(8,128)(2,1)S(1)}, bf16[64,512]{1,0:T(8,128)(2,1)S(1)}, u32[]{:S(2)}, u32[]{:S(2)}) %collective-permute-start.15) | collective-permute-done | bytes 65568 | tf_op jit(solution)/shard_map/ppermute | solution.py:277
  50.6 2.4 %collective-permute-start.18 = (bf16[64,512]{1,0:T(8,128)(2,1)S(1)}, bf16[64,512]{1,0:T(8,128)(2,1)S(1)}, u32[]{:S(2)}, u32[]{:S(2)}) collective-permute-start(bf16[64,512]{1,0:T(8,128)(2,1)S(1)} %shard_map.43.refs_0_.first), channel_id=1, source_target_pairs={{0,6},{1,7},{2,4},{3,5},{4,2},{5,3},{6,0},{7,1},{8,14},{9,15},{10,... | collective-permute-start | bytes 196616 | tf_op jit(solution)/shard_map/ppermute | solution.py:277
  55.8 1.5 %collective-permute-done.19.far = bf16[256,512]{1,0:T(8,128)(2,1)S(1)} collective-permute-done((bf16[256,512]{1,0:T(8,128)(2,1)S(1)}, bf16[256,512]{1,0:T(8,128)(2,1)S(1)}, u32[]{:S(2)}, u32[]{:S(2)}) %collective-permute-start.19) | collective-permute-done | bytes 262176 | tf_op jit(solution)/shard_map/ppermute | solution.py:277
  57.9 2.9 %collective-permute-done.20.end_in = bf16[512,1024]{1,0:T(8,128)(2,1)} collective-permute-done((bf16[512,1024]{1,0:T(8,128)(2,1)}, bf16[512,1024]{1,0:T(8,128)(2,1)}, u32[]{:S(2)}, u32[]{:S(2)}) %collective-permute-start.20) | collective-permute-done | bytes 1048608 | tf_op jit(solution)/shard_map/ppermute | solution.py:342
  61.5 2.1 %shard_map.47 = (bf16[512,1024]{1,0:T(8,128)(2,1)S(1)}, f32[1,1024]{1,0:T(1,128)S(1)}, f32[256,512]{1,0:T(8,128)S(1)}, bf16[256,1024]{1,0:T(8,128)(2,1)S(1)}) custom-call(s32[1]{0:T(128)} %bitcast.middle, bf16[512,1024]{1,0:T(8,128)(2,1)S(1)} %get-tuple-element.71.turned, bf16[256,1024]{1,0:T(8,128)(2,1)S(1)} %get-tuple-element.65.sent_early, ...), custom_call_target="tpu_custom_call" | custom-call | tf_op jit(solution)/shard_map/pallas_call | solution.py:17
  65.6 1.6 %collective-permute-start.22 = (bf16[64,1024]{1,0:T(8,128)(2,1)S(1)}, bf16[64,1024]{1,0:T(8,128)(2,1)S(1)}, u32[]{:S(2)}, u32[]{:S(2)}) collective-permute-start(bf16[64,1024]{1,0:T(8,128)(2,1)S(1)} %get-tuple-element.76), channel_id=1, source_target_pairs={{0,2},{1,3},{2,0},{3,1},{4,6},{5,7},{6,4},{7,5},{8,10},{9,11},{10,... | collective-permute-start | bytes 393224 | tf_op jit(solution)/shard_map/ppermute | solution.py:277
  67.2 1.5 %collective-permute-start.23 = (bf16[64,1024]{1,0:T(8,128)(2,1)S(1)}, bf16[64,1024]{1,0:T(8,128)(2,1)S(1)}, u32[]{:S(2)}, u32[]{:S(2)}) collective-permute-start(bf16[64,1024]{1,0:T(8,128)(2,1)S(1)} %get-tuple-element.77), channel_id=1, source_target_pairs={{0,4},{1,5},{2,6},{3,7},{4,0},{5,1},{6,2},{7,3},{8,12},{9,13},{10,... | collective-permute-start | bytes 393224 | tf_op jit(solution)/shard_map/ppermute | solution.py:277
  69.2 2.6 %shard_map.50.held = f32[512,1024]{1,0:T(8,128)S(1)} custom-call(s32[8]{0:T(128)S(1)} %broadcast_xor_fusion.order, s32[1]{0:T(128)} %bitcast.middle, bf16[256,640]{1,0:T(8,128)(2,1)S(1)} %pad_maximum_fusion.near, bf16[256,640]{1,0:T(8,128)(2,1)S(1)} %collective-permute-done.25.far, bf16[512,1024]{1,0:T(8,128)(2,1)S(1)} %get-tuple-element.79.own, ...), custom_call_target="tpu_custom_call" | custom-call | tf_op jit(solution)/shard_map/pallas_call | solution.py:17
  71.8 3.5 %collective-permute-done.23.b = bf16[64,1024]{1,0:T(8,128)(2,1)S(1)} collective-permute-done((bf16[64,1024]{1,0:T(8,128)(2,1)S(1)}, bf16[64,1024]{1,0:T(8,128)(2,1)S(1)}, u32[]{:S(2)}, u32[]{:S(2)}) %collective-permute-start.23) | collective-permute-done | bytes 131104 | tf_op jit(solution)/shard_map/ppermute | solution.py:277
  77.4 1.4 %collective-permute-start.28 = (bf16[64,1024]{1,0:T(8,128)(2,1)S(1)}, bf16[64,1024]{1,0:T(8,128)(2,1)S(1)}, u32[]{:S(2)}, u32[]{:S(2)}) collective-permute-start(bf16[64,1024]{1,0:T(8,128)(2,1)S(1)} %shard_map.49.refs_0_), channel_id=1, source_target_pairs={{0,6},{1,7},{2,4},{3,5},{4,2},{5,3},{6,0},{7,1},{8,14},{9,15},{10,... | collective-permute-start | bytes 393224 | tf_op jit(solution)/shard_map/ppermute | solution.py:277
  78.9 2.5 %collective-permute-done.26.refs_1_ = bf16[64,1024]{1,0:T(8,128)(2,1)S(1)} collective-permute-done((bf16[64,1024]{1,0:T(8,128)(2,1)S(1)}, bf16[64,1024]{1,0:T(8,128)(2,1)S(1)}, u32[]{:S(2)}, u32[]{:S(2)}) %collective-permute-start.26) | collective-permute-done | bytes 131104 | tf_op jit(solution)/shard_map/ppermute | solution.py:277
  81.3 2.5 %collective-permute-done.27.refs_2_ = bf16[64,1024]{1,0:T(8,128)(2,1)S(1)} collective-permute-done((bf16[64,1024]{1,0:T(8,128)(2,1)S(1)}, bf16[64,1024]{1,0:T(8,128)(2,1)S(1)}, u32[]{:S(2)}, u32[]{:S(2)}) %collective-permute-start.27) | collective-permute-done | bytes 131104 | tf_op jit(solution)/shard_map/ppermute | solution.py:277
  84.0 7.2 %collective-permute-done.31.out = bf16[512,1024]{1,0:T(8,128)(2,1)S(1)} collective-permute-done((bf16[512,1024]{1,0:T(8,128)(2,1)S(1)}, bf16[512,1024]{1,0:T(8,128)(2,1)S(1)}, u32[]{:S(2)}, u32[]{:S(2)}) %collective-permute-start.31) | collective-permute-done | bytes 1048608 | tf_op jit(solution)/shard_map/ppermute | solution.py:358
  91.2 3.0 %shard_map.52 = f32[512,1024]{1,0:T(8,128)} custom-call(s32[8]{0:T(128)S(1)} %broadcast_xor_fusion.order, s32[1]{0:T(128)} %bitcast.middle, bf16[256,1024]{1,0:T(8,128)(2,1)S(1)} %shard_map.51.near, bf16[256,1024]{1,0:T(8,128)(2,1)S(1)} %collective-permute-done.30.far, bf16[512,1024]{1,0:T(8,128)(2,1)S(1)} %get-tuple-element.62.beside, ...), custom_call_target="tpu_custom_call" | custom-call | tf_op jit(solution)/shard_map/pallas_call | solution.py:17
  (53 shorter events, 19.1 us)
Async XLA Ops:
  1.8 10.9 %collective-permute-start.2 = (f32[2,1024]{1,0:T(2,128)S(1)}, f32[2,1024]{1,0:T(2,128)S(1)}, u32[]{:S(2)}, u32[]{:S(2)}) collective-permute-start(f32[2,1024]{1,0:T(2,128)S(1)} %shard_map.37), channel_id=1, source_target_pairs={{0,24},{8,0},{16,8},{24,16},{1,25},{9,1},{17,9},{25,17},{2,26},{10... | collective-permute-start | bytes 24584 | tf_op jit(solution)/shard_map/ppermute | solution.py:323
  6.9 5.8 %collective-permute-start.1 = (f32[2,1024]{1,0:T(2,128)S(1)}, f32[2,1024]{1,0:T(2,128)S(1)}, u32[]{:S(2)}, u32[]{:S(2)}) collective-permute-start(f32[2,1024]{1,0:T(2,128)S(1)} %shard_map.37), channel_id=1, source_target_pairs={{0,16},{8,24},{16,0},{24,8},{1,17},{9,25},{17,1},{25,9},{2,18},{10... | collective-permute-start | bytes 24584 | tf_op jit(solution)/shard_map/ppermute | solution.py:323
  6.9 5.8 %collective-permute-start = (f32[2,1024]{1,0:T(2,128)S(1)}, f32[2,1024]{1,0:T(2,128)S(1)}, u32[]{:S(2)}, u32[]{:S(2)}) collective-permute-start(f32[2,1024]{1,0:T(2,128)S(1)} %shard_map.37), channel_id=1, source_target_pairs={{0,8},{8,16},{16,24},{24,0},{1,9},{9,17},{17,25},{25,1},{2,10},{10... | collective-permute-start | bytes 24584 | tf_op jit(solution)/shard_map/ppermute | solution.py:323
  7.9 25.3 %collective-permute-start.10 = (bf16[512,1024]{1,0:T(8,128)(2,1)}, bf16[512,1024]{1,0:T(8,128)(2,1)S(1)}, u32[]{:S(2)}, u32[]{:S(2)}) collective-permute-start(bf16[512,1024]{1,0:T(8,128)(2,1)} %z.5), channel_id=1, source_target_pairs={{0,8},{8,0},{16,24},{24,16},{1,9},{9,1},{17,25},{25,17},{2,10},{10... | collective-permute-start | bytes 3145736 | tf_op jit(solution)/shard_map/ppermute | solution.py:326
  10.4 22.8 %collective-permute-start.11 = (bf16[512,1024]{1,0:T(8,128)(2,1)}, bf16[512,1024]{1,0:T(8,128)(2,1)}, u32[]{:S(2)}, u32[]{:S(2)}) collective-permute-start(bf16[512,1024]{1,0:T(8,128)(2,1)} %z.5), channel_id=1, source_target_pairs={{8,16},{16,8},{9,17},{17,9},{10,18},{18,10},{11,19},{19,11},{12,20... | collective-permute-start | bytes 3145736 | tf_op jit(solution)/shard_map/ppermute | solution.py:327
  15.1 1.7 %collective-permute-start.3 = (bf16[256,640]{1,0:T(8,128)(2,1)S(1)}, bf16[256,640]{1,0:T(8,128)(2,1)S(1)}, u32[]{:S(2)}, u32[]{:S(2)}) collective-permute-start(bf16[256,640]{1,0:T(8,128)(2,1)S(1)} %get-tuple-element.48), channel_id=1, source_target_pairs={{0,1},{1,0},{2,3},{3,2},{4,5},{5,4},{6,7},{7,6},{8,9},{9,8},{10,11... | collective-permute-start | bytes 983048 | tf_op jit(solution)/shard_map/ppermute | solution.py:277
  17.0 4.6 %collective-permute-start.4 = (bf16[64,640]{1,0:T(8,128)(2,1)S(1)}, bf16[64,640]{1,0:T(8,128)(2,1)S(1)}, u32[]{:S(2)}, u32[]{:S(2)}) collective-permute-start(bf16[64,640]{1,0:T(8,128)(2,1)S(1)} %get-tuple-element.50), channel_id=1, source_target_pairs={{0,2},{1,3},{2,0},{3,1},{4,6},{5,7},{6,4},{7,5},{8,10},{9,11},{10,... | collective-permute-start | bytes 245768 | tf_op jit(solution)/shard_map/ppermute | solution.py:277
  18.5 5.3 %collective-permute-start.5 = (bf16[64,640]{1,0:T(8,128)(2,1)S(1)}, bf16[64,640]{1,0:T(8,128)(2,1)S(1)}, u32[]{:S(2)}, u32[]{:S(2)}) collective-permute-start(bf16[64,640]{1,0:T(8,128)(2,1)S(1)} %get-tuple-element.51), channel_id=1, source_target_pairs={{0,4},{1,5},{2,6},{3,7},{4,0},{5,1},{6,2},{7,3},{8,12},{9,13},{10,... | collective-permute-start | bytes 245768 | tf_op jit(solution)/shard_map/ppermute | solution.py:277
  20.0 5.3 %collective-permute-start.6 = (bf16[64,640]{1,0:T(8,128)(2,1)S(1)}, bf16[64,640]{1,0:T(8,128)(2,1)S(1)}, u32[]{:S(2)}, u32[]{:S(2)}) collective-permute-start(bf16[64,640]{1,0:T(8,128)(2,1)S(1)} %get-tuple-element.52), channel_id=1, source_target_pairs={{0,6},{1,7},{2,4},{3,5},{4,2},{5,3},{6,0},{7,1},{8,14},{9,15},{10,... | collective-permute-start | bytes 245768 | tf_op jit(solution)/shard_map/ppermute | solution.py:277
  25.5 5.5 %collective-permute-start.9 = (bf16[64,640]{1,0:T(8,128)(2,1)S(1)}, bf16[64,640]{1,0:T(8,128)(2,1)S(1)}, u32[]{:S(2)}, u32[]{:S(2)}) collective-permute-start(bf16[64,640]{1,0:T(8,128)(2,1)S(1)} %shard_map.40), channel_id=1, source_target_pairs={{0,6},{1,7},{2,4},{3,5},{4,2},{5,3},{6,0},{7,1},{8,14},{9,15},{10,... | collective-permute-start | bytes 245768 | tf_op jit(solution)/shard_map/ppermute | solution.py:277
  26.4 5.3 %collective-permute-start.8 = (bf16[64,640]{1,0:T(8,128)(2,1)S(1)}, bf16[64,640]{1,0:T(8,128)(2,1)S(1)}, u32[]{:S(2)}, u32[]{:S(2)}) collective-permute-start(bf16[64,640]{1,0:T(8,128)(2,1)S(1)} %shard_map.40), channel_id=1, source_target_pairs={{0,4},{1,5},{2,6},{3,7},{4,0},{5,1},{6,2},{7,3},{8,12},{9,13},{10,... | collective-permute-start | bytes 245768 | tf_op jit(solution)/shard_map/ppermute | solution.py:277
  27.6 4.4 %collective-permute-start.7 = (bf16[64,640]{1,0:T(8,128)(2,1)S(1)}, bf16[64,640]{1,0:T(8,128)(2,1)S(1)}, u32[]{:S(2)}, u32[]{:S(2)}) collective-permute-start(bf16[64,640]{1,0:T(8,128)(2,1)S(1)} %shard_map.40), channel_id=1, source_target_pairs={{0,2},{1,3},{2,0},{3,1},{4,6},{5,7},{6,4},{7,5},{8,10},{9,11},{10,... | collective-permute-start | bytes 245768 | tf_op jit(solution)/shard_map/ppermute | solution.py:277
  33.2 27.6 %collective-permute-start.20 = (bf16[512,1024]{1,0:T(8,128)(2,1)}, bf16[512,1024]{1,0:T(8,128)(2,1)}, u32[]{:S(2)}, u32[]{:S(2)}) collective-permute-start(bf16[512,1024]{1,0:T(8,128)(2,1)} %z.5), channel_id=1, source_target_pairs={{0,24},{24,0},{1,25},{25,1},{2,26},{26,2},{3,27},{27,3},{4,28},{28... | collective-permute-start | bytes 3145736 | tf_op jit(solution)/shard_map/ppermute | solution.py:342
  39.5 1.6 %collective-permute-start.12 = (bf16[256,512]{1,0:T(8,128)(2,1)S(1)}, bf16[256,512]{1,0:T(8,128)(2,1)S(1)}, u32[]{:S(2)}, u32[]{:S(2)}) collective-permute-start(bf16[256,512]{1,0:T(8,128)(2,1)S(1)} %get-tuple-element.56), channel_id=1, source_target_pairs={{0,1},{1,0},{2,3},{3,2},{4,5},{5,4},{6,7},{7,6},{8,9},{9,8},{10,11... | collective-permute-start | bytes 786440 | tf_op jit(solution)/shard_map/ppermute | solution.py:277
  41.2 4.3 %collective-permute-start.13 = (bf16[64,512]{1,0:T(8,128)(2,1)S(1)}, bf16[64,512]{1,0:T(8,128)(2,1)S(1)}, u32[]{:S(2)}, u32[]{:S(2)}) collective-permute-start(bf16[64,512]{1,0:T(8,128)(2,1)S(1)} %get-tuple-element.58), channel_id=1, source_target_pairs={{0,2},{1,3},{2,0},{3,1},{4,6},{5,7},{6,4},{7,5},{8,10},{9,11},{10,... | collective-permute-start | bytes 196616 | tf_op jit(solution)/shard_map/ppermute | solution.py:277
  42.7 4.3 %collective-permute-start.14 = (bf16[64,512]{1,0:T(8,128)(2,1)S(1)}, bf16[64,512]{1,0:T(8,128)(2,1)S(1)}, u32[]{:S(2)}, u32[]{:S(2)}) collective-permute-start(bf16[64,512]{1,0:T(8,128)(2,1)S(1)} %get-tuple-element.59), channel_id=1, source_target_pairs={{0,4},{1,5},{2,6},{3,7},{4,0},{5,1},{6,2},{7,3},{8,12},{9,13},{10,... | collective-permute-start | bytes 196616 | tf_op jit(solution)/shard_map/ppermute | solution.py:277
  44.3 5.2 %collective-permute-start.15 = (bf16[64,512]{1,0:T(8,128)(2,1)S(1)}, bf16[64,512]{1,0:T(8,128)(2,1)S(1)}, u32[]{:S(2)}, u32[]{:S(2)}) collective-permute-start(bf16[64,512]{1,0:T(8,128)(2,1)S(1)} %get-tuple-element.60), channel_id=1, source_target_pairs={{0,6},{1,7},{2,4},{3,5},{4,2},{5,3},{6,0},{7,1},{8,14},{9,15},{10,... | collective-permute-start | bytes 196616 | tf_op jit(solution)/shard_map/ppermute | solution.py:277
  49.5 4.4 %collective-permute-start.16 = (bf16[64,512]{1,0:T(8,128)(2,1)S(1)}, bf16[64,512]{1,0:T(8,128)(2,1)S(1)}, u32[]{:S(2)}, u32[]{:S(2)}) collective-permute-start(bf16[64,512]{1,0:T(8,128)(2,1)S(1)} %shard_map.43.refs_0_.first), channel_id=1, source_target_pairs={{0,2},{1,3},{2,0},{3,1},{4,6},{5,7},{6,4},{7,5},{8,10},{9,11},{10,... | collective-permute-start | bytes 196616 | tf_op jit(solution)/shard_map/ppermute | solution.py:277
  50.1 4.3 %collective-permute-start.17 = (bf16[64,512]{1,0:T(8,128)(2,1)S(1)}, bf16[64,512]{1,0:T(8,128)(2,1)S(1)}, u32[]{:S(2)}, u32[]{:S(2)}) collective-permute-start(bf16[64,512]{1,0:T(8,128)(2,1)S(1)} %shard_map.43.refs_0_.first), channel_id=1, source_target_pairs={{0,4},{1,5},{2,6},{3,7},{4,0},{5,1},{6,2},{7,3},{8,12},{9,13},{10,... | collective-permute-start | bytes 196616 | tf_op jit(solution)/shard_map/ppermute | solution.py:277
  50.6 5.2 %collective-permute-start.18 = (bf16[64,512]{1,0:T(8,128)(2,1)S(1)}, bf16[64,512]{1,0:T(8,128)(2,1)S(1)}, u32[]{:S(2)}, u32[]{:S(2)}) collective-permute-start(bf16[64,512]{1,0:T(8,128)(2,1)S(1)} %shard_map.43.refs_0_.first), channel_id=1, source_target_pairs={{0,6},{1,7},{2,4},{3,5},{4,2},{5,3},{6,0},{7,1},{8,14},{9,15},{10,... | collective-permute-start | bytes 196616 | tf_op jit(solution)/shard_map/ppermute | solution.py:277
  55.8 1.6 %collective-permute-start.19 = (bf16[256,512]{1,0:T(8,128)(2,1)S(1)}, bf16[256,512]{1,0:T(8,128)(2,1)S(1)}, u32[]{:S(2)}, u32[]{:S(2)}) collective-permute-start(bf16[256,512]{1,0:T(8,128)(2,1)S(1)} %shard_map.45.near), channel_id=1, source_target_pairs={{0,1},{1,0},{2,3},{3,2},{4,5},{5,4},{6,7},{7,6},{8,9},{9,8},{10,11... | collective-permute-start | bytes 786440 | tf_op jit(solution)/shard_map/ppermute | solution.py:277
  60.8 23.1 %collective-permute-start.29 = (bf16[512,1024]{1,0:T(8,128)(2,1)S(1)}, bf16[512,1024]{1,0:T(8,128)(2,1)S(1)}, u32[]{:S(2)}, u32[]{:S(2)}) collective-permute-start(bf16[512,1024]{1,0:T(8,128)(2,1)S(1)} %get-tuple-element.84), channel_id=1, source_target_pairs={{8,16},{16,8},{9,17},{17,9},{10,18},{18,10},{11,19},{19,11},{12,20... | collective-permute-start | bytes 3145736 | tf_op jit(solution)/shard_map/ppermute | solution.py:358
  63.6 2.0 %collective-permute-start.21 = (bf16[256,1024]{1,0:T(8,128)(2,1)S(1)}, bf16[256,1024]{1,0:T(8,128)(2,1)S(1)}, u32[]{:S(2)}, u32[]{:S(2)}) collective-permute-start(bf16[256,1024]{1,0:T(8,128)(2,1)S(1)} %get-tuple-element.74), channel_id=1, source_target_pairs={{0,1},{1,0},{2,3},{3,2},{4,5},{5,4},{6,7},{7,6},{8,9},{9,8},{10,11... | collective-permute-start | bytes 1572872 | tf_op jit(solution)/shard_map/ppermute | solution.py:277
  63.7 5.0 %collective-permute-start.25 = (bf16[256,640]{1,0:T(8,128)(2,1)S(1)}, bf16[256,640]{1,0:T(8,128)(2,1)S(1)}, u32[]{:S(2)}, u32[]{:S(2)}) collective-permute-start(bf16[256,640]{1,0:T(8,128)(2,1)S(1)} %pad_maximum_fusion.near), channel_id=1, source_target_pairs={{0,1},{1,0},{2,3},{3,2},{4,5},{5,4},{6,7},{7,6},{8,9},{9,8},{10,11... | collective-permute-start | bytes 983048 | tf_op jit(solution)/shard_map/ppermute | solution.py:277
  64.2 27.0 %collective-permute-start.31 = (bf16[512,1024]{1,0:T(8,128)(2,1)S(1)}, bf16[512,1024]{1,0:T(8,128)(2,1)S(1)}, u32[]{:S(2)}, u32[]{:S(2)}) collective-permute-start(bf16[512,1024]{1,0:T(8,128)(2,1)S(1)} %get-tuple-element.69), channel_id=1, source_target_pairs={{8,0},{16,24},{9,1},{17,25},{10,2},{18,26},{11,3},{19,27},{12,4},{... | collective-permute-start | bytes 3145736 | tf_op jit(solution)/shard_map/ppermute | solution.py:358
  65.6 6.2 %collective-permute-start.22 = (bf16[64,1024]{1,0:T(8,128)(2,1)S(1)}, bf16[64,1024]{1,0:T(8,128)(2,1)S(1)}, u32[]{:S(2)}, u32[]{:S(2)}) collective-permute-start(bf16[64,1024]{1,0:T(8,128)(2,1)S(1)} %get-tuple-element.76), channel_id=1, source_target_pairs={{0,2},{1,3},{2,0},{3,1},{4,6},{5,7},{6,4},{7,5},{8,10},{9,11},{10,... | collective-permute-start | bytes 393224 | tf_op jit(solution)/shard_map/ppermute | solution.py:277
  67.2 8.1 %collective-permute-start.23 = (bf16[64,1024]{1,0:T(8,128)(2,1)S(1)}, bf16[64,1024]{1,0:T(8,128)(2,1)S(1)}, u32[]{:S(2)}, u32[]{:S(2)}) collective-permute-start(bf16[64,1024]{1,0:T(8,128)(2,1)S(1)} %get-tuple-element.77), channel_id=1, source_target_pairs={{0,4},{1,5},{2,6},{3,7},{4,0},{5,1},{6,2},{7,3},{8,12},{9,13},{10,... | collective-permute-start | bytes 393224 | tf_op jit(solution)/shard_map/ppermute | solution.py:277
  68.7 6.5 %collective-permute-start.24 = (bf16[64,1024]{1,0:T(8,128)(2,1)S(1)}, bf16[64,1024]{1,0:T(8,128)(2,1)S(1)}, u32[]{:S(2)}, u32[]{:S(2)}) collective-permute-start(bf16[64,1024]{1,0:T(8,128)(2,1)S(1)} %get-tuple-element.78), channel_id=1, source_target_pairs={{0,6},{1,7},{2,4},{3,5},{4,2},{5,3},{6,0},{7,1},{8,14},{9,15},{10,... | collective-permute-start | bytes 393224 | tf_op jit(solution)/shard_map/ppermute | solution.py:277
  75.3 6.0 %collective-permute-start.26 = (bf16[64,1024]{1,0:T(8,128)(2,1)S(1)}, bf16[64,1024]{1,0:T(8,128)(2,1)S(1)}, u32[]{:S(2)}, u32[]{:S(2)}) collective-permute-start(bf16[64,1024]{1,0:T(8,128)(2,1)S(1)} %shard_map.49.refs_0_), channel_id=1, source_target_pairs={{0,2},{1,3},{2,0},{3,1},{4,6},{5,7},{6,4},{7,5},{8,10},{9,11},{10,... | collective-permute-start | bytes 393224 | tf_op jit(solution)/shard_map/ppermute | solution.py:277
  76.6 7.2 %collective-permute-start.27 = (bf16[64,1024]{1,0:T(8,128)(2,1)S(1)}, bf16[64,1024]{1,0:T(8,128)(2,1)S(1)}, u32[]{:S(2)}, u32[]{:S(2)}) collective-permute-start(bf16[64,1024]{1,0:T(8,128)(2,1)S(1)} %shard_map.49.refs_0_), channel_id=1, source_target_pairs={{0,4},{1,5},{2,6},{3,7},{4,0},{5,1},{6,2},{7,3},{8,12},{9,13},{10,... | collective-permute-start | bytes 393224 | tf_op jit(solution)/shard_map/ppermute | solution.py:277
  77.4 6.4 %collective-permute-start.28 = (bf16[64,1024]{1,0:T(8,128)(2,1)S(1)}, bf16[64,1024]{1,0:T(8,128)(2,1)S(1)}, u32[]{:S(2)}, u32[]{:S(2)}) collective-permute-start(bf16[64,1024]{1,0:T(8,128)(2,1)S(1)} %shard_map.49.refs_0_), channel_id=1, source_target_pairs={{0,6},{1,7},{2,4},{3,5},{4,2},{5,3},{6,0},{7,1},{8,14},{9,15},{10,... | collective-permute-start | bytes 393224 | tf_op jit(solution)/shard_map/ppermute | solution.py:277
  83.9 7.3 %collective-permute-start.30 = (bf16[256,1024]{1,0:T(8,128)(2,1)S(1)}, bf16[256,1024]{1,0:T(8,128)(2,1)S(1)}, u32[]{:S(2)}, u32[]{:S(2)}) collective-permute-start(bf16[256,1024]{1,0:T(8,128)(2,1)S(1)} %shard_map.51.near), channel_id=1, source_target_pairs={{0,1},{1,0},{2,3},{3,2},{4,5},{5,4},{6,7},{7,6},{8,9},{9,8},{10,11... | collective-permute-start | bytes 1572872 | tf_op jit(solution)/shard_map/ppermute | solution.py:277
  (1 other events, 7.7 us)

commit v22 on v20

--- a/solution.py
+++ b/solution.py
@@ -117,22 +117,18 @@
 
 def first_kernel(
     order, middle, turned, beside_in, opposite_in, mean,
-    beside, beside_square, opposite, opposite_square, kept, sent, turned_beside, landed, sem,
+    beside, beside_square, opposite, opposite_square, kept, sent, turned_beside,
 ):
-    copies = pieces_in(opposite_in, landed, sem)
+    centered_into(beside, beside_in, mean[...], beside_square)
 
     @pl.when(middle[0] == 1)
     def _():
-        for copy in copies:
-            copy.start()
-        centered_into(beside, beside_in, mean[...], beside_square)
+        centered_into(opposite, opposite_in, mean[...], opposite_square)
         turn_into(turned_beside, order, beside)
-        centered_pieces(opposite, copies, landed, mean[...], opposite_square)
         split_sum(gram(turned_beside[...], opposite[...]), kept, sent, slice(None))
 
     @pl.when(middle[0] == 0)
     def _():
-        centered_into(beside, beside_in, mean[...], beside_square)
         split_sum(gram(turned[...], beside[...]), kept, sent, slice(None))
 
 
@@ -376,7 +372,7 @@
 
     beside, beside_square, swapped, swapped_square, kept, sent = kernel_call(
         first_kernel, [block, flat, block, flat, *summands(rows)],
-        smem=2, scratch=12, temps=[block, block], sems=4, outside=4,
+        smem=2, scratch=12, temps=[block],
     )(order, middle, after(turned, near_own), beside_in, swapped, mean)
     first = scatter(*halve(kept, sent))
     kept_early, sent_early = kernel_call(
@@ -386,7 +382,7 @@
     near = after(gather_chips(first), sent_early)
     ready = kernel_call(
         push_kernel, [block, block], smem=2, scratch=12, temps=[((rows, rows), jnp.bfloat16)]
-    )(order, middle, near, after(to_partner(near, 1), far_own), beside, swapped, beside_square, swapped_square)
+    )(order, middle, near, to_partner(near, 1), beside, swapped, beside_square, swapped_square)
     out, over = ready
     pushed = [
         lax.ppermute(out, "dp", outward), lax.ppermute(after(over, end), "dp", across)

time: 92.5 us -> 90.3 us (0.976)
  waiting for transfers between devices: 34.2 us -> 32.3 us
    ppermute x1, waiting for transfers between devices: 4.9 us -> 1.89 us  [by_line(): swapped = lax.ppermute(ahead, 'dp', across)]
    ppermute x1, waiting for transfers between devices: 0.1 us -> 1.64 us  [by_line(): beside_in = lax.ppermute(ahead, 'dp', [(i, i ^ 1) for i in range(4)])]
    ppermute x1, starting transfers between devices: 2.94 us -> 1.44 us  [by_line(): lax.ppermute(out, 'dp', outward)]
    ppermute x1, starting transfers between devices: 1.91 us -> 3.08 us  [by_line(): swapped = lax.ppermute(ahead, 'dp', across)]
  transfers between devices with their start and end apart: 32 -> 32, of which waited for: 21 -> 22; matrix products, arithmetic and copies ran while one was open for 1% -> 1% of each run, Pallas kernels for 13% -> 12%
where the time goes in v22:
time: 90.3 us; the launch traced here: 89 us
  starting transfers between devices  40 us (44%)
  waiting for transfers between devices  32.3 us (36%)
  Pallas kernels  15.7 us (17%)
    ppermute x24, starting transfers between devices, to_partner(): return lax.ppermute(x, 'feat', [(i, i ^ step) for i in range(8)])  26.3 us
    ppermute x24, waiting for transfers between devices, to_partner(): return lax.ppermute(x, 'feat', [(i, i ^ step) for i in range(8)])  21.8 us
    pallas_call x16, Pallas kernels, call(): pl.pallas_call(body, out_shape=[jax.ShapeDtypeStruct(s, t) for s, t in ou...  15.7 us
    ppermute x3, starting transfers between devices, by_line(): lax.ppermute(stats, 'dp', [(i, (i + k) % 4) for i in range(4)])  4.72 us
    ppermute x1, waiting for transfers between devices, by_line(): lax.ppermute(after(over, end), 'dp', across)  3.81 us
    ppermute x1, waiting for transfers between devices, by_line(): lax.ppermute(out, 'dp', outward)  3.16 us
    ppermute x1, starting transfers between devices, by_line(): swapped = lax.ppermute(ahead, 'dp', across)  3.08 us
    ppermute x1, starting transfers between devices, by_line(): lax.ppermute(after(over, end), 'dp', across)  2.77 us
  transfers between devices with their start and end apart: 32, of which 22 were waited for; matrix products, arithmetic and copies ran while one was open for 1% of the time, Pallas kernels for 12%

profile of v22, /device:TPU:9, one launch (start us, length us, event | category | flops | bytes accessed | tf_op | source)
XLA Modules:
  0.0 89.0 jit_solution(12658677436861376999)
XLA Ops:
  0.0 1.8 %shard_map.37 = f32[2,1024]{1,0:T(2,128)S(1)} custom-call(bf16[512,1024]{1,0:T(8,128)(2,1)} %z.5), custom_call_target="tpu_custom_call" | custom-call | tf_op jit(solution)/shard_map/pallas_call | solution.py:19
  1.9 2.5 %collective-permute-start.1 = (f32[2,1024]{1,0:T(2,128)S(1)}, f32[2,1024]{1,0:T(2,128)S(1)}, u32[]{:S(2)}, u32[]{:S(2)}) collective-permute-start(f32[2,1024]{1,0:T(2,128)S(1)} %shard_map.37), channel_id=1, source_target_pairs={{0,16},{8,24},{16,0},{24,8},{1,17},{9,25},{17,1},{25,9},{2,18},{10... | collective-permute-start | bytes 24584 | tf_op jit(solution)/shard_map/ppermute | solution.py:352
  4.3 2.2 %collective-permute-start = (f32[2,1024]{1,0:T(2,128)S(1)}, f32[2,1024]{1,0:T(2,128)S(1)}, u32[]{:S(2)}, u32[]{:S(2)}) collective-permute-start(f32[2,1024]{1,0:T(2,128)S(1)} %shard_map.37), channel_id=1, source_target_pairs={{0,8},{8,16},{16,24},{24,0},{1,9},{9,17},{17,25},{25,1},{2,10},{10... | collective-permute-start | bytes 24584 | tf_op jit(solution)/shard_map/ppermute | solution.py:352
  6.5 3.1 %collective-permute-start.11 = (bf16[512,1024]{1,0:T(8,128)(2,1)}, bf16[512,1024]{1,0:T(8,128)(2,1)}, u32[]{:S(2)}, u32[]{:S(2)}) collective-permute-start(bf16[512,1024]{1,0:T(8,128)(2,1)} %z.5), channel_id=1, source_target_pairs={{8,16},{16,8},{9,17},{17,9},{10,18},{18,10},{11,19},{19,11},{12,20... | collective-permute-start | bytes 3145736 | tf_op jit(solution)/shard_map/ppermute | solution.py:356
  10.4 2.4 %shard_map.38 = (bf16[512,1024]{1,0:T(8,128)(2,1)S(1)}, bf16[512,1024]{1,0:T(8,128)(2,1)S(1)}, f32[1,1024]{1,0:T(1,128)S(1)}, f32[256,640]{1,0:T(8,128)S(1)}, bf16[256,640]{1,0:T(8,128)(2,1)S(1)}) custom-call(s32[8]{0:T(128)S(1)} %broadcast_xor_fusion.order, bf16[512,1024]{1,0:T(8,128)(2,1)} %z.5, f32[1,1024]{1,0:T(1,128)S(1)} %get-tuple-element.88.mean), custom_call_target="tpu_custom_call" | custom-call | tf_op jit(solution)/shard_map/pallas_call | solution.py:19
  12.7 1.9 %collective-permute-start.3 = (bf16[256,640]{1,0:T(8,128)(2,1)S(1)}, bf16[256,640]{1,0:T(8,128)(2,1)S(1)}, u32[]{:S(2)}, u32[]{:S(2)}) collective-permute-start(bf16[256,640]{1,0:T(8,128)(2,1)S(1)} %get-tuple-element.48), channel_id=1, source_target_pairs={{0,1},{1,0},{2,3},{3,2},{4,5},{5,4},{6,7},{7,6},{8,9},{9,8},{10,11... | collective-permute-start | bytes 983048 | tf_op jit(solution)/shard_map/ppermute | solution.py:306
  14.6 1.3 %collective-permute-done.3.got = bf16[256,640]{1,0:T(8,128)(2,1)S(1)} collective-permute-done((bf16[256,640]{1,0:T(8,128)(2,1)S(1)}, bf16[256,640]{1,0:T(8,128)(2,1)S(1)}, u32[]{:S(2)}, u32[]{:S(2)}) %collective-permute-start.3) | collective-permute-done | bytes 327712 | tf_op jit(solution)/shard_map/ppermute | solution.py:306
  16.0 1.3 %collective-permute-start.4 = (bf16[64,640]{1,0:T(8,128)(2,1)S(1)}, bf16[64,640]{1,0:T(8,128)(2,1)S(1)}, u32[]{:S(2)}, u32[]{:S(2)}) collective-permute-start(bf16[64,640]{1,0:T(8,128)(2,1)S(1)} %get-tuple-element.50), channel_id=1, source_target_pairs={{0,2},{1,3},{2,0},{3,1},{4,6},{5,7},{6,4},{7,5},{8,10},{9,11},{10,... | collective-permute-start | bytes 245768 | tf_op jit(solution)/shard_map/ppermute | solution.py:306
  20.9 1.7 %collective-permute-done.6.c = bf16[64,640]{1,0:T(8,128)(2,1)S(1)} collective-permute-done((bf16[64,640]{1,0:T(8,128)(2,1)S(1)}, bf16[64,640]{1,0:T(8,128)(2,1)S(1)}, u32[]{:S(2)}, u32[]{:S(2)}) %collective-permute-start.6) | collective-permute-done | bytes 81952 | tf_op jit(solution)/shard_map/ppermute | solution.py:306
  25.5 1.6 %collective-permute-done.9 = bf16[64,640]{1,0:T(8,128)(2,1)S(1)} collective-permute-done((bf16[64,640]{1,0:T(8,128)(2,1)S(1)}, bf16[64,640]{1,0:T(8,128)(2,1)S(1)}, u32[]{:S(2)}, u32[]{:S(2)}) %collective-permute-start.9) | collective-permute-done | bytes 81952 | tf_op jit(solution)/shard_map/ppermute | solution.py:306
  28.4 1.6 %collective-permute-done.10.beside_in = bf16[512,1024]{1,0:T(8,128)(2,1)S(1)} collective-permute-done((bf16[512,1024]{1,0:T(8,128)(2,1)}, bf16[512,1024]{1,0:T(8,128)(2,1)S(1)}, u32[]{:S(2)}, u32[]{:S(2)}) %collective-permute-start.10) | collective-permute-done | bytes 1048608 | tf_op jit(solution)/shard_map/ppermute | solution.py:355
  30.0 1.9 %collective-permute-done.11.opposite_in = bf16[512,1024]{1,0:T(8,128)(2,1)} collective-permute-done((bf16[512,1024]{1,0:T(8,128)(2,1)}, bf16[512,1024]{1,0:T(8,128)(2,1)}, u32[]{:S(2)}, u32[]{:S(2)}) %collective-permute-start.11) | collective-permute-done | bytes 1048608 | tf_op jit(solution)/shard_map/ppermute | solution.py:356
  31.9 1.6 %collective-permute-start.20 = (bf16[512,1024]{1,0:T(8,128)(2,1)}, bf16[512,1024]{1,0:T(8,128)(2,1)}, u32[]{:S(2)}, u32[]{:S(2)}) collective-permute-start(bf16[512,1024]{1,0:T(8,128)(2,1)} %z.5), channel_id=1, source_target_pairs={{0,24},{24,0},{1,25},{25,1},{2,26},{26,2},{3,27},{27,3},{4,28},{28... | collective-permute-start | bytes 3145736 | tf_op jit(solution)/shard_map/ppermute | solution.py:371
  33.5 2.2 %shard_map.41 = (bf16[512,1024]{1,0:T(8,128)(2,1)S(1)}, f32[1,1024]{1,0:T(1,128)S(1)}, bf16[512,1024]{1,0:T(8,128)(2,1)S(1)}, f32[1,1024]{1,0:T(1,128)S(1)}, f32...) custom-call(s32[8]{0:T(128)S(1)} %broadcast_xor_fusion.order, s32[1]{0:T(128)} %bitcast.middle, ...), custom_call_target="tpu_custom_call" | custom-call | tf_op jit(solution)/shard_map/pallas_call | solution.py:19
  35.7 2.5 %collective-permute-start.12 = (bf16[256,512]{1,0:T(8,128)(2,1)S(1)}, bf16[256,512]{1,0:T(8,128)(2,1)S(1)}, u32[]{:S(2)}, u32[]{:S(2)}) collective-permute-start(bf16[256,512]{1,0:T(8,128)(2,1)S(1)} %get-tuple-element.56), channel_id=1, source_target_pairs={{0,1},{1,0},{2,3},{3,2},{4,5},{5,4},{6,7},{7,6},{8,9},{9,8},{10,11... | collective-permute-start | bytes 786440 | tf_op jit(solution)/shard_map/ppermute | solution.py:306
  39.5 1.3 %collective-permute-start.13 = (bf16[64,512]{1,0:T(8,128)(2,1)S(1)}, bf16[64,512]{1,0:T(8,128)(2,1)S(1)}, u32[]{:S(2)}, u32[]{:S(2)}) collective-permute-start(bf16[64,512]{1,0:T(8,128)(2,1)S(1)} %get-tuple-element.58), channel_id=1, source_target_pairs={{0,2},{1,3},{2,0},{3,1},{4,6},{5,7},{6,4},{7,5},{8,10},{9,11},{10,... | collective-permute-start | bytes 196616 | tf_op jit(solution)/shard_map/ppermute | solution.py:306
  43.9 2.1 %collective-permute-done.15.c = bf16[64,512]{1,0:T(8,128)(2,1)S(1)} collective-permute-done((bf16[64,512]{1,0:T(8,128)(2,1)S(1)}, bf16[64,512]{1,0:T(8,128)(2,1)S(1)}, u32[]{:S(2)}, u32[]{:S(2)}) %collective-permute-start.15) | collective-permute-done | bytes 65568 | tf_op jit(solution)/shard_map/ppermute | solution.py:306
  46.7 2.0 %collective-permute-start.18 = (bf16[64,512]{1,0:T(8,128)(2,1)S(1)}, bf16[64,512]{1,0:T(8,128)(2,1)S(1)}, u32[]{:S(2)}, u32[]{:S(2)}) collective-permute-start(bf16[64,512]{1,0:T(8,128)(2,1)S(1)} %shard_map.43.refs_0_.first), channel_id=1, source_target_pairs={{0,6},{1,7},{2,4},{3,5},{4,2},{5,3},{6,0},{7,1},{8,14},{9,15},{10,... | collective-permute-start | bytes 196616 | tf_op jit(solution)/shard_map/ppermute | solution.py:306
  48.7 1.3 %shard_map.44 = (f32[256,1024]{1,0:T(8,128)S(1)}, bf16[256,1024]{1,0:T(8,128)(2,1)S(1)}) custom-call(s32[1]{0:T(128)} %bitcast.middle, bf16[512,1024]{1,0:T(8,128)(2,1)S(1)} %get-tuple-element.71.turned, bf16[512,1024]{1,0:T(8,128)(2,1)S(1)} %get-tuple-element.62.beside, bf16[512,1024]{1,0:T(8,128)(2,1)S(1)} %get-tuple-element.63.opposite.swapped), custom_call_target="tpu_custom_call" | custom-call | tf_op jit(solution)/shard_map/pallas_call | solution.py:19
  50.8 3.7 %collective-permute-start.19 = (bf16[256,512]{1,0:T(8,128)(2,1)S(1)}, bf16[256,512]{1,0:T(8,128)(2,1)S(1)}, u32[]{:S(2)}, u32[]{:S(2)}) collective-permute-start(bf16[256,512]{1,0:T(8,128)(2,1)S(1)} %shard_map.45.near), channel_id=1, source_target_pairs={{0,1},{1,0},{2,3},{3,2},{4,5},{5,4},{6,7},{7,6},{8,9},{9,8},{10,11... | collective-permute-start | bytes 786440 | tf_op jit(solution)/shard_map/ppermute | solution.py:306
  55.6 1.8 %shard_map.46 = (bf16[512,1024]{1,0:T(8,128)(2,1)S(1)}, bf16[512,1024]{1,0:T(8,128)(2,1)S(1)}) custom-call(s32[8]{0:T(128)S(1)} %broadcast_xor_fusion.order, s32[1]{0:T(128)} %bitcast.middle, bf16[256,512]{1,0:T(8,128)(2,1)S(1)} %shard_map.45.near, bf16[256,512]{1,0:T(8,128)(2,1)S(1)} %collective-permute-done.19.far, ...), custom_call_target="tpu_custom_call" | custom-call | tf_op jit(solution)/shard_map/pallas_call | solution.py:19
  57.5 1.4 %collective-permute-start.29 = (bf16[512,1024]{1,0:T(8,128)(2,1)S(1)}, bf16[512,1024]{1,0:T(8,128)(2,1)S(1)}, u32[]{:S(2)}, u32[]{:S(2)}) collective-permute-start(bf16[512,1024]{1,0:T(8,128)(2,1)S(1)} %get-tuple-element.69), channel_id=1, source_target_pairs={{8,0},{16,24},{9,1},{17,25},{10,2},{18,26},{11,3},{19,27},{12,4},{... | collective-permute-start | bytes 3145736 | tf_op jit(solution)/shard_map/ppermute | solution.py:388
  59.8 2.8 %collective-permute-start.31 = (bf16[512,1024]{1,0:T(8,128)(2,1)S(1)}, bf16[512,1024]{1,0:T(8,128)(2,1)S(1)}, u32[]{:S(2)}, u32[]{:S(2)}) collective-permute-start(bf16[512,1024]{1,0:T(8,128)(2,1)S(1)} %get-tuple-element.86), channel_id=1, source_target_pairs={{8,16},{16,8},{9,17},{17,9},{10,18},{18,10},{11,19},{19,11},{12,20... | collective-permute-start | bytes 3145736 | tf_op jit(solution)/shard_map/ppermute | solution.py:388
  62.7 1.3 %collective-permute-start.22 = (bf16[64,1024]{1,0:T(8,128)(2,1)S(1)}, bf16[64,1024]{1,0:T(8,128)(2,1)S(1)}, u32[]{:S(2)}, u32[]{:S(2)}) collective-permute-start(bf16[64,1024]{1,0:T(8,128)(2,1)S(1)} %get-tuple-element.76), channel_id=1, source_target_pairs={{0,2},{1,3},{2,0},{3,1},{4,6},{5,7},{6,4},{7,5},{8,10},{9,11},{10,... | collective-permute-start | bytes 393224 | tf_op jit(solution)/shard_map/ppermute | solution.py:306
  65.4 2.6 %shard_map.50.held = f32[512,1024]{1,0:T(8,128)S(1)} custom-call(s32[8]{0:T(128)S(1)} %broadcast_xor_fusion.order, s32[1]{0:T(128)} %bitcast.middle, bf16[256,640]{1,0:T(8,128)(2,1)S(1)} %pad_maximum_fusion.near, bf16[256,640]{1,0:T(8,128)(2,1)S(1)} %collective-permute-done.25.far, bf16[512,1024]{1,0:T(8,128)(2,1)S(1)} %get-tuple-element.79.own, ...), custom_call_target="tpu_custom_call" | custom-call | tf_op jit(solution)/shard_map/pallas_call | solution.py:19
  68.1 2.7 %collective-permute-done.24.c = bf16[64,1024]{1,0:T(8,128)(2,1)S(1)} collective-permute-done((bf16[64,1024]{1,0:T(8,128)(2,1)S(1)}, bf16[64,1024]{1,0:T(8,128)(2,1)S(1)}, u32[]{:S(2)}, u32[]{:S(2)}) %collective-permute-start.24) | collective-permute-done | bytes 131104 | tf_op jit(solution)/shard_map/ppermute | solution.py:306
  70.9 1.4 %collective-permute-start.26 = (bf16[64,1024]{1,0:T(8,128)(2,1)S(1)}, bf16[64,1024]{1,0:T(8,128)(2,1)S(1)}, u32[]{:S(2)}, u32[]{:S(2)}) collective-permute-start(bf16[64,1024]{1,0:T(8,128)(2,1)S(1)} %shard_map.49.refs_0_), channel_id=1, source_target_pairs={{0,2},{1,3},{2,0},{3,1},{4,6},{5,7},{6,4},{7,5},{8,10},{9,11},{10,... | collective-permute-start | bytes 393224 | tf_op jit(solution)/shard_map/ppermute | solution.py:306
  73.6 1.5 %collective-permute-done.26.refs_1_ = bf16[64,1024]{1,0:T(8,128)(2,1)S(1)} collective-permute-done((bf16[64,1024]{1,0:T(8,128)(2,1)S(1)}, bf16[64,1024]{1,0:T(8,128)(2,1)S(1)}, u32[]{:S(2)}, u32[]{:S(2)}) %collective-permute-start.26) | collective-permute-done | bytes 131104 | tf_op jit(solution)/shard_map/ppermute | solution.py:306
  75.0 2.6 %collective-permute-done.27.refs_2_ = bf16[64,1024]{1,0:T(8,128)(2,1)S(1)} collective-permute-done((bf16[64,1024]{1,0:T(8,128)(2,1)S(1)}, bf16[64,1024]{1,0:T(8,128)(2,1)S(1)}, u32[]{:S(2)}, u32[]{:S(2)}) %collective-permute-start.27) | collective-permute-done | bytes 131104 | tf_op jit(solution)/shard_map/ppermute | solution.py:306
  77.8 3.2 %collective-permute-done.29.out = bf16[512,1024]{1,0:T(8,128)(2,1)S(1)} collective-permute-done((bf16[512,1024]{1,0:T(8,128)(2,1)S(1)}, bf16[512,1024]{1,0:T(8,128)(2,1)S(1)}, u32[]{:S(2)}, u32[]{:S(2)}) %collective-permute-start.29) | collective-permute-done | bytes 1048608 | tf_op jit(solution)/shard_map/ppermute | solution.py:388
  82.2 3.8 %collective-permute-done.31.over = bf16[512,1024]{1,0:T(8,128)(2,1)S(1)} collective-permute-done((bf16[512,1024]{1,0:T(8,128)(2,1)S(1)}, bf16[512,1024]{1,0:T(8,128)(2,1)S(1)}, u32[]{:S(2)}, u32[]{:S(2)}) %collective-permute-start.31) | collective-permute-done | bytes 1048608 | tf_op jit(solution)/shard_map/ppermute | solution.py:388
  86.0 3.0 %shard_map.52 = f32[512,1024]{1,0:T(8,128)} custom-call(s32[8]{0:T(128)S(1)} %broadcast_xor_fusion.order, s32[1]{0:T(128)} %bitcast.middle, bf16[256,1024]{1,0:T(8,128)(2,1)S(1)} %shard_map.51.near, bf16[256,1024]{1,0:T(8,128)(2,1)S(1)} %collective-permute-done.30.far, bf16[512,1024]{1,0:T(8,128)(2,1)S(1)} %get-tuple-element.62.beside, ...), custom_call_target="tpu_custom_call" | custom-call | tf_op jit(solution)/shard_map/pallas_call | solution.py:19
  (53 shorter events, 20.8 us)
Async XLA Ops:
  1.8 8.5 %collective-permute-start.2 = (f32[2,1024]{1,0:T(2,128)S(1)}, f32[2,1024]{1,0:T(2,128)S(1)}, u32[]{:S(2)}, u32[]{:S(2)}) collective-permute-start(f32[2,1024]{1,0:T(2,128)S(1)} %shard_map.37), channel_id=1, source_target_pairs={{0,24},{8,0},{16,8},{24,16},{1,25},{9,1},{17,9},{25,17},{2,26},{10... | collective-permute-start | bytes 24584 | tf_op jit(solution)/shard_map/ppermute | solution.py:352
  1.9 8.4 %collective-permute-start.1 = (f32[2,1024]{1,0:T(2,128)S(1)}, f32[2,1024]{1,0:T(2,128)S(1)}, u32[]{:S(2)}, u32[]{:S(2)}) collective-permute-start(f32[2,1024]{1,0:T(2,128)S(1)} %shard_map.37), channel_id=1, source_target_pairs={{0,16},{8,24},{16,0},{24,8},{1,17},{9,25},{17,1},{25,9},{2,18},{10... | collective-permute-start | bytes 24584 | tf_op jit(solution)/shard_map/ppermute | solution.py:352
  4.3 6.0 %collective-permute-start = (f32[2,1024]{1,0:T(2,128)S(1)}, f32[2,1024]{1,0:T(2,128)S(1)}, u32[]{:S(2)}, u32[]{:S(2)}) collective-permute-start(f32[2,1024]{1,0:T(2,128)S(1)} %shard_map.37), channel_id=1, source_target_pairs={{0,8},{8,16},{16,24},{24,0},{1,9},{9,17},{17,25},{25,1},{2,10},{10... | collective-permute-start | bytes 24584 | tf_op jit(solution)/shard_map/ppermute | solution.py:352
  6.5 23.4 %collective-permute-start.10 = (bf16[512,1024]{1,0:T(8,128)(2,1)}, bf16[512,1024]{1,0:T(8,128)(2,1)S(1)}, u32[]{:S(2)}, u32[]{:S(2)}) collective-permute-start(bf16[512,1024]{1,0:T(8,128)(2,1)} %z.5), channel_id=1, source_target_pairs={{0,8},{8,0},{16,24},{24,16},{1,9},{9,1},{17,25},{25,17},{2,10},{10... | collective-permute-start | bytes 3145736 | tf_op jit(solution)/shard_map/ppermute | solution.py:355
  6.5 25.3 %collective-permute-start.11 = (bf16[512,1024]{1,0:T(8,128)(2,1)}, bf16[512,1024]{1,0:T(8,128)(2,1)}, u32[]{:S(2)}, u32[]{:S(2)}) collective-permute-start(bf16[512,1024]{1,0:T(8,128)(2,1)} %z.5), channel_id=1, source_target_pairs={{8,16},{16,8},{9,17},{17,9},{10,18},{18,10},{11,19},{19,11},{12,20... | collective-permute-start | bytes 3145736 | tf_op jit(solution)/shard_map/ppermute | solution.py:356
  12.7 3.1 %collective-permute-start.3 = (bf16[256,640]{1,0:T(8,128)(2,1)S(1)}, bf16[256,640]{1,0:T(8,128)(2,1)S(1)}, u32[]{:S(2)}, u32[]{:S(2)}) collective-permute-start(bf16[256,640]{1,0:T(8,128)(2,1)S(1)} %get-tuple-element.48), channel_id=1, source_target_pairs={{0,1},{1,0},{2,3},{3,2},{4,5},{5,4},{6,7},{7,6},{8,9},{9,8},{10,11... | collective-permute-start | bytes 983048 | tf_op jit(solution)/shard_map/ppermute | solution.py:306
  16.0 3.8 %collective-permute-start.4 = (bf16[64,640]{1,0:T(8,128)(2,1)S(1)}, bf16[64,640]{1,0:T(8,128)(2,1)S(1)}, u32[]{:S(2)}, u32[]{:S(2)}) collective-permute-start(bf16[64,640]{1,0:T(8,128)(2,1)S(1)} %get-tuple-element.50), channel_id=1, source_target_pairs={{0,2},{1,3},{2,0},{3,1},{4,6},{5,7},{6,4},{7,5},{8,10},{9,11},{10,... | collective-permute-start | bytes 245768 | tf_op jit(solution)/shard_map/ppermute | solution.py:306
  17.3 3.7 %collective-permute-start.5 = (bf16[64,640]{1,0:T(8,128)(2,1)S(1)}, bf16[64,640]{1,0:T(8,128)(2,1)S(1)}, u32[]{:S(2)}, u32[]{:S(2)}) collective-permute-start(bf16[64,640]{1,0:T(8,128)(2,1)S(1)} %get-tuple-element.51), channel_id=1, source_target_pairs={{0,4},{1,5},{2,6},{3,7},{4,0},{5,1},{6,2},{7,3},{8,12},{9,13},{10,... | collective-permute-start | bytes 245768 | tf_op jit(solution)/shard_map/ppermute | solution.py:306
  18.5 4.2 %collective-permute-start.6 = (bf16[64,640]{1,0:T(8,128)(2,1)S(1)}, bf16[64,640]{1,0:T(8,128)(2,1)S(1)}, u32[]{:S(2)}, u32[]{:S(2)}) collective-permute-start(bf16[64,640]{1,0:T(8,128)(2,1)S(1)} %get-tuple-element.52), channel_id=1, source_target_pairs={{0,6},{1,7},{2,4},{3,5},{4,2},{5,3},{6,0},{7,1},{8,14},{9,15},{10,... | collective-permute-start | bytes 245768 | tf_op jit(solution)/shard_map/ppermute | solution.py:306
  22.8 4.4 %collective-permute-start.9 = (bf16[64,640]{1,0:T(8,128)(2,1)S(1)}, bf16[64,640]{1,0:T(8,128)(2,1)S(1)}, u32[]{:S(2)}, u32[]{:S(2)}) collective-permute-start(bf16[64,640]{1,0:T(8,128)(2,1)S(1)} %shard_map.40), channel_id=1, source_target_pairs={{0,6},{1,7},{2,4},{3,5},{4,2},{5,3},{6,0},{7,1},{8,14},{9,15},{10,... | collective-permute-start | bytes 245768 | tf_op jit(solution)/shard_map/ppermute | solution.py:306
  23.4 4.6 %collective-permute-start.8 = (bf16[64,640]{1,0:T(8,128)(2,1)S(1)}, bf16[64,640]{1,0:T(8,128)(2,1)S(1)}, u32[]{:S(2)}, u32[]{:S(2)}) collective-permute-start(bf16[64,640]{1,0:T(8,128)(2,1)S(1)} %shard_map.40), channel_id=1, source_target_pairs={{0,4},{1,5},{2,6},{3,7},{4,0},{5,1},{6,2},{7,3},{8,12},{9,13},{10,... | collective-permute-start | bytes 245768 | tf_op jit(solution)/shard_map/ppermute | solution.py:306
  24.6 3.7 %collective-permute-start.7 = (bf16[64,640]{1,0:T(8,128)(2,1)S(1)}, bf16[64,640]{1,0:T(8,128)(2,1)S(1)}, u32[]{:S(2)}, u32[]{:S(2)}) collective-permute-start(bf16[64,640]{1,0:T(8,128)(2,1)S(1)} %shard_map.40), channel_id=1, source_target_pairs={{0,2},{1,3},{2,0},{3,1},{4,6},{5,7},{6,4},{7,5},{8,10},{9,11},{10,... | collective-permute-start | bytes 245768 | tf_op jit(solution)/shard_map/ppermute | solution.py:306
  31.9 27.0 %collective-permute-start.20 = (bf16[512,1024]{1,0:T(8,128)(2,1)}, bf16[512,1024]{1,0:T(8,128)(2,1)}, u32[]{:S(2)}, u32[]{:S(2)}) collective-permute-start(bf16[512,1024]{1,0:T(8,128)(2,1)} %z.5), channel_id=1, source_target_pairs={{0,24},{24,0},{1,25},{25,1},{2,26},{26,2},{3,27},{27,3},{4,28},{28... | collective-permute-start | bytes 3145736 | tf_op jit(solution)/shard_map/ppermute | solution.py:371
  35.7 3.7 %collective-permute-start.12 = (bf16[256,512]{1,0:T(8,128)(2,1)S(1)}, bf16[256,512]{1,0:T(8,128)(2,1)S(1)}, u32[]{:S(2)}, u32[]{:S(2)}) collective-permute-start(bf16[256,512]{1,0:T(8,128)(2,1)S(1)} %get-tuple-element.56), channel_id=1, source_target_pairs={{0,1},{1,0},{2,3},{3,2},{4,5},{5,4},{6,7},{7,6},{8,9},{9,8},{10,11... | collective-permute-start | bytes 786440 | tf_op jit(solution)/shard_map/ppermute | solution.py:306
  39.5 3.2 %collective-permute-start.13 = (bf16[64,512]{1,0:T(8,128)(2,1)S(1)}, bf16[64,512]{1,0:T(8,128)(2,1)S(1)}, u32[]{:S(2)}, u32[]{:S(2)}) collective-permute-start(bf16[64,512]{1,0:T(8,128)(2,1)S(1)} %get-tuple-element.58), channel_id=1, source_target_pairs={{0,2},{1,3},{2,0},{3,1},{4,6},{5,7},{6,4},{7,5},{8,10},{9,11},{10,... | collective-permute-start | bytes 196616 | tf_op jit(solution)/shard_map/ppermute | solution.py:306
  40.7 3.1 %collective-permute-start.14 = (bf16[64,512]{1,0:T(8,128)(2,1)S(1)}, bf16[64,512]{1,0:T(8,128)(2,1)S(1)}, u32[]{:S(2)}, u32[]{:S(2)}) collective-permute-start(bf16[64,512]{1,0:T(8,128)(2,1)S(1)} %get-tuple-element.59), channel_id=1, source_target_pairs={{0,4},{1,5},{2,6},{3,7},{4,0},{5,1},{6,2},{7,3},{8,12},{9,13},{10,... | collective-permute-start | bytes 196616 | tf_op jit(solution)/shard_map/ppermute | solution.py:306
  42.0 4.0 %collective-permute-start.15 = (bf16[64,512]{1,0:T(8,128)(2,1)S(1)}, bf16[64,512]{1,0:T(8,128)(2,1)S(1)}, u32[]{:S(2)}, u32[]{:S(2)}) collective-permute-start(bf16[64,512]{1,0:T(8,128)(2,1)S(1)} %get-tuple-element.60), channel_id=1, source_target_pairs={{0,6},{1,7},{2,4},{3,5},{4,2},{5,3},{6,0},{7,1},{8,14},{9,15},{10,... | collective-permute-start | bytes 196616 | tf_op jit(solution)/shard_map/ppermute | solution.py:306
  46.0 4.0 %collective-permute-start.16 = (bf16[64,512]{1,0:T(8,128)(2,1)S(1)}, bf16[64,512]{1,0:T(8,128)(2,1)S(1)}, u32[]{:S(2)}, u32[]{:S(2)}) collective-permute-start(bf16[64,512]{1,0:T(8,128)(2,1)S(1)} %shard_map.43.refs_0_.first), channel_id=1, source_target_pairs={{0,2},{1,3},{2,0},{3,1},{4,6},{5,7},{6,4},{7,5},{8,10},{9,11},{10,... | collective-permute-start | bytes 196616 | tf_op jit(solution)/shard_map/ppermute | solution.py:306
  46.4 3.6 %collective-permute-start.17 = (bf16[64,512]{1,0:T(8,128)(2,1)S(1)}, bf16[64,512]{1,0:T(8,128)(2,1)S(1)}, u32[]{:S(2)}, u32[]{:S(2)}) collective-permute-start(bf16[64,512]{1,0:T(8,128)(2,1)S(1)} %shard_map.43.refs_0_.first), channel_id=1, source_target_pairs={{0,4},{1,5},{2,6},{3,7},{4,0},{5,1},{6,2},{7,3},{8,12},{9,13},{10,... | collective-permute-start | bytes 196616 | tf_op jit(solution)/shard_map/ppermute | solution.py:306
  46.7 4.0 %collective-permute-start.18 = (bf16[64,512]{1,0:T(8,128)(2,1)S(1)}, bf16[64,512]{1,0:T(8,128)(2,1)S(1)}, u32[]{:S(2)}, u32[]{:S(2)}) collective-permute-start(bf16[64,512]{1,0:T(8,128)(2,1)S(1)} %shard_map.43.refs_0_.first), channel_id=1, source_target_pairs={{0,6},{1,7},{2,4},{3,5},{4,2},{5,3},{6,0},{7,1},{8,14},{9,15},{10,... | collective-permute-start | bytes 196616 | tf_op jit(solution)/shard_map/ppermute | solution.py:306
  50.8 4.9 %collective-permute-start.19 = (bf16[256,512]{1,0:T(8,128)(2,1)S(1)}, bf16[256,512]{1,0:T(8,128)(2,1)S(1)}, u32[]{:S(2)}, u32[]{:S(2)}) collective-permute-start(bf16[256,512]{1,0:T(8,128)(2,1)S(1)} %shard_map.45.near), channel_id=1, source_target_pairs={{0,1},{1,0},{2,3},{3,2},{4,5},{5,4},{6,7},{7,6},{8,9},{9,8},{10,11... | collective-permute-start | bytes 786440 | tf_op jit(solution)/shard_map/ppermute | solution.py:306
  57.5 23.5 %collective-permute-start.29 = (bf16[512,1024]{1,0:T(8,128)(2,1)S(1)}, bf16[512,1024]{1,0:T(8,128)(2,1)S(1)}, u32[]{:S(2)}, u32[]{:S(2)}) collective-permute-start(bf16[512,1024]{1,0:T(8,128)(2,1)S(1)} %get-tuple-element.69), channel_id=1, source_target_pairs={{8,0},{16,24},{9,1},{17,25},{10,2},{18,26},{11,3},{19,27},{12,4},{... | collective-permute-start | bytes 3145736 | tf_op jit(solution)/shard_map/ppermute | solution.py:388
  59.0 3.6 %collective-permute-start.21 = (bf16[256,1024]{1,0:T(8,128)(2,1)S(1)}, bf16[256,1024]{1,0:T(8,128)(2,1)S(1)}, u32[]{:S(2)}, u32[]{:S(2)}) collective-permute-start(bf16[256,1024]{1,0:T(8,128)(2,1)S(1)} %get-tuple-element.74), channel_id=1, source_target_pairs={{0,1},{1,0},{2,3},{3,2},{4,5},{5,4},{6,7},{7,6},{8,9},{9,8},{10,11... | collective-permute-start | bytes 1572872 | tf_op jit(solution)/shard_map/ppermute | solution.py:306
  59.7 5.5 %collective-permute-start.25 = (bf16[256,640]{1,0:T(8,128)(2,1)S(1)}, bf16[256,640]{1,0:T(8,128)(2,1)S(1)}, u32[]{:S(2)}, u32[]{:S(2)}) collective-permute-start(bf16[256,640]{1,0:T(8,128)(2,1)S(1)} %pad_maximum_fusion.near), channel_id=1, source_target_pairs={{0,1},{1,0},{2,3},{3,2},{4,5},{5,4},{6,7},{7,6},{8,9},{9,8},{10,11... | collective-permute-start | bytes 983048 | tf_op jit(solution)/shard_map/ppermute | solution.py:306
  59.8 26.2 %collective-permute-start.31 = (bf16[512,1024]{1,0:T(8,128)(2,1)S(1)}, bf16[512,1024]{1,0:T(8,128)(2,1)S(1)}, u32[]{:S(2)}, u32[]{:S(2)}) collective-permute-start(bf16[512,1024]{1,0:T(8,128)(2,1)S(1)} %get-tuple-element.86), channel_id=1, source_target_pairs={{8,16},{16,8},{9,17},{17,9},{10,18},{18,10},{11,19},{19,11},{12,20... | collective-permute-start | bytes 3145736 | tf_op jit(solution)/shard_map/ppermute | solution.py:388
  62.7 5.3 %collective-permute-start.22 = (bf16[64,1024]{1,0:T(8,128)(2,1)S(1)}, bf16[64,1024]{1,0:T(8,128)(2,1)S(1)}, u32[]{:S(2)}, u32[]{:S(2)}) collective-permute-start(bf16[64,1024]{1,0:T(8,128)(2,1)S(1)} %get-tuple-element.76), channel_id=1, source_target_pairs={{0,2},{1,3},{2,0},{3,1},{4,6},{5,7},{6,4},{7,5},{8,10},{9,11},{10,... | collective-permute-start | bytes 393224 | tf_op jit(solution)/shard_map/ppermute | solution.py:306
  64.0 4.1 %collective-permute-start.23 = (bf16[64,1024]{1,0:T(8,128)(2,1)S(1)}, bf16[64,1024]{1,0:T(8,128)(2,1)S(1)}, u32[]{:S(2)}, u32[]{:S(2)}) collective-permute-start(bf16[64,1024]{1,0:T(8,128)(2,1)S(1)} %get-tuple-element.77), channel_id=1, source_target_pairs={{0,4},{1,5},{2,6},{3,7},{4,0},{5,1},{6,2},{7,3},{8,12},{9,13},{10,... | collective-permute-start | bytes 393224 | tf_op jit(solution)/shard_map/ppermute | solution.py:306
  65.2 5.5 %collective-permute-start.24 = (bf16[64,1024]{1,0:T(8,128)(2,1)S(1)}, bf16[64,1024]{1,0:T(8,128)(2,1)S(1)}, u32[]{:S(2)}, u32[]{:S(2)}) collective-permute-start(bf16[64,1024]{1,0:T(8,128)(2,1)S(1)} %get-tuple-element.78), channel_id=1, source_target_pairs={{0,6},{1,7},{2,4},{3,5},{4,2},{5,3},{6,0},{7,1},{8,14},{9,15},{10,... | collective-permute-start | bytes 393224 | tf_op jit(solution)/shard_map/ppermute | solution.py:306
  70.9 4.2 %collective-permute-start.26 = (bf16[64,1024]{1,0:T(8,128)(2,1)S(1)}, bf16[64,1024]{1,0:T(8,128)(2,1)S(1)}, u32[]{:S(2)}, u32[]{:S(2)}) collective-permute-start(bf16[64,1024]{1,0:T(8,128)(2,1)S(1)} %shard_map.49.refs_0_), channel_id=1, source_target_pairs={{0,2},{1,3},{2,0},{3,1},{4,6},{5,7},{6,4},{7,5},{8,10},{9,11},{10,... | collective-permute-start | bytes 393224 | tf_op jit(solution)/shard_map/ppermute | solution.py:306
  72.3 5.4 %collective-permute-start.27 = (bf16[64,1024]{1,0:T(8,128)(2,1)S(1)}, bf16[64,1024]{1,0:T(8,128)(2,1)S(1)}, u32[]{:S(2)}, u32[]{:S(2)}) collective-permute-start(bf16[64,1024]{1,0:T(8,128)(2,1)S(1)} %shard_map.49.refs_0_), channel_id=1, source_target_pairs={{0,4},{1,5},{2,6},{3,7},{4,0},{5,1},{6,2},{7,3},{8,12},{9,13},{10,... | collective-permute-start | bytes 393224 | tf_op jit(solution)/shard_map/ppermute | solution.py:306
  72.5 5.3 %collective-permute-start.28 = (bf16[64,1024]{1,0:T(8,128)(2,1)S(1)}, bf16[64,1024]{1,0:T(8,128)(2,1)S(1)}, u32[]{:S(2)}, u32[]{:S(2)}) collective-permute-start(bf16[64,1024]{1,0:T(8,128)(2,1)S(1)} %shard_map.49.refs_0_), channel_id=1, source_target_pairs={{0,6},{1,7},{2,4},{3,5},{4,2},{5,3},{6,0},{7,1},{8,14},{9,15},{10,... | collective-permute-start | bytes 393224 | tf_op jit(solution)/shard_map/ppermute | solution.py:306
  81.0 5.0 %collective-permute-start.30 = (bf16[256,1024]{1,0:T(8,128)(2,1)S(1)}, bf16[256,1024]{1,0:T(8,128)(2,1)S(1)}, u32[]{:S(2)}, u32[]{:S(2)}) collective-permute-start(bf16[256,1024]{1,0:T(8,128)(2,1)S(1)} %shard_map.51.near), channel_id=1, source_target_pairs={{0,1},{1,0},{2,3},{3,2},{4,5},{5,4},{6,7},{7,6},{8,9},{9,8},{10,11... | collective-permute-start | bytes 1572872 | tf_op jit(solution)/shard_map/ppermute | solution.py:306
  (1 other events, 6.5 us)

commit v23 on v22

--- a/solution.py
+++ b/solution.py
@@ -278,18 +278,22 @@
 
 
 def last_kernel(
-    total, order, middle, near, far, beside, swapped, end, held, out, over, result, second, made, sem
+    total, order, middle, near, far, beside, swapped, end, held, out, over, result, made, sem
 ):
     rows, width = beside.shape
-    place_into(second, order, near, far)
+    eighth = rows // 8
 
     def put(opposite, arrived):
         for k in range(4):
             here = slice(k * width // 4, (k + 1) * width // 4)
-            product = dot(second[:, rows:], beside[:, here])
-            product = product + dot(second[:, :rows], opposite[:, here])
-            product = product + arrived[:, here].astype(jnp.float32)
-            made[:, here] = held[:, here] + coefficient(total) * product
+            for side, part in enumerate((near, far)):
+                product = dot(part[:, rows:], beside[:, here])
+                product = product + dot(part[:, :rows], opposite[:, here])
+                for n in range(4):
+                    start = pl.multiple_of(order[4 * side + n] * eighth, eighth)
+                    to = pl.ds(start, eighth)
+                    sums = product[n * eighth:(n + 1) * eighth] + arrived[to, here].astype(jnp.float32)
+                    made[to, here] = held[to, here] + coefficient(total) * sums
             to_result(k).start()
 
     def to_result(k):
@@ -411,7 +415,7 @@
     near = after(gather_chips(after(second, held)), pushed[0])
     return kernel_call(
         functools.partial(last_kernel, total), [result],
-        smem=2, scratch=12, temps=[((rows, 2 * rows), jnp.bfloat16), result], sems=4, out=pl.ANY,
+        smem=2, scratch=12, temps=[result], sems=4, out=pl.ANY,
     )(
         order, middle, near, to_partner(near, 1), beside, swapped, end, held, *pushed
     )[0]

time: 90.3 us -> 90.5 us (level)
  no operation moved by 1% of the time
where the time goes in v23:
time: 90.5 us; the launch traced here: 89.2 us
  starting transfers between devices  40 us (44%)
  waiting for transfers between devices  32.3 us (36%)
  Pallas kernels  15.8 us (17%)
    ppermute x24, starting transfers between devices, to_partner(): return lax.ppermute(x, 'feat', [(i, i ^ step) for i in range(8)])  26.3 us
    ppermute x24, waiting for transfers between devices, to_partner(): return lax.ppermute(x, 'feat', [(i, i ^ step) for i in range(8)])  21.8 us
    pallas_call x16, Pallas kernels, call(): pl.pallas_call(body, out_shape=[jax.ShapeDtypeStruct(s, t) for s, t in ou...  15.8 us
    ppermute x3, starting transfers between devices, by_line(): lax.ppermute(stats, 'dp', [(i, (i + k) % 4) for i in range(4)])  4.72 us
    ppermute x1, waiting for transfers between devices, by_line(): lax.ppermute(after(over, end), 'dp', across)  3.81 us
    ppermute x1, waiting for transfers between devices, by_line(): lax.ppermute(out, 'dp', outward)  3.16 us
    ppermute x1, starting transfers between devices, by_line(): swapped = lax.ppermute(ahead, 'dp', across)  3.08 us
    ppermute x1, starting transfers between devices, by_line(): lax.ppermute(after(over, end), 'dp', across)  2.77 us
  transfers between devices with their start and end apart: 32, of which 22 were waited for; matrix products, arithmetic and copies ran while one was open for 1% of the time, Pallas kernels for 12%

profile of v23, /device:TPU:9, one launch (start us, length us, event | category | flops | bytes accessed | tf_op | source)
XLA Modules:
  0.0 89.2 jit_solution(4935246902520944468)
XLA Ops:
  0.0 1.8 %shard_map.37 = f32[2,1024]{1,0:T(2,128)S(1)} custom-call(bf16[512,1024]{1,0:T(8,128)(2,1)} %z.5), custom_call_target="tpu_custom_call" | custom-call | tf_op jit(solution)/shard_map/pallas_call | solution.py:19
  1.9 2.5 %collective-permute-start.1 = (f32[2,1024]{1,0:T(2,128)S(1)}, f32[2,1024]{1,0:T(2,128)S(1)}, u32[]{:S(2)}, u32[]{:S(2)}) collective-permute-start(f32[2,1024]{1,0:T(2,128)S(1)} %shard_map.37), channel_id=1, source_target_pairs={{0,16},{8,24},{16,0},{24,8},{1,17},{9,25},{17,1},{25,9},{2,18},{10... | collective-permute-start | bytes 24584 | tf_op jit(solution)/shard_map/ppermute | solution.py:356
  4.3 2.2 %collective-permute-start = (f32[2,1024]{1,0:T(2,128)S(1)}, f32[2,1024]{1,0:T(2,128)S(1)}, u32[]{:S(2)}, u32[]{:S(2)}) collective-permute-start(f32[2,1024]{1,0:T(2,128)S(1)} %shard_map.37), channel_id=1, source_target_pairs={{0,8},{8,16},{16,24},{24,0},{1,9},{9,17},{17,25},{25,1},{2,10},{10... | collective-permute-start | bytes 24584 | tf_op jit(solution)/shard_map/ppermute | solution.py:356
  6.5 3.1 %collective-permute-start.11 = (bf16[512,1024]{1,0:T(8,128)(2,1)}, bf16[512,1024]{1,0:T(8,128)(2,1)}, u32[]{:S(2)}, u32[]{:S(2)}) collective-permute-start(bf16[512,1024]{1,0:T(8,128)(2,1)} %z.5), channel_id=1, source_target_pairs={{8,16},{16,8},{9,17},{17,9},{10,18},{18,10},{11,19},{19,11},{12,20... | collective-permute-start | bytes 3145736 | tf_op jit(solution)/shard_map/ppermute | solution.py:360
  10.4 2.4 %shard_map.38 = (bf16[512,1024]{1,0:T(8,128)(2,1)S(1)}, bf16[512,1024]{1,0:T(8,128)(2,1)S(1)}, f32[1,1024]{1,0:T(1,128)S(1)}, f32[256,640]{1,0:T(8,128)S(1)}, bf16[256,640]{1,0:T(8,128)(2,1)S(1)}) custom-call(s32[8]{0:T(128)S(1)} %broadcast_xor_fusion.order, bf16[512,1024]{1,0:T(8,128)(2,1)} %z.5, f32[1,1024]{1,0:T(1,128)S(1)} %get-tuple-element.88.mean), custom_call_target="tpu_custom_call" | custom-call | tf_op jit(solution)/shard_map/pallas_call | solution.py:19
  12.7 1.9 %collective-permute-start.3 = (bf16[256,640]{1,0:T(8,128)(2,1)S(1)}, bf16[256,640]{1,0:T(8,128)(2,1)S(1)}, u32[]{:S(2)}, u32[]{:S(2)}) collective-permute-start(bf16[256,640]{1,0:T(8,128)(2,1)S(1)} %get-tuple-element.48), channel_id=1, source_target_pairs={{0,1},{1,0},{2,3},{3,2},{4,5},{5,4},{6,7},{7,6},{8,9},{9,8},{10,11... | collective-permute-start | bytes 983048 | tf_op jit(solution)/shard_map/ppermute | solution.py:310
  14.6 1.3 %collective-permute-done.3.got = bf16[256,640]{1,0:T(8,128)(2,1)S(1)} collective-permute-done((bf16[256,640]{1,0:T(8,128)(2,1)S(1)}, bf16[256,640]{1,0:T(8,128)(2,1)S(1)}, u32[]{:S(2)}, u32[]{:S(2)}) %collective-permute-start.3) | collective-permute-done | bytes 327712 | tf_op jit(solution)/shard_map/ppermute | solution.py:310
  16.0 1.3 %collective-permute-start.4 = (bf16[64,640]{1,0:T(8,128)(2,1)S(1)}, bf16[64,640]{1,0:T(8,128)(2,1)S(1)}, u32[]{:S(2)}, u32[]{:S(2)}) collective-permute-start(bf16[64,640]{1,0:T(8,128)(2,1)S(1)} %get-tuple-element.50), channel_id=1, source_target_pairs={{0,2},{1,3},{2,0},{3,1},{4,6},{5,7},{6,4},{7,5},{8,10},{9,11},{10,... | collective-permute-start | bytes 245768 | tf_op jit(solution)/shard_map/ppermute | solution.py:310
  20.9 1.7 %collective-permute-done.6.c = bf16[64,640]{1,0:T(8,128)(2,1)S(1)} collective-permute-done((bf16[64,640]{1,0:T(8,128)(2,1)S(1)}, bf16[64,640]{1,0:T(8,128)(2,1)S(1)}, u32[]{:S(2)}, u32[]{:S(2)}) %collective-permute-start.6) | collective-permute-done | bytes 81952 | tf_op jit(solution)/shard_map/ppermute | solution.py:310
  25.5 1.6 %collective-permute-done.9 = bf16[64,640]{1,0:T(8,128)(2,1)S(1)} collective-permute-done((bf16[64,640]{1,0:T(8,128)(2,1)S(1)}, bf16[64,640]{1,0:T(8,128)(2,1)S(1)}, u32[]{:S(2)}, u32[]{:S(2)}) %collective-permute-start.9) | collective-permute-done | bytes 81952 | tf_op jit(solution)/shard_map/ppermute | solution.py:310
  28.4 1.6 %collective-permute-done.10.beside_in = bf16[512,1024]{1,0:T(8,128)(2,1)S(1)} collective-permute-done((bf16[512,1024]{1,0:T(8,128)(2,1)}, bf16[512,1024]{1,0:T(8,128)(2,1)S(1)}, u32[]{:S(2)}, u32[]{:S(2)}) %collective-permute-start.10) | collective-permute-done | bytes 1048608 | tf_op jit(solution)/shard_map/ppermute | solution.py:359
  30.0 1.9 %collective-permute-done.11.opposite_in = bf16[512,1024]{1,0:T(8,128)(2,1)} collective-permute-done((bf16[512,1024]{1,0:T(8,128)(2,1)}, bf16[512,1024]{1,0:T(8,128)(2,1)}, u32[]{:S(2)}, u32[]{:S(2)}) %collective-permute-start.11) | collective-permute-done | bytes 1048608 | tf_op jit(solution)/shard_map/ppermute | solution.py:360
  31.9 1.6 %collective-permute-start.20 = (bf16[512,1024]{1,0:T(8,128)(2,1)}, bf16[512,1024]{1,0:T(8,128)(2,1)}, u32[]{:S(2)}, u32[]{:S(2)}) collective-permute-start(bf16[512,1024]{1,0:T(8,128)(2,1)} %z.5), channel_id=1, source_target_pairs={{0,24},{24,0},{1,25},{25,1},{2,26},{26,2},{3,27},{27,3},{4,28},{28... | collective-permute-start | bytes 3145736 | tf_op jit(solution)/shard_map/ppermute | solution.py:375
  33.5 2.2 %shard_map.41 = (bf16[512,1024]{1,0:T(8,128)(2,1)S(1)}, f32[1,1024]{1,0:T(1,128)S(1)}, bf16[512,1024]{1,0:T(8,128)(2,1)S(1)}, f32[1,1024]{1,0:T(1,128)S(1)}, f32...) custom-call(s32[8]{0:T(128)S(1)} %broadcast_xor_fusion.order, s32[1]{0:T(128)} %bitcast.middle, ...), custom_call_target="tpu_custom_call" | custom-call | tf_op jit(solution)/shard_map/pallas_call | solution.py:19
  35.7 2.5 %collective-permute-start.12 = (bf16[256,512]{1,0:T(8,128)(2,1)S(1)}, bf16[256,512]{1,0:T(8,128)(2,1)S(1)}, u32[]{:S(2)}, u32[]{:S(2)}) collective-permute-start(bf16[256,512]{1,0:T(8,128)(2,1)S(1)} %get-tuple-element.56), channel_id=1, source_target_pairs={{0,1},{1,0},{2,3},{3,2},{4,5},{5,4},{6,7},{7,6},{8,9},{9,8},{10,11... | collective-permute-start | bytes 786440 | tf_op jit(solution)/shard_map/ppermute | solution.py:310
  39.5 1.3 %collective-permute-start.13 = (bf16[64,512]{1,0:T(8,128)(2,1)S(1)}, bf16[64,512]{1,0:T(8,128)(2,1)S(1)}, u32[]{:S(2)}, u32[]{:S(2)}) collective-permute-start(bf16[64,512]{1,0:T(8,128)(2,1)S(1)} %get-tuple-element.58), channel_id=1, source_target_pairs={{0,2},{1,3},{2,0},{3,1},{4,6},{5,7},{6,4},{7,5},{8,10},{9,11},{10,... | collective-permute-start | bytes 196616 | tf_op jit(solution)/shard_map/ppermute | solution.py:310
  43.9 2.1 %collective-permute-done.15.c = bf16[64,512]{1,0:T(8,128)(2,1)S(1)} collective-permute-done((bf16[64,512]{1,0:T(8,128)(2,1)S(1)}, bf16[64,512]{1,0:T(8,128)(2,1)S(1)}, u32[]{:S(2)}, u32[]{:S(2)}) %collective-permute-start.15) | collective-permute-done | bytes 65568 | tf_op jit(solution)/shard_map/ppermute | solution.py:310
  46.7 2.0 %collective-permute-start.18 = (bf16[64,512]{1,0:T(8,128)(2,1)S(1)}, bf16[64,512]{1,0:T(8,128)(2,1)S(1)}, u32[]{:S(2)}, u32[]{:S(2)}) collective-permute-start(bf16[64,512]{1,0:T(8,128)(2,1)S(1)} %shard_map.43.refs_0_.first), channel_id=1, source_target_pairs={{0,6},{1,7},{2,4},{3,5},{4,2},{5,3},{6,0},{7,1},{8,14},{9,15},{10,... | collective-permute-start | bytes 196616 | tf_op jit(solution)/shard_map/ppermute | solution.py:310
  48.7 1.3 %shard_map.44 = (f32[256,1024]{1,0:T(8,128)S(1)}, bf16[256,1024]{1,0:T(8,128)(2,1)S(1)}) custom-call(s32[1]{0:T(128)} %bitcast.middle, bf16[512,1024]{1,0:T(8,128)(2,1)S(1)} %get-tuple-element.71.turned, bf16[512,1024]{1,0:T(8,128)(2,1)S(1)} %get-tuple-element.62.beside, bf16[512,1024]{1,0:T(8,128)(2,1)S(1)} %get-tuple-element.63.opposite.swapped), custom_call_target="tpu_custom_call" | custom-call | tf_op jit(solution)/shard_map/pallas_call | solution.py:19
  50.8 3.7 %collective-permute-start.19 = (bf16[256,512]{1,0:T(8,128)(2,1)S(1)}, bf16[256,512]{1,0:T(8,128)(2,1)S(1)}, u32[]{:S(2)}, u32[]{:S(2)}) collective-permute-start(bf16[256,512]{1,0:T(8,128)(2,1)S(1)} %shard_map.45.near), channel_id=1, source_target_pairs={{0,1},{1,0},{2,3},{3,2},{4,5},{5,4},{6,7},{7,6},{8,9},{9,8},{10,11... | collective-permute-start | bytes 786440 | tf_op jit(solution)/shard_map/ppermute | solution.py:310
  55.6 1.8 %shard_map.46 = (bf16[512,1024]{1,0:T(8,128)(2,1)S(1)}, bf16[512,1024]{1,0:T(8,128)(2,1)S(1)}) custom-call(s32[8]{0:T(128)S(1)} %broadcast_xor_fusion.order, s32[1]{0:T(128)} %bitcast.middle, bf16[256,512]{1,0:T(8,128)(2,1)S(1)} %shard_map.45.near, bf16[256,512]{1,0:T(8,128)(2,1)S(1)} %collective-permute-done.19.far, ...), custom_call_target="tpu_custom_call" | custom-call | tf_op jit(solution)/shard_map/pallas_call | solution.py:19
  57.5 1.4 %collective-permute-start.29 = (bf16[512,1024]{1,0:T(8,128)(2,1)S(1)}, bf16[512,1024]{1,0:T(8,128)(2,1)S(1)}, u32[]{:S(2)}, u32[]{:S(2)}) collective-permute-start(bf16[512,1024]{1,0:T(8,128)(2,1)S(1)} %get-tuple-element.69), channel_id=1, source_target_pairs={{8,0},{16,24},{9,1},{17,25},{10,2},{18,26},{11,3},{19,27},{12,4},{... | collective-permute-start | bytes 3145736 | tf_op jit(solution)/shard_map/ppermute | solution.py:392
  59.8 2.8 %collective-permute-start.31 = (bf16[512,1024]{1,0:T(8,128)(2,1)S(1)}, bf16[512,1024]{1,0:T(8,128)(2,1)S(1)}, u32[]{:S(2)}, u32[]{:S(2)}) collective-permute-start(bf16[512,1024]{1,0:T(8,128)(2,1)S(1)} %get-tuple-element.86), channel_id=1, source_target_pairs={{8,16},{16,8},{9,17},{17,9},{10,18},{18,10},{11,19},{19,11},{12,20... | collective-permute-start | bytes 3145736 | tf_op jit(solution)/shard_map/ppermute | solution.py:392
  62.7 1.3 %collective-permute-start.22 = (bf16[64,1024]{1,0:T(8,128)(2,1)S(1)}, bf16[64,1024]{1,0:T(8,128)(2,1)S(1)}, u32[]{:S(2)}, u32[]{:S(2)}) collective-permute-start(bf16[64,1024]{1,0:T(8,128)(2,1)S(1)} %get-tuple-element.76), channel_id=1, source_target_pairs={{0,2},{1,3},{2,0},{3,1},{4,6},{5,7},{6,4},{7,5},{8,10},{9,11},{10,... | collective-permute-start | bytes 393224 | tf_op jit(solution)/shard_map/ppermute | solution.py:310
  65.4 2.6 %shard_map.50.held = f32[512,1024]{1,0:T(8,128)S(1)} custom-call(s32[8]{0:T(128)S(1)} %broadcast_xor_fusion.order, s32[1]{0:T(128)} %bitcast.middle, bf16[256,640]{1,0:T(8,128)(2,1)S(1)} %pad_maximum_fusion.near, bf16[256,640]{1,0:T(8,128)(2,1)S(1)} %collective-permute-done.25.far, bf16[512,1024]{1,0:T(8,128)(2,1)S(1)} %get-tuple-element.79.own, ...), custom_call_target="tpu_custom_call" | custom-call | tf_op jit(solution)/shard_map/pallas_call | solution.py:19
  68.1 2.7 %collective-permute-done.24.c = bf16[64,1024]{1,0:T(8,128)(2,1)S(1)} collective-permute-done((bf16[64,1024]{1,0:T(8,128)(2,1)S(1)}, bf16[64,1024]{1,0:T(8,128)(2,1)S(1)}, u32[]{:S(2)}, u32[]{:S(2)}) %collective-permute-start.24) | collective-permute-done | bytes 131104 | tf_op jit(solution)/shard_map/ppermute | solution.py:310
  70.9 1.4 %collective-permute-start.26 = (bf16[64,1024]{1,0:T(8,128)(2,1)S(1)}, bf16[64,1024]{1,0:T(8,128)(2,1)S(1)}, u32[]{:S(2)}, u32[]{:S(2)}) collective-permute-start(bf16[64,1024]{1,0:T(8,128)(2,1)S(1)} %shard_map.49.refs_0_), channel_id=1, source_target_pairs={{0,2},{1,3},{2,0},{3,1},{4,6},{5,7},{6,4},{7,5},{8,10},{9,11},{10,... | collective-permute-start | bytes 393224 | tf_op jit(solution)/shard_map/ppermute | solution.py:310
  73.6 1.5 %collective-permute-done.26.refs_1_ = bf16[64,1024]{1,0:T(8,128)(2,1)S(1)} collective-permute-done((bf16[64,1024]{1,0:T(8,128)(2,1)S(1)}, bf16[64,1024]{1,0:T(8,128)(2,1)S(1)}, u32[]{:S(2)}, u32[]{:S(2)}) %collective-permute-start.26) | collective-permute-done | bytes 131104 | tf_op jit(solution)/shard_map/ppermute | solution.py:310
  75.0 2.6 %collective-permute-done.27.refs_2_ = bf16[64,1024]{1,0:T(8,128)(2,1)S(1)} collective-permute-done((bf16[64,1024]{1,0:T(8,128)(2,1)S(1)}, bf16[64,1024]{1,0:T(8,128)(2,1)S(1)}, u32[]{:S(2)}, u32[]{:S(2)}) %collective-permute-start.27) | collective-permute-done | bytes 131104 | tf_op jit(solution)/shard_map/ppermute | solution.py:310
  77.8 3.2 %collective-permute-done.29.out = bf16[512,1024]{1,0:T(8,128)(2,1)S(1)} collective-permute-done((bf16[512,1024]{1,0:T(8,128)(2,1)S(1)}, bf16[512,1024]{1,0:T(8,128)(2,1)S(1)}, u32[]{:S(2)}, u32[]{:S(2)}) %collective-permute-start.29) | collective-permute-done | bytes 1048608 | tf_op jit(solution)/shard_map/ppermute | solution.py:392
  82.2 3.8 %collective-permute-done.31.over = bf16[512,1024]{1,0:T(8,128)(2,1)S(1)} collective-permute-done((bf16[512,1024]{1,0:T(8,128)(2,1)S(1)}, bf16[512,1024]{1,0:T(8,128)(2,1)S(1)}, u32[]{:S(2)}, u32[]{:S(2)}) %collective-permute-start.31) | collective-permute-done | bytes 1048608 | tf_op jit(solution)/shard_map/ppermute | solution.py:392
  86.0 3.1 %shard_map.52 = f32[512,1024]{1,0:T(8,128)} custom-call(s32[8]{0:T(128)S(1)} %broadcast_xor_fusion.order, s32[1]{0:T(128)} %bitcast.middle, bf16[256,1024]{1,0:T(8,128)(2,1)S(1)} %shard_map.51.near, bf16[256,1024]{1,0:T(8,128)(2,1)S(1)} %collective-permute-done.30.far, bf16[512,1024]{1,0:T(8,128)(2,1)S(1)} %get-tuple-element.62.beside, ...), custom_call_target="tpu_custom_call" | custom-call | tf_op jit(solution)/shard_map/pallas_call | solution.py:19
  (53 shorter events, 20.7 us)
Async XLA Ops:
  1.8 8.5 %collective-permute-start.2 = (f32[2,1024]{1,0:T(2,128)S(1)}, f32[2,1024]{1,0:T(2,128)S(1)}, u32[]{:S(2)}, u32[]{:S(2)}) collective-permute-start(f32[2,1024]{1,0:T(2,128)S(1)} %shard_map.37), channel_id=1, source_target_pairs={{0,24},{8,0},{16,8},{24,16},{1,25},{9,1},{17,9},{25,17},{2,26},{10... | collective-permute-start | bytes 24584 | tf_op jit(solution)/shard_map/ppermute | solution.py:356
  1.9 8.4 %collective-permute-start.1 = (f32[2,1024]{1,0:T(2,128)S(1)}, f32[2,1024]{1,0:T(2,128)S(1)}, u32[]{:S(2)}, u32[]{:S(2)}) collective-permute-start(f32[2,1024]{1,0:T(2,128)S(1)} %shard_map.37), channel_id=1, source_target_pairs={{0,16},{8,24},{16,0},{24,8},{1,17},{9,25},{17,1},{25,9},{2,18},{10... | collective-permute-start | bytes 24584 | tf_op jit(solution)/shard_map/ppermute | solution.py:356
  4.3 6.0 %collective-permute-start = (f32[2,1024]{1,0:T(2,128)S(1)}, f32[2,1024]{1,0:T(2,128)S(1)}, u32[]{:S(2)}, u32[]{:S(2)}) collective-permute-start(f32[2,1024]{1,0:T(2,128)S(1)} %shard_map.37), channel_id=1, source_target_pairs={{0,8},{8,16},{16,24},{24,0},{1,9},{9,17},{17,25},{25,1},{2,10},{10... | collective-permute-start | bytes 24584 | tf_op jit(solution)/shard_map/ppermute | solution.py:356
  6.5 23.4 %collective-permute-start.10 = (bf16[512,1024]{1,0:T(8,128)(2,1)}, bf16[512,1024]{1,0:T(8,128)(2,1)S(1)}, u32[]{:S(2)}, u32[]{:S(2)}) collective-permute-start(bf16[512,1024]{1,0:T(8,128)(2,1)} %z.5), channel_id=1, source_target_pairs={{0,8},{8,0},{16,24},{24,16},{1,9},{9,1},{17,25},{25,17},{2,10},{10... | collective-permute-start | bytes 3145736 | tf_op jit(solution)/shard_map/ppermute | solution.py:359
  6.5 25.3 %collective-permute-start.11 = (bf16[512,1024]{1,0:T(8,128)(2,1)}, bf16[512,1024]{1,0:T(8,128)(2,1)}, u32[]{:S(2)}, u32[]{:S(2)}) collective-permute-start(bf16[512,1024]{1,0:T(8,128)(2,1)} %z.5), channel_id=1, source_target_pairs={{8,16},{16,8},{9,17},{17,9},{10,18},{18,10},{11,19},{19,11},{12,20... | collective-permute-start | bytes 3145736 | tf_op jit(solution)/shard_map/ppermute | solution.py:360
  12.7 3.1 %collective-permute-start.3 = (bf16[256,640]{1,0:T(8,128)(2,1)S(1)}, bf16[256,640]{1,0:T(8,128)(2,1)S(1)}, u32[]{:S(2)}, u32[]{:S(2)}) collective-permute-start(bf16[256,640]{1,0:T(8,128)(2,1)S(1)} %get-tuple-element.48), channel_id=1, source_target_pairs={{0,1},{1,0},{2,3},{3,2},{4,5},{5,4},{6,7},{7,6},{8,9},{9,8},{10,11... | collective-permute-start | bytes 983048 | tf_op jit(solution)/shard_map/ppermute | solution.py:310
  16.0 3.8 %collective-permute-start.4 = (bf16[64,640]{1,0:T(8,128)(2,1)S(1)}, bf16[64,640]{1,0:T(8,128)(2,1)S(1)}, u32[]{:S(2)}, u32[]{:S(2)}) collective-permute-start(bf16[64,640]{1,0:T(8,128)(2,1)S(1)} %get-tuple-element.50), channel_id=1, source_target_pairs={{0,2},{1,3},{2,0},{3,1},{4,6},{5,7},{6,4},{7,5},{8,10},{9,11},{10,... | collective-permute-start | bytes 245768 | tf_op jit(solution)/shard_map/ppermute | solution.py:310
  17.3 3.7 %collective-permute-start.5 = (bf16[64,640]{1,0:T(8,128)(2,1)S(1)}, bf16[64,640]{1,0:T(8,128)(2,1)S(1)}, u32[]{:S(2)}, u32[]{:S(2)}) collective-permute-start(bf16[64,640]{1,0:T(8,128)(2,1)S(1)} %get-tuple-element.51), channel_id=1, source_target_pairs={{0,4},{1,5},{2,6},{3,7},{4,0},{5,1},{6,2},{7,3},{8,12},{9,13},{10,... | collective-permute-start | bytes 245768 | tf_op jit(solution)/shard_map/ppermute | solution.py:310
  18.5 4.2 %collective-permute-start.6 = (bf16[64,640]{1,0:T(8,128)(2,1)S(1)}, bf16[64,640]{1,0:T(8,128)(2,1)S(1)}, u32[]{:S(2)}, u32[]{:S(2)}) collective-permute-start(bf16[64,640]{1,0:T(8,128)(2,1)S(1)} %get-tuple-element.52), channel_id=1, source_target_pairs={{0,6},{1,7},{2,4},{3,5},{4,2},{5,3},{6,0},{7,1},{8,14},{9,15},{10,... | collective-permute-start | bytes 245768 | tf_op jit(solution)/shard_map/ppermute | solution.py:310
  22.8 4.4 %collective-permute-start.9 = (bf16[64,640]{1,0:T(8,128)(2,1)S(1)}, bf16[64,640]{1,0:T(8,128)(2,1)S(1)}, u32[]{:S(2)}, u32[]{:S(2)}) collective-permute-start(bf16[64,640]{1,0:T(8,128)(2,1)S(1)} %shard_map.40), channel_id=1, source_target_pairs={{0,6},{1,7},{2,4},{3,5},{4,2},{5,3},{6,0},{7,1},{8,14},{9,15},{10,... | collective-permute-start | bytes 245768 | tf_op jit(solution)/shard_map/ppermute | solution.py:310
  23.4 4.6 %collective-permute-start.8 = (bf16[64,640]{1,0:T(8,128)(2,1)S(1)}, bf16[64,640]{1,0:T(8,128)(2,1)S(1)}, u32[]{:S(2)}, u32[]{:S(2)}) collective-permute-start(bf16[64,640]{1,0:T(8,128)(2,1)S(1)} %shard_map.40), channel_id=1, source_target_pairs={{0,4},{1,5},{2,6},{3,7},{4,0},{5,1},{6,2},{7,3},{8,12},{9,13},{10,... | collective-permute-start | bytes 245768 | tf_op jit(solution)/shard_map/ppermute | solution.py:310
  24.6 3.7 %collective-permute-start.7 = (bf16[64,640]{1,0:T(8,128)(2,1)S(1)}, bf16[64,640]{1,0:T(8,128)(2,1)S(1)}, u32[]{:S(2)}, u32[]{:S(2)}) collective-permute-start(bf16[64,640]{1,0:T(8,128)(2,1)S(1)} %shard_map.40), channel_id=1, source_target_pairs={{0,2},{1,3},{2,0},{3,1},{4,6},{5,7},{6,4},{7,5},{8,10},{9,11},{10,... | collective-permute-start | bytes 245768 | tf_op jit(solution)/shard_map/ppermute | solution.py:310
  31.9 27.0 %collective-permute-start.20 = (bf16[512,1024]{1,0:T(8,128)(2,1)}, bf16[512,1024]{1,0:T(8,128)(2,1)}, u32[]{:S(2)}, u32[]{:S(2)}) collective-permute-start(bf16[512,1024]{1,0:T(8,128)(2,1)} %z.5), channel_id=1, source_target_pairs={{0,24},{24,0},{1,25},{25,1},{2,26},{26,2},{3,27},{27,3},{4,28},{28... | collective-permute-start | bytes 3145736 | tf_op jit(solution)/shard_map/ppermute | solution.py:375
  35.7 3.7 %collective-permute-start.12 = (bf16[256,512]{1,0:T(8,128)(2,1)S(1)}, bf16[256,512]{1,0:T(8,128)(2,1)S(1)}, u32[]{:S(2)}, u32[]{:S(2)}) collective-permute-start(bf16[256,512]{1,0:T(8,128)(2,1)S(1)} %get-tuple-element.56), channel_id=1, source_target_pairs={{0,1},{1,0},{2,3},{3,2},{4,5},{5,4},{6,7},{7,6},{8,9},{9,8},{10,11... | collective-permute-start | bytes 786440 | tf_op jit(solution)/shard_map/ppermute | solution.py:310
  39.5 3.2 %collective-permute-start.13 = (bf16[64,512]{1,0:T(8,128)(2,1)S(1)}, bf16[64,512]{1,0:T(8,128)(2,1)S(1)}, u32[]{:S(2)}, u32[]{:S(2)}) collective-permute-start(bf16[64,512]{1,0:T(8,128)(2,1)S(1)} %get-tuple-element.58), channel_id=1, source_target_pairs={{0,2},{1,3},{2,0},{3,1},{4,6},{5,7},{6,4},{7,5},{8,10},{9,11},{10,... | collective-permute-start | bytes 196616 | tf_op jit(solution)/shard_map/ppermute | solution.py:310
  40.7 3.1 %collective-permute-start.14 = (bf16[64,512]{1,0:T(8,128)(2,1)S(1)}, bf16[64,512]{1,0:T(8,128)(2,1)S(1)}, u32[]{:S(2)}, u32[]{:S(2)}) collective-permute-start(bf16[64,512]{1,0:T(8,128)(2,1)S(1)} %get-tuple-element.59), channel_id=1, source_target_pairs={{0,4},{1,5},{2,6},{3,7},{4,0},{5,1},{6,2},{7,3},{8,12},{9,13},{10,... | collective-permute-start | bytes 196616 | tf_op jit(solution)/shard_map/ppermute | solution.py:310
  42.0 4.0 %collective-permute-start.15 = (bf16[64,512]{1,0:T(8,128)(2,1)S(1)}, bf16[64,512]{1,0:T(8,128)(2,1)S(1)}, u32[]{:S(2)}, u32[]{:S(2)}) collective-permute-start(bf16[64,512]{1,0:T(8,128)(2,1)S(1)} %get-tuple-element.60), channel_id=1, source_target_pairs={{0,6},{1,7},{2,4},{3,5},{4,2},{5,3},{6,0},{7,1},{8,14},{9,15},{10,... | collective-permute-start | bytes 196616 | tf_op jit(solution)/shard_map/ppermute | solution.py:310
  46.0 4.0 %collective-permute-start.16 = (bf16[64,512]{1,0:T(8,128)(2,1)S(1)}, bf16[64,512]{1,0:T(8,128)(2,1)S(1)}, u32[]{:S(2)}, u32[]{:S(2)}) collective-permute-start(bf16[64,512]{1,0:T(8,128)(2,1)S(1)} %shard_map.43.refs_0_.first), channel_id=1, source_target_pairs={{0,2},{1,3},{2,0},{3,1},{4,6},{5,7},{6,4},{7,5},{8,10},{9,11},{10,... | collective-permute-start | bytes 196616 | tf_op jit(solution)/shard_map/ppermute | solution.py:310
  46.4 3.6 %collective-permute-start.17 = (bf16[64,512]{1,0:T(8,128)(2,1)S(1)}, bf16[64,512]{1,0:T(8,128)(2,1)S(1)}, u32[]{:S(2)}, u32[]{:S(2)}) collective-permute-start(bf16[64,512]{1,0:T(8,128)(2,1)S(1)} %shard_map.43.refs_0_.first), channel_id=1, source_target_pairs={{0,4},{1,5},{2,6},{3,7},{4,0},{5,1},{6,2},{7,3},{8,12},{9,13},{10,... | collective-permute-start | bytes 196616 | tf_op jit(solution)/shard_map/ppermute | solution.py:310
  46.7 4.0 %collective-permute-start.18 = (bf16[64,512]{1,0:T(8,128)(2,1)S(1)}, bf16[64,512]{1,0:T(8,128)(2,1)S(1)}, u32[]{:S(2)}, u32[]{:S(2)}) collective-permute-start(bf16[64,512]{1,0:T(8,128)(2,1)S(1)} %shard_map.43.refs_0_.first), channel_id=1, source_target_pairs={{0,6},{1,7},{2,4},{3,5},{4,2},{5,3},{6,0},{7,1},{8,14},{9,15},{10,... | collective-permute-start | bytes 196616 | tf_op jit(solution)/shard_map/ppermute | solution.py:310
  50.8 4.9 %collective-permute-start.19 = (bf16[256,512]{1,0:T(8,128)(2,1)S(1)}, bf16[256,512]{1,0:T(8,128)(2,1)S(1)}, u32[]{:S(2)}, u32[]{:S(2)}) collective-permute-start(bf16[256,512]{1,0:T(8,128)(2,1)S(1)} %shard_map.45.near), channel_id=1, source_target_pairs={{0,1},{1,0},{2,3},{3,2},{4,5},{5,4},{6,7},{7,6},{8,9},{9,8},{10,11... | collective-permute-start | bytes 786440 | tf_op jit(solution)/shard_map/ppermute | solution.py:310
  57.5 23.5 %collective-permute-start.29 = (bf16[512,1024]{1,0:T(8,128)(2,1)S(1)}, bf16[512,1024]{1,0:T(8,128)(2,1)S(1)}, u32[]{:S(2)}, u32[]{:S(2)}) collective-permute-start(bf16[512,1024]{1,0:T(8,128)(2,1)S(1)} %get-tuple-element.69), channel_id=1, source_target_pairs={{8,0},{16,24},{9,1},{17,25},{10,2},{18,26},{11,3},{19,27},{12,4},{... | collective-permute-start | bytes 3145736 | tf_op jit(solution)/shard_map/ppermute | solution.py:392
  59.0 3.6 %collective-permute-start.21 = (bf16[256,1024]{1,0:T(8,128)(2,1)S(1)}, bf16[256,1024]{1,0:T(8,128)(2,1)S(1)}, u32[]{:S(2)}, u32[]{:S(2)}) collective-permute-start(bf16[256,1024]{1,0:T(8,128)(2,1)S(1)} %get-tuple-element.74), channel_id=1, source_target_pairs={{0,1},{1,0},{2,3},{3,2},{4,5},{5,4},{6,7},{7,6},{8,9},{9,8},{10,11... | collective-permute-start | bytes 1572872 | tf_op jit(solution)/shard_map/ppermute | solution.py:310
  59.7 5.5 %collective-permute-start.25 = (bf16[256,640]{1,0:T(8,128)(2,1)S(1)}, bf16[256,640]{1,0:T(8,128)(2,1)S(1)}, u32[]{:S(2)}, u32[]{:S(2)}) collective-permute-start(bf16[256,640]{1,0:T(8,128)(2,1)S(1)} %pad_maximum_fusion.near), channel_id=1, source_target_pairs={{0,1},{1,0},{2,3},{3,2},{4,5},{5,4},{6,7},{7,6},{8,9},{9,8},{10,11... | collective-permute-start | bytes 983048 | tf_op jit(solution)/shard_map/ppermute | solution.py:310
  59.8 26.2 %collective-permute-start.31 = (bf16[512,1024]{1,0:T(8,128)(2,1)S(1)}, bf16[512,1024]{1,0:T(8,128)(2,1)S(1)}, u32[]{:S(2)}, u32[]{:S(2)}) collective-permute-start(bf16[512,1024]{1,0:T(8,128)(2,1)S(1)} %get-tuple-element.86), channel_id=1, source_target_pairs={{8,16},{16,8},{9,17},{17,9},{10,18},{18,10},{11,19},{19,11},{12,20... | collective-permute-start | bytes 3145736 | tf_op jit(solution)/shard_map/ppermute | solution.py:392
  62.7 5.3 %collective-permute-start.22 = (bf16[64,1024]{1,0:T(8,128)(2,1)S(1)}, bf16[64,1024]{1,0:T(8,128)(2,1)S(1)}, u32[]{:S(2)}, u32[]{:S(2)}) collective-permute-start(bf16[64,1024]{1,0:T(8,128)(2,1)S(1)} %get-tuple-element.76), channel_id=1, source_target_pairs={{0,2},{1,3},{2,0},{3,1},{4,6},{5,7},{6,4},{7,5},{8,10},{9,11},{10,... | collective-permute-start | bytes 393224 | tf_op jit(solution)/shard_map/ppermute | solution.py:310
  64.0 4.1 %collective-permute-start.23 = (bf16[64,1024]{1,0:T(8,128)(2,1)S(1)}, bf16[64,1024]{1,0:T(8,128)(2,1)S(1)}, u32[]{:S(2)}, u32[]{:S(2)}) collective-permute-start(bf16[64,1024]{1,0:T(8,128)(2,1)S(1)} %get-tuple-element.77), channel_id=1, source_target_pairs={{0,4},{1,5},{2,6},{3,7},{4,0},{5,1},{6,2},{7,3},{8,12},{9,13},{10,... | collective-permute-start | bytes 393224 | tf_op jit(solution)/shard_map/ppermute | solution.py:310
  65.2 5.5 %collective-permute-start.24 = (bf16[64,1024]{1,0:T(8,128)(2,1)S(1)}, bf16[64,1024]{1,0:T(8,128)(2,1)S(1)}, u32[]{:S(2)}, u32[]{:S(2)}) collective-permute-start(bf16[64,1024]{1,0:T(8,128)(2,1)S(1)} %get-tuple-element.78), channel_id=1, source_target_pairs={{0,6},{1,7},{2,4},{3,5},{4,2},{5,3},{6,0},{7,1},{8,14},{9,15},{10,... | collective-permute-start | bytes 393224 | tf_op jit(solution)/shard_map/ppermute | solution.py:310
  70.9 4.2 %collective-permute-start.26 = (bf16[64,1024]{1,0:T(8,128)(2,1)S(1)}, bf16[64,1024]{1,0:T(8,128)(2,1)S(1)}, u32[]{:S(2)}, u32[]{:S(2)}) collective-permute-start(bf16[64,1024]{1,0:T(8,128)(2,1)S(1)} %shard_map.49.refs_0_), channel_id=1, source_target_pairs={{0,2},{1,3},{2,0},{3,1},{4,6},{5,7},{6,4},{7,5},{8,10},{9,11},{10,... | collective-permute-start | bytes 393224 | tf_op jit(solution)/shard_map/ppermute | solution.py:310
  72.3 5.4 %collective-permute-start.27 = (bf16[64,1024]{1,0:T(8,128)(2,1)S(1)}, bf16[64,1024]{1,0:T(8,128)(2,1)S(1)}, u32[]{:S(2)}, u32[]{:S(2)}) collective-permute-start(bf16[64,1024]{1,0:T(8,128)(2,1)S(1)} %shard_map.49.refs_0_), channel_id=1, source_target_pairs={{0,4},{1,5},{2,6},{3,7},{4,0},{5,1},{6,2},{7,3},{8,12},{9,13},{10,... | collective-permute-start | bytes 393224 | tf_op jit(solution)/shard_map/ppermute | solution.py:310
  72.5 5.3 %collective-permute-start.28 = (bf16[64,1024]{1,0:T(8,128)(2,1)S(1)}, bf16[64,1024]{1,0:T(8,128)(2,1)S(1)}, u32[]{:S(2)}, u32[]{:S(2)}) collective-permute-start(bf16[64,1024]{1,0:T(8,128)(2,1)S(1)} %shard_map.49.refs_0_), channel_id=1, source_target_pairs={{0,6},{1,7},{2,4},{3,5},{4,2},{5,3},{6,0},{7,1},{8,14},{9,15},{10,... | collective-permute-start | bytes 393224 | tf_op jit(solution)/shard_map/ppermute | solution.py:310
  81.0 5.0 %collective-permute-start.30 = (bf16[256,1024]{1,0:T(8,128)(2,1)S(1)}, bf16[256,1024]{1,0:T(8,128)(2,1)S(1)}, u32[]{:S(2)}, u32[]{:S(2)}) collective-permute-start(bf16[256,1024]{1,0:T(8,128)(2,1)S(1)} %shard_map.51.near), channel_id=1, source_target_pairs={{0,1},{1,0},{2,3},{3,2},{4,5},{5,4},{6,7},{7,6},{8,9},{9,8},{10,11... | collective-permute-start | bytes 1572872 | tf_op jit(solution)/shard_map/ppermute | solution.py:310
  (1 other events, 6.5 us)

commit v24 on v22

--- a/solution.py
+++ b/solution.py
@@ -160,14 +160,23 @@
         sent[:, rows:] = jnp.zeros_like(sent[:, rows:])
 
 
-def stats_kernel(z, out):
-    rows = z.shape[0]
-    base = z[:16, :].astype(jnp.float32)[:1]
-    apart = z[...].astype(jnp.float32) - base
-    total = jnp.sum(apart, axis=0, keepdims=True)
+def stats_kernel(z, out, landed, sem):
+    rows = landed.shape[0]
+    copies = pieces_in(z, landed, sem)
+    for copy in copies:
+        copy.start()
+    total, square = 0.0, 0.0
+    for k, copy in enumerate(copies):
+        copy.wait()
+        if k == 0:
+            base = landed[:16, :].astype(jnp.float32)[:1]
+        piece = landed[k * rows // 4:(k + 1) * rows // 4, :]
+        apart = piece.astype(jnp.float32) - base
+        total = total + jnp.sum(apart, axis=0, keepdims=True)
+        square = square + jnp.sum(apart * apart, axis=0, keepdims=True)
     away = total / rows
     out[:1, :] = base + away
-    out[1:, :] = jnp.sum(apart * apart, axis=0, keepdims=True) - total * away
+    out[1:, :] = square - total * away
 
 
 def with_norm(x, last):
@@ -347,7 +356,9 @@
     half = rows // 2
     flat, block = ((1, width), jnp.float32), ((rows, width), jnp.bfloat16)
 
-    stats = kernel_call(stats_kernel, [((2, width), jnp.float32)], scratch=12)(z_anchor)[0]
+    stats = kernel_call(
+        stats_kernel, [((2, width), jnp.float32)], scratch=12, temps=[block], sems=4, outside=0
+    )(z_anchor)[0]
     all_stats = [stats] + [
         lax.ppermute(stats, "dp", [(i, (i + k) % 4) for i in range(4)]) for k in (1, 2, 3)
     ]

time: 90.3 us -> 90 us (level)
  no operation moved by 1% of the time
where the time goes in v24:
time: 90 us; the launch traced here: 88.8 us
  starting transfers between devices  40 us (44%)
  waiting for transfers between devices  32.3 us (36%)
  Pallas kernels  15.5 us (17%)
    ppermute x24, starting transfers between devices, to_partner(): return lax.ppermute(x, 'feat', [(i, i ^ step) for i in range(8)])  26.3 us
    ppermute x24, waiting for transfers between devices, to_partner(): return lax.ppermute(x, 'feat', [(i, i ^ step) for i in range(8)])  21.8 us
    pallas_call x16, Pallas kernels, call(): pl.pallas_call(body, out_shape=[jax.ShapeDtypeStruct(s, t) for s, t in ou...  15.5 us
    ppermute x3, starting transfers between devices, by_line(): lax.ppermute(stats, 'dp', [(i, (i + k) % 4) for i in range(4)])  4.72 us
    ppermute x1, waiting for transfers between devices, by_line(): lax.ppermute(after(over, end), 'dp', across)  3.81 us
    ppermute x1, waiting for transfers between devices, by_line(): lax.ppermute(out, 'dp', outward)  3.16 us
    ppermute x1, starting transfers between devices, by_line(): swapped = lax.ppermute(ahead, 'dp', across)  3.08 us
    ppermute x1, starting transfers between devices, by_line(): lax.ppermute(after(over, end), 'dp', across)  2.77 us
  transfers between devices with their start and end apart: 32, of which 22 were waited for; matrix products, arithmetic and copies ran while one was open for 1% of the time, Pallas kernels for 12%

profile of v24, /device:TPU:9, one launch (start us, length us, event | category | flops | bytes accessed | tf_op | source)
XLA Modules:
  0.0 88.8 jit_solution(6770137258635073484)
XLA Ops:
  0.0 1.5 %shard_map.37 = f32[2,1024]{1,0:T(2,128)S(1)} custom-call(bf16[512,1024]{1,0:T(8,128)(2,1)} %z.5), custom_call_target="tpu_custom_call" | custom-call | tf_op jit(solution)/shard_map/pallas_call | solution.py:19
  1.6 2.5 %collective-permute-start.1 = (f32[2,1024]{1,0:T(2,128)S(1)}, f32[2,1024]{1,0:T(2,128)S(1)}, u32[]{:S(2)}, u32[]{:S(2)}) collective-permute-start(f32[2,1024]{1,0:T(2,128)S(1)} %shard_map.37), channel_id=1, source_target_pairs={{0,16},{8,24},{16,0},{24,8},{1,17},{9,25},{17,1},{25,9},{2,18},{10... | collective-permute-start | bytes 24584 | tf_op jit(solution)/shard_map/ppermute | solution.py:363
  4.1 2.2 %collective-permute-start = (f32[2,1024]{1,0:T(2,128)S(1)}, f32[2,1024]{1,0:T(2,128)S(1)}, u32[]{:S(2)}, u32[]{:S(2)}) collective-permute-start(f32[2,1024]{1,0:T(2,128)S(1)} %shard_map.37), channel_id=1, source_target_pairs={{0,8},{8,16},{16,24},{24,0},{1,9},{9,17},{17,25},{25,1},{2,10},{10... | collective-permute-start | bytes 24584 | tf_op jit(solution)/shard_map/ppermute | solution.py:363
  6.3 3.1 %collective-permute-start.11 = (bf16[512,1024]{1,0:T(8,128)(2,1)}, bf16[512,1024]{1,0:T(8,128)(2,1)}, u32[]{:S(2)}, u32[]{:S(2)}) collective-permute-start(bf16[512,1024]{1,0:T(8,128)(2,1)} %z.5), channel_id=1, source_target_pairs={{8,16},{16,8},{9,17},{17,9},{10,18},{18,10},{11,19},{19,11},{12,20... | collective-permute-start | bytes 3145736 | tf_op jit(solution)/shard_map/ppermute | solution.py:367
  10.1 2.4 %shard_map.38 = (bf16[512,1024]{1,0:T(8,128)(2,1)S(1)}, bf16[512,1024]{1,0:T(8,128)(2,1)S(1)}, f32[1,1024]{1,0:T(1,128)S(1)}, f32[256,640]{1,0:T(8,128)S(1)}, bf16[256,640]{1,0:T(8,128)(2,1)S(1)}) custom-call(s32[8]{0:T(128)S(1)} %broadcast_xor_fusion.order, bf16[512,1024]{1,0:T(8,128)(2,1)} %z.5, f32[1,1024]{1,0:T(1,128)S(1)} %get-tuple-element.88.mean), custom_call_target="tpu_custom_call" | custom-call | tf_op jit(solution)/shard_map/pallas_call | solution.py:19
  12.5 1.9 %collective-permute-start.3 = (bf16[256,640]{1,0:T(8,128)(2,1)S(1)}, bf16[256,640]{1,0:T(8,128)(2,1)S(1)}, u32[]{:S(2)}, u32[]{:S(2)}) collective-permute-start(bf16[256,640]{1,0:T(8,128)(2,1)S(1)} %get-tuple-element.48), channel_id=1, source_target_pairs={{0,1},{1,0},{2,3},{3,2},{4,5},{5,4},{6,7},{7,6},{8,9},{9,8},{10,11... | collective-permute-start | bytes 983048 | tf_op jit(solution)/shard_map/ppermute | solution.py:315
  14.3 1.3 %collective-permute-done.3.got = bf16[256,640]{1,0:T(8,128)(2,1)S(1)} collective-permute-done((bf16[256,640]{1,0:T(8,128)(2,1)S(1)}, bf16[256,640]{1,0:T(8,128)(2,1)S(1)}, u32[]{:S(2)}, u32[]{:S(2)}) %collective-permute-start.3) | collective-permute-done | bytes 327712 | tf_op jit(solution)/shard_map/ppermute | solution.py:315
  15.7 1.3 %collective-permute-start.4 = (bf16[64,640]{1,0:T(8,128)(2,1)S(1)}, bf16[64,640]{1,0:T(8,128)(2,1)S(1)}, u32[]{:S(2)}, u32[]{:S(2)}) collective-permute-start(bf16[64,640]{1,0:T(8,128)(2,1)S(1)} %get-tuple-element.50), channel_id=1, source_target_pairs={{0,2},{1,3},{2,0},{3,1},{4,6},{5,7},{6,4},{7,5},{8,10},{9,11},{10,... | collective-permute-start | bytes 245768 | tf_op jit(solution)/shard_map/ppermute | solution.py:315
  20.7 1.7 %collective-permute-done.6.c = bf16[64,640]{1,0:T(8,128)(2,1)S(1)} collective-permute-done((bf16[64,640]{1,0:T(8,128)(2,1)S(1)}, bf16[64,640]{1,0:T(8,128)(2,1)S(1)}, u32[]{:S(2)}, u32[]{:S(2)}) %collective-permute-start.6) | collective-permute-done | bytes 81952 | tf_op jit(solution)/shard_map/ppermute | solution.py:315
  25.2 1.6 %collective-permute-done.9 = bf16[64,640]{1,0:T(8,128)(2,1)S(1)} collective-permute-done((bf16[64,640]{1,0:T(8,128)(2,1)S(1)}, bf16[64,640]{1,0:T(8,128)(2,1)S(1)}, u32[]{:S(2)}, u32[]{:S(2)}) %collective-permute-start.9) | collective-permute-done | bytes 81952 | tf_op jit(solution)/shard_map/ppermute | solution.py:315
  28.1 1.6 %collective-permute-done.10.beside_in = bf16[512,1024]{1,0:T(8,128)(2,1)S(1)} collective-permute-done((bf16[512,1024]{1,0:T(8,128)(2,1)}, bf16[512,1024]{1,0:T(8,128)(2,1)S(1)}, u32[]{:S(2)}, u32[]{:S(2)}) %collective-permute-start.10) | collective-permute-done | bytes 1048608 | tf_op jit(solution)/shard_map/ppermute | solution.py:366
  29.7 1.9 %collective-permute-done.11.opposite_in = bf16[512,1024]{1,0:T(8,128)(2,1)} collective-permute-done((bf16[512,1024]{1,0:T(8,128)(2,1)}, bf16[512,1024]{1,0:T(8,128)(2,1)}, u32[]{:S(2)}, u32[]{:S(2)}) %collective-permute-start.11) | collective-permute-done | bytes 1048608 | tf_op jit(solution)/shard_map/ppermute | solution.py:367
  31.6 1.6 %collective-permute-start.20 = (bf16[512,1024]{1,0:T(8,128)(2,1)}, bf16[512,1024]{1,0:T(8,128)(2,1)}, u32[]{:S(2)}, u32[]{:S(2)}) collective-permute-start(bf16[512,1024]{1,0:T(8,128)(2,1)} %z.5), channel_id=1, source_target_pairs={{0,24},{24,0},{1,25},{25,1},{2,26},{26,2},{3,27},{27,3},{4,28},{28... | collective-permute-start | bytes 3145736 | tf_op jit(solution)/shard_map/ppermute | solution.py:382
  33.2 2.2 %shard_map.41 = (bf16[512,1024]{1,0:T(8,128)(2,1)S(1)}, f32[1,1024]{1,0:T(1,128)S(1)}, bf16[512,1024]{1,0:T(8,128)(2,1)S(1)}, f32[1,1024]{1,0:T(1,128)S(1)}, f32...) custom-call(s32[8]{0:T(128)S(1)} %broadcast_xor_fusion.order, s32[1]{0:T(128)} %bitcast.middle, ...), custom_call_target="tpu_custom_call" | custom-call | tf_op jit(solution)/shard_map/pallas_call | solution.py:19
  35.5 2.5 %collective-permute-start.12 = (bf16[256,512]{1,0:T(8,128)(2,1)S(1)}, bf16[256,512]{1,0:T(8,128)(2,1)S(1)}, u32[]{:S(2)}, u32[]{:S(2)}) collective-permute-start(bf16[256,512]{1,0:T(8,128)(2,1)S(1)} %get-tuple-element.56), channel_id=1, source_target_pairs={{0,1},{1,0},{2,3},{3,2},{4,5},{5,4},{6,7},{7,6},{8,9},{9,8},{10,11... | collective-permute-start | bytes 786440 | tf_op jit(solution)/shard_map/ppermute | solution.py:315
  39.2 1.3 %collective-permute-start.13 = (bf16[64,512]{1,0:T(8,128)(2,1)S(1)}, bf16[64,512]{1,0:T(8,128)(2,1)S(1)}, u32[]{:S(2)}, u32[]{:S(2)}) collective-permute-start(bf16[64,512]{1,0:T(8,128)(2,1)S(1)} %get-tuple-element.58), channel_id=1, source_target_pairs={{0,2},{1,3},{2,0},{3,1},{4,6},{5,7},{6,4},{7,5},{8,10},{9,11},{10,... | collective-permute-start | bytes 196616 | tf_op jit(solution)/shard_map/ppermute | solution.py:315
  43.6 2.1 %collective-permute-done.15.c = bf16[64,512]{1,0:T(8,128)(2,1)S(1)} collective-permute-done((bf16[64,512]{1,0:T(8,128)(2,1)S(1)}, bf16[64,512]{1,0:T(8,128)(2,1)S(1)}, u32[]{:S(2)}, u32[]{:S(2)}) %collective-permute-start.15) | collective-permute-done | bytes 65568 | tf_op jit(solution)/shard_map/ppermute | solution.py:315
  46.5 2.0 %collective-permute-start.18 = (bf16[64,512]{1,0:T(8,128)(2,1)S(1)}, bf16[64,512]{1,0:T(8,128)(2,1)S(1)}, u32[]{:S(2)}, u32[]{:S(2)}) collective-permute-start(bf16[64,512]{1,0:T(8,128)(2,1)S(1)} %shard_map.43.refs_0_.first), channel_id=1, source_target_pairs={{0,6},{1,7},{2,4},{3,5},{4,2},{5,3},{6,0},{7,1},{8,14},{9,15},{10,... | collective-permute-start | bytes 196616 | tf_op jit(solution)/shard_map/ppermute | solution.py:315
  48.5 1.3 %shard_map.44 = (f32[256,1024]{1,0:T(8,128)S(1)}, bf16[256,1024]{1,0:T(8,128)(2,1)S(1)}) custom-call(s32[1]{0:T(128)} %bitcast.middle, bf16[512,1024]{1,0:T(8,128)(2,1)S(1)} %get-tuple-element.71.turned, bf16[512,1024]{1,0:T(8,128)(2,1)S(1)} %get-tuple-element.62.beside, bf16[512,1024]{1,0:T(8,128)(2,1)S(1)} %get-tuple-element.63.opposite.swapped), custom_call_target="tpu_custom_call" | custom-call | tf_op jit(solution)/shard_map/pallas_call | solution.py:19
  50.5 3.7 %collective-permute-start.19 = (bf16[256,512]{1,0:T(8,128)(2,1)S(1)}, bf16[256,512]{1,0:T(8,128)(2,1)S(1)}, u32[]{:S(2)}, u32[]{:S(2)}) collective-permute-start(bf16[256,512]{1,0:T(8,128)(2,1)S(1)} %shard_map.45.near), channel_id=1, source_target_pairs={{0,1},{1,0},{2,3},{3,2},{4,5},{5,4},{6,7},{7,6},{8,9},{9,8},{10,11... | collective-permute-start | bytes 786440 | tf_op jit(solution)/shard_map/ppermute | solution.py:315
  55.4 1.8 %shard_map.46 = (bf16[512,1024]{1,0:T(8,128)(2,1)S(1)}, bf16[512,1024]{1,0:T(8,128)(2,1)S(1)}) custom-call(s32[8]{0:T(128)S(1)} %broadcast_xor_fusion.order, s32[1]{0:T(128)} %bitcast.middle, bf16[256,512]{1,0:T(8,128)(2,1)S(1)} %shard_map.45.near, bf16[256,512]{1,0:T(8,128)(2,1)S(1)} %collective-permute-done.19.far, ...), custom_call_target="tpu_custom_call" | custom-call | tf_op jit(solution)/shard_map/pallas_call | solution.py:19
  57.2 1.4 %collective-permute-start.29 = (bf16[512,1024]{1,0:T(8,128)(2,1)S(1)}, bf16[512,1024]{1,0:T(8,128)(2,1)S(1)}, u32[]{:S(2)}, u32[]{:S(2)}) collective-permute-start(bf16[512,1024]{1,0:T(8,128)(2,1)S(1)} %get-tuple-element.69), channel_id=1, source_target_pairs={{8,0},{16,24},{9,1},{17,25},{10,2},{18,26},{11,3},{19,27},{12,4},{... | collective-permute-start | bytes 3145736 | tf_op jit(solution)/shard_map/ppermute | solution.py:399
  59.6 2.8 %collective-permute-start.31 = (bf16[512,1024]{1,0:T(8,128)(2,1)S(1)}, bf16[512,1024]{1,0:T(8,128)(2,1)S(1)}, u32[]{:S(2)}, u32[]{:S(2)}) collective-permute-start(bf16[512,1024]{1,0:T(8,128)(2,1)S(1)} %get-tuple-element.86), channel_id=1, source_target_pairs={{8,16},{16,8},{9,17},{17,9},{10,18},{18,10},{11,19},{19,11},{12,20... | collective-permute-start | bytes 3145736 | tf_op jit(solution)/shard_map/ppermute | solution.py:399
  62.5 1.3 %collective-permute-start.22 = (bf16[64,1024]{1,0:T(8,128)(2,1)S(1)}, bf16[64,1024]{1,0:T(8,128)(2,1)S(1)}, u32[]{:S(2)}, u32[]{:S(2)}) collective-permute-start(bf16[64,1024]{1,0:T(8,128)(2,1)S(1)} %get-tuple-element.76), channel_id=1, source_target_pairs={{0,2},{1,3},{2,0},{3,1},{4,6},{5,7},{6,4},{7,5},{8,10},{9,11},{10,... | collective-permute-start | bytes 393224 | tf_op jit(solution)/shard_map/ppermute | solution.py:315
  65.2 2.6 %shard_map.50.held = f32[512,1024]{1,0:T(8,128)S(1)} custom-call(s32[8]{0:T(128)S(1)} %broadcast_xor_fusion.order, s32[1]{0:T(128)} %bitcast.middle, bf16[256,640]{1,0:T(8,128)(2,1)S(1)} %pad_maximum_fusion.near, bf16[256,640]{1,0:T(8,128)(2,1)S(1)} %collective-permute-done.25.far, bf16[512,1024]{1,0:T(8,128)(2,1)S(1)} %get-tuple-element.79.own, ...), custom_call_target="tpu_custom_call" | custom-call | tf_op jit(solution)/shard_map/pallas_call | solution.py:19
  67.8 2.7 %collective-permute-done.24.c = bf16[64,1024]{1,0:T(8,128)(2,1)S(1)} collective-permute-done((bf16[64,1024]{1,0:T(8,128)(2,1)S(1)}, bf16[64,1024]{1,0:T(8,128)(2,1)S(1)}, u32[]{:S(2)}, u32[]{:S(2)}) %collective-permute-start.24) | collective-permute-done | bytes 131104 | tf_op jit(solution)/shard_map/ppermute | solution.py:315
  70.6 1.4 %collective-permute-start.26 = (bf16[64,1024]{1,0:T(8,128)(2,1)S(1)}, bf16[64,1024]{1,0:T(8,128)(2,1)S(1)}, u32[]{:S(2)}, u32[]{:S(2)}) collective-permute-start(bf16[64,1024]{1,0:T(8,128)(2,1)S(1)} %shard_map.49.refs_0_), channel_id=1, source_target_pairs={{0,2},{1,3},{2,0},{3,1},{4,6},{5,7},{6,4},{7,5},{8,10},{9,11},{10,... | collective-permute-start | bytes 393224 | tf_op jit(solution)/shard_map/ppermute | solution.py:315
  73.3 1.5 %collective-permute-done.26.refs_1_ = bf16[64,1024]{1,0:T(8,128)(2,1)S(1)} collective-permute-done((bf16[64,1024]{1,0:T(8,128)(2,1)S(1)}, bf16[64,1024]{1,0:T(8,128)(2,1)S(1)}, u32[]{:S(2)}, u32[]{:S(2)}) %collective-permute-start.26) | collective-permute-done | bytes 131104 | tf_op jit(solution)/shard_map/ppermute | solution.py:315
  74.8 2.6 %collective-permute-done.27.refs_2_ = bf16[64,1024]{1,0:T(8,128)(2,1)S(1)} collective-permute-done((bf16[64,1024]{1,0:T(8,128)(2,1)S(1)}, bf16[64,1024]{1,0:T(8,128)(2,1)S(1)}, u32[]{:S(2)}, u32[]{:S(2)}) %collective-permute-start.27) | collective-permute-done | bytes 131104 | tf_op jit(solution)/shard_map/ppermute | solution.py:315
  77.6 3.2 %collective-permute-done.29.out = bf16[512,1024]{1,0:T(8,128)(2,1)S(1)} collective-permute-done((bf16[512,1024]{1,0:T(8,128)(2,1)S(1)}, bf16[512,1024]{1,0:T(8,128)(2,1)S(1)}, u32[]{:S(2)}, u32[]{:S(2)}) %collective-permute-start.29) | collective-permute-done | bytes 1048608 | tf_op jit(solution)/shard_map/ppermute | solution.py:399
  81.9 3.8 %collective-permute-done.31.over = bf16[512,1024]{1,0:T(8,128)(2,1)S(1)} collective-permute-done((bf16[512,1024]{1,0:T(8,128)(2,1)S(1)}, bf16[512,1024]{1,0:T(8,128)(2,1)S(1)}, u32[]{:S(2)}, u32[]{:S(2)}) %collective-permute-start.31) | collective-permute-done | bytes 1048608 | tf_op jit(solution)/shard_map/ppermute | solution.py:399
  85.7 3.0 %shard_map.52 = f32[512,1024]{1,0:T(8,128)} custom-call(s32[8]{0:T(128)S(1)} %broadcast_xor_fusion.order, s32[1]{0:T(128)} %bitcast.middle, bf16[256,1024]{1,0:T(8,128)(2,1)S(1)} %shard_map.51.near, bf16[256,1024]{1,0:T(8,128)(2,1)S(1)} %collective-permute-done.30.far, bf16[512,1024]{1,0:T(8,128)(2,1)S(1)} %get-tuple-element.62.beside, ...), custom_call_target="tpu_custom_call" | custom-call | tf_op jit(solution)/shard_map/pallas_call | solution.py:19
  (53 shorter events, 20.8 us)
Async XLA Ops:
  1.5 8.5 %collective-permute-start.2 = (f32[2,1024]{1,0:T(2,128)S(1)}, f32[2,1024]{1,0:T(2,128)S(1)}, u32[]{:S(2)}, u32[]{:S(2)}) collective-permute-start(f32[2,1024]{1,0:T(2,128)S(1)} %shard_map.37), channel_id=1, source_target_pairs={{0,24},{8,0},{16,8},{24,16},{1,25},{9,1},{17,9},{25,17},{2,26},{10... | collective-permute-start | bytes 24584 | tf_op jit(solution)/shard_map/ppermute | solution.py:363
  1.6 8.4 %collective-permute-start.1 = (f32[2,1024]{1,0:T(2,128)S(1)}, f32[2,1024]{1,0:T(2,128)S(1)}, u32[]{:S(2)}, u32[]{:S(2)}) collective-permute-start(f32[2,1024]{1,0:T(2,128)S(1)} %shard_map.37), channel_id=1, source_target_pairs={{0,16},{8,24},{16,0},{24,8},{1,17},{9,25},{17,1},{25,9},{2,18},{10... | collective-permute-start | bytes 24584 | tf_op jit(solution)/shard_map/ppermute | solution.py:363
  4.1 6.0 %collective-permute-start = (f32[2,1024]{1,0:T(2,128)S(1)}, f32[2,1024]{1,0:T(2,128)S(1)}, u32[]{:S(2)}, u32[]{:S(2)}) collective-permute-start(f32[2,1024]{1,0:T(2,128)S(1)} %shard_map.37), channel_id=1, source_target_pairs={{0,8},{8,16},{16,24},{24,0},{1,9},{9,17},{17,25},{25,1},{2,10},{10... | collective-permute-start | bytes 24584 | tf_op jit(solution)/shard_map/ppermute | solution.py:363
  6.3 23.4 %collective-permute-start.10 = (bf16[512,1024]{1,0:T(8,128)(2,1)}, bf16[512,1024]{1,0:T(8,128)(2,1)S(1)}, u32[]{:S(2)}, u32[]{:S(2)}) collective-permute-start(bf16[512,1024]{1,0:T(8,128)(2,1)} %z.5), channel_id=1, source_target_pairs={{0,8},{8,0},{16,24},{24,16},{1,9},{9,1},{17,25},{25,17},{2,10},{10... | collective-permute-start | bytes 3145736 | tf_op jit(solution)/shard_map/ppermute | solution.py:366
  6.3 25.3 %collective-permute-start.11 = (bf16[512,1024]{1,0:T(8,128)(2,1)}, bf16[512,1024]{1,0:T(8,128)(2,1)}, u32[]{:S(2)}, u32[]{:S(2)}) collective-permute-start(bf16[512,1024]{1,0:T(8,128)(2,1)} %z.5), channel_id=1, source_target_pairs={{8,16},{16,8},{9,17},{17,9},{10,18},{18,10},{11,19},{19,11},{12,20... | collective-permute-start | bytes 3145736 | tf_op jit(solution)/shard_map/ppermute | solution.py:367
  12.5 3.1 %collective-permute-start.3 = (bf16[256,640]{1,0:T(8,128)(2,1)S(1)}, bf16[256,640]{1,0:T(8,128)(2,1)S(1)}, u32[]{:S(2)}, u32[]{:S(2)}) collective-permute-start(bf16[256,640]{1,0:T(8,128)(2,1)S(1)} %get-tuple-element.48), channel_id=1, source_target_pairs={{0,1},{1,0},{2,3},{3,2},{4,5},{5,4},{6,7},{7,6},{8,9},{9,8},{10,11... | collective-permute-start | bytes 983048 | tf_op jit(solution)/shard_map/ppermute | solution.py:315
  15.7 3.8 %collective-permute-start.4 = (bf16[64,640]{1,0:T(8,128)(2,1)S(1)}, bf16[64,640]{1,0:T(8,128)(2,1)S(1)}, u32[]{:S(2)}, u32[]{:S(2)}) collective-permute-start(bf16[64,640]{1,0:T(8,128)(2,1)S(1)} %get-tuple-element.50), channel_id=1, source_target_pairs={{0,2},{1,3},{2,0},{3,1},{4,6},{5,7},{6,4},{7,5},{8,10},{9,11},{10,... | collective-permute-start | bytes 245768 | tf_op jit(solution)/shard_map/ppermute | solution.py:315
  17.0 3.7 %collective-permute-start.5 = (bf16[64,640]{1,0:T(8,128)(2,1)S(1)}, bf16[64,640]{1,0:T(8,128)(2,1)S(1)}, u32[]{:S(2)}, u32[]{:S(2)}) collective-permute-start(bf16[64,640]{1,0:T(8,128)(2,1)S(1)} %get-tuple-element.51), channel_id=1, source_target_pairs={{0,4},{1,5},{2,6},{3,7},{4,0},{5,1},{6,2},{7,3},{8,12},{9,13},{10,... | collective-permute-start | bytes 245768 | tf_op jit(solution)/shard_map/ppermute | solution.py:315
  18.2 4.2 %collective-permute-start.6 = (bf16[64,640]{1,0:T(8,128)(2,1)S(1)}, bf16[64,640]{1,0:T(8,128)(2,1)S(1)}, u32[]{:S(2)}, u32[]{:S(2)}) collective-permute-start(bf16[64,640]{1,0:T(8,128)(2,1)S(1)} %get-tuple-element.52), channel_id=1, source_target_pairs={{0,6},{1,7},{2,4},{3,5},{4,2},{5,3},{6,0},{7,1},{8,14},{9,15},{10,... | collective-permute-start | bytes 245768 | tf_op jit(solution)/shard_map/ppermute | solution.py:315
  22.5 4.4 %collective-permute-start.9 = (bf16[64,640]{1,0:T(8,128)(2,1)S(1)}, bf16[64,640]{1,0:T(8,128)(2,1)S(1)}, u32[]{:S(2)}, u32[]{:S(2)}) collective-permute-start(bf16[64,640]{1,0:T(8,128)(2,1)S(1)} %shard_map.40), channel_id=1, source_target_pairs={{0,6},{1,7},{2,4},{3,5},{4,2},{5,3},{6,0},{7,1},{8,14},{9,15},{10,... | collective-permute-start | bytes 245768 | tf_op jit(solution)/shard_map/ppermute | solution.py:315
  23.2 4.6 %collective-permute-start.8 = (bf16[64,640]{1,0:T(8,128)(2,1)S(1)}, bf16[64,640]{1,0:T(8,128)(2,1)S(1)}, u32[]{:S(2)}, u32[]{:S(2)}) collective-permute-start(bf16[64,640]{1,0:T(8,128)(2,1)S(1)} %shard_map.40), channel_id=1, source_target_pairs={{0,4},{1,5},{2,6},{3,7},{4,0},{5,1},{6,2},{7,3},{8,12},{9,13},{10,... | collective-permute-start | bytes 245768 | tf_op jit(solution)/shard_map/ppermute | solution.py:315
  24.4 3.7 %collective-permute-start.7 = (bf16[64,640]{1,0:T(8,128)(2,1)S(1)}, bf16[64,640]{1,0:T(8,128)(2,1)S(1)}, u32[]{:S(2)}, u32[]{:S(2)}) collective-permute-start(bf16[64,640]{1,0:T(8,128)(2,1)S(1)} %shard_map.40), channel_id=1, source_target_pairs={{0,2},{1,3},{2,0},{3,1},{4,6},{5,7},{6,4},{7,5},{8,10},{9,11},{10,... | collective-permute-start | bytes 245768 | tf_op jit(solution)/shard_map/ppermute | solution.py:315
  31.6 27.0 %collective-permute-start.20 = (bf16[512,1024]{1,0:T(8,128)(2,1)}, bf16[512,1024]{1,0:T(8,128)(2,1)}, u32[]{:S(2)}, u32[]{:S(2)}) collective-permute-start(bf16[512,1024]{1,0:T(8,128)(2,1)} %z.5), channel_id=1, source_target_pairs={{0,24},{24,0},{1,25},{25,1},{2,26},{26,2},{3,27},{27,3},{4,28},{28... | collective-permute-start | bytes 3145736 | tf_op jit(solution)/shard_map/ppermute | solution.py:382
  35.5 3.7 %collective-permute-start.12 = (bf16[256,512]{1,0:T(8,128)(2,1)S(1)}, bf16[256,512]{1,0:T(8,128)(2,1)S(1)}, u32[]{:S(2)}, u32[]{:S(2)}) collective-permute-start(bf16[256,512]{1,0:T(8,128)(2,1)S(1)} %get-tuple-element.56), channel_id=1, source_target_pairs={{0,1},{1,0},{2,3},{3,2},{4,5},{5,4},{6,7},{7,6},{8,9},{9,8},{10,11... | collective-permute-start | bytes 786440 | tf_op jit(solution)/shard_map/ppermute | solution.py:315
  39.2 3.2 %collective-permute-start.13 = (bf16[64,512]{1,0:T(8,128)(2,1)S(1)}, bf16[64,512]{1,0:T(8,128)(2,1)S(1)}, u32[]{:S(2)}, u32[]{:S(2)}) collective-permute-start(bf16[64,512]{1,0:T(8,128)(2,1)S(1)} %get-tuple-element.58), channel_id=1, source_target_pairs={{0,2},{1,3},{2,0},{3,1},{4,6},{5,7},{6,4},{7,5},{8,10},{9,11},{10,... | collective-permute-start | bytes 196616 | tf_op jit(solution)/shard_map/ppermute | solution.py:315
  40.5 3.1 %collective-permute-start.14 = (bf16[64,512]{1,0:T(8,128)(2,1)S(1)}, bf16[64,512]{1,0:T(8,128)(2,1)S(1)}, u32[]{:S(2)}, u32[]{:S(2)}) collective-permute-start(bf16[64,512]{1,0:T(8,128)(2,1)S(1)} %get-tuple-element.59), channel_id=1, source_target_pairs={{0,4},{1,5},{2,6},{3,7},{4,0},{5,1},{6,2},{7,3},{8,12},{9,13},{10,... | collective-permute-start | bytes 196616 | tf_op jit(solution)/shard_map/ppermute | solution.py:315
  41.7 4.0 %collective-permute-start.15 = (bf16[64,512]{1,0:T(8,128)(2,1)S(1)}, bf16[64,512]{1,0:T(8,128)(2,1)S(1)}, u32[]{:S(2)}, u32[]{:S(2)}) collective-permute-start(bf16[64,512]{1,0:T(8,128)(2,1)S(1)} %get-tuple-element.60), channel_id=1, source_target_pairs={{0,6},{1,7},{2,4},{3,5},{4,2},{5,3},{6,0},{7,1},{8,14},{9,15},{10,... | collective-permute-start | bytes 196616 | tf_op jit(solution)/shard_map/ppermute | solution.py:315
  45.8 4.0 %collective-permute-start.16 = (bf16[64,512]{1,0:T(8,128)(2,1)S(1)}, bf16[64,512]{1,0:T(8,128)(2,1)S(1)}, u32[]{:S(2)}, u32[]{:S(2)}) collective-permute-start(bf16[64,512]{1,0:T(8,128)(2,1)S(1)} %shard_map.43.refs_0_.first), channel_id=1, source_target_pairs={{0,2},{1,3},{2,0},{3,1},{4,6},{5,7},{6,4},{7,5},{8,10},{9,11},{10,... | collective-permute-start | bytes 196616 | tf_op jit(solution)/shard_map/ppermute | solution.py:315
  46.2 3.6 %collective-permute-start.17 = (bf16[64,512]{1,0:T(8,128)(2,1)S(1)}, bf16[64,512]{1,0:T(8,128)(2,1)S(1)}, u32[]{:S(2)}, u32[]{:S(2)}) collective-permute-start(bf16[64,512]{1,0:T(8,128)(2,1)S(1)} %shard_map.43.refs_0_.first), channel_id=1, source_target_pairs={{0,4},{1,5},{2,6},{3,7},{4,0},{5,1},{6,2},{7,3},{8,12},{9,13},{10,... | collective-permute-start | bytes 196616 | tf_op jit(solution)/shard_map/ppermute | solution.py:315
  46.5 4.0 %collective-permute-start.18 = (bf16[64,512]{1,0:T(8,128)(2,1)S(1)}, bf16[64,512]{1,0:T(8,128)(2,1)S(1)}, u32[]{:S(2)}, u32[]{:S(2)}) collective-permute-start(bf16[64,512]{1,0:T(8,128)(2,1)S(1)} %shard_map.43.refs_0_.first), channel_id=1, source_target_pairs={{0,6},{1,7},{2,4},{3,5},{4,2},{5,3},{6,0},{7,1},{8,14},{9,15},{10,... | collective-permute-start | bytes 196616 | tf_op jit(solution)/shard_map/ppermute | solution.py:315
  50.5 4.9 %collective-permute-start.19 = (bf16[256,512]{1,0:T(8,128)(2,1)S(1)}, bf16[256,512]{1,0:T(8,128)(2,1)S(1)}, u32[]{:S(2)}, u32[]{:S(2)}) collective-permute-start(bf16[256,512]{1,0:T(8,128)(2,1)S(1)} %shard_map.45.near), channel_id=1, source_target_pairs={{0,1},{1,0},{2,3},{3,2},{4,5},{5,4},{6,7},{7,6},{8,9},{9,8},{10,11... | collective-permute-start | bytes 786440 | tf_op jit(solution)/shard_map/ppermute | solution.py:315
  57.2 23.5 %collective-permute-start.29 = (bf16[512,1024]{1,0:T(8,128)(2,1)S(1)}, bf16[512,1024]{1,0:T(8,128)(2,1)S(1)}, u32[]{:S(2)}, u32[]{:S(2)}) collective-permute-start(bf16[512,1024]{1,0:T(8,128)(2,1)S(1)} %get-tuple-element.69), channel_id=1, source_target_pairs={{8,0},{16,24},{9,1},{17,25},{10,2},{18,26},{11,3},{19,27},{12,4},{... | collective-permute-start | bytes 3145736 | tf_op jit(solution)/shard_map/ppermute | solution.py:399
  58.8 3.6 %collective-permute-start.21 = (bf16[256,1024]{1,0:T(8,128)(2,1)S(1)}, bf16[256,1024]{1,0:T(8,128)(2,1)S(1)}, u32[]{:S(2)}, u32[]{:S(2)}) collective-permute-start(bf16[256,1024]{1,0:T(8,128)(2,1)S(1)} %get-tuple-element.74), channel_id=1, source_target_pairs={{0,1},{1,0},{2,3},{3,2},{4,5},{5,4},{6,7},{7,6},{8,9},{9,8},{10,11... | collective-permute-start | bytes 1572872 | tf_op jit(solution)/shard_map/ppermute | solution.py:315
  59.5 5.5 %collective-permute-start.25 = (bf16[256,640]{1,0:T(8,128)(2,1)S(1)}, bf16[256,640]{1,0:T(8,128)(2,1)S(1)}, u32[]{:S(2)}, u32[]{:S(2)}) collective-permute-start(bf16[256,640]{1,0:T(8,128)(2,1)S(1)} %pad_maximum_fusion.near), channel_id=1, source_target_pairs={{0,1},{1,0},{2,3},{3,2},{4,5},{5,4},{6,7},{7,6},{8,9},{9,8},{10,11... | collective-permute-start | bytes 983048 | tf_op jit(solution)/shard_map/ppermute | solution.py:315
  59.6 26.2 %collective-permute-start.31 = (bf16[512,1024]{1,0:T(8,128)(2,1)S(1)}, bf16[512,1024]{1,0:T(8,128)(2,1)S(1)}, u32[]{:S(2)}, u32[]{:S(2)}) collective-permute-start(bf16[512,1024]{1,0:T(8,128)(2,1)S(1)} %get-tuple-element.86), channel_id=1, source_target_pairs={{8,16},{16,8},{9,17},{17,9},{10,18},{18,10},{11,19},{19,11},{12,20... | collective-permute-start | bytes 3145736 | tf_op jit(solution)/shard_map/ppermute | solution.py:399
  62.5 5.3 %collective-permute-start.22 = (bf16[64,1024]{1,0:T(8,128)(2,1)S(1)}, bf16[64,1024]{1,0:T(8,128)(2,1)S(1)}, u32[]{:S(2)}, u32[]{:S(2)}) collective-permute-start(bf16[64,1024]{1,0:T(8,128)(2,1)S(1)} %get-tuple-element.76), channel_id=1, source_target_pairs={{0,2},{1,3},{2,0},{3,1},{4,6},{5,7},{6,4},{7,5},{8,10},{9,11},{10,... | collective-permute-start | bytes 393224 | tf_op jit(solution)/shard_map/ppermute | solution.py:315
  63.7 4.1 %collective-permute-start.23 = (bf16[64,1024]{1,0:T(8,128)(2,1)S(1)}, bf16[64,1024]{1,0:T(8,128)(2,1)S(1)}, u32[]{:S(2)}, u32[]{:S(2)}) collective-permute-start(bf16[64,1024]{1,0:T(8,128)(2,1)S(1)} %get-tuple-element.77), channel_id=1, source_target_pairs={{0,4},{1,5},{2,6},{3,7},{4,0},{5,1},{6,2},{7,3},{8,12},{9,13},{10,... | collective-permute-start | bytes 393224 | tf_op jit(solution)/shard_map/ppermute | solution.py:315
  65.0 5.5 %collective-permute-start.24 = (bf16[64,1024]{1,0:T(8,128)(2,1)S(1)}, bf16[64,1024]{1,0:T(8,128)(2,1)S(1)}, u32[]{:S(2)}, u32[]{:S(2)}) collective-permute-start(bf16[64,1024]{1,0:T(8,128)(2,1)S(1)} %get-tuple-element.78), channel_id=1, source_target_pairs={{0,6},{1,7},{2,4},{3,5},{4,2},{5,3},{6,0},{7,1},{8,14},{9,15},{10,... | collective-permute-start | bytes 393224 | tf_op jit(solution)/shard_map/ppermute | solution.py:315
  70.6 4.2 %collective-permute-start.26 = (bf16[64,1024]{1,0:T(8,128)(2,1)S(1)}, bf16[64,1024]{1,0:T(8,128)(2,1)S(1)}, u32[]{:S(2)}, u32[]{:S(2)}) collective-permute-start(bf16[64,1024]{1,0:T(8,128)(2,1)S(1)} %shard_map.49.refs_0_), channel_id=1, source_target_pairs={{0,2},{1,3},{2,0},{3,1},{4,6},{5,7},{6,4},{7,5},{8,10},{9,11},{10,... | collective-permute-start | bytes 393224 | tf_op jit(solution)/shard_map/ppermute | solution.py:315
  72.0 5.3 %collective-permute-start.27 = (bf16[64,1024]{1,0:T(8,128)(2,1)S(1)}, bf16[64,1024]{1,0:T(8,128)(2,1)S(1)}, u32[]{:S(2)}, u32[]{:S(2)}) collective-permute-start(bf16[64,1024]{1,0:T(8,128)(2,1)S(1)} %shard_map.49.refs_0_), channel_id=1, source_target_pairs={{0,4},{1,5},{2,6},{3,7},{4,0},{5,1},{6,2},{7,3},{8,12},{9,13},{10,... | collective-permute-start | bytes 393224 | tf_op jit(solution)/shard_map/ppermute | solution.py:315
  72.3 5.3 %collective-permute-start.28 = (bf16[64,1024]{1,0:T(8,128)(2,1)S(1)}, bf16[64,1024]{1,0:T(8,128)(2,1)S(1)}, u32[]{:S(2)}, u32[]{:S(2)}) collective-permute-start(bf16[64,1024]{1,0:T(8,128)(2,1)S(1)} %shard_map.49.refs_0_), channel_id=1, source_target_pairs={{0,6},{1,7},{2,4},{3,5},{4,2},{5,3},{6,0},{7,1},{8,14},{9,15},{10,... | collective-permute-start | bytes 393224 | tf_op jit(solution)/shard_map/ppermute | solution.py:315
  80.7 5.0 %collective-permute-start.30 = (bf16[256,1024]{1,0:T(8,128)(2,1)S(1)}, bf16[256,1024]{1,0:T(8,128)(2,1)S(1)}, u32[]{:S(2)}, u32[]{:S(2)}) collective-permute-start(bf16[256,1024]{1,0:T(8,128)(2,1)S(1)} %shard_map.51.near), channel_id=1, source_target_pairs={{0,1},{1,0},{2,3},{3,2},{4,5},{5,4},{6,7},{7,6},{8,9},{9,8},{10,11... | collective-permute-start | bytes 1572872 | tf_op jit(solution)/shard_map/ppermute | solution.py:315
  (1 other events, 6.5 us)

commit v25 on v24

--- a/solution.py
+++ b/solution.py
@@ -357,7 +357,7 @@
     flat, block = ((1, width), jnp.float32), ((rows, width), jnp.bfloat16)
 
     stats = kernel_call(
-        stats_kernel, [((2, width), jnp.float32)], scratch=12, temps=[block], sems=4, outside=0
+        stats_kernel, [((2, width), jnp.float32)], scratch=8, temps=[block], sems=4, outside=0
     )(z_anchor)[0]
     all_stats = [stats] + [
         lax.ppermute(stats, "dp", [(i, (i + k) % 4) for i in range(4)]) for k in (1, 2, 3)
@@ -375,7 +375,7 @@
         return [((half, n), jnp.float32), ((half, n), jnp.bfloat16)]
 
     own, turned, own_square, kept, sent = kernel_call(
-        own_kernel, [block, block, flat, *summands(rows + NORM)], smem=1, scratch=12
+        own_kernel, [block, block, flat, *summands(rows + NORM)], smem=1, scratch=8
     )(order, z_anchor, mean)
     near_own = scatter(*halve(kept, sent, rows), last=rows)
     near_own = jnp.concatenate([near_own] + [to_partner(near_own, 2 * k) for k in (1, 2, 3)])
@@ -383,16 +383,16 @@
 
     beside, beside_square, swapped, swapped_square, kept, sent = kernel_call(
         first_kernel, [block, flat, block, flat, *summands(rows)],
-        smem=2, scratch=12, temps=[block],
+        smem=2, scratch=8, temps=[block],
     )(order, middle, after(turned, near_own), beside_in, swapped, mean)
     first = scatter(*halve(kept, sent))
     kept_early, sent_early = kernel_call(
-        early_kernel, summands(2 * rows), smem=1, scratch=12
+        early_kernel, summands(2 * rows), smem=1, scratch=8
     )(middle, after(turned, first), beside, swapped)
     far_own = to_partner(near_own, 1)
     near = after(gather_chips(first), sent_early)
     ready = kernel_call(
-        push_kernel, [block, block], smem=2, scratch=12, temps=[((rows, rows), jnp.bfloat16)]
+        push_kernel, [block, block], smem=2, scratch=8, temps=[((rows, rows), jnp.bfloat16)]
     )(order, middle, near, to_partner(near, 1), beside, swapped, beside_square, swapped_square)
     out, over = ready
     pushed = [
@@ -401,7 +401,7 @@
 
     end, end_square, kept, sent = kernel_call(
         late_kernel, [block, flat, summands(rows)[0], summands(2 * rows)[1]],
-        smem=1, scratch=12, temps=[block], sems=4, outside=3,
+        smem=1, scratch=8, temps=[block], sems=4, outside=3,
     )(middle, after(turned, *ready), sent_early, end, mean)
     eighth = (rows // 8, 2 * rows)
     halved = kernel_call(
@@ -410,7 +410,7 @@
     result = ((rows, width), jnp.float32)
     held = kernel_call(
         functools.partial(held_kernel, total), [result],
-        smem=2, scratch=12, temps=[((rows, rows + NORM), jnp.bfloat16)],
+        smem=2, scratch=8, temps=[((rows, rows + NORM), jnp.bfloat16)],
     )(
         order, middle, near_own, far_own, own, z_anchor, z_other,
         own_square, beside_square, swapped_square, after(end_square, halved[0]), mean, spread,
@@ -422,7 +422,7 @@
     near = after(gather_chips(after(second, held)), pushed[0])
     return kernel_call(
         functools.partial(last_kernel, total), [result],
-        smem=2, scratch=12, temps=[((rows, 2 * rows), jnp.bfloat16), result], sems=4, out=pl.ANY,
+        smem=2, scratch=8, temps=[((rows, 2 * rows), jnp.bfloat16), result], sems=4, out=pl.ANY,
     )(
         order, middle, near, to_partner(near, 1), beside, swapped, end, held, *pushed
     )[0]

time: 90 us -> 90 us (level)
  no operation moved by 1% of the time
where the time goes in v25:
time: 90 us; the launch traced here: 88.8 us
  starting transfers between devices  40 us (44%)
  waiting for transfers between devices  32.3 us (36%)
  Pallas kernels  15.5 us (17%)
    ppermute x24, starting transfers between devices, to_partner(): return lax.ppermute(x, 'feat', [(i, i ^ step) for i in range(8)])  26.3 us
    ppermute x24, waiting for transfers between devices, to_partner(): return lax.ppermute(x, 'feat', [(i, i ^ step) for i in range(8)])  21.8 us
    pallas_call x16, Pallas kernels, call(): pl.pallas_call(body, out_shape=[jax.ShapeDtypeStruct(s, t) for s, t in ou...  15.5 us
    ppermute x3, starting transfers between devices, by_line(): lax.ppermute(stats, 'dp', [(i, (i + k) % 4) for i in range(4)])  4.72 us
    ppermute x1, waiting for transfers between devices, by_line(): lax.ppermute(after(over, end), 'dp', across)  3.81 us
    ppermute x1, waiting for transfers between devices, by_line(): lax.ppermute(out, 'dp', outward)  3.16 us
    ppermute x1, starting transfers between devices, by_line(): swapped = lax.ppermute(ahead, 'dp', across)  3.08 us
    ppermute x1, starting transfers between devices, by_line(): lax.ppermute(after(over, end), 'dp', across)  2.77 us
  transfers between devices with their start and end apart: 32, of which 22 were waited for; matrix products, arithmetic and copies ran while one was open for 1% of the time, Pallas kernels for 12%

profile of v25, /device:TPU:9, one launch (start us, length us, event | category | flops | bytes accessed | tf_op | source)
XLA Modules:
  0.0 88.8 jit_solution(17627516340536184991)
XLA Ops:
  0.0 1.5 %shard_map.37 = f32[2,1024]{1,0:T(2,128)S(1)} custom-call(bf16[512,1024]{1,0:T(8,128)(2,1)} %z.5), custom_call_target="tpu_custom_call" | custom-call | tf_op jit(solution)/shard_map/pallas_call | solution.py:19
  1.6 2.5 %collective-permute-start.1 = (f32[2,1024]{1,0:T(2,128)S(1)}, f32[2,1024]{1,0:T(2,128)S(1)}, u32[]{:S(2)}, u32[]{:S(2)}) collective-permute-start(f32[2,1024]{1,0:T(2,128)S(1)} %shard_map.37), channel_id=1, source_target_pairs={{0,16},{8,24},{16,0},{24,8},{1,17},{9,25},{17,1},{25,9},{2,18},{10... | collective-permute-start | bytes 24584 | tf_op jit(solution)/shard_map/ppermute | solution.py:363
  4.1 2.2 %collective-permute-start = (f32[2,1024]{1,0:T(2,128)S(1)}, f32[2,1024]{1,0:T(2,128)S(1)}, u32[]{:S(2)}, u32[]{:S(2)}) collective-permute-start(f32[2,1024]{1,0:T(2,128)S(1)} %shard_map.37), channel_id=1, source_target_pairs={{0,8},{8,16},{16,24},{24,0},{1,9},{9,17},{17,25},{25,1},{2,10},{10... | collective-permute-start | bytes 24584 | tf_op jit(solution)/shard_map/ppermute | solution.py:363
  6.3 3.1 %collective-permute-start.11 = (bf16[512,1024]{1,0:T(8,128)(2,1)}, bf16[512,1024]{1,0:T(8,128)(2,1)}, u32[]{:S(2)}, u32[]{:S(2)}) collective-permute-start(bf16[512,1024]{1,0:T(8,128)(2,1)} %z.5), channel_id=1, source_target_pairs={{8,16},{16,8},{9,17},{17,9},{10,18},{18,10},{11,19},{19,11},{12,20... | collective-permute-start | bytes 3145736 | tf_op jit(solution)/shard_map/ppermute | solution.py:367
  10.1 2.4 %shard_map.38 = (bf16[512,1024]{1,0:T(8,128)(2,1)S(1)}, bf16[512,1024]{1,0:T(8,128)(2,1)S(1)}, f32[1,1024]{1,0:T(1,128)S(1)}, f32[256,640]{1,0:T(8,128)S(1)}, bf16[256,640]{1,0:T(8,128)(2,1)S(1)}) custom-call(s32[8]{0:T(128)S(1)} %broadcast_xor_fusion.order, bf16[512,1024]{1,0:T(8,128)(2,1)} %z.5, f32[1,1024]{1,0:T(1,128)S(1)} %get-tuple-element.88.mean), custom_call_target="tpu_custom_call" | custom-call | tf_op jit(solution)/shard_map/pallas_call | solution.py:19
  12.5 1.9 %collective-permute-start.3 = (bf16[256,640]{1,0:T(8,128)(2,1)S(1)}, bf16[256,640]{1,0:T(8,128)(2,1)S(1)}, u32[]{:S(2)}, u32[]{:S(2)}) collective-permute-start(bf16[256,640]{1,0:T(8,128)(2,1)S(1)} %get-tuple-element.48), channel_id=1, source_target_pairs={{0,1},{1,0},{2,3},{3,2},{4,5},{5,4},{6,7},{7,6},{8,9},{9,8},{10,11... | collective-permute-start | bytes 983048 | tf_op jit(solution)/shard_map/ppermute | solution.py:315
  14.3 1.3 %collective-permute-done.3.got = bf16[256,640]{1,0:T(8,128)(2,1)S(1)} collective-permute-done((bf16[256,640]{1,0:T(8,128)(2,1)S(1)}, bf16[256,640]{1,0:T(8,128)(2,1)S(1)}, u32[]{:S(2)}, u32[]{:S(2)}) %collective-permute-start.3) | collective-permute-done | bytes 327712 | tf_op jit(solution)/shard_map/ppermute | solution.py:315
  15.7 1.3 %collective-permute-start.4 = (bf16[64,640]{1,0:T(8,128)(2,1)S(1)}, bf16[64,640]{1,0:T(8,128)(2,1)S(1)}, u32[]{:S(2)}, u32[]{:S(2)}) collective-permute-start(bf16[64,640]{1,0:T(8,128)(2,1)S(1)} %get-tuple-element.50), channel_id=1, source_target_pairs={{0,2},{1,3},{2,0},{3,1},{4,6},{5,7},{6,4},{7,5},{8,10},{9,11},{10,... | collective-permute-start | bytes 245768 | tf_op jit(solution)/shard_map/ppermute | solution.py:315
  20.7 1.7 %collective-permute-done.6.c = bf16[64,640]{1,0:T(8,128)(2,1)S(1)} collective-permute-done((bf16[64,640]{1,0:T(8,128)(2,1)S(1)}, bf16[64,640]{1,0:T(8,128)(2,1)S(1)}, u32[]{:S(2)}, u32[]{:S(2)}) %collective-permute-start.6) | collective-permute-done | bytes 81952 | tf_op jit(solution)/shard_map/ppermute | solution.py:315
  25.2 1.6 %collective-permute-done.9 = bf16[64,640]{1,0:T(8,128)(2,1)S(1)} collective-permute-done((bf16[64,640]{1,0:T(8,128)(2,1)S(1)}, bf16[64,640]{1,0:T(8,128)(2,1)S(1)}, u32[]{:S(2)}, u32[]{:S(2)}) %collective-permute-start.9) | collective-permute-done | bytes 81952 | tf_op jit(solution)/shard_map/ppermute | solution.py:315
  28.1 1.6 %collective-permute-done.10.beside_in = bf16[512,1024]{1,0:T(8,128)(2,1)S(1)} collective-permute-done((bf16[512,1024]{1,0:T(8,128)(2,1)}, bf16[512,1024]{1,0:T(8,128)(2,1)S(1)}, u32[]{:S(2)}, u32[]{:S(2)}) %collective-permute-start.10) | collective-permute-done | bytes 1048608 | tf_op jit(solution)/shard_map/ppermute | solution.py:366
  29.7 1.9 %collective-permute-done.11.opposite_in = bf16[512,1024]{1,0:T(8,128)(2,1)} collective-permute-done((bf16[512,1024]{1,0:T(8,128)(2,1)}, bf16[512,1024]{1,0:T(8,128)(2,1)}, u32[]{:S(2)}, u32[]{:S(2)}) %collective-permute-start.11) | collective-permute-done | bytes 1048608 | tf_op jit(solution)/shard_map/ppermute | solution.py:367
  31.6 1.6 %collective-permute-start.20 = (bf16[512,1024]{1,0:T(8,128)(2,1)}, bf16[512,1024]{1,0:T(8,128)(2,1)}, u32[]{:S(2)}, u32[]{:S(2)}) collective-permute-start(bf16[512,1024]{1,0:T(8,128)(2,1)} %z.5), channel_id=1, source_target_pairs={{0,24},{24,0},{1,25},{25,1},{2,26},{26,2},{3,27},{27,3},{4,28},{28... | collective-permute-start | bytes 3145736 | tf_op jit(solution)/shard_map/ppermute | solution.py:382
  33.2 2.2 %shard_map.41 = (bf16[512,1024]{1,0:T(8,128)(2,1)S(1)}, f32[1,1024]{1,0:T(1,128)S(1)}, bf16[512,1024]{1,0:T(8,128)(2,1)S(1)}, f32[1,1024]{1,0:T(1,128)S(1)}, f32...) custom-call(s32[8]{0:T(128)S(1)} %broadcast_xor_fusion.order, s32[1]{0:T(128)} %bitcast.middle, ...), custom_call_target="tpu_custom_call" | custom-call | tf_op jit(solution)/shard_map/pallas_call | solution.py:19
  35.5 2.5 %collective-permute-start.12 = (bf16[256,512]{1,0:T(8,128)(2,1)S(1)}, bf16[256,512]{1,0:T(8,128)(2,1)S(1)}, u32[]{:S(2)}, u32[]{:S(2)}) collective-permute-start(bf16[256,512]{1,0:T(8,128)(2,1)S(1)} %get-tuple-element.56), channel_id=1, source_target_pairs={{0,1},{1,0},{2,3},{3,2},{4,5},{5,4},{6,7},{7,6},{8,9},{9,8},{10,11... | collective-permute-start | bytes 786440 | tf_op jit(solution)/shard_map/ppermute | solution.py:315
  39.2 1.3 %collective-permute-start.13 = (bf16[64,512]{1,0:T(8,128)(2,1)S(1)}, bf16[64,512]{1,0:T(8,128)(2,1)S(1)}, u32[]{:S(2)}, u32[]{:S(2)}) collective-permute-start(bf16[64,512]{1,0:T(8,128)(2,1)S(1)} %get-tuple-element.58), channel_id=1, source_target_pairs={{0,2},{1,3},{2,0},{3,1},{4,6},{5,7},{6,4},{7,5},{8,10},{9,11},{10,... | collective-permute-start | bytes 196616 | tf_op jit(solution)/shard_map/ppermute | solution.py:315
  43.6 2.1 %collective-permute-done.15.c = bf16[64,512]{1,0:T(8,128)(2,1)S(1)} collective-permute-done((bf16[64,512]{1,0:T(8,128)(2,1)S(1)}, bf16[64,512]{1,0:T(8,128)(2,1)S(1)}, u32[]{:S(2)}, u32[]{:S(2)}) %collective-permute-start.15) | collective-permute-done | bytes 65568 | tf_op jit(solution)/shard_map/ppermute | solution.py:315
  46.5 2.0 %collective-permute-start.18 = (bf16[64,512]{1,0:T(8,128)(2,1)S(1)}, bf16[64,512]{1,0:T(8,128)(2,1)S(1)}, u32[]{:S(2)}, u32[]{:S(2)}) collective-permute-start(bf16[64,512]{1,0:T(8,128)(2,1)S(1)} %shard_map.43.refs_0_.first), channel_id=1, source_target_pairs={{0,6},{1,7},{2,4},{3,5},{4,2},{5,3},{6,0},{7,1},{8,14},{9,15},{10,... | collective-permute-start | bytes 196616 | tf_op jit(solution)/shard_map/ppermute | solution.py:315
  48.5 1.3 %shard_map.44 = (f32[256,1024]{1,0:T(8,128)S(1)}, bf16[256,1024]{1,0:T(8,128)(2,1)S(1)}) custom-call(s32[1]{0:T(128)} %bitcast.middle, bf16[512,1024]{1,0:T(8,128)(2,1)S(1)} %get-tuple-element.71.turned, bf16[512,1024]{1,0:T(8,128)(2,1)S(1)} %get-tuple-element.62.beside, bf16[512,1024]{1,0:T(8,128)(2,1)S(1)} %get-tuple-element.63.opposite.swapped), custom_call_target="tpu_custom_call" | custom-call | tf_op jit(solution)/shard_map/pallas_call | solution.py:19
  50.5 3.7 %collective-permute-start.19 = (bf16[256,512]{1,0:T(8,128)(2,1)S(1)}, bf16[256,512]{1,0:T(8,128)(2,1)S(1)}, u32[]{:S(2)}, u32[]{:S(2)}) collective-permute-start(bf16[256,512]{1,0:T(8,128)(2,1)S(1)} %shard_map.45.near), channel_id=1, source_target_pairs={{0,1},{1,0},{2,3},{3,2},{4,5},{5,4},{6,7},{7,6},{8,9},{9,8},{10,11... | collective-permute-start | bytes 786440 | tf_op jit(solution)/shard_map/ppermute | solution.py:315
  55.4 1.8 %shard_map.46 = (bf16[512,1024]{1,0:T(8,128)(2,1)S(1)}, bf16[512,1024]{1,0:T(8,128)(2,1)S(1)}) custom-call(s32[8]{0:T(128)S(1)} %broadcast_xor_fusion.order, s32[1]{0:T(128)} %bitcast.middle, bf16[256,512]{1,0:T(8,128)(2,1)S(1)} %shard_map.45.near, bf16[256,512]{1,0:T(8,128)(2,1)S(1)} %collective-permute-done.19.far, ...), custom_call_target="tpu_custom_call" | custom-call | tf_op jit(solution)/shard_map/pallas_call | solution.py:19
  57.2 1.4 %collective-permute-start.29 = (bf16[512,1024]{1,0:T(8,128)(2,1)S(1)}, bf16[512,1024]{1,0:T(8,128)(2,1)S(1)}, u32[]{:S(2)}, u32[]{:S(2)}) collective-permute-start(bf16[512,1024]{1,0:T(8,128)(2,1)S(1)} %get-tuple-element.69), channel_id=1, source_target_pairs={{8,0},{16,24},{9,1},{17,25},{10,2},{18,26},{11,3},{19,27},{12,4},{... | collective-permute-start | bytes 3145736 | tf_op jit(solution)/shard_map/ppermute | solution.py:399
  59.6 2.8 %collective-permute-start.31 = (bf16[512,1024]{1,0:T(8,128)(2,1)S(1)}, bf16[512,1024]{1,0:T(8,128)(2,1)S(1)}, u32[]{:S(2)}, u32[]{:S(2)}) collective-permute-start(bf16[512,1024]{1,0:T(8,128)(2,1)S(1)} %get-tuple-element.86), channel_id=1, source_target_pairs={{8,16},{16,8},{9,17},{17,9},{10,18},{18,10},{11,19},{19,11},{12,20... | collective-permute-start | bytes 3145736 | tf_op jit(solution)/shard_map/ppermute | solution.py:399
  62.5 1.3 %collective-permute-start.22 = (bf16[64,1024]{1,0:T(8,128)(2,1)S(1)}, bf16[64,1024]{1,0:T(8,128)(2,1)S(1)}, u32[]{:S(2)}, u32[]{:S(2)}) collective-permute-start(bf16[64,1024]{1,0:T(8,128)(2,1)S(1)} %get-tuple-element.76), channel_id=1, source_target_pairs={{0,2},{1,3},{2,0},{3,1},{4,6},{5,7},{6,4},{7,5},{8,10},{9,11},{10,... | collective-permute-start | bytes 393224 | tf_op jit(solution)/shard_map/ppermute | solution.py:315
  65.2 2.6 %shard_map.50.held = f32[512,1024]{1,0:T(8,128)S(1)} custom-call(s32[8]{0:T(128)S(1)} %broadcast_xor_fusion.order, s32[1]{0:T(128)} %bitcast.middle, bf16[256,640]{1,0:T(8,128)(2,1)S(1)} %pad_maximum_fusion.near, bf16[256,640]{1,0:T(8,128)(2,1)S(1)} %collective-permute-done.25.far, bf16[512,1024]{1,0:T(8,128)(2,1)S(1)} %get-tuple-element.79.own, ...), custom_call_target="tpu_custom_call" | custom-call | tf_op jit(solution)/shard_map/pallas_call | solution.py:19
  67.8 2.7 %collective-permute-done.24.c = bf16[64,1024]{1,0:T(8,128)(2,1)S(1)} collective-permute-done((bf16[64,1024]{1,0:T(8,128)(2,1)S(1)}, bf16[64,1024]{1,0:T(8,128)(2,1)S(1)}, u32[]{:S(2)}, u32[]{:S(2)}) %collective-permute-start.24) | collective-permute-done | bytes 131104 | tf_op jit(solution)/shard_map/ppermute | solution.py:315
  70.6 1.4 %collective-permute-start.26 = (bf16[64,1024]{1,0:T(8,128)(2,1)S(1)}, bf16[64,1024]{1,0:T(8,128)(2,1)S(1)}, u32[]{:S(2)}, u32[]{:S(2)}) collective-permute-start(bf16[64,1024]{1,0:T(8,128)(2,1)S(1)} %shard_map.49.refs_0_), channel_id=1, source_target_pairs={{0,2},{1,3},{2,0},{3,1},{4,6},{5,7},{6,4},{7,5},{8,10},{9,11},{10,... | collective-permute-start | bytes 393224 | tf_op jit(solution)/shard_map/ppermute | solution.py:315
  73.3 1.5 %collective-permute-done.26.refs_1_ = bf16[64,1024]{1,0:T(8,128)(2,1)S(1)} collective-permute-done((bf16[64,1024]{1,0:T(8,128)(2,1)S(1)}, bf16[64,1024]{1,0:T(8,128)(2,1)S(1)}, u32[]{:S(2)}, u32[]{:S(2)}) %collective-permute-start.26) | collective-permute-done | bytes 131104 | tf_op jit(solution)/shard_map/ppermute | solution.py:315
  74.8 2.6 %collective-permute-done.27.refs_2_ = bf16[64,1024]{1,0:T(8,128)(2,1)S(1)} collective-permute-done((bf16[64,1024]{1,0:T(8,128)(2,1)S(1)}, bf16[64,1024]{1,0:T(8,128)(2,1)S(1)}, u32[]{:S(2)}, u32[]{:S(2)}) %collective-permute-start.27) | collective-permute-done | bytes 131104 | tf_op jit(solution)/shard_map/ppermute | solution.py:315
  77.6 3.2 %collective-permute-done.29.out = bf16[512,1024]{1,0:T(8,128)(2,1)S(1)} collective-permute-done((bf16[512,1024]{1,0:T(8,128)(2,1)S(1)}, bf16[512,1024]{1,0:T(8,128)(2,1)S(1)}, u32[]{:S(2)}, u32[]{:S(2)}) %collective-permute-start.29) | collective-permute-done | bytes 1048608 | tf_op jit(solution)/shard_map/ppermute | solution.py:399
  81.9 3.8 %collective-permute-done.31.over = bf16[512,1024]{1,0:T(8,128)(2,1)S(1)} collective-permute-done((bf16[512,1024]{1,0:T(8,128)(2,1)S(1)}, bf16[512,1024]{1,0:T(8,128)(2,1)S(1)}, u32[]{:S(2)}, u32[]{:S(2)}) %collective-permute-start.31) | collective-permute-done | bytes 1048608 | tf_op jit(solution)/shard_map/ppermute | solution.py:399
  85.7 3.0 %shard_map.52 = f32[512,1024]{1,0:T(8,128)} custom-call(s32[8]{0:T(128)S(1)} %broadcast_xor_fusion.order, s32[1]{0:T(128)} %bitcast.middle, bf16[256,1024]{1,0:T(8,128)(2,1)S(1)} %shard_map.51.near, bf16[256,1024]{1,0:T(8,128)(2,1)S(1)} %collective-permute-done.30.far, bf16[512,1024]{1,0:T(8,128)(2,1)S(1)} %get-tuple-element.62.beside, ...), custom_call_target="tpu_custom_call" | custom-call | tf_op jit(solution)/shard_map/pallas_call | solution.py:19
  (53 shorter events, 20.8 us)
Async XLA Ops:
  1.5 8.5 %collective-permute-start.2 = (f32[2,1024]{1,0:T(2,128)S(1)}, f32[2,1024]{1,0:T(2,128)S(1)}, u32[]{:S(2)}, u32[]{:S(2)}) collective-permute-start(f32[2,1024]{1,0:T(2,128)S(1)} %shard_map.37), channel_id=1, source_target_pairs={{0,24},{8,0},{16,8},{24,16},{1,25},{9,1},{17,9},{25,17},{2,26},{10... | collective-permute-start | bytes 24584 | tf_op jit(solution)/shard_map/ppermute | solution.py:363
  1.6 8.4 %collective-permute-start.1 = (f32[2,1024]{1,0:T(2,128)S(1)}, f32[2,1024]{1,0:T(2,128)S(1)}, u32[]{:S(2)}, u32[]{:S(2)}) collective-permute-start(f32[2,1024]{1,0:T(2,128)S(1)} %shard_map.37), channel_id=1, source_target_pairs={{0,16},{8,24},{16,0},{24,8},{1,17},{9,25},{17,1},{25,9},{2,18},{10... | collective-permute-start | bytes 24584 | tf_op jit(solution)/shard_map/ppermute | solution.py:363
  4.1 6.0 %collective-permute-start = (f32[2,1024]{1,0:T(2,128)S(1)}, f32[2,1024]{1,0:T(2,128)S(1)}, u32[]{:S(2)}, u32[]{:S(2)}) collective-permute-start(f32[2,1024]{1,0:T(2,128)S(1)} %shard_map.37), channel_id=1, source_target_pairs={{0,8},{8,16},{16,24},{24,0},{1,9},{9,17},{17,25},{25,1},{2,10},{10... | collective-permute-start | bytes 24584 | tf_op jit(solution)/shard_map/ppermute | solution.py:363
  6.3 23.4 %collective-permute-start.10 = (bf16[512,1024]{1,0:T(8,128)(2,1)}, bf16[512,1024]{1,0:T(8,128)(2,1)S(1)}, u32[]{:S(2)}, u32[]{:S(2)}) collective-permute-start(bf16[512,1024]{1,0:T(8,128)(2,1)} %z.5), channel_id=1, source_target_pairs={{0,8},{8,0},{16,24},{24,16},{1,9},{9,1},{17,25},{25,17},{2,10},{10... | collective-permute-start | bytes 3145736 | tf_op jit(solution)/shard_map/ppermute | solution.py:366
  6.3 25.3 %collective-permute-start.11 = (bf16[512,1024]{1,0:T(8,128)(2,1)}, bf16[512,1024]{1,0:T(8,128)(2,1)}, u32[]{:S(2)}, u32[]{:S(2)}) collective-permute-start(bf16[512,1024]{1,0:T(8,128)(2,1)} %z.5), channel_id=1, source_target_pairs={{8,16},{16,8},{9,17},{17,9},{10,18},{18,10},{11,19},{19,11},{12,20... | collective-permute-start | bytes 3145736 | tf_op jit(solution)/shard_map/ppermute | solution.py:367
  12.5 3.1 %collective-permute-start.3 = (bf16[256,640]{1,0:T(8,128)(2,1)S(1)}, bf16[256,640]{1,0:T(8,128)(2,1)S(1)}, u32[]{:S(2)}, u32[]{:S(2)}) collective-permute-start(bf16[256,640]{1,0:T(8,128)(2,1)S(1)} %get-tuple-element.48), channel_id=1, source_target_pairs={{0,1},{1,0},{2,3},{3,2},{4,5},{5,4},{6,7},{7,6},{8,9},{9,8},{10,11... | collective-permute-start | bytes 983048 | tf_op jit(solution)/shard_map/ppermute | solution.py:315
  15.7 3.8 %collective-permute-start.4 = (bf16[64,640]{1,0:T(8,128)(2,1)S(1)}, bf16[64,640]{1,0:T(8,128)(2,1)S(1)}, u32[]{:S(2)}, u32[]{:S(2)}) collective-permute-start(bf16[64,640]{1,0:T(8,128)(2,1)S(1)} %get-tuple-element.50), channel_id=1, source_target_pairs={{0,2},{1,3},{2,0},{3,1},{4,6},{5,7},{6,4},{7,5},{8,10},{9,11},{10,... | collective-permute-start | bytes 245768 | tf_op jit(solution)/shard_map/ppermute | solution.py:315
  17.0 3.7 %collective-permute-start.5 = (bf16[64,640]{1,0:T(8,128)(2,1)S(1)}, bf16[64,640]{1,0:T(8,128)(2,1)S(1)}, u32[]{:S(2)}, u32[]{:S(2)}) collective-permute-start(bf16[64,640]{1,0:T(8,128)(2,1)S(1)} %get-tuple-element.51), channel_id=1, source_target_pairs={{0,4},{1,5},{2,6},{3,7},{4,0},{5,1},{6,2},{7,3},{8,12},{9,13},{10,... | collective-permute-start | bytes 245768 | tf_op jit(solution)/shard_map/ppermute | solution.py:315
  18.2 4.2 %collective-permute-start.6 = (bf16[64,640]{1,0:T(8,128)(2,1)S(1)}, bf16[64,640]{1,0:T(8,128)(2,1)S(1)}, u32[]{:S(2)}, u32[]{:S(2)}) collective-permute-start(bf16[64,640]{1,0:T(8,128)(2,1)S(1)} %get-tuple-element.52), channel_id=1, source_target_pairs={{0,6},{1,7},{2,4},{3,5},{4,2},{5,3},{6,0},{7,1},{8,14},{9,15},{10,... | collective-permute-start | bytes 245768 | tf_op jit(solution)/shard_map/ppermute | solution.py:315
  22.5 4.4 %collective-permute-start.9 = (bf16[64,640]{1,0:T(8,128)(2,1)S(1)}, bf16[64,640]{1,0:T(8,128)(2,1)S(1)}, u32[]{:S(2)}, u32[]{:S(2)}) collective-permute-start(bf16[64,640]{1,0:T(8,128)(2,1)S(1)} %shard_map.40), channel_id=1, source_target_pairs={{0,6},{1,7},{2,4},{3,5},{4,2},{5,3},{6,0},{7,1},{8,14},{9,15},{10,... | collective-permute-start | bytes 245768 | tf_op jit(solution)/shard_map/ppermute | solution.py:315
  23.2 4.6 %collective-permute-start.8 = (bf16[64,640]{1,0:T(8,128)(2,1)S(1)}, bf16[64,640]{1,0:T(8,128)(2,1)S(1)}, u32[]{:S(2)}, u32[]{:S(2)}) collective-permute-start(bf16[64,640]{1,0:T(8,128)(2,1)S(1)} %shard_map.40), channel_id=1, source_target_pairs={{0,4},{1,5},{2,6},{3,7},{4,0},{5,1},{6,2},{7,3},{8,12},{9,13},{10,... | collective-permute-start | bytes 245768 | tf_op jit(solution)/shard_map/ppermute | solution.py:315
  24.4 3.7 %collective-permute-start.7 = (bf16[64,640]{1,0:T(8,128)(2,1)S(1)}, bf16[64,640]{1,0:T(8,128)(2,1)S(1)}, u32[]{:S(2)}, u32[]{:S(2)}) collective-permute-start(bf16[64,640]{1,0:T(8,128)(2,1)S(1)} %shard_map.40), channel_id=1, source_target_pairs={{0,2},{1,3},{2,0},{3,1},{4,6},{5,7},{6,4},{7,5},{8,10},{9,11},{10,... | collective-permute-start | bytes 245768 | tf_op jit(solution)/shard_map/ppermute | solution.py:315
  31.6 27.0 %collective-permute-start.20 = (bf16[512,1024]{1,0:T(8,128)(2,1)}, bf16[512,1024]{1,0:T(8,128)(2,1)}, u32[]{:S(2)}, u32[]{:S(2)}) collective-permute-start(bf16[512,1024]{1,0:T(8,128)(2,1)} %z.5), channel_id=1, source_target_pairs={{0,24},{24,0},{1,25},{25,1},{2,26},{26,2},{3,27},{27,3},{4,28},{28... | collective-permute-start | bytes 3145736 | tf_op jit(solution)/shard_map/ppermute | solution.py:382
  35.5 3.7 %collective-permute-start.12 = (bf16[256,512]{1,0:T(8,128)(2,1)S(1)}, bf16[256,512]{1,0:T(8,128)(2,1)S(1)}, u32[]{:S(2)}, u32[]{:S(2)}) collective-permute-start(bf16[256,512]{1,0:T(8,128)(2,1)S(1)} %get-tuple-element.56), channel_id=1, source_target_pairs={{0,1},{1,0},{2,3},{3,2},{4,5},{5,4},{6,7},{7,6},{8,9},{9,8},{10,11... | collective-permute-start | bytes 786440 | tf_op jit(solution)/shard_map/ppermute | solution.py:315
  39.2 3.2 %collective-permute-start.13 = (bf16[64,512]{1,0:T(8,128)(2,1)S(1)}, bf16[64,512]{1,0:T(8,128)(2,1)S(1)}, u32[]{:S(2)}, u32[]{:S(2)}) collective-permute-start(bf16[64,512]{1,0:T(8,128)(2,1)S(1)} %get-tuple-element.58), channel_id=1, source_target_pairs={{0,2},{1,3},{2,0},{3,1},{4,6},{5,7},{6,4},{7,5},{8,10},{9,11},{10,... | collective-permute-start | bytes 196616 | tf_op jit(solution)/shard_map/ppermute | solution.py:315
  40.5 3.1 %collective-permute-start.14 = (bf16[64,512]{1,0:T(8,128)(2,1)S(1)}, bf16[64,512]{1,0:T(8,128)(2,1)S(1)}, u32[]{:S(2)}, u32[]{:S(2)}) collective-permute-start(bf16[64,512]{1,0:T(8,128)(2,1)S(1)} %get-tuple-element.59), channel_id=1, source_target_pairs={{0,4},{1,5},{2,6},{3,7},{4,0},{5,1},{6,2},{7,3},{8,12},{9,13},{10,... | collective-permute-start | bytes 196616 | tf_op jit(solution)/shard_map/ppermute | solution.py:315
  41.7 4.0 %collective-permute-start.15 = (bf16[64,512]{1,0:T(8,128)(2,1)S(1)}, bf16[64,512]{1,0:T(8,128)(2,1)S(1)}, u32[]{:S(2)}, u32[]{:S(2)}) collective-permute-start(bf16[64,512]{1,0:T(8,128)(2,1)S(1)} %get-tuple-element.60), channel_id=1, source_target_pairs={{0,6},{1,7},{2,4},{3,5},{4,2},{5,3},{6,0},{7,1},{8,14},{9,15},{10,... | collective-permute-start | bytes 196616 | tf_op jit(solution)/shard_map/ppermute | solution.py:315
  45.8 4.0 %collective-permute-start.16 = (bf16[64,512]{1,0:T(8,128)(2,1)S(1)}, bf16[64,512]{1,0:T(8,128)(2,1)S(1)}, u32[]{:S(2)}, u32[]{:S(2)}) collective-permute-start(bf16[64,512]{1,0:T(8,128)(2,1)S(1)} %shard_map.43.refs_0_.first), channel_id=1, source_target_pairs={{0,2},{1,3},{2,0},{3,1},{4,6},{5,7},{6,4},{7,5},{8,10},{9,11},{10,... | collective-permute-start | bytes 196616 | tf_op jit(solution)/shard_map/ppermute | solution.py:315
  46.2 3.6 %collective-permute-start.17 = (bf16[64,512]{1,0:T(8,128)(2,1)S(1)}, bf16[64,512]{1,0:T(8,128)(2,1)S(1)}, u32[]{:S(2)}, u32[]{:S(2)}) collective-permute-start(bf16[64,512]{1,0:T(8,128)(2,1)S(1)} %shard_map.43.refs_0_.first), channel_id=1, source_target_pairs={{0,4},{1,5},{2,6},{3,7},{4,0},{5,1},{6,2},{7,3},{8,12},{9,13},{10,... | collective-permute-start | bytes 196616 | tf_op jit(solution)/shard_map/ppermute | solution.py:315
  46.5 4.0 %collective-permute-start.18 = (bf16[64,512]{1,0:T(8,128)(2,1)S(1)}, bf16[64,512]{1,0:T(8,128)(2,1)S(1)}, u32[]{:S(2)}, u32[]{:S(2)}) collective-permute-start(bf16[64,512]{1,0:T(8,128)(2,1)S(1)} %shard_map.43.refs_0_.first), channel_id=1, source_target_pairs={{0,6},{1,7},{2,4},{3,5},{4,2},{5,3},{6,0},{7,1},{8,14},{9,15},{10,... | collective-permute-start | bytes 196616 | tf_op jit(solution)/shard_map/ppermute | solution.py:315
  50.5 4.9 %collective-permute-start.19 = (bf16[256,512]{1,0:T(8,128)(2,1)S(1)}, bf16[256,512]{1,0:T(8,128)(2,1)S(1)}, u32[]{:S(2)}, u32[]{:S(2)}) collective-permute-start(bf16[256,512]{1,0:T(8,128)(2,1)S(1)} %shard_map.45.near), channel_id=1, source_target_pairs={{0,1},{1,0},{2,3},{3,2},{4,5},{5,4},{6,7},{7,6},{8,9},{9,8},{10,11... | collective-permute-start | bytes 786440 | tf_op jit(solution)/shard_map/ppermute | solution.py:315
  57.2 23.5 %collective-permute-start.29 = (bf16[512,1024]{1,0:T(8,128)(2,1)S(1)}, bf16[512,1024]{1,0:T(8,128)(2,1)S(1)}, u32[]{:S(2)}, u32[]{:S(2)}) collective-permute-start(bf16[512,1024]{1,0:T(8,128)(2,1)S(1)} %get-tuple-element.69), channel_id=1, source_target_pairs={{8,0},{16,24},{9,1},{17,25},{10,2},{18,26},{11,3},{19,27},{12,4},{... | collective-permute-start | bytes 3145736 | tf_op jit(solution)/shard_map/ppermute | solution.py:399
  58.8 3.6 %collective-permute-start.21 = (bf16[256,1024]{1,0:T(8,128)(2,1)S(1)}, bf16[256,1024]{1,0:T(8,128)(2,1)S(1)}, u32[]{:S(2)}, u32[]{:S(2)}) collective-permute-start(bf16[256,1024]{1,0:T(8,128)(2,1)S(1)} %get-tuple-element.74), channel_id=1, source_target_pairs={{0,1},{1,0},{2,3},{3,2},{4,5},{5,4},{6,7},{7,6},{8,9},{9,8},{10,11... | collective-permute-start | bytes 1572872 | tf_op jit(solution)/shard_map/ppermute | solution.py:315
  59.5 5.5 %collective-permute-start.25 = (bf16[256,640]{1,0:T(8,128)(2,1)S(1)}, bf16[256,640]{1,0:T(8,128)(2,1)S(1)}, u32[]{:S(2)}, u32[]{:S(2)}) collective-permute-start(bf16[256,640]{1,0:T(8,128)(2,1)S(1)} %pad_maximum_fusion.near), channel_id=1, source_target_pairs={{0,1},{1,0},{2,3},{3,2},{4,5},{5,4},{6,7},{7,6},{8,9},{9,8},{10,11... | collective-permute-start | bytes 983048 | tf_op jit(solution)/shard_map/ppermute | solution.py:315
  59.6 26.2 %collective-permute-start.31 = (bf16[512,1024]{1,0:T(8,128)(2,1)S(1)}, bf16[512,1024]{1,0:T(8,128)(2,1)S(1)}, u32[]{:S(2)}, u32[]{:S(2)}) collective-permute-start(bf16[512,1024]{1,0:T(8,128)(2,1)S(1)} %get-tuple-element.86), channel_id=1, source_target_pairs={{8,16},{16,8},{9,17},{17,9},{10,18},{18,10},{11,19},{19,11},{12,20... | collective-permute-start | bytes 3145736 | tf_op jit(solution)/shard_map/ppermute | solution.py:399
  62.5 5.3 %collective-permute-start.22 = (bf16[64,1024]{1,0:T(8,128)(2,1)S(1)}, bf16[64,1024]{1,0:T(8,128)(2,1)S(1)}, u32[]{:S(2)}, u32[]{:S(2)}) collective-permute-start(bf16[64,1024]{1,0:T(8,128)(2,1)S(1)} %get-tuple-element.76), channel_id=1, source_target_pairs={{0,2},{1,3},{2,0},{3,1},{4,6},{5,7},{6,4},{7,5},{8,10},{9,11},{10,... | collective-permute-start | bytes 393224 | tf_op jit(solution)/shard_map/ppermute | solution.py:315
  63.7 4.1 %collective-permute-start.23 = (bf16[64,1024]{1,0:T(8,128)(2,1)S(1)}, bf16[64,1024]{1,0:T(8,128)(2,1)S(1)}, u32[]{:S(2)}, u32[]{:S(2)}) collective-permute-start(bf16[64,1024]{1,0:T(8,128)(2,1)S(1)} %get-tuple-element.77), channel_id=1, source_target_pairs={{0,4},{1,5},{2,6},{3,7},{4,0},{5,1},{6,2},{7,3},{8,12},{9,13},{10,... | collective-permute-start | bytes 393224 | tf_op jit(solution)/shard_map/ppermute | solution.py:315
  65.0 5.5 %collective-permute-start.24 = (bf16[64,1024]{1,0:T(8,128)(2,1)S(1)}, bf16[64,1024]{1,0:T(8,128)(2,1)S(1)}, u32[]{:S(2)}, u32[]{:S(2)}) collective-permute-start(bf16[64,1024]{1,0:T(8,128)(2,1)S(1)} %get-tuple-element.78), channel_id=1, source_target_pairs={{0,6},{1,7},{2,4},{3,5},{4,2},{5,3},{6,0},{7,1},{8,14},{9,15},{10,... | collective-permute-start | bytes 393224 | tf_op jit(solution)/shard_map/ppermute | solution.py:315
  70.6 4.2 %collective-permute-start.26 = (bf16[64,1024]{1,0:T(8,128)(2,1)S(1)}, bf16[64,1024]{1,0:T(8,128)(2,1)S(1)}, u32[]{:S(2)}, u32[]{:S(2)}) collective-permute-start(bf16[64,1024]{1,0:T(8,128)(2,1)S(1)} %shard_map.49.refs_0_), channel_id=1, source_target_pairs={{0,2},{1,3},{2,0},{3,1},{4,6},{5,7},{6,4},{7,5},{8,10},{9,11},{10,... | collective-permute-start | bytes 393224 | tf_op jit(solution)/shard_map/ppermute | solution.py:315
  72.0 5.3 %collective-permute-start.27 = (bf16[64,1024]{1,0:T(8,128)(2,1)S(1)}, bf16[64,1024]{1,0:T(8,128)(2,1)S(1)}, u32[]{:S(2)}, u32[]{:S(2)}) collective-permute-start(bf16[64,1024]{1,0:T(8,128)(2,1)S(1)} %shard_map.49.refs_0_), channel_id=1, source_target_pairs={{0,4},{1,5},{2,6},{3,7},{4,0},{5,1},{6,2},{7,3},{8,12},{9,13},{10,... | collective-permute-start | bytes 393224 | tf_op jit(solution)/shard_map/ppermute | solution.py:315
  72.3 5.3 %collective-permute-start.28 = (bf16[64,1024]{1,0:T(8,128)(2,1)S(1)}, bf16[64,1024]{1,0:T(8,128)(2,1)S(1)}, u32[]{:S(2)}, u32[]{:S(2)}) collective-permute-start(bf16[64,1024]{1,0:T(8,128)(2,1)S(1)} %shard_map.49.refs_0_), channel_id=1, source_target_pairs={{0,6},{1,7},{2,4},{3,5},{4,2},{5,3},{6,0},{7,1},{8,14},{9,15},{10,... | collective-permute-start | bytes 393224 | tf_op jit(solution)/shard_map/ppermute | solution.py:315
  80.7 5.0 %collective-permute-start.30 = (bf16[256,1024]{1,0:T(8,128)(2,1)S(1)}, bf16[256,1024]{1,0:T(8,128)(2,1)S(1)}, u32[]{:S(2)}, u32[]{:S(2)}) collective-permute-start(bf16[256,1024]{1,0:T(8,128)(2,1)S(1)} %shard_map.51.near), channel_id=1, source_target_pairs={{0,1},{1,0},{2,3},{3,2},{4,5},{5,4},{6,7},{7,6},{8,9},{9,8},{10,11... | collective-permute-start | bytes 1572872 | tf_op jit(solution)/shard_map/ppermute | solution.py:315
  (1 other events, 6.5 us)
